TPU v7x, 32 devices: a whole 2x2x4 slice. The times are simulated.
32 devices in a mesh: ka: 4 (over z), band: 8 (over y, x, core).
Axes of the slice: x: 2, y: 2, z: 4, core: 2. Of those that a mesh axis runs over, the one named last changes fastest.
Arguments:
- start_vec: float32 [12, 4096], P('ka', 'band'), may hold values from -360 to 360
- val_energy: float32 [12, 64], P('ka', 'band'), may hold values from -3 to -0.5
- cond_energy: float32 [12, 64], P('ka'), may hold values from 0.5 to 3
- val_orb: bfloat16 [12, 64, 8192], P('ka', 'band'), may hold values from -6 to 6
- cond_orb: bfloat16 [12, 64, 8192], P('ka'), may hold values from -6 to 6
- coulomb: bfloat16 [8192, 8192], P(('ka', 'band')), may hold values from -3 to 3
- screened: bfloat16 [8192, 8192], P('band', 'ka'), may hold values from -6 to 6
Outputs:
- next_vec: float32 [12, 4096], P('ka', 'band')
- coeffs: float32 [4], replicated
All inputs are finite; a program needn't handle non-finite values.
Results may differ from a plain program's by a relative error of at most 0.0075.
Values may be sent and summed in bfloat16 or wider, within the bound.
No kernel may reach another device: no remote copies, remote signals or barrier semaphores. Data moves between devices by JAX's collectives and lax.ppermute only.
A program may use at most 128 MiB of HBM per device.

v0:
```python
import math

import jax
import jax.numpy as jnp
from jax import lax
from jax.sharding import PartitionSpec as P

STEPS = 2


def per_device(start_vec, val_energy, cond_energy, val_orb, cond_orb, coulomb, screened):
    n_ka = lax.axis_size("ka")
    n_band = lax.axis_size("band")
    devices = n_ka * n_band
    k_dev = start_vec.shape[0]
    pair_blk = start_vec.shape[1]
    nv_blk = val_orb.shape[1]
    n_cond = cond_orb.shape[1]
    n_val = nv_blk * n_band
    npt_all = cond_orb.shape[2]
    k_points = k_dev * n_ka
    mu_blk = screened.shape[0]
    count_all = k_points * n_val * n_cond
    kernel_scale = 1.0 / (npt_all * math.sqrt(count_all))
    cond_local = lax.dynamic_slice_in_dim(cond_orb, lax.axis_index("band") * mu_blk, mu_blk, 2)
    cond_pts = lax.all_gather(cond_local, "ka", axis=0, tiled=True)
    val_wide = lax.all_gather(val_orb, "band", axis=1, tiled=True)
    val_pts = lax.all_to_all(val_wide, "ka", split_axis=2, concat_axis=0, tiled=True)
    val_f = val_orb.astype(jnp.float32)
    energy_gap = (cond_energy[:, None, :] - val_energy[:, :, None]).reshape(k_dev, pair_blk)
    screen_f = screened.astype(jnp.float32)
    start_sq = lax.psum(jnp.sum(start_vec * start_vec), ("ka", "band"))
    current = start_vec / jnp.sqrt(start_sq / count_all + 1e-06)
    previous = jnp.zeros_like(start_vec)
    beta_val = jnp.float32(0.0)
    alphas = []
    betas = []
    for turn_index in range(STEPS):
        vec_bf = current.astype(jnp.bfloat16)
        local_vec = vec_bf.reshape(k_dev, nv_blk, n_cond)
        gathered = lax.all_gather(vec_bf[None], ("ka", "band"), axis=0, tiled=True)
        full_vec = (
            gathered.reshape(n_ka, n_band, k_dev, nv_blk, n_cond)
            .transpose(0, 2, 1, 3, 4)
            .reshape(k_points, n_val, n_cond)
        )
        pair_part = jnp.einsum(
            "kvc,kcp->kvp", local_vec, cond_orb, preferred_element_type=jnp.float32
        )
        density_part = jnp.sum(val_f * pair_part, axis=(0, 1))
        density = lax.psum(density_part, ("ka", "band"))
        pot_block = kernel_scale * jnp.dot(
            coulomb, density.astype(jnp.bfloat16), preferred_element_type=jnp.float32
        )
        potential = lax.all_gather(pot_block, ("ka", "band"), axis=0, tiled=True)
        weighted = (val_f * potential).astype(jnp.bfloat16)
        exchange_term = jnp.einsum(
            "kvp,kcp->kvc", weighted, cond_orb, preferred_element_type=jnp.float32
        )
        mixed_val = jnp.einsum(
            "kvc,kvn->kcn", full_vec, val_pts, preferred_element_type=jnp.float32
        ).astype(jnp.bfloat16)
        amp = jnp.einsum("kcm,kcn->mn", cond_pts, mixed_val, preferred_element_type=jnp.float32)
        kern = (screen_f * amp * kernel_scale).astype(jnp.bfloat16)
        folded = jnp.einsum("mn,kvn->kvm", kern, val_pts, preferred_element_type=jnp.float32)
        folded_high = folded.astype(jnp.bfloat16)
        folded_low = (folded - folded_high.astype(jnp.float32)).astype(jnp.bfloat16)
        folded_pair = jnp.concatenate([folded_high, folded_low], axis=1)
        direct_both = jnp.einsum(
            "kcm,kvm->kvc", cond_pts, folded_pair, preferred_element_type=jnp.float32
        )
        direct_part = direct_both[:, :n_val] + direct_both[:, n_val:]
        arranged = (
            direct_part.reshape(n_ka, k_dev, n_band, nv_blk, n_cond)
            .transpose(0, 2, 1, 3, 4)
            .reshape(devices, k_dev, pair_blk)
        )
        direct_term = lax.psum_scatter(arranged, ("ka", "band"), scatter_dimension=0, tiled=True)[0]
        resid_vec = (
            energy_gap * current + 2.0 * exchange_term.reshape(k_dev, pair_blk) - direct_term
        )
        if turn_index > 0:
            resid_vec = resid_vec - beta_val * previous
        cross_sum = lax.psum(jnp.sum(current * resid_vec), ("ka", "band"))
        alpha_val = cross_sum / count_all
        resid_vec = resid_vec - alpha_val * current
        square_sum = lax.psum(jnp.sum(resid_vec * resid_vec), ("ka", "band"))
        mean_sq = square_sum / count_all
        beta_val = jnp.sqrt(mean_sq + 1e-06)
        previous = current
        current = resid_vec / beta_val
        alphas.append(alpha_val)
        betas.append(beta_val)
    coeffs = jnp.stack(alphas + betas)
    return (current, coeffs)


def solution(mesh):
    in_specs = (
        P("ka", "band"),
        P("ka", "band"),
        P("ka", None),
        P("ka", "band", None),
        P("ka", None, None),
        P(("ka", "band"), None),
        P("band", "ka"),
    )
    out_specs = (P("ka", "band"), P())
    return jax.shard_map(
        per_device, mesh=mesh, in_specs=in_specs, out_specs=out_specs, check_vma=False
    )
```

profile of v0, /device:TPU:0, one launch (start us, length us, event | category | flops | bytes accessed | tf_op | source)
XLA Modules:
  0.0 852.4 jit_solution(17776955811351894035)
XLA Ops:
  8.7 37.1 %all-gather.11.cloned.1.call-done = bf16[3,64,8192]{2,1,0:T(8,128)(2,1)} async-done(((bf16[3,8,8192]{2,1,0:T(8,128)(2,1)}), bf16[3,64,8192]{2,1,0:T(8,128)(2,1)}) %all-gather.11.cloned.1.call-update) | async-done | bytes 3145744 | tf_op jit(solution)/shard_map/all_gather | solution.py:27
  45.8 11.2 %copy.37 = bf16[3,64,8192]{1,0,2:T(4,128)(2,1)} copy(bf16[3,64,8192]{2,1,0:T(8,128)(2,1)} %all-gather.11.cloned.1.call-done) | data formatting | bytes 6291456 | tf_op jit(solution)/shard_map/all_gather | solution.py:27
  57.0 8.6 %reshape.83 = bf16[4,2,196608]{2,1,0:T(2,128)(2,1)} reshape(bf16[8192,3,64]{2,1,0:T(4,128)(2,1)} %bitcast.95) | data formatting | bytes 6291456
  65.7 4.8 all-to-all-start
  72.1 114.5 %psum.49 = f32[]{:T(128)} all-reduce(f32[]{:T(128)} %multiply_reduce_fusion.4), channel_id=1, replica_groups=mesh['ka'=4,'band'=8] {'ka','band'}, use_global_device_ids=true, to_apply=%region_1.0 | all-reduce | flops 1 | bytes 8 | tf_op jit(solution)/shard_map/psum | solution.py:32
  187.2 41.8 %all-gather.3 = bf16[32,3,512]{2,1,0:T(4,128)(2,1)S(1)} all-gather(bf16[1,3,512]{2,1,0:T(4,128)(2,1)S(1)} %fusion.55), channel_id=2, replica_groups=mesh['ka'=4,'band'=8] {'ka','band'}, dimensions={0}, use_global_device_ids=true | all-gather | bytes 101376 | tf_op jit(solution)/shard_map/all_gather | solution.py:41
  229.7 1.7 reshape.49
  231.4 1.6 copy.36
  234.4 1.1 fusion.18
  235.5 37.7 %psum.50 = bf16[8192]{0:T(1024)(128)(2,1)} all-reduce(f32[8192]{0:T(1024)} %fusion.18), channel_id=1, replica_groups=mesh['ka'=4,'band'=8] {'ka','band'}, use_global_device_ids=true, to_apply=%region_3.0 | all-reduce | flops 8192 | bytes 49152 | tf_op jit(solution)/shard_map/psum | solution.py:51
  274.0 3.4 fusion.33
  277.3 40.4 %all-gather.2 = f32[32,1,256]{2,1,0:T(1,128)S(1)} all-gather(f32[1,1,256]{2,1,0:T(1,128)S(1)} %bitcast.112), channel_id=1, replica_groups=mesh['ka'=4,'band'=8] {'ka','band'}, dimensions={0}, use_global_device_ids=true | all-gather | bytes 33792 | tf_op jit(solution)/shard_map/all_gather | solution.py:55
  317.8 1.5 convolution_multiply_fusion.3
  319.3 8.2 reshape.84
  327.5 12.3 %copy.38 = bf16[3,64,4,2048]{3,1,0,2:T(8,128)(2,1)} copy(bf16[3,64,4,2048]{1,0,3,2:T(4,128)(2,1)} %bitcast.96) | data formatting | bytes 6291456 | tf_op jit(solution)/shard_map/all_to_all | solution.py:28
  339.7 8.7 %fusion.1 = bf16[1024,2048]{1,0:T(8,128)(2,1)} fusion(bf16[1024,2048]{1,0:T(8,128)(2,1)} %param.13, bf16[12,64,1024]{2,1,0:T(8,128)(2,1)} %all-gather.9.cloned.1.call-done, bf16[12,64,64]{2,1,0:T(8,128)(2,1)} %bitcast.105, bf16[12,64,2048]{2,1,0:T(8,128)(2,1)} %bitcast.97), kind=kOutput, calls=%fused_computation.5 | convolution fusion | flops 3432513536 | bytes 13205504 | tf_op jit(solution)/shard_map/kcm,kcn->mn/dot_general | solution.py:63
  348.4 6.7 fusion.17
  355.1 1.2 fusion.8
  356.4 0.9 slice_add_fusion.1
  357.3 1.9 copy.40
  359.2 1.8 copy.41
  361.0 1.8 reshape.52
  363.6 1.4 mul.99
  365.7 115.9 %all-reduce.5.cloned.1.call-done = f32[32,3,512]{2,0,1:T(8,128)} async-done(((f32[32,3,512]{2,0,1:T(8,128)}), f32[32,3,512]{2,0,1:T(8,128)}) %all-reduce.5.cloned.1.call-update) | async-done | bytes 196624
  482.5 1.9 multiply_reduce_fusion.3
  484.4 41.3 %psum.51 = f32[]{:T(128)} all-reduce(f32[]{:T(128)} %get-tuple-element.8), channel_id=1, replica_groups=mesh['ka'=4,'band'=8] {'ka','band'}, use_global_device_ids=true, to_apply=%region_6.0 | all-reduce | flops 1 | bytes 8 | tf_op jit(solution)/shard_map/psum | solution.py:84
  526.3 1.3 multiply_reduce_fusion.2
  527.6 40.3 %psum.52 = f32[]{:T(128)} all-reduce(f32[]{:T(128)} %multiply_reduce_fusion.2), channel_id=1, replica_groups=mesh['ka'=4,'band'=8] {'ka','band'}, use_global_device_ids=true, to_apply=%region_8.0 | all-reduce | flops 1 | bytes 8 | tf_op jit(solution)/shard_map/psum | solution.py:87
  568.7 1.3 fusion.32
  570.0 1.3 reshape.53
  571.3 41.3 %all-gather.5 = bf16[32,3,512]{2,1,0:T(4,128)(2,1)S(1)} all-gather(bf16[1,3,512]{2,1,0:T(4,128)(2,1)} %bitcast.109), channel_id=3, replica_groups=mesh['ka'=4,'band'=8] {'ka','band'}, dimensions={0}, use_global_device_ids=true | all-gather | bytes 101376 | tf_op jit(solution)/shard_map/all_gather | solution.py:41
  613.3 1.7 reshape.54
  615.0 1.6 copy.43
  616.6 8.6 %fusion.3 = bf16[1024,2048]{1,0:T(8,128)(2,1)} fusion(bf16[1024,2048]{1,0:T(8,128)(2,1)} %param.13, bf16[12,64,1024]{2,1,0:T(8,128)(2,1)} %all-gather.9.cloned.1.call-done, bf16[12,64,64]{2,1,0:T(8,128)(2,1)} %bitcast.106, bf16[12,64,2048]{2,1,0:T(8,128)(2,1)} %bitcast.99), kind=kOutput, calls=%fused_computation.7 | convolution fusion | flops 3432513536 | bytes 13205504 | tf_op jit(solution)/shard_map/kcm,kcn->mn/dot_general | solution.py:63
  625.3 6.7 fusion.16
  632.0 1.2 fusion.12
  634.1 1.9 copy.45
  636.0 1.8 copy.50
  637.8 1.9 reshape.80
  639.7 1.8 fusion.19
  641.5 37.7 %psum.53 = bf16[8192]{0:T(1024)(128)(2,1)} all-reduce(f32[8192]{0:T(1024)} %fusion.19), channel_id=1, replica_groups=mesh['ka'=4,'band'=8] {'ka','band'}, use_global_device_ids=true, to_apply=%region_10.0 | all-reduce | flops 8192 | bytes 49152 | tf_op jit(solution)/shard_map/psum | solution.py:51
  679.9 3.4 fusion.34
  683.3 40.2 %all-gather.4 = f32[32,1,256]{2,1,0:T(1,128)S(1)} all-gather(f32[1,1,256]{2,1,0:T(1,128)S(1)} %bitcast.113), channel_id=1, replica_groups=mesh['ka'=4,'band'=8] {'ka','band'}, dimensions={0}, use_global_device_ids=true | all-gather | bytes 33792 | tf_op jit(solution)/shard_map/all_gather | solution.py:55
  723.5 1.5 convolution_multiply_fusion.2
  725.8 34.8 %all-reduce.7.cloned.1.call-done = f32[32,3,512]{2,1,0:T(4,128)} async-done(((f32[32,3,512]{2,1,0:T(4,128)}), f32[32,3,512]{2,1,0:T(4,128)}) %all-reduce.7.cloned.1.call-update) | async-done | bytes 196624
  760.6 1.3 multiply_reduce_fusion.1
  762.0 39.4 %psum.54 = f32[]{:T(128)} all-reduce(f32[]{:T(128)} %get-tuple-element.2), channel_id=1, replica_groups=mesh['ka'=4,'band'=8] {'ka','band'}, use_global_device_ids=true, to_apply=%region_13.0 | all-reduce | flops 1 | bytes 8 | tf_op jit(solution)/shard_map/psum | solution.py:84
  802.6 40.4 %psum.55 = f32[]{:T(128)} all-reduce(f32[]{:T(128)} %multiply_reduce_fusion), channel_id=1, replica_groups=mesh['ka'=4,'band'=8] {'ka','band'}, use_global_device_ids=true, to_apply=%region_15.0 | all-reduce | flops 1 | bytes 8 | tf_op jit(solution)/shard_map/psum | solution.py:87
  (45 shorter events, 12.3 us)
Async XLA Ops:
  8.0 62.6 %copy-start = (bf16[3,64,8192]{2,1,0:T(8,128)(2,1)S(1)}, bf16[3,64,8192]{2,1,0:T(8,128)(2,1)}, u32[]{:S(2)}) copy-start(bf16[3,64,8192]{2,1,0:T(8,128)(2,1)} %param.11) | copy-start | bytes 9437188
  8.0 37.8 %all-gather.11.cloned.1.call-start = ((), (), s32[]{:S(2)}) async-start(), calls=%async_computation.2 | async-start | bytes 3538944 | tf_op jit(solution)/shard_map/all_gather | solution.py:27
  65.7 5.8 copy-start.2
  65.7 168.7 %copy-start.1 = (bf16[3,8,8192]{2,1,0:T(8,128)(2,1)S(1)}, bf16[3,8,8192]{2,1,0:T(8,128)(2,1)}, u32[]{:S(2)}) copy-start(bf16[3,8,8192]{2,1,0:T(8,128)(2,1)} %param.10) | copy-start | bytes 1179652
  65.7 253.6 %all-to-all-start = ((bf16[4,2,196608]{2,1,0:T(2,128)(2,1)}), bf16[4,2,196608]{2,1,0:T(2,128)(2,1)}, u32[]{:S(2)}, u32[]{:S(2)}) async-start(bf16[4,2,196608]{2,1,0:T(2,128)(2,1)} %reshape.83), calls=%async_computation | async-start | bytes 6291456 | tf_op jit(solution)/shard_map/all_to_all | solution.py:28
  70.5 269.2 %all-gather.9.cloned.1.call-start = ((), (), s32[]{:S(2)}) async-start(), calls=%async_computation.1 | async-start | bytes 1966080 | tf_op jit(solution)/shard_map/all_gather | solution.py:26
  71.4 410.3 %all-reduce.5.cloned.1.call-start = ((), (), s32[]{:S(2)}) async-start(), calls=%async_computation.3 | async-start | bytes 393216
  348.4 6.7 copy-start.6
  356.3 6.5 copy-start.4
  356.3 6.5 copy-start.5
  362.8 397.8 %all-reduce.7.cloned.1.call-start = ((), (), s32[]{:S(2)}) async-start(), calls=%async_computation.4 | async-start | bytes 524288
  365.7 202.9 %copy-start.3 = (f32[3,512]{1,0:T(4,128)}, f32[3,512]{1,0:T(4,128)S(1)}, u32[]{:S(2)}) copy-start(f32[3,512]{1,0:T(4,128)S(1)} %sub.41) | copy-start | bytes 18436
  625.3 6.7 copy-start.7
Sparse Core Ops, SparseCore 0:
  10.8 35.0 all-gather.10
Sparse Core Ops, SparseCore 1:
  72.6 59.2 all-gather.8
  362.9 118.7 all-reduce.4
  639.8 120.8 all-reduce.6
where the time goes:
time: 855 us; the launch traced here: 852 us
  blocking collectives  515 us (60%)
  waiting for transfers between devices  189 us (22%)
  local copies, waits for them, and re-layouts  67.6 us (8%)
  matrix products  45.9 us (5%)
  between operations  19.2 us (2%)
  other arithmetic  11.4 us (1%)
    unnamed x6, waiting for transfers between devices  152 us
    psum x1, blocking collectives, per_device(): start_sq = lax.psum(jnp.sum(start_vec * start_vec), ('ka', 'band'))  114 us
    all_gather x2, blocking collectives, per_device(): gathered = lax.all_gather(vec_bf[None], ('ka', 'band'), axis=0, tiled=True)  83.1 us
    psum x2, blocking collectives, per_device(): square_sum = lax.psum(jnp.sum(resid_vec * resid_vec), ('ka', 'band'))  80.7 us
    psum x2, blocking collectives, per_device(): cross_sum = lax.psum(jnp.sum(current * resid_vec), ('ka', 'band'))  80.7 us
    all_gather x2, blocking collectives, per_device(): potential = lax.all_gather(pot_block, ('ka', 'band'), axis=0, tiled=True)  80.6 us
    psum x2, blocking collectives, per_device(): density = lax.psum(density_part, ('ka', 'band'))  75.3 us
    all_gather x1, waiting for transfers between devices, per_device(): val_wide = lax.all_gather(val_orb, 'band', axis=1, tiled=True)  37.1 us
  transfers between devices with their start and end apart: 5, of which 3 were waited for; matrix products, arithmetic and copies ran while one was open for 5% of the time, Pallas kernels for 0%

commit v1 on v0

v1 whole, which is shorter than its diff:
```python
import math

import jax
import jax.numpy as jnp
from jax import lax
from jax.sharding import PartitionSpec as P

STEPS = 2
AXES = ("ka", "band")


def gather_all(block, devices):
    wide = jnp.broadcast_to(block[None], (devices,) + block.shape)
    return lax.all_to_all(wide, AXES, split_axis=0, concat_axis=0, tiled=True)


def scatter_sum(parts):
    return jnp.sum(lax.all_to_all(parts, AXES, split_axis=0, concat_axis=0, tiled=True), axis=0)


def per_device(start_vec, val_energy, cond_energy, val_orb, cond_orb, coulomb, screened):
    n_ka = lax.axis_size("ka")
    n_band = lax.axis_size("band")
    devices = n_ka * n_band
    ka, band = lax.axis_index("ka"), lax.axis_index("band")
    me = ka * n_band + band
    k_dev, pair_blk = start_vec.shape
    nv_blk = val_orb.shape[1]
    n_cond = cond_orb.shape[1]
    n_val = nv_blk * n_band
    npt_all = cond_orb.shape[2]
    k_points = k_dev * n_ka
    mu_blk, nu_blk = screened.shape
    own_pts = coulomb.shape[0]
    count_all = k_points * n_val * n_cond
    kernel_scale = 1.0 / (npt_all * math.sqrt(count_all))
    bf, f32 = jnp.bfloat16, jnp.float32

    start_all = gather_all(start_vec, devices)
    val_cut = lax.all_to_all(
        val_orb.reshape(k_dev, nv_blk, n_ka, nu_blk).transpose(2, 0, 1, 3),
        "ka", split_axis=0, concat_axis=0, tiled=True,
    ).reshape(k_points, nv_blk, nu_blk)
    val_pts = lax.all_gather(val_cut, "band", axis=1, tiled=True)
    cond_local = lax.dynamic_slice_in_dim(cond_orb, band * mu_blk, mu_blk, 2)
    cond_pts = lax.all_gather(cond_local, "ka", axis=0, tiled=True)
    cond_rows = cond_orb.reshape(k_dev, n_cond, n_ka, n_band, own_pts)
    cond_rows = lax.dynamic_index_in_dim(cond_rows, band, 3, keepdims=False)
    cond_own = lax.all_to_all(
        cond_rows.transpose(2, 0, 1, 3), "ka", split_axis=0, concat_axis=0, tiled=True
    ).reshape(k_points, n_cond, own_pts)
    val_own = lax.dynamic_slice_in_dim(val_pts, band * own_pts, own_pts, 2)

    energy_gap = (cond_energy[:, None, :] - val_energy[:, :, None]).reshape(k_dev, pair_blk)
    start_sq = jnp.sum(start_all * start_all)
    current = start_all / jnp.sqrt(start_sq / count_all + 1e-06)
    previous = jnp.zeros_like(current)
    beta_val = jnp.float32(0.0)
    alphas = []
    betas = []
    for turn_index in range(STEPS):
        full_vec = (
            current.astype(bf)
            .reshape(n_ka, n_band, k_dev, nv_blk, n_cond)
            .transpose(0, 2, 1, 3, 4)
            .reshape(k_points, n_val, n_cond)
        )
        mixed_f = jnp.einsum("kvc,kvn->kcn", full_vec, val_pts, preferred_element_type=f32)
        mixed_own = lax.dynamic_slice_in_dim(mixed_f, band * own_pts, own_pts, 2)
        density_own = jnp.sum(mixed_own * cond_own.astype(f32), axis=(0, 1))
        density = gather_all(density_own.astype(bf), devices).reshape(npt_all)
        mixed_val = mixed_f.astype(bf)
        amp = jnp.einsum("kcm,kcn->mn", cond_pts, mixed_val, preferred_element_type=f32)
        kern = (screened.astype(f32) * amp * kernel_scale).astype(bf)
        folded = jnp.einsum("mn,kvn->kvm", kern, val_pts, preferred_element_type=f32).astype(bf)
        direct_part = jnp.einsum("kcm,kvm->kvc", cond_pts, folded, preferred_element_type=f32)
        potential = kernel_scale * jnp.dot(coulomb, density, preferred_element_type=f32)
        weighted = (val_own.astype(f32) * potential).astype(bf)
        exchange = jnp.einsum("kvp,kcp->kvc", weighted, cond_own, preferred_element_type=f32)
        part = 2.0 * exchange - direct_part
        arranged = (
            part.reshape(n_ka, k_dev, n_band, nv_blk, n_cond)
            .transpose(0, 2, 1, 3, 4)
            .reshape(devices, k_dev, pair_blk)
        )
        inter_own = scatter_sum(arranged)
        current_own = lax.dynamic_index_in_dim(current, me, 0, keepdims=False)
        resid_vec = gather_all(energy_gap * current_own + inter_own, devices)
        resid_vec = resid_vec - beta_val * previous
        alpha_val = jnp.sum(current * resid_vec) / count_all
        resid_vec = resid_vec - alpha_val * current
        beta_val = jnp.sqrt(jnp.sum(resid_vec * resid_vec) / count_all + 1e-06)
        previous = current
        current = resid_vec / beta_val
        alphas.append(alpha_val)
        betas.append(beta_val)
    coeffs = jnp.stack(alphas + betas)
    return (lax.dynamic_index_in_dim(current, me, 0, keepdims=False), coeffs)


def solution(mesh):
    in_specs = (
        P("ka", "band"),
        P("ka", "band"),
        P("ka", None),
        P("ka", "band", None),
        P("ka", None, None),
        P(("ka", "band"), None),
        P("band", "ka"),
    )
    out_specs = (P("ka", "band"), P())
    return jax.shard_map(
        per_device, mesh=mesh, in_specs=in_specs, out_specs=out_specs, check_vma=False
    )
```

time: 855 us -> 243 us (0.28)
  blocking collectives: 515 us -> 59.5 us
  waiting for transfers between devices: 189 us -> 51.6 us
  local copies, waits for them, and re-layouts: 67.6 us -> 25.7 us
  starting transfers between devices: 5 us -> 18.9 us
    psum x7 -> x0, blocking collectives: 351 us -> none  [the longest x1 114 us: per_device(): start_sq = lax.psum(jnp.sum(start_vec * start_vec), ('ka', 'band'))]
    all_gather x4 -> x0, blocking collectives: 164 us -> none  [the longest x2 83.1 us: per_device(): gathered = lax.all_gather(vec_bf[None], ('ka', 'band'), axis=0, tiled=True)]
    unnamed x6 -> x2, waiting for transfers between devices: 152 us -> 0.03 us
    all_to_all x0 -> x4, blocking collectives: none -> 59.5 us  [the longest x2 25.6 us: gather_all(): return lax.all_to_all(wide, AXES, split_axis=0, concat_axis=0, tiled=True)]
    all_gather x1, waiting for transfers between devices: 37.1 us -> 11.1 us  [per_device(): val_pts = lax.all_gather(val_cut, 'band', axis=1, tiled=True)]
    all_gather x1, waiting for transfers between devices: 0.01 us -> 25.5 us  [per_device(): cond_pts = lax.all_gather(cond_local, 'ka', axis=0, tiled=True)]
    all_to_all x1 -> x5, waiting for transfers between devices: 0.01 us -> 15 us  [the longest x1 9.09 us: scatter_sum(): lax.all_to_all(parts, AXES, split_axis=0, concat_axis=0, tiled=True)]
    all_to_all x1 -> x5, starting transfers between devices: 4.83 us -> 18.9 us  [the longest x3 11.9 us: gather_all(): return lax.all_to_all(wide, AXES, split_axis=0, concat_axis=0, tiled=True)]
  transfers between devices with their start and end apart: 5 -> 7, of which waited for: 3 -> 4; matrix products, arithmetic and copies ran while one was open for 5% -> 22% of each run, Pallas kernels for 0% -> 0%
where the time goes in v1:
time: 243 us; the launch traced here: 241 us
  blocking collectives  59.5 us (24%)
  waiting for transfers between devices  51.6 us (21%)
  matrix products  49 us (20%)
  local copies, waits for them, and re-layouts  25.7 us (11%)
  other arithmetic  19 us (8%)
  starting transfers between devices  18.9 us (8%)
  between operations  17.7 us (7%)
    all_to_all x2, blocking collectives, gather_all(): return lax.all_to_all(wide, AXES, split_axis=0, concat_axis=0, tiled=True)  25.6 us
    all_gather x1, waiting for transfers between devices, per_device(): cond_pts = lax.all_gather(cond_local, 'ka', axis=0, tiled=True)  25.5 us
    dot_general x2, matrix products, per_device(): jnp.einsum('kcm,kcn->mn', cond_pts, mixed_val, preferred_element_type=f32)  20.4 us
    all_to_all x1, blocking collectives, per_device(): lax.all_to_all(val_orb.reshape(k_dev, nv_blk, n_ka, nu_blk).transpose(2,...  17.9 us
    all_to_all x1, blocking collectives, scatter_sum(): lax.all_to_all(parts, AXES, split_axis=0, concat_axis=0, tiled=True)  16 us
    dot_general x2, matrix products, per_device(): jnp.einsum('kcm,kvm->kvc', cond_pts, folded, preferred_element_type=f32)  14.6 us
    all_to_all x3, starting transfers between devices, gather_all(): return lax.all_to_all(wide, AXES, split_axis=0, concat_axis=0, tiled=True)  11.9 us
    all_gather x1, waiting for transfers between devices, per_device(): val_pts = lax.all_gather(val_cut, 'band', axis=1, tiled=True)  11.1 us
  transfers between devices with their start and end apart: 7, of which 4 were waited for; matrix products, arithmetic and copies ran while one was open for 22% of the time, Pallas kernels for 0%

profile of v1, /device:TPU:0, one launch (start us, length us, event | category | flops | bytes accessed | tf_op | source)
XLA Modules:
  0.0 241.5 jit_solution(8285036433889748164)
XLA Ops:
  7.2 1.0 copy.44
  8.2 17.9 %all_to_all.47 = bf16[4,3,8,2048]{3,2,1,0:T(8,128)(2,1)} all-to-all(bf16[4,3,8,2048]{3,2,1,0:T(8,128)(2,1)S(1)} %bitcast.114), channel_id=1, replica_groups=mesh['ka'=4,'band'=8] {'ka'}, dimensions={0} | all-to-all | bytes 786432 | tf_op jit(solution)/shard_map/all_to_all | solution.py:40
  26.2 1.8 constant_dynamic-slice_fusion
  28.1 0.7 broadcast_in_dim.14
  28.8 3.7 %all-to-all-start = ((f32[32,3,512]{2,1,0:T(4,128)}), f32[32,3,512]{2,1,0:T(4,128)S(1)}, u32[]{:S(2)}, u32[]{:S(2)}) async-start(f32[32,3,512]{2,1,0:T(4,128)} %broadcast_in_dim.14), calls=%async_computation | async-start | bytes 524288 | tf_op jit(solution)/shard_map/all_to_all | solution.py:14
  32.5 3.0 %copy.36 = bf16[24,8,32,256]{3,2,1,0:T(8,128)(2,1)S(1)} copy(bf16[24,8,32,256]{3,1,2,0:T(8,128)(2,1)} %bitcast.110) | data formatting | bytes 6291456
  35.5 0.8 constant_dynamic-slice_fusion.1
  36.4 0.9 copy.43
  37.2 5.9 %all-to-all-done = f32[32,3,512]{2,1,0:T(4,128)S(1)} async-done(((f32[32,3,512]{2,1,0:T(4,128)}), f32[32,3,512]{2,1,0:T(4,128)S(1)}, u32[]{:S(2)}, u32[]{:S(2)}) %all-to-all-start) | async-done | bytes 196640 | tf_op jit(solution)/shard_map/all_to_all | solution.py:14
  43.1 3.5 %all-to-all-start.2 = ((bf16[4,3,64,256]{3,2,1,0:T(8,128)(2,1)}), bf16[4,3,64,256]{3,2,1,0:T(8,128)(2,1)S(1)}, u32[]{:S(2)}, u32[]{:S(2)}) async-start(bf16[4,3,64,256]{3,2,1,0:T(8,128)(2,1)} %bitcast.105), calls=%async_computation.2 | async-start | bytes 786432 | tf_op jit(solution)/shard_map/all_to_all | solution.py:49
  46.6 0.7 multiply_reduce_fusion.4
  48.0 0.8 fusion.46
  49.0 11.1 %all-gather.3.cloned.1.call-done = bf16[12,64,2048]{2,1,0:T(8,128)(2,1)} async-done(((bf16[12,8,2048]{2,1,0:T(8,128)(2,1)}), bf16[12,64,2048]{2,1,0:T(8,128)(2,1)}) %all-gather.3.cloned.1.call-update) | async-done | bytes 3145744 | tf_op jit(solution)/shard_map/all_gather | solution.py:44
  60.1 5.6 %fusion.47 = f32[12,64,2048]{2,1,0:T(8,128)} fusion(bf16[12,64,64]{2,1,0:T(8,128)(2,1)S(1)} %bitcast.119, bf16[12,64,2048]{2,1,0:T(8,128)(2,1)} %all-gather.3.cloned.1.call-done), kind=kOutput, calls=%fused_computation.64 | convolution fusion | flops 201326592 | bytes 9535488 | tf_op jit(solution)/shard_map/kvc,kvn->kcn/dot_general | solution.py:68
  65.7 1.3 fusion.32
  67.5 0.7 reduce
  68.9 4.8 %all-to-all-start.3 = ((bf16[32,2,128]{2,1,0:T(2,128)(2,1)}), bf16[32,2,128]{2,1,0:T(2,128)(2,1)S(1)}, u32[]{:S(2)}, u32[]{:S(2)}) async-start(bf16[32,2,128]{2,1,0:T(2,128)(2,1)} %reshape.120), calls=%async_computation.3 | async-start | bytes 32768 | tf_op jit(solution)/shard_map/all_to_all | solution.py:14
  73.7 25.5 %all-gather.5.cloned.1.call-done = bf16[12,64,1024]{2,1,0:T(8,128)(2,1)} async-done(((bf16[3,64,1024]{2,1,0:T(8,128)(2,1)}), bf16[12,64,1024]{2,1,0:T(8,128)(2,1)}) %all-gather.5.cloned.1.call-update) | async-done | bytes 1572880 | tf_op jit(solution)/shard_map/all_gather | solution.py:46
  99.2 10.2 %fusion.1 = bf16[1024,2048]{1,0:T(8,128)(2,1)} fusion(bf16[1024,2048]{1,0:T(8,128)(2,1)} %param.13, bf16[12,64,1024]{2,1,0:T(8,128)(2,1)} %all-gather.5.cloned.1.call-done, f32[12,64,2048]{2,1,0:T(8,128)} %fusion.47), kind=kOutput, calls=%fused_computation.3 | convolution fusion | flops 3231186944 | bytes 16252928 | tf_op jit(solution)/shard_map/kcm,kcn->mn/dot_general | solution.py:73
  109.4 7.3 %fusion.22 = f32[12,64,64]{2,1,0:T(8,128)} fusion(bf16[12,64,1024]{2,1,0:T(8,128)(2,1)} %all-gather.5.cloned.1.call-done, bf16[12,64,2048]{2,1,0:T(8,128)(2,1)S(1)} %copy-done, bf16[1024,2048]{1,0:T(8,128)(2,1)} %fusion.1), kind=kOutput, calls=%fused_computation.16 | convolution fusion | flops 3322675200 | bytes 9109504 | tf_op jit(solution)/shard_map/kcm,kvm->kvc/dot_general | solution.py:76
  117.3 3.4 %fusion.48 = f32[1,256]{1,0:T(1,128)S(1)} fusion(bf16[8192,1]{0,1:T(2,128)(2,1)} %bitcast.122, bf16[256,8192]{1,0:T(8,128)(2,1)} %param.12), kind=kOutput, calls=%fused_computation.65 | convolution fusion | flops 4194304 | bytes 4211712 | tf_op jit(solution)/shard_map/dot_general | solution.py:77
  121.1 0.8 copy.42
  121.8 1.8 reshape.104
  123.6 1.8 copy.28
  125.4 3.5 %all-to-all-start.4 = ((f32[32,3,512]{2,1,0:T(4,128)}), f32[32,3,512]{2,1,0:T(4,128)}, u32[]{:S(2)}, u32[]{:S(2)}) async-start(f32[32,3,512]{2,1,0:T(4,128)} %copy.28), calls=%async_computation.4 | async-start | bytes 524288 | tf_op jit(solution)/shard_map/all_to_all | solution.py:18
  129.6 0.8 sub.43
  130.4 9.1 %all-to-all-done.4 = f32[32,3,512]{2,1,0:T(4,128)} async-done(((f32[32,3,512]{2,1,0:T(4,128)}), f32[32,3,512]{2,1,0:T(4,128)}, u32[]{:S(2)}, u32[]{:S(2)}) %all-to-all-start.4) | async-done | bytes 196640 | tf_op jit(solution)/shard_map/all_to_all | solution.py:18
  139.5 1.0 reduce_sum.87
  141.2 12.8 %all_to_all.48 = f32[32,3,512]{2,1,0:T(4,128)S(1)} all-to-all(f32[32,3,512]{2,1,0:T(4,128)S(1)} %broadcast_in_dim.17), channel_id=1, replica_groups=mesh['ka'=4,'band'=8] {'ka','band'}, dimensions={0} | all-to-all | bytes 393216 | tf_op jit(solution)/shard_map/all_to_all | solution.py:14
  154.1 0.7 copy-done.2
  154.8 1.7 multiply_reduce_fusion.3
  157.1 1.8 multiply_reduce_fusion.2
  159.6 1.8 fusion.45
  162.1 1.7 reshape.105
  163.8 0.9 copy.30
  164.8 1.0 fusion.49
  165.8 2.7 %copy-done.1 = f32[12,64,2048]{2,1,0:T(8,128)} copy-done((f32[12,64,2048]{2,1,0:T(8,128)}, f32[12,64,2048]{2,1,0:T(8,128)S(1)}, u32[]{:S(2)}) %copy-start.1) | copy-done | bytes 6291480
  169.3 2.1 reduce.1
  171.3 1.3 reshape.122
  172.7 3.4 %all-to-all-start.6 = ((bf16[32,2,128]{2,1,0:T(2,128)(2,1)}), bf16[32,2,128]{2,1,0:T(2,128)(2,1)}, u32[]{:S(2)}, u32[]{:S(2)}) async-start(bf16[32,2,128]{2,1,0:T(2,128)(2,1)} %reshape.122), calls=%async_computation.6 | async-start | bytes 32768 | tf_op jit(solution)/shard_map/all_to_all | solution.py:14
  176.1 10.2 %fusion.3 = bf16[1024,2048]{1,0:T(8,128)(2,1)} fusion(bf16[1024,2048]{1,0:T(8,128)(2,1)} %param.13, bf16[12,64,1024]{2,1,0:T(8,128)(2,1)} %all-gather.5.cloned.1.call-done, f32[12,64,2048]{2,1,0:T(8,128)} %copy-done.1), kind=kOutput, calls=%fused_computation.5 | convolution fusion | flops 3231186944 | bytes 16252928 | tf_op jit(solution)/shard_map/kcm,kcn->mn/dot_general | solution.py:73
  186.3 7.3 %fusion.16 = f32[12,64,64]{2,1,0:T(8,128)} fusion(bf16[12,64,1024]{2,1,0:T(8,128)(2,1)} %all-gather.5.cloned.1.call-done, bf16[12,64,2048]{2,1,0:T(8,128)(2,1)S(1)} %copy-done, bf16[1024,2048]{1,0:T(8,128)(2,1)} %fusion.3), kind=kOutput, calls=%fused_computation.14 | convolution fusion | flops 3322675200 | bytes 9109504 | tf_op jit(solution)/shard_map/kcm,kvm->kvc/dot_general | solution.py:76
  193.6 1.3 reshape.123
  194.9 3.4 %fusion.50 = f32[1,256]{1,0:T(1,128)S(1)} fusion(bf16[8192,1]{0,1:T(2,128)(2,1)} %bitcast.123, bf16[256,8192]{1,0:T(8,128)(2,1)} %param.12), kind=kOutput, calls=%fused_computation.67 | convolution fusion | flops 4194304 | bytes 4211712 | tf_op jit(solution)/shard_map/dot_general | solution.py:77
  199.0 16.0 %all_to_all.49 = f32[32,3,512]{2,1,0:T(4,128)S(1)} all-to-all(f32[32,3,512]{2,1,0:T(4,128)S(1)} %copy.33), channel_id=1, replica_groups=mesh['ka'=4,'band'=8] {'ka','band'}, dimensions={0} | all-to-all | bytes 393216 | tf_op jit(solution)/shard_map/all_to_all | solution.py:18
  215.7 12.8 %all_to_all.50 = f32[32,3,512]{2,1,0:T(4,128)S(1)} all-to-all(f32[32,3,512]{2,1,0:T(4,128)S(1)} %broadcast_in_dim.20), channel_id=1, replica_groups=mesh['ka'=4,'band'=8] {'ka','band'}, dimensions={0} | all-to-all | bytes 393216 | tf_op jit(solution)/shard_map/all_to_all | solution.py:14
  228.5 1.8 multiply_reduce_fusion.1
  231.0 1.8 multiply_reduce_fusion
  (46 shorter events, 7.8 us)
Async XLA Ops:
  7.2 20.9 %copy-start.5 = (f32[3,512]{1,0:T(4,128)S(1)}, f32[3,512]{1,0:T(4,128)}, u32[]{:S(2)}) copy-start(f32[3,512]{1,0:T(4,128)} %param.7) | copy-start | bytes 18436
  7.2 53.0 %all-gather.3.cloned.1.call-start = ((), (), s32[]{:S(2)}) async-start(), calls=%async_computation.9 | async-start | bytes 3538944 | tf_op jit(solution)/shard_map/all_gather | solution.py:44
  26.2 73.0 %all-gather.5.cloned.1.call-start = ((), (), s32[]{:S(2)}) async-start(), calls=%async_computation.10 | async-start | bytes 1966080 | tf_op jit(solution)/shard_map/all_gather | solution.py:46
  28.8 14.3 %all-to-all-start = ((f32[32,3,512]{2,1,0:T(4,128)}), f32[32,3,512]{2,1,0:T(4,128)S(1)}, u32[]{:S(2)}, u32[]{:S(2)}) async-start(f32[32,3,512]{2,1,0:T(4,128)} %broadcast_in_dim.14), calls=%async_computation | async-start | bytes 524288 | tf_op jit(solution)/shard_map/all_to_all | solution.py:14
  43.1 22.6 %all-to-all-start.2 = ((bf16[4,3,64,256]{3,2,1,0:T(8,128)(2,1)}), bf16[4,3,64,256]{3,2,1,0:T(8,128)(2,1)S(1)}, u32[]{:S(2)}, u32[]{:S(2)}) async-start(bf16[4,3,64,256]{3,2,1,0:T(8,128)(2,1)} %bitcast.105), calls=%async_computation.2 | async-start | bytes 786432 | tf_op jit(solution)/shard_map/all_to_all | solution.py:49
  68.9 47.8 %all-to-all-start.3 = ((bf16[32,2,128]{2,1,0:T(2,128)(2,1)}), bf16[32,2,128]{2,1,0:T(2,128)(2,1)S(1)}, u32[]{:S(2)}, u32[]{:S(2)}) async-start(bf16[32,2,128]{2,1,0:T(2,128)(2,1)} %reshape.120), calls=%async_computation.3 | async-start | bytes 32768 | tf_op jit(solution)/shard_map/all_to_all | solution.py:14
  73.7 35.7 %copy-start = (bf16[12,64,2048]{2,1,0:T(8,128)(2,1)S(1)}, bf16[12,64,2048]{2,1,0:T(8,128)(2,1)}, u32[]{:S(2)}) copy-start(bf16[12,64,2048]{2,1,0:T(8,128)(2,1)} %all-gather.3.cloned.1.call-done) | copy-start | bytes 9437188
  117.3 3.5 %copy-start.4 = (f32[12,64,64]{2,1,0:T(8,128)S(1)}, f32[12,64,64]{2,1,0:T(8,128)}, u32[]{:S(2)}) copy-start(f32[12,64,64]{2,1,0:T(8,128)} %fusion.22) | copy-start | bytes 589828
  117.3 11.6 %copy-start.6 = (f32[3,8]{1,0:T(4,128)S(1)}, f32[3,8]{1,0:T(4,128)}, u32[]{:S(2)}) copy-start(f32[3,8]{1,0:T(4,128)} %param.8) | copy-start | bytes 292
  117.3 11.6 %copy-start.7 = (f32[3,64]{1,0:T(4,128)S(1)}, f32[3,64]{1,0:T(4,128)}, u32[]{:S(2)}) copy-start(f32[3,64]{1,0:T(4,128)} %param.9) | copy-start | bytes 2308
  125.4 14.1 %all-to-all-start.4 = ((f32[32,3,512]{2,1,0:T(4,128)}), f32[32,3,512]{2,1,0:T(4,128)}, u32[]{:S(2)}, u32[]{:S(2)}) async-start(f32[32,3,512]{2,1,0:T(4,128)} %copy.28), calls=%async_computation.4 | async-start | bytes 524288 | tf_op jit(solution)/shard_map/all_to_all | solution.py:18
  154.1 0.7 copy-start.2
  165.8 2.7 %copy-start.1 = (f32[12,64,2048]{2,1,0:T(8,128)}, f32[12,64,2048]{2,1,0:T(8,128)S(1)}, u32[]{:S(2)}) copy-start(f32[12,64,2048]{2,1,0:T(8,128)S(1)} %fusion.49) | copy-start | bytes 18874372
  172.7 20.9 %all-to-all-start.6 = ((bf16[32,2,128]{2,1,0:T(2,128)(2,1)}), bf16[32,2,128]{2,1,0:T(2,128)(2,1)}, u32[]{:S(2)}, u32[]{:S(2)}) async-start(bf16[32,2,128]{2,1,0:T(2,128)(2,1)} %reshape.122), calls=%async_computation.6 | async-start | bytes 32768 | tf_op jit(solution)/shard_map/all_to_all | solution.py:14
  194.9 3.5 %copy-start.3 = (f32[12,64,64]{2,1,0:T(8,128)S(1)}, f32[12,64,64]{2,1,0:T(8,128)}, u32[]{:S(2)}) copy-start(f32[12,64,64]{2,1,0:T(8,128)} %fusion.16) | copy-start | bytes 589828
Sparse Core Ops, SparseCore 0:
  26.3 33.8 all-gather.2
  61.7 37.4 all-gather.4

commit v2 on v1

--- a/solution.py
+++ b/solution.py
@@ -1,24 +1,391 @@
+import functools
 import math
 
 import jax
 import jax.numpy as jnp
 from jax import lax
+from jax.experimental import pallas as pl
+from jax.experimental.pallas import tpu as pltpu
 from jax.sharding import PartitionSpec as P
 
 STEPS = 2
 AXES = ("ka", "band")
+BF, F32 = jnp.bfloat16, jnp.float32
+LANES = 128
+HALF = 64
+ROWS = 8
+MIB = 1 << 20
+
+VMEM = pl.BlockSpec(memory_space=pltpu.VMEM)
+SMEM = pl.BlockSpec(memory_space=pltpu.SMEM)
+ANY = pl.BlockSpec(memory_space=pl.ANY)
 
 
 def gather_all(block, devices):
     wide = jnp.broadcast_to(block[None], (devices,) + block.shape)
-    return lax.all_to_all(wide, AXES, split_axis=0, concat_axis=0, tiled=True)
-
-
-def scatter_sum(parts):
-    return jnp.sum(lax.all_to_all(parts, AXES, split_axis=0, concat_axis=0, tiled=True), axis=0)
-
-
-def per_device(start_vec, val_energy, cond_energy, val_orb, cond_orb, coulomb, screened):
+    return exchange_all(wide)
+
+
+def exchange_all(parts):
+    return lax.all_to_all(parts, AXES, split_axis=0, concat_axis=0, tiled=True)
+
+
+def dot_nt(lhs, rhs):
+    return lax.dot_general(lhs, rhs, (((1,), (1,)), ((), ())), preferred_element_type=F32)
+
+
+def dot_tn(lhs, rhs):
+    return lax.dot_general(lhs, rhs, (((0,), (0,)), ((), ())), preferred_element_type=F32)
+
+
+def pack_vector(block, k_dev):
+    groups = (k_dev + 1) // 2
+    block = jnp.pad(block, ((0, 2 * groups - k_dev), (0, 0)))
+    block = block.reshape(groups, 2, ROWS, HALF).transpose(0, 2, 1, 3)
+    return block.reshape(groups * ROWS, LANES)
+
+
+def lane_half(tile, have, want):
+    if have != want:
+        tile = pltpu.roll(tile, HALF, axis=1)
+    lane = lax.broadcasted_iota(jnp.int32, tile.shape, 1)
+    keep = lane < HALF if want == 0 else lane >= HALF
+    return jnp.where(keep, tile, 0.0)
+
+
+def piece_copies(val_refs, column, width, dest, sems):
+    copies = []
+    for d, refs in enumerate(val_refs):
+        row = 0
+        for ref in refs:
+            copies.append(
+                pltpu.make_async_copy(
+                    ref.at[:, pl.ds(column, width)],
+                    dest.at[d, pl.ds(row, ref.shape[0]), :],
+                    sems.at[len(copies)],
+                )
+            )
+            row += ref.shape[0]
+    return copies
+
+
+def split_refs(refs, counts):
+    out, at = [], 0
+    for count in counts:
+        out.append(refs[at : at + count])
+        at += count
+    return out
+
+
+def density_kernel(first, cfg, *refs):
+    n_band, k_dev, k_points, own, count_all, counts = cfg
+    n_val = sum(counts)
+    lead, refs = refs[: 1 if first else 2], refs[1 if first else 2 :]
+    cond_ref, refs = refs[0], refs[1:]
+    val_refs, refs = split_refs(refs[:n_val], counts), refs[n_val:]
+    q_ref, qx_ref, rho_ref, coef_ref, xs, vown, sems = refs
+    band = lax.axis_index("band")
+    copies = piece_copies(val_refs, pl.multiple_of(band * own, LANES), own, vown, sems)
+    for copy in copies:
+        copy.start()
+    if first:
+        vec = lead[0][...]
+        norm = jnp.sum(vec * vec) / count_all
+        q_ref[...] = vec / jnp.sqrt(norm + 1e-06)
+        coef_ref[0] = 0.0
+        coef_ref[1] = 0.0
+    else:
+        vec, prev = lead[0][...], lead[1][...]
+        alpha = jnp.sum(vec * prev) / count_all
+        vec = vec - alpha * prev
+        beta = jnp.sqrt(jnp.sum(vec * vec) / count_all + 1e-06)
+        q_ref[...] = vec / beta
+        coef_ref[0] = alpha
+        coef_ref[1] = beta
+    for d in range(n_band):
+        for k in range(k_points):
+            z, kl = divmod(k, k_dev)
+            tile = q_ref[z * n_band + jnp.bitwise_xor(band, d), pl.ds(kl // 2 * ROWS, ROWS), :]
+            xs[k // 2, pl.ds(d * 2 * ROWS + k % 2 * ROWS, ROWS), :] = lane_half(tile, kl % 2, k % 2)
+    qx_ref[...] = xs[...].astype(BF)
+    for copy in copies:
+        copy.wait()
+    rho = jnp.zeros((1, own), F32)
+    for kp in range(k_points // 2):
+        rows = vown[:, kp * 2 * ROWS : (kp + 1) * 2 * ROWS, :].reshape(n_band * 2 * ROWS, own)
+        mixed = dot_tn(qx_ref[kp], rows)
+        cond = cond_ref[kp * LANES : (kp + 1) * LANES, :].astype(F32)
+        rho = rho + jnp.sum(mixed * cond, axis=0, keepdims=True)
+    for r in range(own // LANES):
+        part = rho[:, r * LANES : (r + 1) * LANES]
+        rho_ref[:, r, :] = jnp.broadcast_to(part, (rho_ref.shape[0], LANES))
+
+
+def direct_kernel(cfg, tile_m, tile_n, scale, *refs):
+    n_band, k_points, counts = cfg
+    n_val = sum(counts)
+    qx_ref, cond_ref, scr_ref = refs[:3]
+    val_refs, refs = split_refs(refs[3 : 3 + n_val], counts), refs[3 + n_val :]
+    di_ref, vals, conds, scrs, mixed, kern, folded, val_sems, cond_sem, scr_sems = refs
+    mu, nu = scr_ref.shape
+    val_copies = piece_copies(val_refs, 0, nu, vals, val_sems)
+    cond_copy = pltpu.make_async_copy(cond_ref, conds, cond_sem.at[0])
+    scr_copies = [
+        pltpu.make_async_copy(
+            scr_ref.at[pl.ds(i * tile_m, tile_m), :], scrs.at[pl.ds(i * tile_m, tile_m), :], scr_sems.at[i]
+        )
+        for i in range(mu // tile_m)
+    ]
+    for copy in val_copies + [cond_copy] + scr_copies:
+        copy.start()
+    for copy in val_copies:
+        copy.wait()
+    pairs = k_points // 2
+    for kp in range(pairs):
+        rows = vals[:, kp * 2 * ROWS : (kp + 1) * 2 * ROWS, :].reshape(n_band * 2 * ROWS, nu)
+        mixed[kp * LANES : (kp + 1) * LANES, :] = dot_tn(qx_ref[kp], rows).astype(BF)
+    cond_copy.wait()
+    all_vals = vals[...].reshape(-1, nu)
+    for i in range(mu // tile_m):
+        at_m = slice(i * tile_m, (i + 1) * tile_m)
+        cond_t = conds[:, at_m].T
+        scr_copies[i].wait()
+        for j in range(nu // tile_n):
+            at_n = slice(j * tile_n, (j + 1) * tile_n)
+            amp = jnp.dot(cond_t, mixed[:, at_n], preferred_element_type=F32)
+            kern[:, at_n] = (scrs[at_m, at_n].astype(F32) * amp * scale).astype(BF)
+        folded[:, at_m] = dot_nt(all_vals, kern[...]).astype(BF)
+    per_piece = pairs * 2 * ROWS
+    for kp in range(pairs):
+        rows = [folded[d * per_piece + kp * 2 * ROWS : d * per_piece + (kp + 1) * 2 * ROWS, :] for d in range(n_band)]
+        di_ref[kp] = dot_nt(jnp.concatenate(rows, axis=0), conds[kp * LANES : (kp + 1) * LANES, :])
+
+
+def exchange_kernel(cfg, chunk, scale, *refs):
+    n_band, k_dev, k_points, own, counts = cfg
+    n_val = sum(counts)
+    rho_ref, di_ref, cond_ref, coul_ref = refs[:4]
+    val_refs, refs = split_refs(refs[4 : 4 + n_val], counts), refs[4 + n_val :]
+    msg_ref, coul, vown, part, msg, val_sems, coul_sems = refs
+    band = lax.axis_index("band")
+    npt = coul_ref.shape[1]
+    coul_copies = [
+        pltpu.make_async_copy(
+            coul_ref.at[:, pl.ds(i * chunk, chunk)], coul.at[:, pl.ds(i * chunk, chunk)], coul_sems.at[i]
+        )
+        for i in range(npt // chunk)
+    ]
+    val_copies = piece_copies(val_refs, pl.multiple_of(band * own, LANES), own, vown, val_sems)
+    for copy in coul_copies + val_copies:
+        copy.start()
+    acc = jnp.zeros((own, LANES), F32)
+    per_dev = own // LANES
+    for i in range(npt // chunk):
+        coul_copies[i].wait()
+        for j in range(i * chunk // LANES, (i + 1) * chunk // LANES):
+            rho = rho_ref[j // per_dev, pl.ds(j % per_dev, 1), :].astype(BF).astype(F32)
+            acc = acc + coul[:, j * LANES : (j + 1) * LANES].astype(F32) * rho
+    potential = scale * jnp.sum(acc.T, axis=0, keepdims=True)
+    for copy in val_copies:
+        copy.wait()
+    for kp in range(k_points // 2):
+        rows = vown[:, kp * 2 * ROWS : (kp + 1) * 2 * ROWS, :].reshape(n_band * 2 * ROWS, own)
+        weighted = (rows.astype(F32) * potential).astype(BF)
+        ex = dot_nt(weighted, cond_ref[kp * LANES : (kp + 1) * LANES, :])
+        part[kp] = 2.0 * ex - di_ref[kp]
+    for d in range(n_band):
+        for z in range(k_points // k_dev):
+            for g in range((k_dev + 1) // 2):
+                tile = None
+                for kl in range(2 * g, min(2 * g + 2, k_dev)):
+                    k = z * k_dev + kl
+                    piece = part[k // 2, pl.ds(d * 2 * ROWS + k % 2 * ROWS, ROWS), :]
+                    piece = lane_half(piece, k % 2, kl % 2)
+                    tile = piece if tile is None else tile + piece
+                msg[z * n_band + jnp.bitwise_xor(band, d), pl.ds(g * ROWS, ROWS), :] = tile
+    msg_ref[...] = msg[...].astype(BF)
+
+
+def owner_kernel(first, n_band, *refs):
+    if first:
+        recv_ref, gap_ref, q_ref, out_ref = refs
+    else:
+        recv_ref, gap_ref, q_ref, prev_ref, coef_ref, out_ref = refs
+    me = lax.axis_index("ka") * n_band + lax.axis_index("band")
+    total = jnp.sum(recv_ref[...].astype(F32), axis=0)
+    total = total + gap_ref[...] * q_ref[me]
+    if not first:
+        total = total - coef_ref[1] * prev_ref[me]
+    out_ref[...] = jnp.broadcast_to(total[None], out_ref.shape)
+
+
+def finish_kernel(n_band, count_all, w_ref, q_ref, coef_ref, out_ref, coeffs_ref):
+    me = lax.axis_index("ka") * n_band + lax.axis_index("band")
+    vec, cur = w_ref[...], q_ref[...]
+    alpha = jnp.sum(vec * cur) / count_all
+    vec = vec - alpha * cur
+    beta = jnp.sqrt(jnp.sum(vec * vec) / count_all + 1e-06)
+    own = (w_ref[me] - alpha * q_ref[me]) / beta
+    coeffs_ref[0] = coef_ref[0]
+    coeffs_ref[1] = alpha
+    coeffs_ref[2] = coef_ref[1]
+    coeffs_ref[3] = beta
+    for kl in range(out_ref.shape[0]):
+        tile = own[kl // 2 * ROWS : (kl // 2 + 1) * ROWS, :]
+        other = pltpu.roll(tile, HALF, axis=1)
+        left, right = (tile, other) if kl % 2 == 0 else (other, tile)
+        low = lax.broadcasted_iota(jnp.int32, (1, LANES), 1) < HALF
+        for j in range(ROWS // 2):
+            row = jnp.where(low, left[2 * j : 2 * j + 1], right[2 * j + 1 : 2 * j + 2])
+            out_ref[pl.ds(kl, 1), pl.ds(j * LANES, LANES)] = row
+
+
+def params(mib):
+    return pltpu.CompilerParams(vmem_limit_bytes=mib * MIB)
+
+
+def shape_of(dims, kind=F32):
+    return jax.ShapeDtypeStruct(dims, kind)
+
+
+def plane_pieces(own_piece, n_band):
+    def move(block, d):
+        return lax.ppermute(block, "band", [(i, i ^ d) for i in range(n_band)])
+
+    half = own_piece.shape[0] // 2
+    by_x, by_y = move(own_piece, 2), move(own_piece, 4)
+    diag = [move(by_x[:half], 4), move(by_y[half:], 2)]
+    pieces = [[own_piece], [move(own_piece, 1)], [by_x], [move(by_x, 1)], [by_y], [move(by_y, 1)]]
+    return pieces + [diag, [move(part, 1) for part in diag]]
+
+
+def kernel_path(start_vec, val_energy, cond_energy, val_orb, cond_orb, coulomb, screened):
+    n_ka = lax.axis_size("ka")
+    n_band = lax.axis_size("band")
+    devices = n_ka * n_band
+    band = lax.axis_index("band")
+    k_dev = start_vec.shape[0]
+    nv_blk = val_orb.shape[1]
+    n_cond = cond_orb.shape[1]
+    npt_all = cond_orb.shape[2]
+    k_points = k_dev * n_ka
+    pairs = k_points // 2
+    mu_blk, nu_blk = screened.shape
+    own = coulomb.shape[0]
+    count_all = k_points * nv_blk * n_band * n_cond
+    scale = 1.0 / (npt_all * math.sqrt(count_all))
+    piece_rows = k_points * nv_blk
+
+    cond_local = lax.dynamic_slice_in_dim(cond_orb, band * mu_blk, mu_blk, 2)
+    cond_pts = lax.all_gather(
+        cond_local.reshape(k_dev * n_cond, mu_blk), "ka", axis=0, tiled=True
+    )
+    val_cut = lax.all_to_all(
+        val_orb.reshape(k_dev, nv_blk, n_ka, nu_blk).transpose(2, 0, 1, 3),
+        "ka", split_axis=0, concat_axis=0, tiled=True,
+    ).reshape(piece_rows, nu_blk)
+    pieces = plane_pieces(val_cut, n_band)
+    counts = tuple(len(piece) for piece in pieces)
+    flat = [ref for piece in pieces for ref in piece]
+    start_all = gather_all(pack_vector(start_vec, k_dev), devices)
+    cond_cut = jnp.stack(
+        [lax.dynamic_slice_in_dim(cond_orb, z * nu_blk + band * own, own, 2) for z in range(n_ka)]
+    ).reshape(n_ka, k_dev * n_cond, own)
+    cond_own = lax.all_to_all(
+        cond_cut, "ka", split_axis=0, concat_axis=0, tiled=True
+    ).reshape(k_points * n_cond, own)
+    gap = (cond_energy[:, None, :] - val_energy[:, :, None]).reshape(k_dev, nv_blk * n_cond)
+    gap = pack_vector(gap, k_dev)
+
+    block = start_all.shape[1:]
+    vec_shape = shape_of((devices,) + block)
+    n_copies = len(flat)
+    own_scratch = pltpu.VMEM((n_band, piece_rows, own), BF)
+    vec, prev, coef = start_all, None, None
+    for step in range(STEPS):
+        first = step == 0
+        lead = [vec] if first else [vec, prev]
+        cur, qx, rho, coef = pl.pallas_call(
+            functools.partial(density_kernel, first, (n_band, k_dev, k_points, own, count_all, counts)),
+            out_shape=(
+                vec_shape,
+                shape_of((pairs, LANES, LANES), BF),
+                shape_of((devices, own // LANES, LANES)),
+                shape_of((2,)),
+            ),
+            in_specs=[VMEM] * len(lead) + [VMEM] + [ANY] * n_copies,
+            out_specs=(VMEM, VMEM, VMEM, SMEM),
+            scratch_shapes=[
+                pltpu.VMEM((pairs, LANES, LANES), F32),
+                own_scratch,
+                pltpu.SemaphoreType.DMA((n_copies,)),
+            ],
+            compiler_params=params(16),
+            name="density",
+        )(*lead, cond_own, *flat)
+        density = exchange_all(rho)
+        tile_m, tile_n = 256, 512
+        direct = pl.pallas_call(
+            functools.partial(direct_kernel, (n_band, k_points, counts), tile_m, tile_n, scale),
+            out_shape=shape_of((pairs, LANES, LANES)),
+            in_specs=[VMEM] + [ANY] * (2 + n_copies),
+            out_specs=VMEM,
+            scratch_shapes=[
+                pltpu.VMEM((n_band, piece_rows, nu_blk), BF),
+                pltpu.VMEM((k_points * n_cond, mu_blk), BF),
+                pltpu.VMEM((mu_blk, nu_blk), BF),
+                pltpu.VMEM((k_points * n_cond, nu_blk), BF),
+                pltpu.VMEM((tile_m, nu_blk), BF),
+                pltpu.VMEM((n_band * piece_rows, mu_blk), BF),
+                pltpu.SemaphoreType.DMA((n_copies,)),
+                pltpu.SemaphoreType.DMA((1,)),
+                pltpu.SemaphoreType.DMA((mu_blk // tile_m,)),
+            ],
+            compiler_params=params(40),
+            cost_estimate=pl.CostEstimate(
+                flops=4 * mu_blk * nu_blk * k_points * n_cond, bytes_accessed=9 * MIB, transcendentals=0
+            ),
+            name="direct",
+        )(qx, cond_pts, screened, *flat)
+        chunk = 1024
+        message = pl.pallas_call(
+            functools.partial(exchange_kernel, (n_band, k_dev, k_points, own, counts), chunk, scale),
+            out_shape=shape_of((devices,) + block, BF),
+            in_specs=[VMEM] * 3 + [ANY] * (1 + n_copies),
+            out_specs=VMEM,
+            scratch_shapes=[
+                pltpu.VMEM((own, npt_all), BF),
+                own_scratch,
+                pltpu.VMEM((pairs, LANES, LANES), F32),
+                pltpu.VMEM((devices,) + block, F32),
+                pltpu.SemaphoreType.DMA((n_copies,)),
+                pltpu.SemaphoreType.DMA((npt_all // chunk,)),
+            ],
+            compiler_params=params(24),
+            name="exchange",
+        )(density, direct, cond_own, coulomb, *flat)
+        recv = exchange_all(message)
+        extra = [] if first else [prev, coef]
+        wide = pl.pallas_call(
+            functools.partial(owner_kernel, first, n_band),
+            out_shape=vec_shape,
+            in_specs=[VMEM] * 3 + ([] if first else [VMEM, SMEM]),
+            out_specs=VMEM,
+            compiler_params=params(8),
+            name="owner",
+        )(recv, gap, cur, *extra)
+        vec, prev = exchange_all(wide), cur
+    return pl.pallas_call(
+        functools.partial(finish_kernel, n_band, count_all),
+        out_shape=(shape_of(start_vec.shape), shape_of((2 * STEPS,))),
+        in_specs=[VMEM, VMEM, SMEM],
+        out_specs=(VMEM, SMEM),
+        compiler_params=params(8),
+        name="finish",
+    )(vec, prev, coef)
+
+
+def array_path(start_vec, val_energy, cond_energy, val_orb, cond_orb, coulomb, screened):
     n_ka = lax.axis_size("ka")
     n_band = lax.axis_size("band")
     devices = n_ka * n_band
@@ -34,7 +401,6 @@
     own_pts = coulomb.shape[0]
     count_all = k_points * n_val * n_cond
     kernel_scale = 1.0 / (npt_all * math.sqrt(count_all))
-    bf, f32 = jnp.bfloat16, jnp.float32
 
     start_all = gather_all(start_vec, devices)
     val_cut = lax.all_to_all(
@@ -60,30 +426,30 @@
     betas = []
     for turn_index in range(STEPS):
         full_vec = (
-            current.astype(bf)
+            current.astype(BF)
             .reshape(n_ka, n_band, k_dev, nv_blk, n_cond)
             .transpose(0, 2, 1, 3, 4)
             .reshape(k_points, n_val, n_cond)
         )
-        mixed_f = jnp.einsum("kvc,kvn->kcn", full_vec, val_pts, preferred_element_type=f32)
+        mixed_f = jnp.einsum("kvc,kvn->kcn", full_vec, val_pts, preferred_element_type=F32)
         mixed_own = lax.dynamic_slice_in_dim(mixed_f, band * own_pts, own_pts, 2)
-        density_own = jnp.sum(mixed_own * cond_own.astype(f32), axis=(0, 1))
-        density = gather_all(density_own.astype(bf), devices).reshape(npt_all)
-        mixed_val = mixed_f.astype(bf)
-        amp = jnp.einsum("kcm,kcn->mn", cond_pts, mixed_val, preferred_element_type=f32)
-        kern = (screened.astype(f32) * amp * kernel_scale).astype(bf)
-        folded = jnp.einsum("mn,kvn->kvm", kern, val_pts, preferred_element_type=f32).astype(bf)
-        direct_part = jnp.einsum("kcm,kvm->kvc", cond_pts, folded, preferred_element_type=f32)
-        potential = kernel_scale * jnp.dot(coulomb, density, preferred_element_type=f32)
-        weighted = (val_own.astype(f32) * potential).astype(bf)
-        exchange = jnp.einsum("kvp,kcp->kvc", weighted, cond_own, preferred_element_type=f32)
+        density_own = jnp.sum(mixed_own * cond_own.astype(F32), axis=(0, 1))
+        density = gather_all(density_own.astype(BF), devices).reshape(npt_all)
+        mixed_val = mixed_f.astype(BF)
+        amp = jnp.einsum("kcm,kcn->mn", cond_pts, mixed_val, preferred_element_type=F32)
+        kern = (screened.astype(F32) * amp * kernel_scale).astype(BF)
+        folded = jnp.einsum("mn,kvn->kvm", kern, val_pts, preferred_element_type=F32).astype(BF)
+        direct_part = jnp.einsum("kcm,kvm->kvc", cond_pts, folded, preferred_element_type=F32)
+        potential = kernel_scale * jnp.dot(coulomb, density, preferred_element_type=F32)
+        weighted = (val_own.astype(F32) * potential).astype(BF)
+        exchange = jnp.einsum("kvp,kcp->kvc", weighted, cond_own, preferred_element_type=F32)
         part = 2.0 * exchange - direct_part
         arranged = (
             part.reshape(n_ka, k_dev, n_band, nv_blk, n_cond)
             .transpose(0, 2, 1, 3, 4)
             .reshape(devices, k_dev, pair_blk)
         )
-        inter_own = scatter_sum(arranged)
+        inter_own = jnp.sum(exchange_all(arranged), axis=0)
         current_own = lax.dynamic_index_in_dim(current, me, 0, keepdims=False)
         resid_vec = gather_all(energy_gap * current_own + inter_own, devices)
         resid_vec = resid_vec - beta_val * previous
@@ -96,6 +462,23 @@
         betas.append(beta_val)
     coeffs = jnp.stack(alphas + betas)
     return (lax.dynamic_index_in_dim(current, me, 0, keepdims=False), coeffs)
+
+
+def per_device(*args):
+    start_vec, _, _, val_orb, cond_orb, coulomb, screened = args
+    n_ka, n_band = lax.axis_size("ka"), lax.axis_size("band")
+    fits = (
+        n_band == 8
+        and val_orb.shape[1] == ROWS
+        and cond_orb.shape[1] == HALF
+        and start_vec.shape[0] * n_ka % 2 == 0
+        and coulomb.shape[0] % LANES == 0
+        and coulomb.shape[1] % 1024 == 0
+        and screened.shape[0] % 256 == 0
+        and screened.shape[1] % 512 == 0
+        and screened.shape[0] * screened.shape[1] <= 2 * MIB
+    )
+    return (kernel_path if fits else array_path)(*args)
 
 
 def solution(mesh):

time: 243 us -> 206 us (0.85)
  matrix products: 49 us -> 0 us
  Pallas kernels: 0 us -> 38.6 us
  blocking collectives: 59.5 us -> 38.8 us
  other arithmetic: 19 us -> 1.58 us
  starting transfers between devices: 18.9 us -> 34.6 us
  waiting for transfers between devices: 51.6 us -> 41.6 us
  local copies, waits for them, and re-layouts: 25.7 us -> 35.5 us
  between operations: 17.7 us -> 14.3 us
    dot_general x10 -> x0, matrix products: 49 us -> none  [the longest x2 20.4 us: per_device(): jnp.einsum('kcm,kcn->mn', cond_pts, mixed_val, preferred_element_type=f32)]
    pallas_call x0 -> x9, Pallas kernels: none -> 38.6 us  [the longest x2 26.7 us: kernel_path(): pl.pallas_call(functools.partial(direct_kernel, (n_band, k_points, counts...]
    all_gather x2 -> x1, waiting for transfers between devices: 36.6 us -> 0.02 us  [kernel_path(): lax.all_gather(cond_local.reshape(k_dev * n_cond, mu_blk), 'ka', axis=0,...]
    all_to_all x5 -> x6, waiting for transfers between devices: 15 us -> 36.5 us  [the longest x1 19.6 us: kernel_path(): lax.all_to_all(val_orb.reshape(k_dev, nv_blk, n_ka, nu_blk).transpose(2,...]
    all_to_all x4 -> x3, blocking collectives: 59.5 us -> 38.8 us  [exchange_all(): return lax.all_to_all(parts, AXES, split_axis=0, concat_axis=0, tiled=True)]
    unnamed x21 -> x52, local copies, waits for them, and re-layouts: 10.3 us -> 25.1 us
    reduce_sum x9 -> x0, other arithmetic: 10.3 us -> none  [the longest x2 3.55 us: per_device(): beta_val = jnp.sqrt(jnp.sum(resid_vec * resid_vec) / count_all + 1e-06)]
    all_to_all x5 -> x6, starting transfers between devices: 18.9 us -> 27.7 us  [the longest x4 17.9 us: exchange_all(): return lax.all_to_all(parts, AXES, split_axis=0, concat_axis=0, tiled=True)]
  transfers between devices with their start and end apart: 7 -> 16, of which waited for: 4 -> 6; matrix products, arithmetic and copies ran while one was open for 22% -> 5% of each run, Pallas kernels for 0% -> 14%
where the time goes in v2:
time: 206 us; the launch traced here: 205 us
  waiting for transfers between devices  41.6 us (20%)
  blocking collectives  38.8 us (19%)
  Pallas kernels  38.6 us (19%)
  local copies, waits for them, and re-layouts  35.5 us (17%)
  starting transfers between devices  34.6 us (17%)
  between operations  14.3 us (7%)
    all_to_all x3, blocking collectives, exchange_all(): return lax.all_to_all(parts, AXES, split_axis=0, concat_axis=0, tiled=True)  38.8 us
    pallas_call x2, Pallas kernels, kernel_path(): pl.pallas_call(functools.partial(direct_kernel, (n_band, k_points, counts...  26.7 us
    unnamed x52, local copies, waits for them, and re-layouts  25.1 us
    all_to_all x1, waiting for transfers between devices, kernel_path(): lax.all_to_all(val_orb.reshape(k_dev, nv_blk, n_ka, nu_blk).transpose(2,...  19.6 us
    all_to_all x4, starting transfers between devices, exchange_all(): return lax.all_to_all(parts, AXES, split_axis=0, concat_axis=0, tiled=True)  17.9 us
    all_to_all x4, waiting for transfers between devices, exchange_all(): return lax.all_to_all(parts, AXES, split_axis=0, concat_axis=0, tiled=True)  13.5 us
    ppermute x9, starting transfers between devices, move(): return lax.ppermute(block, 'band', [(i, i ^ d) for i in range(n_band)])  6.83 us
    pallas_call x2, Pallas kernels, kernel_path(): pl.pallas_call(functools.partial(exchange_kernel, (n_band, k_dev, k_point...  6.41 us
  transfers between devices with their start and end apart: 16, of which 6 were waited for; matrix products, arithmetic and copies ran while one was open for 5% of the time, Pallas kernels for 14%

profile of v2, /device:TPU:0, one launch (start us, length us, event | category | flops | bytes accessed | tf_op | source)
XLA Modules:
  0.0 205.0 jit_solution(12725290233712989977)
XLA Ops:
  7.2 1.8 constant_dynamic-slice_fusion
  9.0 1.8 copy.15
  10.8 6.3 %all-to-all-start.2 = ((bf16[4,3,8,2048]{3,2,1,0:T(8,128)(2,1)}), bf16[4,3,8,2048]{3,2,1,0:T(8,128)(2,1)S(1)}, u32[]{:S(2)}, u32[]{:S(2)}) async-start(bf16[4,3,8,2048]{3,2,1,0:T(8,128)(2,1)} %bitcast.12), calls=%async_computation.2 | async-start | bytes 786432 | tf_op jit(solution)/shard_map/all_to_all | solution.py:283
  18.0 19.6 %all-to-all-done.2 = bf16[4,3,8,2048]{3,2,1,0:T(8,128)(2,1)S(1)} async-done(((bf16[4,3,8,2048]{3,2,1,0:T(8,128)(2,1)}), bf16[4,3,8,2048]{3,2,1,0:T(8,128)(2,1)S(1)}, u32[]{:S(2)}, u32[]{:S(2)}) %all-to-all-start.2) | async-done | bytes 393248 | tf_op jit(solution)/shard_map/all_to_all | solution.py:283
  38.3 4.8 %all-to-all-start = ((f32[32,16,128]{2,1,0:T(8,128)}), f32[32,16,128]{2,1,0:T(8,128)S(1)}, u32[]{:S(2)}, u32[]{:S(2)}) async-start(f32[32,16,128]{2,1,0:T(8,128)} %broadcast_in_dim.10), calls=%async_computation | async-start | bytes 524288 | tf_op jit(solution)/shard_map/all_to_all | solution.py:30
  43.1 1.8 collective-permute-start.3
  44.9 1.5 collective-permute-start.1
  46.4 1.1 constant_dynamic-slice_fusion.4
  47.5 0.8 pad_maximum_fusion
  48.3 10.3 %all-to-all-done.refs_0_ = f32[32,16,128]{2,1,0:T(8,128)S(1)} async-done(((f32[32,16,128]{2,1,0:T(8,128)}), f32[32,16,128]{2,1,0:T(8,128)S(1)}, u32[]{:S(2)}, u32[]{:S(2)}) %all-to-all-start) | async-done | bytes 262176 | tf_op jit(solution)/shard_map/all_to_all | solution.py:30
  59.2 3.5 %all-to-all-start.1 = ((bf16[4,192,256]{2,1,0:T(8,128)(2,1)}), bf16[4,192,256]{2,1,0:T(8,128)(2,1)S(1)}, u32[]{:S(2)}, u32[]{:S(2)}) async-start(bf16[4,192,256]{2,1,0:T(8,128)(2,1)} %pad_maximum_fusion), calls=%async_computation.1 | async-start | bytes 786432 | tf_op jit(solution)/shard_map/all_to_all | solution.py:294
  62.8 1.5 collective-permute-start.6
  64.4 1.4 collective-permute-start.5
  66.3 3.9 %collective-permute-done.6.refs_9_.refs_10_.refs_11_ = bf16[48,2048]{1,0:T(8,128)(2,1)S(1)} collective-permute-done((bf16[48,2048]{1,0:T(8,128)(2,1)S(1)}, bf16[48,2048]{1,0:T(8,128)(2,1)S(1)}, u32[]{:S(2)}, u32[]{:S(2)}) %collective-permute-start.6) | collective-permute-done | bytes 196640 | tf_op jit(solution)/shard_map/ppermute | solution.py:253
  70.2 1.1 collective-permute-done.5.refs_8_.refs_9_.refs_10_
  71.3 3.4 %all-to-all-done.1 = bf16[4,192,256]{2,1,0:T(8,128)(2,1)S(1)} async-done(((bf16[4,192,256]{2,1,0:T(8,128)(2,1)}), bf16[4,192,256]{2,1,0:T(8,128)(2,1)S(1)}, u32[]{:S(2)}, u32[]{:S(2)}) %all-to-all-start.1) | async-done | bytes 393248 | tf_op jit(solution)/shard_map/all_to_all | solution.py:294
  74.7 0.9 copy-done.9
  75.7 1.0 density.2
  78.7 3.9 %all-to-all-start.3 = ((f32[32,2,128]{2,1,0:T(2,128)}), f32[32,2,128]{2,1,0:T(2,128)}, u32[]{:S(2)}, u32[]{:S(2)}) async-start(f32[32,2,128]{2,1,0:T(2,128)} %copy-done.15), calls=%async_computation.3 | async-start | bytes 65536 | tf_op jit(solution)/shard_map/all_to_all | solution.py:30
  82.7 2.2 %copy-done.17 = bf16[1024,2048]{1,0:T(8,128)(2,1)S(1)} copy-done((bf16[1024,2048]{1,0:T(8,128)(2,1)S(1)}, bf16[1024,2048]{1,0:T(8,128)(2,1)}, u32[]{:S(2)}) %copy-start.17) | copy-done | bytes 4194328
  84.9 1.4 copy-done.19
  86.3 0.9 copy-done.22
  87.2 13.3 %direct.2.refs_1_ = f32[6,128,128]{2,1,0:T(8,128)S(1)} custom-call(bf16[6,128,128]{2,1,0:T(8,128)(2,1)S(1)} %copy-done.22, bf16[768,1024]{1,0:T(8,128)(2,1)S(1)} %copy-done.19, bf16[1024,2048]{1,0:T(8,128)(2,1)S(1)} %copy-done.17, bf16[96,2048]{1,0:T(8,128)(2,1)S(1)} %bitcast.17, bf16[96,2048]{1,0:T(8,128)(2,1)S(1)} %collective-permute-done.refs_3_.refs_4_.refs_5_, ...), custom_call_target="tpu_custom_call" | custom-call | flops 6442450944 | bytes 9437184 | tf_op jit(solution)/shard_map/direct/pallas_call | solution.py:328
  101.3 2.2 %copy-done = bf16[256,8192]{1,0:T(8,128)(2,1)S(1)} copy-done((bf16[256,8192]{1,0:T(8,128)(2,1)S(1)}, bf16[256,8192]{1,0:T(8,128)(2,1)}, u32[]{:S(2)}) %copy-start) | copy-done | bytes 4194328
  103.5 1.0 copy-done.14
  104.5 3.2 %exchange.2 = bf16[32,16,128]{2,1,0:T(8,128)(2,1)S(1)} custom-call(f32[32,2,128]{2,1,0:T(2,128)} %all-to-all-done.3.refs_0_, f32[6,128,128]{2,1,0:T(8,128)S(1)} %copy-done.14, bf16[768,256]{1,0:T(8,128)(2,1)S(1)} %bitcast.23, bf16[256,8192]{1,0:T(8,128)(2,1)S(1)} %copy-done, bf16[96,2048]{1,0:T(8,128)(2,1)S(1)} %bitcast.18, ...), custom_call_target="tpu_custom_call" | custom-call | tf_op jit(solution)/shard_map/exchange/pallas_call | solution.py:351
  108.4 5.7 %all-to-all-start.4 = ((bf16[32,16,128]{2,1,0:T(8,128)(2,1)}), bf16[32,16,128]{2,1,0:T(8,128)(2,1)}, u32[]{:S(2)}, u32[]{:S(2)}) async-start(bf16[32,16,128]{2,1,0:T(8,128)(2,1)} %copy-done.10), calls=%async_computation.4 | async-start | bytes 262144 | tf_op jit(solution)/shard_map/all_to_all | solution.py:30
  114.1 0.8 broadcast_subtract_fusion
  115.5 1.3 pad.8
  116.8 0.8 reshape.46
  118.2 0.8 reshape.47.refs_1_
  119.0 3.3 %all-to-all-done.4.refs_0_ = bf16[32,16,128]{2,1,0:T(8,128)(2,1)} async-done(((bf16[32,16,128]{2,1,0:T(8,128)(2,1)}), bf16[32,16,128]{2,1,0:T(8,128)(2,1)}, u32[]{:S(2)}, u32[]{:S(2)}) %all-to-all-start.4) | async-done | bytes 131104 | tf_op jit(solution)/shard_map/all_to_all | solution.py:30
  122.3 0.9 copy-done.3
  123.3 1.0 owner.2
  124.2 12.9 %all_to_all.45.refs_0_ = f32[32,16,128]{2,1,0:T(8,128)S(1)} all-to-all(f32[32,16,128]{2,1,0:T(8,128)S(1)} %owner.2), channel_id=1, replica_groups=mesh['ka'=4,'band'=8] {'ka','band'}, dimensions={0} | all-to-all | bytes 524288 | tf_op jit(solution)/shard_map/all_to_all | solution.py:30
  137.1 0.9 copy-done.4
  138.0 1.3 density.3
  141.4 3.5 %all-to-all-start.6 = ((f32[32,2,128]{2,1,0:T(2,128)}), f32[32,2,128]{2,1,0:T(2,128)}, u32[]{:S(2)}, u32[]{:S(2)}) async-start(f32[32,2,128]{2,1,0:T(2,128)} %copy-done.16), calls=%async_computation.6 | async-start | bytes 65536 | tf_op jit(solution)/shard_map/all_to_all | solution.py:30
  144.9 2.2 %copy-done.18 = bf16[1024,2048]{1,0:T(8,128)(2,1)S(1)} copy-done((bf16[1024,2048]{1,0:T(8,128)(2,1)S(1)}, bf16[1024,2048]{1,0:T(8,128)(2,1)}, u32[]{:S(2)}) %copy-start.18) | copy-done | bytes 4194328
  147.1 1.4 copy-done.20
  148.5 0.9 copy-done.24
  149.4 13.3 %direct.3.refs_1_ = f32[6,128,128]{2,1,0:T(8,128)S(1)} custom-call(bf16[6,128,128]{2,1,0:T(8,128)(2,1)S(1)} %copy-done.24, bf16[768,1024]{1,0:T(8,128)(2,1)S(1)} %copy-done.20, bf16[1024,2048]{1,0:T(8,128)(2,1)S(1)} %copy-done.18, bf16[96,2048]{1,0:T(8,128)(2,1)S(1)} %bitcast.20, bf16[96,2048]{1,0:T(8,128)(2,1)S(1)} %collective-permute-done.refs_3_.refs_4_.refs_5_, ...), custom_call_target="tpu_custom_call" | custom-call | flops 6442450944 | bytes 9437184 | tf_op jit(solution)/shard_map/direct/pallas_call | solution.py:328
  163.5 2.2 %copy-done.1 = bf16[256,8192]{1,0:T(8,128)(2,1)S(1)} copy-done((bf16[256,8192]{1,0:T(8,128)(2,1)S(1)}, bf16[256,8192]{1,0:T(8,128)(2,1)}, u32[]{:S(2)}) %copy-start.1) | copy-done | bytes 4194328
  165.7 1.0 copy-done.12
  166.7 3.2 %exchange.3 = bf16[32,16,128]{2,1,0:T(8,128)(2,1)S(1)} custom-call(f32[32,2,128]{2,1,0:T(2,128)} %all-to-all-done.6.refs_0_, f32[6,128,128]{2,1,0:T(8,128)S(1)} %copy-done.12, bf16[768,256]{1,0:T(8,128)(2,1)S(1)} %bitcast.25, bf16[256,8192]{1,0:T(8,128)(2,1)S(1)} %copy-done.1, bf16[96,2048]{1,0:T(8,128)(2,1)S(1)} %bitcast.21, ...), custom_call_target="tpu_custom_call" | custom-call | tf_op jit(solution)/shard_map/exchange/pallas_call | solution.py:351
  169.9 13.6 %all_to_all.46.refs_0_ = bf16[32,16,128]{2,1,0:T(8,128)(2,1)S(1)} all-to-all(bf16[32,16,128]{2,1,0:T(8,128)(2,1)S(1)} %exchange.3), channel_id=1, replica_groups=mesh['ka'=4,'band'=8] {'ka','band'}, dimensions={0} | all-to-all | bytes 262144 | tf_op jit(solution)/shard_map/all_to_all | solution.py:30
  184.1 12.4 %all_to_all.47.w_ref = f32[32,16,128]{2,1,0:T(8,128)S(1)} all-to-all(f32[32,16,128]{2,1,0:T(8,128)S(1)} %owner.3), channel_id=1, replica_groups=mesh['ka'=4,'band'=8] {'ka','band'}, dimensions={0} | all-to-all | bytes 524288 | tf_op jit(solution)/shard_map/all_to_all | solution.py:30
  196.5 1.6 finish.1
  (66 shorter events, 11.0 us)
Async XLA Ops:
  7.2 75.5 %all-gather.2.cloned.1.call-start = ((), (), s32[]{:S(2)}) async-start(), calls=%async_computation.9 | async-start | bytes 1966080 | tf_op jit(solution)/shard_map/all_gather | solution.py:280
  10.8 26.8 %all-to-all-start.2 = ((bf16[4,3,8,2048]{3,2,1,0:T(8,128)(2,1)}), bf16[4,3,8,2048]{3,2,1,0:T(8,128)(2,1)S(1)}, u32[]{:S(2)}, u32[]{:S(2)}) async-start(bf16[4,3,8,2048]{3,2,1,0:T(8,128)(2,1)} %bitcast.12), calls=%async_computation.2 | async-start | bytes 786432 | tf_op jit(solution)/shard_map/all_to_all | solution.py:283
  38.3 20.2 %all-to-all-start = ((f32[32,16,128]{2,1,0:T(8,128)}), f32[32,16,128]{2,1,0:T(8,128)S(1)}, u32[]{:S(2)}, u32[]{:S(2)}) async-start(f32[32,16,128]{2,1,0:T(8,128)} %broadcast_in_dim.10), calls=%async_computation | async-start | bytes 524288 | tf_op jit(solution)/shard_map/all_to_all | solution.py:30
  43.1 19.7 %collective-permute-start.3 = (bf16[96,2048]{1,0:T(8,128)(2,1)S(1)}, bf16[96,2048]{1,0:T(8,128)(2,1)S(1)}, u32[]{:S(2)}, u32[]{:S(2)}) collective-permute-start(bf16[96,2048]{1,0:T(8,128)(2,1)S(1)} %bitcast.13), channel_id=1, source_target_pairs={{0,4},{1,5},{2,6},{3,7},{4,0},{5,1},{6,2},{7,3},{8,12},{9,13},{10,... | collective-permute-start | bytes 1179656 | tf_op jit(solution)/shard_map/ppermute | solution.py:253
  44.9 19.4 %collective-permute-start.1 = (bf16[96,2048]{1,0:T(8,128)(2,1)S(1)}, bf16[96,2048]{1,0:T(8,128)(2,1)S(1)}, u32[]{:S(2)}, u32[]{:S(2)}) collective-permute-start(bf16[96,2048]{1,0:T(8,128)(2,1)S(1)} %bitcast.14), channel_id=1, source_target_pairs={{0,2},{1,3},{2,0},{3,1},{4,6},{5,7},{6,4},{7,5},{8,10},{9,11},{10,... | collective-permute-start | bytes 1179656 | tf_op jit(solution)/shard_map/ppermute | solution.py:253
  58.5 0.7 copy-start.8
  59.2 15.4 %all-to-all-start.1 = ((bf16[4,192,256]{2,1,0:T(8,128)(2,1)}), bf16[4,192,256]{2,1,0:T(8,128)(2,1)S(1)}, u32[]{:S(2)}, u32[]{:S(2)}) async-start(bf16[4,192,256]{2,1,0:T(8,128)(2,1)} %pad_maximum_fusion), calls=%async_computation.1 | async-start | bytes 786432 | tf_op jit(solution)/shard_map/all_to_all | solution.py:294
  62.7 12.0 %collective-permute-start = (bf16[96,2048]{1,0:T(8,128)(2,1)S(1)}, bf16[96,2048]{1,0:T(8,128)(2,1)S(1)}, u32[]{:S(2)}, u32[]{:S(2)}) collective-permute-start(bf16[96,2048]{1,0:T(8,128)(2,1)S(1)} %bitcast.15), channel_id=1, source_target_pairs={{0,1},{1,0},{2,3},{3,2},{4,5},{5,4},{6,7},{7,6},{8,9},{9,8},{10,11... | collective-permute-start | bytes 1179656 | tf_op jit(solution)/shard_map/ppermute | solution.py:253
  62.8 7.4 %collective-permute-start.6 = (bf16[48,2048]{1,0:T(8,128)(2,1)S(1)}, bf16[48,2048]{1,0:T(8,128)(2,1)S(1)}, u32[]{:S(2)}, u32[]{:S(2)}) collective-permute-start(bf16[48,2048]{1,0:T(8,128)(2,1)S(1)} %slice.9), channel_id=1, source_target_pairs={{0,2},{1,3},{2,0},{3,1},{4,6},{5,7},{6,4},{7,5},{8,10},{9,11},{10,... | collective-permute-start | bytes 589832 | tf_op jit(solution)/shard_map/ppermute | solution.py:253
  64.4 6.9 %collective-permute-start.5 = (bf16[48,2048]{1,0:T(8,128)(2,1)S(1)}, bf16[48,2048]{1,0:T(8,128)(2,1)S(1)}, u32[]{:S(2)}, u32[]{:S(2)}) collective-permute-start(bf16[48,2048]{1,0:T(8,128)(2,1)S(1)} %slice.8), channel_id=1, source_target_pairs={{0,4},{1,5},{2,6},{3,7},{4,0},{5,1},{6,2},{7,3},{8,12},{9,13},{10,... | collective-permute-start | bytes 589832 | tf_op jit(solution)/shard_map/ppermute | solution.py:253
  65.8 8.9 %collective-permute-start.4 = (bf16[96,2048]{1,0:T(8,128)(2,1)S(1)}, bf16[96,2048]{1,0:T(8,128)(2,1)S(1)}, u32[]{:S(2)}, u32[]{:S(2)}) collective-permute-start(bf16[96,2048]{1,0:T(8,128)(2,1)S(1)} %collective-permute-done.3.refs_6_.refs_7_.refs_8_), channel_id=1, source_target_pairs={{0,1},{1,0},{2,3},{3,2},{4,5},{5,4},{6,7},{7,6},{8,9},{9,8},{10,11... | collective-permute-start | bytes 1179656 | tf_op jit(solution)/shard_map/ppermute | solution.py:253
  65.8 8.9 %collective-permute-start.2 = (bf16[96,2048]{1,0:T(8,128)(2,1)S(1)}, bf16[96,2048]{1,0:T(8,128)(2,1)S(1)}, u32[]{:S(2)}, u32[]{:S(2)}) collective-permute-start(bf16[96,2048]{1,0:T(8,128)(2,1)S(1)} %collective-permute-done.1.refs_4_.refs_5_.refs_6_), channel_id=1, source_target_pairs={{0,1},{1,0},{2,3},{3,2},{4,5},{5,4},{6,7},{7,6},{8,9},{9,8},{10,11... | collective-permute-start | bytes 1179656 | tf_op jit(solution)/shard_map/ppermute | solution.py:253
  70.2 4.5 %collective-permute-start.8 = (bf16[48,2048]{1,0:T(8,128)(2,1)S(1)}, bf16[48,2048]{1,0:T(8,128)(2,1)S(1)}, u32[]{:S(2)}, u32[]{:S(2)}) collective-permute-start(bf16[48,2048]{1,0:T(8,128)(2,1)S(1)} %collective-permute-done.6.refs_9_.refs_10_.refs_11_), channel_id=1, source_target_pairs={{0,1},{1,0},{2,3},{3,2},{4,5},{5,4},{6,7},{7,6},{8,9},{9,8},{10,11... | collective-permute-start | bytes 589832 | tf_op jit(solution)/shard_map/ppermute | solution.py:253
  71.3 3.4 %collective-permute-start.7 = (bf16[48,2048]{1,0:T(8,128)(2,1)S(1)}, bf16[48,2048]{1,0:T(8,128)(2,1)S(1)}, u32[]{:S(2)}, u32[]{:S(2)}) collective-permute-start(bf16[48,2048]{1,0:T(8,128)(2,1)S(1)} %collective-permute-done.5.refs_8_.refs_9_.refs_10_), channel_id=1, source_target_pairs={{0,1},{1,0},{2,3},{3,2},{4,5},{5,4},{6,7},{7,6},{8,9},{9,8},{10,11... | collective-permute-start | bytes 589832 | tf_op jit(solution)/shard_map/ppermute | solution.py:253
  74.7 1.0 copy-start.9
  76.7 0.7 copy-start.2
  77.4 0.6 copy-start.15
  78.1 0.7 copy-start.21
  78.7 22.6 %all-to-all-start.3 = ((f32[32,2,128]{2,1,0:T(2,128)}), f32[32,2,128]{2,1,0:T(2,128)}, u32[]{:S(2)}, u32[]{:S(2)}) async-start(f32[32,2,128]{2,1,0:T(2,128)} %copy-done.15), calls=%async_computation.3 | async-start | bytes 65536 | tf_op jit(solution)/shard_map/all_to_all | solution.py:30
  82.7 2.2 %copy-start.17 = (bf16[1024,2048]{1,0:T(8,128)(2,1)S(1)}, bf16[1024,2048]{1,0:T(8,128)(2,1)}, u32[]{:S(2)}) copy-start(bf16[1024,2048]{1,0:T(8,128)(2,1)} %refs_2_.3) | copy-start | bytes 12582916
  84.9 1.4 copy-start.19
  86.3 0.9 copy-start.22
  100.6 0.8 copy-start.13
  101.3 2.2 %copy-start = (bf16[256,8192]{1,0:T(8,128)(2,1)S(1)}, bf16[256,8192]{1,0:T(8,128)(2,1)}, u32[]{:S(2)}) copy-start(bf16[256,8192]{1,0:T(8,128)(2,1)} %refs_3_.3) | copy-start | bytes 12582916
  103.5 1.0 copy-start.14
  104.5 9.6 %copy-start.25 = (f32[3,8]{1,0:T(4,128)S(1)}, f32[3,8]{1,0:T(4,128)}, u32[]{:S(2)}) copy-start(f32[3,8]{1,0:T(4,128)} %param.8) | copy-start | bytes 292
  107.7 0.6 copy-start.10
  108.4 13.9 %all-to-all-start.4 = ((bf16[32,16,128]{2,1,0:T(8,128)(2,1)}), bf16[32,16,128]{2,1,0:T(8,128)(2,1)}, u32[]{:S(2)}, u32[]{:S(2)}) async-start(bf16[32,16,128]{2,1,0:T(8,128)(2,1)} %copy-done.10), calls=%async_computation.4 | async-start | bytes 262144 | tf_op jit(solution)/shard_map/all_to_all | solution.py:30
  122.3 1.0 copy-start.3
  137.1 1.0 copy-start.4
  139.4 0.7 copy-start.6
  140.1 0.6 copy-start.16
  140.7 0.7 copy-start.23
  141.4 22.1 %all-to-all-start.6 = ((f32[32,2,128]{2,1,0:T(2,128)}), f32[32,2,128]{2,1,0:T(2,128)}, u32[]{:S(2)}, u32[]{:S(2)}) async-start(f32[32,2,128]{2,1,0:T(2,128)} %copy-done.16), calls=%async_computation.6 | async-start | bytes 65536 | tf_op jit(solution)/shard_map/all_to_all | solution.py:30
  144.9 2.2 %copy-start.18 = (bf16[1024,2048]{1,0:T(8,128)(2,1)S(1)}, bf16[1024,2048]{1,0:T(8,128)(2,1)}, u32[]{:S(2)}) copy-start(bf16[1024,2048]{1,0:T(8,128)(2,1)} %refs_2_.3) | copy-start | bytes 12582916
  147.1 1.4 copy-start.20
  148.5 0.9 copy-start.24
  162.7 0.8 copy-start.11
  163.5 2.2 %copy-start.1 = (bf16[256,8192]{1,0:T(8,128)(2,1)S(1)}, bf16[256,8192]{1,0:T(8,128)(2,1)}, u32[]{:S(2)}) copy-start(bf16[256,8192]{1,0:T(8,128)(2,1)} %refs_3_.3) | copy-start | bytes 12582916
  165.7 1.0 copy-start.12
  166.7 16.8 %copy-start.5 = (f32[32,16,128]{2,1,0:T(8,128)S(1)}, f32[32,16,128]{2,1,0:T(8,128)}, u32[]{:S(2)}) copy-start(f32[32,16,128]{2,1,0:T(8,128)} %copy-done.2) | copy-start | bytes 786436
  166.7 16.8 %copy-start.7 = (f32[32,16,128]{2,1,0:T(8,128)S(1)}, f32[32,16,128]{2,1,0:T(8,128)}, u32[]{:S(2)}) copy-start(f32[32,16,128]{2,1,0:T(8,128)} %copy-done.6) | copy-start | bytes 786436
Sparse Core Ops, SparseCore 0:
  9.6 50.6 all-gather.1

commit v3 on v2

v3 whole, which is shorter than its diff:
```python
import functools
import math

import jax
import jax.numpy as jnp
from jax import lax
from jax.experimental import pallas as pl
from jax.experimental.pallas import tpu as pltpu
from jax.sharding import PartitionSpec as P

STEPS = 2
AXES = ("ka", "band")
BF, F32 = jnp.bfloat16, jnp.float32
LANES = 128
HALF = 64
ROWS = 8
MIB = 1 << 20

VMEM = pl.BlockSpec(memory_space=pltpu.VMEM)
SMEM = pl.BlockSpec(memory_space=pltpu.SMEM)
ANY = pl.BlockSpec(memory_space=pl.ANY)


def gather_all(block, devices):
    wide = jnp.broadcast_to(block[None], (devices,) + block.shape)
    return exchange_all(wide)


def exchange_all(parts):
    return lax.all_to_all(parts, AXES, split_axis=0, concat_axis=0, tiled=True)


def dot_nt(lhs, rhs):
    return lax.dot_general(lhs, rhs, (((1,), (1,)), ((), ())), preferred_element_type=F32)


def dot_tn(lhs, rhs):
    return lax.dot_general(lhs, rhs, (((0,), (0,)), ((), ())), preferred_element_type=F32)


def pack_vector(block, k_dev):
    groups = (k_dev + 1) // 2
    block = jnp.pad(block, ((0, 2 * groups - k_dev), (0, 0)))
    block = block.reshape(groups, 2, ROWS, HALF).transpose(0, 2, 1, 3)
    return block.reshape(groups * ROWS, LANES)


def lane_half(tile, have, want):
    if have != want:
        tile = pltpu.roll(tile, HALF, axis=1)
    lane = lax.broadcasted_iota(jnp.int32, tile.shape, 1)
    keep = lane < HALF if want == 0 else lane >= HALF
    return jnp.where(keep, tile, 0.0)


def with_sums(block, sums):
    row = lax.broadcasted_iota(jnp.int32, block.shape, 0)
    lane = lax.broadcasted_iota(jnp.int32, block.shape, 1)
    free = row == block.shape[0] - ROWS
    for i, total in enumerate(sums):
        rest = jnp.full(block.shape, total, F32)
        for part in range(3):
            piece = rest.astype(BF).astype(F32)
            block = jnp.where(free & (lane == HALF + 3 * i + part), piece, block)
            rest = rest - piece
    return block


def read_sums(msgs_ref, count):
    rows = msgs_ref.shape[1]
    tile = jnp.sum(msgs_ref[...].astype(F32), axis=0)[rows - ROWS :, :]
    row = lax.broadcasted_iota(jnp.int32, tile.shape, 0)
    lane = lax.broadcasted_iota(jnp.int32, tile.shape, 1)
    out = []
    for i in range(count):
        mine = (row == 0) & (lane >= HALF + 3 * i) & (lane < HALF + 3 * i + 3)
        out.append(jnp.sum(jnp.where(mine, tile, 0.0)))
    return out


def block_copies(groups, width, dest, sems, column=0):
    copies = []
    for d, refs in enumerate(groups):
        row = 0
        for ref in refs:
            copies.append(
                pltpu.make_async_copy(
                    ref.at[:, pl.ds(column, width)],
                    dest.at[d, pl.ds(row, ref.shape[0]), :],
                    sems.at[len(copies)],
                )
            )
            row += ref.shape[0]
    return copies


def split_refs(refs, counts):
    out, at = [], 0
    for count in counts:
        out.append(refs[at : at + count])
        at += count
    return out


def start_all(copies):
    for copy in copies:
        copy.start()


def wait_all(copies):
    for copy in copies:
        copy.wait()


def device_at(n_band, j, d):
    ka = jnp.bitwise_xor(lax.axis_index("ka"), j)
    return ka * n_band + jnp.bitwise_xor(lax.axis_index("band"), d)


def pair_rows(ref, kp):
    part = ref[:, kp * 2 * ROWS : (kp + 1) * 2 * ROWS, :]
    return part.reshape(part.shape[0] * 2 * ROWS, part.shape[2])


def pack_kernel(start_ref, gap_ref, own_ref, msg_ref):
    own_ref[...] = jnp.zeros_like(own_ref)
    for kl in range(start_ref.shape[0]):
        for j in range(ROWS // 2):
            row = start_ref[pl.ds(kl, 1), pl.ds(j * LANES, LANES)]
            for v in range(2):
                at = pl.ds(kl // 2 * ROWS + 2 * j + v, 1)
                own_ref[at, :] = own_ref[at, :] + lane_half(row, v, kl % 2)
    own = own_ref[...]
    square = own * own
    block = with_sums(own, [jnp.sum(square), jnp.sum(gap_ref[...] * square)])
    msg_ref[...] = jnp.broadcast_to(block.astype(BF)[None], msg_ref.shape)


def density_kernel(cfg, *refs):
    n_ka, n_band, k_dev, own, counts = cfg
    n_val = sum(counts)
    k_points = n_ka * k_dev
    msgs_ref, cond_refs, refs = refs[0], refs[1 : 1 + n_ka], refs[1 + n_ka :]
    val_refs, refs = split_refs(refs[:n_val], counts), refs[n_val:]
    qx_ref, rho_ref, xs, conds, vown, cond_sems, val_sems = refs
    column = pl.multiple_of(lax.axis_index("band") * own, LANES)
    copies = block_copies([[ref] for ref in cond_refs], own, conds, cond_sems)
    copies += block_copies(val_refs, own, vown, val_sems, column)
    start_all(copies)
    for d in range(n_band):
        for k in range(k_points):
            j, kl = divmod(k, k_dev)
            tile = msgs_ref[device_at(n_band, j, d), :, :].astype(F32)
            tile = tile[kl // 2 * ROWS : (kl // 2 + 1) * ROWS, :]
            xs[k // 2, pl.ds(d * 2 * ROWS + k % 2 * ROWS, ROWS), :] = lane_half(tile, kl % 2, k % 2)
    qx_ref[...] = xs[...].astype(BF)
    wait_all(copies)
    cond_rows = conds[...].reshape(-1, own)
    rho = jnp.zeros((1, own), F32)
    for kp in range(k_points // 2):
        mixed = dot_tn(qx_ref[kp], pair_rows(vown, kp))
        cond = cond_rows[kp * LANES : (kp + 1) * LANES, :].astype(F32)
        rho = rho + jnp.sum(mixed * cond, axis=0, keepdims=True)
    for r in range(own // LANES):
        part = rho[:, r * LANES : (r + 1) * LANES]
        rho_ref[:, r, :] = jnp.broadcast_to(part, (rho_ref.shape[0], LANES))


def direct_kernel(first, cfg, tile, scale, *refs):
    n_ka, n_band, k_points, counts = cfg
    n_val = sum(counts)
    qx_ref, cond_ref, scr_ref = refs[:3]
    val_refs, refs = split_refs(refs[3 : 3 + n_val], counts), refs[3 + n_val :]
    if first:
        di_ref, cond_out, conds, refs = refs[0], refs[1], refs[2], refs[3:]
    else:
        di_ref, refs = refs[0], refs[1:]
    cond_t, vals, scrs, mixed, kern, folded, cond_sems, val_sems, scr_sems = refs
    mu, nu = scr_ref.shape
    pairs = k_points // 2
    val_copies = block_copies(val_refs, nu, vals, val_sems)
    if first:
        rows = cond_ref.shape[0] // n_ka
        cond_copies = [
            pltpu.make_async_copy(
                cond_ref.at[pl.ds(jnp.bitwise_xor(lax.axis_index("ka"), j) * rows, rows), :],
                conds.at[pl.ds(j * rows, rows), :],
                cond_sems.at[j],
            )
            for j in range(n_ka)
        ]
    else:
        cond_copies = [pltpu.make_async_copy(cond_ref, cond_t, cond_sems.at[0])]
    scr_copies = [
        pltpu.make_async_copy(
            scr_ref.at[:, pl.ds(j * tile, tile)], scrs.at[:, pl.ds(j * tile, tile)], scr_sems.at[j]
        )
        for j in range(nu // tile)
    ]
    start_all(val_copies + cond_copies + scr_copies)
    wait_all(val_copies)
    for kp in range(pairs):
        mixed[kp * LANES : (kp + 1) * LANES, :] = dot_tn(qx_ref[kp], pair_rows(vals, kp)).astype(BF)
    wait_all(cond_copies)
    if first:
        cond_t[...] = conds[...].T
        out_copy = pltpu.make_async_copy(cond_t, cond_out, cond_sems.at[0])
        out_copy.start()
    for j in range(nu // tile):
        at = slice(j * tile, (j + 1) * tile)
        scr_copies[j].wait()
        amp = jnp.dot(cond_t[...], mixed[:, at], preferred_element_type=F32)
        kern[:, at] = (scrs[:, at].astype(F32) * amp * scale).astype(BF)
    all_vals = vals[...].reshape(-1, nu)
    for i in range(mu // tile):
        at = slice(i * tile, (i + 1) * tile)
        folded[:, at] = dot_nt(all_vals, kern[at, :]).astype(BF)
    per_piece = pairs * 2 * ROWS
    for kp in range(pairs):
        rows = [
            folded[d * per_piece + kp * 2 * ROWS : d * per_piece + (kp + 1) * 2 * ROWS, :]
            for d in range(n_band)
        ]
        di_ref[kp] = jnp.dot(
            jnp.concatenate(rows, axis=0),
            cond_t[:, kp * LANES : (kp + 1) * LANES],
            preferred_element_type=F32,
        )
    if first:
        out_copy.wait()


def exchange_kernel(cfg, chunk, scale, *refs):
    n_ka, n_band, k_dev, own, counts = cfg
    n_val = sum(counts)
    k_points = n_ka * k_dev
    rho_ref, di_ref, coul_ref = refs[:3]
    cond_refs, refs = refs[3 : 3 + n_ka], refs[3 + n_ka :]
    val_refs, refs = split_refs(refs[:n_val], counts), refs[n_val:]
    msg_ref, coul, conds, vown, part, msg, coul_sems, cond_sems, val_sems = refs
    npt = coul_ref.shape[1]
    column = pl.multiple_of(lax.axis_index("band") * own, LANES)
    coul_copies = [
        pltpu.make_async_copy(
            coul_ref.at[:, pl.ds(i * chunk, chunk)], coul.at[:, pl.ds(i * chunk, chunk)], coul_sems.at[i]
        )
        for i in range(npt // chunk)
    ]
    copies = block_copies([[ref] for ref in cond_refs], own, conds, cond_sems)
    copies += block_copies(val_refs, own, vown, val_sems, column)
    start_all(coul_copies + copies)
    acc = jnp.zeros((own, LANES), F32)
    per_dev = own // LANES
    for i in range(npt // chunk):
        coul_copies[i].wait()
        for j in range(i * chunk // LANES, (i + 1) * chunk // LANES):
            rho = rho_ref[j // per_dev, pl.ds(j % per_dev, 1), :].astype(BF).astype(F32)
            acc = acc + coul[:, j * LANES : (j + 1) * LANES].astype(F32) * rho
    potential = scale * jnp.sum(acc.T, axis=0, keepdims=True)
    wait_all(copies)
    cond_rows = conds[...].reshape(-1, own)
    for kp in range(k_points // 2):
        weighted = (pair_rows(vown, kp).astype(F32) * potential).astype(BF)
        ex = dot_nt(weighted, cond_rows[kp * LANES : (kp + 1) * LANES, :])
        part[kp] = 2.0 * ex - di_ref[kp]
    for d in range(n_band):
        for j in range(n_ka):
            for g in range((k_dev + 1) // 2):
                tile = None
                for kl in range(2 * g, min(2 * g + 2, k_dev)):
                    k = j * k_dev + kl
                    piece = part[k // 2, pl.ds(d * 2 * ROWS + k % 2 * ROWS, ROWS), :]
                    piece = lane_half(piece, k % 2, kl % 2)
                    tile = piece if tile is None else tile + piece
                msg[device_at(n_band, j, d), pl.ds(g * ROWS, ROWS), :] = tile
    msg_ref[...] = msg[...].astype(BF)


def received(recv_ref):
    return jnp.sum(recv_ref[...].astype(F32), axis=0)


def shifted(count_all, shift, square, cross_sum, square_sum):
    alpha = shift * square + cross_sum / count_all
    d = alpha - shift
    mean_sq = (square_sum - 2.0 * d * cross_sum) / count_all + d * d * square
    mean_sq = jnp.maximum(mean_sq, 0.0)
    return alpha, d, mean_sq


def first_owner_kernel(count_all, recv_ref, msgs_ref, gap_ref, own_ref, state_ref, coef_ref, msg_ref):
    start_sq, gap_sq = read_sums(msgs_ref, 2)
    norm = start_sq / count_all
    inv = 1.0 / jnp.sqrt(norm + 1e-06)
    square = norm / (norm + 1e-06)
    shift = gap_sq / jnp.maximum(start_sq, 1e-30)
    cur = own_ref[...] * inv
    inter = received(recv_ref) * inv
    gap = gap_ref[...]
    resid = (gap - shift) * cur + inter
    state_ref[0] = cur
    state_ref[1] = resid
    state_ref[2] = inter
    coef_ref[0] = shift
    coef_ref[1] = square
    coef_ref[2] = gap_sq * inv * inv
    sums = [
        jnp.sum(cur * resid),
        jnp.sum(resid * resid),
        jnp.sum(gap * resid * resid),
        jnp.sum(gap * resid * cur),
    ]
    msg_ref[...] = jnp.broadcast_to(with_sums(resid, sums).astype(BF)[None], msg_ref.shape)


def second_owner_kernel(count_all, recv_ref, msgs_ref, gap_ref, state_ref, coef_ref, out_ref, coef_out, msg_ref):
    cross, total, gap_rr, gap_rq = read_sums(msgs_ref, 4)
    alpha, d, mean_sq = shifted(count_all, coef_ref[0], coef_ref[1], cross, total)
    beta = jnp.sqrt(mean_sq + 1e-06)
    square = mean_sq / (mean_sq + 1e-06)
    gap_qq = gap_rr - 2.0 * d * gap_rq + d * d * coef_ref[2]
    shift = gap_qq / (mean_sq + 1e-06) / count_all
    prev = state_ref[0]
    cur = (state_ref[1] - d * prev) / beta
    inter = (received(recv_ref) - d * state_ref[2]) / beta
    resid = (gap_ref[...] - shift) * cur + inter - beta * prev
    out_ref[0] = cur
    out_ref[1] = resid
    coef_out[0] = alpha
    coef_out[1] = beta
    coef_out[2] = shift
    coef_out[3] = square
    dims = msg_ref.shape[:1] + msg_ref.shape[2:]
    msg_ref[:, 0, :] = jnp.full(dims, jnp.sum(cur * resid), F32)
    msg_ref[:, 1, :] = jnp.full(dims, jnp.sum(resid * resid), F32)


def finish_kernel(count_all, msgs_ref, state_ref, coef_ref, out_ref, coeffs_ref):
    sums = jnp.sum(msgs_ref[...], axis=0)
    alpha, d, mean_sq = shifted(count_all, coef_ref[2], coef_ref[3], sums[0, 0], sums[1, 0])
    beta = jnp.sqrt(mean_sq + 1e-06)
    own = (state_ref[1] - d * state_ref[0]) / beta
    coeffs_ref[0] = coef_ref[0]
    coeffs_ref[1] = alpha
    coeffs_ref[2] = coef_ref[1]
    coeffs_ref[3] = beta
    for kl in range(out_ref.shape[0]):
        tile = own[kl // 2 * ROWS : (kl // 2 + 1) * ROWS, :]
        other = pltpu.roll(tile, HALF, axis=1)
        left, right = (tile, other) if kl % 2 == 0 else (other, tile)
        low = lax.broadcasted_iota(jnp.int32, (1, LANES), 1) < HALF
        for j in range(ROWS // 2):
            row = jnp.where(low, left[2 * j : 2 * j + 1], right[2 * j + 1 : 2 * j + 2])
            out_ref[pl.ds(kl, 1), pl.ds(j * LANES, LANES)] = row


def shape_of(dims, kind=F32):
    return jax.ShapeDtypeStruct(dims, kind)


def call(kernel, name, out_shape, in_specs, out_specs, scratch=(), flops=0, moved=0):
    return pl.pallas_call(
        kernel,
        out_shape=out_shape,
        in_specs=in_specs,
        out_specs=out_specs,
        scratch_shapes=list(scratch),
        compiler_params=pltpu.CompilerParams(vmem_limit_bytes=58 * MIB),
        cost_estimate=pl.CostEstimate(flops=flops, bytes_accessed=moved, transcendentals=0),
        name=name,
    )


def swap(block, axis, d):
    return lax.ppermute(block, axis, [(i, i ^ d) for i in range(lax.axis_size(axis))])


def plane_pieces(own_piece):
    def move(block, d):
        return swap(block, "band", d)

    half = own_piece.shape[0] // 2
    by_x, by_y = move(own_piece, 2), move(own_piece, 4)
    diag = [move(by_x[:half], 4), move(by_y[half:], 2)]
    pieces = [[own_piece], [move(own_piece, 1)], [by_x], [move(by_x, 1)], [by_y], [move(by_y, 1)]]
    return pieces + [diag, [move(part, 1) for part in diag]]


def kernel_path(start_vec, val_energy, cond_energy, val_orb, cond_orb, coulomb, screened):
    n_ka = lax.axis_size("ka")
    n_band = lax.axis_size("band")
    devices = n_ka * n_band
    ka, band = lax.axis_index("ka"), lax.axis_index("band")
    k_dev = start_vec.shape[0]
    nv_blk = val_orb.shape[1]
    n_cond = cond_orb.shape[1]
    npt_all = cond_orb.shape[2]
    k_points = k_dev * n_ka
    pairs = k_points // 2
    mu_blk, nu_blk = screened.shape
    own = coulomb.shape[0]
    count_all = k_points * nv_blk * n_band * n_cond
    scale = 1.0 / (npt_all * math.sqrt(count_all))
    piece_rows = k_points * nv_blk

    cond_local = lax.dynamic_slice_in_dim(cond_orb, band * mu_blk, mu_blk, 2)
    cond_pts = lax.all_gather(
        cond_local.reshape(k_dev * n_cond, mu_blk), "ka", axis=0, tiled=True
    )

    def val_to(j):
        part = lax.dynamic_slice_in_dim(val_orb, jnp.bitwise_xor(ka, j) * nu_blk, nu_blk, 2)
        return part.reshape(k_dev * nv_blk, nu_blk)

    def cond_to(j):
        at = jnp.bitwise_xor(ka, j) * nu_blk + band * own
        return lax.dynamic_slice_in_dim(cond_orb, at, own, 2).reshape(k_dev * n_cond, own)

    val_cut = jnp.concatenate(
        [val_to(0)] + [swap(val_to(j), "ka", j) for j in range(1, n_ka)], axis=0
    )
    cond_own = [cond_to(0)] + [swap(cond_to(j), "ka", j) for j in range(1, n_ka)]
    pieces = plane_pieces(val_cut)
    counts = tuple(len(piece) for piece in pieces)
    flat = [ref for piece in pieces for ref in piece]
    n_copies = len(flat)
    gap = (cond_energy[:, None, :] - val_energy[:, :, None]).reshape(k_dev, nv_blk * n_cond)
    gap = pack_vector(gap, k_dev)

    block = gap.shape
    msg_shape = shape_of((devices,) + block, BF)
    start_own, message = call(
        pack_kernel, "pack", (shape_of(block), msg_shape), [VMEM] * 2, (VMEM, VMEM)
    )(start_vec, gap)
    msgs = exchange_all(message)

    own_scratch = [
        pltpu.VMEM((n_ka, k_dev * n_cond, own), BF),
        pltpu.VMEM((n_band, piece_rows, own), BF),
    ]
    own_sems = [pltpu.SemaphoreType.DMA((n_ka,)), pltpu.SemaphoreType.DMA((n_copies,))]
    tile, chunk = 256, 1024
    cond_side, state, coef = cond_pts, None, None
    for step in range(STEPS):
        first = step == 0
        qx, rho = call(
            functools.partial(density_kernel, (n_ka, n_band, k_dev, own, counts)),
            "density",
            (shape_of((pairs, LANES, LANES), BF), shape_of((devices, own // LANES, LANES))),
            [VMEM] + [ANY] * (n_ka + n_copies),
            (VMEM, VMEM),
            [pltpu.VMEM((pairs, LANES, LANES), F32)] + own_scratch + own_sems,
        )(msgs, *cond_own, *flat)
        density = exchange_all(rho)
        cond_t_dims = (mu_blk, k_points * n_cond)
        out = call(
            functools.partial(direct_kernel, first, (n_ka, n_band, k_points, counts), tile, scale),
            "direct",
            (shape_of((pairs, LANES, LANES)),) + ((shape_of(cond_t_dims, BF),) if first else ()),
            [VMEM] + [ANY] * (2 + n_copies),
            (VMEM,) + ((ANY,) if first else ()),
            ([pltpu.VMEM((k_points * n_cond, mu_blk), BF)] if first else [])
            + [
                pltpu.VMEM(cond_t_dims, BF),
                pltpu.VMEM((n_band, piece_rows, nu_blk), BF),
                pltpu.VMEM((mu_blk, nu_blk), BF),
                pltpu.VMEM((k_points * n_cond, nu_blk), BF),
                pltpu.VMEM((mu_blk, nu_blk), BF),
                pltpu.VMEM((n_band * piece_rows, mu_blk), BF),
                pltpu.SemaphoreType.DMA((n_ka,)),
                pltpu.SemaphoreType.DMA((n_copies,)),
                pltpu.SemaphoreType.DMA((nu_blk // tile,)),
            ],
            4 * mu_blk * nu_blk * k_points * n_cond,
            9 * MIB,
        )(qx, cond_side, screened, *flat)
        direct = out[0]
        if first:
            cond_side = out[1]
        parts = call(
            functools.partial(exchange_kernel, (n_ka, n_band, k_dev, own, counts), chunk, scale),
            "exchange",
            msg_shape,
            [VMEM] * 2 + [ANY] * (1 + n_ka + n_copies),
            VMEM,
            [pltpu.VMEM((own, npt_all), BF)]
            + own_scratch
            + [
                pltpu.VMEM((pairs, LANES, LANES), F32),
                pltpu.VMEM((devices,) + block, F32),
                pltpu.SemaphoreType.DMA((npt_all // chunk,)),
            ]
            + own_sems,
        )(density, direct, coulomb, *cond_own, *flat)
        recv = exchange_all(parts)
        if first:
            state, coef, message = call(
                functools.partial(first_owner_kernel, count_all),
                "first_owner",
                (shape_of((3,) + block), shape_of((3,)), msg_shape),
                [VMEM] * 4,
                (VMEM, SMEM, VMEM),
            )(recv, msgs, gap, start_own)
        else:
            state, coef, message = call(
                functools.partial(second_owner_kernel, count_all),
                "second_owner",
                (shape_of((2,) + block), shape_of((4,)), shape_of((devices, 2, LANES))),
                [VMEM] * 4 + [SMEM],
                (VMEM, SMEM, VMEM),
            )(recv, msgs, gap, state, coef)
        msgs = exchange_all(message)
    return call(
        functools.partial(finish_kernel, count_all),
        "finish",
        (shape_of(start_vec.shape), shape_of((2 * STEPS,))),
        [VMEM] * 2 + [SMEM],
        (VMEM, SMEM),
    )(msgs, state, coef)


def array_path(start_vec, val_energy, cond_energy, val_orb, cond_orb, coulomb, screened):
    n_ka = lax.axis_size("ka")
    n_band = lax.axis_size("band")
    devices = n_ka * n_band
    ka, band = lax.axis_index("ka"), lax.axis_index("band")
    me = ka * n_band + band
    k_dev, pair_blk = start_vec.shape
    nv_blk = val_orb.shape[1]
    n_cond = cond_orb.shape[1]
    n_val = nv_blk * n_band
    npt_all = cond_orb.shape[2]
    k_points = k_dev * n_ka
    mu_blk, nu_blk = screened.shape
    own_pts = coulomb.shape[0]
    count_all = k_points * n_val * n_cond
    kernel_scale = 1.0 / (npt_all * math.sqrt(count_all))

    start_all = gather_all(start_vec, devices)
    val_cut = lax.all_to_all(
        val_orb.reshape(k_dev, nv_blk, n_ka, nu_blk).transpose(2, 0, 1, 3),
        "ka", split_axis=0, concat_axis=0, tiled=True,
    ).reshape(k_points, nv_blk, nu_blk)
    val_pts = lax.all_gather(val_cut, "band", axis=1, tiled=True)
    cond_local = lax.dynamic_slice_in_dim(cond_orb, band * mu_blk, mu_blk, 2)
    cond_pts = lax.all_gather(cond_local, "ka", axis=0, tiled=True)
    cond_rows = cond_orb.reshape(k_dev, n_cond, n_ka, n_band, own_pts)
    cond_rows = lax.dynamic_index_in_dim(cond_rows, band, 3, keepdims=False)
    cond_own = lax.all_to_all(
        cond_rows.transpose(2, 0, 1, 3), "ka", split_axis=0, concat_axis=0, tiled=True
    ).reshape(k_points, n_cond, own_pts)
    val_own = lax.dynamic_slice_in_dim(val_pts, band * own_pts, own_pts, 2)

    energy_gap = (cond_energy[:, None, :] - val_energy[:, :, None]).reshape(k_dev, pair_blk)
    start_sq = jnp.sum(start_all * start_all)
    current = start_all / jnp.sqrt(start_sq / count_all + 1e-06)
    previous = jnp.zeros_like(current)
    beta_val = jnp.float32(0.0)
    alphas = []
    betas = []
    for turn_index in range(STEPS):
        full_vec = (
            current.astype(BF)
            .reshape(n_ka, n_band, k_dev, nv_blk, n_cond)
            .transpose(0, 2, 1, 3, 4)
            .reshape(k_points, n_val, n_cond)
        )
        mixed_f = jnp.einsum("kvc,kvn->kcn", full_vec, val_pts, preferred_element_type=F32)
        mixed_own = lax.dynamic_slice_in_dim(mixed_f, band * own_pts, own_pts, 2)
        density_own = jnp.sum(mixed_own * cond_own.astype(F32), axis=(0, 1))
        density = gather_all(density_own.astype(BF), devices).reshape(npt_all)
        mixed_val = mixed_f.astype(BF)
        amp = jnp.einsum("kcm,kcn->mn", cond_pts, mixed_val, preferred_element_type=F32)
        kern = (screened.astype(F32) * amp * kernel_scale).astype(BF)
        folded = jnp.einsum("mn,kvn->kvm", kern, val_pts, preferred_element_type=F32).astype(BF)
        direct_part = jnp.einsum("kcm,kvm->kvc", cond_pts, folded, preferred_element_type=F32)
        potential = kernel_scale * jnp.dot(coulomb, density, preferred_element_type=F32)
        weighted = (val_own.astype(F32) * potential).astype(BF)
        exchange = jnp.einsum("kvp,kcp->kvc", weighted, cond_own, preferred_element_type=F32)
        part = 2.0 * exchange - direct_part
        arranged = (
            part.reshape(n_ka, k_dev, n_band, nv_blk, n_cond)
            .transpose(0, 2, 1, 3, 4)
            .reshape(devices, k_dev, pair_blk)
        )
        inter_own = jnp.sum(exchange_all(arranged), axis=0)
        current_own = lax.dynamic_index_in_dim(current, me, 0, keepdims=False)
        resid_vec = gather_all(energy_gap * current_own + inter_own, devices)
        resid_vec = resid_vec - beta_val * previous
        alpha_val = jnp.sum(current * resid_vec) / count_all
        resid_vec = resid_vec - alpha_val * current
        beta_val = jnp.sqrt(jnp.sum(resid_vec * resid_vec) / count_all + 1e-06)
        previous = current
        current = resid_vec / beta_val
        alphas.append(alpha_val)
        betas.append(beta_val)
    coeffs = jnp.stack(alphas + betas)
    return (lax.dynamic_index_in_dim(current, me, 0, keepdims=False), coeffs)


def per_device(*args):
    start_vec, _, _, val_orb, cond_orb, coulomb, screened = args
    n_ka, n_band = lax.axis_size("ka"), lax.axis_size("band")
    fits = (
        n_band == 8
        and n_ka & (n_ka - 1) == 0
        and start_vec.shape[0] % 2 == 1
        and val_orb.shape[1] == ROWS
        and cond_orb.shape[1] == HALF
        and start_vec.shape[0] * n_ka % 2 == 0
        and coulomb.shape[0] % LANES == 0
        and coulomb.shape[1] % 1024 == 0
        and screened.shape[0] % 256 == 0
        and screened.shape[1] % 512 == 0
        and screened.shape[0] * screened.shape[1] <= 2 * MIB
    )
    return (kernel_path if fits else array_path)(*args)


def solution(mesh):
    in_specs = (
        P("ka", "band"),
        P("ka", "band"),
        P("ka", None),
        P("ka", "band", None),
        P("ka", None, None),
        P(("ka", "band"), None),
        P("band", "ka"),
    )
    out_specs = (P("ka", "band"), P())
    return jax.shard_map(
        per_device, mesh=mesh, in_specs=in_specs, out_specs=out_specs, check_vma=False
    )
```

time: 206 us -> 193 us (0.937)
  local copies, waits for them, and re-layouts: 35.5 us -> 7.76 us
  Pallas kernels: 38.6 us -> 58.4 us
  waiting for transfers between devices: 41.6 us -> 26.6 us
  blocking collectives: 38.8 us -> 50 us
    all_to_all x2 -> x0, waiting for transfers between devices: 23 us -> none  [the longest x1 19.6 us: kernel_path(): lax.all_to_all(val_orb.reshape(k_dev, nv_blk, n_ka, nu_blk).transpose(2,...]
    unnamed x52 -> x34, local copies, waits for them, and re-layouts: 25.1 us -> 2.32 us
    pallas_call x9 -> x10, Pallas kernels: 38.6 us -> 58.4 us  [the longest x2 35.2 us: kernel_path(): call(functools.partial(direct_kernel, first, (n_ka, n_band, k_points, cou...]
    ppermute x9 -> x15, starting transfers between devices: 6.83 us -> 21.2 us  [swap(): lax.ppermute(block, axis, [(i, i ^ d) for i in range(lax.axis_size(axis))])]
    ppermute x9 -> x15, waiting for transfers between devices: 5 us -> 19 us  [swap(): lax.ppermute(block, axis, [(i, i ^ d) for i in range(lax.axis_size(axis))])]
    all_to_all x3 -> x4, blocking collectives: 38.8 us -> 50 us  [exchange_all(): return lax.all_to_all(parts, AXES, split_axis=0, concat_axis=0, tiled=True)]
    all_to_all x2 -> x0, starting transfers between devices: 9.78 us -> none  [the longest x1 6.32 us: kernel_path(): lax.all_to_all(val_orb.reshape(k_dev, nv_blk, n_ka, nu_blk).transpose(2,...]
    all_to_all x4 -> x3, waiting for transfers between devices: 13.5 us -> 7.61 us  [exchange_all(): return lax.all_to_all(parts, AXES, split_axis=0, concat_axis=0, tiled=True)]
  transfers between devices with their start and end apart: 16 -> 19, of which waited for: 6 -> 7; matrix products, arithmetic and copies ran while one was open for 5% -> 2% of each run, Pallas kernels for 14% -> 21%
where the time goes in v3:
time: 193 us; the launch traced here: 192 us
  Pallas kernels  58.4 us (30%)
  blocking collectives  50 us (26%)
  starting transfers between devices  34.7 us (18%)
  waiting for transfers between devices  26.6 us (14%)
  between operations  14.4 us (7%)
  local copies, waits for them, and re-layouts  7.76 us (4%)
    all_to_all x4, blocking collectives, exchange_all(): return lax.all_to_all(parts, AXES, split_axis=0, concat_axis=0, tiled=True)  50 us
    pallas_call x2, Pallas kernels, kernel_path(): call(functools.partial(direct_kernel, first, (n_ka, n_band, k_points, cou...  35.2 us
    ppermute x15, starting transfers between devices, swap(): lax.ppermute(block, axis, [(i, i ^ d) for i in range(lax.axis_size(axis))])  21.2 us
    ppermute x15, waiting for transfers between devices, swap(): lax.ppermute(block, axis, [(i, i ^ d) for i in range(lax.axis_size(axis))])  19 us
    all_to_all x3, starting transfers between devices, exchange_all(): return lax.all_to_all(parts, AXES, split_axis=0, concat_axis=0, tiled=True)  13.5 us
    pallas_call x2, Pallas kernels, kernel_path(): call(functools.partial(exchange_kernel, (n_ka, n_band, k_dev, own, counts...  9.59 us
    all_to_all x3, waiting for transfers between devices, exchange_all(): return lax.all_to_all(parts, AXES, split_axis=0, concat_axis=0, tiled=True)  7.61 us
    pallas_call x2, Pallas kernels, kernel_path(): call(functools.partial(density_kernel, (n_ka, n_band, k_dev, own, counts)...  6.43 us
  transfers between devices with their start and end apart: 19, of which 7 were waited for; matrix products, arithmetic and copies ran while one was open for 2% of the time, Pallas kernels for 21%

profile of v3, /device:TPU:0, one launch (start us, length us, event | category | flops | bytes accessed | tf_op | source)
XLA Modules:
  0.0 192.1 jit_solution(11823842676506053047)
XLA Ops:
  7.2 1.8 constant_dynamic-slice_fusion
  9.1 1.1 dynamic-slice_bitcast_fusion.3
  10.1 3.1 %collective-permute-start.3 = (bf16[24,2048]{1,0:T(8,128)(2,1)S(1)}, bf16[24,2048]{1,0:T(8,128)(2,1)S(1)}, u32[]{:S(2)}, u32[]{:S(2)}) collective-permute-start(bf16[24,2048]{1,0:T(8,128)(2,1)S(1)} %get-tuple-element.35), channel_id=1, source_target_pairs={{0,8},{8,0},{16,24},{24,16},{1,9},{9,1},{17,25},{25,17},{2,10},{10... | collective-permute-start | bytes 294920 | tf_op jit(solution)/shard_map/ppermute | solution.py:375
  13.2 2.5 %collective-permute-start.5 = (bf16[24,2048]{1,0:T(8,128)(2,1)S(1)}, bf16[24,2048]{1,0:T(8,128)(2,1)S(1)}, u32[]{:S(2)}, u32[]{:S(2)}) collective-permute-start(bf16[24,2048]{1,0:T(8,128)(2,1)S(1)} %get-tuple-element.36), channel_id=1, source_target_pairs={{0,24},{8,16},{16,8},{24,0},{1,25},{9,17},{17,9},{25,1},{2,26},{10... | collective-permute-start | bytes 294920 | tf_op jit(solution)/shard_map/ppermute | solution.py:375
  15.7 0.1 collective-permute-start.4
  15.8 0.2 collective-permute-done.3
  16.0 5.4 %collective-permute-done.5 = bf16[24,2048]{1,0:T(8,128)(2,1)S(1)} collective-permute-done((bf16[24,2048]{1,0:T(8,128)(2,1)S(1)}, bf16[24,2048]{1,0:T(8,128)(2,1)S(1)}, u32[]{:S(2)}, u32[]{:S(2)}) %collective-permute-start.5) | collective-permute-done | bytes 98336 | tf_op jit(solution)/shard_map/ppermute | solution.py:375
  21.4 6.8 %collective-permute-done.4 = bf16[24,2048]{1,0:T(8,128)(2,1)S(1)} collective-permute-done((bf16[24,2048]{1,0:T(8,128)(2,1)S(1)}, bf16[24,2048]{1,0:T(8,128)(2,1)S(1)}, u32[]{:S(2)}, u32[]{:S(2)}) %collective-permute-start.4) | collective-permute-done | bytes 98336 | tf_op jit(solution)/shard_map/ppermute | solution.py:375
  28.2 1.6 collective-permute-start.9
  29.9 1.5 collective-permute-start.7
  31.4 1.7 constant_dynamic-slice_fusion.1
  33.1 1.0 collective-permute-start.1
  34.1 8.7 %collective-permute-start.2 = (bf16[192,256]{1,0:T(8,128)(2,1)S(1)}, bf16[192,256]{1,0:T(8,128)(2,1)S(1)}, u32[]{:S(2)}, u32[]{:S(2)}) collective-permute-start(bf16[192,256]{1,0:T(8,128)(2,1)S(1)} %bitcast.20), channel_id=1, source_target_pairs={{0,24},{8,16},{16,8},{24,0},{1,25},{9,17},{17,9},{25,1},{2,26},{10... | collective-permute-start | bytes 294920 | tf_op jit(solution)/shard_map/ppermute | solution.py:375
  42.8 0.6 collective-permute-start
  43.4 0.4 collective-permute-start.12
  43.8 3.7 %collective-permute-done.1.refs_3_.refs_5_ = bf16[192,256]{1,0:T(8,128)(2,1)S(1)} collective-permute-done((bf16[192,256]{1,0:T(8,128)(2,1)S(1)}, bf16[192,256]{1,0:T(8,128)(2,1)S(1)}, u32[]{:S(2)}, u32[]{:S(2)}) %collective-permute-start.1) | collective-permute-done | bytes 98336 | tf_op jit(solution)/shard_map/ppermute | solution.py:375
  47.6 1.1 collective-permute-start.11
  48.7 1.7 collective-permute-done.2.refs_4_.refs_6_
  50.4 1.1 collective-permute-done.refs_2_.refs_4_
  51.7 0.1 reshape.43
  51.8 0.7 reshape.44.gap_ref
  52.5 1.6 pack.1
  54.1 8.0 %all-to-all-start = ((bf16[32,16,128]{2,1,0:T(8,128)(2,1)}), bf16[32,16,128]{2,1,0:T(8,128)(2,1)}, u32[]{:S(2)}, u32[]{:S(2)}) async-start(bf16[32,16,128]{2,1,0:T(8,128)(2,1)} %get-tuple-element.16), calls=%async_computation | async-start | bytes 262144 | tf_op jit(solution)/shard_map/all_to_all | solution.py:30
  62.1 0.2 collective-permute-start.14
  62.3 0.3 collective-permute-start.13
  62.7 7.6 %all-to-all-done.refs_0_.msgs_ref = bf16[32,16,128]{2,1,0:T(8,128)(2,1)} async-done(((bf16[32,16,128]{2,1,0:T(8,128)(2,1)}), bf16[32,16,128]{2,1,0:T(8,128)(2,1)}, u32[]{:S(2)}, u32[]{:S(2)}) %all-to-all-start) | async-done | bytes 131104 | tf_op jit(solution)/shard_map/all_to_all | solution.py:30
  70.4 0.6 copy-done.3
  71.0 0.1 copy-done.8
  71.1 0.1 copy-done.4
  71.2 0.1 copy-done.9
  71.3 0.2 copy-done.5
  71.5 3.2 %density.2 = (bf16[6,128,128]{2,1,0:T(8,128)(2,1)}, f32[32,2,128]{2,1,0:T(2,128)}) custom-call(bf16[32,16,128]{2,1,0:T(8,128)(2,1)} %all-to-all-done.refs_0_.msgs_ref, bf16[192,256]{1,0:T(8,128)(2,1)} %bitcast.14, bf16[192,256]{1,0:T(8,128)(2,1)} %copy-done.12, bf16[192,256]{1,0:T(8,128)(2,1)} %copy-done.10, bf16[192,256]{1,0:T(8,128)(2,1)} %copy-done.11, ...), custom_call_target="tpu_custom_call" | custom-call | tf_op jit(solution)/shard_map/density/pallas_call | solution.py:446
  74.7 2.8 %all-to-all-start.1 = ((f32[32,2,128]{2,1,0:T(2,128)}), f32[32,2,128]{2,1,0:T(2,128)S(1)}, u32[]{:S(2)}, u32[]{:S(2)}) async-start(f32[32,2,128]{2,1,0:T(2,128)} %get-tuple-element.17), calls=%async_computation.1 | async-start | bytes 65536 | tf_op jit(solution)/shard_map/all_to_all | solution.py:30
  77.5 18.0 %direct.2 = (f32[6,128,128]{2,1,0:T(8,128)}, bf16[1024,768]{1,0:T(8,128)(2,1)}) custom-call(bf16[6,128,128]{2,1,0:T(8,128)(2,1)} %get-tuple-element.18.refs_0_, bf16[768,1024]{1,0:T(8,128)(2,1)} %all-gather.2.cloned.1.call-done.refs_1_, bf16[1024,2048]{1,0:T(8,128)(2,1)} %refs_2_.6, bf16[96,2048]{1,0:T(8,128)(2,1)} %copy-done, bf16[96,2048]{1,0:T(8,128)(2,1)} %copy-done.3, ...), custom_call_target="tpu_custom_call" | custom-call | flops 6442450944 | bytes 9437184 | tf_op jit(solution)/shard_map/direct/pallas_call | solution.py:456
  95.6 0.6 copy-done.14
  96.2 4.8 %exchange.2 = bf16[32,16,128]{2,1,0:T(8,128)(2,1)} custom-call(f32[32,2,128]{2,1,0:T(2,128)} %copy-done.14, f32[6,128,128]{2,1,0:T(8,128)} %get-tuple-element.19.refs_1_, bf16[256,8192]{1,0:T(8,128)(2,1)} %refs_2_.7, bf16[192,256]{1,0:T(8,128)(2,1)} %bitcast.15, bf16[192,256]{1,0:T(8,128)(2,1)} %copy-done.12, bf16[192,256]{1,0:T(8,128)(2,1)} %copy-done.10, ...), custom_call_target="tpu_custom_call" | custom-call | tf_op jit(solution)/shard_map/exchange/pallas_call | solution.py:480
  101.0 14.0 %all_to_all.35.recv_ref = bf16[32,16,128]{2,1,0:T(8,128)(2,1)} all-to-all(bf16[32,16,128]{2,1,0:T(8,128)(2,1)} %exchange.2), channel_id=1, replica_groups=mesh['ka'=4,'band'=8] {'ka','band'}, dimensions={0} | all-to-all | bytes 262144 | tf_op jit(solution)/shard_map/all_to_all | solution.py:30
  115.0 2.0 %first_owner.1 = (f32[3,16,128]{2,1,0:T(8,128)}, f32[3]{0:T(128)}, bf16[32,16,128]{2,1,0:T(8,128)(2,1)}) custom-call(bf16[32,16,128]{2,1,0:T(8,128)(2,1)} %all_to_all.35.recv_ref, bf16[32,16,128]{2,1,0:T(8,128)(2,1)} %all-to-all-done.refs_0_.msgs_ref, f32[16,128]{1,0:T(8,128)} %reshape.44.gap_ref, f32[16,128]{1,0:T(8,128)} %get-tuple-element.20.own_ref), custom_call_target="tpu_custom_call" | custom-call | tf_op jit(solution)/shard_map/first_owner/pallas_call | solution.py:497
  117.0 11.5 %all_to_all.36.refs_0_.msgs_ref = bf16[32,16,128]{2,1,0:T(8,128)(2,1)} all-to-all(bf16[32,16,128]{2,1,0:T(8,128)(2,1)} %get-tuple-element.21), channel_id=1, replica_groups=mesh['ka'=4,'band'=8] {'ka','band'}, dimensions={0} | all-to-all | bytes 262144 | tf_op jit(solution)/shard_map/all_to_all | solution.py:30
  128.5 3.2 %density.3 = (bf16[6,128,128]{2,1,0:T(8,128)(2,1)}, f32[32,2,128]{2,1,0:T(2,128)}) custom-call(bf16[32,16,128]{2,1,0:T(8,128)(2,1)} %all_to_all.36.refs_0_.msgs_ref, bf16[192,256]{1,0:T(8,128)(2,1)} %bitcast.16, bf16[192,256]{1,0:T(8,128)(2,1)} %copy-done.12, bf16[192,256]{1,0:T(8,128)(2,1)} %copy-done.10, bf16[192,256]{1,0:T(8,128)(2,1)} %copy-done.11, ...), custom_call_target="tpu_custom_call" | custom-call | tf_op jit(solution)/shard_map/density/pallas_call | solution.py:446
  131.7 2.8 %all-to-all-start.4 = ((f32[32,2,128]{2,1,0:T(2,128)}), f32[32,2,128]{2,1,0:T(2,128)S(1)}, u32[]{:S(2)}, u32[]{:S(2)}) async-start(f32[32,2,128]{2,1,0:T(2,128)} %get-tuple-element.22), calls=%async_computation.4 | async-start | bytes 65536 | tf_op jit(solution)/shard_map/all_to_all | solution.py:30
  134.5 17.2 %direct.3.refs_1_ = f32[6,128,128]{2,1,0:T(8,128)} custom-call(bf16[6,128,128]{2,1,0:T(8,128)(2,1)} %get-tuple-element.23.refs_0_, bf16[1024,768]{1,0:T(8,128)(2,1)} %get-tuple-element.24.refs_1_, bf16[1024,2048]{1,0:T(8,128)(2,1)} %refs_2_.6, bf16[96,2048]{1,0:T(8,128)(2,1)} %copy-done, bf16[96,2048]{1,0:T(8,128)(2,1)} %copy-done.3, ...), custom_call_target="tpu_custom_call" | custom-call | flops 6442450944 | bytes 9437184 | tf_op jit(solution)/shard_map/direct/pallas_call | solution.py:456
  151.7 0.6 copy-done.13
  152.4 4.8 %exchange.3 = bf16[32,16,128]{2,1,0:T(8,128)(2,1)} custom-call(f32[32,2,128]{2,1,0:T(2,128)} %copy-done.13, f32[6,128,128]{2,1,0:T(8,128)} %direct.3.refs_1_, bf16[256,8192]{1,0:T(8,128)(2,1)} %refs_2_.7, bf16[192,256]{1,0:T(8,128)(2,1)} %bitcast.17, bf16[192,256]{1,0:T(8,128)(2,1)} %copy-done.12, bf16[192,256]{1,0:T(8,128)(2,1)} %copy-done.10, ...), custom_call_target="tpu_custom_call" | custom-call | tf_op jit(solution)/shard_map/exchange/pallas_call | solution.py:480
  157.2 14.0 %all_to_all.37.recv_ref = bf16[32,16,128]{2,1,0:T(8,128)(2,1)} all-to-all(bf16[32,16,128]{2,1,0:T(8,128)(2,1)} %exchange.3), channel_id=1, replica_groups=mesh['ka'=4,'band'=8] {'ka','band'}, dimensions={0} | all-to-all | bytes 262144 | tf_op jit(solution)/shard_map/all_to_all | solution.py:30
  171.1 1.9 %second_owner.1 = (f32[2,16,128]{2,1,0:T(8,128)}, f32[4]{0:T(128)}, f32[32,2,128]{2,1,0:T(2,128)}) custom-call(bf16[32,16,128]{2,1,0:T(8,128)(2,1)} %all_to_all.37.recv_ref, bf16[32,16,128]{2,1,0:T(8,128)(2,1)} %all_to_all.36.refs_0_.msgs_ref, f32[16,128]{1,0:T(8,128)} %reshape.44.gap_ref, f32[3,16,128]{2,1,0:T(8,128)} %get-tuple-element.25.state_ref, ...), custom_call_target="tpu_custom_call" | custom-call | tf_op jit(solution)/shard_map/second_owner/pallas_call | solution.py:505
  173.1 10.5 %all_to_all.38.msgs_ref = f32[32,2,128]{2,1,0:T(2,128)} all-to-all(f32[32,2,128]{2,1,0:T(2,128)} %get-tuple-element.27), channel_id=1, replica_groups=mesh['ka'=4,'band'=8] {'ka','band'}, dimensions={0} | all-to-all | bytes 65536 | tf_op jit(solution)/shard_map/all_to_all | solution.py:30
  183.6 1.6 finish.1
  (51 shorter events, 0.4 us)
Async XLA Ops:
  7.2 44.4 %copy-start.16 = (f32[3,64]{1,0:T(4,128)S(1)}, f32[3,64]{1,0:T(4,128)}, u32[]{:S(2)}) copy-start(f32[3,64]{1,0:T(4,128)} %param.9) | copy-start | bytes 2308
  7.2 44.3 %copy-start.15 = (f32[3,8]{1,0:T(4,128)S(1)}, f32[3,8]{1,0:T(4,128)}, u32[]{:S(2)}) copy-start(f32[3,8]{1,0:T(4,128)} %param.8) | copy-start | bytes 292
  7.2 70.3 %all-gather.2.cloned.1.call-start = ((), (), s32[]{:S(2)}) async-start(), calls=%async_computation.7 | async-start | bytes 1966080 | tf_op jit(solution)/shard_map/all_gather | solution.py:407
  10.1 5.9 %collective-permute-start.3 = (bf16[24,2048]{1,0:T(8,128)(2,1)S(1)}, bf16[24,2048]{1,0:T(8,128)(2,1)S(1)}, u32[]{:S(2)}, u32[]{:S(2)}) collective-permute-start(bf16[24,2048]{1,0:T(8,128)(2,1)S(1)} %get-tuple-element.35), channel_id=1, source_target_pairs={{0,8},{8,0},{16,24},{24,16},{1,9},{9,1},{17,25},{25,17},{2,10},{10... | collective-permute-start | bytes 294920 | tf_op jit(solution)/shard_map/ppermute | solution.py:375
  13.2 8.2 %collective-permute-start.5 = (bf16[24,2048]{1,0:T(8,128)(2,1)S(1)}, bf16[24,2048]{1,0:T(8,128)(2,1)S(1)}, u32[]{:S(2)}, u32[]{:S(2)}) collective-permute-start(bf16[24,2048]{1,0:T(8,128)(2,1)S(1)} %get-tuple-element.36), channel_id=1, source_target_pairs={{0,24},{8,16},{16,8},{24,0},{1,25},{9,17},{17,9},{25,1},{2,26},{10... | collective-permute-start | bytes 294920 | tf_op jit(solution)/shard_map/ppermute | solution.py:375
  15.7 12.5 %collective-permute-start.4 = (bf16[24,2048]{1,0:T(8,128)(2,1)S(1)}, bf16[24,2048]{1,0:T(8,128)(2,1)S(1)}, u32[]{:S(2)}, u32[]{:S(2)}) collective-permute-start(bf16[24,2048]{1,0:T(8,128)(2,1)S(1)} %get-tuple-element.37), channel_id=1, source_target_pairs={{0,16},{8,24},{16,0},{24,8},{1,17},{9,25},{17,1},{25,9},{2,18},{10... | collective-permute-start | bytes 294920 | tf_op jit(solution)/shard_map/ppermute | solution.py:375
  28.2 42.1 %copy-start = (bf16[96,2048]{1,0:T(8,128)(2,1)}, bf16[96,2048]{1,0:T(8,128)(2,1)S(1)}, u32[]{:S(2)}) copy-start(bf16[96,2048]{1,0:T(8,128)(2,1)S(1)} %pad_maximum_fusion.refs_5_.refs_3_.refs_7_) | copy-start | bytes 1179652
  28.2 15.1 %collective-permute-start.9 = (bf16[96,2048]{1,0:T(8,128)(2,1)S(1)}, bf16[96,2048]{1,0:T(8,128)(2,1)S(1)}, u32[]{:S(2)}, u32[]{:S(2)}) collective-permute-start(bf16[96,2048]{1,0:T(8,128)(2,1)S(1)} %pad_maximum_fusion.refs_5_.refs_3_.refs_7_), channel_id=1, source_target_pairs={{0,4},{1,5},{2,6},{3,7},{4,0},{5,1},{6,2},{7,3},{8,12},{9,13},{10,... | collective-permute-start | bytes 1179656 | tf_op jit(solution)/shard_map/ppermute | solution.py:375
  29.9 13.5 %collective-permute-start.7 = (bf16[96,2048]{1,0:T(8,128)(2,1)S(1)}, bf16[96,2048]{1,0:T(8,128)(2,1)S(1)}, u32[]{:S(2)}, u32[]{:S(2)}) collective-permute-start(bf16[96,2048]{1,0:T(8,128)(2,1)S(1)} %pad_maximum_fusion.refs_5_.refs_3_.refs_7_), channel_id=1, source_target_pairs={{0,2},{1,3},{2,0},{3,1},{4,6},{5,7},{6,4},{7,5},{8,10},{9,11},{10,... | collective-permute-start | bytes 1179656 | tf_op jit(solution)/shard_map/ppermute | solution.py:375
  33.1 14.5 %collective-permute-start.1 = (bf16[192,256]{1,0:T(8,128)(2,1)S(1)}, bf16[192,256]{1,0:T(8,128)(2,1)S(1)}, u32[]{:S(2)}, u32[]{:S(2)}) collective-permute-start(bf16[192,256]{1,0:T(8,128)(2,1)S(1)} %bitcast.21), channel_id=1, source_target_pairs={{0,16},{8,24},{16,0},{24,8},{1,17},{9,25},{17,1},{25,9},{2,18},{10... | collective-permute-start | bytes 294920 | tf_op jit(solution)/shard_map/ppermute | solution.py:375
  34.1 16.3 %collective-permute-start.2 = (bf16[192,256]{1,0:T(8,128)(2,1)S(1)}, bf16[192,256]{1,0:T(8,128)(2,1)S(1)}, u32[]{:S(2)}, u32[]{:S(2)}) collective-permute-start(bf16[192,256]{1,0:T(8,128)(2,1)S(1)} %bitcast.20), channel_id=1, source_target_pairs={{0,24},{8,16},{16,8},{24,0},{1,25},{9,17},{17,9},{25,1},{2,26},{10... | collective-permute-start | bytes 294920 | tf_op jit(solution)/shard_map/ppermute | solution.py:375
  42.8 8.7 %collective-permute-start = (bf16[192,256]{1,0:T(8,128)(2,1)S(1)}, bf16[192,256]{1,0:T(8,128)(2,1)S(1)}, u32[]{:S(2)}, u32[]{:S(2)}) collective-permute-start(bf16[192,256]{1,0:T(8,128)(2,1)S(1)} %bitcast.19), channel_id=1, source_target_pairs={{0,8},{8,0},{16,24},{24,16},{1,9},{9,1},{17,25},{25,17},{2,10},{10... | collective-permute-start | bytes 294920 | tf_op jit(solution)/shard_map/ppermute | solution.py:375
  43.4 27.0 %copy-start.1 = (bf16[96,2048]{1,0:T(8,128)(2,1)}, bf16[96,2048]{1,0:T(8,128)(2,1)S(1)}, u32[]{:S(2)}) copy-start(bf16[96,2048]{1,0:T(8,128)(2,1)S(1)} %collective-permute-done.9.refs_9_.refs_7_.refs_11_) | copy-start | bytes 1179652
  43.4 26.9 %collective-permute-start.6 = (bf16[96,2048]{1,0:T(8,128)(2,1)S(1)}, bf16[96,2048]{1,0:T(8,128)(2,1)S(1)}, u32[]{:S(2)}, u32[]{:S(2)}) collective-permute-start(bf16[96,2048]{1,0:T(8,128)(2,1)S(1)} %pad_maximum_fusion.refs_5_.refs_3_.refs_7_), channel_id=1, source_target_pairs={{0,1},{1,0},{2,3},{3,2},{4,5},{5,4},{6,7},{7,6},{8,9},{9,8},{10,11... | collective-permute-start | bytes 1179656 | tf_op jit(solution)/shard_map/ppermute | solution.py:375
  43.4 27.0 %copy-start.2 = (bf16[96,2048]{1,0:T(8,128)(2,1)}, bf16[96,2048]{1,0:T(8,128)(2,1)S(1)}, u32[]{:S(2)}) copy-start(bf16[96,2048]{1,0:T(8,128)(2,1)S(1)} %collective-permute-done.7.refs_7_.refs_5_.refs_9_) | copy-start | bytes 1179652
  43.4 18.7 %collective-permute-start.12 = (bf16[48,2048]{1,0:T(8,128)(2,1)S(1)}, bf16[48,2048]{1,0:T(8,128)(2,1)S(1)}, u32[]{:S(2)}, u32[]{:S(2)}) collective-permute-start(bf16[48,2048]{1,0:T(8,128)(2,1)S(1)} %slice.9), channel_id=1, source_target_pairs={{0,2},{1,3},{2,0},{3,1},{4,6},{5,7},{6,4},{7,5},{8,10},{9,11},{10,... | collective-permute-start | bytes 589832 | tf_op jit(solution)/shard_map/ppermute | solution.py:375
  47.6 22.8 %copy-start.10 = (bf16[192,256]{1,0:T(8,128)(2,1)}, bf16[192,256]{1,0:T(8,128)(2,1)S(1)}, u32[]{:S(2)}) copy-start(bf16[192,256]{1,0:T(8,128)(2,1)S(1)} %collective-permute-done.1.refs_3_.refs_5_) | copy-start | bytes 294916
  47.6 14.8 %collective-permute-start.11 = (bf16[48,2048]{1,0:T(8,128)(2,1)S(1)}, bf16[48,2048]{1,0:T(8,128)(2,1)S(1)}, u32[]{:S(2)}, u32[]{:S(2)}) collective-permute-start(bf16[48,2048]{1,0:T(8,128)(2,1)S(1)} %slice.8), channel_id=1, source_target_pairs={{0,4},{1,5},{2,6},{3,7},{4,0},{5,1},{6,2},{7,3},{8,12},{9,13},{10,... | collective-permute-start | bytes 589832 | tf_op jit(solution)/shard_map/ppermute | solution.py:375
  50.4 20.0 %copy-start.11 = (bf16[192,256]{1,0:T(8,128)(2,1)}, bf16[192,256]{1,0:T(8,128)(2,1)S(1)}, u32[]{:S(2)}) copy-start(bf16[192,256]{1,0:T(8,128)(2,1)S(1)} %collective-permute-done.2.refs_4_.refs_6_) | copy-start | bytes 294916
  50.4 19.9 %collective-permute-start.10 = (bf16[96,2048]{1,0:T(8,128)(2,1)S(1)}, bf16[96,2048]{1,0:T(8,128)(2,1)S(1)}, u32[]{:S(2)}, u32[]{:S(2)}) collective-permute-start(bf16[96,2048]{1,0:T(8,128)(2,1)S(1)} %collective-permute-done.9.refs_9_.refs_7_.refs_11_), channel_id=1, source_target_pairs={{0,1},{1,0},{2,3},{3,2},{4,5},{5,4},{6,7},{7,6},{8,9},{9,8},{10,11... | collective-permute-start | bytes 1179656 | tf_op jit(solution)/shard_map/ppermute | solution.py:375
  51.5 18.9 %copy-start.12 = (bf16[192,256]{1,0:T(8,128)(2,1)}, bf16[192,256]{1,0:T(8,128)(2,1)S(1)}, u32[]{:S(2)}) copy-start(bf16[192,256]{1,0:T(8,128)(2,1)S(1)} %collective-permute-done.refs_2_.refs_4_) | copy-start | bytes 294916
  51.5 18.8 %collective-permute-start.8 = (bf16[96,2048]{1,0:T(8,128)(2,1)S(1)}, bf16[96,2048]{1,0:T(8,128)(2,1)S(1)}, u32[]{:S(2)}, u32[]{:S(2)}) collective-permute-start(bf16[96,2048]{1,0:T(8,128)(2,1)S(1)} %collective-permute-done.7.refs_7_.refs_5_.refs_9_), channel_id=1, source_target_pairs={{0,1},{1,0},{2,3},{3,2},{4,5},{5,4},{6,7},{7,6},{8,9},{9,8},{10,11... | collective-permute-start | bytes 1179656 | tf_op jit(solution)/shard_map/ppermute | solution.py:375
  54.1 16.2 %all-to-all-start = ((bf16[32,16,128]{2,1,0:T(8,128)(2,1)}), bf16[32,16,128]{2,1,0:T(8,128)(2,1)}, u32[]{:S(2)}, u32[]{:S(2)}) async-start(bf16[32,16,128]{2,1,0:T(8,128)(2,1)} %get-tuple-element.16), calls=%async_computation | async-start | bytes 262144 | tf_op jit(solution)/shard_map/all_to_all | solution.py:30
  62.1 8.3 %copy-start.6 = (bf16[48,2048]{1,0:T(8,128)(2,1)}, bf16[48,2048]{1,0:T(8,128)(2,1)S(1)}, u32[]{:S(2)}) copy-start(bf16[48,2048]{1,0:T(8,128)(2,1)S(1)} %collective-permute-done.12.refs_12_.refs_10_.refs_14_) | copy-start | bytes 589828
  62.1 8.2 %collective-permute-start.14 = (bf16[48,2048]{1,0:T(8,128)(2,1)S(1)}, bf16[48,2048]{1,0:T(8,128)(2,1)S(1)}, u32[]{:S(2)}, u32[]{:S(2)}) collective-permute-start(bf16[48,2048]{1,0:T(8,128)(2,1)S(1)} %collective-permute-done.12.refs_12_.refs_10_.refs_14_), channel_id=1, source_target_pairs={{0,1},{1,0},{2,3},{3,2},{4,5},{5,4},{6,7},{7,6},{8,9},{9,8},{10,11... | collective-permute-start | bytes 589832 | tf_op jit(solution)/shard_map/ppermute | solution.py:375
  62.3 8.1 %copy-start.7 = (bf16[48,2048]{1,0:T(8,128)(2,1)}, bf16[48,2048]{1,0:T(8,128)(2,1)S(1)}, u32[]{:S(2)}) copy-start(bf16[48,2048]{1,0:T(8,128)(2,1)S(1)} %collective-permute-done.11.refs_11_.refs_9_.refs_13_) | copy-start | bytes 589828
  62.3 8.0 %collective-permute-start.13 = (bf16[48,2048]{1,0:T(8,128)(2,1)S(1)}, bf16[48,2048]{1,0:T(8,128)(2,1)S(1)}, u32[]{:S(2)}, u32[]{:S(2)}) collective-permute-start(bf16[48,2048]{1,0:T(8,128)(2,1)S(1)} %collective-permute-done.11.refs_11_.refs_9_.refs_13_), channel_id=1, source_target_pairs={{0,1},{1,0},{2,3},{3,2},{4,5},{5,4},{6,7},{7,6},{8,9},{9,8},{10,11... | collective-permute-start | bytes 589832 | tf_op jit(solution)/shard_map/ppermute | solution.py:375
  70.3 0.8 copy-start.3
  70.3 0.8 copy-start.8
  70.3 0.9 copy-start.4
  70.3 1.0 copy-start.9
  70.3 1.1 copy-start.5
  74.7 20.8 %all-to-all-start.1 = ((f32[32,2,128]{2,1,0:T(2,128)}), f32[32,2,128]{2,1,0:T(2,128)S(1)}, u32[]{:S(2)}, u32[]{:S(2)}) async-start(f32[32,2,128]{2,1,0:T(2,128)} %get-tuple-element.17), calls=%async_computation.1 | async-start | bytes 65536 | tf_op jit(solution)/shard_map/all_to_all | solution.py:30
  95.6 0.6 copy-start.14
  131.7 20.0 %all-to-all-start.4 = ((f32[32,2,128]{2,1,0:T(2,128)}), f32[32,2,128]{2,1,0:T(2,128)S(1)}, u32[]{:S(2)}, u32[]{:S(2)}) async-start(f32[32,2,128]{2,1,0:T(2,128)} %get-tuple-element.22), calls=%async_computation.4 | async-start | bytes 65536 | tf_op jit(solution)/shard_map/all_to_all | solution.py:30
  151.7 0.6 copy-start.13
Sparse Core Ops, SparseCore 0:
  9.6 49.1 all-gather.1

commit v4 on v3

--- a/solution.py
+++ b/solution.py
@@ -136,133 +136,182 @@
     msg_ref[...] = jnp.broadcast_to(block.astype(BF)[None], msg_ref.shape)
 
 
+def cut_kernel(cond_ref, msgs_ref, *refs):
+    outs, sems = refs[:-1], refs[-1]
+    k_dev, n_cond, npt = cond_ref.shape
+    own = outs[0].shape[1]
+    nu = npt // len(outs)
+    copies = []
+    for j, out in enumerate(outs):
+        at = jnp.bitwise_xor(lax.axis_index("ka"), j) * nu + lax.axis_index("band") * own
+        for kl in range(k_dev):
+            copies.append(
+                pltpu.make_async_copy(
+                    cond_ref.at[kl, :, pl.ds(pl.multiple_of(at, LANES), own)],
+                    out.at[pl.ds(kl * n_cond, n_cond), :],
+                    sems.at[len(copies)],
+                )
+            )
+    start_all(copies)
+    wait_all(copies)
+
+
+def turn_kernel(tile, scr_ref, out_ref, scrs, turned, in_sems, out_sems):
+    nu = scr_ref.shape[1]
+    ins, outs = [], []
+    for j in range(nu // tile):
+        at = pl.ds(j * tile, tile)
+        ins.append(pltpu.make_async_copy(scr_ref.at[:, at], scrs.at[:, at], in_sems.at[j]))
+        outs.append(pltpu.make_async_copy(turned.at[at, :], out_ref.at[at, :], out_sems.at[j]))
+    start_all(ins)
+    for j in range(nu // tile):
+        ins[j].wait()
+        turned[j * tile : (j + 1) * tile, :] = scrs[:, j * tile : (j + 1) * tile].T
+        outs[j].start()
+    wait_all(outs)
+
+
+def order_kernel(counts, *refs):
+    n_val = sum(counts)
+    val_refs, refs = split_refs(refs[:n_val], counts), refs[n_val:]
+    rows_out, turned_out, own_out, vals, ordered, turned, val_sems, out_sems = refs
+    own = own_out.shape[1]
+    nu = ordered.shape[1]
+    copies = block_copies(val_refs, nu, vals, val_sems)
+    start_all(copies)
+    wait_all(copies)
+    group = vals.shape[0] * 2 * ROWS
+    outs = []
+    for kp in range(ordered.shape[0] // group):
+        at = slice(kp * group, (kp + 1) * group)
+        ordered[at, :] = pair_rows(vals, kp)
+        turned[:, at] = ordered[at, :].T
+    column = pl.multiple_of(lax.axis_index("band") * own, LANES)
+    outs = [
+        pltpu.make_async_copy(ordered, rows_out, out_sems.at[0]),
+        pltpu.make_async_copy(turned, turned_out, out_sems.at[1]),
+        pltpu.make_async_copy(ordered.at[:, pl.ds(column, own)], own_out, out_sems.at[2]),
+    ]
+    start_all(outs)
+    wait_all(outs)
+
+
 def density_kernel(cfg, *refs):
-    n_ka, n_band, k_dev, own, counts = cfg
-    n_val = sum(counts)
+    n_ka, n_band, k_dev = cfg
     k_points = n_ka * k_dev
-    msgs_ref, cond_refs, refs = refs[0], refs[1 : 1 + n_ka], refs[1 + n_ka :]
-    val_refs, refs = split_refs(refs[:n_val], counts), refs[n_val:]
-    qx_ref, rho_ref, xs, conds, vown, cond_sems, val_sems = refs
-    column = pl.multiple_of(lax.axis_index("band") * own, LANES)
+    msgs_ref, vown_ref, cond_refs, refs = refs[0], refs[1], refs[2 : 2 + n_ka], refs[2 + n_ka :]
+    qx_ref, rho_ref, xs, conds, cond_sems = refs
+    own = vown_ref.shape[1]
     copies = block_copies([[ref] for ref in cond_refs], own, conds, cond_sems)
-    copies += block_copies(val_refs, own, vown, val_sems, column)
     start_all(copies)
+    xs[...] = jnp.zeros_like(xs)
     for d in range(n_band):
         for k in range(k_points):
             j, kl = divmod(k, k_dev)
             tile = msgs_ref[device_at(n_band, j, d), :, :].astype(F32)
             tile = tile[kl // 2 * ROWS : (kl // 2 + 1) * ROWS, :]
-            xs[k // 2, pl.ds(d * 2 * ROWS + k % 2 * ROWS, ROWS), :] = lane_half(tile, kl % 2, k % 2)
+            base = k // 2 % 2 * LANES
+            at = pl.ds(base + d * 2 * ROWS + k % 2 * ROWS, ROWS)
+            xs[k // 4, at, pl.ds(base, LANES)] = lane_half(tile, kl % 2, k % 2)
     qx_ref[...] = xs[...].astype(BF)
     wait_all(copies)
     cond_rows = conds[...].reshape(-1, own)
     rho = jnp.zeros((1, own), F32)
-    for kp in range(k_points // 2):
-        mixed = dot_tn(qx_ref[kp], pair_rows(vown, kp))
-        cond = cond_rows[kp * LANES : (kp + 1) * LANES, :].astype(F32)
-        rho = rho + jnp.sum(mixed * cond, axis=0, keepdims=True)
+    quad = 2 * LANES
+    for kq in range(k_points // 4):
+        at = slice(kq * quad, (kq + 1) * quad)
+        mixed = dot_tn(qx_ref[kq], vown_ref[at, :])
+        rho = rho + jnp.sum(mixed * cond_rows[at, :].astype(F32), axis=0, keepdims=True)
     for r in range(own // LANES):
         part = rho[:, r * LANES : (r + 1) * LANES]
         rho_ref[:, r, :] = jnp.broadcast_to(part, (rho_ref.shape[0], LANES))
 
 
-def direct_kernel(first, cfg, tile, scale, *refs):
-    n_ka, n_band, k_points, counts = cfg
-    n_val = sum(counts)
-    qx_ref, cond_ref, scr_ref = refs[:3]
-    val_refs, refs = split_refs(refs[3 : 3 + n_val], counts), refs[3 + n_val :]
-    if first:
-        di_ref, cond_out, conds, refs = refs[0], refs[1], refs[2], refs[3:]
-    else:
-        di_ref, refs = refs[0], refs[1:]
-    cond_t, vals, scrs, mixed, kern, folded, cond_sems, val_sems, scr_sems = refs
-    mu, nu = scr_ref.shape
-    pairs = k_points // 2
-    val_copies = block_copies(val_refs, nu, vals, val_sems)
-    if first:
-        rows = cond_ref.shape[0] // n_ka
-        cond_copies = [
-            pltpu.make_async_copy(
-                cond_ref.at[pl.ds(jnp.bitwise_xor(lax.axis_index("ka"), j) * rows, rows), :],
-                conds.at[pl.ds(j * rows, rows), :],
-                cond_sems.at[j],
-            )
-            for j in range(n_ka)
-        ]
-    else:
-        cond_copies = [pltpu.make_async_copy(cond_ref, cond_t, cond_sems.at[0])]
-    scr_copies = [
+def direct_kernel(n_ka, tile, scale, *refs):
+    qx_ref, cond_ref, scr_ref, turned_ref, rows_ref, di_ref = refs[:6]
+    qx, conds, scrs, turned, vals, mixed, kern, folded, qx_sem, cond_sems, row_sem, chunk_sems = refs[6:]
+    nu, mu = scr_ref.shape
+    quad = 2 * LANES
+    part = cond_ref.shape[0] // n_ka
+    qx_copy = pltpu.make_async_copy(qx_ref, qx, qx_sem.at[0])
+    cond_copies = [
         pltpu.make_async_copy(
-            scr_ref.at[:, pl.ds(j * tile, tile)], scrs.at[:, pl.ds(j * tile, tile)], scr_sems.at[j]
+            cond_ref.at[pl.ds(jnp.bitwise_xor(lax.axis_index("ka"), j) * part, part), :],
+            conds.at[pl.ds(j * part, part), :],
+            cond_sems.at[j],
         )
-        for j in range(nu // tile)
+        for j in range(n_ka)
     ]
-    start_all(val_copies + cond_copies + scr_copies)
-    wait_all(val_copies)
-    for kp in range(pairs):
-        mixed[kp * LANES : (kp + 1) * LANES, :] = dot_tn(qx_ref[kp], pair_rows(vals, kp)).astype(BF)
-    wait_all(cond_copies)
-    if first:
-        cond_t[...] = conds[...].T
-        out_copy = pltpu.make_async_copy(cond_t, cond_out, cond_sems.at[0])
-        out_copy.start()
-    for j in range(nu // tile):
-        at = slice(j * tile, (j + 1) * tile)
-        scr_copies[j].wait()
-        amp = jnp.dot(cond_t[...], mixed[:, at], preferred_element_type=F32)
-        kern[:, at] = (scrs[:, at].astype(F32) * amp * scale).astype(BF)
-    all_vals = vals[...].reshape(-1, nu)
-    for i in range(mu // tile):
+    turned_copies, scr_copies = [], []
+    for i in range(nu // tile):
+        at = pl.ds(i * tile, tile)
+        turned_copies.append(
+            pltpu.make_async_copy(turned_ref.at[at, :], turned.at[at, :], chunk_sems.at[0, i])
+        )
+        scr_copies.append(
+            pltpu.make_async_copy(scr_ref.at[at, :], scrs.at[at, :], chunk_sems.at[1, i])
+        )
+    row_copy = pltpu.make_async_copy(rows_ref, vals, row_sem.at[0])
+    start_all([qx_copy, turned_copies[0]] + cond_copies + [scr_copies[0]])
+    for i in range(1, nu // tile):
+        start_all([turned_copies[i], scr_copies[i]])
+    row_copy.start()
+    qx_copy.wait()
+    for i in range(nu // tile):
         at = slice(i * tile, (i + 1) * tile)
-        folded[:, at] = dot_nt(all_vals, kern[at, :]).astype(BF)
-    per_piece = pairs * 2 * ROWS
-    for kp in range(pairs):
-        rows = [
-            folded[d * per_piece + kp * 2 * ROWS : d * per_piece + (kp + 1) * 2 * ROWS, :]
-            for d in range(n_band)
-        ]
-        di_ref[kp] = jnp.dot(
-            jnp.concatenate(rows, axis=0),
-            cond_t[:, kp * LANES : (kp + 1) * LANES],
-            preferred_element_type=F32,
-        )
-    if first:
-        out_copy.wait()
+        turned_copies[i].wait()
+        for kq in range(qx.shape[0]):
+            cols = slice(kq * quad, (kq + 1) * quad)
+            mixed[at, cols] = jnp.dot(
+                turned[at, cols], qx[kq], preferred_element_type=F32
+            ).astype(BF)
+        if i == 0:
+            wait_all(cond_copies)
+        scr_copies[i].wait()
+        amp = jnp.dot(mixed[at, :], conds[...], preferred_element_type=F32)
+        kern[at, :] = (scrs[at, :].astype(F32) * amp * scale).astype(BF)
+    row_copy.wait()
+    for i in range(mu // quad):
+        at = slice(i * quad, (i + 1) * quad)
+        folded[:, at] = jnp.dot(vals[...], kern[:, at], preferred_element_type=F32).astype(BF)
+    for kp in range(di_ref.shape[0]):
+        at = slice(kp * LANES, (kp + 1) * LANES)
+        di_ref[kp] = dot_nt(folded[at, :], conds[at, :])
 
 
 def exchange_kernel(cfg, chunk, scale, *refs):
-    n_ka, n_band, k_dev, own, counts = cfg
-    n_val = sum(counts)
+    n_ka, n_band, k_dev = cfg
     k_points = n_ka * k_dev
-    rho_ref, di_ref, coul_ref = refs[:3]
-    cond_refs, refs = refs[3 : 3 + n_ka], refs[3 + n_ka :]
-    val_refs, refs = split_refs(refs[:n_val], counts), refs[n_val:]
-    msg_ref, coul, conds, vown, part, msg, coul_sems, cond_sems, val_sems = refs
-    npt = coul_ref.shape[1]
-    column = pl.multiple_of(lax.axis_index("band") * own, LANES)
+    rho_ref, di_ref, coul_ref, vown_ref = refs[:4]
+    cond_refs, refs = refs[4 : 4 + n_ka], refs[4 + n_ka :]
+    msg_ref, rhos, di, coul, conds, vown, part, msg, coul_sems, cond_sems, sems = refs
+    own, npt = coul_ref.shape
     coul_copies = [
         pltpu.make_async_copy(
             coul_ref.at[:, pl.ds(i * chunk, chunk)], coul.at[:, pl.ds(i * chunk, chunk)], coul_sems.at[i]
         )
         for i in range(npt // chunk)
     ]
+    rho_copy = pltpu.make_async_copy(rho_ref, rhos, sems.at[0])
     copies = block_copies([[ref] for ref in cond_refs], own, conds, cond_sems)
-    copies += block_copies(val_refs, own, vown, val_sems, column)
-    start_all(coul_copies + copies)
+    copies.append(pltpu.make_async_copy(di_ref, di, sems.at[1]))
+    copies.append(pltpu.make_async_copy(vown_ref, vown, sems.at[2]))
+    start_all([rho_copy] + coul_copies + copies)
+    rho_copy.wait()
     acc = jnp.zeros((own, LANES), F32)
     per_dev = own // LANES
     for i in range(npt // chunk):
         coul_copies[i].wait()
         for j in range(i * chunk // LANES, (i + 1) * chunk // LANES):
-            rho = rho_ref[j // per_dev, pl.ds(j % per_dev, 1), :].astype(BF).astype(F32)
+            rho = rhos[j // per_dev, pl.ds(j % per_dev, 1), :].astype(BF).astype(F32)
             acc = acc + coul[:, j * LANES : (j + 1) * LANES].astype(F32) * rho
     potential = scale * jnp.sum(acc.T, axis=0, keepdims=True)
     wait_all(copies)
     cond_rows = conds[...].reshape(-1, own)
     for kp in range(k_points // 2):
-        weighted = (pair_rows(vown, kp).astype(F32) * potential).astype(BF)
-        ex = dot_nt(weighted, cond_rows[kp * LANES : (kp + 1) * LANES, :])
-        part[kp] = 2.0 * ex - di_ref[kp]
+        at = slice(kp * LANES, (kp + 1) * LANES)
+        weighted = (vown[at, :].astype(F32) * potential).astype(BF)
+        part[kp] = 2.0 * dot_nt(weighted, cond_rows[at, :]) - di[kp]
     for d in range(n_band):
         for j in range(n_ka):
             for g in range((k_dev + 1) // 2):
@@ -358,17 +407,21 @@
     return jax.ShapeDtypeStruct(dims, kind)
 
 
-def call(kernel, name, out_shape, in_specs, out_specs, scratch=(), flops=0, moved=0):
+def call(kernel, name, out_shape, in_specs, out_specs, scratch=(), mib=58, flops=0, moved=0):
     return pl.pallas_call(
         kernel,
         out_shape=out_shape,
         in_specs=in_specs,
         out_specs=out_specs,
         scratch_shapes=list(scratch),
-        compiler_params=pltpu.CompilerParams(vmem_limit_bytes=58 * MIB),
+        compiler_params=pltpu.CompilerParams(vmem_limit_bytes=mib * MIB),
         cost_estimate=pl.CostEstimate(flops=flops, bytes_accessed=moved, transcendentals=0),
         name=name,
     )
+
+
+def dma(*dims):
+    return pltpu.SemaphoreType.DMA(dims)
 
 
 def swap(block, axis, d):
@@ -412,14 +465,9 @@
         part = lax.dynamic_slice_in_dim(val_orb, jnp.bitwise_xor(ka, j) * nu_blk, nu_blk, 2)
         return part.reshape(k_dev * nv_blk, nu_blk)
 
-    def cond_to(j):
-        at = jnp.bitwise_xor(ka, j) * nu_blk + band * own
-        return lax.dynamic_slice_in_dim(cond_orb, at, own, 2).reshape(k_dev * n_cond, own)
-
     val_cut = jnp.concatenate(
         [val_to(0)] + [swap(val_to(j), "ka", j) for j in range(1, n_ka)], axis=0
     )
-    cond_own = [cond_to(0)] + [swap(cond_to(j), "ka", j) for j in range(1, n_ka)]
     pieces = plane_pieces(val_cut)
     counts = tuple(len(piece) for piece in pieces)
     flat = [ref for piece in pieces for ref in piece]
@@ -430,68 +478,117 @@
     block = gap.shape
     msg_shape = shape_of((devices,) + block, BF)
     start_own, message = call(
-        pack_kernel, "pack", (shape_of(block), msg_shape), [VMEM] * 2, (VMEM, VMEM)
+        pack_kernel, "pack", (shape_of(block), msg_shape), [VMEM] * 2, (VMEM, VMEM), mib=8
     )(start_vec, gap)
     msgs = exchange_all(message)
-
-    own_scratch = [
-        pltpu.VMEM((n_ka, k_dev * n_cond, own), BF),
-        pltpu.VMEM((n_band, piece_rows, own), BF),
-    ]
-    own_sems = [pltpu.SemaphoreType.DMA((n_ka,)), pltpu.SemaphoreType.DMA((n_copies,))]
-    tile, chunk = 256, 1024
-    cond_side, state, coef = cond_pts, None, None
+    own_rows = k_dev * n_cond
+    cuts = call(
+        cut_kernel,
+        "cut",
+        (shape_of((own_rows, own), BF),) * n_ka,
+        [ANY, ANY],
+        (ANY,) * n_ka,
+        [dma(n_ka * k_dev)],
+        mib=8,
+    )(cond_orb, msgs)
+    cond_own = [cuts[0]] + [swap(cuts[j], "ka", j) for j in range(1, n_ka)]
+
+    chunk, tile = 1024, 512
+    rows_all, conds_all = k_points * nv_blk * n_band, k_points * n_cond
+    scr_turned = call(
+        functools.partial(turn_kernel, tile),
+        "turn",
+        shape_of((nu_blk, mu_blk), BF),
+        [ANY],
+        ANY,
+        [pltpu.VMEM((mu_blk, nu_blk), BF), pltpu.VMEM((nu_blk, mu_blk), BF)]
+        + [dma(nu_blk // tile)] * 2,
+        moved=8 * MIB,
+    )(screened)
+    val_rows, val_turned, val_own = call(
+        functools.partial(order_kernel, counts),
+        "order",
+        (
+            shape_of((rows_all, nu_blk), BF),
+            shape_of((nu_blk, rows_all), BF),
+            shape_of((rows_all, own), BF),
+        ),
+        [ANY] * n_copies,
+        (ANY, ANY, ANY),
+        [
+            pltpu.VMEM((n_band, piece_rows, nu_blk), BF),
+            pltpu.VMEM((rows_all, nu_blk), BF),
+            pltpu.VMEM((nu_blk, rows_all), BF),
+            dma(n_copies),
+            dma(3),
+        ],
+        moved=9 * MIB,
+    )(*flat)
+
+    cfg = (n_ka, n_band, k_dev)
+    quads = k_points // 4
+    state, coef = None, None
     for step in range(STEPS):
         first = step == 0
         qx, rho = call(
-            functools.partial(density_kernel, (n_ka, n_band, k_dev, own, counts)),
+            functools.partial(density_kernel, cfg),
             "density",
-            (shape_of((pairs, LANES, LANES), BF), shape_of((devices, own // LANES, LANES))),
-            [VMEM] + [ANY] * (n_ka + n_copies),
+            (
+                shape_of((quads, 2 * LANES, 2 * LANES), BF),
+                shape_of((devices, own // LANES, LANES)),
+            ),
+            [VMEM] * 2 + [ANY] * n_ka,
             (VMEM, VMEM),
-            [pltpu.VMEM((pairs, LANES, LANES), F32)] + own_scratch + own_sems,
-        )(msgs, *cond_own, *flat)
+            [
+                pltpu.VMEM((quads, 2 * LANES, 2 * LANES), F32),
+                pltpu.VMEM((n_ka, own_rows, own), BF),
+                dma(n_ka),
+            ],
+            mib=8,
+        )(msgs, val_own, *cond_own)
         density = exchange_all(rho)
-        cond_t_dims = (mu_blk, k_points * n_cond)
-        out = call(
-            functools.partial(direct_kernel, first, (n_ka, n_band, k_points, counts), tile, scale),
+        direct = call(
+            functools.partial(direct_kernel, n_ka, tile, scale),
             "direct",
-            (shape_of((pairs, LANES, LANES)),) + ((shape_of(cond_t_dims, BF),) if first else ()),
-            [VMEM] + [ANY] * (2 + n_copies),
-            (VMEM,) + ((ANY,) if first else ()),
-            ([pltpu.VMEM((k_points * n_cond, mu_blk), BF)] if first else [])
-            + [
-                pltpu.VMEM(cond_t_dims, BF),
-                pltpu.VMEM((n_band, piece_rows, nu_blk), BF),
-                pltpu.VMEM((mu_blk, nu_blk), BF),
-                pltpu.VMEM((k_points * n_cond, nu_blk), BF),
-                pltpu.VMEM((mu_blk, nu_blk), BF),
-                pltpu.VMEM((n_band * piece_rows, mu_blk), BF),
-                pltpu.SemaphoreType.DMA((n_ka,)),
-                pltpu.SemaphoreType.DMA((n_copies,)),
-                pltpu.SemaphoreType.DMA((nu_blk // tile,)),
+            shape_of((pairs, LANES, LANES)),
+            [ANY] * 5,
+            VMEM,
+            [
+                pltpu.VMEM((quads, 2 * LANES, 2 * LANES), BF),
+                pltpu.VMEM((conds_all, mu_blk), BF),
+                pltpu.VMEM((nu_blk, mu_blk), BF),
+                pltpu.VMEM((nu_blk, rows_all), BF),
+                pltpu.VMEM((rows_all, nu_blk), BF),
+                pltpu.VMEM((nu_blk, conds_all), BF),
+                pltpu.VMEM((nu_blk, mu_blk), BF),
+                pltpu.VMEM((rows_all, mu_blk), BF),
+                dma(1),
+                dma(n_ka),
+                dma(1),
+                dma(2, nu_blk // tile),
             ],
-            4 * mu_blk * nu_blk * k_points * n_cond,
-            9 * MIB,
-        )(qx, cond_side, screened, *flat)
-        direct = out[0]
-        if first:
-            cond_side = out[1]
+            flops=4 * mu_blk * nu_blk * conds_all,
+            moved=12 * MIB,
+        )(qx, cond_pts, scr_turned, val_turned, val_rows)
         parts = call(
-            functools.partial(exchange_kernel, (n_ka, n_band, k_dev, own, counts), chunk, scale),
+            functools.partial(exchange_kernel, cfg, chunk, scale),
             "exchange",
             msg_shape,
-            [VMEM] * 2 + [ANY] * (1 + n_ka + n_copies),
+            [ANY] * (4 + n_ka),
             VMEM,
-            [pltpu.VMEM((own, npt_all), BF)]
-            + own_scratch
-            + [
+            [
+                pltpu.VMEM((devices, own // LANES, LANES), F32),
+                pltpu.VMEM((pairs, LANES, LANES), F32),
+                pltpu.VMEM((own, npt_all), BF),
+                pltpu.VMEM((n_ka, own_rows, own), BF),
+                pltpu.VMEM((rows_all, own), BF),
                 pltpu.VMEM((pairs, LANES, LANES), F32),
                 pltpu.VMEM((devices,) + block, F32),
-                pltpu.SemaphoreType.DMA((npt_all // chunk,)),
-            ]
-            + own_sems,
-        )(density, direct, coulomb, *cond_own, *flat)
+                dma(npt_all // chunk),
+                dma(n_ka),
+                dma(3),
+            ],
+        )(density, direct, coulomb, val_own, *cond_own)
         recv = exchange_all(parts)
         if first:
             state, coef, message = call(
@@ -500,6 +597,7 @@
                 (shape_of((3,) + block), shape_of((3,)), msg_shape),
                 [VMEM] * 4,
                 (VMEM, SMEM, VMEM),
+                mib=8,
             )(recv, msgs, gap, start_own)
         else:
             state, coef, message = call(
@@ -508,6 +606,7 @@
                 (shape_of((2,) + block), shape_of((4,)), shape_of((devices, 2, LANES))),
                 [VMEM] * 4 + [SMEM],
                 (VMEM, SMEM, VMEM),
+                mib=8,
             )(recv, msgs, gap, state, coef)
         msgs = exchange_all(message)
     return call(
@@ -516,6 +615,7 @@
         (shape_of(start_vec.shape), shape_of((2 * STEPS,))),
         [VMEM] * 2 + [SMEM],
         (VMEM, SMEM),
+        mib=8,
     )(msgs, state, coef)
 
 
@@ -607,7 +707,7 @@
         and start_vec.shape[0] % 2 == 1
         and val_orb.shape[1] == ROWS
         and cond_orb.shape[1] == HALF
-        and start_vec.shape[0] * n_ka % 2 == 0
+        and start_vec.shape[0] * n_ka % 4 == 0
         and coulomb.shape[0] % LANES == 0
         and coulomb.shape[1] % 1024 == 0
         and screened.shape[0] % 256 == 0

time: 193 us -> 184 us (0.953)
  Pallas kernels: 58.4 us -> 52.3 us
  blocking collectives: 50 us -> 46.8 us
  local copies, waits for them, and re-layouts: 7.76 us -> 10.3 us
  starting transfers between devices: 34.7 us -> 32.4 us
    ppermute x15, starting transfers between devices: 21.2 us -> 17.4 us  [swap(): lax.ppermute(block, axis, [(i, i ^ d) for i in range(lax.axis_size(axis))])]
    pallas_call x6 -> x9, Pallas kernels: 51.3 us -> 47.9 us  [the longest x2 27.2 us: kernel_path(): call(functools.partial(direct_kernel, n_ka, tile, scale), 'direct', shape...]
    slice x2, local copies, waits for them, and re-layouts: 0.03 us -> 3.26 us  [plane_pieces(): diag = [move(by_x[:half], 4), move(by_y[half:], 2)]]
    all_to_all x4, blocking collectives: 50 us -> 46.8 us  [exchange_all(): return lax.all_to_all(parts, AXES, split_axis=0, concat_axis=0, tiled=True)]
  transfers between devices with their start and end apart: 19 -> 19, of which waited for: 7 -> 5; matrix products, arithmetic and copies ran while one was open for 2% -> 3% of each run, Pallas kernels for 21% -> 21%
where the time goes in v4:
time: 184 us; the launch traced here: 183 us
  Pallas kernels  52.3 us (28%)
  blocking collectives  46.8 us (25%)
  starting transfers between devices  32.4 us (18%)
  waiting for transfers between devices  26 us (14%)
  between operations  14.5 us (8%)
  local copies, waits for them, and re-layouts  10.3 us (6%)
    all_to_all x4, blocking collectives, exchange_all(): return lax.all_to_all(parts, AXES, split_axis=0, concat_axis=0, tiled=True)  46.8 us
    pallas_call x2, Pallas kernels, kernel_path(): call(functools.partial(direct_kernel, n_ka, tile, scale), 'direct', shape...  27.2 us
    ppermute x15, waiting for transfers between devices, swap(): lax.ppermute(block, axis, [(i, i ^ d) for i in range(lax.axis_size(axis))])  18.3 us
    ppermute x15, starting transfers between devices, swap(): lax.ppermute(block, axis, [(i, i ^ d) for i in range(lax.axis_size(axis))])  17.4 us
    all_to_all x3, starting transfers between devices, exchange_all(): return lax.all_to_all(parts, AXES, split_axis=0, concat_axis=0, tiled=True)  15 us
    pallas_call x2, Pallas kernels, kernel_path(): call(functools.partial(exchange_kernel, cfg, chunk, scale), 'exchange', m...  8.25 us
    all_to_all x3, waiting for transfers between devices, exchange_all(): return lax.all_to_all(parts, AXES, split_axis=0, concat_axis=0, tiled=True)  7.63 us
    pallas_call x1, Pallas kernels, kernel_path(): call(functools.partial(order_kernel, counts), 'order', (shape_of((rows_al...  5.47 us
  transfers between devices with their start and end apart: 19, of which 5 were waited for; matrix products, arithmetic and copies ran while one was open for 3% of the time, Pallas kernels for 21%

profile of v4, /device:TPU:0, one launch (start us, length us, event | category | flops | bytes accessed | tf_op | source)
XLA Modules:
  0.0 183.2 jit_solution(127240657409852479)
XLA Ops:
  7.3 1.9 %constant_dynamic-slice_fusion = bf16[3,64,1024]{2,1,0:T(8,128)(2,1)} fusion(bf16[3,64,8192]{2,1,0:T(8,128)(2,1)} %cond_ref.1, s32[]{:T(128)S(6)} %select_n.19), kind=kLoop, calls=%fused_computation.6 | loop fusion | bytes 786436 | tf_op jit(solution)/shard_map/dynamic_slice | solution.py:459
  9.2 1.1 dynamic-slice_bitcast_fusion.3
  10.3 3.1 %collective-permute-start = (bf16[24,2048]{1,0:T(8,128)(2,1)S(1)}, bf16[24,2048]{1,0:T(8,128)(2,1)S(1)}, u32[]{:S(2)}, u32[]{:S(2)}) collective-permute-start(bf16[24,2048]{1,0:T(8,128)(2,1)S(1)} %get-tuple-element.41), channel_id=1, source_target_pairs={{0,8},{8,0},{16,24},{24,16},{1,9},{9,1},{17,25},{25,17},{2,10},{10... | collective-permute-start | bytes 294920 | tf_op jit(solution)/shard_map/ppermute | solution.py:428
  13.4 2.5 %collective-permute-start.2 = (bf16[24,2048]{1,0:T(8,128)(2,1)S(1)}, bf16[24,2048]{1,0:T(8,128)(2,1)S(1)}, u32[]{:S(2)}, u32[]{:S(2)}) collective-permute-start(bf16[24,2048]{1,0:T(8,128)(2,1)S(1)} %get-tuple-element.42), channel_id=1, source_target_pairs={{0,24},{8,16},{16,8},{24,0},{1,25},{9,17},{17,9},{25,1},{2,26},{10... | collective-permute-start | bytes 294920 | tf_op jit(solution)/shard_map/ppermute | solution.py:428
  15.9 0.1 collective-permute-start.1
  16.0 0.2 collective-permute-done
  16.2 5.4 %collective-permute-done.2 = bf16[24,2048]{1,0:T(8,128)(2,1)S(1)} collective-permute-done((bf16[24,2048]{1,0:T(8,128)(2,1)S(1)}, bf16[24,2048]{1,0:T(8,128)(2,1)S(1)}, u32[]{:S(2)}, u32[]{:S(2)}) %collective-permute-start.2) | collective-permute-done | bytes 98336 | tf_op jit(solution)/shard_map/ppermute | solution.py:428
  21.6 7.0 %collective-permute-done.1 = bf16[24,2048]{1,0:T(8,128)(2,1)S(1)} collective-permute-done((bf16[24,2048]{1,0:T(8,128)(2,1)S(1)}, bf16[24,2048]{1,0:T(8,128)(2,1)S(1)}, u32[]{:S(2)}, u32[]{:S(2)}) %collective-permute-start.1) | collective-permute-done | bytes 98336 | tf_op jit(solution)/shard_map/ppermute | solution.py:428
  28.5 0.8 pad_maximum_fusion.refs_0_
  29.3 1.6 collective-permute-start.6
  30.9 1.5 collective-permute-start.4
  32.4 5.7 %collective-permute-done.6.refs_4_ = bf16[96,2048]{1,0:T(8,128)(2,1)} collective-permute-done((bf16[96,2048]{1,0:T(8,128)(2,1)}, bf16[96,2048]{1,0:T(8,128)(2,1)}, u32[]{:S(2)}, u32[]{:S(2)}) %collective-permute-start.6) | collective-permute-done | bytes 393248 | tf_op jit(solution)/shard_map/ppermute | solution.py:428
  38.1 1.6 slice.9
  39.7 1.5 collective-permute-start.9
  41.3 1.7 slice.8
  42.9 1.6 collective-permute-start.8
  44.5 0.5 collective-permute-start.5
  45.3 0.9 pack.1
  46.2 9.6 %all-to-all-start = ((bf16[32,16,128]{2,1,0:T(8,128)(2,1)}), bf16[32,16,128]{2,1,0:T(8,128)(2,1)S(1)}, u32[]{:S(2)}, u32[]{:S(2)}) async-start(bf16[32,16,128]{2,1,0:T(8,128)(2,1)} %get-tuple-element.21), calls=%async_computation | async-start | bytes 262144 | tf_op jit(solution)/shard_map/all_to_all | solution.py:30
  55.8 0.3 collective-permute-start.11
  56.1 0.3 collective-permute-start.10
  56.4 7.6 %all-to-all-done.msgs_ref.refs_0_ = bf16[32,16,128]{2,1,0:T(8,128)(2,1)S(1)} async-done(((bf16[32,16,128]{2,1,0:T(8,128)(2,1)}), bf16[32,16,128]{2,1,0:T(8,128)(2,1)S(1)}, u32[]{:S(2)}, u32[]{:S(2)}) %all-to-all-start) | async-done | bytes 131104 | tf_op jit(solution)/shard_map/all_to_all | solution.py:30
  64.0 0.2 cut.1
  64.3 0.7 collective-permute-start.12
  65.0 1.2 collective-permute-start.13
  66.2 2.5 %collective-permute-start.14 = (bf16[192,256]{1,0:T(8,128)(2,1)S(1)}, bf16[192,256]{1,0:T(8,128)(2,1)S(1)}, u32[]{:S(2)}, u32[]{:S(2)}) collective-permute-start(bf16[192,256]{1,0:T(8,128)(2,1)S(1)} %get-tuple-element.26), channel_id=1, source_target_pairs={{0,24},{8,16},{16,8},{24,0},{1,25},{9,17},{17,9},{25,1},{2,26},{10... | collective-permute-start | bytes 294920 | tf_op jit(solution)/shard_map/ppermute | solution.py:428
  68.7 3.7 %turn.1.refs_2_ = bf16[2048,1024]{1,0:T(8,128)(2,1)} custom-call(bf16[1024,2048]{1,0:T(8,128)(2,1)} %scr_ref.1), custom_call_target="tpu_custom_call" | custom-call | bytes 8388608 | tf_op jit(solution)/shard_map/turn/pallas_call | solution.py:498
  72.4 5.5 %order.1 = (bf16[768,2048]{1,0:T(8,128)(2,1)}, bf16[2048,768]{1,0:T(8,128)(2,1)}, bf16[768,256]{1,0:T(8,128)(2,1)}) custom-call(bf16[96,2048]{1,0:T(8,128)(2,1)} %pad_maximum_fusion.refs_0_, bf16[96,2048]{1,0:T(8,128)(2,1)} %collective-permute-done.3.refs_1_, bf16[96,2048]{1,0:T(8,128)(2,1)} %collective-permute-done.4.refs_2_, ...), custom_call_target="tpu_custom_call" | custom-call | bytes 9437184 | tf_op jit(solution)/shard_map/order/pallas_call | solution.py:508
  78.0 1.1 copy-done
  79.0 1.6 density.2
  80.6 0.7 copy-done.12
  81.4 2.7 %all-to-all-start.1 = ((f32[32,2,128]{2,1,0:T(2,128)}), f32[32,2,128]{2,1,0:T(2,128)S(1)}, u32[]{:S(2)}, u32[]{:S(2)}) async-start(f32[32,2,128]{2,1,0:T(2,128)} %get-tuple-element.27), calls=%async_computation.1 | async-start | bytes 65536 | tf_op jit(solution)/shard_map/all_to_all | solution.py:30
  84.1 13.6 %direct.2.refs_1_ = f32[6,128,128]{2,1,0:T(8,128)} custom-call(bf16[3,256,256]{2,1,0:T(8,128)(2,1)} %copy-done.12, bf16[768,1024]{1,0:T(8,128)(2,1)} %all-gather.2.cloned.1.call-done.refs_1_, bf16[2048,1024]{1,0:T(8,128)(2,1)} %turn.1.refs_2_, bf16[2048,768]{1,0:T(8,128)(2,1)} %get-tuple-element.29.refs_3_, bf16[768,2048]{1,0:T(8,128)(2,1)} %get-tuple-element.30.refs_4_), custom_call_target="tpu_custom_call" | custom-call | flops 6442450944 | bytes 12582912 | tf_op jit(solution)/shard_map/direct/pallas_call | solution.py:550
  97.8 0.6 copy-done.16
  98.4 4.2 %exchange.2 = bf16[32,16,128]{2,1,0:T(8,128)(2,1)} custom-call(f32[32,2,128]{2,1,0:T(2,128)} %copy-done.16, f32[6,128,128]{2,1,0:T(8,128)} %direct.2.refs_1_, bf16[256,8192]{1,0:T(8,128)(2,1)} %refs_2_.3, bf16[768,256]{1,0:T(8,128)(2,1)} %get-tuple-element.22.refs_1_.refs_3_, bf16[192,256]{1,0:T(8,128)(2,1)} %copy-done.3, bf16[192,256]{1,0:T(8,128)(2,1)} %copy-done.5, ...), custom_call_target="tpu_custom_call" | custom-call | tf_op jit(solution)/shard_map/exchange/pallas_call | solution.py:573
  102.5 13.9 %all_to_all.35.recv_ref = bf16[32,16,128]{2,1,0:T(8,128)(2,1)S(1)} all-to-all(bf16[32,16,128]{2,1,0:T(8,128)(2,1)} %exchange.2), channel_id=1, replica_groups=mesh['ka'=4,'band'=8] {'ka','band'}, dimensions={0} | all-to-all | bytes 262144 | tf_op jit(solution)/shard_map/all_to_all | solution.py:30
  116.4 0.8 first_owner.1
  117.3 10.0 %all_to_all.36.refs_0_.msgs_ref = bf16[32,16,128]{2,1,0:T(8,128)(2,1)S(1)} all-to-all(bf16[32,16,128]{2,1,0:T(8,128)(2,1)S(1)} %get-tuple-element.32), channel_id=1, replica_groups=mesh['ka'=4,'band'=8] {'ka','band'}, dimensions={0} | all-to-all | bytes 262144 | tf_op jit(solution)/shard_map/all_to_all | solution.py:30
  127.3 1.6 density.3
  128.9 0.7 copy-done.13
  129.7 2.7 %all-to-all-start.4 = ((f32[32,2,128]{2,1,0:T(2,128)}), f32[32,2,128]{2,1,0:T(2,128)S(1)}, u32[]{:S(2)}, u32[]{:S(2)}) async-start(f32[32,2,128]{2,1,0:T(2,128)} %get-tuple-element.33), calls=%async_computation.4 | async-start | bytes 65536 | tf_op jit(solution)/shard_map/all_to_all | solution.py:30
  132.4 13.6 %direct.3.refs_1_ = f32[6,128,128]{2,1,0:T(8,128)} custom-call(bf16[3,256,256]{2,1,0:T(8,128)(2,1)} %copy-done.13, bf16[768,1024]{1,0:T(8,128)(2,1)} %all-gather.2.cloned.1.call-done.refs_1_, bf16[2048,1024]{1,0:T(8,128)(2,1)} %turn.1.refs_2_, bf16[2048,768]{1,0:T(8,128)(2,1)} %get-tuple-element.29.refs_3_, bf16[768,2048]{1,0:T(8,128)(2,1)} %get-tuple-element.30.refs_4_), custom_call_target="tpu_custom_call" | custom-call | flops 6442450944 | bytes 12582912 | tf_op jit(solution)/shard_map/direct/pallas_call | solution.py:550
  146.0 0.6 copy-done.15
  146.6 4.1 %exchange.3 = bf16[32,16,128]{2,1,0:T(8,128)(2,1)} custom-call(f32[32,2,128]{2,1,0:T(2,128)} %copy-done.15, f32[6,128,128]{2,1,0:T(8,128)} %direct.3.refs_1_, bf16[256,8192]{1,0:T(8,128)(2,1)} %refs_2_.3, bf16[768,256]{1,0:T(8,128)(2,1)} %get-tuple-element.22.refs_1_.refs_3_, bf16[192,256]{1,0:T(8,128)(2,1)} %copy-done.3, bf16[192,256]{1,0:T(8,128)(2,1)} %copy-done.5, ...), custom_call_target="tpu_custom_call" | custom-call | tf_op jit(solution)/shard_map/exchange/pallas_call | solution.py:573
  150.7 13.9 %all_to_all.37.recv_ref = bf16[32,16,128]{2,1,0:T(8,128)(2,1)S(1)} all-to-all(bf16[32,16,128]{2,1,0:T(8,128)(2,1)} %exchange.3), channel_id=1, replica_groups=mesh['ka'=4,'band'=8] {'ka','band'}, dimensions={0} | all-to-all | bytes 262144 | tf_op jit(solution)/shard_map/all_to_all | solution.py:30
  164.6 1.3 second_owner.1
  165.9 9.0 %all_to_all.38.msgs_ref = f32[32,2,128]{2,1,0:T(2,128)S(1)} all-to-all(f32[32,2,128]{2,1,0:T(2,128)S(1)} %get-tuple-element.37), channel_id=1, replica_groups=mesh['ka'=4,'band'=8] {'ka','band'}, dimensions={0} | all-to-all | bytes 65536 | tf_op jit(solution)/shard_map/all_to_all | solution.py:30
  175.0 1.3 finish.1
  (57 shorter events, 0.5 us)
Async XLA Ops:
  7.2 56.9 %copy-start.2 = (bf16[3,64,8192]{2,1,0:T(8,128)(2,1)S(1)}, bf16[3,64,8192]{2,1,0:T(8,128)(2,1)}, u32[]{:S(2)}) copy-start(bf16[3,64,8192]{2,1,0:T(8,128)(2,1)} %cond_ref.1) | copy-start | bytes 9437188
  7.2 37.8 %copy-start.18 = (f32[3,64]{1,0:T(4,128)S(1)}, f32[3,64]{1,0:T(4,128)}, u32[]{:S(2)}) copy-start(f32[3,64]{1,0:T(4,128)} %param.9) | copy-start | bytes 2308
  7.2 37.8 %copy-start.17 = (f32[3,8]{1,0:T(4,128)S(1)}, f32[3,8]{1,0:T(4,128)}, u32[]{:S(2)}) copy-start(f32[3,8]{1,0:T(4,128)} %param.8) | copy-start | bytes 292
  7.2 38.1 %copy-start.11 = (f32[3,512]{1,0:T(4,128)S(1)}, f32[3,512]{1,0:T(4,128)}, u32[]{:S(2)}) copy-start(f32[3,512]{1,0:T(4,128)} %start_ref.1) | copy-start | bytes 18436
  7.2 76.9 %all-gather.2.cloned.1.call-start = ((), (), s32[]{:S(2)}) async-start(), calls=%async_computation.7 | async-start | bytes 1966080 | tf_op jit(solution)/shard_map/all_gather | solution.py:460
  10.3 5.9 %collective-permute-start = (bf16[24,2048]{1,0:T(8,128)(2,1)S(1)}, bf16[24,2048]{1,0:T(8,128)(2,1)S(1)}, u32[]{:S(2)}, u32[]{:S(2)}) collective-permute-start(bf16[24,2048]{1,0:T(8,128)(2,1)S(1)} %get-tuple-element.41), channel_id=1, source_target_pairs={{0,8},{8,0},{16,24},{24,16},{1,9},{9,1},{17,25},{25,17},{2,10},{10... | collective-permute-start | bytes 294920 | tf_op jit(solution)/shard_map/ppermute | solution.py:428
  13.4 8.2 %collective-permute-start.2 = (bf16[24,2048]{1,0:T(8,128)(2,1)S(1)}, bf16[24,2048]{1,0:T(8,128)(2,1)S(1)}, u32[]{:S(2)}, u32[]{:S(2)}) collective-permute-start(bf16[24,2048]{1,0:T(8,128)(2,1)S(1)} %get-tuple-element.42), channel_id=1, source_target_pairs={{0,24},{8,16},{16,8},{24,0},{1,25},{9,17},{17,9},{25,1},{2,26},{10... | collective-permute-start | bytes 294920 | tf_op jit(solution)/shard_map/ppermute | solution.py:428
  15.9 12.6 %collective-permute-start.1 = (bf16[24,2048]{1,0:T(8,128)(2,1)S(1)}, bf16[24,2048]{1,0:T(8,128)(2,1)S(1)}, u32[]{:S(2)}, u32[]{:S(2)}) collective-permute-start(bf16[24,2048]{1,0:T(8,128)(2,1)S(1)} %get-tuple-element.43), channel_id=1, source_target_pairs={{0,16},{8,24},{16,0},{24,8},{1,17},{9,25},{17,1},{25,9},{2,18},{10... | collective-permute-start | bytes 294920 | tf_op jit(solution)/shard_map/ppermute | solution.py:428
  29.3 8.8 %collective-permute-start.6 = (bf16[96,2048]{1,0:T(8,128)(2,1)}, bf16[96,2048]{1,0:T(8,128)(2,1)}, u32[]{:S(2)}, u32[]{:S(2)}) collective-permute-start(bf16[96,2048]{1,0:T(8,128)(2,1)} %pad_maximum_fusion.refs_0_), channel_id=1, source_target_pairs={{0,4},{1,5},{2,6},{3,7},{4,0},{5,1},{6,2},{7,3},{8,12},{9,13},{10,... | collective-permute-start | bytes 1179656 | tf_op jit(solution)/shard_map/ppermute | solution.py:428
  30.9 10.4 %collective-permute-start.4 = (bf16[96,2048]{1,0:T(8,128)(2,1)}, bf16[96,2048]{1,0:T(8,128)(2,1)}, u32[]{:S(2)}, u32[]{:S(2)}) collective-permute-start(bf16[96,2048]{1,0:T(8,128)(2,1)} %pad_maximum_fusion.refs_0_), channel_id=1, source_target_pairs={{0,2},{1,3},{2,0},{3,1},{4,6},{5,7},{6,4},{7,5},{8,10},{9,11},{10,... | collective-permute-start | bytes 1179656 | tf_op jit(solution)/shard_map/ppermute | solution.py:428
  32.4 31.9 %collective-permute-start.3 = (bf16[96,2048]{1,0:T(8,128)(2,1)}, bf16[96,2048]{1,0:T(8,128)(2,1)}, u32[]{:S(2)}, u32[]{:S(2)}) collective-permute-start(bf16[96,2048]{1,0:T(8,128)(2,1)} %pad_maximum_fusion.refs_0_), channel_id=1, source_target_pairs={{0,1},{1,0},{2,3},{3,2},{4,5},{5,4},{6,7},{7,6},{8,9},{9,8},{10,11... | collective-permute-start | bytes 1179656 | tf_op jit(solution)/shard_map/ppermute | solution.py:428
  39.7 16.1 %collective-permute-start.9 = (bf16[48,2048]{1,0:T(8,128)(2,1)}, bf16[48,2048]{1,0:T(8,128)(2,1)S(1)}, u32[]{:S(2)}, u32[]{:S(2)}) collective-permute-start(bf16[48,2048]{1,0:T(8,128)(2,1)} %slice.9), channel_id=1, source_target_pairs={{0,2},{1,3},{2,0},{3,1},{4,6},{5,7},{6,4},{7,5},{8,10},{9,11},{10,... | collective-permute-start | bytes 589832 | tf_op jit(solution)/shard_map/ppermute | solution.py:428
  42.9 13.2 %collective-permute-start.8 = (bf16[48,2048]{1,0:T(8,128)(2,1)}, bf16[48,2048]{1,0:T(8,128)(2,1)}, u32[]{:S(2)}, u32[]{:S(2)}) collective-permute-start(bf16[48,2048]{1,0:T(8,128)(2,1)} %slice.8), channel_id=1, source_target_pairs={{0,4},{1,5},{2,6},{3,7},{4,0},{5,1},{6,2},{7,3},{8,12},{9,13},{10,... | collective-permute-start | bytes 589832 | tf_op jit(solution)/shard_map/ppermute | solution.py:428
  44.5 21.8 %collective-permute-start.7 = (bf16[96,2048]{1,0:T(8,128)(2,1)}, bf16[96,2048]{1,0:T(8,128)(2,1)}, u32[]{:S(2)}, u32[]{:S(2)}) collective-permute-start(bf16[96,2048]{1,0:T(8,128)(2,1)} %collective-permute-done.6.refs_4_), channel_id=1, source_target_pairs={{0,1},{1,0},{2,3},{3,2},{4,5},{5,4},{6,7},{7,6},{8,9},{9,8},{10,11... | collective-permute-start | bytes 1179656 | tf_op jit(solution)/shard_map/ppermute | solution.py:428
  44.5 28.0 %collective-permute-start.5 = (bf16[96,2048]{1,0:T(8,128)(2,1)}, bf16[96,2048]{1,0:T(8,128)(2,1)}, u32[]{:S(2)}, u32[]{:S(2)}) collective-permute-start(bf16[96,2048]{1,0:T(8,128)(2,1)} %collective-permute-done.4.refs_2_), channel_id=1, source_target_pairs={{0,1},{1,0},{2,3},{3,2},{4,5},{5,4},{6,7},{7,6},{8,9},{9,8},{10,11... | collective-permute-start | bytes 1179656 | tf_op jit(solution)/shard_map/ppermute | solution.py:428
  46.2 17.8 %all-to-all-start = ((bf16[32,16,128]{2,1,0:T(8,128)(2,1)}), bf16[32,16,128]{2,1,0:T(8,128)(2,1)S(1)}, u32[]{:S(2)}, u32[]{:S(2)}) async-start(bf16[32,16,128]{2,1,0:T(8,128)(2,1)} %get-tuple-element.21), calls=%async_computation | async-start | bytes 262144 | tf_op jit(solution)/shard_map/all_to_all | solution.py:30
  55.8 16.6 %copy-start.14 = (bf16[48,2048]{1,0:T(8,128)(2,1)}, bf16[48,2048]{1,0:T(8,128)(2,1)S(1)}, u32[]{:S(2)}) copy-start(bf16[48,2048]{1,0:T(8,128)(2,1)S(1)} %collective-permute-done.9.refs_7_) | copy-start | bytes 589828
  55.8 9.2 %collective-permute-start.11 = (bf16[48,2048]{1,0:T(8,128)(2,1)S(1)}, bf16[48,2048]{1,0:T(8,128)(2,1)}, u32[]{:S(2)}, u32[]{:S(2)}) collective-permute-start(bf16[48,2048]{1,0:T(8,128)(2,1)S(1)} %collective-permute-done.9.refs_7_), channel_id=1, source_target_pairs={{0,1},{1,0},{2,3},{3,2},{4,5},{5,4},{6,7},{7,6},{8,9},{9,8},{10,11... | collective-permute-start | bytes 589832 | tf_op jit(solution)/shard_map/ppermute | solution.py:428
  56.1 16.3 %collective-permute-start.10 = (bf16[48,2048]{1,0:T(8,128)(2,1)}, bf16[48,2048]{1,0:T(8,128)(2,1)}, u32[]{:S(2)}, u32[]{:S(2)}) collective-permute-start(bf16[48,2048]{1,0:T(8,128)(2,1)} %collective-permute-done.8.refs_6_), channel_id=1, source_target_pairs={{0,1},{1,0},{2,3},{3,2},{4,5},{5,4},{6,7},{7,6},{8,9},{9,8},{10,11... | collective-permute-start | bytes 589832 | tf_op jit(solution)/shard_map/ppermute | solution.py:428
  64.2 13.7 %copy-start.3 = (bf16[192,256]{1,0:T(8,128)(2,1)}, bf16[192,256]{1,0:T(8,128)(2,1)S(1)}, u32[]{:S(2)}) copy-start(bf16[192,256]{1,0:T(8,128)(2,1)S(1)} %get-tuple-element.23.refs_2_.refs_4_) | copy-start | bytes 294916
  64.3 13.7 %collective-permute-start.12 = (bf16[192,256]{1,0:T(8,128)(2,1)S(1)}, bf16[192,256]{1,0:T(8,128)(2,1)S(1)}, u32[]{:S(2)}, u32[]{:S(2)}) collective-permute-start(bf16[192,256]{1,0:T(8,128)(2,1)S(1)} %get-tuple-element.24), channel_id=1, source_target_pairs={{0,8},{8,0},{16,24},{24,16},{1,9},{9,1},{17,25},{25,17},{2,10},{10... | collective-permute-start | bytes 294920 | tf_op jit(solution)/shard_map/ppermute | solution.py:428
  65.0 13.0 %collective-permute-start.13 = (bf16[192,256]{1,0:T(8,128)(2,1)S(1)}, bf16[192,256]{1,0:T(8,128)(2,1)S(1)}, u32[]{:S(2)}, u32[]{:S(2)}) collective-permute-start(bf16[192,256]{1,0:T(8,128)(2,1)S(1)} %get-tuple-element.25), channel_id=1, source_target_pairs={{0,16},{8,24},{16,0},{24,8},{1,17},{9,25},{17,1},{25,9},{2,18},{10... | collective-permute-start | bytes 294920 | tf_op jit(solution)/shard_map/ppermute | solution.py:428
  66.2 11.7 %collective-permute-start.14 = (bf16[192,256]{1,0:T(8,128)(2,1)S(1)}, bf16[192,256]{1,0:T(8,128)(2,1)S(1)}, u32[]{:S(2)}, u32[]{:S(2)}) collective-permute-start(bf16[192,256]{1,0:T(8,128)(2,1)S(1)} %get-tuple-element.26), channel_id=1, source_target_pairs={{0,24},{8,16},{16,8},{24,0},{1,25},{9,17},{17,9},{25,1},{2,26},{10... | collective-permute-start | bytes 294920 | tf_op jit(solution)/shard_map/ppermute | solution.py:428
  77.9 19.8 %copy-start.5 = (bf16[192,256]{1,0:T(8,128)(2,1)}, bf16[192,256]{1,0:T(8,128)(2,1)S(1)}, u32[]{:S(2)}) copy-start(bf16[192,256]{1,0:T(8,128)(2,1)S(1)} %collective-permute-done.12.refs_3_.refs_5_) | copy-start | bytes 294916
  77.9 19.8 %copy-start.7 = (bf16[192,256]{1,0:T(8,128)(2,1)}, bf16[192,256]{1,0:T(8,128)(2,1)S(1)}, u32[]{:S(2)}) copy-start(bf16[192,256]{1,0:T(8,128)(2,1)S(1)} %collective-permute-done.13.refs_4_.refs_6_) | copy-start | bytes 294916
  78.0 19.7 %copy-start.9 = (bf16[192,256]{1,0:T(8,128)(2,1)}, bf16[192,256]{1,0:T(8,128)(2,1)S(1)}, u32[]{:S(2)}) copy-start(bf16[192,256]{1,0:T(8,128)(2,1)S(1)} %collective-permute-done.14.refs_5_.refs_7_) | copy-start | bytes 294916
  78.0 1.1 copy-start
  80.6 0.7 copy-start.12
  81.4 16.4 %all-to-all-start.1 = ((f32[32,2,128]{2,1,0:T(2,128)}), f32[32,2,128]{2,1,0:T(2,128)S(1)}, u32[]{:S(2)}, u32[]{:S(2)}) async-start(f32[32,2,128]{2,1,0:T(2,128)} %get-tuple-element.27), calls=%async_computation.1 | async-start | bytes 65536 | tf_op jit(solution)/shard_map/all_to_all | solution.py:30
  97.7 29.6 %copy-start.1 = (bf16[768,256]{1,0:T(8,128)(2,1)S(1)}, bf16[768,256]{1,0:T(8,128)(2,1)}, u32[]{:S(2)}) copy-start(bf16[768,256]{1,0:T(8,128)(2,1)} %get-tuple-element.22.refs_1_.refs_3_) | copy-start | bytes 1179652
  97.7 29.5 %copy-start.4 = (bf16[192,256]{1,0:T(8,128)(2,1)S(1)}, bf16[192,256]{1,0:T(8,128)(2,1)}, u32[]{:S(2)}) copy-start(bf16[192,256]{1,0:T(8,128)(2,1)} %copy-done.3) | copy-start | bytes 294916
  97.7 0.6 copy-start.16
  98.4 28.9 %copy-start.6 = (bf16[192,256]{1,0:T(8,128)(2,1)S(1)}, bf16[192,256]{1,0:T(8,128)(2,1)}, u32[]{:S(2)}) copy-start(bf16[192,256]{1,0:T(8,128)(2,1)} %copy-done.5) | copy-start | bytes 294916
  98.4 28.9 %copy-start.8 = (bf16[192,256]{1,0:T(8,128)(2,1)S(1)}, bf16[192,256]{1,0:T(8,128)(2,1)}, u32[]{:S(2)}) copy-start(bf16[192,256]{1,0:T(8,128)(2,1)} %copy-done.7) | copy-start | bytes 294916
  98.4 28.9 %copy-start.10 = (bf16[192,256]{1,0:T(8,128)(2,1)S(1)}, bf16[192,256]{1,0:T(8,128)(2,1)}, u32[]{:S(2)}) copy-start(bf16[192,256]{1,0:T(8,128)(2,1)} %copy-done.9) | copy-start | bytes 294916
  128.9 0.7 copy-start.13
  129.7 16.3 %all-to-all-start.4 = ((f32[32,2,128]{2,1,0:T(2,128)}), f32[32,2,128]{2,1,0:T(2,128)S(1)}, u32[]{:S(2)}, u32[]{:S(2)}) async-start(f32[32,2,128]{2,1,0:T(2,128)} %get-tuple-element.33), calls=%async_computation.4 | async-start | bytes 65536 | tf_op jit(solution)/shard_map/all_to_all | solution.py:30
  146.0 0.6 copy-start.15
Sparse Core Ops, SparseCore 0:
  9.6 40.8 all-gather.1

commit v5 on v4

--- a/solution.py
+++ b/solution.py
@@ -136,7 +136,7 @@
     msg_ref[...] = jnp.broadcast_to(block.astype(BF)[None], msg_ref.shape)
 
 
-def cut_kernel(cond_ref, msgs_ref, *refs):
+def cut_kernel(cond_ref, after_ref, *refs):
     outs, sems = refs[:-1], refs[-1]
     k_dev, n_cond, npt = cond_ref.shape
     own = outs[0].shape[1]
@@ -181,18 +181,21 @@
     start_all(copies)
     wait_all(copies)
     group = vals.shape[0] * 2 * ROWS
+    column = pl.multiple_of(lax.axis_index("band") * own, LANES)
     outs = []
     for kp in range(ordered.shape[0] // group):
         at = slice(kp * group, (kp + 1) * group)
         ordered[at, :] = pair_rows(vals, kp)
         turned[:, at] = ordered[at, :].T
-    column = pl.multiple_of(lax.axis_index("band") * own, LANES)
-    outs = [
-        pltpu.make_async_copy(ordered, rows_out, out_sems.at[0]),
-        pltpu.make_async_copy(turned, turned_out, out_sems.at[1]),
-        pltpu.make_async_copy(ordered.at[:, pl.ds(column, own)], own_out, out_sems.at[2]),
-    ]
-    start_all(outs)
+        at = pl.ds(kp * group, group)
+        outs += [
+            pltpu.make_async_copy(ordered.at[at, :], rows_out.at[at, :], out_sems.at[0, kp]),
+            pltpu.make_async_copy(turned.at[:, at], turned_out.at[:, at], out_sems.at[1, kp]),
+            pltpu.make_async_copy(
+                ordered.at[at, pl.ds(column, own)], own_out.at[at, :], out_sems.at[2, kp]
+            ),
+        ]
+        start_all(outs[-3:])
     wait_all(outs)
 
 
@@ -321,12 +324,18 @@
                     piece = part[k // 2, pl.ds(d * 2 * ROWS + k % 2 * ROWS, ROWS), :]
                     piece = lane_half(piece, k % 2, kl % 2)
                     tile = piece if tile is None else tile + piece
-                msg[device_at(n_band, j, d), pl.ds(g * ROWS, ROWS), :] = tile
+                to_ka = jnp.bitwise_xor(lax.axis_index("ka"), j)
+                to_band = jnp.bitwise_xor(lax.axis_index("band"), d)
+                msg[to_band, to_ka, pl.ds(g * ROWS, ROWS), :] = tile
     msg_ref[...] = msg[...].astype(BF)
 
 
+def plane_sum_kernel(parts_ref, out_ref):
+    out_ref[...] = jnp.sum(parts_ref[...].astype(F32), axis=0)
+
+
 def received(recv_ref):
-    return jnp.sum(recv_ref[...].astype(F32), axis=0)
+    return jnp.sum(recv_ref[...], axis=0)
 
 
 def shifted(count_all, shift, square, cross_sum, square_sum):
@@ -468,10 +477,6 @@
     val_cut = jnp.concatenate(
         [val_to(0)] + [swap(val_to(j), "ka", j) for j in range(1, n_ka)], axis=0
     )
-    pieces = plane_pieces(val_cut)
-    counts = tuple(len(piece) for piece in pieces)
-    flat = [ref for piece in pieces for ref in piece]
-    n_copies = len(flat)
     gap = (cond_energy[:, None, :] - val_energy[:, :, None]).reshape(k_dev, nv_blk * n_cond)
     gap = pack_vector(gap, k_dev)
 
@@ -481,6 +486,23 @@
         pack_kernel, "pack", (shape_of(block), msg_shape), [VMEM] * 2, (VMEM, VMEM), mib=8
     )(start_vec, gap)
     msgs = exchange_all(message)
+    chunk, tile = 1024, 1024
+    rows_all, conds_all = k_points * nv_blk * n_band, k_points * n_cond
+    scr_turned = call(
+        functools.partial(turn_kernel, tile // 2),
+        "turn",
+        shape_of((nu_blk, mu_blk), BF),
+        [ANY],
+        ANY,
+        [pltpu.VMEM((mu_blk, nu_blk), BF), pltpu.VMEM((nu_blk, mu_blk), BF)]
+        + [dma(2 * nu_blk // tile)] * 2,
+        moved=8 * MIB,
+    )(screened)
+    val_cut, msgs, scr_turned = lax.optimization_barrier((val_cut, msgs, scr_turned))
+    pieces = plane_pieces(val_cut)
+    counts = tuple(len(piece) for piece in pieces)
+    flat = [ref for piece in pieces for ref in piece]
+    n_copies = len(flat)
     own_rows = k_dev * n_cond
     cuts = call(
         cut_kernel,
@@ -490,21 +512,9 @@
         (ANY,) * n_ka,
         [dma(n_ka * k_dev)],
         mib=8,
-    )(cond_orb, msgs)
+    )(cond_orb, val_cut)
     cond_own = [cuts[0]] + [swap(cuts[j], "ka", j) for j in range(1, n_ka)]
 
-    chunk, tile = 1024, 512
-    rows_all, conds_all = k_points * nv_blk * n_band, k_points * n_cond
-    scr_turned = call(
-        functools.partial(turn_kernel, tile),
-        "turn",
-        shape_of((nu_blk, mu_blk), BF),
-        [ANY],
-        ANY,
-        [pltpu.VMEM((mu_blk, nu_blk), BF), pltpu.VMEM((nu_blk, mu_blk), BF)]
-        + [dma(nu_blk // tile)] * 2,
-        moved=8 * MIB,
-    )(screened)
     val_rows, val_turned, val_own = call(
         functools.partial(order_kernel, counts),
         "order",
@@ -520,7 +530,7 @@
             pltpu.VMEM((rows_all, nu_blk), BF),
             pltpu.VMEM((nu_blk, rows_all), BF),
             dma(n_copies),
-            dma(3),
+            dma(3, pairs),
         ],
         moved=9 * MIB,
     )(*flat)
@@ -573,7 +583,7 @@
         parts = call(
             functools.partial(exchange_kernel, cfg, chunk, scale),
             "exchange",
-            msg_shape,
+            shape_of((n_band, n_ka) + block, BF),
             [ANY] * (4 + n_ka),
             VMEM,
             [
@@ -583,13 +593,17 @@
                 pltpu.VMEM((n_ka, own_rows, own), BF),
                 pltpu.VMEM((rows_all, own), BF),
                 pltpu.VMEM((pairs, LANES, LANES), F32),
-                pltpu.VMEM((devices,) + block, F32),
+                pltpu.VMEM((n_band, n_ka) + block, F32),
                 dma(npt_all // chunk),
                 dma(n_ka),
                 dma(3),
             ],
         )(density, direct, coulomb, val_own, *cond_own)
-        recv = exchange_all(parts)
+        parts = lax.all_to_all(parts, "band", split_axis=0, concat_axis=0, tiled=True)
+        plane = call(
+            plane_sum_kernel, "plane_sum", shape_of((n_ka,) + block), [VMEM], VMEM, mib=8
+        )(parts)
+        recv = lax.all_to_all(plane, "ka", split_axis=0, concat_axis=0, tiled=True)
         if first:
             state, coef, message = call(
                 functools.partial(first_owner_kernel, count_all),
@@ -711,7 +725,7 @@
         and coulomb.shape[0] % LANES == 0
         and coulomb.shape[1] % 1024 == 0
         and screened.shape[0] % 256 == 0
-        and screened.shape[1] % 512 == 0
+        and screened.shape[1] % 1024 == 0
         and screened.shape[0] * screened.shape[1] <= 2 * MIB
     )
     return (kernel_path if fits else array_path)(*args)

time: 184 us -> 192 us (1.043)
  blocking collectives: 46.8 us -> 57.7 us
  waiting for transfers between devices: 26 us -> 21.6 us
    all_to_all x0 -> x4, blocking collectives: none -> 38.8 us  [the longest x2 20.3 us: kernel_path(): recv = lax.all_to_all(plane, 'ka', split_axis=0, concat_axis=0, tiled=True)]
    all_to_all x4 -> x2, blocking collectives: 46.8 us -> 18.9 us  [exchange_all(): return lax.all_to_all(parts, AXES, split_axis=0, concat_axis=0, tiled=True)]
    ppermute x15, waiting for transfers between devices: 18.3 us -> 13.6 us  [swap(): lax.ppermute(block, axis, [(i, i ^ d) for i in range(lax.axis_size(axis))])]
    slice x2, local copies, waits for them, and re-layouts: 3.26 us -> 0.03 us  [plane_pieces(): diag = [move(by_x[:half], 4), move(by_y[half:], 2)]]
    unnamed x38 -> x56, local copies, waits for them, and re-layouts: 3.78 us -> 6.51 us
    pallas_call x2, Pallas kernels: 27.2 us -> 25.2 us  [kernel_path(): call(functools.partial(direct_kernel, n_ka, tile, scale), 'direct', shape...]
    pallas_call x3 -> x5, Pallas kernels: 11.9 us -> 12.2 us  [the longest x2 8.27 us: kernel_path(): call(functools.partial(exchange_kernel, cfg, chunk, scale), 'exchange', s...]
  transfers between devices with their start and end apart: 19 -> 19, of which waited for: 5 -> 6; matrix products, arithmetic and copies ran while one was open for 3% -> 2% of each run, Pallas kernels for 21% -> 20%
where the time goes in v5:
time: 192 us; the launch traced here: 191 us
  blocking collectives  57.7 us (30%)
  Pallas kernels  51.9 us (27%)
  starting transfers between devices  33.1 us (17%)
  waiting for transfers between devices  21.6 us (11%)
  between operations  14.5 us (8%)
  local copies, waits for them, and re-layouts  10.3 us (5%)
    pallas_call x2, Pallas kernels, kernel_path(): call(functools.partial(direct_kernel, n_ka, tile, scale), 'direct', shape...  25.2 us
    all_to_all x2, blocking collectives, kernel_path(): recv = lax.all_to_all(plane, 'ka', split_axis=0, concat_axis=0, tiled=True)  20.3 us
    all_to_all x2, blocking collectives, exchange_all(): return lax.all_to_all(parts, AXES, split_axis=0, concat_axis=0, tiled=True)  18.9 us
    ppermute x15, starting transfers between devices, swap(): lax.ppermute(block, axis, [(i, i ^ d) for i in range(lax.axis_size(axis))])  18.8 us
    all_to_all x2, blocking collectives, kernel_path(): lax.all_to_all(parts, 'band', split_axis=0, concat_axis=0, tiled=True)  18.5 us
    all_to_all x3, starting transfers between devices, exchange_all(): return lax.all_to_all(parts, AXES, split_axis=0, concat_axis=0, tiled=True)  14.2 us
    ppermute x15, waiting for transfers between devices, swap(): lax.ppermute(block, axis, [(i, i ^ d) for i in range(lax.axis_size(axis))])  13.6 us
    pallas_call x2, Pallas kernels, kernel_path(): call(functools.partial(exchange_kernel, cfg, chunk, scale), 'exchange', s...  8.27 us
  transfers between devices with their start and end apart: 19, of which 6 were waited for; matrix products, arithmetic and copies ran while one was open for 2% of the time, Pallas kernels for 20%

profile of v5, /device:TPU:0, one launch (start us, length us, event | category | flops | bytes accessed | tf_op | source)
XLA Modules:
  0.0 190.9 jit_solution(17640984664516818122)
XLA Ops:
  7.2 1.8 constant_dynamic-slice_fusion
  9.1 1.7 dynamic-slice_bitcast_fusion.3
  10.8 3.0 %collective-permute-start = (bf16[24,2048]{1,0:T(8,128)(2,1)S(1)}, bf16[24,2048]{1,0:T(8,128)(2,1)}, u32[]{:S(2)}, u32[]{:S(2)}) collective-permute-start(bf16[24,2048]{1,0:T(8,128)(2,1)S(1)} %get-tuple-element.47), channel_id=1, source_target_pairs={{0,8},{8,0},{16,24},{24,16},{1,9},{9,1},{17,25},{25,17},{2,10},{10... | collective-permute-start | bytes 294920 | tf_op jit(solution)/shard_map/ppermute | solution.py:437
  13.8 2.6 %collective-permute-start.1 = (bf16[24,2048]{1,0:T(8,128)(2,1)S(1)}, bf16[24,2048]{1,0:T(8,128)(2,1)}, u32[]{:S(2)}, u32[]{:S(2)}) collective-permute-start(bf16[24,2048]{1,0:T(8,128)(2,1)S(1)} %get-tuple-element.49), channel_id=1, source_target_pairs={{0,16},{8,24},{16,0},{24,8},{1,17},{9,25},{17,1},{25,9},{2,18},{10... | collective-permute-start | bytes 294920 | tf_op jit(solution)/shard_map/ppermute | solution.py:437
  16.4 0.8 broadcast_subtract_fusion
  17.4 0.7 copy-done.12
  18.1 0.9 pack.1
  19.0 6.2 %all-to-all-start = ((bf16[32,16,128]{2,1,0:T(8,128)(2,1)}), bf16[32,16,128]{2,1,0:T(8,128)(2,1)}, u32[]{:S(2)}, u32[]{:S(2)}) async-start(bf16[32,16,128]{2,1,0:T(8,128)(2,1)} %get-tuple-element.24), calls=%async_computation | async-start | bytes 262144 | tf_op jit(solution)/shard_map/all_to_all | solution.py:30
  25.2 3.9 %turn.1.refs_2_ = bf16[2048,1024]{1,0:T(8,128)(2,1)} custom-call(bf16[1024,2048]{1,0:T(8,128)(2,1)} %scr_ref.1), custom_call_target="tpu_custom_call" | custom-call | bytes 8388608 | tf_op jit(solution)/shard_map/turn/pallas_call | solution.py:491
  29.2 0.6 copy-done.27
  29.8 1.0 pad_maximum_fusion.refs_0_.after_ref
  30.8 8.0 %all-to-all-done.refs_0_.msgs_ref = bf16[32,16,128]{2,1,0:T(8,128)(2,1)} async-done(((bf16[32,16,128]{2,1,0:T(8,128)(2,1)}), bf16[32,16,128]{2,1,0:T(8,128)(2,1)}, u32[]{:S(2)}, u32[]{:S(2)}) %all-to-all-start) | async-done | bytes 131104 | tf_op jit(solution)/shard_map/all_to_all | solution.py:30
  38.8 1.3 collective-permute-start.4
  40.1 1.6 collective-permute-start.6
  41.7 8.1 %collective-permute-done.4.refs_2_ = bf16[96,2048]{1,0:T(8,128)(2,1)S(1)} collective-permute-done((bf16[96,2048]{1,0:T(8,128)(2,1)S(1)}, bf16[96,2048]{1,0:T(8,128)(2,1)S(1)}, u32[]{:S(2)}, u32[]{:S(2)}) %collective-permute-start.4) | collective-permute-done | bytes 393248 | tf_op jit(solution)/shard_map/ppermute | solution.py:437
  49.8 1.0 collective-permute-start.8
  51.2 1.1 collective-permute-start.9
  52.3 0.5 collective-permute-start.7
  52.8 3.0 %collective-permute-done.8.refs_6_ = bf16[48,2048]{1,0:T(8,128)(2,1)S(1)} collective-permute-done((bf16[48,2048]{1,0:T(8,128)(2,1)S(1)}, bf16[48,2048]{1,0:T(8,128)(2,1)S(1)}, u32[]{:S(2)}, u32[]{:S(2)}) %collective-permute-start.8) | collective-permute-done | bytes 196640 | tf_op jit(solution)/shard_map/ppermute | solution.py:437
  55.8 1.6 collective-permute-done.9.refs_7_
  57.7 1.4 collective-permute-start.12
  59.1 5.3 %collective-permute-start.13 = (bf16[192,256]{1,0:T(8,128)(2,1)S(1)}, bf16[192,256]{1,0:T(8,128)(2,1)S(1)}, u32[]{:S(2)}, u32[]{:S(2)}) collective-permute-start(bf16[192,256]{1,0:T(8,128)(2,1)S(1)} %get-tuple-element.30), channel_id=1, source_target_pairs={{0,16},{8,24},{16,0},{24,8},{1,17},{9,25},{17,1},{25,9},{2,18},{10... | collective-permute-start | bytes 294920 | tf_op jit(solution)/shard_map/ppermute | solution.py:437
  64.5 0.9 collective-permute-start.14
  65.5 0.7 copy-done.18
  66.2 0.7 copy-done.19
  66.9 5.0 %order.1 = (bf16[768,2048]{1,0:T(8,128)(2,1)}, bf16[2048,768]{1,0:T(8,128)(2,1)}, bf16[768,256]{1,0:T(8,128)(2,1)}) custom-call(bf16[96,2048]{1,0:T(8,128)(2,1)} %copy-done.3, bf16[96,2048]{1,0:T(8,128)(2,1)} %copy-done.17, bf16[96,2048]{1,0:T(8,128)(2,1)} %copy-done.15, bf16[96,2048]{1,0:T(8,128)(2,1)} %copy-done.18, bf16[96,2048]{1,0:T(8,128)(2,1)} %copy-done.16, ...), custom_call_target="tpu_custom_call" | custom-call | bytes 9437184 | tf_op jit(solution)/shard_map/order/pallas_call | solution.py:518
  72.4 1.0 copy-done
  73.4 2.5 %density.2 = (bf16[3,256,256]{2,1,0:T(8,128)(2,1)S(1)}, f32[32,2,128]{2,1,0:T(2,128)}) custom-call(bf16[32,16,128]{2,1,0:T(8,128)(2,1)} %all-to-all-done.refs_0_.msgs_ref, bf16[768,256]{1,0:T(8,128)(2,1)S(1)} %copy-done, bf16[192,256]{1,0:T(8,128)(2,1)S(1)} %get-tuple-element.28.refs_2_.refs_4_, ...), custom_call_target="tpu_custom_call" | custom-call | tf_op jit(solution)/shard_map/density/pallas_call | solution.py:543
  75.9 0.7 copy-done.13
  76.7 5.3 %all-to-all-start.1 = ((f32[32,2,128]{2,1,0:T(2,128)}), f32[32,2,128]{2,1,0:T(2,128)S(1)}, u32[]{:S(2)}, u32[]{:S(2)}) async-start(f32[32,2,128]{2,1,0:T(2,128)} %get-tuple-element.32), calls=%async_computation.1 | async-start | bytes 65536 | tf_op jit(solution)/shard_map/all_to_all | solution.py:30
  82.0 12.6 %direct.2.refs_1_ = f32[6,128,128]{2,1,0:T(8,128)} custom-call(bf16[3,256,256]{2,1,0:T(8,128)(2,1)} %copy-done.13, bf16[768,1024]{1,0:T(8,128)(2,1)} %all-gather.2.cloned.1.call-done.refs_1_, bf16[2048,1024]{1,0:T(8,128)(2,1)} %turn.1.refs_2_, bf16[2048,768]{1,0:T(8,128)(2,1)} %get-tuple-element.35.refs_3_, bf16[768,2048]{1,0:T(8,128)(2,1)} %get-tuple-element.36.refs_4_), custom_call_target="tpu_custom_call" | custom-call | flops 6442450944 | bytes 12582912 | tf_op jit(solution)/shard_map/direct/pallas_call | solution.py:560
  94.6 0.6 copy-done.26
  95.2 4.2 %exchange.2 = bf16[8,4,16,128]{3,2,1,0:T(8,128)(2,1)} custom-call(f32[32,2,128]{2,1,0:T(2,128)} %copy-done.26, f32[6,128,128]{2,1,0:T(8,128)} %direct.2.refs_1_, bf16[256,8192]{1,0:T(8,128)(2,1)} %refs_2_.3, bf16[768,256]{1,0:T(8,128)(2,1)} %get-tuple-element.27.refs_1_.refs_3_, bf16[192,256]{1,0:T(8,128)(2,1)} %copy-done.4, bf16[192,256]{1,0:T(8,128)(2,1)} %copy-done.6, ...), custom_call_target="tpu_custom_call" | custom-call | tf_op jit(solution)/shard_map/exchange/pallas_call | solution.py:583
  99.4 9.3 %all_to_all.45.parts_ref = bf16[8,4,16,128]{3,2,1,0:T(8,128)(2,1)S(1)} all-to-all(bf16[8,4,16,128]{3,2,1,0:T(8,128)(2,1)} %exchange.2), channel_id=1, replica_groups=mesh['ka'=4,'band'=8] {'band'}, dimensions={0} | all-to-all | bytes 262144 | tf_op jit(solution)/shard_map/all_to_all | solution.py:602
  108.7 10.1 %all_to_all.46.recv_ref = f32[4,16,128]{2,1,0:T(8,128)S(1)} all-to-all(f32[4,16,128]{2,1,0:T(8,128)S(1)} %plane_sum.2), channel_id=1, replica_groups=mesh['ka'=4,'band'=8] {'ka'}, dimensions={0} | all-to-all | bytes 65536 | tf_op jit(solution)/shard_map/all_to_all | solution.py:606
  118.8 1.7 first_owner.1
  120.6 9.9 %all_to_all.47.refs_0_.msgs_ref = bf16[32,16,128]{2,1,0:T(8,128)(2,1)S(1)} all-to-all(bf16[32,16,128]{2,1,0:T(8,128)(2,1)S(1)} %get-tuple-element.38), channel_id=1, replica_groups=mesh['ka'=4,'band'=8] {'ka','band'}, dimensions={0} | all-to-all | bytes 262144 | tf_op jit(solution)/shard_map/all_to_all | solution.py:30
  130.5 1.6 density.3
  132.2 0.7 copy-done.14
  132.9 2.8 %all-to-all-start.5 = ((f32[32,2,128]{2,1,0:T(2,128)}), f32[32,2,128]{2,1,0:T(2,128)S(1)}, u32[]{:S(2)}, u32[]{:S(2)}) async-start(f32[32,2,128]{2,1,0:T(2,128)} %get-tuple-element.39), calls=%async_computation.5 | async-start | bytes 65536 | tf_op jit(solution)/shard_map/all_to_all | solution.py:30
  135.7 12.6 %direct.3.refs_1_ = f32[6,128,128]{2,1,0:T(8,128)} custom-call(bf16[3,256,256]{2,1,0:T(8,128)(2,1)} %copy-done.14, bf16[768,1024]{1,0:T(8,128)(2,1)} %all-gather.2.cloned.1.call-done.refs_1_, bf16[2048,1024]{1,0:T(8,128)(2,1)} %turn.1.refs_2_, bf16[2048,768]{1,0:T(8,128)(2,1)} %get-tuple-element.35.refs_3_, bf16[768,2048]{1,0:T(8,128)(2,1)} %get-tuple-element.36.refs_4_), custom_call_target="tpu_custom_call" | custom-call | flops 6442450944 | bytes 12582912 | tf_op jit(solution)/shard_map/direct/pallas_call | solution.py:560
  148.3 0.6 copy-done.25
  148.9 4.1 %exchange.3 = bf16[8,4,16,128]{3,2,1,0:T(8,128)(2,1)} custom-call(f32[32,2,128]{2,1,0:T(2,128)} %copy-done.25, f32[6,128,128]{2,1,0:T(8,128)} %direct.3.refs_1_, bf16[256,8192]{1,0:T(8,128)(2,1)} %refs_2_.3, bf16[768,256]{1,0:T(8,128)(2,1)} %get-tuple-element.27.refs_1_.refs_3_, bf16[192,256]{1,0:T(8,128)(2,1)} %copy-done.4, bf16[192,256]{1,0:T(8,128)(2,1)} %copy-done.6, ...), custom_call_target="tpu_custom_call" | custom-call | tf_op jit(solution)/shard_map/exchange/pallas_call | solution.py:583
  153.0 9.2 %all_to_all.48.parts_ref = bf16[8,4,16,128]{3,2,1,0:T(8,128)(2,1)S(1)} all-to-all(bf16[8,4,16,128]{3,2,1,0:T(8,128)(2,1)} %exchange.3), channel_id=1, replica_groups=mesh['ka'=4,'band'=8] {'band'}, dimensions={0} | all-to-all | bytes 262144 | tf_op jit(solution)/shard_map/all_to_all | solution.py:602
  162.2 10.2 %all_to_all.49.recv_ref = f32[4,16,128]{2,1,0:T(8,128)S(1)} all-to-all(f32[4,16,128]{2,1,0:T(8,128)S(1)} %plane_sum.3), channel_id=1, replica_groups=mesh['ka'=4,'band'=8] {'ka'}, dimensions={0} | all-to-all | bytes 65536 | tf_op jit(solution)/shard_map/all_to_all | solution.py:606
  172.4 1.3 second_owner.1
  173.8 8.9 %all_to_all.50.msgs_ref = f32[32,2,128]{2,1,0:T(2,128)S(1)} all-to-all(f32[32,2,128]{2,1,0:T(2,128)S(1)} %get-tuple-element.43), channel_id=1, replica_groups=mesh['ka'=4,'band'=8] {'ka','band'}, dimensions={0} | all-to-all | bytes 65536 | tf_op jit(solution)/shard_map/all_to_all | solution.py:30
  182.7 1.3 finish.1
  (79 shorter events, 1.6 us)
Async XLA Ops:
  7.2 74.8 %all-gather.2.cloned.1.call-start = ((), (), s32[]{:S(2)}) async-start(), calls=%async_computation.9 | async-start | bytes 1966080 | tf_op jit(solution)/shard_map/all_gather | solution.py:469
  10.8 18.3 %collective-permute-start = (bf16[24,2048]{1,0:T(8,128)(2,1)S(1)}, bf16[24,2048]{1,0:T(8,128)(2,1)}, u32[]{:S(2)}, u32[]{:S(2)}) collective-permute-start(bf16[24,2048]{1,0:T(8,128)(2,1)S(1)} %get-tuple-element.47), channel_id=1, source_target_pairs={{0,8},{8,0},{16,24},{24,16},{1,9},{9,1},{17,25},{25,17},{2,10},{10... | collective-permute-start | bytes 294920 | tf_op jit(solution)/shard_map/ppermute | solution.py:437
  13.8 15.3 %collective-permute-start.1 = (bf16[24,2048]{1,0:T(8,128)(2,1)S(1)}, bf16[24,2048]{1,0:T(8,128)(2,1)}, u32[]{:S(2)}, u32[]{:S(2)}) collective-permute-start(bf16[24,2048]{1,0:T(8,128)(2,1)S(1)} %get-tuple-element.49), channel_id=1, source_target_pairs={{0,16},{8,24},{16,0},{24,8},{1,17},{9,25},{17,1},{25,9},{2,18},{10... | collective-permute-start | bytes 294920 | tf_op jit(solution)/shard_map/ppermute | solution.py:437
  16.4 12.7 %collective-permute-start.2 = (bf16[24,2048]{1,0:T(8,128)(2,1)S(1)}, bf16[24,2048]{1,0:T(8,128)(2,1)S(1)}, u32[]{:S(2)}, u32[]{:S(2)}) collective-permute-start(bf16[24,2048]{1,0:T(8,128)(2,1)S(1)} %get-tuple-element.48), channel_id=1, source_target_pairs={{0,24},{8,16},{16,8},{24,0},{1,25},{9,17},{17,9},{25,1},{2,26},{10... | collective-permute-start | bytes 294920 | tf_op jit(solution)/shard_map/ppermute | solution.py:437
  17.4 0.7 copy-start.12
  19.0 19.8 %all-to-all-start = ((bf16[32,16,128]{2,1,0:T(8,128)(2,1)}), bf16[32,16,128]{2,1,0:T(8,128)(2,1)}, u32[]{:S(2)}, u32[]{:S(2)}) async-start(bf16[32,16,128]{2,1,0:T(8,128)(2,1)} %get-tuple-element.24), calls=%async_computation | async-start | bytes 262144 | tf_op jit(solution)/shard_map/all_to_all | solution.py:30
  25.2 4.6 %copy-start.20 = (bf16[24,2048]{1,0:T(8,128)(2,1)S(1)}, bf16[24,2048]{1,0:T(8,128)(2,1)}, u32[]{:S(2)}) copy-start(bf16[24,2048]{1,0:T(8,128)(2,1)} %get-tuple-element.46) | copy-start | bytes 294916
  25.2 32.2 %copy-start.2 = (bf16[3,64,8192]{2,1,0:T(8,128)(2,1)S(1)}, bf16[3,64,8192]{2,1,0:T(8,128)(2,1)}, u32[]{:S(2)}) copy-start(bf16[3,64,8192]{2,1,0:T(8,128)(2,1)} %cond_ref.1) | copy-start | bytes 9437188
  29.2 0.6 copy-start.27
  30.8 34.6 %copy-start.3 = (bf16[96,2048]{1,0:T(8,128)(2,1)}, bf16[96,2048]{1,0:T(8,128)(2,1)S(1)}, u32[]{:S(2)}) copy-start(bf16[96,2048]{1,0:T(8,128)(2,1)S(1)} %pad_maximum_fusion.refs_0_.after_ref) | copy-start | bytes 1179652
  38.8 11.0 %collective-permute-start.4 = (bf16[96,2048]{1,0:T(8,128)(2,1)S(1)}, bf16[96,2048]{1,0:T(8,128)(2,1)S(1)}, u32[]{:S(2)}, u32[]{:S(2)}) collective-permute-start(bf16[96,2048]{1,0:T(8,128)(2,1)S(1)} %pad_maximum_fusion.refs_0_.after_ref), channel_id=1, source_target_pairs={{0,2},{1,3},{2,0},{3,1},{4,6},{5,7},{6,4},{7,5},{8,10},{9,11},{10,... | collective-permute-start | bytes 1179656 | tf_op jit(solution)/shard_map/ppermute | solution.py:437
  40.1 11.1 %collective-permute-start.6 = (bf16[96,2048]{1,0:T(8,128)(2,1)S(1)}, bf16[96,2048]{1,0:T(8,128)(2,1)S(1)}, u32[]{:S(2)}, u32[]{:S(2)}) collective-permute-start(bf16[96,2048]{1,0:T(8,128)(2,1)S(1)} %pad_maximum_fusion.refs_0_.after_ref), channel_id=1, source_target_pairs={{0,4},{1,5},{2,6},{3,7},{4,0},{5,1},{6,2},{7,3},{8,12},{9,13},{10,... | collective-permute-start | bytes 1179656 | tf_op jit(solution)/shard_map/ppermute | solution.py:437
  41.7 16.0 %collective-permute-start.3 = (bf16[96,2048]{1,0:T(8,128)(2,1)S(1)}, bf16[96,2048]{1,0:T(8,128)(2,1)S(1)}, u32[]{:S(2)}, u32[]{:S(2)}) collective-permute-start(bf16[96,2048]{1,0:T(8,128)(2,1)S(1)} %pad_maximum_fusion.refs_0_.after_ref), channel_id=1, source_target_pairs={{0,1},{1,0},{2,3},{3,2},{4,5},{5,4},{6,7},{7,6},{8,9},{9,8},{10,11... | collective-permute-start | bytes 1179656 | tf_op jit(solution)/shard_map/ppermute | solution.py:437
  49.7 15.7 %copy-start.15 = (bf16[96,2048]{1,0:T(8,128)(2,1)}, bf16[96,2048]{1,0:T(8,128)(2,1)S(1)}, u32[]{:S(2)}) copy-start(bf16[96,2048]{1,0:T(8,128)(2,1)S(1)} %collective-permute-done.4.refs_2_) | copy-start | bytes 1179652
  49.8 6.1 %collective-permute-start.8 = (bf16[48,2048]{1,0:T(8,128)(2,1)S(1)}, bf16[48,2048]{1,0:T(8,128)(2,1)S(1)}, u32[]{:S(2)}, u32[]{:S(2)}) collective-permute-start(bf16[48,2048]{1,0:T(8,128)(2,1)S(1)} %slice.8), channel_id=1, source_target_pairs={{0,4},{1,5},{2,6},{3,7},{4,0},{5,1},{6,2},{7,3},{8,12},{9,13},{10,... | collective-permute-start | bytes 589832 | tf_op jit(solution)/shard_map/ppermute | solution.py:437
  51.2 14.2 %copy-start.16 = (bf16[96,2048]{1,0:T(8,128)(2,1)}, bf16[96,2048]{1,0:T(8,128)(2,1)S(1)}, u32[]{:S(2)}) copy-start(bf16[96,2048]{1,0:T(8,128)(2,1)S(1)} %collective-permute-done.6.refs_4_) | copy-start | bytes 1179652
  51.2 6.2 %collective-permute-start.9 = (bf16[48,2048]{1,0:T(8,128)(2,1)S(1)}, bf16[48,2048]{1,0:T(8,128)(2,1)S(1)}, u32[]{:S(2)}, u32[]{:S(2)}) collective-permute-start(bf16[48,2048]{1,0:T(8,128)(2,1)S(1)} %slice.9), channel_id=1, source_target_pairs={{0,2},{1,3},{2,0},{3,1},{4,6},{5,7},{6,4},{7,5},{8,10},{9,11},{10,... | collective-permute-start | bytes 589832 | tf_op jit(solution)/shard_map/ppermute | solution.py:437
  52.3 13.1 %collective-permute-start.5 = (bf16[96,2048]{1,0:T(8,128)(2,1)S(1)}, bf16[96,2048]{1,0:T(8,128)(2,1)S(1)}, u32[]{:S(2)}, u32[]{:S(2)}) collective-permute-start(bf16[96,2048]{1,0:T(8,128)(2,1)S(1)} %collective-permute-done.4.refs_2_), channel_id=1, source_target_pairs={{0,1},{1,0},{2,3},{3,2},{4,5},{5,4},{6,7},{7,6},{8,9},{9,8},{10,11... | collective-permute-start | bytes 1179656 | tf_op jit(solution)/shard_map/ppermute | solution.py:437
  52.3 13.1 %collective-permute-start.7 = (bf16[96,2048]{1,0:T(8,128)(2,1)S(1)}, bf16[96,2048]{1,0:T(8,128)(2,1)S(1)}, u32[]{:S(2)}, u32[]{:S(2)}) collective-permute-start(bf16[96,2048]{1,0:T(8,128)(2,1)S(1)} %collective-permute-done.6.refs_4_), channel_id=1, source_target_pairs={{0,1},{1,0},{2,3},{3,2},{4,5},{5,4},{6,7},{7,6},{8,9},{9,8},{10,11... | collective-permute-start | bytes 1179656 | tf_op jit(solution)/shard_map/ppermute | solution.py:437
  55.8 9.6 %copy-start.21 = (bf16[48,2048]{1,0:T(8,128)(2,1)}, bf16[48,2048]{1,0:T(8,128)(2,1)S(1)}, u32[]{:S(2)}) copy-start(bf16[48,2048]{1,0:T(8,128)(2,1)S(1)} %collective-permute-done.8.refs_6_) | copy-start | bytes 589828
  55.8 3.3 %collective-permute-start.10 = (bf16[48,2048]{1,0:T(8,128)(2,1)S(1)}, bf16[48,2048]{1,0:T(8,128)(2,1)S(1)}, u32[]{:S(2)}, u32[]{:S(2)}) collective-permute-start(bf16[48,2048]{1,0:T(8,128)(2,1)S(1)} %collective-permute-done.8.refs_6_), channel_id=1, source_target_pairs={{0,1},{1,0},{2,3},{3,2},{4,5},{5,4},{6,7},{7,6},{8,9},{9,8},{10,11... | collective-permute-start | bytes 589832 | tf_op jit(solution)/shard_map/ppermute | solution.py:437
  57.4 8.0 %copy-start.22 = (bf16[48,2048]{1,0:T(8,128)(2,1)}, bf16[48,2048]{1,0:T(8,128)(2,1)S(1)}, u32[]{:S(2)}) copy-start(bf16[48,2048]{1,0:T(8,128)(2,1)S(1)} %collective-permute-done.9.refs_7_) | copy-start | bytes 589828
  57.4 7.0 %collective-permute-start.11 = (bf16[48,2048]{1,0:T(8,128)(2,1)S(1)}, bf16[48,2048]{1,0:T(8,128)(2,1)S(1)}, u32[]{:S(2)}, u32[]{:S(2)}) collective-permute-start(bf16[48,2048]{1,0:T(8,128)(2,1)S(1)} %collective-permute-done.9.refs_7_), channel_id=1, source_target_pairs={{0,1},{1,0},{2,3},{3,2},{4,5},{5,4},{6,7},{7,6},{8,9},{9,8},{10,11... | collective-permute-start | bytes 589832 | tf_op jit(solution)/shard_map/ppermute | solution.py:437
  57.7 18.2 %copy-start.4 = (bf16[192,256]{1,0:T(8,128)(2,1)}, bf16[192,256]{1,0:T(8,128)(2,1)S(1)}, u32[]{:S(2)}) copy-start(bf16[192,256]{1,0:T(8,128)(2,1)S(1)} %get-tuple-element.28.refs_2_.refs_4_) | copy-start | bytes 294916
  57.7 7.8 %copy-start.17 = (bf16[96,2048]{1,0:T(8,128)(2,1)}, bf16[96,2048]{1,0:T(8,128)(2,1)S(1)}, u32[]{:S(2)}) copy-start(bf16[96,2048]{1,0:T(8,128)(2,1)S(1)} %collective-permute-done.3.refs_1_) | copy-start | bytes 1179652
  57.7 14.2 %collective-permute-start.12 = (bf16[192,256]{1,0:T(8,128)(2,1)S(1)}, bf16[192,256]{1,0:T(8,128)(2,1)S(1)}, u32[]{:S(2)}, u32[]{:S(2)}) collective-permute-start(bf16[192,256]{1,0:T(8,128)(2,1)S(1)} %get-tuple-element.29), channel_id=1, source_target_pairs={{0,8},{8,0},{16,24},{24,16},{1,9},{9,1},{17,25},{25,17},{2,10},{10... | collective-permute-start | bytes 294920 | tf_op jit(solution)/shard_map/ppermute | solution.py:437
  59.1 6.3 %copy-start.23 = (bf16[48,2048]{1,0:T(8,128)(2,1)}, bf16[48,2048]{1,0:T(8,128)(2,1)S(1)}, u32[]{:S(2)}) copy-start(bf16[48,2048]{1,0:T(8,128)(2,1)S(1)} %collective-permute-done.10.refs_8_) | copy-start | bytes 589828
  59.1 12.8 %collective-permute-start.13 = (bf16[192,256]{1,0:T(8,128)(2,1)S(1)}, bf16[192,256]{1,0:T(8,128)(2,1)S(1)}, u32[]{:S(2)}, u32[]{:S(2)}) collective-permute-start(bf16[192,256]{1,0:T(8,128)(2,1)S(1)} %get-tuple-element.30), channel_id=1, source_target_pairs={{0,16},{8,24},{16,0},{24,8},{1,17},{9,25},{17,1},{25,9},{2,18},{10... | collective-permute-start | bytes 294920 | tf_op jit(solution)/shard_map/ppermute | solution.py:437
  64.5 0.9 copy-start.24
  64.5 7.9 %collective-permute-start.14 = (bf16[192,256]{1,0:T(8,128)(2,1)S(1)}, bf16[192,256]{1,0:T(8,128)(2,1)S(1)}, u32[]{:S(2)}, u32[]{:S(2)}) collective-permute-start(bf16[192,256]{1,0:T(8,128)(2,1)S(1)} %get-tuple-element.31), channel_id=1, source_target_pairs={{0,24},{8,16},{16,8},{24,0},{1,25},{9,17},{17,9},{25,1},{2,26},{10... | collective-permute-start | bytes 294920 | tf_op jit(solution)/shard_map/ppermute | solution.py:437
  65.4 0.8 copy-start.18
  66.2 0.7 copy-start.19
  71.9 22.7 %copy-start.6 = (bf16[192,256]{1,0:T(8,128)(2,1)}, bf16[192,256]{1,0:T(8,128)(2,1)S(1)}, u32[]{:S(2)}) copy-start(bf16[192,256]{1,0:T(8,128)(2,1)S(1)} %collective-permute-done.12.refs_3_.refs_5_) | copy-start | bytes 294916
  71.9 22.7 %copy-start.8 = (bf16[192,256]{1,0:T(8,128)(2,1)}, bf16[192,256]{1,0:T(8,128)(2,1)S(1)}, u32[]{:S(2)}) copy-start(bf16[192,256]{1,0:T(8,128)(2,1)S(1)} %collective-permute-done.13.refs_4_.refs_6_) | copy-start | bytes 294916
  72.4 22.2 %copy-start.10 = (bf16[192,256]{1,0:T(8,128)(2,1)}, bf16[192,256]{1,0:T(8,128)(2,1)S(1)}, u32[]{:S(2)}) copy-start(bf16[192,256]{1,0:T(8,128)(2,1)S(1)} %collective-permute-done.14.refs_5_.refs_7_) | copy-start | bytes 294916
  72.4 1.0 copy-start
  75.9 0.7 copy-start.13
  76.7 18.0 %all-to-all-start.1 = ((f32[32,2,128]{2,1,0:T(2,128)}), f32[32,2,128]{2,1,0:T(2,128)S(1)}, u32[]{:S(2)}, u32[]{:S(2)}) async-start(f32[32,2,128]{2,1,0:T(2,128)} %get-tuple-element.32), calls=%async_computation.1 | async-start | bytes 65536 | tf_op jit(solution)/shard_map/all_to_all | solution.py:30
  94.6 35.9 %copy-start.1 = (bf16[768,256]{1,0:T(8,128)(2,1)S(1)}, bf16[768,256]{1,0:T(8,128)(2,1)}, u32[]{:S(2)}) copy-start(bf16[768,256]{1,0:T(8,128)(2,1)} %get-tuple-element.27.refs_1_.refs_3_) | copy-start | bytes 1179652
  94.6 35.9 %copy-start.5 = (bf16[192,256]{1,0:T(8,128)(2,1)S(1)}, bf16[192,256]{1,0:T(8,128)(2,1)}, u32[]{:S(2)}) copy-start(bf16[192,256]{1,0:T(8,128)(2,1)} %copy-done.4) | copy-start | bytes 294916
  94.6 0.6 copy-start.26
  95.2 35.3 %copy-start.7 = (bf16[192,256]{1,0:T(8,128)(2,1)S(1)}, bf16[192,256]{1,0:T(8,128)(2,1)}, u32[]{:S(2)}) copy-start(bf16[192,256]{1,0:T(8,128)(2,1)} %copy-done.6) | copy-start | bytes 294916
  95.2 35.3 %copy-start.9 = (bf16[192,256]{1,0:T(8,128)(2,1)S(1)}, bf16[192,256]{1,0:T(8,128)(2,1)}, u32[]{:S(2)}) copy-start(bf16[192,256]{1,0:T(8,128)(2,1)} %copy-done.8) | copy-start | bytes 294916
  95.2 35.3 %copy-start.11 = (bf16[192,256]{1,0:T(8,128)(2,1)S(1)}, bf16[192,256]{1,0:T(8,128)(2,1)}, u32[]{:S(2)}) copy-start(bf16[192,256]{1,0:T(8,128)(2,1)} %copy-done.10) | copy-start | bytes 294916
  132.2 0.7 copy-start.14
  132.9 15.4 %all-to-all-start.5 = ((f32[32,2,128]{2,1,0:T(2,128)}), f32[32,2,128]{2,1,0:T(2,128)S(1)}, u32[]{:S(2)}, u32[]{:S(2)}) async-start(f32[32,2,128]{2,1,0:T(2,128)} %get-tuple-element.39), calls=%async_computation.5 | async-start | bytes 65536 | tf_op jit(solution)/shard_map/all_to_all | solution.py:30
  148.3 0.6 copy-start.25
Sparse Core Ops, SparseCore 0:
  9.6 44.2 all-gather.1

commit v6 on v5

--- a/solution.py
+++ b/solution.py
@@ -136,7 +136,7 @@
     msg_ref[...] = jnp.broadcast_to(block.astype(BF)[None], msg_ref.shape)
 
 
-def cut_kernel(cond_ref, after_ref, *refs):
+def cut_kernel(cond_ref, *refs):
     outs, sems = refs[:-1], refs[-1]
     k_dev, n_cond, npt = cond_ref.shape
     own = outs[0].shape[1]
@@ -230,63 +230,92 @@
         rho_ref[:, r, :] = jnp.broadcast_to(part, (rho_ref.shape[0], LANES))
 
 
-def direct_kernel(n_ka, tile, scale, *refs):
-    qx_ref, cond_ref, scr_ref, turned_ref, rows_ref, di_ref = refs[:6]
-    qx, conds, scrs, turned, vals, mixed, kern, folded, qx_sem, cond_sems, row_sem, chunk_sems = refs[6:]
-    nu, mu = scr_ref.shape
+def direct_kernel(n_ka, halves, mixed_in, mixed_out, tile, scale, *refs):
+    n_half = len(halves)
+    lead_ref, scr_ref, rows_ref, refs = refs[0], refs[1], refs[2], refs[3:]
+    if not mixed_in:
+        qx_ref, refs = refs[0], refs[1:]
+    cond_refs, di_ref, refs = refs[:n_half], refs[n_half], refs[n_half + 1 :]
+    if mixed_out:
+        mixed_ref, refs = refs[0], refs[1:]
+    if not mixed_in:
+        qx, turned, refs = refs[0], refs[1], refs[2:]
+    conds, scrs, vals, mixed, kern, folded, qx_sem, cond_sems, row_sem, chunk_sems = refs
+    nu = lead_ref.shape[0]
+    half = cond_refs[0].shape[1]
+    mu = half * n_half
     quad = 2 * LANES
-    part = cond_ref.shape[0] // n_ka
-    qx_copy = pltpu.make_async_copy(qx_ref, qx, qx_sem.at[0])
+    part = cond_refs[0].shape[0] // n_ka
     cond_copies = [
         pltpu.make_async_copy(
-            cond_ref.at[pl.ds(jnp.bitwise_xor(lax.axis_index("ka"), j) * part, part), :],
-            conds.at[pl.ds(j * part, part), :],
-            cond_sems.at[j],
+            ref.at[pl.ds(jnp.bitwise_xor(lax.axis_index("ka"), j) * part, part), :],
+            conds.at[pl.ds(j * part, part), pl.ds(h * half, half)],
+            cond_sems.at[h, j],
         )
+        for h, ref in enumerate(cond_refs)
         for j in range(n_ka)
     ]
-    turned_copies, scr_copies = [], []
+    lead = mixed if mixed_in else turned
+    lead_copies, scr_copies = [], []
     for i in range(nu // tile):
         at = pl.ds(i * tile, tile)
-        turned_copies.append(
-            pltpu.make_async_copy(turned_ref.at[at, :], turned.at[at, :], chunk_sems.at[0, i])
+        lead_copies.append(
+            pltpu.make_async_copy(lead_ref.at[at, :], lead.at[at, :], chunk_sems.at[0, i])
         )
         scr_copies.append(
-            pltpu.make_async_copy(scr_ref.at[at, :], scrs.at[at, :], chunk_sems.at[1, i])
+            pltpu.make_async_copy(
+                scr_ref.at[at, pl.ds(halves[0] * half, mu)], scrs.at[at, :], chunk_sems.at[1, i]
+            )
         )
     row_copy = pltpu.make_async_copy(rows_ref, vals, row_sem.at[0])
-    start_all([qx_copy, turned_copies[0]] + cond_copies + [scr_copies[0]])
+    if not mixed_in:
+        qx_copy = pltpu.make_async_copy(qx_ref, qx, qx_sem.at[0])
+        qx_copy.start()
+    start_all([lead_copies[0]] + cond_copies + [scr_copies[0]])
     for i in range(1, nu // tile):
-        start_all([turned_copies[i], scr_copies[i]])
+        start_all([lead_copies[i], scr_copies[i]])
     row_copy.start()
-    qx_copy.wait()
+    if not mixed_in:
+        qx_copy.wait()
+    out_copies = []
     for i in range(nu // tile):
-        at = slice(i * tile, (i + 1) * tile)
-        turned_copies[i].wait()
-        for kq in range(qx.shape[0]):
-            cols = slice(kq * quad, (kq + 1) * quad)
-            mixed[at, cols] = jnp.dot(
-                turned[at, cols], qx[kq], preferred_element_type=F32
-            ).astype(BF)
+        rows = slice(i * tile, (i + 1) * tile)
+        lead_copies[i].wait()
+        if not mixed_in:
+            for kq in range(qx.shape[0]):
+                cols = slice(kq * quad, (kq + 1) * quad)
+                mixed[rows, cols] = jnp.dot(
+                    turned[rows, cols], qx[kq], preferred_element_type=F32
+                ).astype(BF)
+        if mixed_out:
+            at = pl.ds(i * tile, tile)
+            out_copies.append(
+                pltpu.make_async_copy(mixed.at[at, :], mixed_ref.at[at, :], chunk_sems.at[2, i])
+            )
+            out_copies[-1].start()
         if i == 0:
             wait_all(cond_copies)
         scr_copies[i].wait()
-        amp = jnp.dot(mixed[at, :], conds[...], preferred_element_type=F32)
-        kern[at, :] = (scrs[at, :].astype(F32) * amp * scale).astype(BF)
+        for m in range(mu // quad):
+            cols = slice(m * quad, (m + 1) * quad)
+            amp = jnp.dot(mixed[rows, :], conds[:, cols], preferred_element_type=F32)
+            kern[rows, cols] = (scrs[rows, cols].astype(F32) * amp * scale).astype(BF)
     row_copy.wait()
-    for i in range(mu // quad):
-        at = slice(i * quad, (i + 1) * quad)
-        folded[:, at] = jnp.dot(vals[...], kern[:, at], preferred_element_type=F32).astype(BF)
+    for m in range(mu // quad):
+        cols = slice(m * quad, (m + 1) * quad)
+        folded[:, cols] = jnp.dot(vals[...], kern[:, cols], preferred_element_type=F32).astype(BF)
     for kp in range(di_ref.shape[0]):
         at = slice(kp * LANES, (kp + 1) * LANES)
         di_ref[kp] = dot_nt(folded[at, :], conds[at, :])
-
-
-def exchange_kernel(cfg, chunk, scale, *refs):
+    wait_all(out_copies)
+
+
+def exchange_kernel(cfg, n_di, chunk, scale, *refs):
     n_ka, n_band, k_dev = cfg
     k_points = n_ka * k_dev
-    rho_ref, di_ref, coul_ref, vown_ref = refs[:4]
-    cond_refs, refs = refs[4 : 4 + n_ka], refs[4 + n_ka :]
+    rho_ref, coul_ref, vown_ref, refs = refs[0], refs[1], refs[2], refs[3:]
+    di_refs, refs = refs[:n_di], refs[n_di:]
+    cond_refs, refs = refs[:n_ka], refs[n_ka:]
     msg_ref, rhos, di, coul, conds, vown, part, msg, coul_sems, cond_sems, sems = refs
     own, npt = coul_ref.shape
     coul_copies = [
@@ -297,8 +326,9 @@
     ]
     rho_copy = pltpu.make_async_copy(rho_ref, rhos, sems.at[0])
     copies = block_copies([[ref] for ref in cond_refs], own, conds, cond_sems)
-    copies.append(pltpu.make_async_copy(di_ref, di, sems.at[1]))
-    copies.append(pltpu.make_async_copy(vown_ref, vown, sems.at[2]))
+    copies.append(pltpu.make_async_copy(vown_ref, vown, sems.at[1]))
+    for i, ref in enumerate(di_refs):
+        copies.append(pltpu.make_async_copy(ref, di.at[i], sems.at[2 + i]))
     start_all([rho_copy] + coul_copies + copies)
     rho_copy.wait()
     acc = jnp.zeros((own, LANES), F32)
@@ -314,7 +344,10 @@
     for kp in range(k_points // 2):
         at = slice(kp * LANES, (kp + 1) * LANES)
         weighted = (vown[at, :].astype(F32) * potential).astype(BF)
-        part[kp] = 2.0 * dot_nt(weighted, cond_rows[at, :]) - di[kp]
+        term = 2.0 * dot_nt(weighted, cond_rows[at, :])
+        for i in range(n_di):
+            term = term - di[i, kp]
+        part[kp] = term
     for d in range(n_band):
         for j in range(n_ka):
             for g in range((k_dev + 1) // 2):
@@ -324,18 +357,12 @@
                     piece = part[k // 2, pl.ds(d * 2 * ROWS + k % 2 * ROWS, ROWS), :]
                     piece = lane_half(piece, k % 2, kl % 2)
                     tile = piece if tile is None else tile + piece
-                to_ka = jnp.bitwise_xor(lax.axis_index("ka"), j)
-                to_band = jnp.bitwise_xor(lax.axis_index("band"), d)
-                msg[to_band, to_ka, pl.ds(g * ROWS, ROWS), :] = tile
+                msg[device_at(n_band, j, d), pl.ds(g * ROWS, ROWS), :] = tile
     msg_ref[...] = msg[...].astype(BF)
 
 
-def plane_sum_kernel(parts_ref, out_ref):
-    out_ref[...] = jnp.sum(parts_ref[...].astype(F32), axis=0)
-
-
 def received(recv_ref):
-    return jnp.sum(recv_ref[...], axis=0)
+    return jnp.sum(recv_ref[...].astype(F32), axis=0)
 
 
 def shifted(count_all, shift, square, cross_sum, square_sum):
@@ -437,15 +464,16 @@
     return lax.ppermute(block, axis, [(i, i ^ d) for i in range(lax.axis_size(axis))])
 
 
-def plane_pieces(own_piece):
+def plane_pieces(own_piece, others):
     def move(block, d):
         return swap(block, "band", d)
 
     half = own_piece.shape[0] // 2
-    by_x, by_y = move(own_piece, 2), move(own_piece, 4)
+    core, by_x, by_y = move(own_piece, 1), move(own_piece, 2), move(own_piece, 4)
+    by_x, by_y, others = lax.optimization_barrier((by_x, by_y, others))
     diag = [move(by_x[:half], 4), move(by_y[half:], 2)]
-    pieces = [[own_piece], [move(own_piece, 1)], [by_x], [move(by_x, 1)], [by_y], [move(by_y, 1)]]
-    return pieces + [diag, [move(part, 1) for part in diag]]
+    pieces = [[own_piece], [core], [by_x], [move(by_x, 1)], [by_y], [move(by_y, 1)]]
+    return pieces + [diag, [move(part, 1) for part in diag]], others
 
 
 def kernel_path(start_vec, val_energy, cond_energy, val_orb, cond_orb, coulomb, screened):
@@ -465,18 +493,20 @@
     scale = 1.0 / (npt_all * math.sqrt(count_all))
     piece_rows = k_points * nv_blk
 
-    cond_local = lax.dynamic_slice_in_dim(cond_orb, band * mu_blk, mu_blk, 2)
-    cond_pts = lax.all_gather(
-        cond_local.reshape(k_dev * n_cond, mu_blk), "ka", axis=0, tiled=True
-    )
-
     def val_to(j):
         part = lax.dynamic_slice_in_dim(val_orb, jnp.bitwise_xor(ka, j) * nu_blk, nu_blk, 2)
         return part.reshape(k_dev * nv_blk, nu_blk)
 
-    val_cut = jnp.concatenate(
-        [val_to(0)] + [swap(val_to(j), "ka", j) for j in range(1, n_ka)], axis=0
-    )
+    val_parts = [val_to(0)] + [swap(val_to(j), "ka", j) for j in range(1, n_ka)]
+    base, val_parts = lax.optimization_barrier((band * mu_blk, val_parts))
+    val_cut = jnp.concatenate(val_parts, axis=0)
+    half = mu_blk // 2
+    cond_pts = []
+    for h in range(2):
+        cut = lax.dynamic_slice_in_dim(cond_orb, base + h * half, half, 2)
+        cond_pts.append(
+            lax.all_gather(cut.reshape(k_dev * n_cond, half), "ka", axis=0, tiled=True)
+        )
     gap = (cond_energy[:, None, :] - val_energy[:, :, None]).reshape(k_dev, nv_blk * n_cond)
     gap = pack_vector(gap, k_dev)
 
@@ -498,22 +528,21 @@
         + [dma(2 * nu_blk // tile)] * 2,
         moved=8 * MIB,
     )(screened)
-    val_cut, msgs, scr_turned = lax.optimization_barrier((val_cut, msgs, scr_turned))
-    pieces = plane_pieces(val_cut)
-    counts = tuple(len(piece) for piece in pieces)
-    flat = [ref for piece in pieces for ref in piece]
-    n_copies = len(flat)
     own_rows = k_dev * n_cond
     cuts = call(
         cut_kernel,
         "cut",
         (shape_of((own_rows, own), BF),) * n_ka,
-        [ANY, ANY],
+        [ANY],
         (ANY,) * n_ka,
         [dma(n_ka * k_dev)],
         mib=8,
-    )(cond_orb, val_cut)
+    )(cond_orb)
     cond_own = [cuts[0]] + [swap(cuts[j], "ka", j) for j in range(1, n_ka)]
+    pieces, (msgs, cond_own, scr_turned) = plane_pieces(val_cut, (msgs, cond_own, scr_turned))
+    counts = tuple(len(piece) for piece in pieces)
+    flat = [ref for piece in pieces for ref in piece]
+    n_copies = len(flat)
 
     val_rows, val_turned, val_own = call(
         functools.partial(order_kernel, counts),
@@ -557,53 +586,69 @@
             mib=8,
         )(msgs, val_own, *cond_own)
         density = exchange_all(rho)
-        direct = call(
-            functools.partial(direct_kernel, n_ka, tile, scale),
-            "direct",
-            shape_of((pairs, LANES, LANES)),
-            [ANY] * 5,
-            VMEM,
-            [
-                pltpu.VMEM((quads, 2 * LANES, 2 * LANES), BF),
-                pltpu.VMEM((conds_all, mu_blk), BF),
-                pltpu.VMEM((nu_blk, mu_blk), BF),
-                pltpu.VMEM((nu_blk, rows_all), BF),
-                pltpu.VMEM((rows_all, nu_blk), BF),
-                pltpu.VMEM((nu_blk, conds_all), BF),
-                pltpu.VMEM((nu_blk, mu_blk), BF),
-                pltpu.VMEM((rows_all, mu_blk), BF),
-                dma(1),
-                dma(n_ka),
-                dma(1),
-                dma(2, nu_blk // tile),
-            ],
-            flops=4 * mu_blk * nu_blk * conds_all,
-            moved=12 * MIB,
-        )(qx, cond_pts, scr_turned, val_turned, val_rows)
+        direct, mixed = [], None
+        for halves in ((0,), (1,)) if first else ((0, 1),):
+            mixed_in, mixed_out = mixed is not None, first and mixed is None
+            mu = half * len(halves)
+            out = call(
+                functools.partial(direct_kernel, n_ka, halves, mixed_in, mixed_out, tile, scale),
+                "direct",
+                (shape_of((pairs, LANES, LANES)),)
+                + ((shape_of((nu_blk, conds_all), BF),) if mixed_out else ()),
+                [ANY] * (3 + (not mixed_in) + len(halves)),
+                (VMEM,) + ((ANY,) if mixed_out else ()),
+                (
+                    []
+                    if mixed_in
+                    else [
+                        pltpu.VMEM((quads, 2 * LANES, 2 * LANES), BF),
+                        pltpu.VMEM((nu_blk, rows_all), BF),
+                    ]
+                )
+                + [
+                    pltpu.VMEM((conds_all, mu), BF),
+                    pltpu.VMEM((nu_blk, mu), BF),
+                    pltpu.VMEM((rows_all, nu_blk), BF),
+                    pltpu.VMEM((nu_blk, conds_all), BF),
+                    pltpu.VMEM((nu_blk, mu), BF),
+                    pltpu.VMEM((rows_all, mu), BF),
+                    dma(1),
+                    dma(len(halves), n_ka),
+                    dma(1),
+                    dma(3, nu_blk // tile),
+                ],
+                flops=4 * mu * nu_blk * conds_all,
+                moved=12 * MIB,
+            )(
+                mixed if mixed_in else val_turned,
+                scr_turned,
+                val_rows,
+                *([] if mixed_in else [qx]),
+                *[cond_pts[h] for h in halves],
+            )
+            direct.append(out[0])
+            if mixed_out:
+                mixed = out[1]
         parts = call(
-            functools.partial(exchange_kernel, cfg, chunk, scale),
+            functools.partial(exchange_kernel, cfg, len(direct), chunk, scale),
             "exchange",
-            shape_of((n_band, n_ka) + block, BF),
-            [ANY] * (4 + n_ka),
+            msg_shape,
+            [ANY] * (3 + len(direct) + n_ka),
             VMEM,
             [
                 pltpu.VMEM((devices, own // LANES, LANES), F32),
-                pltpu.VMEM((pairs, LANES, LANES), F32),
+                pltpu.VMEM((len(direct), pairs, LANES, LANES), F32),
                 pltpu.VMEM((own, npt_all), BF),
                 pltpu.VMEM((n_ka, own_rows, own), BF),
                 pltpu.VMEM((rows_all, own), BF),
                 pltpu.VMEM((pairs, LANES, LANES), F32),
-                pltpu.VMEM((n_band, n_ka) + block, F32),
+                pltpu.VMEM((devices,) + block, F32),
                 dma(npt_all // chunk),
                 dma(n_ka),
-                dma(3),
+                dma(2 + len(direct)),
             ],
-        )(density, direct, coulomb, val_own, *cond_own)
-        parts = lax.all_to_all(parts, "band", split_axis=0, concat_axis=0, tiled=True)
-        plane = call(
-            plane_sum_kernel, "plane_sum", shape_of((n_ka,) + block), [VMEM], VMEM, mib=8
-        )(parts)
-        recv = lax.all_to_all(plane, "ka", split_axis=0, concat_axis=0, tiled=True)
+        )(density, coulomb, val_own, *direct, *cond_own)
+        recv = exchange_all(parts)
         if first:
             state, coef, message = call(
                 functools.partial(first_owner_kernel, count_all),
@@ -724,7 +769,7 @@
         and start_vec.shape[0] * n_ka % 4 == 0
         and coulomb.shape[0] % LANES == 0
         and coulomb.shape[1] % 1024 == 0
-        and screened.shape[0] % 256 == 0
+        and screened.shape[0] % 512 == 0
         and screened.shape[1] % 1024 == 0
         and screened.shape[0] * screened.shape[1] <= 2 * MIB
     )

time: 192 us -> 188 us (0.979)
  blocking collectives: 57.7 us -> 84.5 us
  between operations: 14.5 us -> 1.36 us
  waiting for transfers between devices: 21.6 us -> 10.7 us
  starting transfers between devices: 33.1 us -> 25.8 us
    all_to_all x4 -> x0, blocking collectives: 38.8 us -> none  [the longest x2 20.3 us: kernel_path(): recv = lax.all_to_all(plane, 'ka', split_axis=0, concat_axis=0, tiled=True)]
    all_gather x0 -> x2, blocking collectives: none -> 37.7 us  [kernel_path(): lax.all_gather(cut.reshape(k_dev * n_cond, half), 'ka', axis=0, tiled=True)]
    all_to_all x2 -> x4, blocking collectives: 18.9 us -> 46.8 us  [exchange_all(): return lax.all_to_all(parts, AXES, split_axis=0, concat_axis=0, tiled=True)]
    all_to_all x3, waiting for transfers between devices: 7.98 us -> 0.01 us  [exchange_all(): return lax.all_to_all(parts, AXES, split_axis=0, concat_axis=0, tiled=True)]
    all_to_all x3, starting transfers between devices: 14.2 us -> 8.39 us  [exchange_all(): return lax.all_to_all(parts, AXES, split_axis=0, concat_axis=0, tiled=True)]
    pallas_call x7 -> x6, Pallas kernels: 33.7 us -> 36.8 us  [the longest x3 28.5 us: kernel_path(): call(functools.partial(direct_kernel, n_ka, halves, mixed_in, mixed_out,...]
    ppermute x15, waiting for transfers between devices: 13.6 us -> 10.7 us  [swap(): lax.ppermute(block, axis, [(i, i ^ d) for i in range(lax.axis_size(axis))])]
    unnamed x56 -> x55, local copies, waits for them, and re-layouts: 6.51 us -> 8.05 us
  transfers between devices with their start and end apart: 19 -> 18, of which waited for: 6 -> 4; matrix products, arithmetic and copies ran while one was open for 2% -> 1% of each run, Pallas kernels for 20% -> 18%
where the time goes in v6:
time: 188 us; the launch traced here: 187 us
  blocking collectives  84.5 us (45%)
  Pallas kernels  53.1 us (28%)
  starting transfers between devices  25.8 us (14%)
  local copies, waits for them, and re-layouts  10.7 us (6%)
  waiting for transfers between devices  10.7 us (6%)
    all_to_all x4, blocking collectives, exchange_all(): return lax.all_to_all(parts, AXES, split_axis=0, concat_axis=0, tiled=True)  46.8 us
    all_gather x2, blocking collectives, kernel_path(): lax.all_gather(cut.reshape(k_dev * n_cond, half), 'ka', axis=0, tiled=True)  37.7 us
    pallas_call x3, Pallas kernels, kernel_path(): call(functools.partial(direct_kernel, n_ka, halves, mixed_in, mixed_out,...  28.5 us
    ppermute x15, starting transfers between devices, swap(): lax.ppermute(block, axis, [(i, i ^ d) for i in range(lax.axis_size(axis))])  17.4 us
    ppermute x15, waiting for transfers between devices, swap(): lax.ppermute(block, axis, [(i, i ^ d) for i in range(lax.axis_size(axis))])  10.7 us
    all_to_all x3, starting transfers between devices, exchange_all(): return lax.all_to_all(parts, AXES, split_axis=0, concat_axis=0, tiled=True)  8.39 us
    pallas_call x2, Pallas kernels, kernel_path(): call(functools.partial(exchange_kernel, cfg, len(direct), chunk, scale),...  8.1 us
    unnamed x55, local copies, waits for them, and re-layouts  8.05 us
  transfers between devices with their start and end apart: 18, of which 4 were waited for; matrix products, arithmetic and copies ran while one was open for 1% of the time, Pallas kernels for 18%

profile of v6, /device:TPU:0, one launch (start us, length us, event | category | flops | bytes accessed | tf_op | source)
XLA Modules:
  0.0 187.0 jit_solution(8059016211750044110)
XLA Ops:
  0.7 1.1 dynamic-slice_bitcast_fusion
  1.7 5.1 %collective-permute-start.2 = (bf16[24,2048]{1,0:T(8,128)(2,1)S(1)}, bf16[24,2048]{1,0:T(8,128)(2,1)S(1)}, u32[]{:S(2)}, u32[]{:S(2)}) collective-permute-start(bf16[24,2048]{1,0:T(8,128)(2,1)S(1)} %get-tuple-element.72), channel_id=1, source_target_pairs={{0,24},{8,16},{16,8},{24,0},{1,25},{9,17},{17,9},{25,1},{2,26},{10... | collective-permute-start | bytes 294920 | tf_op jit(solution)/shard_map/ppermute | solution.py:464
  6.8 0.6 collective-permute-start.1
  7.5 3.0 %collective-permute-done.2 = bf16[24,2048]{1,0:T(8,128)(2,1)S(1)} collective-permute-done((bf16[24,2048]{1,0:T(8,128)(2,1)S(1)}, bf16[24,2048]{1,0:T(8,128)(2,1)S(1)}, u32[]{:S(2)}, u32[]{:S(2)}) %collective-permute-start.2) | collective-permute-done | bytes 98336 | tf_op jit(solution)/shard_map/ppermute | solution.py:464
  10.5 2.3 %collective-permute-done = bf16[24,2048]{1,0:T(8,128)(2,1)S(1)} collective-permute-done((bf16[24,2048]{1,0:T(8,128)(2,1)S(1)}, bf16[24,2048]{1,0:T(8,128)(2,1)S(1)}, u32[]{:S(2)}, u32[]{:S(2)}) %collective-permute-start) | collective-permute-done | bytes 98336 | tf_op jit(solution)/shard_map/ppermute | solution.py:464
  12.9 2.3 %collective-permute-done.1 = bf16[24,2048]{1,0:T(8,128)(2,1)S(1)} collective-permute-done((bf16[24,2048]{1,0:T(8,128)(2,1)S(1)}, bf16[24,2048]{1,0:T(8,128)(2,1)S(1)}, u32[]{:S(2)}, u32[]{:S(2)}) %collective-permute-start.1) | collective-permute-done | bytes 98336 | tf_op jit(solution)/shard_map/ppermute | solution.py:464
  15.2 1.6 collective-permute-start.4
  16.8 1.5 collective-permute-start.3
  18.3 0.8 broadcast_subtract_fusion
  19.3 0.7 copy-done.11
  20.0 0.9 pack.1
  20.9 2.9 %all-to-all-start = ((bf16[32,16,128]{2,1,0:T(8,128)(2,1)}), bf16[32,16,128]{2,1,0:T(8,128)(2,1)S(1)}, u32[]{:S(2)}, u32[]{:S(2)}) async-start(bf16[32,16,128]{2,1,0:T(8,128)(2,1)} %get-tuple-element.40), calls=%async_computation | async-start | bytes 262144 | tf_op jit(solution)/shard_map/all_to_all | solution.py:30
  23.8 1.9 %copy-done.2 = bf16[3,64,8192]{2,1,0:T(8,128)(2,1)S(1)} copy-done((bf16[3,64,8192]{2,1,0:T(8,128)(2,1)S(1)}, bf16[3,64,8192]{2,1,0:T(8,128)(2,1)}, u32[]{:S(2)}) %copy-start.2) | copy-done | bytes 3145752
  25.9 1.8 collective-permute-start.5
  27.8 2.4 %collective-permute-start.6 = (bf16[192,256]{1,0:T(8,128)(2,1)S(1)}, bf16[192,256]{1,0:T(8,128)(2,1)S(1)}, u32[]{:S(2)}, u32[]{:S(2)}) collective-permute-start(bf16[192,256]{1,0:T(8,128)(2,1)S(1)} %get-tuple-element.43), channel_id=1, source_target_pairs={{0,16},{8,24},{16,0},{24,8},{1,17},{9,25},{17,1},{25,9},{2,18},{10... | collective-permute-start | bytes 294920 | tf_op jit(solution)/shard_map/ppermute | solution.py:464
  30.4 3.7 %turn.1.refs_1_ = bf16[2048,1024]{1,0:T(8,128)(2,1)} custom-call(bf16[1024,2048]{1,0:T(8,128)(2,1)} %scr_ref.1), custom_call_target="tpu_custom_call" | custom-call | bytes 8388608 | tf_op jit(solution)/shard_map/turn/pallas_call | solution.py:521
  34.1 1.3 constant_dynamic-slice_fusion
  35.4 3.1 %collective-permute-done.6.refs_4_.refs_7_.refs_6_ = bf16[192,256]{1,0:T(8,128)(2,1)S(1)} collective-permute-done((bf16[192,256]{1,0:T(8,128)(2,1)S(1)}, bf16[192,256]{1,0:T(8,128)(2,1)S(1)}, u32[]{:S(2)}, u32[]{:S(2)}) %collective-permute-start.6) | collective-permute-done | bytes 98336 | tf_op jit(solution)/shard_map/ppermute | solution.py:464
  38.7 0.6 collective-permute-start.10
  39.2 1.5 collective-permute-start.12
  40.7 1.4 collective-permute-start.11
  42.2 19.0 %all_gather.6.refs_4_ = bf16[768,512]{1,0:T(8,128)(2,1)} all-gather(bf16[192,512]{1,0:T(8,128)(2,1)S(1)} %bitcast.12), channel_id=1, replica_groups=mesh['ka'=4,'band'=8] {'ka'}, dimensions={0}, use_global_device_ids=true | all-gather | bytes 983040 | tf_op jit(solution)/shard_map/all_gather | solution.py:508
  61.2 0.5 collective-permute-start.13
  61.7 18.7 %all_gather.7.refs_3_.refs_5_ = bf16[768,512]{1,0:T(8,128)(2,1)} all-gather(bf16[192,512]{1,0:T(8,128)(2,1)S(1)} %bitcast.11), channel_id=1, replica_groups=mesh['ka'=4,'band'=8] {'ka'}, dimensions={0}, use_global_device_ids=true | all-gather | bytes 983040 | tf_op jit(solution)/shard_map/all_gather | solution.py:508
  80.6 0.7 copy-done.17
  81.5 0.8 copy-done.19
  82.3 5.0 %order.1 = (bf16[768,2048]{1,0:T(8,128)(2,1)}, bf16[2048,768]{1,0:T(8,128)(2,1)}, bf16[768,256]{1,0:T(8,128)(2,1)}) custom-call(bf16[96,2048]{1,0:T(8,128)(2,1)} %copy-done.16, bf16[96,2048]{1,0:T(8,128)(2,1)} %copy-done.17, bf16[96,2048]{1,0:T(8,128)(2,1)} %copy-done.15, bf16[96,2048]{1,0:T(8,128)(2,1)} %copy-done.18, bf16[96,2048]{1,0:T(8,128)(2,1)} %copy-done.14, ...), custom_call_target="tpu_custom_call" | custom-call | bytes 9437184 | tf_op jit(solution)/shard_map/order/pallas_call | solution.py:547
  87.3 1.0 copy-done
  88.3 1.6 density.2
  89.9 0.7 copy-done.13
  90.6 2.8 %all-to-all-start.1 = ((f32[32,2,128]{2,1,0:T(2,128)}), f32[32,2,128]{2,1,0:T(2,128)S(1)}, u32[]{:S(2)}, u32[]{:S(2)}) async-start(f32[32,2,128]{2,1,0:T(2,128)} %get-tuple-element.53), calls=%async_computation.1 | async-start | bytes 65536 | tf_op jit(solution)/shard_map/all_to_all | solution.py:30
  93.4 8.7 %direct.3 = (f32[6,128,128]{2,1,0:T(8,128)}, bf16[2048,768]{1,0:T(8,128)(2,1)}) custom-call(bf16[2048,768]{1,0:T(8,128)(2,1)} %get-tuple-element.54.refs_0_, bf16[2048,1024]{1,0:T(8,128)(2,1)} %turn.1.refs_1_, bf16[768,2048]{1,0:T(8,128)(2,1)} %get-tuple-element.56.refs_2_, bf16[3,256,256]{2,1,0:T(8,128)(2,1)} %copy-done.13, bf16[768,512]{1,0:T(8,128)(2,1)} %all_gather.6.refs_4_), custom_call_target="tpu_custom_call" | custom-call | flops 3221225472 | bytes 12582912 | tf_op jit(solution)/shard_map/direct/pallas_call | solution.py:593
  102.1 7.2 %direct.4.refs_4_ = f32[6,128,128]{2,1,0:T(8,128)} custom-call(bf16[2048,768]{1,0:T(8,128)(2,1)} %get-tuple-element.60.refs_0_, bf16[2048,1024]{1,0:T(8,128)(2,1)} %turn.1.refs_1_, bf16[768,2048]{1,0:T(8,128)(2,1)} %get-tuple-element.56.refs_2_, bf16[768,512]{1,0:T(8,128)(2,1)} %all_gather.7.refs_3_.refs_5_), custom_call_target="tpu_custom_call" | custom-call | flops 3221225472 | bytes 12582912 | tf_op jit(solution)/shard_map/direct/pallas_call | solution.py:593
  109.3 0.6 copy-done.25
  109.9 4.0 %exchange.2 = bf16[32,16,128]{2,1,0:T(8,128)(2,1)} custom-call(f32[32,2,128]{2,1,0:T(2,128)} %copy-done.25, bf16[256,8192]{1,0:T(8,128)(2,1)} %refs_1_.3, bf16[768,256]{1,0:T(8,128)(2,1)} %get-tuple-element.48.refs_1_.refs_2_, f32[6,128,128]{2,1,0:T(8,128)} %get-tuple-element.59.refs_3_, f32[6,128,128]{2,1,0:T(8,128)} %direct.4.refs_4_, ...), custom_call_target="tpu_custom_call" | custom-call | tf_op jit(solution)/shard_map/exchange/pallas_call | solution.py:632
  113.9 13.9 %all_to_all.35.recv_ref = bf16[32,16,128]{2,1,0:T(8,128)(2,1)S(1)} all-to-all(bf16[32,16,128]{2,1,0:T(8,128)(2,1)} %exchange.2), channel_id=1, replica_groups=mesh['ka'=4,'band'=8] {'ka','band'}, dimensions={0} | all-to-all | bytes 262144 | tf_op jit(solution)/shard_map/all_to_all | solution.py:30
  127.8 0.8 first_owner.1
  128.6 10.0 %all_to_all.36.refs_0_.msgs_ref = bf16[32,16,128]{2,1,0:T(8,128)(2,1)S(1)} all-to-all(bf16[32,16,128]{2,1,0:T(8,128)(2,1)S(1)} %get-tuple-element.62), channel_id=1, replica_groups=mesh['ka'=4,'band'=8] {'ka','band'}, dimensions={0} | all-to-all | bytes 262144 | tf_op jit(solution)/shard_map/all_to_all | solution.py:30
  138.7 1.6 density.3
  140.3 0.7 copy-done.12
  141.0 2.7 %all-to-all-start.4 = ((f32[32,2,128]{2,1,0:T(2,128)}), f32[32,2,128]{2,1,0:T(2,128)S(1)}, u32[]{:S(2)}, u32[]{:S(2)}) async-start(f32[32,2,128]{2,1,0:T(2,128)} %get-tuple-element.63), calls=%async_computation.4 | async-start | bytes 65536 | tf_op jit(solution)/shard_map/all_to_all | solution.py:30
  143.8 12.7 %direct.5.refs_3_ = f32[6,128,128]{2,1,0:T(8,128)} custom-call(bf16[2048,768]{1,0:T(8,128)(2,1)} %get-tuple-element.54.refs_0_, bf16[2048,1024]{1,0:T(8,128)(2,1)} %turn.1.refs_1_, bf16[768,2048]{1,0:T(8,128)(2,1)} %get-tuple-element.56.refs_2_, bf16[3,256,256]{2,1,0:T(8,128)(2,1)} %copy-done.12, bf16[768,512]{1,0:T(8,128)(2,1)} %all_gather.6.refs_4_, ...), custom_call_target="tpu_custom_call" | custom-call | flops 6442450944 | bytes 12582912 | tf_op jit(solution)/shard_map/direct/pallas_call | solution.py:593
  156.5 0.6 copy-done.24
  157.1 4.1 %exchange.3 = bf16[32,16,128]{2,1,0:T(8,128)(2,1)} custom-call(f32[32,2,128]{2,1,0:T(2,128)} %copy-done.24, bf16[256,8192]{1,0:T(8,128)(2,1)} %refs_1_.3, bf16[768,256]{1,0:T(8,128)(2,1)} %get-tuple-element.48.refs_1_.refs_2_, f32[6,128,128]{2,1,0:T(8,128)} %direct.5.refs_3_, bf16[192,256]{1,0:T(8,128)(2,1)} %copy-done.3, bf16[192,256]{1,0:T(8,128)(2,1)} %copy-done.5, ...), custom_call_target="tpu_custom_call" | custom-call | tf_op jit(solution)/shard_map/exchange/pallas_call | solution.py:632
  161.2 13.9 %all_to_all.37.recv_ref = bf16[32,16,128]{2,1,0:T(8,128)(2,1)S(1)} all-to-all(bf16[32,16,128]{2,1,0:T(8,128)(2,1)} %exchange.3), channel_id=1, replica_groups=mesh['ka'=4,'band'=8] {'ka','band'}, dimensions={0} | all-to-all | bytes 262144 | tf_op jit(solution)/shard_map/all_to_all | solution.py:30
  175.1 1.3 second_owner.1
  176.4 9.0 %all_to_all.38.msgs_ref = f32[32,2,128]{2,1,0:T(2,128)S(1)} all-to-all(f32[32,2,128]{2,1,0:T(2,128)S(1)} %get-tuple-element.67), channel_id=1, replica_groups=mesh['ka'=4,'band'=8] {'ka','band'}, dimensions={0} | all-to-all | bytes 65536 | tf_op jit(solution)/shard_map/all_to_all | solution.py:30
  185.4 1.3 finish.1
  (74 shorter events, 1.3 us)
Async XLA Ops:
  1.7 8.8 %collective-permute-start.2 = (bf16[24,2048]{1,0:T(8,128)(2,1)S(1)}, bf16[24,2048]{1,0:T(8,128)(2,1)S(1)}, u32[]{:S(2)}, u32[]{:S(2)}) collective-permute-start(bf16[24,2048]{1,0:T(8,128)(2,1)S(1)} %get-tuple-element.72), channel_id=1, source_target_pairs={{0,24},{8,16},{16,8},{24,0},{1,25},{9,17},{17,9},{25,1},{2,26},{10... | collective-permute-start | bytes 294920 | tf_op jit(solution)/shard_map/ppermute | solution.py:464
  6.8 6.0 %collective-permute-start = (bf16[24,2048]{1,0:T(8,128)(2,1)S(1)}, bf16[24,2048]{1,0:T(8,128)(2,1)S(1)}, u32[]{:S(2)}, u32[]{:S(2)}) collective-permute-start(bf16[24,2048]{1,0:T(8,128)(2,1)S(1)} %get-tuple-element.73), channel_id=1, source_target_pairs={{0,8},{8,0},{16,24},{24,16},{1,9},{9,1},{17,25},{25,17},{2,10},{10... | collective-permute-start | bytes 294920 | tf_op jit(solution)/shard_map/ppermute | solution.py:464
  6.8 8.3 %collective-permute-start.1 = (bf16[24,2048]{1,0:T(8,128)(2,1)S(1)}, bf16[24,2048]{1,0:T(8,128)(2,1)S(1)}, u32[]{:S(2)}, u32[]{:S(2)}) collective-permute-start(bf16[24,2048]{1,0:T(8,128)(2,1)S(1)} %get-tuple-element.75), channel_id=1, source_target_pairs={{0,16},{8,24},{16,0},{24,8},{1,17},{9,25},{17,1},{25,9},{2,18},{10... | collective-permute-start | bytes 294920 | tf_op jit(solution)/shard_map/ppermute | solution.py:464
  15.2 20.2 %copy-start.16 = (bf16[96,2048]{1,0:T(8,128)(2,1)}, bf16[96,2048]{1,0:T(8,128)(2,1)S(1)}, u32[]{:S(2)}) copy-start(bf16[96,2048]{1,0:T(8,128)(2,1)S(1)} %constant_dynamic-update-slice_fusion.refs_0_) | copy-start | bytes 1179652
  15.2 23.3 %collective-permute-start.4 = (bf16[96,2048]{1,0:T(8,128)(2,1)S(1)}, bf16[96,2048]{1,0:T(8,128)(2,1)S(1)}, u32[]{:S(2)}, u32[]{:S(2)}) collective-permute-start(bf16[96,2048]{1,0:T(8,128)(2,1)S(1)} %constant_dynamic-update-slice_fusion.refs_0_), channel_id=1, source_target_pairs={{0,4},{1,5},{2,6},{3,7},{4,0},{5,1},{6,2},{7,3},{8,12},{9,13},{10,... | collective-permute-start | bytes 1179656 | tf_op jit(solution)/shard_map/ppermute | solution.py:464
  16.8 21.8 %collective-permute-start.3 = (bf16[96,2048]{1,0:T(8,128)(2,1)S(1)}, bf16[96,2048]{1,0:T(8,128)(2,1)S(1)}, u32[]{:S(2)}, u32[]{:S(2)}) collective-permute-start(bf16[96,2048]{1,0:T(8,128)(2,1)S(1)} %constant_dynamic-update-slice_fusion.refs_0_), channel_id=1, source_target_pairs={{0,2},{1,3},{2,0},{3,1},{4,6},{5,7},{6,4},{7,5},{8,10},{9,11},{10,... | collective-permute-start | bytes 1179656 | tf_op jit(solution)/shard_map/ppermute | solution.py:464
  19.3 0.7 copy-start.11
  20.9 17.6 %all-to-all-start = ((bf16[32,16,128]{2,1,0:T(8,128)(2,1)}), bf16[32,16,128]{2,1,0:T(8,128)(2,1)S(1)}, u32[]{:S(2)}, u32[]{:S(2)}) async-start(bf16[32,16,128]{2,1,0:T(8,128)(2,1)} %get-tuple-element.40), calls=%async_computation | async-start | bytes 262144 | tf_op jit(solution)/shard_map/all_to_all | solution.py:30
  23.8 1.9 %copy-start.2 = (bf16[3,64,8192]{2,1,0:T(8,128)(2,1)S(1)}, bf16[3,64,8192]{2,1,0:T(8,128)(2,1)}, u32[]{:S(2)}) copy-start(bf16[3,64,8192]{2,1,0:T(8,128)(2,1)} %cond_ref.1) | copy-start | bytes 9437188
  25.9 61.4 %copy-start.3 = (bf16[192,256]{1,0:T(8,128)(2,1)}, bf16[192,256]{1,0:T(8,128)(2,1)S(1)}, u32[]{:S(2)}) copy-start(bf16[192,256]{1,0:T(8,128)(2,1)S(1)} %get-tuple-element.49.refs_2_.refs_5_.refs_4_) | copy-start | bytes 294916
  25.9 9.4 %collective-permute-start.5 = (bf16[192,256]{1,0:T(8,128)(2,1)S(1)}, bf16[192,256]{1,0:T(8,128)(2,1)S(1)}, u32[]{:S(2)}, u32[]{:S(2)}) collective-permute-start(bf16[192,256]{1,0:T(8,128)(2,1)S(1)} %get-tuple-element.42), channel_id=1, source_target_pairs={{0,8},{8,0},{16,24},{24,16},{1,9},{9,1},{17,25},{25,17},{2,10},{10... | collective-permute-start | bytes 294920 | tf_op jit(solution)/shard_map/ppermute | solution.py:464
  27.8 10.8 %collective-permute-start.6 = (bf16[192,256]{1,0:T(8,128)(2,1)S(1)}, bf16[192,256]{1,0:T(8,128)(2,1)S(1)}, u32[]{:S(2)}, u32[]{:S(2)}) collective-permute-start(bf16[192,256]{1,0:T(8,128)(2,1)S(1)} %get-tuple-element.43), channel_id=1, source_target_pairs={{0,16},{8,24},{16,0},{24,8},{1,17},{9,25},{17,1},{25,9},{2,18},{10... | collective-permute-start | bytes 294920 | tf_op jit(solution)/shard_map/ppermute | solution.py:464
  30.2 8.3 %collective-permute-start.7 = (bf16[192,256]{1,0:T(8,128)(2,1)S(1)}, bf16[192,256]{1,0:T(8,128)(2,1)S(1)}, u32[]{:S(2)}, u32[]{:S(2)}) collective-permute-start(bf16[192,256]{1,0:T(8,128)(2,1)S(1)} %get-tuple-element.44), channel_id=1, source_target_pairs={{0,24},{8,16},{16,8},{24,0},{1,25},{9,17},{17,9},{25,1},{2,26},{10... | collective-permute-start | bytes 294920 | tf_op jit(solution)/shard_map/ppermute | solution.py:464
  35.4 54.5 %copy-start.5 = (bf16[192,256]{1,0:T(8,128)(2,1)}, bf16[192,256]{1,0:T(8,128)(2,1)S(1)}, u32[]{:S(2)}) copy-start(bf16[192,256]{1,0:T(8,128)(2,1)S(1)} %collective-permute-done.5.refs_3_.refs_6_.refs_5_) | copy-start | bytes 294916
  35.4 45.1 %collective-permute-start.8 = (bf16[96,2048]{1,0:T(8,128)(2,1)S(1)}, bf16[96,2048]{1,0:T(8,128)(2,1)S(1)}, u32[]{:S(2)}, u32[]{:S(2)}) collective-permute-start(bf16[96,2048]{1,0:T(8,128)(2,1)S(1)} %constant_dynamic-update-slice_fusion.refs_0_), channel_id=1, source_target_pairs={{0,1},{1,0},{2,3},{3,2},{4,5},{5,4},{6,7},{7,6},{8,9},{9,8},{10,11... | collective-permute-start | bytes 1179656 | tf_op jit(solution)/shard_map/ppermute | solution.py:464
  38.5 51.4 %copy-start.7 = (bf16[192,256]{1,0:T(8,128)(2,1)}, bf16[192,256]{1,0:T(8,128)(2,1)S(1)}, u32[]{:S(2)}) copy-start(bf16[192,256]{1,0:T(8,128)(2,1)S(1)} %collective-permute-done.6.refs_4_.refs_7_.refs_6_) | copy-start | bytes 294916
  38.5 51.4 %copy-start.9 = (bf16[192,256]{1,0:T(8,128)(2,1)}, bf16[192,256]{1,0:T(8,128)(2,1)S(1)}, u32[]{:S(2)}) copy-start(bf16[192,256]{1,0:T(8,128)(2,1)S(1)} %collective-permute-done.7.refs_5_.refs_8_.refs_7_) | copy-start | bytes 294916
  38.5 42.0 %copy-start.14 = (bf16[96,2048]{1,0:T(8,128)(2,1)}, bf16[96,2048]{1,0:T(8,128)(2,1)S(1)}, u32[]{:S(2)}) copy-start(bf16[96,2048]{1,0:T(8,128)(2,1)S(1)} %collective-permute-done.4.refs_4_) | copy-start | bytes 1179652
  38.6 42.0 %copy-start.15 = (bf16[96,2048]{1,0:T(8,128)(2,1)}, bf16[96,2048]{1,0:T(8,128)(2,1)S(1)}, u32[]{:S(2)}) copy-start(bf16[96,2048]{1,0:T(8,128)(2,1)S(1)} %collective-permute-done.3.refs_2_) | copy-start | bytes 1179652
  38.6 41.9 %collective-permute-start.9 = (bf16[96,2048]{1,0:T(8,128)(2,1)S(1)}, bf16[96,2048]{1,0:T(8,128)(2,1)S(1)}, u32[]{:S(2)}, u32[]{:S(2)}) collective-permute-start(bf16[96,2048]{1,0:T(8,128)(2,1)S(1)} %collective-permute-done.3.refs_2_), channel_id=1, source_target_pairs={{0,1},{1,0},{2,3},{3,2},{4,5},{5,4},{6,7},{7,6},{8,9},{9,8},{10,11... | collective-permute-start | bytes 1179656 | tf_op jit(solution)/shard_map/ppermute | solution.py:464
  38.7 41.8 %collective-permute-start.10 = (bf16[96,2048]{1,0:T(8,128)(2,1)S(1)}, bf16[96,2048]{1,0:T(8,128)(2,1)S(1)}, u32[]{:S(2)}, u32[]{:S(2)}) collective-permute-start(bf16[96,2048]{1,0:T(8,128)(2,1)S(1)} %collective-permute-done.4.refs_4_), channel_id=1, source_target_pairs={{0,1},{1,0},{2,3},{3,2},{4,5},{5,4},{6,7},{7,6},{8,9},{9,8},{10,11... | collective-permute-start | bytes 1179656 | tf_op jit(solution)/shard_map/ppermute | solution.py:464
  39.2 21.9 %collective-permute-start.12 = (bf16[48,2048]{1,0:T(8,128)(2,1)S(1)}, bf16[48,2048]{1,0:T(8,128)(2,1)S(1)}, u32[]{:S(2)}, u32[]{:S(2)}) collective-permute-start(bf16[48,2048]{1,0:T(8,128)(2,1)S(1)} %slice.7), channel_id=1, source_target_pairs={{0,2},{1,3},{2,0},{3,1},{4,6},{5,7},{6,4},{7,5},{8,10},{9,11},{10,... | collective-permute-start | bytes 589832 | tf_op jit(solution)/shard_map/ppermute | solution.py:464
  40.7 20.5 %collective-permute-start.11 = (bf16[48,2048]{1,0:T(8,128)(2,1)S(1)}, bf16[48,2048]{1,0:T(8,128)(2,1)S(1)}, u32[]{:S(2)}, u32[]{:S(2)}) collective-permute-start(bf16[48,2048]{1,0:T(8,128)(2,1)S(1)} %slice.6), channel_id=1, source_target_pairs={{0,4},{1,5},{2,6},{3,7},{4,0},{5,1},{6,2},{7,3},{8,12},{9,13},{10,... | collective-permute-start | bytes 589832 | tf_op jit(solution)/shard_map/ppermute | solution.py:464
  61.1 19.4 %copy-start.20 = (bf16[48,2048]{1,0:T(8,128)(2,1)}, bf16[48,2048]{1,0:T(8,128)(2,1)S(1)}, u32[]{:S(2)}) copy-start(bf16[48,2048]{1,0:T(8,128)(2,1)S(1)} %collective-permute-done.12.refs_7_) | copy-start | bytes 589828
  61.1 19.3 %collective-permute-start.14 = (bf16[48,2048]{1,0:T(8,128)(2,1)S(1)}, bf16[48,2048]{1,0:T(8,128)(2,1)S(1)}, u32[]{:S(2)}, u32[]{:S(2)}) collective-permute-start(bf16[48,2048]{1,0:T(8,128)(2,1)S(1)} %collective-permute-done.12.refs_7_), channel_id=1, source_target_pairs={{0,1},{1,0},{2,3},{3,2},{4,5},{5,4},{6,7},{7,6},{8,9},{9,8},{10,11... | collective-permute-start | bytes 589832 | tf_op jit(solution)/shard_map/ppermute | solution.py:464
  61.2 19.3 %copy-start.21 = (bf16[48,2048]{1,0:T(8,128)(2,1)}, bf16[48,2048]{1,0:T(8,128)(2,1)S(1)}, u32[]{:S(2)}) copy-start(bf16[48,2048]{1,0:T(8,128)(2,1)S(1)} %collective-permute-done.11.refs_6_) | copy-start | bytes 589828
  61.2 19.2 %collective-permute-start.13 = (bf16[48,2048]{1,0:T(8,128)(2,1)S(1)}, bf16[48,2048]{1,0:T(8,128)(2,1)S(1)}, u32[]{:S(2)}, u32[]{:S(2)}) collective-permute-start(bf16[48,2048]{1,0:T(8,128)(2,1)S(1)} %collective-permute-done.11.refs_6_), channel_id=1, source_target_pairs={{0,1},{1,0},{2,3},{3,2},{4,5},{5,4},{6,7},{7,6},{8,9},{9,8},{10,11... | collective-permute-start | bytes 589832 | tf_op jit(solution)/shard_map/ppermute | solution.py:464
  80.4 0.8 copy-start.17
  80.5 0.8 copy-start.22
  80.5 0.9 copy-start.23
  80.5 1.0 copy-start.18
  81.5 0.8 copy-start.19
  87.3 1.0 copy-start
  89.9 0.7 copy-start.13
  90.6 18.6 %all-to-all-start.1 = ((f32[32,2,128]{2,1,0:T(2,128)}), f32[32,2,128]{2,1,0:T(2,128)S(1)}, u32[]{:S(2)}, u32[]{:S(2)}) async-start(f32[32,2,128]{2,1,0:T(2,128)} %get-tuple-element.53), calls=%async_computation.1 | async-start | bytes 65536 | tf_op jit(solution)/shard_map/all_to_all | solution.py:30
  109.3 0.6 copy-start.25
  109.9 28.8 %copy-start.1 = (bf16[768,256]{1,0:T(8,128)(2,1)S(1)}, bf16[768,256]{1,0:T(8,128)(2,1)}, u32[]{:S(2)}) copy-start(bf16[768,256]{1,0:T(8,128)(2,1)} %get-tuple-element.48.refs_1_.refs_2_) | copy-start | bytes 1179652
  109.9 28.8 %copy-start.4 = (bf16[192,256]{1,0:T(8,128)(2,1)S(1)}, bf16[192,256]{1,0:T(8,128)(2,1)}, u32[]{:S(2)}) copy-start(bf16[192,256]{1,0:T(8,128)(2,1)} %copy-done.3) | copy-start | bytes 294916
  109.9 28.8 %copy-start.6 = (bf16[192,256]{1,0:T(8,128)(2,1)S(1)}, bf16[192,256]{1,0:T(8,128)(2,1)}, u32[]{:S(2)}) copy-start(bf16[192,256]{1,0:T(8,128)(2,1)} %copy-done.5) | copy-start | bytes 294916
  109.9 28.8 %copy-start.8 = (bf16[192,256]{1,0:T(8,128)(2,1)S(1)}, bf16[192,256]{1,0:T(8,128)(2,1)}, u32[]{:S(2)}) copy-start(bf16[192,256]{1,0:T(8,128)(2,1)} %copy-done.7) | copy-start | bytes 294916
  109.9 28.8 %copy-start.10 = (bf16[192,256]{1,0:T(8,128)(2,1)S(1)}, bf16[192,256]{1,0:T(8,128)(2,1)}, u32[]{:S(2)}) copy-start(bf16[192,256]{1,0:T(8,128)(2,1)} %copy-done.9) | copy-start | bytes 294916
  140.3 0.8 copy-start.12
  141.0 15.4 %all-to-all-start.4 = ((f32[32,2,128]{2,1,0:T(2,128)}), f32[32,2,128]{2,1,0:T(2,128)S(1)}, u32[]{:S(2)}, u32[]{:S(2)}) async-start(f32[32,2,128]{2,1,0:T(2,128)} %get-tuple-element.63), calls=%async_computation.4 | async-start | bytes 65536 | tf_op jit(solution)/shard_map/all_to_all | solution.py:30
  156.5 0.6 copy-start.24

commit v7 on v5

--- a/solution.py
+++ b/solution.py
@@ -136,7 +136,7 @@
     msg_ref[...] = jnp.broadcast_to(block.astype(BF)[None], msg_ref.shape)
 
 
-def cut_kernel(cond_ref, after_ref, *refs):
+def cut_kernel(cond_ref, *refs):
     outs, sems = refs[:-1], refs[-1]
     k_dev, n_cond, npt = cond_ref.shape
     own = outs[0].shape[1]
@@ -230,21 +230,37 @@
         rho_ref[:, r, :] = jnp.broadcast_to(part, (rho_ref.shape[0], LANES))
 
 
+def line_blocks(n_ka):
+    return [(way, hop) for way in (-1, 1) for hop in range(1, n_ka)]
+
+
 def direct_kernel(n_ka, tile, scale, *refs):
-    qx_ref, cond_ref, scr_ref, turned_ref, rows_ref, di_ref = refs[:6]
-    qx, conds, scrs, turned, vals, mixed, kern, folded, qx_sem, cond_sems, row_sem, chunk_sems = refs[6:]
+    turned_ref, scr_ref, rows_ref, qx_ref, refs = refs[0], refs[1], refs[2], refs[3], refs[4:]
+    hops = [(0, 0)] + line_blocks(n_ka)
+    cond_refs, refs = split_refs(refs, [2] * len(hops)), refs[2 * len(hops) :]
+    di_ref, qx, turned, conds, scrs, vals, mixed, kern, folded = refs[:9]
+    qx_sem, cond_sems, row_sem, chunk_sems = refs[9:]
     nu, mu = scr_ref.shape
+    part, half = cond_refs[0][0].shape
     quad = 2 * LANES
-    part = cond_ref.shape[0] // n_ka
+    ka = lax.axis_index("ka")
+
+    def each_block(act):
+        for i, (way, hop) in enumerate(hops):
+            origin = ka + way * hop
+
+            def act_on(i=i, origin=origin):
+                row = pl.multiple_of(jnp.bitwise_xor(ka, origin) * part, part)
+                for h, ref in enumerate(cond_refs[i]):
+                    dest = conds.at[pl.ds(row, part), pl.ds(h * half, half)]
+                    act(pltpu.make_async_copy(ref, dest, cond_sems.at[i, h]))
+
+            if hop == 0:
+                act_on()
+            else:
+                pl.when((origin >= 0) & (origin < n_ka))(act_on)
+
     qx_copy = pltpu.make_async_copy(qx_ref, qx, qx_sem.at[0])
-    cond_copies = [
-        pltpu.make_async_copy(
-            cond_ref.at[pl.ds(jnp.bitwise_xor(lax.axis_index("ka"), j) * part, part), :],
-            conds.at[pl.ds(j * part, part), :],
-            cond_sems.at[j],
-        )
-        for j in range(n_ka)
-    ]
     turned_copies, scr_copies = [], []
     for i in range(nu // tile):
         at = pl.ds(i * tile, tile)
@@ -255,28 +271,32 @@
             pltpu.make_async_copy(scr_ref.at[at, :], scrs.at[at, :], chunk_sems.at[1, i])
         )
     row_copy = pltpu.make_async_copy(rows_ref, vals, row_sem.at[0])
-    start_all([qx_copy, turned_copies[0]] + cond_copies + [scr_copies[0]])
+    start_all([qx_copy, turned_copies[0]])
+    each_block(lambda copy: copy.start())
+    scr_copies[0].start()
     for i in range(1, nu // tile):
         start_all([turned_copies[i], scr_copies[i]])
     row_copy.start()
     qx_copy.wait()
     for i in range(nu // tile):
-        at = slice(i * tile, (i + 1) * tile)
+        rows = slice(i * tile, (i + 1) * tile)
         turned_copies[i].wait()
         for kq in range(qx.shape[0]):
             cols = slice(kq * quad, (kq + 1) * quad)
-            mixed[at, cols] = jnp.dot(
-                turned[at, cols], qx[kq], preferred_element_type=F32
+            mixed[rows, cols] = jnp.dot(
+                turned[rows, cols], qx[kq], preferred_element_type=F32
             ).astype(BF)
         if i == 0:
-            wait_all(cond_copies)
+            each_block(lambda copy: copy.wait())
         scr_copies[i].wait()
-        amp = jnp.dot(mixed[at, :], conds[...], preferred_element_type=F32)
-        kern[at, :] = (scrs[at, :].astype(F32) * amp * scale).astype(BF)
+        for m in range(mu // quad):
+            cols = slice(m * quad, (m + 1) * quad)
+            amp = jnp.dot(mixed[rows, :], conds[:, cols], preferred_element_type=F32)
+            kern[rows, cols] = (scrs[rows, cols].astype(F32) * amp * scale).astype(BF)
     row_copy.wait()
-    for i in range(mu // quad):
-        at = slice(i * quad, (i + 1) * quad)
-        folded[:, at] = jnp.dot(vals[...], kern[:, at], preferred_element_type=F32).astype(BF)
+    for m in range(mu // quad):
+        cols = slice(m * quad, (m + 1) * quad)
+        folded[:, cols] = jnp.dot(vals[...], kern[:, cols], preferred_element_type=F32).astype(BF)
     for kp in range(di_ref.shape[0]):
         at = slice(kp * LANES, (kp + 1) * LANES)
         di_ref[kp] = dot_nt(folded[at, :], conds[at, :])
@@ -285,8 +305,8 @@
 def exchange_kernel(cfg, chunk, scale, *refs):
     n_ka, n_band, k_dev = cfg
     k_points = n_ka * k_dev
-    rho_ref, di_ref, coul_ref, vown_ref = refs[:4]
-    cond_refs, refs = refs[4 : 4 + n_ka], refs[4 + n_ka :]
+    rho_ref, di_ref, coul_ref, vown_ref, refs = refs[0], refs[1], refs[2], refs[3], refs[4:]
+    cond_refs, refs = refs[:n_ka], refs[n_ka:]
     msg_ref, rhos, di, coul, conds, vown, part, msg, coul_sems, cond_sems, sems = refs
     own, npt = coul_ref.shape
     coul_copies = [
@@ -297,8 +317,8 @@
     ]
     rho_copy = pltpu.make_async_copy(rho_ref, rhos, sems.at[0])
     copies = block_copies([[ref] for ref in cond_refs], own, conds, cond_sems)
-    copies.append(pltpu.make_async_copy(di_ref, di, sems.at[1]))
-    copies.append(pltpu.make_async_copy(vown_ref, vown, sems.at[2]))
+    copies.append(pltpu.make_async_copy(vown_ref, vown, sems.at[1]))
+    copies.append(pltpu.make_async_copy(di_ref, di, sems.at[2]))
     start_all([rho_copy] + coul_copies + copies)
     rho_copy.wait()
     acc = jnp.zeros((own, LANES), F32)
@@ -324,18 +344,12 @@
                     piece = part[k // 2, pl.ds(d * 2 * ROWS + k % 2 * ROWS, ROWS), :]
                     piece = lane_half(piece, k % 2, kl % 2)
                     tile = piece if tile is None else tile + piece
-                to_ka = jnp.bitwise_xor(lax.axis_index("ka"), j)
-                to_band = jnp.bitwise_xor(lax.axis_index("band"), d)
-                msg[to_band, to_ka, pl.ds(g * ROWS, ROWS), :] = tile
+                msg[device_at(n_band, j, d), pl.ds(g * ROWS, ROWS), :] = tile
     msg_ref[...] = msg[...].astype(BF)
 
 
-def plane_sum_kernel(parts_ref, out_ref):
-    out_ref[...] = jnp.sum(parts_ref[...].astype(F32), axis=0)
-
-
 def received(recv_ref):
-    return jnp.sum(recv_ref[...], axis=0)
+    return jnp.sum(recv_ref[...].astype(F32), axis=0)
 
 
 def shifted(count_all, shift, square, cross_sum, square_sum):
@@ -437,15 +451,28 @@
     return lax.ppermute(block, axis, [(i, i ^ d) for i in range(lax.axis_size(axis))])
 
 
-def plane_pieces(own_piece):
+def line_gather(block, axis):
+    n = lax.axis_size(axis)
+    out = [block]
+    for way in (-1, 1):
+        moving = block
+        for hop in range(1, n):
+            pairs = [(i, i - way) for i in range(n) if 0 <= i + way * (hop - 1) < n and 0 <= i - way < n]
+            moving = lax.ppermute(moving, axis, pairs)
+            out.append(moving)
+    return out
+
+
+def plane_pieces(own_piece, others):
     def move(block, d):
         return swap(block, "band", d)
 
     half = own_piece.shape[0] // 2
-    by_x, by_y = move(own_piece, 2), move(own_piece, 4)
+    core, by_x, by_y = move(own_piece, 1), move(own_piece, 2), move(own_piece, 4)
+    by_x, by_y, others = lax.optimization_barrier((by_x, by_y, others))
     diag = [move(by_x[:half], 4), move(by_y[half:], 2)]
-    pieces = [[own_piece], [move(own_piece, 1)], [by_x], [move(by_x, 1)], [by_y], [move(by_y, 1)]]
-    return pieces + [diag, [move(part, 1) for part in diag]]
+    pieces = [[own_piece], [core], [by_x], [move(by_x, 1)], [by_y], [move(by_y, 1)]]
+    return pieces + [diag, [move(part, 1) for part in diag]], others
 
 
 def kernel_path(start_vec, val_energy, cond_energy, val_orb, cond_orb, coulomb, screened):
@@ -465,18 +492,18 @@
     scale = 1.0 / (npt_all * math.sqrt(count_all))
     piece_rows = k_points * nv_blk
 
-    cond_local = lax.dynamic_slice_in_dim(cond_orb, band * mu_blk, mu_blk, 2)
-    cond_pts = lax.all_gather(
-        cond_local.reshape(k_dev * n_cond, mu_blk), "ka", axis=0, tiled=True
-    )
-
     def val_to(j):
         part = lax.dynamic_slice_in_dim(val_orb, jnp.bitwise_xor(ka, j) * nu_blk, nu_blk, 2)
         return part.reshape(k_dev * nv_blk, nu_blk)
 
-    val_cut = jnp.concatenate(
-        [val_to(0)] + [swap(val_to(j), "ka", j) for j in range(1, n_ka)], axis=0
-    )
+    val_parts = [val_to(0)] + [swap(val_to(j), "ka", j) for j in range(1, n_ka)]
+    val_cut = jnp.concatenate(val_parts, axis=0)
+    half = mu_blk // 2
+    cond_halves = []
+    for h in range(2):
+        cut = lax.dynamic_slice_in_dim(cond_orb, band * mu_blk + h * half, half, 2)
+        cond_halves.append(line_gather(cut.reshape(k_dev * n_cond, half), "ka"))
+    cond_pts = [ref for pair in zip(*cond_halves) for ref in pair]
     gap = (cond_energy[:, None, :] - val_energy[:, :, None]).reshape(k_dev, nv_blk * n_cond)
     gap = pack_vector(gap, k_dev)
 
@@ -498,22 +525,20 @@
         + [dma(2 * nu_blk // tile)] * 2,
         moved=8 * MIB,
     )(screened)
-    val_cut, msgs, scr_turned = lax.optimization_barrier((val_cut, msgs, scr_turned))
-    pieces = plane_pieces(val_cut)
-    counts = tuple(len(piece) for piece in pieces)
-    flat = [ref for piece in pieces for ref in piece]
-    n_copies = len(flat)
     own_rows = k_dev * n_cond
     cuts = call(
         cut_kernel,
         "cut",
         (shape_of((own_rows, own), BF),) * n_ka,
-        [ANY, ANY],
+        [ANY],
         (ANY,) * n_ka,
         [dma(n_ka * k_dev)],
-        mib=8,
-    )(cond_orb, val_cut)
+    )(cond_orb)
     cond_own = [cuts[0]] + [swap(cuts[j], "ka", j) for j in range(1, n_ka)]
+    pieces, (msgs, cond_own, scr_turned) = plane_pieces(val_cut, (msgs, cond_own, scr_turned))
+    counts = tuple(len(piece) for piece in pieces)
+    flat = [ref for piece in pieces for ref in piece]
+    n_copies = len(flat)
 
     val_rows, val_turned, val_own = call(
         functools.partial(order_kernel, counts),
@@ -561,29 +586,29 @@
             functools.partial(direct_kernel, n_ka, tile, scale),
             "direct",
             shape_of((pairs, LANES, LANES)),
-            [ANY] * 5,
+            [ANY] * (4 + len(cond_pts)),
             VMEM,
             [
                 pltpu.VMEM((quads, 2 * LANES, 2 * LANES), BF),
+                pltpu.VMEM((nu_blk, rows_all), BF),
                 pltpu.VMEM((conds_all, mu_blk), BF),
                 pltpu.VMEM((nu_blk, mu_blk), BF),
-                pltpu.VMEM((nu_blk, rows_all), BF),
                 pltpu.VMEM((rows_all, nu_blk), BF),
                 pltpu.VMEM((nu_blk, conds_all), BF),
                 pltpu.VMEM((nu_blk, mu_blk), BF),
                 pltpu.VMEM((rows_all, mu_blk), BF),
                 dma(1),
-                dma(n_ka),
+                dma(len(cond_pts) // 2, 2),
                 dma(1),
                 dma(2, nu_blk // tile),
             ],
             flops=4 * mu_blk * nu_blk * conds_all,
             moved=12 * MIB,
-        )(qx, cond_pts, scr_turned, val_turned, val_rows)
+        )(val_turned, scr_turned, val_rows, qx, *cond_pts)
         parts = call(
             functools.partial(exchange_kernel, cfg, chunk, scale),
             "exchange",
-            shape_of((n_band, n_ka) + block, BF),
+            msg_shape,
             [ANY] * (4 + n_ka),
             VMEM,
             [
@@ -593,17 +618,13 @@
                 pltpu.VMEM((n_ka, own_rows, own), BF),
                 pltpu.VMEM((rows_all, own), BF),
                 pltpu.VMEM((pairs, LANES, LANES), F32),
-                pltpu.VMEM((n_band, n_ka) + block, F32),
+                pltpu.VMEM((devices,) + block, F32),
                 dma(npt_all // chunk),
                 dma(n_ka),
                 dma(3),
             ],
         )(density, direct, coulomb, val_own, *cond_own)
-        parts = lax.all_to_all(parts, "band", split_axis=0, concat_axis=0, tiled=True)
-        plane = call(
-            plane_sum_kernel, "plane_sum", shape_of((n_ka,) + block), [VMEM], VMEM, mib=8
-        )(parts)
-        recv = lax.all_to_all(plane, "ka", split_axis=0, concat_axis=0, tiled=True)
+        recv = exchange_all(parts)
         if first:
             state, coef, message = call(
                 functools.partial(first_owner_kernel, count_all),
@@ -724,7 +745,7 @@
         and start_vec.shape[0] * n_ka % 4 == 0
         and coulomb.shape[0] % LANES == 0
         and coulomb.shape[1] % 1024 == 0
-        and screened.shape[0] % 256 == 0
+        and screened.shape[0] % 512 == 0
         and screened.shape[1] % 1024 == 0
         and screened.shape[0] * screened.shape[1] <= 2 * MIB
     )

time: 192 us -> 187 us (0.974)
  starting transfers between devices: 33.1 us -> 49.2 us
  between operations: 14.5 us -> 1.66 us
  Pallas kernels: 51.9 us -> 64.5 us
  blocking collectives: 57.7 us -> 46.9 us
  waiting for transfers between devices: 21.6 us -> 16.5 us
  local copies, waits for them, and re-layouts: 10.3 us -> 7.76 us
    all_to_all x4 -> x0, blocking collectives: 38.8 us -> none  [the longest x2 20.3 us: kernel_path(): recv = lax.all_to_all(plane, 'ka', split_axis=0, concat_axis=0, tiled=True)]
    all_to_all x2 -> x4, blocking collectives: 18.9 us -> 46.9 us  [exchange_all(): return lax.all_to_all(parts, AXES, split_axis=0, concat_axis=0, tiled=True)]
    ppermute x0 -> x12, starting transfers between devices: none -> 18.4 us  [line_gather(): moving = lax.ppermute(moving, axis, pairs)]
    pallas_call x5 -> x3, Pallas kernels: 8.53 us -> 21.4 us  [the longest x1 13.1 us: kernel_path(): call(cut_kernel, 'cut', (shape_of((own_rows, own), BF),) * n_ka, [ANY], (...]
    ppermute x0 -> x12, waiting for transfers between devices: none -> 10.7 us  [line_gather(): moving = lax.ppermute(moving, axis, pairs)]
    all_to_all x3, waiting for transfers between devices: 7.98 us -> 0.01 us  [exchange_all(): return lax.all_to_all(parts, AXES, split_axis=0, concat_axis=0, tiled=True)]
    ppermute x15, waiting for transfers between devices: 13.6 us -> 5.84 us  [swap(): lax.ppermute(block, axis, [(i, i ^ d) for i in range(lax.axis_size(axis))])]
    unnamed x56 -> x78, local copies, waits for them, and re-layouts: 6.51 us -> 5.35 us
  transfers between devices with their start and end apart: 19 -> 30, of which waited for: 6 -> 5; matrix products, arithmetic and copies ran while one was open for 2% -> 1% of each run, Pallas kernels for 20% -> 27%
where the time goes in v7:
time: 187 us
  Pallas kernels  64.5 us (34%)
  starting transfers between devices  49.2 us (26%)
  blocking collectives  46.9 us (25%)
  waiting for transfers between devices  16.5 us (9%)
  local copies, waits for them, and re-layouts  7.76 us (4%)
    all_to_all x4, blocking collectives, exchange_all(): return lax.all_to_all(parts, AXES, split_axis=0, concat_axis=0, tiled=True)  46.9 us
    pallas_call x2, Pallas kernels, kernel_path(): call(functools.partial(direct_kernel, n_ka, tile, scale), 'direct', shape...  26.8 us
    ppermute x12, starting transfers between devices, line_gather(): moving = lax.ppermute(moving, axis, pairs)  18.4 us
    ppermute x15, starting transfers between devices, swap(): lax.ppermute(block, axis, [(i, i ^ d) for i in range(lax.axis_size(axis))])  18.3 us
    pallas_call x1, Pallas kernels, kernel_path(): call(cut_kernel, 'cut', (shape_of((own_rows, own), BF),) * n_ka, [ANY], (...  13.1 us
    all_to_all x3, starting transfers between devices, exchange_all(): return lax.all_to_all(parts, AXES, split_axis=0, concat_axis=0, tiled=True)  12.4 us
    ppermute x12, waiting for transfers between devices, line_gather(): moving = lax.ppermute(moving, axis, pairs)  10.7 us
    pallas_call x2, Pallas kernels, kernel_path(): call(functools.partial(exchange_kernel, cfg, chunk, scale), 'exchange', m...  8.22 us
  transfers between devices with their start and end apart: 30, of which 5 were waited for; matrix products, arithmetic and copies ran while one was open for 1% of the time, Pallas kernels for 27%

profile of v7, /device:TPU:0, one launch (start us, length us, event | category | flops | bytes accessed | tf_op | source)
XLA Modules:
  0.0 186.6 jit_solution(14755846717027589332)
XLA Ops:
  0.7 1.1 dynamic-slice_bitcast_fusion.3
  1.8 5.1 %collective-permute-start.2 = (bf16[24,2048]{1,0:T(8,128)(2,1)S(1)}, bf16[24,2048]{1,0:T(8,128)(2,1)S(1)}, u32[]{:S(2)}, u32[]{:S(2)}) collective-permute-start(bf16[24,2048]{1,0:T(8,128)(2,1)S(1)} %get-tuple-element.60), channel_id=1, source_target_pairs={{0,24},{8,16},{16,8},{24,0},{1,25},{9,17},{17,9},{25,1},{2,26},{10... | collective-permute-start | bytes 294920 | tf_op jit(solution)/shard_map/ppermute | solution.py:451
  7.5 1.0 constant_dynamic-slice_fusion
  8.6 3.3 %collective-permute-start.15 = (bf16[192,512]{1,0:T(8,128)(2,1)S(1)}, bf16[192,512]{1,0:T(8,128)(2,1)S(1)}, u32[]{:S(2)}, u32[]{:S(2)}) collective-permute-start(bf16[192,512]{1,0:T(8,128)(2,1)S(1)} %bitcast.15), channel_id=1, source_target_pairs={{0,8},{8,16},{16,24},{1,9},{9,17},{17,25},{2,10},{10,18},{18,26},{... | collective-permute-start | bytes 589832 | tf_op jit(solution)/shard_map/ppermute | solution.py:461
  11.9 1.3 collective-permute-start.21
  13.2 13.1 %cut.1 = (bf16[192,256]{1,0:T(8,128)(2,1)}, bf16[192,256]{1,0:T(8,128)(2,1)}, bf16[192,256]{1,0:T(8,128)(2,1)}, bf16[192,256]{1,0:T(8,128)(2,1)}) custom-call(bf16[3,64,8192]{2,1,0:T(8,128)(2,1)} %cond_ref.1), custom_call_target="tpu_custom_call" | custom-call | tf_op jit(solution)/shard_map/cut/pallas_call | solution.py:529
  26.4 2.7 %collective-permute-start.5 = (bf16[192,256]{1,0:T(8,128)(2,1)}, bf16[192,256]{1,0:T(8,128)(2,1)S(1)}, u32[]{:S(2)}, u32[]{:S(2)}) collective-permute-start(bf16[192,256]{1,0:T(8,128)(2,1)} %get-tuple-element.31), channel_id=1, source_target_pairs={{0,8},{8,0},{16,24},{24,16},{1,9},{9,1},{17,25},{25,17},{2,10},{10... | collective-permute-start | bytes 294920 | tf_op jit(solution)/shard_map/ppermute | solution.py:451
  29.1 2.9 %collective-permute-start.6 = (bf16[192,256]{1,0:T(8,128)(2,1)}, bf16[192,256]{1,0:T(8,128)(2,1)S(1)}, u32[]{:S(2)}, u32[]{:S(2)}) collective-permute-start(bf16[192,256]{1,0:T(8,128)(2,1)} %get-tuple-element.32), channel_id=1, source_target_pairs={{0,16},{8,24},{16,0},{24,8},{1,17},{9,25},{17,1},{25,9},{2,18},{10... | collective-permute-start | bytes 294920 | tf_op jit(solution)/shard_map/ppermute | solution.py:451
  32.0 0.7 collective-permute-done.5.refs_3_.refs_5_
  32.7 4.0 %collective-permute-start.16 = (bf16[192,512]{1,0:T(8,128)(2,1)S(1)}, bf16[192,512]{1,0:T(8,128)(2,1)S(1)}, u32[]{:S(2)}, u32[]{:S(2)}) collective-permute-start(bf16[192,512]{1,0:T(8,128)(2,1)S(1)} %bitcast.11), channel_id=1, source_target_pairs={{0,8},{8,16},{16,24},{1,9},{9,17},{17,25},{2,10},{10,18},{18,26},{... | collective-permute-start | bytes 589832 | tf_op jit(solution)/shard_map/ppermute | solution.py:461
  36.7 0.8 collective-permute-done.6.refs_4_.refs_6_
  37.5 1.3 collective-permute-start.22
  38.8 1.6 collective-permute-start.3
  40.4 1.5 collective-permute-start.4
  42.3 0.9 pack.1
  43.2 4.7 %all-to-all-start = ((bf16[32,16,128]{2,1,0:T(8,128)(2,1)}), bf16[32,16,128]{2,1,0:T(8,128)(2,1)S(1)}, u32[]{:S(2)}, u32[]{:S(2)}) async-start(bf16[32,16,128]{2,1,0:T(8,128)(2,1)} %get-tuple-element.29), calls=%async_computation | async-start | bytes 262144 | tf_op jit(solution)/shard_map/all_to_all | solution.py:30
  47.8 0.7 collective-permute-start.17
  48.5 1.3 collective-permute-start.18
  49.9 1.3 collective-permute-start.23
  51.2 3.7 %turn.1.refs_1_ = bf16[2048,1024]{1,0:T(8,128)(2,1)} custom-call(bf16[1024,2048]{1,0:T(8,128)(2,1)} %scr_ref.1), custom_call_target="tpu_custom_call" | custom-call | bytes 8388608 | tf_op jit(solution)/shard_map/turn/pallas_call | solution.py:518
  55.0 1.3 collective-permute-start.24
  57.3 6.5 %collective-permute-done.23.refs_14_ = bf16[192,512]{1,0:T(8,128)(2,1)} collective-permute-done((bf16[192,512]{1,0:T(8,128)(2,1)S(1)}, bf16[192,512]{1,0:T(8,128)(2,1)}, u32[]{:S(2)}, u32[]{:S(2)}) %collective-permute-start.23) | collective-permute-done | bytes 196640 | tf_op jit(solution)/shard_map/ppermute | solution.py:461
  63.8 1.5 collective-permute-start.11
  65.3 4.1 %collective-permute-done.24.refs_15_ = bf16[192,512]{1,0:T(8,128)(2,1)S(1)} collective-permute-done((bf16[192,512]{1,0:T(8,128)(2,1)S(1)}, bf16[192,512]{1,0:T(8,128)(2,1)S(1)}, u32[]{:S(2)}, u32[]{:S(2)}) %collective-permute-start.24) | collective-permute-done | bytes 196640 | tf_op jit(solution)/shard_map/ppermute | solution.py:461
  69.4 1.5 collective-permute-start.12
  70.9 4.3 %collective-permute-done.12.refs_7_ = bf16[48,2048]{1,0:T(8,128)(2,1)S(1)} collective-permute-done((bf16[48,2048]{1,0:T(8,128)(2,1)S(1)}, bf16[48,2048]{1,0:T(8,128)(2,1)S(1)}, u32[]{:S(2)}, u32[]{:S(2)}) %collective-permute-start.12) | collective-permute-done | bytes 196640 | tf_op jit(solution)/shard_map/ppermute | solution.py:451
  75.2 0.7 collective-permute-start.19
  76.6 1.3 collective-permute-start.25
  78.0 1.3 collective-permute-start.26
  80.0 5.0 %order.1 = (bf16[768,2048]{1,0:T(8,128)(2,1)}, bf16[2048,768]{1,0:T(8,128)(2,1)}, bf16[768,256]{1,0:T(8,128)(2,1)}) custom-call(bf16[96,2048]{1,0:T(8,128)(2,1)} %copy-done.13, bf16[96,2048]{1,0:T(8,128)(2,1)} %copy-done.16, bf16[96,2048]{1,0:T(8,128)(2,1)} %copy-done.14, bf16[96,2048]{1,0:T(8,128)(2,1)} %copy-done.17, bf16[96,2048]{1,0:T(8,128)(2,1)} %copy-done.15, ...), custom_call_target="tpu_custom_call" | custom-call | bytes 9437184 | tf_op jit(solution)/shard_map/order/pallas_call | solution.py:543
  85.1 1.0 copy-done
  86.1 1.6 density.2
  87.7 0.8 copy-done.12
  88.4 5.1 %all-to-all-start.1 = ((f32[32,2,128]{2,1,0:T(2,128)}), f32[32,2,128]{2,1,0:T(2,128)S(1)}, u32[]{:S(2)}, u32[]{:S(2)}) async-start(f32[32,2,128]{2,1,0:T(2,128)} %get-tuple-element.42), calls=%async_computation.1 | async-start | bytes 65536 | tf_op jit(solution)/shard_map/all_to_all | solution.py:30
  94.4 13.4 %direct.2.refs_1_ = f32[6,128,128]{2,1,0:T(8,128)} custom-call(bf16[2048,768]{1,0:T(8,128)(2,1)} %get-tuple-element.43.refs_0_, bf16[2048,1024]{1,0:T(8,128)(2,1)} %turn.1.refs_1_, bf16[768,2048]{1,0:T(8,128)(2,1)} %get-tuple-element.45.refs_2_, bf16[3,256,256]{2,1,0:T(8,128)(2,1)} %copy-done.12, bf16[192,512]{1,0:T(8,128)(2,1)} %bitcast.17, ...), custom_call_target="tpu_custom_call" | custom-call | flops 6442450944 | bytes 12582912 | tf_op jit(solution)/shard_map/direct/pallas_call | solution.py:585
  108.5 4.1 %exchange.2 = bf16[32,16,128]{2,1,0:T(8,128)(2,1)} custom-call(f32[32,2,128]{2,1,0:T(2,128)} %copy-done.26, f32[6,128,128]{2,1,0:T(8,128)} %direct.2.refs_1_, bf16[256,8192]{1,0:T(8,128)(2,1)} %refs_2_.3, bf16[768,256]{1,0:T(8,128)(2,1)} %get-tuple-element.37.refs_1_.refs_3_, bf16[192,256]{1,0:T(8,128)(2,1)} %get-tuple-element.38.refs_2_.refs_4_, ...), custom_call_target="tpu_custom_call" | custom-call | tf_op jit(solution)/shard_map/exchange/pallas_call | solution.py:608
  112.6 14.0 %all_to_all.35.recv_ref = bf16[32,16,128]{2,1,0:T(8,128)(2,1)S(1)} all-to-all(bf16[32,16,128]{2,1,0:T(8,128)(2,1)} %exchange.2), channel_id=1, replica_groups=mesh['ka'=4,'band'=8] {'ka','band'}, dimensions={0} | all-to-all | bytes 262144 | tf_op jit(solution)/shard_map/all_to_all | solution.py:30
  126.6 0.8 first_owner.1
  127.4 10.0 %all_to_all.36.refs_0_.msgs_ref = bf16[32,16,128]{2,1,0:T(8,128)(2,1)S(1)} all-to-all(bf16[32,16,128]{2,1,0:T(8,128)(2,1)S(1)} %get-tuple-element.48), channel_id=1, replica_groups=mesh['ka'=4,'band'=8] {'ka','band'}, dimensions={0} | all-to-all | bytes 262144 | tf_op jit(solution)/shard_map/all_to_all | solution.py:30
  137.5 1.6 density.3
  139.1 0.8 copy-done.11
  139.8 2.7 %all-to-all-start.4 = ((f32[32,2,128]{2,1,0:T(2,128)}), f32[32,2,128]{2,1,0:T(2,128)S(1)}, u32[]{:S(2)}, u32[]{:S(2)}) async-start(f32[32,2,128]{2,1,0:T(2,128)} %get-tuple-element.49), calls=%async_computation.4 | async-start | bytes 65536 | tf_op jit(solution)/shard_map/all_to_all | solution.py:30
  142.6 13.4 %direct.3.refs_1_ = f32[6,128,128]{2,1,0:T(8,128)} custom-call(bf16[2048,768]{1,0:T(8,128)(2,1)} %get-tuple-element.43.refs_0_, bf16[2048,1024]{1,0:T(8,128)(2,1)} %turn.1.refs_1_, bf16[768,2048]{1,0:T(8,128)(2,1)} %get-tuple-element.45.refs_2_, bf16[3,256,256]{2,1,0:T(8,128)(2,1)} %copy-done.11, bf16[192,512]{1,0:T(8,128)(2,1)} %bitcast.18, ...), custom_call_target="tpu_custom_call" | custom-call | flops 6442450944 | bytes 12582912 | tf_op jit(solution)/shard_map/direct/pallas_call | solution.py:585
  156.6 4.1 %exchange.3 = bf16[32,16,128]{2,1,0:T(8,128)(2,1)} custom-call(f32[32,2,128]{2,1,0:T(2,128)} %copy-done.25, f32[6,128,128]{2,1,0:T(8,128)} %direct.3.refs_1_, bf16[256,8192]{1,0:T(8,128)(2,1)} %refs_2_.3, bf16[768,256]{1,0:T(8,128)(2,1)} %get-tuple-element.37.refs_1_.refs_3_, bf16[192,256]{1,0:T(8,128)(2,1)} %get-tuple-element.38.refs_2_.refs_4_, ...), custom_call_target="tpu_custom_call" | custom-call | tf_op jit(solution)/shard_map/exchange/pallas_call | solution.py:608
  160.8 13.9 %all_to_all.37.recv_ref = bf16[32,16,128]{2,1,0:T(8,128)(2,1)S(1)} all-to-all(bf16[32,16,128]{2,1,0:T(8,128)(2,1)} %exchange.3), channel_id=1, replica_groups=mesh['ka'=4,'band'=8] {'ka','band'}, dimensions={0} | all-to-all | bytes 262144 | tf_op jit(solution)/shard_map/all_to_all | solution.py:30
  174.7 1.3 second_owner.1
  176.0 9.0 %all_to_all.38.msgs_ref = f32[32,2,128]{2,1,0:T(2,128)S(1)} all-to-all(f32[32,2,128]{2,1,0:T(2,128)S(1)} %get-tuple-element.53), channel_id=1, replica_groups=mesh['ka'=4,'band'=8] {'ka','band'}, dimensions={0} | all-to-all | bytes 65536 | tf_op jit(solution)/shard_map/all_to_all | solution.py:30
  185.1 1.3 finish.1
  (118 shorter events, 5.5 us)
Async XLA Ops:
  0.6 41.3 %copy-start.27 = (f32[3,8]{1,0:T(4,128)S(1)}, f32[3,8]{1,0:T(4,128)}, u32[]{:S(2)}) copy-start(f32[3,8]{1,0:T(4,128)} %param.8) | copy-start | bytes 292
  0.6 41.3 %copy-start.28 = (f32[3,64]{1,0:T(4,128)S(1)}, f32[3,64]{1,0:T(4,128)}, u32[]{:S(2)}) copy-start(f32[3,64]{1,0:T(4,128)} %param.9) | copy-start | bytes 2308
  0.7 41.6 %copy-start.10 = (f32[3,512]{1,0:T(4,128)S(1)}, f32[3,512]{1,0:T(4,128)}, u32[]{:S(2)}) copy-start(f32[3,512]{1,0:T(4,128)} %start_ref.1) | copy-start | bytes 18436
  1.8 24.6 %collective-permute-start.2 = (bf16[24,2048]{1,0:T(8,128)(2,1)S(1)}, bf16[24,2048]{1,0:T(8,128)(2,1)S(1)}, u32[]{:S(2)}, u32[]{:S(2)}) collective-permute-start(bf16[24,2048]{1,0:T(8,128)(2,1)S(1)} %get-tuple-element.60), channel_id=1, source_target_pairs={{0,24},{8,16},{16,8},{24,0},{1,25},{9,17},{17,9},{25,1},{2,26},{10... | collective-permute-start | bytes 294920 | tf_op jit(solution)/shard_map/ppermute | solution.py:451
  6.9 22.2 %collective-permute-start.1 = (bf16[24,2048]{1,0:T(8,128)(2,1)S(1)}, bf16[24,2048]{1,0:T(8,128)(2,1)S(1)}, u32[]{:S(2)}, u32[]{:S(2)}) collective-permute-start(bf16[24,2048]{1,0:T(8,128)(2,1)S(1)} %get-tuple-element.61), channel_id=1, source_target_pairs={{0,16},{8,24},{16,0},{24,8},{1,17},{9,25},{17,1},{25,9},{2,18},{10... | collective-permute-start | bytes 294920 | tf_op jit(solution)/shard_map/ppermute | solution.py:451
  6.9 25.1 %collective-permute-start = (bf16[24,2048]{1,0:T(8,128)(2,1)S(1)}, bf16[24,2048]{1,0:T(8,128)(2,1)S(1)}, u32[]{:S(2)}, u32[]{:S(2)}) collective-permute-start(bf16[24,2048]{1,0:T(8,128)(2,1)S(1)} %get-tuple-element.59), channel_id=1, source_target_pairs={{0,8},{8,0},{16,24},{24,16},{1,9},{9,1},{17,25},{25,17},{2,10},{10... | collective-permute-start | bytes 294920 | tf_op jit(solution)/shard_map/ppermute | solution.py:451
  8.6 46.3 %copy-start.23 = (bf16[3,64,512]{2,1,0:T(8,128)(2,1)}, bf16[3,64,512]{2,1,0:T(8,128)(2,1)S(1)}, u32[]{:S(2)}) copy-start(bf16[3,64,512]{2,1,0:T(8,128)(2,1)S(1)} %get-tuple-element.56) | copy-start | bytes 589828
  8.6 46.3 %copy-start.24 = (bf16[3,64,512]{2,1,0:T(8,128)(2,1)}, bf16[3,64,512]{2,1,0:T(8,128)(2,1)S(1)}, u32[]{:S(2)}) copy-start(bf16[3,64,512]{2,1,0:T(8,128)(2,1)S(1)} %get-tuple-element.57) | copy-start | bytes 589828
  8.6 31.8 %collective-permute-start.15 = (bf16[192,512]{1,0:T(8,128)(2,1)S(1)}, bf16[192,512]{1,0:T(8,128)(2,1)S(1)}, u32[]{:S(2)}, u32[]{:S(2)}) collective-permute-start(bf16[192,512]{1,0:T(8,128)(2,1)S(1)} %bitcast.15), channel_id=1, source_target_pairs={{0,8},{8,16},{16,24},{1,9},{9,17},{17,25},{2,10},{10,18},{18,26},{... | collective-permute-start | bytes 589832 | tf_op jit(solution)/shard_map/ppermute | solution.py:461
  11.9 36.6 %collective-permute-start.21 = (bf16[192,512]{1,0:T(8,128)(2,1)S(1)}, bf16[192,512]{1,0:T(8,128)(2,1)S(1)}, u32[]{:S(2)}, u32[]{:S(2)}) collective-permute-start(bf16[192,512]{1,0:T(8,128)(2,1)S(1)} %bitcast.16), channel_id=1, source_target_pairs={{8,0},{16,8},{24,16},{9,1},{17,9},{25,17},{10,2},{18,10},{26,18},{... | collective-permute-start | bytes 589832 | tf_op jit(solution)/shard_map/ppermute | solution.py:461
  26.4 6.4 %collective-permute-start.5 = (bf16[192,256]{1,0:T(8,128)(2,1)}, bf16[192,256]{1,0:T(8,128)(2,1)S(1)}, u32[]{:S(2)}, u32[]{:S(2)}) collective-permute-start(bf16[192,256]{1,0:T(8,128)(2,1)} %get-tuple-element.31), channel_id=1, source_target_pairs={{0,8},{8,0},{16,24},{24,16},{1,9},{9,1},{17,25},{25,17},{2,10},{10... | collective-permute-start | bytes 294920 | tf_op jit(solution)/shard_map/ppermute | solution.py:451
  29.1 8.5 %collective-permute-start.6 = (bf16[192,256]{1,0:T(8,128)(2,1)}, bf16[192,256]{1,0:T(8,128)(2,1)S(1)}, u32[]{:S(2)}, u32[]{:S(2)}) collective-permute-start(bf16[192,256]{1,0:T(8,128)(2,1)} %get-tuple-element.32), channel_id=1, source_target_pairs={{0,16},{8,24},{16,0},{24,8},{1,17},{9,25},{17,1},{25,9},{2,18},{10... | collective-permute-start | bytes 294920 | tf_op jit(solution)/shard_map/ppermute | solution.py:451
  32.0 6.8 %collective-permute-start.7 = (bf16[192,256]{1,0:T(8,128)(2,1)}, bf16[192,256]{1,0:T(8,128)(2,1)S(1)}, u32[]{:S(2)}, u32[]{:S(2)}) collective-permute-start(bf16[192,256]{1,0:T(8,128)(2,1)} %get-tuple-element.33), channel_id=1, source_target_pairs={{0,24},{8,16},{16,8},{24,0},{1,25},{9,17},{17,9},{25,1},{2,26},{10... | collective-permute-start | bytes 294920 | tf_op jit(solution)/shard_map/ppermute | solution.py:451
  32.0 24.3 %copy-start.13 = (bf16[96,2048]{1,0:T(8,128)(2,1)}, bf16[96,2048]{1,0:T(8,128)(2,1)S(1)}, u32[]{:S(2)}) copy-start(bf16[96,2048]{1,0:T(8,128)(2,1)S(1)} %pad_maximum_fusion.refs_0_) | copy-start | bytes 1179652
  32.7 52.3 %copy-start.4 = (bf16[192,256]{1,0:T(8,128)(2,1)}, bf16[192,256]{1,0:T(8,128)(2,1)S(1)}, u32[]{:S(2)}) copy-start(bf16[192,256]{1,0:T(8,128)(2,1)S(1)} %collective-permute-done.5.refs_3_.refs_5_) | copy-start | bytes 294916
  32.7 15.1 %collective-permute-start.16 = (bf16[192,512]{1,0:T(8,128)(2,1)S(1)}, bf16[192,512]{1,0:T(8,128)(2,1)S(1)}, u32[]{:S(2)}, u32[]{:S(2)}) collective-permute-start(bf16[192,512]{1,0:T(8,128)(2,1)S(1)} %bitcast.11), channel_id=1, source_target_pairs={{0,8},{8,16},{16,24},{1,9},{9,17},{17,25},{2,10},{10,18},{18,26},{... | collective-permute-start | bytes 589832 | tf_op jit(solution)/shard_map/ppermute | solution.py:461
  37.5 47.5 %copy-start.6 = (bf16[192,256]{1,0:T(8,128)(2,1)}, bf16[192,256]{1,0:T(8,128)(2,1)S(1)}, u32[]{:S(2)}) copy-start(bf16[192,256]{1,0:T(8,128)(2,1)S(1)} %collective-permute-done.6.refs_4_.refs_6_) | copy-start | bytes 294916
  37.5 12.4 %collective-permute-start.22 = (bf16[192,512]{1,0:T(8,128)(2,1)S(1)}, bf16[192,512]{1,0:T(8,128)(2,1)S(1)}, u32[]{:S(2)}, u32[]{:S(2)}) collective-permute-start(bf16[192,512]{1,0:T(8,128)(2,1)S(1)} %bitcast.12), channel_id=1, source_target_pairs={{8,0},{16,8},{24,16},{9,1},{17,9},{25,17},{10,2},{18,10},{26,18},{... | collective-permute-start | bytes 589832 | tf_op jit(solution)/shard_map/ppermute | solution.py:461
  38.8 46.2 %copy-start.8 = (bf16[192,256]{1,0:T(8,128)(2,1)}, bf16[192,256]{1,0:T(8,128)(2,1)S(1)}, u32[]{:S(2)}) copy-start(bf16[192,256]{1,0:T(8,128)(2,1)S(1)} %collective-permute-done.7.refs_5_.refs_7_) | copy-start | bytes 294916
  38.8 16.1 %collective-permute-start.3 = (bf16[96,2048]{1,0:T(8,128)(2,1)S(1)}, bf16[96,2048]{1,0:T(8,128)(2,1)S(1)}, u32[]{:S(2)}, u32[]{:S(2)}) collective-permute-start(bf16[96,2048]{1,0:T(8,128)(2,1)S(1)} %pad_maximum_fusion.refs_0_), channel_id=1, source_target_pairs={{0,2},{1,3},{2,0},{3,1},{4,6},{5,7},{6,4},{7,5},{8,10},{9,11},{10,... | collective-permute-start | bytes 1179656 | tf_op jit(solution)/shard_map/ppermute | solution.py:451
  40.4 15.9 %collective-permute-start.4 = (bf16[96,2048]{1,0:T(8,128)(2,1)S(1)}, bf16[96,2048]{1,0:T(8,128)(2,1)S(1)}, u32[]{:S(2)}, u32[]{:S(2)}) collective-permute-start(bf16[96,2048]{1,0:T(8,128)(2,1)S(1)} %pad_maximum_fusion.refs_0_), channel_id=1, source_target_pairs={{0,4},{1,5},{2,6},{3,7},{4,0},{5,1},{6,2},{7,3},{8,12},{9,13},{10,... | collective-permute-start | bytes 1179656 | tf_op jit(solution)/shard_map/ppermute | solution.py:451
  43.2 13.5 %all-to-all-start = ((bf16[32,16,128]{2,1,0:T(8,128)(2,1)}), bf16[32,16,128]{2,1,0:T(8,128)(2,1)S(1)}, u32[]{:S(2)}, u32[]{:S(2)}) async-start(bf16[32,16,128]{2,1,0:T(8,128)(2,1)} %get-tuple-element.29), calls=%async_computation | async-start | bytes 262144 | tf_op jit(solution)/shard_map/all_to_all | solution.py:30
  47.8 8.8 %collective-permute-start.17 = (bf16[192,512]{1,0:T(8,128)(2,1)S(1)}, bf16[192,512]{1,0:T(8,128)(2,1)S(1)}, u32[]{:S(2)}, u32[]{:S(2)}) collective-permute-start(bf16[192,512]{1,0:T(8,128)(2,1)S(1)} %collective-permute-done.15.refs_6_), channel_id=1, source_target_pairs={{8,16},{16,24},{9,17},{17,25},{10,18},{18,26},{11,19},{19,27},{12,... | collective-permute-start | bytes 589832 | tf_op jit(solution)/shard_map/ppermute | solution.py:461
  48.5 8.5 %collective-permute-start.18 = (bf16[192,512]{1,0:T(8,128)(2,1)S(1)}, bf16[192,512]{1,0:T(8,128)(2,1)}, u32[]{:S(2)}, u32[]{:S(2)}) collective-permute-start(bf16[192,512]{1,0:T(8,128)(2,1)S(1)} %collective-permute-done.16.refs_7_), channel_id=1, source_target_pairs={{8,16},{16,24},{9,17},{17,25},{10,18},{18,26},{11,19},{19,27},{12,... | collective-permute-start | bytes 589832 | tf_op jit(solution)/shard_map/ppermute | solution.py:461
  49.9 13.9 %collective-permute-start.23 = (bf16[192,512]{1,0:T(8,128)(2,1)S(1)}, bf16[192,512]{1,0:T(8,128)(2,1)}, u32[]{:S(2)}, u32[]{:S(2)}) collective-permute-start(bf16[192,512]{1,0:T(8,128)(2,1)S(1)} %collective-permute-done.21.refs_12_), channel_id=1, source_target_pairs={{8,0},{16,8},{9,1},{17,9},{10,2},{18,10},{11,3},{19,11},{12,4},{20... | collective-permute-start | bytes 589832 | tf_op jit(solution)/shard_map/ppermute | solution.py:461
  54.9 30.1 %copy-start.2 = (bf16[192,256]{1,0:T(8,128)(2,1)S(1)}, bf16[192,256]{1,0:T(8,128)(2,1)}, u32[]{:S(2)}) copy-start(bf16[192,256]{1,0:T(8,128)(2,1)} %get-tuple-element.38.refs_2_.refs_4_) | copy-start | bytes 294916
  55.0 24.3 %copy-start.14 = (bf16[96,2048]{1,0:T(8,128)(2,1)}, bf16[96,2048]{1,0:T(8,128)(2,1)S(1)}, u32[]{:S(2)}) copy-start(bf16[96,2048]{1,0:T(8,128)(2,1)S(1)} %collective-permute-done.3.refs_2_) | copy-start | bytes 1179652
  55.0 14.4 %collective-permute-start.24 = (bf16[192,512]{1,0:T(8,128)(2,1)S(1)}, bf16[192,512]{1,0:T(8,128)(2,1)S(1)}, u32[]{:S(2)}, u32[]{:S(2)}) collective-permute-start(bf16[192,512]{1,0:T(8,128)(2,1)S(1)} %collective-permute-done.22.refs_13_), channel_id=1, source_target_pairs={{8,0},{16,8},{9,1},{17,9},{10,2},{18,10},{11,3},{19,11},{12,4},{20... | collective-permute-start | bytes 589832 | tf_op jit(solution)/shard_map/ppermute | solution.py:461
  56.3 18.9 %collective-permute-start.8 = (bf16[96,2048]{1,0:T(8,128)(2,1)S(1)}, bf16[96,2048]{1,0:T(8,128)(2,1)S(1)}, u32[]{:S(2)}, u32[]{:S(2)}) collective-permute-start(bf16[96,2048]{1,0:T(8,128)(2,1)S(1)} %pad_maximum_fusion.refs_0_), channel_id=1, source_target_pairs={{0,1},{1,0},{2,3},{3,2},{4,5},{5,4},{6,7},{7,6},{8,9},{9,8},{10,11... | collective-permute-start | bytes 1179656 | tf_op jit(solution)/shard_map/ppermute | solution.py:451
  56.7 36.9 %copy-start.33 = (bf16[192,512]{1,0:T(8,128)(2,1)}, bf16[192,512]{1,0:T(8,128)(2,1)S(1)}, u32[]{:S(2)}) copy-start(bf16[192,512]{1,0:T(8,128)(2,1)S(1)} %collective-permute-done.17.refs_8_) | copy-start | bytes 589828
  56.7 19.2 %collective-permute-start.9 = (bf16[96,2048]{1,0:T(8,128)(2,1)S(1)}, bf16[96,2048]{1,0:T(8,128)(2,1)S(1)}, u32[]{:S(2)}, u32[]{:S(2)}) collective-permute-start(bf16[96,2048]{1,0:T(8,128)(2,1)S(1)} %collective-permute-done.3.refs_2_), channel_id=1, source_target_pairs={{0,1},{1,0},{2,3},{3,2},{4,5},{5,4},{6,7},{7,6},{8,9},{9,8},{10,11... | collective-permute-start | bytes 1179656 | tf_op jit(solution)/shard_map/ppermute | solution.py:451
  57.0 19.6 %collective-permute-start.10 = (bf16[96,2048]{1,0:T(8,128)(2,1)S(1)}, bf16[96,2048]{1,0:T(8,128)(2,1)S(1)}, u32[]{:S(2)}, u32[]{:S(2)}) collective-permute-start(bf16[96,2048]{1,0:T(8,128)(2,1)S(1)} %collective-permute-done.4.refs_4_), channel_id=1, source_target_pairs={{0,1},{1,0},{2,3},{3,2},{4,5},{5,4},{6,7},{7,6},{8,9},{9,8},{10,11... | collective-permute-start | bytes 1179656 | tf_op jit(solution)/shard_map/ppermute | solution.py:451
  63.8 7.1 %collective-permute-start.11 = (bf16[48,2048]{1,0:T(8,128)(2,1)S(1)}, bf16[48,2048]{1,0:T(8,128)(2,1)S(1)}, u32[]{:S(2)}, u32[]{:S(2)}) collective-permute-start(bf16[48,2048]{1,0:T(8,128)(2,1)S(1)} %slice.6), channel_id=1, source_target_pairs={{0,4},{1,5},{2,6},{3,7},{4,0},{5,1},{6,2},{7,3},{8,12},{9,13},{10,... | collective-permute-start | bytes 589832 | tf_op jit(solution)/shard_map/ppermute | solution.py:451
  69.4 24.2 %copy-start.34 = (bf16[192,512]{1,0:T(8,128)(2,1)}, bf16[192,512]{1,0:T(8,128)(2,1)S(1)}, u32[]{:S(2)}) copy-start(bf16[192,512]{1,0:T(8,128)(2,1)S(1)} %collective-permute-done.24.refs_15_) | copy-start | bytes 589828
  69.4 5.8 %collective-permute-start.12 = (bf16[48,2048]{1,0:T(8,128)(2,1)S(1)}, bf16[48,2048]{1,0:T(8,128)(2,1)S(1)}, u32[]{:S(2)}, u32[]{:S(2)}) collective-permute-start(bf16[48,2048]{1,0:T(8,128)(2,1)S(1)} %slice.7), channel_id=1, source_target_pairs={{0,2},{1,3},{2,0},{3,1},{4,6},{5,7},{6,4},{7,5},{8,10},{9,11},{10,... | collective-permute-start | bytes 589832 | tf_op jit(solution)/shard_map/ppermute | solution.py:451
  70.9 7.1 %collective-permute-start.13 = (bf16[48,2048]{1,0:T(8,128)(2,1)S(1)}, bf16[48,2048]{1,0:T(8,128)(2,1)S(1)}, u32[]{:S(2)}, u32[]{:S(2)}) collective-permute-start(bf16[48,2048]{1,0:T(8,128)(2,1)S(1)} %collective-permute-done.11.refs_6_), channel_id=1, source_target_pairs={{0,1},{1,0},{2,3},{3,2},{4,5},{5,4},{6,7},{7,6},{8,9},{9,8},{10,11... | collective-permute-start | bytes 589832 | tf_op jit(solution)/shard_map/ppermute | solution.py:451
  75.2 4.0 %collective-permute-start.14 = (bf16[48,2048]{1,0:T(8,128)(2,1)S(1)}, bf16[48,2048]{1,0:T(8,128)(2,1)S(1)}, u32[]{:S(2)}, u32[]{:S(2)}) collective-permute-start(bf16[48,2048]{1,0:T(8,128)(2,1)S(1)} %collective-permute-done.12.refs_7_), channel_id=1, source_target_pairs={{0,1},{1,0},{2,3},{3,2},{4,5},{5,4},{6,7},{7,6},{8,9},{9,8},{10,11... | collective-permute-start | bytes 589832 | tf_op jit(solution)/shard_map/ppermute | solution.py:451
  75.2 18.2 %collective-permute-start.19 = (bf16[192,512]{1,0:T(8,128)(2,1)S(1)}, bf16[192,512]{1,0:T(8,128)(2,1)S(1)}, u32[]{:S(2)}, u32[]{:S(2)}) collective-permute-start(bf16[192,512]{1,0:T(8,128)(2,1)S(1)} %collective-permute-done.17.refs_8_), channel_id=1, source_target_pairs={{16,24},{17,25},{18,26},{19,27},{20,28},{21,29},{22,30},{23,31}} | collective-permute-start | bytes 589832 | tf_op jit(solution)/shard_map/ppermute | solution.py:461
  75.9 17.6 %collective-permute-start.20 = (bf16[192,512]{1,0:T(8,128)(2,1)}, bf16[192,512]{1,0:T(8,128)(2,1)S(1)}, u32[]{:S(2)}, u32[]{:S(2)}) collective-permute-start(bf16[192,512]{1,0:T(8,128)(2,1)} %collective-permute-done.18.refs_9_), channel_id=1, source_target_pairs={{16,24},{17,25},{18,26},{19,27},{20,28},{21,29},{22,30},{23,31}} | collective-permute-start | bytes 589832 | tf_op jit(solution)/shard_map/ppermute | solution.py:461
  76.6 16.9 %collective-permute-start.25 = (bf16[192,512]{1,0:T(8,128)(2,1)}, bf16[192,512]{1,0:T(8,128)(2,1)S(1)}, u32[]{:S(2)}, u32[]{:S(2)}) collective-permute-start(bf16[192,512]{1,0:T(8,128)(2,1)} %collective-permute-done.23.refs_14_), channel_id=1, source_target_pairs={{8,0},{9,1},{10,2},{11,3},{12,4},{13,5},{14,6},{15,7}} | collective-permute-start | bytes 589832 | tf_op jit(solution)/shard_map/ppermute | solution.py:461
  78.0 15.6 %collective-permute-start.26 = (bf16[192,512]{1,0:T(8,128)(2,1)S(1)}, bf16[192,512]{1,0:T(8,128)(2,1)S(1)}, u32[]{:S(2)}, u32[]{:S(2)}) collective-permute-start(bf16[192,512]{1,0:T(8,128)(2,1)S(1)} %collective-permute-done.24.refs_15_), channel_id=1, source_target_pairs={{8,0},{9,1},{10,2},{11,3},{12,4},{13,5},{14,6},{15,7}} | collective-permute-start | bytes 589832 | tf_op jit(solution)/shard_map/ppermute | solution.py:461
  88.4 19.5 %all-to-all-start.1 = ((f32[32,2,128]{2,1,0:T(2,128)}), f32[32,2,128]{2,1,0:T(2,128)S(1)}, u32[]{:S(2)}, u32[]{:S(2)}) async-start(f32[32,2,128]{2,1,0:T(2,128)} %get-tuple-element.42), calls=%async_computation.1 | async-start | bytes 65536 | tf_op jit(solution)/shard_map/all_to_all | solution.py:30
  107.8 29.6 %copy-start.1 = (bf16[768,256]{1,0:T(8,128)(2,1)S(1)}, bf16[768,256]{1,0:T(8,128)(2,1)}, u32[]{:S(2)}) copy-start(bf16[768,256]{1,0:T(8,128)(2,1)} %get-tuple-element.37.refs_1_.refs_3_) | copy-start | bytes 1179652
  107.8 29.6 %copy-start.3 = (bf16[192,256]{1,0:T(8,128)(2,1)S(1)}, bf16[192,256]{1,0:T(8,128)(2,1)}, u32[]{:S(2)}) copy-start(bf16[192,256]{1,0:T(8,128)(2,1)} %get-tuple-element.38.refs_2_.refs_4_) | copy-start | bytes 294916
  107.9 29.6 %copy-start.5 = (bf16[192,256]{1,0:T(8,128)(2,1)S(1)}, bf16[192,256]{1,0:T(8,128)(2,1)}, u32[]{:S(2)}) copy-start(bf16[192,256]{1,0:T(8,128)(2,1)} %copy-done.4) | copy-start | bytes 294916
  107.9 29.6 %copy-start.7 = (bf16[192,256]{1,0:T(8,128)(2,1)S(1)}, bf16[192,256]{1,0:T(8,128)(2,1)}, u32[]{:S(2)}) copy-start(bf16[192,256]{1,0:T(8,128)(2,1)} %copy-done.6) | copy-start | bytes 294916
  107.9 29.6 %copy-start.9 = (bf16[192,256]{1,0:T(8,128)(2,1)S(1)}, bf16[192,256]{1,0:T(8,128)(2,1)}, u32[]{:S(2)}) copy-start(bf16[192,256]{1,0:T(8,128)(2,1)} %copy-done.8) | copy-start | bytes 294916
  139.8 16.2 %all-to-all-start.4 = ((f32[32,2,128]{2,1,0:T(2,128)}), f32[32,2,128]{2,1,0:T(2,128)S(1)}, u32[]{:S(2)}, u32[]{:S(2)}) async-start(f32[32,2,128]{2,1,0:T(2,128)} %get-tuple-element.49), calls=%async_computation.4 | async-start | bytes 65536 | tf_op jit(solution)/shard_map/all_to_all | solution.py:30
  (21 other events, 87.7 us)

commit v8 on v7

--- a/solution.py
+++ b/solution.py
@@ -117,6 +117,15 @@
     return ka * n_band + jnp.bitwise_xor(lax.axis_index("band"), d)
 
 
+def own_copies(ref, dest, sems):
+    return [
+        pltpu.make_async_copy(
+            ref.at[jnp.bitwise_xor(lax.axis_index("ka"), j)], dest.at[j], sems.at[j]
+        )
+        for j in range(dest.shape[0])
+    ]
+
+
 def pair_rows(ref, kp):
     part = ref[:, kp * 2 * ROWS : (kp + 1) * 2 * ROWS, :]
     return part.reshape(part.shape[0] * 2 * ROWS, part.shape[2])
@@ -133,22 +142,20 @@
     own = own_ref[...]
     square = own * own
     block = with_sums(own, [jnp.sum(square), jnp.sum(gap_ref[...] * square)])
-    msg_ref[...] = jnp.broadcast_to(block.astype(BF)[None], msg_ref.shape)
-
-
-def cut_kernel(cond_ref, *refs):
-    outs, sems = refs[:-1], refs[-1]
+    msg_ref[...] = block.astype(BF)
+
+
+def cut_kernel(cond_ref, out_ref, sems):
+    n_ka, _, own = out_ref.shape
     k_dev, n_cond, npt = cond_ref.shape
-    own = outs[0].shape[1]
-    nu = npt // len(outs)
     copies = []
-    for j, out in enumerate(outs):
-        at = jnp.bitwise_xor(lax.axis_index("ka"), j) * nu + lax.axis_index("band") * own
+    for z in range(n_ka):
+        at = z * (npt // n_ka) + lax.axis_index("band") * own
         for kl in range(k_dev):
             copies.append(
                 pltpu.make_async_copy(
                     cond_ref.at[kl, :, pl.ds(pl.multiple_of(at, LANES), own)],
-                    out.at[pl.ds(kl * n_cond, n_cond), :],
+                    out_ref.at[z, pl.ds(kl * n_cond, n_cond), :],
                     sems.at[len(copies)],
                 )
             )
@@ -171,16 +178,17 @@
     wait_all(outs)
 
 
-def order_kernel(counts, *refs):
+def order_kernel(counts, n_ka, *refs):
     n_val = sum(counts)
     val_refs, refs = split_refs(refs[:n_val], counts), refs[n_val:]
-    rows_out, turned_out, own_out, vals, ordered, turned, val_sems, out_sems = refs
+    rows_out, turned_out, own_out, msgs_out, vals, heads, ordered, turned, val_sems, out_sems = refs
     own = own_out.shape[1]
     nu = ordered.shape[1]
-    copies = block_copies(val_refs, nu, vals, val_sems)
-    start_all(copies)
+    copies = block_copies(val_refs, nu, vals, val_sems.at[0])
+    head_copies = block_copies(val_refs, LANES, heads, val_sems.at[1], nu)
+    start_all(copies + head_copies)
     wait_all(copies)
-    group = vals.shape[0] * 2 * ROWS
+    n_band, group = vals.shape[0], vals.shape[0] * 2 * ROWS
     column = pl.multiple_of(lax.axis_index("band") * own, LANES)
     outs = []
     for kp in range(ordered.shape[0] // group):
@@ -196,16 +204,22 @@
             ),
         ]
         start_all(outs[-3:])
+    wait_all(head_copies)
+    rows = msgs_out.shape[1]
+    step = heads.shape[1] // n_ka
+    for d in range(n_band):
+        head = heads[d].astype(F32)
+        for j in range(n_ka):
+            msgs_out[device_at(n_band, j, d)] = head[j * step : j * step + rows, :].astype(BF)
     wait_all(outs)
 
 
 def density_kernel(cfg, *refs):
     n_ka, n_band, k_dev = cfg
     k_points = n_ka * k_dev
-    msgs_ref, vown_ref, cond_refs, refs = refs[0], refs[1], refs[2 : 2 + n_ka], refs[2 + n_ka :]
-    qx_ref, rho_ref, xs, conds, cond_sems = refs
+    msgs_ref, vown_ref, cond_ref, qx_ref, rho_ref, xs, conds, cond_sems = refs
     own = vown_ref.shape[1]
-    copies = block_copies([[ref] for ref in cond_refs], own, conds, cond_sems)
+    copies = own_copies(cond_ref, conds, cond_sems)
     start_all(copies)
     xs[...] = jnp.zeros_like(xs)
     for d in range(n_band):
@@ -230,37 +244,15 @@
         rho_ref[:, r, :] = jnp.broadcast_to(part, (rho_ref.shape[0], LANES))
 
 
-def line_blocks(n_ka):
-    return [(way, hop) for way in (-1, 1) for hop in range(1, n_ka)]
-
-
 def direct_kernel(n_ka, tile, scale, *refs):
     turned_ref, scr_ref, rows_ref, qx_ref, refs = refs[0], refs[1], refs[2], refs[3], refs[4:]
-    hops = [(0, 0)] + line_blocks(n_ka)
-    cond_refs, refs = split_refs(refs, [2] * len(hops)), refs[2 * len(hops) :]
+    cond_refs, refs = refs[:n_ka], refs[n_ka:]
     di_ref, qx, turned, conds, scrs, vals, mixed, kern, folded = refs[:9]
     qx_sem, cond_sems, row_sem, chunk_sems = refs[9:]
     nu, mu = scr_ref.shape
-    part, half = cond_refs[0][0].shape
     quad = 2 * LANES
-    ka = lax.axis_index("ka")
-
-    def each_block(act):
-        for i, (way, hop) in enumerate(hops):
-            origin = ka + way * hop
-
-            def act_on(i=i, origin=origin):
-                row = pl.multiple_of(jnp.bitwise_xor(ka, origin) * part, part)
-                for h, ref in enumerate(cond_refs[i]):
-                    dest = conds.at[pl.ds(row, part), pl.ds(h * half, half)]
-                    act(pltpu.make_async_copy(ref, dest, cond_sems.at[i, h]))
-
-            if hop == 0:
-                act_on()
-            else:
-                pl.when((origin >= 0) & (origin < n_ka))(act_on)
-
     qx_copy = pltpu.make_async_copy(qx_ref, qx, qx_sem.at[0])
+    cond_copies = block_copies([[ref] for ref in cond_refs], mu, conds, cond_sems)
     turned_copies, scr_copies = [], []
     for i in range(nu // tile):
         at = pl.ds(i * tile, tile)
@@ -271,9 +263,7 @@
             pltpu.make_async_copy(scr_ref.at[at, :], scrs.at[at, :], chunk_sems.at[1, i])
         )
     row_copy = pltpu.make_async_copy(rows_ref, vals, row_sem.at[0])
-    start_all([qx_copy, turned_copies[0]])
-    each_block(lambda copy: copy.start())
-    scr_copies[0].start()
+    start_all([qx_copy, turned_copies[0]] + cond_copies + [scr_copies[0]])
     for i in range(1, nu // tile):
         start_all([turned_copies[i], scr_copies[i]])
     row_copy.start()
@@ -287,26 +277,24 @@
                 turned[rows, cols], qx[kq], preferred_element_type=F32
             ).astype(BF)
         if i == 0:
-            each_block(lambda copy: copy.wait())
+            wait_all(cond_copies)
+            cond_rows = conds[...].reshape(-1, mu)
         scr_copies[i].wait()
-        for m in range(mu // quad):
-            cols = slice(m * quad, (m + 1) * quad)
-            amp = jnp.dot(mixed[rows, :], conds[:, cols], preferred_element_type=F32)
-            kern[rows, cols] = (scrs[rows, cols].astype(F32) * amp * scale).astype(BF)
+        amp = jnp.dot(mixed[rows, :], cond_rows, preferred_element_type=F32)
+        kern[rows, :] = (scrs[rows, :].astype(F32) * amp * scale).astype(BF)
     row_copy.wait()
     for m in range(mu // quad):
         cols = slice(m * quad, (m + 1) * quad)
         folded[:, cols] = jnp.dot(vals[...], kern[:, cols], preferred_element_type=F32).astype(BF)
     for kp in range(di_ref.shape[0]):
         at = slice(kp * LANES, (kp + 1) * LANES)
-        di_ref[kp] = dot_nt(folded[at, :], conds[at, :])
+        di_ref[kp] = dot_nt(folded[at, :], cond_rows[at, :])
 
 
 def exchange_kernel(cfg, chunk, scale, *refs):
     n_ka, n_band, k_dev = cfg
     k_points = n_ka * k_dev
-    rho_ref, di_ref, coul_ref, vown_ref, refs = refs[0], refs[1], refs[2], refs[3], refs[4:]
-    cond_refs, refs = refs[:n_ka], refs[n_ka:]
+    rho_ref, di_ref, coul_ref, vown_ref, cond_ref, refs = refs[:5] + (refs[5:],)
     msg_ref, rhos, di, coul, conds, vown, part, msg, coul_sems, cond_sems, sems = refs
     own, npt = coul_ref.shape
     coul_copies = [
@@ -316,7 +304,7 @@
         for i in range(npt // chunk)
     ]
     rho_copy = pltpu.make_async_copy(rho_ref, rhos, sems.at[0])
-    copies = block_copies([[ref] for ref in cond_refs], own, conds, cond_sems)
+    copies = own_copies(cond_ref, conds, cond_sems)
     copies.append(pltpu.make_async_copy(vown_ref, vown, sems.at[1]))
     copies.append(pltpu.make_async_copy(di_ref, di, sems.at[2]))
     start_all([rho_copy] + coul_copies + copies)
@@ -451,18 +439,6 @@
     return lax.ppermute(block, axis, [(i, i ^ d) for i in range(lax.axis_size(axis))])
 
 
-def line_gather(block, axis):
-    n = lax.axis_size(axis)
-    out = [block]
-    for way in (-1, 1):
-        moving = block
-        for hop in range(1, n):
-            pairs = [(i, i - way) for i in range(n) if 0 <= i + way * (hop - 1) < n and 0 <= i - way < n]
-            moving = lax.ppermute(moving, axis, pairs)
-            out.append(moving)
-    return out
-
-
 def plane_pieces(own_piece, others):
     def move(block, d):
         return swap(block, "band", d)
@@ -492,27 +468,37 @@
     scale = 1.0 / (npt_all * math.sqrt(count_all))
     piece_rows = k_points * nv_blk
 
-    def val_to(j):
-        part = lax.dynamic_slice_in_dim(val_orb, jnp.bitwise_xor(ka, j) * nu_blk, nu_blk, 2)
-        return part.reshape(k_dev * nv_blk, nu_blk)
-
-    val_parts = [val_to(0)] + [swap(val_to(j), "ka", j) for j in range(1, n_ka)]
-    val_cut = jnp.concatenate(val_parts, axis=0)
-    half = mu_blk // 2
-    cond_halves = []
-    for h in range(2):
-        cut = lax.dynamic_slice_in_dim(cond_orb, band * mu_blk + h * half, half, 2)
-        cond_halves.append(line_gather(cut.reshape(k_dev * n_cond, half), "ka"))
-    cond_pts = [ref for pair in zip(*cond_halves) for ref in pair]
     gap = (cond_energy[:, None, :] - val_energy[:, :, None]).reshape(k_dev, nv_blk * n_cond)
     gap = pack_vector(gap, k_dev)
-
     block = gap.shape
     msg_shape = shape_of((devices,) + block, BF)
     start_own, message = call(
-        pack_kernel, "pack", (shape_of(block), msg_shape), [VMEM] * 2, (VMEM, VMEM), mib=8
+        pack_kernel, "pack", (shape_of(block), shape_of(block, BF)), [VMEM] * 2, (VMEM, VMEM), mib=8
     )(start_vec, gap)
-    msgs = exchange_all(message)
+
+    head = jnp.pad(message, ((0, k_dev * nv_blk - block[0]), (0, 0)))
+
+    def val_to(j):
+        part = lax.dynamic_slice_in_dim(val_orb, jnp.bitwise_xor(ka, j) * nu_blk, nu_blk, 2)
+        return jnp.concatenate([part.reshape(k_dev * nv_blk, nu_blk), head], axis=1)
+
+    val_cut = jnp.concatenate(
+        [val_to(0)] + [swap(val_to(j), "ka", j) for j in range(1, n_ka)], axis=0
+    )
+    cond_local = lax.dynamic_slice_in_dim(cond_orb, band * mu_blk, mu_blk, 2)
+    cond_local = cond_local.reshape(k_dev * n_cond, mu_blk)
+    cond_pts = [cond_local] + [swap(cond_local, "ka", j) for j in range(1, n_ka)]
+    own_rows = k_dev * n_cond
+    cuts = call(
+        cut_kernel,
+        "cut",
+        shape_of((n_ka, own_rows, own), BF),
+        [ANY],
+        VMEM,
+        [dma(n_ka * k_dev)],
+    )(cond_orb)
+    cond_own = lax.all_to_all(cuts, "ka", split_axis=0, concat_axis=0, tiled=True)
+
     chunk, tile = 1024, 1024
     rows_all, conds_all = k_points * nv_blk * n_band, k_points * n_cond
     scr_turned = call(
@@ -525,36 +511,29 @@
         + [dma(2 * nu_blk // tile)] * 2,
         moved=8 * MIB,
     )(screened)
-    own_rows = k_dev * n_cond
-    cuts = call(
-        cut_kernel,
-        "cut",
-        (shape_of((own_rows, own), BF),) * n_ka,
-        [ANY],
-        (ANY,) * n_ka,
-        [dma(n_ka * k_dev)],
-    )(cond_orb)
-    cond_own = [cuts[0]] + [swap(cuts[j], "ka", j) for j in range(1, n_ka)]
-    pieces, (msgs, cond_own, scr_turned) = plane_pieces(val_cut, (msgs, cond_own, scr_turned))
+    pieces, (scr_turned, cond_pts[1 : n_ka - 1]) = plane_pieces(
+        val_cut, (scr_turned, cond_pts[1 : n_ka - 1])
+    )
     counts = tuple(len(piece) for piece in pieces)
     flat = [ref for piece in pieces for ref in piece]
     n_copies = len(flat)
-
-    val_rows, val_turned, val_own = call(
-        functools.partial(order_kernel, counts),
+    val_rows, val_turned, val_own, msgs = call(
+        functools.partial(order_kernel, counts, n_ka),
         "order",
         (
             shape_of((rows_all, nu_blk), BF),
             shape_of((nu_blk, rows_all), BF),
             shape_of((rows_all, own), BF),
+            msg_shape,
         ),
         [ANY] * n_copies,
-        (ANY, ANY, ANY),
+        (ANY, ANY, ANY, VMEM),
         [
             pltpu.VMEM((n_band, piece_rows, nu_blk), BF),
+            pltpu.VMEM((n_band, piece_rows, LANES), BF),
             pltpu.VMEM((rows_all, nu_blk), BF),
             pltpu.VMEM((nu_blk, rows_all), BF),
-            dma(n_copies),
+            dma(2, n_copies),
             dma(3, pairs),
         ],
         moved=9 * MIB,
@@ -572,7 +551,7 @@
                 shape_of((quads, 2 * LANES, 2 * LANES), BF),
                 shape_of((devices, own // LANES, LANES)),
             ),
-            [VMEM] * 2 + [ANY] * n_ka,
+            [VMEM] * 2 + [ANY],
             (VMEM, VMEM),
             [
                 pltpu.VMEM((quads, 2 * LANES, 2 * LANES), F32),
@@ -580,7 +559,7 @@
                 dma(n_ka),
             ],
             mib=8,
-        )(msgs, val_own, *cond_own)
+        )(msgs, val_own, cond_own)
         density = exchange_all(rho)
         direct = call(
             functools.partial(direct_kernel, n_ka, tile, scale),
@@ -591,14 +570,14 @@
             [
                 pltpu.VMEM((quads, 2 * LANES, 2 * LANES), BF),
                 pltpu.VMEM((nu_blk, rows_all), BF),
-                pltpu.VMEM((conds_all, mu_blk), BF),
+                pltpu.VMEM((n_ka, own_rows, mu_blk), BF),
                 pltpu.VMEM((nu_blk, mu_blk), BF),
                 pltpu.VMEM((rows_all, nu_blk), BF),
                 pltpu.VMEM((nu_blk, conds_all), BF),
                 pltpu.VMEM((nu_blk, mu_blk), BF),
                 pltpu.VMEM((rows_all, mu_blk), BF),
                 dma(1),
-                dma(len(cond_pts) // 2, 2),
+                dma(n_ka),
                 dma(1),
                 dma(2, nu_blk // tile),
             ],
@@ -609,7 +588,7 @@
             functools.partial(exchange_kernel, cfg, chunk, scale),
             "exchange",
             msg_shape,
-            [ANY] * (4 + n_ka),
+            [ANY] * 5,
             VMEM,
             [
                 pltpu.VMEM((devices, own // LANES, LANES), F32),
@@ -623,7 +602,7 @@
                 dma(n_ka),
                 dma(3),
             ],
-        )(density, direct, coulomb, val_own, *cond_own)
+        )(density, direct, coulomb, val_own, cond_own)
         recv = exchange_all(parts)
         if first:
             state, coef, message = call(

time: 187 us -> 163 us (0.87)
  starting transfers between devices: 49.2 us -> 33.9 us
  Pallas kernels: 64.5 us -> 51.6 us
  waiting for transfers between devices: 16.5 us -> 18.5 us
    ppermute x12 -> x0, starting transfers between devices: 18.4 us -> none  [line_gather(): moving = lax.ppermute(moving, axis, pairs)]
    ppermute x15, waiting for transfers between devices: 5.84 us -> 18.5 us  [swap(): lax.ppermute(block, axis, [(i, i ^ d) for i in range(lax.axis_size(axis))])]
    pallas_call x3, Pallas kernels: 19 us -> 7.69 us  [the longest x1 5.67 us: kernel_path(): call(functools.partial(order_kernel, counts, n_ka), 'order', (shape_of((r...]
    ppermute x12 -> x0, waiting for transfers between devices: 10.7 us -> none  [line_gather(): moving = lax.ppermute(moving, axis, pairs)]
    all_to_all x3 -> x2, starting transfers between devices: 12.4 us -> 8.66 us  [exchange_all(): return lax.all_to_all(parts, AXES, split_axis=0, concat_axis=0, tiled=True)]
    all_to_all x0 -> x1, starting transfers between devices: none -> 3.47 us  [kernel_path(): lax.all_to_all(cuts, 'ka', split_axis=0, concat_axis=0, tiled=True)]
    ppermute x15, starting transfers between devices: 18.3 us -> 21.8 us  [swap(): lax.ppermute(block, axis, [(i, i ^ d) for i in range(lax.axis_size(axis))])]
    unnamed x78 -> x48, local copies, waits for them, and re-layouts: 5.35 us -> 7.02 us
  transfers between devices with their start and end apart: 30 -> 18, of which waited for: 5 -> 6; matrix products, arithmetic and copies ran while one was open for 1% -> 1% of each run, Pallas kernels for 27% -> 23%
where the time goes in v8:
time: 163 us; the launch traced here: 162 us
  Pallas kernels  51.6 us (32%)
  blocking collectives  46.8 us (29%)
  starting transfers between devices  33.9 us (21%)
  waiting for transfers between devices  18.5 us (11%)
  local copies, waits for them, and re-layouts  9.42 us (6%)
    all_to_all x4, blocking collectives, exchange_all(): return lax.all_to_all(parts, AXES, split_axis=0, concat_axis=0, tiled=True)  46.8 us
    pallas_call x2, Pallas kernels, kernel_path(): call(functools.partial(direct_kernel, n_ka, tile, scale), 'direct', shape...  25.3 us
    ppermute x15, starting transfers between devices, swap(): lax.ppermute(block, axis, [(i, i ^ d) for i in range(lax.axis_size(axis))])  21.8 us
    ppermute x15, waiting for transfers between devices, swap(): lax.ppermute(block, axis, [(i, i ^ d) for i in range(lax.axis_size(axis))])  18.5 us
    all_to_all x2, starting transfers between devices, exchange_all(): return lax.all_to_all(parts, AXES, split_axis=0, concat_axis=0, tiled=True)  8.66 us
    pallas_call x2, Pallas kernels, kernel_path(): call(functools.partial(exchange_kernel, cfg, chunk, scale), 'exchange', m...  8.21 us
    unnamed x48, local copies, waits for them, and re-layouts  7.02 us
    pallas_call x1, Pallas kernels, kernel_path(): call(functools.partial(order_kernel, counts, n_ka), 'order', (shape_of((r...  5.67 us
  transfers between devices with their start and end apart: 18, of which 6 were waited for; matrix products, arithmetic and copies ran while one was open for 1% of the time, Pallas kernels for 23%

profile of v8, /device:TPU:0, one launch (start us, length us, event | category | flops | bytes accessed | tf_op | source)
XLA Modules:
  0.0 162.3 jit_solution(354184628500477714)
XLA Ops:
  0.7 0.8 broadcast_subtract_fusion
  1.7 0.7 copy-done.6
  2.6 1.1 dynamic-slice_bitcast_fusion.3
  3.7 3.1 %collective-permute-start = (bf16[24,2176]{1,0:T(8,128)(2,1)S(1)}, bf16[24,2176]{1,0:T(8,128)(2,1)S(1)}, u32[]{:S(2)}, u32[]{:S(2)}) collective-permute-start(bf16[24,2176]{1,0:T(8,128)(2,1)S(1)} %get-tuple-element.48), channel_id=1, source_target_pairs={{0,8},{8,0},{16,24},{24,16},{1,9},{9,1},{17,25},{25,17},{2,10},{10... | collective-permute-start | bytes 313352 | tf_op jit(solution)/shard_map/ppermute | solution.py:439
  6.8 2.6 %collective-permute-start.1 = (bf16[24,2176]{1,0:T(8,128)(2,1)S(1)}, bf16[24,2176]{1,0:T(8,128)(2,1)S(1)}, u32[]{:S(2)}, u32[]{:S(2)}) collective-permute-start(bf16[24,2176]{1,0:T(8,128)(2,1)S(1)} %get-tuple-element.49), channel_id=1, source_target_pairs={{0,16},{8,24},{16,0},{24,8},{1,17},{9,25},{17,1},{25,9},{2,18},{10... | collective-permute-start | bytes 313352 | tf_op jit(solution)/shard_map/ppermute | solution.py:439
  9.4 0.3 collective-permute-done
  9.8 8.0 %collective-permute-done.1 = bf16[24,2176]{1,0:T(8,128)(2,1)S(1)} collective-permute-done((bf16[24,2176]{1,0:T(8,128)(2,1)S(1)}, bf16[24,2176]{1,0:T(8,128)(2,1)S(1)}, u32[]{:S(2)}, u32[]{:S(2)}) %collective-permute-start.1) | collective-permute-done | bytes 104480 | tf_op jit(solution)/shard_map/ppermute | solution.py:439
  17.8 1.6 collective-permute-start.4
  19.3 1.5 collective-permute-start.5
  20.8 1.0 constant_dynamic-slice_fusion
  21.9 1.7 %collective-permute-start.6 = (bf16[192,1024]{1,0:T(8,128)(2,1)S(1)}, bf16[192,1024]{1,0:T(8,128)(2,1)S(1)}, u32[]{:S(2)}, u32[]{:S(2)}) collective-permute-start(bf16[192,1024]{1,0:T(8,128)(2,1)S(1)} %bitcast.10), channel_id=1, source_target_pairs={{0,8},{8,0},{16,24},{24,16},{1,9},{9,1},{17,25},{25,17},{2,10},{10... | collective-permute-start | bytes 1179656 | tf_op jit(solution)/shard_map/ppermute | solution.py:439
  23.6 1.4 collective-permute-start.7
  25.0 1.8 %cut.1 = bf16[4,192,256]{2,1,0:T(8,128)(2,1)} custom-call(bf16[3,64,8192]{2,1,0:T(8,128)(2,1)} %cond_ref.1), custom_call_target="tpu_custom_call" | custom-call | tf_op jit(solution)/shard_map/cut/pallas_call | solution.py:492
  26.8 3.5 %all-to-all-start = ((bf16[4,192,256]{2,1,0:T(8,128)(2,1)}), bf16[4,192,256]{2,1,0:T(8,128)(2,1)S(1)}, u32[]{:S(2)}, u32[]{:S(2)}) async-start(bf16[4,192,256]{2,1,0:T(8,128)(2,1)} %cut.1), calls=%async_computation | async-start | bytes 786432 | tf_op jit(solution)/shard_map/all_to_all | solution.py:500
  30.3 3.7 %turn.1.refs_1_ = bf16[2048,1024]{1,0:T(8,128)(2,1)} custom-call(bf16[1024,2048]{1,0:T(8,128)(2,1)} %scr_ref.1), custom_call_target="tpu_custom_call" | custom-call | bytes 8388608 | tf_op jit(solution)/shard_map/turn/pallas_call | solution.py:504
  34.0 7.0 %collective-permute-done.6.refs_5_ = bf16[192,1024]{1,0:T(8,128)(2,1)S(1)} collective-permute-done((bf16[192,1024]{1,0:T(8,128)(2,1)S(1)}, bf16[192,1024]{1,0:T(8,128)(2,1)S(1)}, u32[]{:S(2)}, u32[]{:S(2)}) %collective-permute-start.6) | collective-permute-done | bytes 393248 | tf_op jit(solution)/shard_map/ppermute | solution.py:439
  41.0 1.9 %collective-permute-done.7.refs_6_ = bf16[192,1024]{1,0:T(8,128)(2,1)S(1)} collective-permute-done((bf16[192,1024]{1,0:T(8,128)(2,1)S(1)}, bf16[192,1024]{1,0:T(8,128)(2,1)S(1)}, u32[]{:S(2)}, u32[]{:S(2)}) %collective-permute-start.7) | collective-permute-done | bytes 393248 | tf_op jit(solution)/shard_map/ppermute | solution.py:439
  43.0 0.6 collective-permute-start.10
  43.5 0.6 collective-permute-start.11
  44.1 0.5 collective-permute-start.9
  44.7 7.8 %collective-permute-start.14 = (bf16[192,1024]{1,0:T(8,128)(2,1)S(1)}, bf16[192,1024]{1,0:T(8,128)(2,1)}, u32[]{:S(2)}, u32[]{:S(2)}) collective-permute-start(bf16[192,1024]{1,0:T(8,128)(2,1)S(1)} %bitcast.12), channel_id=1, source_target_pairs={{0,24},{8,16},{16,8},{24,0},{1,25},{9,17},{17,9},{25,1},{2,26},{10... | collective-permute-start | bytes 1179656 | tf_op jit(solution)/shard_map/ppermute | solution.py:439
  52.5 0.5 collective-permute-start.13
  53.0 0.9 collective-permute-done.12.refs_8_
  54.3 0.3 copy-done.18
  54.6 0.3 copy-done.19
  55.1 0.8 copy-done.14
  55.8 5.7 %order.1 = (bf16[768,2048]{1,0:T(8,128)(2,1)}, bf16[2048,768]{1,0:T(8,128)(2,1)}, bf16[768,256]{1,0:T(8,128)(2,1)}, bf16[32,16,128]{2,1,0:T(8,128)(2,1)}) custom-call(bf16[96,2176]{1,0:T(8,128)(2,1)} %copy-done.9, bf16[96,2176]{1,0:T(8,128)(2,1)} %copy-done.12, bf16[96,2176]{1,0:T(8,128)(2,1)} %copy-done.10, bf16[96,2176]{1,0:T(8,128)(2,1)} %copy-done.13, ...), custom_call_target="tpu_custom_call" | custom-call | bytes 9437184 | tf_op jit(solution)/shard_map/order/pallas_call | solution.py:520
  61.5 1.1 copy-done.2
  62.7 0.9 copy-done.4
  63.6 1.6 density.2
  65.2 0.7 copy-done.8
  65.9 5.9 %all-to-all-start.1 = ((f32[32,2,128]{2,1,0:T(2,128)}), f32[32,2,128]{2,1,0:T(2,128)S(1)}, u32[]{:S(2)}, u32[]{:S(2)}) async-start(f32[32,2,128]{2,1,0:T(2,128)} %get-tuple-element.28), calls=%async_computation.1 | async-start | bytes 65536 | tf_op jit(solution)/shard_map/all_to_all | solution.py:30
  71.8 12.6 %direct.2.refs_1_ = f32[6,128,128]{2,1,0:T(8,128)} custom-call(bf16[2048,768]{1,0:T(8,128)(2,1)} %get-tuple-element.29.refs_0_, bf16[2048,1024]{1,0:T(8,128)(2,1)} %turn.1.refs_1_, bf16[768,2048]{1,0:T(8,128)(2,1)} %get-tuple-element.31.refs_2_, bf16[3,256,256]{2,1,0:T(8,128)(2,1)} %copy-done.8, bf16[192,1024]{1,0:T(8,128)(2,1)} %bitcast.13, ...), custom_call_target="tpu_custom_call" | custom-call | flops 6442450944 | bytes 12582912 | tf_op jit(solution)/shard_map/direct/pallas_call | solution.py:564
  84.5 0.6 copy-done.21
  85.1 4.1 %exchange.2 = bf16[32,16,128]{2,1,0:T(8,128)(2,1)} custom-call(f32[32,2,128]{2,1,0:T(2,128)} %copy-done.21, f32[6,128,128]{2,1,0:T(8,128)} %direct.2.refs_1_, bf16[256,8192]{1,0:T(8,128)(2,1)} %refs_2_.3, bf16[768,256]{1,0:T(8,128)(2,1)} %get-tuple-element.27.refs_1_.refs_3_, bf16[4,192,256]{2,1,0:T(8,128)(2,1)} %copy-done), custom_call_target="tpu_custom_call" | custom-call | tf_op jit(solution)/shard_map/exchange/pallas_call | solution.py:587
  89.3 13.9 %all_to_all.35.recv_ref = bf16[32,16,128]{2,1,0:T(8,128)(2,1)S(1)} all-to-all(bf16[32,16,128]{2,1,0:T(8,128)(2,1)} %exchange.2), channel_id=1, replica_groups=mesh['ka'=4,'band'=8] {'ka','band'}, dimensions={0} | all-to-all | bytes 262144 | tf_op jit(solution)/shard_map/all_to_all | solution.py:30
  103.2 0.8 first_owner.1
  104.0 10.0 %all_to_all.36.refs_0_.msgs_ref = bf16[32,16,128]{2,1,0:T(8,128)(2,1)S(1)} all-to-all(bf16[32,16,128]{2,1,0:T(8,128)(2,1)S(1)} %get-tuple-element.36), channel_id=1, replica_groups=mesh['ka'=4,'band'=8] {'ka','band'}, dimensions={0} | all-to-all | bytes 262144 | tf_op jit(solution)/shard_map/all_to_all | solution.py:30
  114.0 1.6 density.3
  115.6 0.7 copy-done.7
  116.4 2.8 %all-to-all-start.4 = ((f32[32,2,128]{2,1,0:T(2,128)}), f32[32,2,128]{2,1,0:T(2,128)S(1)}, u32[]{:S(2)}, u32[]{:S(2)}) async-start(f32[32,2,128]{2,1,0:T(2,128)} %get-tuple-element.37), calls=%async_computation.4 | async-start | bytes 65536 | tf_op jit(solution)/shard_map/all_to_all | solution.py:30
  119.1 12.6 %direct.3.refs_1_ = f32[6,128,128]{2,1,0:T(8,128)} custom-call(bf16[2048,768]{1,0:T(8,128)(2,1)} %get-tuple-element.29.refs_0_, bf16[2048,1024]{1,0:T(8,128)(2,1)} %turn.1.refs_1_, bf16[768,2048]{1,0:T(8,128)(2,1)} %get-tuple-element.31.refs_2_, bf16[3,256,256]{2,1,0:T(8,128)(2,1)} %copy-done.7, bf16[192,1024]{1,0:T(8,128)(2,1)} %bitcast.14, ...), custom_call_target="tpu_custom_call" | custom-call | flops 6442450944 | bytes 12582912 | tf_op jit(solution)/shard_map/direct/pallas_call | solution.py:564
  131.8 0.6 copy-done.20
  132.4 4.1 %exchange.3 = bf16[32,16,128]{2,1,0:T(8,128)(2,1)} custom-call(f32[32,2,128]{2,1,0:T(2,128)} %copy-done.20, f32[6,128,128]{2,1,0:T(8,128)} %direct.3.refs_1_, bf16[256,8192]{1,0:T(8,128)(2,1)} %refs_2_.3, bf16[768,256]{1,0:T(8,128)(2,1)} %get-tuple-element.27.refs_1_.refs_3_, bf16[4,192,256]{2,1,0:T(8,128)(2,1)} %copy-done), custom_call_target="tpu_custom_call" | custom-call | tf_op jit(solution)/shard_map/exchange/pallas_call | solution.py:587
  136.5 13.9 %all_to_all.37.recv_ref = bf16[32,16,128]{2,1,0:T(8,128)(2,1)S(1)} all-to-all(bf16[32,16,128]{2,1,0:T(8,128)(2,1)} %exchange.3), channel_id=1, replica_groups=mesh['ka'=4,'band'=8] {'ka','band'}, dimensions={0} | all-to-all | bytes 262144 | tf_op jit(solution)/shard_map/all_to_all | solution.py:30
  150.4 1.3 second_owner.1
  151.7 9.0 %all_to_all.38.msgs_ref = f32[32,2,128]{2,1,0:T(2,128)S(1)} all-to-all(f32[32,2,128]{2,1,0:T(2,128)S(1)} %get-tuple-element.41), channel_id=1, replica_groups=mesh['ka'=4,'band'=8] {'ka','band'}, dimensions={0} | all-to-all | bytes 65536 | tf_op jit(solution)/shard_map/all_to_all | solution.py:30
  160.7 1.3 finish.1
  (66 shorter events, 1.2 us)
Async XLA Ops:
  1.7 0.7 copy-start.6
  3.7 6.0 %collective-permute-start = (bf16[24,2176]{1,0:T(8,128)(2,1)S(1)}, bf16[24,2176]{1,0:T(8,128)(2,1)S(1)}, u32[]{:S(2)}, u32[]{:S(2)}) collective-permute-start(bf16[24,2176]{1,0:T(8,128)(2,1)S(1)} %get-tuple-element.48), channel_id=1, source_target_pairs={{0,8},{8,0},{16,24},{24,16},{1,9},{9,1},{17,25},{25,17},{2,10},{10... | collective-permute-start | bytes 313352 | tf_op jit(solution)/shard_map/ppermute | solution.py:439
  6.8 10.9 %collective-permute-start.1 = (bf16[24,2176]{1,0:T(8,128)(2,1)S(1)}, bf16[24,2176]{1,0:T(8,128)(2,1)S(1)}, u32[]{:S(2)}, u32[]{:S(2)}) collective-permute-start(bf16[24,2176]{1,0:T(8,128)(2,1)S(1)} %get-tuple-element.49), channel_id=1, source_target_pairs={{0,16},{8,24},{16,0},{24,8},{1,17},{9,25},{17,1},{25,9},{2,18},{10... | collective-permute-start | bytes 313352 | tf_op jit(solution)/shard_map/ppermute | solution.py:439
  9.4 8.3 %collective-permute-start.2 = (bf16[24,2176]{1,0:T(8,128)(2,1)S(1)}, bf16[24,2176]{1,0:T(8,128)(2,1)S(1)}, u32[]{:S(2)}, u32[]{:S(2)}) collective-permute-start(bf16[24,2176]{1,0:T(8,128)(2,1)S(1)} %get-tuple-element.50), channel_id=1, source_target_pairs={{0,24},{8,16},{16,8},{24,0},{1,25},{9,17},{17,9},{25,1},{2,26},{10... | collective-permute-start | bytes 313352 | tf_op jit(solution)/shard_map/ppermute | solution.py:439
  17.7 16.2 %copy-start.9 = (bf16[96,2176]{1,0:T(8,128)(2,1)}, bf16[96,2176]{1,0:T(8,128)(2,1)S(1)}, u32[]{:S(2)}) copy-start(bf16[96,2176]{1,0:T(8,128)(2,1)S(1)} %pad_maximum_fusion.refs_0_) | copy-start | bytes 1253380
  17.8 25.2 %collective-permute-start.4 = (bf16[96,2176]{1,0:T(8,128)(2,1)S(1)}, bf16[96,2176]{1,0:T(8,128)(2,1)S(1)}, u32[]{:S(2)}, u32[]{:S(2)}) collective-permute-start(bf16[96,2176]{1,0:T(8,128)(2,1)S(1)} %pad_maximum_fusion.refs_0_), channel_id=1, source_target_pairs={{0,2},{1,3},{2,0},{3,1},{4,6},{5,7},{6,4},{7,5},{8,10},{9,11},{10,... | collective-permute-start | bytes 1253384 | tf_op jit(solution)/shard_map/ppermute | solution.py:439
  19.3 23.6 %collective-permute-start.5 = (bf16[96,2176]{1,0:T(8,128)(2,1)S(1)}, bf16[96,2176]{1,0:T(8,128)(2,1)S(1)}, u32[]{:S(2)}, u32[]{:S(2)}) collective-permute-start(bf16[96,2176]{1,0:T(8,128)(2,1)S(1)} %pad_maximum_fusion.refs_0_), channel_id=1, source_target_pairs={{0,4},{1,5},{2,6},{3,7},{4,0},{5,1},{6,2},{7,3},{8,12},{9,13},{10,... | collective-permute-start | bytes 1253384 | tf_op jit(solution)/shard_map/ppermute | solution.py:439
  21.9 22.8 %copy-start.15 = (bf16[3,64,1024]{2,1,0:T(8,128)(2,1)}, bf16[3,64,1024]{2,1,0:T(8,128)(2,1)S(1)}, u32[]{:S(2)}) copy-start(bf16[3,64,1024]{2,1,0:T(8,128)(2,1)S(1)} %constant_dynamic-slice_fusion) | copy-start | bytes 1179652
  21.9 19.1 %collective-permute-start.6 = (bf16[192,1024]{1,0:T(8,128)(2,1)S(1)}, bf16[192,1024]{1,0:T(8,128)(2,1)S(1)}, u32[]{:S(2)}, u32[]{:S(2)}) collective-permute-start(bf16[192,1024]{1,0:T(8,128)(2,1)S(1)} %bitcast.10), channel_id=1, source_target_pairs={{0,8},{8,0},{16,24},{24,16},{1,9},{9,1},{17,25},{25,17},{2,10},{10... | collective-permute-start | bytes 1179656 | tf_op jit(solution)/shard_map/ppermute | solution.py:439
  23.6 19.3 %collective-permute-start.7 = (bf16[192,1024]{1,0:T(8,128)(2,1)S(1)}, bf16[192,1024]{1,0:T(8,128)(2,1)S(1)}, u32[]{:S(2)}, u32[]{:S(2)}) collective-permute-start(bf16[192,1024]{1,0:T(8,128)(2,1)S(1)} %bitcast.11), channel_id=1, source_target_pairs={{0,16},{8,24},{16,0},{24,8},{1,17},{9,25},{17,1},{25,9},{2,18},{10... | collective-permute-start | bytes 1179656 | tf_op jit(solution)/shard_map/ppermute | solution.py:439
  25.0 19.7 %collective-permute-start.3 = (bf16[96,2176]{1,0:T(8,128)(2,1)S(1)}, bf16[96,2176]{1,0:T(8,128)(2,1)S(1)}, u32[]{:S(2)}, u32[]{:S(2)}) collective-permute-start(bf16[96,2176]{1,0:T(8,128)(2,1)S(1)} %pad_maximum_fusion.refs_0_), channel_id=1, source_target_pairs={{0,1},{1,0},{2,3},{3,2},{4,5},{5,4},{6,7},{7,6},{8,9},{9,8},{10,11... | collective-permute-start | bytes 1253384 | tf_op jit(solution)/shard_map/ppermute | solution.py:439
  26.8 34.7 %all-to-all-start = ((bf16[4,192,256]{2,1,0:T(8,128)(2,1)}), bf16[4,192,256]{2,1,0:T(8,128)(2,1)S(1)}, u32[]{:S(2)}, u32[]{:S(2)}) async-start(bf16[4,192,256]{2,1,0:T(8,128)(2,1)} %cut.1), calls=%async_computation | async-start | bytes 786432 | tf_op jit(solution)/shard_map/all_to_all | solution.py:500
  41.0 30.8 %copy-start.22 = (bf16[192,1024]{1,0:T(8,128)(2,1)}, bf16[192,1024]{1,0:T(8,128)(2,1)S(1)}, u32[]{:S(2)}) copy-start(bf16[192,1024]{1,0:T(8,128)(2,1)S(1)} %collective-permute-done.6.refs_5_) | copy-start | bytes 1179652
  42.9 28.9 %copy-start.23 = (bf16[192,1024]{1,0:T(8,128)(2,1)}, bf16[192,1024]{1,0:T(8,128)(2,1)S(1)}, u32[]{:S(2)}) copy-start(bf16[192,1024]{1,0:T(8,128)(2,1)S(1)} %collective-permute-done.7.refs_6_) | copy-start | bytes 1179652
  42.9 11.3 %copy-start.10 = (bf16[96,2176]{1,0:T(8,128)(2,1)}, bf16[96,2176]{1,0:T(8,128)(2,1)S(1)}, u32[]{:S(2)}) copy-start(bf16[96,2176]{1,0:T(8,128)(2,1)S(1)} %collective-permute-done.4.refs_2_) | copy-start | bytes 1253380
  42.9 11.3 %copy-start.11 = (bf16[96,2176]{1,0:T(8,128)(2,1)}, bf16[96,2176]{1,0:T(8,128)(2,1)S(1)}, u32[]{:S(2)}) copy-start(bf16[96,2176]{1,0:T(8,128)(2,1)S(1)} %collective-permute-done.5.refs_4_) | copy-start | bytes 1253380
  43.0 9.5 %collective-permute-start.10 = (bf16[48,2176]{1,0:T(8,128)(2,1)S(1)}, bf16[48,2176]{1,0:T(8,128)(2,1)S(1)}, u32[]{:S(2)}, u32[]{:S(2)}) collective-permute-start(bf16[48,2176]{1,0:T(8,128)(2,1)S(1)} %slice.6), channel_id=1, source_target_pairs={{0,4},{1,5},{2,6},{3,7},{4,0},{5,1},{6,2},{7,3},{8,12},{9,13},{10,... | collective-permute-start | bytes 626696 | tf_op jit(solution)/shard_map/ppermute | solution.py:439
  43.5 8.9 %collective-permute-start.11 = (bf16[48,2176]{1,0:T(8,128)(2,1)S(1)}, bf16[48,2176]{1,0:T(8,128)(2,1)S(1)}, u32[]{:S(2)}, u32[]{:S(2)}) collective-permute-start(bf16[48,2176]{1,0:T(8,128)(2,1)S(1)} %slice.7), channel_id=1, source_target_pairs={{0,2},{1,3},{2,0},{3,1},{4,6},{5,7},{6,4},{7,5},{8,10},{9,11},{10,... | collective-permute-start | bytes 626696 | tf_op jit(solution)/shard_map/ppermute | solution.py:439
  44.1 10.1 %collective-permute-start.8 = (bf16[96,2176]{1,0:T(8,128)(2,1)S(1)}, bf16[96,2176]{1,0:T(8,128)(2,1)S(1)}, u32[]{:S(2)}, u32[]{:S(2)}) collective-permute-start(bf16[96,2176]{1,0:T(8,128)(2,1)S(1)} %collective-permute-done.4.refs_2_), channel_id=1, source_target_pairs={{0,1},{1,0},{2,3},{3,2},{4,5},{5,4},{6,7},{7,6},{8,9},{9,8},{10,11... | collective-permute-start | bytes 1253384 | tf_op jit(solution)/shard_map/ppermute | solution.py:439
  44.1 10.1 %collective-permute-start.9 = (bf16[96,2176]{1,0:T(8,128)(2,1)S(1)}, bf16[96,2176]{1,0:T(8,128)(2,1)S(1)}, u32[]{:S(2)}, u32[]{:S(2)}) collective-permute-start(bf16[96,2176]{1,0:T(8,128)(2,1)S(1)} %collective-permute-done.5.refs_4_), channel_id=1, source_target_pairs={{0,1},{1,0},{2,3},{3,2},{4,5},{5,4},{6,7},{7,6},{8,9},{9,8},{10,11... | collective-permute-start | bytes 1253384 | tf_op jit(solution)/shard_map/ppermute | solution.py:439
  44.7 9.6 %copy-start.12 = (bf16[96,2176]{1,0:T(8,128)(2,1)}, bf16[96,2176]{1,0:T(8,128)(2,1)S(1)}, u32[]{:S(2)}) copy-start(bf16[96,2176]{1,0:T(8,128)(2,1)S(1)} %collective-permute-done.3.refs_1_) | copy-start | bytes 1253380
  44.7 27.1 %collective-permute-start.14 = (bf16[192,1024]{1,0:T(8,128)(2,1)S(1)}, bf16[192,1024]{1,0:T(8,128)(2,1)}, u32[]{:S(2)}, u32[]{:S(2)}) collective-permute-start(bf16[192,1024]{1,0:T(8,128)(2,1)S(1)} %bitcast.12), channel_id=1, source_target_pairs={{0,24},{8,16},{16,8},{24,0},{1,25},{9,17},{17,9},{25,1},{2,26},{10... | collective-permute-start | bytes 1179656 | tf_op jit(solution)/shard_map/ppermute | solution.py:439
  52.4 1.8 %copy-start.16 = (bf16[48,2176]{1,0:T(8,128)(2,1)}, bf16[48,2176]{1,0:T(8,128)(2,1)S(1)}, u32[]{:S(2)}) copy-start(bf16[48,2176]{1,0:T(8,128)(2,1)S(1)} %collective-permute-done.10.refs_6_) | copy-start | bytes 626692
  52.4 1.5 collective-permute-start.12
  52.5 1.8 %copy-start.17 = (bf16[48,2176]{1,0:T(8,128)(2,1)}, bf16[48,2176]{1,0:T(8,128)(2,1)S(1)}, u32[]{:S(2)}) copy-start(bf16[48,2176]{1,0:T(8,128)(2,1)S(1)} %collective-permute-done.11.refs_7_) | copy-start | bytes 626692
  52.5 1.7 %collective-permute-start.13 = (bf16[48,2176]{1,0:T(8,128)(2,1)S(1)}, bf16[48,2176]{1,0:T(8,128)(2,1)S(1)}, u32[]{:S(2)}, u32[]{:S(2)}) collective-permute-start(bf16[48,2176]{1,0:T(8,128)(2,1)S(1)} %collective-permute-done.11.refs_7_), channel_id=1, source_target_pairs={{0,1},{1,0},{2,3},{3,2},{4,5},{5,4},{6,7},{7,6},{8,9},{9,8},{10,11... | collective-permute-start | bytes 626696 | tf_op jit(solution)/shard_map/ppermute | solution.py:439
  53.9 0.7 copy-start.18
  54.2 0.7 copy-start.19
  54.2 0.9 copy-start.13
  55.1 0.8 copy-start.14
  61.5 23.0 %copy-start = (bf16[4,192,256]{2,1,0:T(8,128)(2,1)}, bf16[4,192,256]{2,1,0:T(8,128)(2,1)S(1)}, u32[]{:S(2)}) copy-start(bf16[4,192,256]{2,1,0:T(8,128)(2,1)S(1)} %all-to-all-done.refs_2_.refs_4_) | copy-start | bytes 1179652
  61.5 1.1 copy-start.2
  62.7 0.9 copy-start.4
  65.2 0.7 copy-start.8
  65.9 18.6 %all-to-all-start.1 = ((f32[32,2,128]{2,1,0:T(2,128)}), f32[32,2,128]{2,1,0:T(2,128)S(1)}, u32[]{:S(2)}, u32[]{:S(2)}) async-start(f32[32,2,128]{2,1,0:T(2,128)} %get-tuple-element.28), calls=%async_computation.1 | async-start | bytes 65536 | tf_op jit(solution)/shard_map/all_to_all | solution.py:30
  84.5 18.7 %copy-start.5 = (bf16[32,16,128]{2,1,0:T(8,128)(2,1)S(1)}, bf16[32,16,128]{2,1,0:T(8,128)(2,1)}, u32[]{:S(2)}) copy-start(bf16[32,16,128]{2,1,0:T(8,128)(2,1)} %get-tuple-element.26.refs_0_.msgs_ref) | copy-start | bytes 393220
  84.5 29.5 %copy-start.3 = (bf16[768,256]{1,0:T(8,128)(2,1)S(1)}, bf16[768,256]{1,0:T(8,128)(2,1)}, u32[]{:S(2)}) copy-start(bf16[768,256]{1,0:T(8,128)(2,1)} %get-tuple-element.27.refs_1_.refs_3_) | copy-start | bytes 1179652
  84.5 0.6 copy-start.21
  85.1 28.9 %copy-start.1 = (bf16[4,192,256]{2,1,0:T(8,128)(2,1)S(1)}, bf16[4,192,256]{2,1,0:T(8,128)(2,1)}, u32[]{:S(2)}) copy-start(bf16[4,192,256]{2,1,0:T(8,128)(2,1)} %copy-done) | copy-start | bytes 1179652
  115.6 0.7 copy-start.7
  116.4 15.4 %all-to-all-start.4 = ((f32[32,2,128]{2,1,0:T(2,128)}), f32[32,2,128]{2,1,0:T(2,128)S(1)}, u32[]{:S(2)}, u32[]{:S(2)}) async-start(f32[32,2,128]{2,1,0:T(2,128)} %get-tuple-element.37), calls=%async_computation.4 | async-start | bytes 65536 | tf_op jit(solution)/shard_map/all_to_all | solution.py:30
  131.8 0.6 copy-start.20

commit v9 on v8

--- a/solution.py
+++ b/solution.py
@@ -36,13 +36,6 @@
 
 def dot_tn(lhs, rhs):
     return lax.dot_general(lhs, rhs, (((0,), (0,)), ((), ())), preferred_element_type=F32)
-
-
-def pack_vector(block, k_dev):
-    groups = (k_dev + 1) // 2
-    block = jnp.pad(block, ((0, 2 * groups - k_dev), (0, 0)))
-    block = block.reshape(groups, 2, ROWS, HALF).transpose(0, 2, 1, 3)
-    return block.reshape(groups * ROWS, LANES)
 
 
 def lane_half(tile, have, want):
@@ -131,14 +124,18 @@
     return part.reshape(part.shape[0] * 2 * ROWS, part.shape[2])
 
 
-def pack_kernel(start_ref, gap_ref, own_ref, msg_ref):
+def pack_kernel(start_ref, cond_ref, val_ref, own_ref, gap_ref, msg_ref):
     own_ref[...] = jnp.zeros_like(own_ref)
+    gap_ref[...] = jnp.zeros_like(gap_ref)
+    cond = jnp.concatenate([cond_ref[...], cond_ref[...]], axis=1)
     for kl in range(start_ref.shape[0]):
-        for j in range(ROWS // 2):
-            row = start_ref[pl.ds(kl, 1), pl.ds(j * LANES, LANES)]
-            for v in range(2):
-                at = pl.ds(kl // 2 * ROWS + 2 * j + v, 1)
-                own_ref[at, :] = own_ref[at, :] + lane_half(row, v, kl % 2)
+        half = kl % 2
+        for v in range(ROWS):
+            at = pl.ds(kl // 2 * ROWS + v, 1)
+            row = start_ref[pl.ds(kl, 1), pl.ds(v // 2 * LANES, LANES)]
+            own_ref[at, :] = own_ref[at, :] + lane_half(row, v % 2, half)
+            gap = cond[kl : kl + 1, :] - val_ref[kl, v]
+            gap_ref[at, :] = gap_ref[at, :] + lane_half(gap, half, half)
     own = own_ref[...]
     square = own * own
     block = with_sums(own, [jnp.sum(square), jnp.sum(gap_ref[...] * square)])
@@ -217,15 +214,19 @@
 def density_kernel(cfg, *refs):
     n_ka, n_band, k_dev = cfg
     k_points = n_ka * k_dev
-    msgs_ref, vown_ref, cond_ref, qx_ref, rho_ref, xs, conds, cond_sems = refs
+    msgs_ref, vown_ref, cond_ref, qx_ref, rho_ref = refs[:5]
+    xs, msgs, vown, conds, cond_sems, sems = refs[5:]
     own = vown_ref.shape[1]
+    msg_copy = pltpu.make_async_copy(msgs_ref, msgs, sems.at[0])
     copies = own_copies(cond_ref, conds, cond_sems)
-    start_all(copies)
+    copies.append(pltpu.make_async_copy(vown_ref, vown, sems.at[1]))
+    start_all([msg_copy] + copies)
     xs[...] = jnp.zeros_like(xs)
+    msg_copy.wait()
     for d in range(n_band):
         for k in range(k_points):
             j, kl = divmod(k, k_dev)
-            tile = msgs_ref[device_at(n_band, j, d), :, :].astype(F32)
+            tile = msgs[device_at(n_band, j, d), :, :].astype(F32)
             tile = tile[kl // 2 * ROWS : (kl // 2 + 1) * ROWS, :]
             base = k // 2 % 2 * LANES
             at = pl.ds(base + d * 2 * ROWS + k % 2 * ROWS, ROWS)
@@ -237,7 +238,7 @@
     quad = 2 * LANES
     for kq in range(k_points // 4):
         at = slice(kq * quad, (kq + 1) * quad)
-        mixed = dot_tn(qx_ref[kq], vown_ref[at, :])
+        mixed = dot_tn(qx_ref[kq], vown[at, :])
         rho = rho + jnp.sum(mixed * cond_rows[at, :].astype(F32), axis=0, keepdims=True)
     for r in range(own // LANES):
         part = rho[:, r * LANES : (r + 1) * LANES]
@@ -283,9 +284,7 @@
         amp = jnp.dot(mixed[rows, :], cond_rows, preferred_element_type=F32)
         kern[rows, :] = (scrs[rows, :].astype(F32) * amp * scale).astype(BF)
     row_copy.wait()
-    for m in range(mu // quad):
-        cols = slice(m * quad, (m + 1) * quad)
-        folded[:, cols] = jnp.dot(vals[...], kern[:, cols], preferred_element_type=F32).astype(BF)
+    folded[...] = jnp.dot(vals[...], kern[...], preferred_element_type=F32).astype(BF)
     for kp in range(di_ref.shape[0]):
         at = slice(kp * LANES, (kp + 1) * LANES)
         di_ref[kp] = dot_nt(folded[at, :], cond_rows[at, :])
@@ -468,13 +467,16 @@
     scale = 1.0 / (npt_all * math.sqrt(count_all))
     piece_rows = k_points * nv_blk
 
-    gap = (cond_energy[:, None, :] - val_energy[:, :, None]).reshape(k_dev, nv_blk * n_cond)
-    gap = pack_vector(gap, k_dev)
-    block = gap.shape
+    block = ((k_dev + 1) // 2 * ROWS, LANES)
     msg_shape = shape_of((devices,) + block, BF)
-    start_own, message = call(
-        pack_kernel, "pack", (shape_of(block), shape_of(block, BF)), [VMEM] * 2, (VMEM, VMEM), mib=8
-    )(start_vec, gap)
+    start_own, gap, message = call(
+        pack_kernel,
+        "pack",
+        (shape_of(block), shape_of(block), shape_of(block, BF)),
+        [VMEM, VMEM, SMEM],
+        (VMEM, VMEM, VMEM),
+        mib=8,
+    )(start_vec, cond_energy, val_energy)
 
     head = jnp.pad(message, ((0, k_dev * nv_blk - block[0]), (0, 0)))
 
@@ -511,8 +513,9 @@
         + [dma(2 * nu_blk // tile)] * 2,
         moved=8 * MIB,
     )(screened)
-    pieces, (scr_turned, cond_pts[1 : n_ka - 1]) = plane_pieces(
-        val_cut, (scr_turned, cond_pts[1 : n_ka - 1])
+    pieces, scr_turned = plane_pieces(val_cut, scr_turned)
+    pieces, cond_pts[1 : n_ka - 1] = lax.optimization_barrier(
+        (pieces, cond_pts[1 : n_ka - 1])
     )
     counts = tuple(len(piece) for piece in pieces)
     flat = [ref for piece in pieces for ref in piece]
@@ -551,14 +554,16 @@
                 shape_of((quads, 2 * LANES, 2 * LANES), BF),
                 shape_of((devices, own // LANES, LANES)),
             ),
-            [VMEM] * 2 + [ANY],
+            [ANY] * 3,
             (VMEM, VMEM),
             [
                 pltpu.VMEM((quads, 2 * LANES, 2 * LANES), F32),
+                pltpu.VMEM((devices,) + block, BF),
+                pltpu.VMEM((rows_all, own), BF),
                 pltpu.VMEM((n_ka, own_rows, own), BF),
                 dma(n_ka),
+                dma(2),
             ],
-            mib=8,
         )(msgs, val_own, cond_own)
         density = exchange_all(rho)
         direct = call(

time: 163 us -> 159 us (0.975)
  starting transfers between devices: 33.9 us -> 30.3 us
  Pallas kernels: 51.6 us -> 53.3 us
    all_to_all x2, starting transfers between devices: 8.66 us -> 5.49 us  [exchange_all(): return lax.all_to_all(parts, AXES, split_axis=0, concat_axis=0, tiled=True)]
    unnamed x48 -> x44, local copies, waits for them, and re-layouts: 7.02 us -> 6.35 us
  transfers between devices with their start and end apart: 18 -> 18, of which waited for: 6 -> 6; matrix products, arithmetic and copies ran while one was open for 1% -> 1% of each run, Pallas kernels for 23% -> 24%
where the time goes in v9:
time: 159 us; the launch traced here: 158 us
  Pallas kernels  53.3 us (34%)
  blocking collectives  47.4 us (30%)
  starting transfers between devices  30.3 us (19%)
  waiting for transfers between devices  17.2 us (11%)
  local copies, waits for them, and re-layouts  8.49 us (5%)
    all_to_all x4, blocking collectives, exchange_all(): return lax.all_to_all(parts, AXES, split_axis=0, concat_axis=0, tiled=True)  47.4 us
    pallas_call x2, Pallas kernels, kernel_path(): call(functools.partial(direct_kernel, n_ka, tile, scale), 'direct', shape...  25.3 us
    ppermute x15, starting transfers between devices, swap(): lax.ppermute(block, axis, [(i, i ^ d) for i in range(lax.axis_size(axis))])  21.3 us
    ppermute x15, waiting for transfers between devices, swap(): lax.ppermute(block, axis, [(i, i ^ d) for i in range(lax.axis_size(axis))])  17.2 us
    pallas_call x2, Pallas kernels, kernel_path(): call(functools.partial(exchange_kernel, cfg, chunk, scale), 'exchange', m...  8.19 us
    unnamed x44, local copies, waits for them, and re-layouts  6.35 us
    pallas_call x1, Pallas kernels, kernel_path(): call(functools.partial(order_kernel, counts, n_ka), 'order', (shape_of((r...  5.7 us
    all_to_all x2, starting transfers between devices, exchange_all(): return lax.all_to_all(parts, AXES, split_axis=0, concat_axis=0, tiled=True)  5.49 us
  transfers between devices with their start and end apart: 18, of which 6 were waited for; matrix products, arithmetic and copies ran while one was open for 1% of the time, Pallas kernels for 24%

profile of v9, /device:TPU:0, one launch (start us, length us, event | category | flops | bytes accessed | tf_op | source)
XLA Modules:
  0.0 158.0 jit_solution(12092593694705774288)
XLA Ops:
  0.7 0.7 copy-done.2
  1.4 0.7 copy-done.3
  2.0 0.7 copy-done.4
  2.7 0.8 pack.1
  3.5 1.1 dynamic-slice_bitcast_fusion.3
  4.6 3.1 %collective-permute-start = (bf16[24,2176]{1,0:T(8,128)(2,1)S(1)}, bf16[24,2176]{1,0:T(8,128)(2,1)S(1)}, u32[]{:S(2)}, u32[]{:S(2)}) collective-permute-start(bf16[24,2176]{1,0:T(8,128)(2,1)S(1)} %get-tuple-element.70), channel_id=1, source_target_pairs={{0,8},{8,0},{16,24},{24,16},{1,9},{9,1},{17,25},{25,17},{2,10},{10... | collective-permute-start | bytes 313352 | tf_op jit(solution)/shard_map/ppermute | solution.py:438
  7.7 2.6 %collective-permute-start.1 = (bf16[24,2176]{1,0:T(8,128)(2,1)S(1)}, bf16[24,2176]{1,0:T(8,128)(2,1)S(1)}, u32[]{:S(2)}, u32[]{:S(2)}) collective-permute-start(bf16[24,2176]{1,0:T(8,128)(2,1)S(1)} %get-tuple-element.71), channel_id=1, source_target_pairs={{0,16},{8,24},{16,0},{24,8},{1,17},{9,25},{17,1},{25,9},{2,18},{10... | collective-permute-start | bytes 313352 | tf_op jit(solution)/shard_map/ppermute | solution.py:438
  10.3 0.3 collective-permute-done
  10.7 8.0 %collective-permute-done.1 = bf16[24,2176]{1,0:T(8,128)(2,1)S(1)} collective-permute-done((bf16[24,2176]{1,0:T(8,128)(2,1)S(1)}, bf16[24,2176]{1,0:T(8,128)(2,1)S(1)}, u32[]{:S(2)}, u32[]{:S(2)}) %collective-permute-start.1) | collective-permute-done | bytes 104480 | tf_op jit(solution)/shard_map/ppermute | solution.py:438
  18.7 1.6 collective-permute-start.4
  20.2 1.5 collective-permute-start.5
  21.7 1.0 constant_dynamic-slice_fusion
  22.8 1.7 %collective-permute-start.12 = (bf16[192,1024]{1,0:T(8,128)(2,1)S(1)}, bf16[192,1024]{1,0:T(8,128)(2,1)S(1)}, u32[]{:S(2)}, u32[]{:S(2)}) collective-permute-start(bf16[192,1024]{1,0:T(8,128)(2,1)S(1)} %bitcast.9), channel_id=1, source_target_pairs={{0,8},{8,0},{16,24},{24,16},{1,9},{9,1},{17,25},{25,17},{2,10},{10... | collective-permute-start | bytes 1179656 | tf_op jit(solution)/shard_map/ppermute | solution.py:438
  24.5 1.4 collective-permute-start.13
  25.9 1.8 %cut.1 = bf16[4,192,256]{2,1,0:T(8,128)(2,1)} custom-call(bf16[3,64,8192]{2,1,0:T(8,128)(2,1)} %cond_ref.3), custom_call_target="tpu_custom_call" | custom-call | tf_op jit(solution)/shard_map/cut/pallas_call | solution.py:494
  27.7 3.5 %all-to-all-start = ((bf16[4,192,256]{2,1,0:T(8,128)(2,1)}), bf16[4,192,256]{2,1,0:T(8,128)(2,1)S(1)}, u32[]{:S(2)}, u32[]{:S(2)}) async-start(bf16[4,192,256]{2,1,0:T(8,128)(2,1)} %cut.1), calls=%async_computation | async-start | bytes 786432 | tf_op jit(solution)/shard_map/all_to_all | solution.py:502
  31.2 3.7 %turn.1.refs_1_ = bf16[2048,1024]{1,0:T(8,128)(2,1)} custom-call(bf16[1024,2048]{1,0:T(8,128)(2,1)} %scr_ref.1), custom_call_target="tpu_custom_call" | custom-call | bytes 8388608 | tf_op jit(solution)/shard_map/turn/pallas_call | solution.py:506
  34.9 0.6 collective-permute-start.8
  35.5 0.6 collective-permute-start.9
  36.1 5.8 %collective-permute-done.12.refs_5_ = bf16[192,1024]{1,0:T(8,128)(2,1)S(1)} collective-permute-done((bf16[192,1024]{1,0:T(8,128)(2,1)S(1)}, bf16[192,1024]{1,0:T(8,128)(2,1)S(1)}, u32[]{:S(2)}, u32[]{:S(2)}) %collective-permute-start.12) | collective-permute-done | bytes 393248 | tf_op jit(solution)/shard_map/ppermute | solution.py:438
  41.9 1.9 %collective-permute-done.13.refs_6_ = bf16[192,1024]{1,0:T(8,128)(2,1)S(1)} collective-permute-done((bf16[192,1024]{1,0:T(8,128)(2,1)S(1)}, bf16[192,1024]{1,0:T(8,128)(2,1)S(1)}, u32[]{:S(2)}, u32[]{:S(2)}) %collective-permute-start.13) | collective-permute-done | bytes 393248 | tf_op jit(solution)/shard_map/ppermute | solution.py:438
  43.8 7.8 %collective-permute-start.14 = (bf16[192,1024]{1,0:T(8,128)(2,1)S(1)}, bf16[192,1024]{1,0:T(8,128)(2,1)S(1)}, u32[]{:S(2)}, u32[]{:S(2)}) collective-permute-start(bf16[192,1024]{1,0:T(8,128)(2,1)S(1)} %bitcast.11), channel_id=1, source_target_pairs={{0,24},{8,16},{16,8},{24,0},{1,25},{9,17},{17,9},{25,1},{2,26},{10... | collective-permute-start | bytes 1179656 | tf_op jit(solution)/shard_map/ppermute | solution.py:438
  51.8 0.3 collective-permute-start.11
  52.1 0.9 collective-permute-done.10.refs_8_
  53.1 0.3 collective-permute-done.11.refs_9_
  53.4 0.3 copy-done.15
  53.8 0.3 copy-done.16
  54.2 0.8 copy-done.11
  55.0 5.7 %order.1 = (bf16[768,2048]{1,0:T(8,128)(2,1)}, bf16[2048,768]{1,0:T(8,128)(2,1)}, bf16[768,256]{1,0:T(8,128)(2,1)}, bf16[32,16,128]{2,1,0:T(8,128)(2,1)}) custom-call(bf16[96,2176]{1,0:T(8,128)(2,1)} %copy-done.6, bf16[96,2176]{1,0:T(8,128)(2,1)} %copy-done.9, bf16[96,2176]{1,0:T(8,128)(2,1)} %copy-done.7, bf16[96,2176]{1,0:T(8,128)(2,1)} %copy-done.10, ...), custom_call_target="tpu_custom_call" | custom-call | bytes 9437184 | tf_op jit(solution)/shard_map/order/pallas_call | solution.py:523
  60.7 0.8 copy-done.5
  61.5 2.2 %density.2 = (bf16[3,256,256]{2,1,0:T(8,128)(2,1)}, f32[32,2,128]{2,1,0:T(2,128)}) custom-call(bf16[32,16,128]{2,1,0:T(8,128)(2,1)} %get-tuple-element.47.refs_0_.msgs_ref, bf16[768,256]{1,0:T(8,128)(2,1)} %get-tuple-element.48.refs_1_.refs_3_, bf16[4,192,256]{2,1,0:T(8,128)(2,1)} %copy-done.5), custom_call_target="tpu_custom_call" | custom-call | tf_op jit(solution)/shard_map/density/pallas_call | solution.py:550
  63.6 2.7 %all-to-all-start.1 = ((f32[32,2,128]{2,1,0:T(2,128)}), f32[32,2,128]{2,1,0:T(2,128)S(1)}, u32[]{:S(2)}, u32[]{:S(2)}) async-start(f32[32,2,128]{2,1,0:T(2,128)} %get-tuple-element.49), calls=%async_computation.1 | async-start | bytes 65536 | tf_op jit(solution)/shard_map/all_to_all | solution.py:30
  66.4 0.7 copy-done.21
  67.2 12.6 %direct.2.refs_1_ = f32[6,128,128]{2,1,0:T(8,128)} custom-call(bf16[2048,768]{1,0:T(8,128)(2,1)} %get-tuple-element.50.refs_0_, bf16[2048,1024]{1,0:T(8,128)(2,1)} %turn.1.refs_1_, bf16[768,2048]{1,0:T(8,128)(2,1)} %get-tuple-element.52.refs_2_, bf16[3,256,256]{2,1,0:T(8,128)(2,1)} %get-tuple-element.53.refs_3_, bf16[192,1024]{1,0:T(8,128)(2,1)} %bitcast.12, ...), custom_call_target="tpu_custom_call" | custom-call | flops 6442450944 | bytes 12582912 | tf_op jit(solution)/shard_map/direct/pallas_call | solution.py:569
  79.8 0.6 copy-done.18
  80.4 4.1 %exchange.2 = bf16[32,16,128]{2,1,0:T(8,128)(2,1)} custom-call(f32[32,2,128]{2,1,0:T(2,128)} %copy-done.18, f32[6,128,128]{2,1,0:T(8,128)} %direct.2.refs_1_, bf16[256,8192]{1,0:T(8,128)(2,1)} %refs_2_.3, bf16[768,256]{1,0:T(8,128)(2,1)} %get-tuple-element.48.refs_1_.refs_3_, bf16[4,192,256]{2,1,0:T(8,128)(2,1)} %copy-done.5), custom_call_target="tpu_custom_call" | custom-call | tf_op jit(solution)/shard_map/exchange/pallas_call | solution.py:592
  84.5 13.9 %all_to_all.35.recv_ref = bf16[32,16,128]{2,1,0:T(8,128)(2,1)S(1)} all-to-all(bf16[32,16,128]{2,1,0:T(8,128)(2,1)} %exchange.2), channel_id=1, replica_groups=mesh['ka'=4,'band'=8] {'ka','band'}, dimensions={0} | all-to-all | bytes 262144 | tf_op jit(solution)/shard_map/all_to_all | solution.py:30
  98.5 0.8 first_owner.1
  99.3 10.6 %all_to_all.36.refs_0_.msgs_ref = bf16[32,16,128]{2,1,0:T(8,128)(2,1)} all-to-all(bf16[32,16,128]{2,1,0:T(8,128)(2,1)S(1)} %get-tuple-element.58), channel_id=1, replica_groups=mesh['ka'=4,'band'=8] {'ka','band'}, dimensions={0} | all-to-all | bytes 262144 | tf_op jit(solution)/shard_map/all_to_all | solution.py:30
  109.9 2.2 %density.3 = (bf16[3,256,256]{2,1,0:T(8,128)(2,1)}, f32[32,2,128]{2,1,0:T(2,128)}) custom-call(bf16[32,16,128]{2,1,0:T(8,128)(2,1)} %all_to_all.36.refs_0_.msgs_ref, bf16[768,256]{1,0:T(8,128)(2,1)} %get-tuple-element.48.refs_1_.refs_3_, bf16[4,192,256]{2,1,0:T(8,128)(2,1)} %copy-done.5), custom_call_target="tpu_custom_call" | custom-call | tf_op jit(solution)/shard_map/density/pallas_call | solution.py:550
  112.1 2.8 %all-to-all-start.4 = ((f32[32,2,128]{2,1,0:T(2,128)}), f32[32,2,128]{2,1,0:T(2,128)S(1)}, u32[]{:S(2)}, u32[]{:S(2)}) async-start(f32[32,2,128]{2,1,0:T(2,128)} %get-tuple-element.59), calls=%async_computation.4 | async-start | bytes 65536 | tf_op jit(solution)/shard_map/all_to_all | solution.py:30
  114.9 12.6 %direct.3.refs_1_ = f32[6,128,128]{2,1,0:T(8,128)} custom-call(bf16[2048,768]{1,0:T(8,128)(2,1)} %get-tuple-element.50.refs_0_, bf16[2048,1024]{1,0:T(8,128)(2,1)} %turn.1.refs_1_, bf16[768,2048]{1,0:T(8,128)(2,1)} %get-tuple-element.52.refs_2_, bf16[3,256,256]{2,1,0:T(8,128)(2,1)} %get-tuple-element.60.refs_3_, bf16[192,1024]{1,0:T(8,128)(2,1)} %bitcast.13, ...), custom_call_target="tpu_custom_call" | custom-call | flops 6442450944 | bytes 12582912 | tf_op jit(solution)/shard_map/direct/pallas_call | solution.py:569
  127.5 0.6 copy-done.17
  128.1 4.1 %exchange.3 = bf16[32,16,128]{2,1,0:T(8,128)(2,1)} custom-call(f32[32,2,128]{2,1,0:T(2,128)} %copy-done.17, f32[6,128,128]{2,1,0:T(8,128)} %direct.3.refs_1_, bf16[256,8192]{1,0:T(8,128)(2,1)} %refs_2_.3, bf16[768,256]{1,0:T(8,128)(2,1)} %get-tuple-element.48.refs_1_.refs_3_, bf16[4,192,256]{2,1,0:T(8,128)(2,1)} %copy-done.5), custom_call_target="tpu_custom_call" | custom-call | tf_op jit(solution)/shard_map/exchange/pallas_call | solution.py:592
  132.3 13.9 %all_to_all.37.recv_ref = bf16[32,16,128]{2,1,0:T(8,128)(2,1)S(1)} all-to-all(bf16[32,16,128]{2,1,0:T(8,128)(2,1)} %exchange.3), channel_id=1, replica_groups=mesh['ka'=4,'band'=8] {'ka','band'}, dimensions={0} | all-to-all | bytes 262144 | tf_op jit(solution)/shard_map/all_to_all | solution.py:30
  146.1 1.3 second_owner.1
  147.5 9.0 %all_to_all.38.msgs_ref = f32[32,2,128]{2,1,0:T(2,128)S(1)} all-to-all(f32[32,2,128]{2,1,0:T(2,128)S(1)} %get-tuple-element.63), channel_id=1, replica_groups=mesh['ka'=4,'band'=8] {'ka','band'}, dimensions={0} | all-to-all | bytes 65536 | tf_op jit(solution)/shard_map/all_to_all | solution.py:30
  156.5 1.3 finish.1
  (56 shorter events, 0.5 us)
Async XLA Ops:
  0.7 0.7 copy-start.2
  1.4 0.7 copy-start.3
  2.0 0.7 copy-start.4
  4.6 6.0 %collective-permute-start = (bf16[24,2176]{1,0:T(8,128)(2,1)S(1)}, bf16[24,2176]{1,0:T(8,128)(2,1)S(1)}, u32[]{:S(2)}, u32[]{:S(2)}) collective-permute-start(bf16[24,2176]{1,0:T(8,128)(2,1)S(1)} %get-tuple-element.70), channel_id=1, source_target_pairs={{0,8},{8,0},{16,24},{24,16},{1,9},{9,1},{17,25},{25,17},{2,10},{10... | collective-permute-start | bytes 313352 | tf_op jit(solution)/shard_map/ppermute | solution.py:438
  7.7 10.9 %collective-permute-start.1 = (bf16[24,2176]{1,0:T(8,128)(2,1)S(1)}, bf16[24,2176]{1,0:T(8,128)(2,1)S(1)}, u32[]{:S(2)}, u32[]{:S(2)}) collective-permute-start(bf16[24,2176]{1,0:T(8,128)(2,1)S(1)} %get-tuple-element.71), channel_id=1, source_target_pairs={{0,16},{8,24},{16,0},{24,8},{1,17},{9,25},{17,1},{25,9},{2,18},{10... | collective-permute-start | bytes 313352 | tf_op jit(solution)/shard_map/ppermute | solution.py:438
  10.3 8.3 %collective-permute-start.2 = (bf16[24,2176]{1,0:T(8,128)(2,1)S(1)}, bf16[24,2176]{1,0:T(8,128)(2,1)S(1)}, u32[]{:S(2)}, u32[]{:S(2)}) collective-permute-start(bf16[24,2176]{1,0:T(8,128)(2,1)S(1)} %get-tuple-element.72), channel_id=1, source_target_pairs={{0,24},{8,16},{16,8},{24,0},{1,25},{9,17},{17,9},{25,1},{2,26},{10... | collective-permute-start | bytes 313352 | tf_op jit(solution)/shard_map/ppermute | solution.py:438
  18.6 16.2 %copy-start.6 = (bf16[96,2176]{1,0:T(8,128)(2,1)}, bf16[96,2176]{1,0:T(8,128)(2,1)S(1)}, u32[]{:S(2)}) copy-start(bf16[96,2176]{1,0:T(8,128)(2,1)S(1)} %pad_maximum_fusion.refs_0_) | copy-start | bytes 1253380
  18.7 16.2 %collective-permute-start.4 = (bf16[96,2176]{1,0:T(8,128)(2,1)S(1)}, bf16[96,2176]{1,0:T(8,128)(2,1)S(1)}, u32[]{:S(2)}, u32[]{:S(2)}) collective-permute-start(bf16[96,2176]{1,0:T(8,128)(2,1)S(1)} %pad_maximum_fusion.refs_0_), channel_id=1, source_target_pairs={{0,2},{1,3},{2,0},{3,1},{4,6},{5,7},{6,4},{7,5},{8,10},{9,11},{10,... | collective-permute-start | bytes 1253384 | tf_op jit(solution)/shard_map/ppermute | solution.py:438
  20.2 14.7 %collective-permute-start.5 = (bf16[96,2176]{1,0:T(8,128)(2,1)S(1)}, bf16[96,2176]{1,0:T(8,128)(2,1)S(1)}, u32[]{:S(2)}, u32[]{:S(2)}) collective-permute-start(bf16[96,2176]{1,0:T(8,128)(2,1)S(1)} %pad_maximum_fusion.refs_0_), channel_id=1, source_target_pairs={{0,4},{1,5},{2,6},{3,7},{4,0},{5,1},{6,2},{7,3},{8,12},{9,13},{10,... | collective-permute-start | bytes 1253384 | tf_op jit(solution)/shard_map/ppermute | solution.py:438
  22.8 21.1 %copy-start.12 = (bf16[3,64,1024]{2,1,0:T(8,128)(2,1)}, bf16[3,64,1024]{2,1,0:T(8,128)(2,1)S(1)}, u32[]{:S(2)}) copy-start(bf16[3,64,1024]{2,1,0:T(8,128)(2,1)S(1)} %constant_dynamic-slice_fusion) | copy-start | bytes 1179652
  22.8 19.1 %collective-permute-start.12 = (bf16[192,1024]{1,0:T(8,128)(2,1)S(1)}, bf16[192,1024]{1,0:T(8,128)(2,1)S(1)}, u32[]{:S(2)}, u32[]{:S(2)}) collective-permute-start(bf16[192,1024]{1,0:T(8,128)(2,1)S(1)} %bitcast.9), channel_id=1, source_target_pairs={{0,8},{8,0},{16,24},{24,16},{1,9},{9,1},{17,25},{25,17},{2,10},{10... | collective-permute-start | bytes 1179656 | tf_op jit(solution)/shard_map/ppermute | solution.py:438
  24.5 19.3 %collective-permute-start.13 = (bf16[192,1024]{1,0:T(8,128)(2,1)S(1)}, bf16[192,1024]{1,0:T(8,128)(2,1)S(1)}, u32[]{:S(2)}, u32[]{:S(2)}) collective-permute-start(bf16[192,1024]{1,0:T(8,128)(2,1)S(1)} %bitcast.10), channel_id=1, source_target_pairs={{0,16},{8,24},{16,0},{24,8},{1,17},{9,25},{17,1},{25,9},{2,18},{10... | collective-permute-start | bytes 1179656 | tf_op jit(solution)/shard_map/ppermute | solution.py:438
  25.9 17.9 %collective-permute-start.3 = (bf16[96,2176]{1,0:T(8,128)(2,1)S(1)}, bf16[96,2176]{1,0:T(8,128)(2,1)S(1)}, u32[]{:S(2)}, u32[]{:S(2)}) collective-permute-start(bf16[96,2176]{1,0:T(8,128)(2,1)S(1)} %pad_maximum_fusion.refs_0_), channel_id=1, source_target_pairs={{0,1},{1,0},{2,3},{3,2},{4,5},{5,4},{6,7},{7,6},{8,9},{9,8},{10,11... | collective-permute-start | bytes 1253384 | tf_op jit(solution)/shard_map/ppermute | solution.py:438
  27.7 33.0 %all-to-all-start = ((bf16[4,192,256]{2,1,0:T(8,128)(2,1)}), bf16[4,192,256]{2,1,0:T(8,128)(2,1)S(1)}, u32[]{:S(2)}, u32[]{:S(2)}) async-start(bf16[4,192,256]{2,1,0:T(8,128)(2,1)} %cut.1), calls=%async_computation | async-start | bytes 786432 | tf_op jit(solution)/shard_map/all_to_all | solution.py:502
  34.9 18.5 %copy-start.7 = (bf16[96,2176]{1,0:T(8,128)(2,1)}, bf16[96,2176]{1,0:T(8,128)(2,1)S(1)}, u32[]{:S(2)}) copy-start(bf16[96,2176]{1,0:T(8,128)(2,1)S(1)} %collective-permute-done.4.refs_2_) | copy-start | bytes 1253380
  34.9 18.5 %copy-start.8 = (bf16[96,2176]{1,0:T(8,128)(2,1)}, bf16[96,2176]{1,0:T(8,128)(2,1)S(1)}, u32[]{:S(2)}) copy-start(bf16[96,2176]{1,0:T(8,128)(2,1)S(1)} %collective-permute-done.5.refs_4_) | copy-start | bytes 1253380
  34.9 16.7 %collective-permute-start.8 = (bf16[48,2176]{1,0:T(8,128)(2,1)S(1)}, bf16[48,2176]{1,0:T(8,128)(2,1)S(1)}, u32[]{:S(2)}, u32[]{:S(2)}) collective-permute-start(bf16[48,2176]{1,0:T(8,128)(2,1)S(1)} %slice.6), channel_id=1, source_target_pairs={{0,4},{1,5},{2,6},{3,7},{4,0},{5,1},{6,2},{7,3},{8,12},{9,13},{10,... | collective-permute-start | bytes 626696 | tf_op jit(solution)/shard_map/ppermute | solution.py:438
  35.5 16.3 %collective-permute-start.9 = (bf16[48,2176]{1,0:T(8,128)(2,1)S(1)}, bf16[48,2176]{1,0:T(8,128)(2,1)S(1)}, u32[]{:S(2)}, u32[]{:S(2)}) collective-permute-start(bf16[48,2176]{1,0:T(8,128)(2,1)S(1)} %slice.7), channel_id=1, source_target_pairs={{0,2},{1,3},{2,0},{3,1},{4,6},{5,7},{6,4},{7,5},{8,10},{9,11},{10,... | collective-permute-start | bytes 626696 | tf_op jit(solution)/shard_map/ppermute | solution.py:438
  41.9 24.5 %copy-start.19 = (bf16[192,1024]{1,0:T(8,128)(2,1)}, bf16[192,1024]{1,0:T(8,128)(2,1)S(1)}, u32[]{:S(2)}) copy-start(bf16[192,1024]{1,0:T(8,128)(2,1)S(1)} %collective-permute-done.12.refs_5_) | copy-start | bytes 1179652
  41.9 11.5 %collective-permute-start.6 = (bf16[96,2176]{1,0:T(8,128)(2,1)S(1)}, bf16[96,2176]{1,0:T(8,128)(2,1)S(1)}, u32[]{:S(2)}, u32[]{:S(2)}) collective-permute-start(bf16[96,2176]{1,0:T(8,128)(2,1)S(1)} %collective-permute-done.4.refs_2_), channel_id=1, source_target_pairs={{0,1},{1,0},{2,3},{3,2},{4,5},{5,4},{6,7},{7,6},{8,9},{9,8},{10,11... | collective-permute-start | bytes 1253384 | tf_op jit(solution)/shard_map/ppermute | solution.py:438
  43.8 22.6 %copy-start.20 = (bf16[192,1024]{1,0:T(8,128)(2,1)}, bf16[192,1024]{1,0:T(8,128)(2,1)S(1)}, u32[]{:S(2)}) copy-start(bf16[192,1024]{1,0:T(8,128)(2,1)S(1)} %collective-permute-done.13.refs_6_) | copy-start | bytes 1179652
  43.8 9.6 %collective-permute-start.7 = (bf16[96,2176]{1,0:T(8,128)(2,1)S(1)}, bf16[96,2176]{1,0:T(8,128)(2,1)S(1)}, u32[]{:S(2)}, u32[]{:S(2)}) collective-permute-start(bf16[96,2176]{1,0:T(8,128)(2,1)S(1)} %collective-permute-done.5.refs_4_), channel_id=1, source_target_pairs={{0,1},{1,0},{2,3},{3,2},{4,5},{5,4},{6,7},{7,6},{8,9},{9,8},{10,11... | collective-permute-start | bytes 1253384 | tf_op jit(solution)/shard_map/ppermute | solution.py:438
  43.8 9.6 %copy-start.9 = (bf16[96,2176]{1,0:T(8,128)(2,1)}, bf16[96,2176]{1,0:T(8,128)(2,1)S(1)}, u32[]{:S(2)}) copy-start(bf16[96,2176]{1,0:T(8,128)(2,1)S(1)} %collective-permute-done.3.refs_1_) | copy-start | bytes 1253380
  43.8 22.5 %collective-permute-start.14 = (bf16[192,1024]{1,0:T(8,128)(2,1)S(1)}, bf16[192,1024]{1,0:T(8,128)(2,1)S(1)}, u32[]{:S(2)}, u32[]{:S(2)}) collective-permute-start(bf16[192,1024]{1,0:T(8,128)(2,1)S(1)} %bitcast.11), channel_id=1, source_target_pairs={{0,24},{8,16},{16,8},{24,0},{1,25},{9,17},{17,9},{25,1},{2,26},{10... | collective-permute-start | bytes 1179656 | tf_op jit(solution)/shard_map/ppermute | solution.py:438
  51.6 1.8 %copy-start.13 = (bf16[48,2176]{1,0:T(8,128)(2,1)}, bf16[48,2176]{1,0:T(8,128)(2,1)S(1)}, u32[]{:S(2)}) copy-start(bf16[48,2176]{1,0:T(8,128)(2,1)S(1)} %collective-permute-done.8.refs_6_) | copy-start | bytes 626692
  51.6 1.5 collective-permute-start.10
  51.8 1.6 %copy-start.14 = (bf16[48,2176]{1,0:T(8,128)(2,1)}, bf16[48,2176]{1,0:T(8,128)(2,1)S(1)}, u32[]{:S(2)}) copy-start(bf16[48,2176]{1,0:T(8,128)(2,1)S(1)} %collective-permute-done.9.refs_7_) | copy-start | bytes 626692
  51.8 1.5 collective-permute-start.11
  53.1 0.7 copy-start.15
  53.4 0.7 copy-start.16
  53.4 0.8 copy-start.10
  54.2 0.8 copy-start.11
  60.7 0.8 copy-start.5
  63.6 16.2 %all-to-all-start.1 = ((f32[32,2,128]{2,1,0:T(2,128)}), f32[32,2,128]{2,1,0:T(2,128)S(1)}, u32[]{:S(2)}, u32[]{:S(2)}) async-start(f32[32,2,128]{2,1,0:T(2,128)} %get-tuple-element.49), calls=%async_computation.1 | async-start | bytes 65536 | tf_op jit(solution)/shard_map/all_to_all | solution.py:30
  66.4 0.8 copy-start.21
  79.8 18.6 %copy-start.1 = (bf16[32,16,128]{2,1,0:T(8,128)(2,1)S(1)}, bf16[32,16,128]{2,1,0:T(8,128)(2,1)}, u32[]{:S(2)}) copy-start(bf16[32,16,128]{2,1,0:T(8,128)(2,1)} %get-tuple-element.47.refs_0_.msgs_ref) | copy-start | bytes 393220
  79.8 0.6 copy-start.18
  112.1 15.4 %all-to-all-start.4 = ((f32[32,2,128]{2,1,0:T(2,128)}), f32[32,2,128]{2,1,0:T(2,128)S(1)}, u32[]{:S(2)}, u32[]{:S(2)}) async-start(f32[32,2,128]{2,1,0:T(2,128)} %get-tuple-element.59), calls=%async_computation.4 | async-start | bytes 65536 | tf_op jit(solution)/shard_map/all_to_all | solution.py:30
  127.5 18.6 %copy-start = (bf16[32,16,128]{2,1,0:T(8,128)(2,1)S(1)}, bf16[32,16,128]{2,1,0:T(8,128)(2,1)}, u32[]{:S(2)}) copy-start(bf16[32,16,128]{2,1,0:T(8,128)(2,1)} %all_to_all.36.refs_0_.msgs_ref) | copy-start | bytes 393220
  127.5 0.6 copy-start.17

commit v10 on v9

--- a/solution.py
+++ b/solution.py
@@ -71,28 +71,20 @@
     return out
 
 
-def block_copies(groups, width, dest, sems, column=0):
+def piece_copies(refs, parts, column, width, dest, sems):
     copies = []
-    for d, refs in enumerate(groups):
+    for d, piece in enumerate(parts):
         row = 0
-        for ref in refs:
+        for ref, start, rows in piece:
             copies.append(
                 pltpu.make_async_copy(
-                    ref.at[:, pl.ds(column, width)],
-                    dest.at[d, pl.ds(row, ref.shape[0]), :],
+                    refs[ref].at[pl.ds(start, rows), pl.ds(column, width)],
+                    dest.at[d, pl.ds(row, rows), :],
                     sems.at[len(copies)],
                 )
             )
-            row += ref.shape[0]
+            row += rows
     return copies
-
-
-def split_refs(refs, counts):
-    out, at = [], 0
-    for count in counts:
-        out.append(refs[at : at + count])
-        at += count
-    return out
 
 
 def start_all(copies):
@@ -124,7 +116,11 @@
     return part.reshape(part.shape[0] * 2 * ROWS, part.shape[2])
 
 
-def pack_kernel(start_ref, cond_ref, val_ref, own_ref, gap_ref, msg_ref):
+def pack_kernel(start_in, cond_in, val_in, own_ref, gap_ref, msg_ref, start_ref, cond_ref, val_ref, sems):
+    ins = ((start_in, start_ref), (cond_in, cond_ref), (val_in, val_ref))
+    copies = [pltpu.make_async_copy(ref, to, sems.at[i]) for i, (ref, to) in enumerate(ins)]
+    start_all(copies)
+    wait_all(copies)
     own_ref[...] = jnp.zeros_like(own_ref)
     gap_ref[...] = jnp.zeros_like(gap_ref)
     cond = jnp.concatenate([cond_ref[...], cond_ref[...]], axis=1)
@@ -175,14 +171,13 @@
     wait_all(outs)
 
 
-def order_kernel(counts, n_ka, *refs):
-    n_val = sum(counts)
-    val_refs, refs = split_refs(refs[:n_val], counts), refs[n_val:]
+def order_kernel(parts, n_ka, *refs):
+    val_refs, refs = refs[:-10], refs[-10:]
     rows_out, turned_out, own_out, msgs_out, vals, heads, ordered, turned, val_sems, out_sems = refs
     own = own_out.shape[1]
     nu = ordered.shape[1]
-    copies = block_copies(val_refs, nu, vals, val_sems.at[0])
-    head_copies = block_copies(val_refs, LANES, heads, val_sems.at[1], nu)
+    copies = piece_copies(val_refs, parts, 0, nu, vals, val_sems.at[0])
+    head_copies = piece_copies(val_refs, parts, nu, LANES, heads, val_sems.at[1])
     start_all(copies + head_copies)
     wait_all(copies)
     n_band, group = vals.shape[0], vals.shape[0] * 2 * ROWS
@@ -247,13 +242,26 @@
 
 def direct_kernel(n_ka, tile, scale, *refs):
     turned_ref, scr_ref, rows_ref, qx_ref, refs = refs[0], refs[1], refs[2], refs[3], refs[4:]
-    cond_refs, refs = refs[:n_ka], refs[n_ka:]
+    hops = [(0, 0)] + [(way, hop) for way in (-1, 1) for hop in range(1, n_ka)]
+    cond_refs, refs = refs[: len(hops)], refs[len(hops) :]
     di_ref, qx, turned, conds, scrs, vals, mixed, kern, folded = refs[:9]
     qx_sem, cond_sems, row_sem, chunk_sems = refs[9:]
     nu, mu = scr_ref.shape
     quad = 2 * LANES
     qx_copy = pltpu.make_async_copy(qx_ref, qx, qx_sem.at[0])
-    cond_copies = block_copies([[ref] for ref in cond_refs], mu, conds, cond_sems)
+    ka = lax.axis_index("ka")
+
+    def each_cond(act):
+        for i, (way, hop) in enumerate(hops):
+            origin = ka + way * hop
+            pl.when((origin >= 0) & (origin < n_ka))(
+                lambda i=i, origin=origin: act(
+                    pltpu.make_async_copy(
+                        cond_refs[i], conds.at[jnp.bitwise_xor(ka, origin)], cond_sems.at[i]
+                    )
+                )
+            )
+
     turned_copies, scr_copies = [], []
     for i in range(nu // tile):
         at = pl.ds(i * tile, tile)
@@ -264,7 +272,9 @@
             pltpu.make_async_copy(scr_ref.at[at, :], scrs.at[at, :], chunk_sems.at[1, i])
         )
     row_copy = pltpu.make_async_copy(rows_ref, vals, row_sem.at[0])
-    start_all([qx_copy, turned_copies[0]] + cond_copies + [scr_copies[0]])
+    start_all([qx_copy, turned_copies[0]])
+    each_cond(lambda copy: copy.start())
+    scr_copies[0].start()
     for i in range(1, nu // tile):
         start_all([turned_copies[i], scr_copies[i]])
     row_copy.start()
@@ -278,7 +288,7 @@
                 turned[rows, cols], qx[kq], preferred_element_type=F32
             ).astype(BF)
         if i == 0:
-            wait_all(cond_copies)
+            each_cond(lambda copy: copy.wait())
             cond_rows = conds[...].reshape(-1, mu)
         scr_copies[i].wait()
         amp = jnp.dot(mixed[rows, :], cond_rows, preferred_element_type=F32)
@@ -438,16 +448,42 @@
     return lax.ppermute(block, axis, [(i, i ^ d) for i in range(lax.axis_size(axis))])
 
 
+def line_gather(block, axis):
+    n = lax.axis_size(axis)
+    flows = []
+    for way in (-1, 1):
+        moving, flow = block, []
+        for hop in range(1, n):
+            senders = [i for i in range(n) if 0 <= i + way * (hop - 1) < n and 0 <= i - way < n]
+            moving = lax.ppermute(moving, axis, [(i, i - way) for i in senders])
+            flow.append(moving)
+        flows.append(flow)
+    return flows
+
+
 def plane_pieces(own_piece, others):
     def move(block, d):
         return swap(block, "band", d)
 
-    half = own_piece.shape[0] // 2
-    core, by_x, by_y = move(own_piece, 1), move(own_piece, 2), move(own_piece, 4)
+    rows = own_piece.shape[0]
+    half = rows // 2
+    by_x, by_y = move(own_piece, 2), move(own_piece, 4)
     by_x, by_y, others = lax.optimization_barrier((by_x, by_y, others))
     diag = [move(by_x[:half], 4), move(by_y[half:], 2)]
-    pieces = [[own_piece], [core], [by_x], [move(by_x, 1)], [by_y], [move(by_y, 1)]]
-    return pieces + [diag, [move(part, 1) for part in diag]], others
+    near = move(jnp.concatenate([own_piece, by_x, by_y], axis=0), 1)
+    far = move(jnp.concatenate(diag, axis=0), 1)
+    arrays = [own_piece, by_x, by_y, diag[0], diag[1], near, far]
+    parts = (
+        ((0, 0, rows),),
+        ((5, 0, rows),),
+        ((1, 0, rows),),
+        ((5, rows, rows),),
+        ((2, 0, rows),),
+        ((5, 2 * rows, rows),),
+        ((3, 0, half), (4, 0, half)),
+        ((6, 0, rows),),
+    )
+    return arrays, parts, others
 
 
 def kernel_path(start_vec, val_energy, cond_energy, val_orb, cond_orb, coulomb, screened):
@@ -473,9 +509,14 @@
         pack_kernel,
         "pack",
         (shape_of(block), shape_of(block), shape_of(block, BF)),
-        [VMEM, VMEM, SMEM],
+        [ANY] * 3,
         (VMEM, VMEM, VMEM),
-        mib=8,
+        [
+            pltpu.VMEM(start_vec.shape, F32),
+            pltpu.VMEM(cond_energy.shape, F32),
+            pltpu.SMEM(val_energy.shape, F32),
+            dma(3),
+        ],
     )(start_vec, cond_energy, val_energy)
 
     head = jnp.pad(message, ((0, k_dev * nv_blk - block[0]), (0, 0)))
@@ -489,7 +530,7 @@
     )
     cond_local = lax.dynamic_slice_in_dim(cond_orb, band * mu_blk, mu_blk, 2)
     cond_local = cond_local.reshape(k_dev * n_cond, mu_blk)
-    cond_pts = [cond_local] + [swap(cond_local, "ka", j) for j in range(1, n_ka)]
+    below, above = line_gather(cond_local, "ka")
     own_rows = k_dev * n_cond
     cuts = call(
         cut_kernel,
@@ -513,15 +554,13 @@
         + [dma(2 * nu_blk // tile)] * 2,
         moved=8 * MIB,
     )(screened)
-    pieces, scr_turned = plane_pieces(val_cut, scr_turned)
-    pieces, cond_pts[1 : n_ka - 1] = lax.optimization_barrier(
-        (pieces, cond_pts[1 : n_ka - 1])
+    pieces, parts, (scr_turned, below[0], above[0]) = plane_pieces(
+        val_cut, (scr_turned, below[0], above[0])
     )
-    counts = tuple(len(piece) for piece in pieces)
-    flat = [ref for piece in pieces for ref in piece]
-    n_copies = len(flat)
+    pieces, below[1:-1], above[1:-1] = lax.optimization_barrier((pieces, below[1:-1], above[1:-1]))
+    cond_pts = [cond_local] + below + above
     val_rows, val_turned, val_own, msgs = call(
-        functools.partial(order_kernel, counts, n_ka),
+        functools.partial(order_kernel, parts, n_ka),
         "order",
         (
             shape_of((rows_all, nu_blk), BF),
@@ -529,18 +568,18 @@
             shape_of((rows_all, own), BF),
             msg_shape,
         ),
-        [ANY] * n_copies,
+        [ANY] * len(pieces),
         (ANY, ANY, ANY, VMEM),
         [
             pltpu.VMEM((n_band, piece_rows, nu_blk), BF),
             pltpu.VMEM((n_band, piece_rows, LANES), BF),
             pltpu.VMEM((rows_all, nu_blk), BF),
             pltpu.VMEM((nu_blk, rows_all), BF),
-            dma(2, n_copies),
+            dma(2, sum(len(piece) for piece in parts)),
             dma(3, pairs),
         ],
         moved=9 * MIB,
-    )(*flat)
+    )(*pieces)
 
     cfg = (n_ka, n_band, k_dev)
     quads = k_points // 4
@@ -582,14 +621,14 @@
                 pltpu.VMEM((nu_blk, mu_blk), BF),
                 pltpu.VMEM((rows_all, mu_blk), BF),
                 dma(1),
-                dma(n_ka),
+                dma(len(cond_pts)),
                 dma(1),
                 dma(2, nu_blk // tile),
             ],
             flops=4 * mu_blk * nu_blk * conds_all,
             moved=12 * MIB,
         )(val_turned, scr_turned, val_rows, qx, *cond_pts)
-        parts = call(
+        summed = call(
             functools.partial(exchange_kernel, cfg, chunk, scale),
             "exchange",
             msg_shape,
@@ -608,7 +647,7 @@
                 dma(3),
             ],
         )(density, direct, coulomb, val_own, cond_own)
-        recv = exchange_all(parts)
+        recv = exchange_all(summed)
         if first:
             state, coef, message = call(
                 functools.partial(first_owner_kernel, count_all),

time: 159 us -> 166 us (1.044)
  starting transfers between devices: 30.3 us -> 39.1 us
  waiting for transfers between devices: 17.2 us -> 11.6 us
  local copies, waits for them, and re-layouts: 8.49 us -> 11 us
    ppermute x15 -> x9, waiting for transfers between devices: 17.2 us -> 4.35 us  [swap(): lax.ppermute(block, axis, [(i, i ^ d) for i in range(lax.axis_size(axis))])]
    ppermute x15 -> x9, starting transfers between devices: 21.3 us -> 10.9 us  [swap(): lax.ppermute(block, axis, [(i, i ^ d) for i in range(lax.axis_size(axis))])]
    ppermute x0 -> x6, starting transfers between devices: none -> 8.78 us  [line_gather(): moving = lax.ppermute(moving, axis, [(i, i - way) for i in senders])]
    ppermute x0 -> x6, waiting for transfers between devices: none -> 7.21 us  [line_gather(): moving = lax.ppermute(moving, axis, [(i, i - way) for i in senders])]
    all_to_all x1, starting transfers between devices: 3.47 us -> 10 us  [kernel_path(): lax.all_to_all(cuts, 'ka', split_axis=0, concat_axis=0, tiled=True)]
    all_to_all x2, starting transfers between devices: 5.49 us -> 9.44 us  [exchange_all(): return lax.all_to_all(parts, AXES, split_axis=0, concat_axis=0, tiled=True)]
    unnamed x44 -> x42, local copies, waits for them, and re-layouts: 6.35 us -> 7.37 us
  transfers between devices with their start and end apart: 18 -> 18, of which waited for: 6 -> 4; matrix products, arithmetic and copies ran while one was open for 1% -> 2% of each run, Pallas kernels for 24% -> 23%
where the time goes in v10:
time: 166 us
  Pallas kernels  54 us (33%)
  blocking collectives  47.9 us (29%)
  starting transfers between devices  39.1 us (24%)
  waiting for transfers between devices  11.6 us (7%)
  local copies, waits for them, and re-layouts  11 us (7%)
    all_to_all x4, blocking collectives, exchange_all(): return lax.all_to_all(parts, AXES, split_axis=0, concat_axis=0, tiled=True)  47.9 us
    pallas_call x2, Pallas kernels, kernel_path(): call(functools.partial(direct_kernel, n_ka, tile, scale), 'direct', shape...  25.2 us
    ppermute x9, starting transfers between devices, swap(): lax.ppermute(block, axis, [(i, i ^ d) for i in range(lax.axis_size(axis))])  10.9 us
    all_to_all x1, starting transfers between devices, kernel_path(): lax.all_to_all(cuts, 'ka', split_axis=0, concat_axis=0, tiled=True)  10 us
    all_to_all x2, starting transfers between devices, exchange_all(): return lax.all_to_all(parts, AXES, split_axis=0, concat_axis=0, tiled=True)  9.44 us
    ppermute x6, starting transfers between devices, line_gather(): moving = lax.ppermute(moving, axis, [(i, i - way) for i in senders])  8.78 us
    pallas_call x2, Pallas kernels, kernel_path(): call(functools.partial(exchange_kernel, cfg, chunk, scale), 'exchange', m...  8.17 us
    unnamed x42, local copies, waits for them, and re-layouts  7.37 us
  transfers between devices with their start and end apart: 18, of which 4 were waited for; matrix products, arithmetic and copies ran while one was open for 2% of the time, Pallas kernels for 23%

profile of v10, /device:TPU:0, one launch (start us, length us, event | category | flops | bytes accessed | tf_op | source)
XLA Modules:
  0.0 165.6 jit_solution(9437022706069858506)
XLA Ops:
  0.7 1.7 %pack.1 = (f32[16,128]{1,0:T(8,128)}, f32[16,128]{1,0:T(8,128)}, bf16[16,128]{1,0:T(8,128)(2,1)}) custom-call(f32[3,512]{1,0:T(4,128)} %start_in.1, f32[3,64]{1,0:T(4,128)} %cond_in.1, f32[3,8]{1,0:T(4,128)} %val_in.1), custom_call_target="tpu_custom_call" | custom-call | tf_op jit(solution)/shard_map/pack/pallas_call | solution.py:508
  2.3 0.7 pad.4
  3.0 1.1 dynamic-slice_bitcast_fusion.3
  4.1 0.7 fusion
  4.8 3.0 %collective-permute-start = (bf16[24,2176]{1,0:T(8,128)(2,1)S(1)}, bf16[24,2176]{1,0:T(8,128)(2,1)S(1)}, u32[]{:S(2)}, u32[]{:S(2)}) collective-permute-start(bf16[24,2176]{1,0:T(8,128)(2,1)S(1)} %get-tuple-element.71), channel_id=1, source_target_pairs={{0,8},{8,0},{16,24},{24,16},{1,9},{9,1},{17,25},{25,17},{2,10},{10... | collective-permute-start | bytes 313352 | tf_op jit(solution)/shard_map/ppermute | solution.py:448
  7.8 2.6 %collective-permute-start.1 = (bf16[24,2176]{1,0:T(8,128)(2,1)S(1)}, bf16[24,2176]{1,0:T(8,128)(2,1)S(1)}, u32[]{:S(2)}, u32[]{:S(2)}) collective-permute-start(bf16[24,2176]{1,0:T(8,128)(2,1)S(1)} %get-tuple-element.69), channel_id=1, source_target_pairs={{0,16},{8,24},{16,0},{24,8},{1,17},{9,25},{17,1},{25,9},{2,18},{10... | collective-permute-start | bytes 313352 | tf_op jit(solution)/shard_map/ppermute | solution.py:448
  10.4 1.0 constant_dynamic-slice_fusion
  11.4 2.8 %collective-permute-start.5 = (bf16[192,1024]{1,0:T(8,128)(2,1)S(1)}, bf16[192,1024]{1,0:T(8,128)(2,1)S(1)}, u32[]{:S(2)}, u32[]{:S(2)}) collective-permute-start(bf16[192,1024]{1,0:T(8,128)(2,1)S(1)} %bitcast.9), channel_id=1, source_target_pairs={{0,8},{8,16},{16,24},{1,9},{9,17},{17,25},{2,10},{10,18},{18,26},{... | collective-permute-start | bytes 1179656 | tf_op jit(solution)/shard_map/ppermute | solution.py:458
  14.2 1.3 collective-permute-start.6
  15.5 3.7 %turn.1.refs_1_ = bf16[2048,1024]{1,0:T(8,128)(2,1)} custom-call(bf16[1024,2048]{1,0:T(8,128)(2,1)} %scr_ref.1), custom_call_target="tpu_custom_call" | custom-call | bytes 8388608 | tf_op jit(solution)/shard_map/turn/pallas_call | solution.py:547
  19.3 1.6 collective-permute-start.3
  20.9 1.5 collective-permute-start.4
  22.4 0.6 constant_dynamic-update-slice_fusion.4
  23.1 0.6 constant_dynamic-update-slice_fusion.3
  23.7 0.6 constant_dynamic-update-slice_fusion.2
  24.3 2.2 %collective-permute-done.6.refs_8_ = bf16[192,1024]{1,0:T(8,128)(2,1)S(1)} collective-permute-done((bf16[192,1024]{1,0:T(8,128)(2,1)S(1)}, bf16[192,1024]{1,0:T(8,128)(2,1)S(1)}, u32[]{:S(2)}, u32[]{:S(2)}) %collective-permute-start.6) | collective-permute-done | bytes 393248 | tf_op jit(solution)/shard_map/ppermute | solution.py:458
  26.5 3.1 %collective-permute-done.3.refs_1_ = bf16[96,2176]{1,0:T(8,128)(2,1)S(1)} collective-permute-done((bf16[96,2176]{1,0:T(8,128)(2,1)S(1)}, bf16[96,2176]{1,0:T(8,128)(2,1)S(1)}, u32[]{:S(2)}, u32[]{:S(2)}) %collective-permute-start.3) | collective-permute-done | bytes 417824 | tf_op jit(solution)/shard_map/ppermute | solution.py:448
  29.7 1.2 collective-permute-done.4.refs_2_
  30.9 0.9 constant_dynamic-update-slice_fusion.1
  31.7 0.8 constant_dynamic-update-slice_fusion
  32.6 1.6 collective-permute-start.7
  34.8 1.4 collective-permute-start.11
  36.2 1.3 collective-permute-start.12
  37.5 1.8 %cut.1 = bf16[4,192,256]{2,1,0:T(8,128)(2,1)} custom-call(bf16[3,64,8192]{2,1,0:T(8,128)(2,1)} %cond_ref.1), custom_call_target="tpu_custom_call" | custom-call | tf_op jit(solution)/shard_map/cut/pallas_call | solution.py:535
  39.3 10.0 %all-to-all-start = ((bf16[4,192,256]{2,1,0:T(8,128)(2,1)}), bf16[4,192,256]{2,1,0:T(8,128)(2,1)S(1)}, u32[]{:S(2)}, u32[]{:S(2)}) async-start(bf16[4,192,256]{2,1,0:T(8,128)(2,1)} %cut.1), calls=%async_computation | async-start | bytes 786432 | tf_op jit(solution)/shard_map/all_to_all | solution.py:543
  49.4 0.7 collective-permute-start.13
  50.1 5.0 %collective-permute-done.12.refs_9_ = bf16[192,1024]{1,0:T(8,128)(2,1)} collective-permute-done((bf16[192,1024]{1,0:T(8,128)(2,1)S(1)}, bf16[192,1024]{1,0:T(8,128)(2,1)}, u32[]{:S(2)}, u32[]{:S(2)}) %collective-permute-start.12) | collective-permute-done | bytes 393248 | tf_op jit(solution)/shard_map/ppermute | solution.py:458
  55.1 1.3 collective-permute-start.14
  56.5 0.7 copy-done.11
  57.2 1.0 copy-done.8
  58.2 5.7 %order.1 = (bf16[768,2048]{1,0:T(8,128)(2,1)}, bf16[2048,768]{1,0:T(8,128)(2,1)}, bf16[768,256]{1,0:T(8,128)(2,1)}, bf16[32,16,128]{2,1,0:T(8,128)(2,1)}) custom-call(bf16[96,2176]{1,0:T(8,128)(2,1)} %copy-done.7, bf16[96,2176]{1,0:T(8,128)(2,1)} %copy-done.5, bf16[96,2176]{1,0:T(8,128)(2,1)} %copy-done.6, bf16[48,2176]{1,0:T(8,128)(2,1)} %copy-done.9, ...), custom_call_target="tpu_custom_call" | custom-call | bytes 9437184 | tf_op jit(solution)/shard_map/order/pallas_call | solution.py:562
  63.9 0.7 copy-done.4
  64.7 2.2 %density.2 = (bf16[3,256,256]{2,1,0:T(8,128)(2,1)}, f32[32,2,128]{2,1,0:T(2,128)}) custom-call(bf16[32,16,128]{2,1,0:T(8,128)(2,1)} %get-tuple-element.43.refs_0_.msgs_ref, bf16[768,256]{1,0:T(8,128)(2,1)} %get-tuple-element.44.refs_1_.refs_3_, bf16[4,192,256]{2,1,0:T(8,128)(2,1)} %copy-done.4), custom_call_target="tpu_custom_call" | custom-call | tf_op jit(solution)/shard_map/density/pallas_call | solution.py:589
  66.9 6.7 %all-to-all-start.1 = ((f32[32,2,128]{2,1,0:T(2,128)}), f32[32,2,128]{2,1,0:T(2,128)S(1)}, u32[]{:S(2)}, u32[]{:S(2)}) async-start(f32[32,2,128]{2,1,0:T(2,128)} %get-tuple-element.45), calls=%async_computation.1 | async-start | bytes 65536 | tf_op jit(solution)/shard_map/all_to_all | solution.py:30
  73.6 0.7 copy-done.17
  74.4 12.6 %direct.2.refs_1_ = f32[6,128,128]{2,1,0:T(8,128)} custom-call(bf16[2048,768]{1,0:T(8,128)(2,1)} %get-tuple-element.46.refs_0_, bf16[2048,1024]{1,0:T(8,128)(2,1)} %turn.1.refs_1_, bf16[768,2048]{1,0:T(8,128)(2,1)} %get-tuple-element.48.refs_2_, bf16[3,256,256]{2,1,0:T(8,128)(2,1)} %get-tuple-element.49.refs_3_, bf16[192,1024]{1,0:T(8,128)(2,1)} %bitcast.11, ...), custom_call_target="tpu_custom_call" | custom-call | flops 6442450944 | bytes 12582912 | tf_op jit(solution)/shard_map/direct/pallas_call | solution.py:608
  87.6 4.1 %exchange.2 = bf16[32,16,128]{2,1,0:T(8,128)(2,1)} custom-call(f32[32,2,128]{2,1,0:T(2,128)} %copy-done.14, f32[6,128,128]{2,1,0:T(8,128)} %direct.2.refs_1_, bf16[256,8192]{1,0:T(8,128)(2,1)} %refs_2_.3, bf16[768,256]{1,0:T(8,128)(2,1)} %get-tuple-element.44.refs_1_.refs_3_, bf16[4,192,256]{2,1,0:T(8,128)(2,1)} %copy-done.4), custom_call_target="tpu_custom_call" | custom-call | tf_op jit(solution)/shard_map/exchange/pallas_call | solution.py:631
  91.8 14.1 %all_to_all.35.recv_ref = bf16[32,16,128]{2,1,0:T(8,128)(2,1)S(1)} all-to-all(bf16[32,16,128]{2,1,0:T(8,128)(2,1)} %exchange.2), channel_id=1, replica_groups=mesh['ka'=4,'band'=8] {'ka','band'}, dimensions={0} | all-to-all | bytes 262144 | tf_op jit(solution)/shard_map/all_to_all | solution.py:30
  105.9 0.8 first_owner.1
  106.7 10.6 %all_to_all.36.refs_0_.msgs_ref = bf16[32,16,128]{2,1,0:T(8,128)(2,1)} all-to-all(bf16[32,16,128]{2,1,0:T(8,128)(2,1)S(1)} %get-tuple-element.56), channel_id=1, replica_groups=mesh['ka'=4,'band'=8] {'ka','band'}, dimensions={0} | all-to-all | bytes 262144 | tf_op jit(solution)/shard_map/all_to_all | solution.py:30
  117.4 2.2 %density.3 = (bf16[3,256,256]{2,1,0:T(8,128)(2,1)}, f32[32,2,128]{2,1,0:T(2,128)}) custom-call(bf16[32,16,128]{2,1,0:T(8,128)(2,1)} %all_to_all.36.refs_0_.msgs_ref, bf16[768,256]{1,0:T(8,128)(2,1)} %get-tuple-element.44.refs_1_.refs_3_, bf16[4,192,256]{2,1,0:T(8,128)(2,1)} %copy-done.4), custom_call_target="tpu_custom_call" | custom-call | tf_op jit(solution)/shard_map/density/pallas_call | solution.py:589
  119.5 2.8 %all-to-all-start.4 = ((f32[32,2,128]{2,1,0:T(2,128)}), f32[32,2,128]{2,1,0:T(2,128)S(1)}, u32[]{:S(2)}, u32[]{:S(2)}) async-start(f32[32,2,128]{2,1,0:T(2,128)} %get-tuple-element.57), calls=%async_computation.4 | async-start | bytes 65536 | tf_op jit(solution)/shard_map/all_to_all | solution.py:30
  122.3 12.6 %direct.3.refs_1_ = f32[6,128,128]{2,1,0:T(8,128)} custom-call(bf16[2048,768]{1,0:T(8,128)(2,1)} %get-tuple-element.46.refs_0_, bf16[2048,1024]{1,0:T(8,128)(2,1)} %turn.1.refs_1_, bf16[768,2048]{1,0:T(8,128)(2,1)} %get-tuple-element.48.refs_2_, bf16[3,256,256]{2,1,0:T(8,128)(2,1)} %get-tuple-element.58.refs_3_, bf16[192,1024]{1,0:T(8,128)(2,1)} %bitcast.12, ...), custom_call_target="tpu_custom_call" | custom-call | flops 6442450944 | bytes 12582912 | tf_op jit(solution)/shard_map/direct/pallas_call | solution.py:608
  135.5 4.1 %exchange.3 = bf16[32,16,128]{2,1,0:T(8,128)(2,1)} custom-call(f32[32,2,128]{2,1,0:T(2,128)} %copy-done.13, f32[6,128,128]{2,1,0:T(8,128)} %direct.3.refs_1_, bf16[256,8192]{1,0:T(8,128)(2,1)} %refs_2_.3, bf16[768,256]{1,0:T(8,128)(2,1)} %get-tuple-element.44.refs_1_.refs_3_, bf16[4,192,256]{2,1,0:T(8,128)(2,1)} %copy-done.4), custom_call_target="tpu_custom_call" | custom-call | tf_op jit(solution)/shard_map/exchange/pallas_call | solution.py:631
  139.6 14.1 %all_to_all.37.recv_ref = bf16[32,16,128]{2,1,0:T(8,128)(2,1)S(1)} all-to-all(bf16[32,16,128]{2,1,0:T(8,128)(2,1)} %exchange.3), channel_id=1, replica_groups=mesh['ka'=4,'band'=8] {'ka','band'}, dimensions={0} | all-to-all | bytes 262144 | tf_op jit(solution)/shard_map/all_to_all | solution.py:30
  153.7 1.3 second_owner.1
  155.0 9.0 %all_to_all.38.msgs_ref = f32[32,2,128]{2,1,0:T(2,128)S(1)} all-to-all(f32[32,2,128]{2,1,0:T(2,128)S(1)} %get-tuple-element.61), channel_id=1, replica_groups=mesh['ka'=4,'band'=8] {'ka','band'}, dimensions={0} | all-to-all | bytes 65536 | tf_op jit(solution)/shard_map/all_to_all | solution.py:30
  164.1 1.3 finish.1
  (56 shorter events, 2.1 us)
Async XLA Ops:
  4.8 14.5 %collective-permute-start = (bf16[24,2176]{1,0:T(8,128)(2,1)S(1)}, bf16[24,2176]{1,0:T(8,128)(2,1)S(1)}, u32[]{:S(2)}, u32[]{:S(2)}) collective-permute-start(bf16[24,2176]{1,0:T(8,128)(2,1)S(1)} %get-tuple-element.71), channel_id=1, source_target_pairs={{0,8},{8,0},{16,24},{24,16},{1,9},{9,1},{17,25},{25,17},{2,10},{10... | collective-permute-start | bytes 313352 | tf_op jit(solution)/shard_map/ppermute | solution.py:448
  7.8 11.5 %collective-permute-start.1 = (bf16[24,2176]{1,0:T(8,128)(2,1)S(1)}, bf16[24,2176]{1,0:T(8,128)(2,1)S(1)}, u32[]{:S(2)}, u32[]{:S(2)}) collective-permute-start(bf16[24,2176]{1,0:T(8,128)(2,1)S(1)} %get-tuple-element.69), channel_id=1, source_target_pairs={{0,16},{8,24},{16,0},{24,8},{1,17},{9,25},{17,1},{25,9},{2,18},{10... | collective-permute-start | bytes 313352 | tf_op jit(solution)/shard_map/ppermute | solution.py:448
  10.4 8.9 %collective-permute-start.2 = (bf16[24,2176]{1,0:T(8,128)(2,1)S(1)}, bf16[24,2176]{1,0:T(8,128)(2,1)S(1)}, u32[]{:S(2)}, u32[]{:S(2)}) collective-permute-start(bf16[24,2176]{1,0:T(8,128)(2,1)S(1)} %get-tuple-element.70), channel_id=1, source_target_pairs={{0,24},{8,16},{16,8},{24,0},{1,25},{9,17},{17,9},{25,1},{2,26},{10... | collective-permute-start | bytes 313352 | tf_op jit(solution)/shard_map/ppermute | solution.py:448
  11.4 7.8 %copy-start.12 = (bf16[3,64,1024]{2,1,0:T(8,128)(2,1)}, bf16[3,64,1024]{2,1,0:T(8,128)(2,1)S(1)}, u32[]{:S(2)}) copy-start(bf16[3,64,1024]{2,1,0:T(8,128)(2,1)S(1)} %constant_dynamic-slice_fusion) | copy-start | bytes 1179652
  11.4 12.9 %collective-permute-start.5 = (bf16[192,1024]{1,0:T(8,128)(2,1)S(1)}, bf16[192,1024]{1,0:T(8,128)(2,1)S(1)}, u32[]{:S(2)}, u32[]{:S(2)}) collective-permute-start(bf16[192,1024]{1,0:T(8,128)(2,1)S(1)} %bitcast.9), channel_id=1, source_target_pairs={{0,8},{8,16},{16,24},{1,9},{9,17},{17,25},{2,10},{10,18},{18,26},{... | collective-permute-start | bytes 1179656 | tf_op jit(solution)/shard_map/ppermute | solution.py:458
  14.2 12.3 %collective-permute-start.6 = (bf16[192,1024]{1,0:T(8,128)(2,1)S(1)}, bf16[192,1024]{1,0:T(8,128)(2,1)S(1)}, u32[]{:S(2)}, u32[]{:S(2)}) collective-permute-start(bf16[192,1024]{1,0:T(8,128)(2,1)S(1)} %bitcast.10), channel_id=1, source_target_pairs={{8,0},{16,8},{24,16},{9,1},{17,9},{25,17},{10,2},{18,10},{26,18},{... | collective-permute-start | bytes 1179656 | tf_op jit(solution)/shard_map/ppermute | solution.py:458
  19.3 13.3 %copy-start.7 = (bf16[96,2176]{1,0:T(8,128)(2,1)}, bf16[96,2176]{1,0:T(8,128)(2,1)S(1)}, u32[]{:S(2)}) copy-start(bf16[96,2176]{1,0:T(8,128)(2,1)S(1)} %pad_maximum_fusion.refs_0_) | copy-start | bytes 1253380
  19.3 10.3 %collective-permute-start.3 = (bf16[96,2176]{1,0:T(8,128)(2,1)S(1)}, bf16[96,2176]{1,0:T(8,128)(2,1)S(1)}, u32[]{:S(2)}, u32[]{:S(2)}) collective-permute-start(bf16[96,2176]{1,0:T(8,128)(2,1)S(1)} %pad_maximum_fusion.refs_0_), channel_id=1, source_target_pairs={{0,2},{1,3},{2,0},{3,1},{4,6},{5,7},{6,4},{7,5},{8,10},{9,11},{10,... | collective-permute-start | bytes 1253384 | tf_op jit(solution)/shard_map/ppermute | solution.py:448
  20.9 10.0 %collective-permute-start.4 = (bf16[96,2176]{1,0:T(8,128)(2,1)S(1)}, bf16[96,2176]{1,0:T(8,128)(2,1)S(1)}, u32[]{:S(2)}, u32[]{:S(2)}) collective-permute-start(bf16[96,2176]{1,0:T(8,128)(2,1)S(1)} %pad_maximum_fusion.refs_0_), channel_id=1, source_target_pairs={{0,4},{1,5},{2,6},{3,7},{4,0},{5,1},{6,2},{7,3},{8,12},{9,13},{10,... | collective-permute-start | bytes 1253384 | tf_op jit(solution)/shard_map/ppermute | solution.py:448
  24.3 10.4 %copy-start.15 = (bf16[192,1024]{1,0:T(8,128)(2,1)}, bf16[192,1024]{1,0:T(8,128)(2,1)S(1)}, u32[]{:S(2)}) copy-start(bf16[192,1024]{1,0:T(8,128)(2,1)S(1)} %collective-permute-done.5.refs_5_) | copy-start | bytes 1179652
  26.5 9.6 %copy-start.16 = (bf16[192,1024]{1,0:T(8,128)(2,1)}, bf16[192,1024]{1,0:T(8,128)(2,1)S(1)}, u32[]{:S(2)}) copy-start(bf16[192,1024]{1,0:T(8,128)(2,1)S(1)} %collective-permute-done.6.refs_8_) | copy-start | bytes 1179652
  29.7 3.0 %copy-start.5 = (bf16[96,2176]{1,0:T(8,128)(2,1)}, bf16[96,2176]{1,0:T(8,128)(2,1)S(1)}, u32[]{:S(2)}) copy-start(bf16[96,2176]{1,0:T(8,128)(2,1)S(1)} %collective-permute-done.3.refs_1_) | copy-start | bytes 1253380
  30.9 1.8 %copy-start.6 = (bf16[96,2176]{1,0:T(8,128)(2,1)}, bf16[96,2176]{1,0:T(8,128)(2,1)S(1)}, u32[]{:S(2)}) copy-start(bf16[96,2176]{1,0:T(8,128)(2,1)S(1)} %collective-permute-done.4.refs_2_) | copy-start | bytes 1253380
  32.5 23.9 %collective-permute-start.9 = (bf16[288,2176]{1,0:T(8,128)(2,1)}, bf16[288,2176]{1,0:T(8,128)(2,1)S(1)}, u32[]{:S(2)}, u32[]{:S(2)}) collective-permute-start(bf16[288,2176]{1,0:T(8,128)(2,1)} %constant_dynamic-update-slice_fusion), channel_id=1, source_target_pairs={{0,1},{1,0},{2,3},{3,2},{4,5},{5,4},{6,7},{7,6},{8,9},{9,8},{10,11... | collective-permute-start | bytes 3760136 | tf_op jit(solution)/shard_map/ppermute | solution.py:448
  32.6 16.7 %collective-permute-start.7 = (bf16[48,2176]{1,0:T(8,128)(2,1)S(1)}, bf16[48,2176]{1,0:T(8,128)(2,1)S(1)}, u32[]{:S(2)}, u32[]{:S(2)}) collective-permute-start(bf16[48,2176]{1,0:T(8,128)(2,1)S(1)} %slice.6), channel_id=1, source_target_pairs={{0,4},{1,5},{2,6},{3,7},{4,0},{5,1},{6,2},{7,3},{8,12},{9,13},{10,... | collective-permute-start | bytes 626696 | tf_op jit(solution)/shard_map/ppermute | solution.py:448
  34.2 15.1 %collective-permute-start.8 = (bf16[48,2176]{1,0:T(8,128)(2,1)S(1)}, bf16[48,2176]{1,0:T(8,128)(2,1)S(1)}, u32[]{:S(2)}, u32[]{:S(2)}) collective-permute-start(bf16[48,2176]{1,0:T(8,128)(2,1)S(1)} %slice.7), channel_id=1, source_target_pairs={{0,2},{1,3},{2,0},{3,1},{4,6},{5,7},{6,4},{7,5},{8,10},{9,11},{10,... | collective-permute-start | bytes 626696 | tf_op jit(solution)/shard_map/ppermute | solution.py:448
  34.8 14.7 %collective-permute-start.11 = (bf16[192,1024]{1,0:T(8,128)(2,1)S(1)}, bf16[192,1024]{1,0:T(8,128)(2,1)}, u32[]{:S(2)}, u32[]{:S(2)}) collective-permute-start(bf16[192,1024]{1,0:T(8,128)(2,1)S(1)} %collective-permute-done.5.refs_5_), channel_id=1, source_target_pairs={{8,16},{16,24},{9,17},{17,25},{10,18},{18,26},{11,19},{19,27},{12,... | collective-permute-start | bytes 1179656 | tf_op jit(solution)/shard_map/ppermute | solution.py:458
  36.2 19.0 %collective-permute-start.12 = (bf16[192,1024]{1,0:T(8,128)(2,1)S(1)}, bf16[192,1024]{1,0:T(8,128)(2,1)}, u32[]{:S(2)}, u32[]{:S(2)}) collective-permute-start(bf16[192,1024]{1,0:T(8,128)(2,1)S(1)} %collective-permute-done.6.refs_8_), channel_id=1, source_target_pairs={{8,0},{16,8},{9,1},{17,9},{10,2},{18,10},{11,3},{19,11},{12,4},{20... | collective-permute-start | bytes 1179656 | tf_op jit(solution)/shard_map/ppermute | solution.py:458
  39.3 24.6 %all-to-all-start = ((bf16[4,192,256]{2,1,0:T(8,128)(2,1)}), bf16[4,192,256]{2,1,0:T(8,128)(2,1)S(1)}, u32[]{:S(2)}, u32[]{:S(2)}) async-start(bf16[4,192,256]{2,1,0:T(8,128)(2,1)} %cut.1), calls=%async_computation | async-start | bytes 786432 | tf_op jit(solution)/shard_map/all_to_all | solution.py:543
  49.3 7.2 %copy-start.9 = (bf16[48,2176]{1,0:T(8,128)(2,1)}, bf16[48,2176]{1,0:T(8,128)(2,1)S(1)}, u32[]{:S(2)}) copy-start(bf16[48,2176]{1,0:T(8,128)(2,1)S(1)} %collective-permute-done.7.refs_3_) | copy-start | bytes 626692
  49.3 7.2 %copy-start.10 = (bf16[48,2176]{1,0:T(8,128)(2,1)}, bf16[48,2176]{1,0:T(8,128)(2,1)S(1)}, u32[]{:S(2)}) copy-start(bf16[48,2176]{1,0:T(8,128)(2,1)S(1)} %collective-permute-done.8.refs_4_) | copy-start | bytes 626692
  49.3 7.1 %collective-permute-start.10 = (bf16[96,2176]{1,0:T(8,128)(2,1)S(1)}, bf16[96,2176]{1,0:T(8,128)(2,1)S(1)}, u32[]{:S(2)}, u32[]{:S(2)}) collective-permute-start(bf16[96,2176]{1,0:T(8,128)(2,1)S(1)} %pad_maximum_fusion.1), channel_id=1, source_target_pairs={{0,1},{1,0},{2,3},{3,2},{4,5},{5,4},{6,7},{7,6},{8,9},{9,8},{10,11... | collective-permute-start | bytes 1253384 | tf_op jit(solution)/shard_map/ppermute | solution.py:448
  49.4 24.1 %collective-permute-start.13 = (bf16[192,1024]{1,0:T(8,128)(2,1)}, bf16[192,1024]{1,0:T(8,128)(2,1)S(1)}, u32[]{:S(2)}, u32[]{:S(2)}) collective-permute-start(bf16[192,1024]{1,0:T(8,128)(2,1)} %collective-permute-done.11.refs_6_), channel_id=1, source_target_pairs={{16,24},{17,25},{18,26},{19,27},{20,28},{21,29},{22,30},{23,31}} | collective-permute-start | bytes 1179656 | tf_op jit(solution)/shard_map/ppermute | solution.py:458
  55.1 18.4 %collective-permute-start.14 = (bf16[192,1024]{1,0:T(8,128)(2,1)}, bf16[192,1024]{1,0:T(8,128)(2,1)S(1)}, u32[]{:S(2)}, u32[]{:S(2)}) collective-permute-start(bf16[192,1024]{1,0:T(8,128)(2,1)} %collective-permute-done.12.refs_9_), channel_id=1, source_target_pairs={{8,0},{9,1},{10,2},{11,3},{12,4},{13,5},{14,6},{15,7}} | collective-permute-start | bytes 1179656 | tf_op jit(solution)/shard_map/ppermute | solution.py:458
  56.4 0.8 copy-start.11
  57.2 1.0 copy-start.8
  63.9 0.7 copy-start.4
  66.9 20.2 %all-to-all-start.1 = ((f32[32,2,128]{2,1,0:T(2,128)}), f32[32,2,128]{2,1,0:T(2,128)S(1)}, u32[]{:S(2)}, u32[]{:S(2)}) async-start(f32[32,2,128]{2,1,0:T(2,128)} %get-tuple-element.45), calls=%async_computation.1 | async-start | bytes 65536 | tf_op jit(solution)/shard_map/all_to_all | solution.py:30
  73.5 0.7 copy-start.17
  73.5 0.9 copy-start.18
  87.0 18.9 %copy-start.1 = (bf16[32,16,128]{2,1,0:T(8,128)(2,1)S(1)}, bf16[32,16,128]{2,1,0:T(8,128)(2,1)}, u32[]{:S(2)}) copy-start(bf16[32,16,128]{2,1,0:T(8,128)(2,1)} %get-tuple-element.43.refs_0_.msgs_ref) | copy-start | bytes 393220
  87.0 18.9 %copy-start.2 = (f32[16,128]{1,0:T(8,128)S(1)}, f32[16,128]{1,0:T(8,128)}, u32[]{:S(2)}) copy-start(f32[16,128]{1,0:T(8,128)} %get-tuple-element.54.gap_ref) | copy-start | bytes 24580
  87.0 18.9 %copy-start.3 = (f32[16,128]{1,0:T(8,128)S(1)}, f32[16,128]{1,0:T(8,128)}, u32[]{:S(2)}) copy-start(f32[16,128]{1,0:T(8,128)} %get-tuple-element.55.own_ref) | copy-start | bytes 24580
  87.0 0.6 copy-start.14
  119.5 15.4 %all-to-all-start.4 = ((f32[32,2,128]{2,1,0:T(2,128)}), f32[32,2,128]{2,1,0:T(2,128)S(1)}, u32[]{:S(2)}, u32[]{:S(2)}) async-start(f32[32,2,128]{2,1,0:T(2,128)} %get-tuple-element.57), calls=%async_computation.4 | async-start | bytes 65536 | tf_op jit(solution)/shard_map/all_to_all | solution.py:30
  134.9 18.8 %copy-start = (bf16[32,16,128]{2,1,0:T(8,128)(2,1)S(1)}, bf16[32,16,128]{2,1,0:T(8,128)(2,1)}, u32[]{:S(2)}) copy-start(bf16[32,16,128]{2,1,0:T(8,128)(2,1)} %all_to_all.36.refs_0_.msgs_ref) | copy-start | bytes 393220
  134.9 0.6 copy-start.13

commit v11 on v10

--- a/solution.py
+++ b/solution.py
@@ -467,22 +467,14 @@
 
     rows = own_piece.shape[0]
     half = rows // 2
-    by_x, by_y = move(own_piece, 2), move(own_piece, 4)
-    by_x, by_y, others = lax.optimization_barrier((by_x, by_y, others))
+    by_x, by_y, core = move(own_piece, 2), move(own_piece, 4), move(own_piece, 1)
+    by_x, by_y, core, others = lax.optimization_barrier((by_x, by_y, core, others))
     diag = [move(by_x[:half], 4), move(by_y[half:], 2)]
-    near = move(jnp.concatenate([own_piece, by_x, by_y], axis=0), 1)
+    near_x, near_y = move(by_x, 1), move(by_y, 1)
     far = move(jnp.concatenate(diag, axis=0), 1)
-    arrays = [own_piece, by_x, by_y, diag[0], diag[1], near, far]
-    parts = (
-        ((0, 0, rows),),
-        ((5, 0, rows),),
-        ((1, 0, rows),),
-        ((5, rows, rows),),
-        ((2, 0, rows),),
-        ((5, 2 * rows, rows),),
-        ((3, 0, half), (4, 0, half)),
-        ((6, 0, rows),),
-    )
+    arrays = [own_piece, core, by_x, near_x, by_y, near_y, diag[0], diag[1], far]
+    parts = tuple(((i, 0, rows),) for i in range(6))
+    parts += (((6, 0, half), (7, 0, half)), ((8, 0, rows),))
     return arrays, parts, others
 
 
@@ -554,11 +546,9 @@
         + [dma(2 * nu_blk // tile)] * 2,
         moved=8 * MIB,
     )(screened)
-    pieces, parts, (scr_turned, below[0], above[0]) = plane_pieces(
-        val_cut, (scr_turned, below[0], above[0])
+    pieces, parts, (scr_turned, cond_own, below[0], above[0]) = plane_pieces(
+        val_cut, (scr_turned, cond_own, below[0], above[0])
     )
-    pieces, below[1:-1], above[1:-1] = lax.optimization_barrier((pieces, below[1:-1], above[1:-1]))
-    cond_pts = [cond_local] + below + above
     val_rows, val_turned, val_own, msgs = call(
         functools.partial(order_kernel, parts, n_ka),
         "order",
@@ -581,6 +571,8 @@
         moved=9 * MIB,
     )(*pieces)
 
+    msgs, below[1:-1], above[1:-1] = lax.optimization_barrier((msgs, below[1:-1], above[1:-1]))
+    cond_pts = [cond_local] + below + above
     cfg = (n_ka, n_band, k_dev)
     quads = k_points // 4
     state, coef = None, None

time: 166 us -> 168 us (1.012)
  waiting for transfers between devices: 11.6 us -> 22.9 us
  local copies, waits for them, and re-layouts: 11 us -> 5.71 us
  starting transfers between devices: 39.1 us -> 35.4 us
    ppermute x6, waiting for transfers between devices: 7.21 us -> 17.6 us  [line_gather(): moving = lax.ppermute(moving, axis, [(i, i - way) for i in senders])]
    all_to_all x1, starting transfers between devices: 10 us -> 5.1 us  [kernel_path(): lax.all_to_all(cuts, 'ka', split_axis=0, concat_axis=0, tiled=True)]
    unnamed x42, local copies, waits for them, and re-layouts: 7.37 us -> 2.92 us
    ppermute x6, starting transfers between devices: 8.78 us -> 11.4 us  [line_gather(): moving = lax.ppermute(moving, axis, [(i, i - way) for i in senders])]
    ppermute x9 -> x11, waiting for transfers between devices: 4.35 us -> 5.28 us  [swap(): lax.ppermute(block, axis, [(i, i ^ d) for i in range(lax.axis_size(axis))])]
    ppermute x9 -> x11, starting transfers between devices: 10.9 us -> 10.3 us  [swap(): lax.ppermute(block, axis, [(i, i ^ d) for i in range(lax.axis_size(axis))])]
  transfers between devices with their start and end apart: 18 -> 20, of which waited for: 4 -> 6; matrix products, arithmetic and copies ran while one was open for 2% -> 1% of each run, Pallas kernels for 23% -> 23%
where the time goes in v11:
time: 168 us; the launch traced here: 167 us
  Pallas kernels  54.1 us (32%)
  blocking collectives  47.9 us (29%)
  starting transfers between devices  35.4 us (21%)
  waiting for transfers between devices  22.9 us (14%)
  local copies, waits for them, and re-layouts  5.71 us (3%)
    all_to_all x4, blocking collectives, exchange_all(): return lax.all_to_all(parts, AXES, split_axis=0, concat_axis=0, tiled=True)  47.9 us
    pallas_call x2, Pallas kernels, kernel_path(): call(functools.partial(direct_kernel, n_ka, tile, scale), 'direct', shape...  25.1 us
    ppermute x6, waiting for transfers between devices, line_gather(): moving = lax.ppermute(moving, axis, [(i, i - way) for i in senders])  17.6 us
    ppermute x6, starting transfers between devices, line_gather(): moving = lax.ppermute(moving, axis, [(i, i - way) for i in senders])  11.4 us
    ppermute x11, starting transfers between devices, swap(): lax.ppermute(block, axis, [(i, i ^ d) for i in range(lax.axis_size(axis))])  10.3 us
    all_to_all x2, starting transfers between devices, exchange_all(): return lax.all_to_all(parts, AXES, split_axis=0, concat_axis=0, tiled=True)  8.62 us
    pallas_call x2, Pallas kernels, kernel_path(): call(functools.partial(exchange_kernel, cfg, chunk, scale), 'exchange', m...  8.16 us
    pallas_call x1, Pallas kernels, kernel_path(): call(functools.partial(order_kernel, parts, n_ka), 'order', (shape_of((ro...  5.77 us
  transfers between devices with their start and end apart: 20, of which 6 were waited for; matrix products, arithmetic and copies ran while one was open for 1% of the time, Pallas kernels for 23%

profile of v11, /device:TPU:0, one launch (start us, length us, event | category | flops | bytes accessed | tf_op | source)
XLA Modules:
  0.0 167.4 jit_solution(10371945932711171180)
XLA Ops:
  0.7 1.7 pack.1
  2.3 0.7 pad.4
  3.0 1.1 dynamic-slice_bitcast_fusion.3
  4.1 3.1 %collective-permute-start = (bf16[24,2176]{1,0:T(8,128)(2,1)S(1)}, bf16[24,2176]{1,0:T(8,128)(2,1)S(1)}, u32[]{:S(2)}, u32[]{:S(2)}) collective-permute-start(bf16[24,2176]{1,0:T(8,128)(2,1)S(1)} %get-tuple-element.60), channel_id=1, source_target_pairs={{0,8},{8,0},{16,24},{24,16},{1,9},{9,1},{17,25},{25,17},{2,10},{10... | collective-permute-start | bytes 313352 | tf_op jit(solution)/shard_map/ppermute | solution.py:448
  7.2 2.6 %collective-permute-start.1 = (bf16[24,2176]{1,0:T(8,128)(2,1)S(1)}, bf16[24,2176]{1,0:T(8,128)(2,1)S(1)}, u32[]{:S(2)}, u32[]{:S(2)}) collective-permute-start(bf16[24,2176]{1,0:T(8,128)(2,1)S(1)} %get-tuple-element.61), channel_id=1, source_target_pairs={{0,16},{8,24},{16,0},{24,8},{1,17},{9,25},{17,1},{25,9},{2,18},{10... | collective-permute-start | bytes 313352 | tf_op jit(solution)/shard_map/ppermute | solution.py:448
  9.8 1.8 %cut.1 = bf16[4,192,256]{2,1,0:T(8,128)(2,1)} custom-call(bf16[3,64,8192]{2,1,0:T(8,128)(2,1)} %cond_ref.1), custom_call_target="tpu_custom_call" | custom-call | tf_op jit(solution)/shard_map/cut/pallas_call | solution.py:527
  11.6 5.1 %all-to-all-start = ((bf16[4,192,256]{2,1,0:T(8,128)(2,1)}), bf16[4,192,256]{2,1,0:T(8,128)(2,1)S(1)}, u32[]{:S(2)}, u32[]{:S(2)}) async-start(bf16[4,192,256]{2,1,0:T(8,128)(2,1)} %cut.1), calls=%async_computation | async-start | bytes 786432 | tf_op jit(solution)/shard_map/all_to_all | solution.py:535
  16.7 1.3 collective-permute-done.1
  18.1 1.6 collective-permute-start.3
  19.7 1.5 collective-permute-start.4
  21.2 1.0 constant_dynamic-slice_fusion
  22.2 5.4 %collective-permute-start.6 = (bf16[192,1024]{1,0:T(8,128)(2,1)S(1)}, bf16[192,1024]{1,0:T(8,128)(2,1)S(1)}, u32[]{:S(2)}, u32[]{:S(2)}) collective-permute-start(bf16[192,1024]{1,0:T(8,128)(2,1)S(1)} %bitcast.9), channel_id=1, source_target_pairs={{0,8},{8,16},{16,24},{1,9},{9,17},{17,25},{2,10},{10,18},{18,26},{... | collective-permute-start | bytes 1179656 | tf_op jit(solution)/shard_map/ppermute | solution.py:458
  27.7 1.3 collective-permute-start.7
  29.0 3.7 %turn.1.refs_1_ = bf16[2048,1024]{1,0:T(8,128)(2,1)} custom-call(bf16[1024,2048]{1,0:T(8,128)(2,1)} %scr_ref.1), custom_call_target="tpu_custom_call" | custom-call | bytes 8388608 | tf_op jit(solution)/shard_map/turn/pallas_call | solution.py:539
  32.7 4.0 %collective-permute-done.6.refs_5_ = bf16[192,1024]{1,0:T(8,128)(2,1)S(1)} collective-permute-done((bf16[192,1024]{1,0:T(8,128)(2,1)S(1)}, bf16[192,1024]{1,0:T(8,128)(2,1)S(1)}, u32[]{:S(2)}, u32[]{:S(2)}) %collective-permute-start.6) | collective-permute-done | bytes 393248 | tf_op jit(solution)/shard_map/ppermute | solution.py:458
  36.7 7.3 %collective-permute-done.7.refs_8_ = bf16[192,1024]{1,0:T(8,128)(2,1)S(1)} collective-permute-done((bf16[192,1024]{1,0:T(8,128)(2,1)S(1)}, bf16[192,1024]{1,0:T(8,128)(2,1)S(1)}, u32[]{:S(2)}, u32[]{:S(2)}) %collective-permute-start.7) | collective-permute-done | bytes 393248 | tf_op jit(solution)/shard_map/ppermute | solution.py:458
  44.1 0.6 collective-permute-start.10
  44.7 0.6 collective-permute-start.11
  45.3 0.7 collective-permute-start.13
  46.0 1.3 collective-permute-start.14
  47.3 0.1 collective-permute-start.8
  47.4 3.6 %collective-permute-done.10.refs_6_ = bf16[48,2176]{1,0:T(8,128)(2,1)S(1)} collective-permute-done((bf16[48,2176]{1,0:T(8,128)(2,1)S(1)}, bf16[48,2176]{1,0:T(8,128)(2,1)S(1)}, u32[]{:S(2)}, u32[]{:S(2)}) %collective-permute-start.10) | collective-permute-done | bytes 208928 | tf_op jit(solution)/shard_map/ppermute | solution.py:448
  51.0 0.3 collective-permute-done.11.refs_7_
  51.3 0.3 collective-permute-start.12
  51.6 1.4 collective-permute-start.15
  53.0 6.3 %collective-permute-done.14.refs_9_ = bf16[192,1024]{1,0:T(8,128)(2,1)S(1)} collective-permute-done((bf16[192,1024]{1,0:T(8,128)(2,1)S(1)}, bf16[192,1024]{1,0:T(8,128)(2,1)S(1)}, u32[]{:S(2)}, u32[]{:S(2)}) %collective-permute-start.14) | collective-permute-done | bytes 393248 | tf_op jit(solution)/shard_map/ppermute | solution.py:458
  59.3 1.3 collective-permute-start.16
  60.7 0.7 copy-done.11
  61.4 0.2 copy-done.12
  61.6 0.8 copy-done.13
  62.4 5.8 %order.1 = (bf16[768,2048]{1,0:T(8,128)(2,1)}, bf16[2048,768]{1,0:T(8,128)(2,1)}, bf16[768,256]{1,0:T(8,128)(2,1)}, bf16[32,16,128]{2,1,0:T(8,128)(2,1)}) custom-call(bf16[96,2176]{1,0:T(8,128)(2,1)} %copy-done.5, bf16[96,2176]{1,0:T(8,128)(2,1)} %copy-done.10, bf16[96,2176]{1,0:T(8,128)(2,1)} %copy-done.6, bf16[96,2176]{1,0:T(8,128)(2,1)} %copy-done.11, ...), custom_call_target="tpu_custom_call" | custom-call | bytes 9437184 | tf_op jit(solution)/shard_map/order/pallas_call | solution.py:552
  68.2 2.2 %density.2 = (bf16[3,256,256]{2,1,0:T(8,128)(2,1)}, f32[32,2,128]{2,1,0:T(2,128)}) custom-call(bf16[32,16,128]{2,1,0:T(8,128)(2,1)} %get-tuple-element.34.refs_0_.msgs_ref, bf16[768,256]{1,0:T(8,128)(2,1)} %get-tuple-element.35.refs_1_.refs_3_, bf16[4,192,256]{2,1,0:T(8,128)(2,1)} %copy-done.4), custom_call_target="tpu_custom_call" | custom-call | tf_op jit(solution)/shard_map/density/pallas_call | solution.py:581
  70.3 5.8 %all-to-all-start.1 = ((f32[32,2,128]{2,1,0:T(2,128)}), f32[32,2,128]{2,1,0:T(2,128)S(1)}, u32[]{:S(2)}, u32[]{:S(2)}) async-start(f32[32,2,128]{2,1,0:T(2,128)} %get-tuple-element.37), calls=%async_computation.1 | async-start | bytes 65536 | tf_op jit(solution)/shard_map/all_to_all | solution.py:30
  76.2 12.6 %direct.2.refs_1_ = f32[6,128,128]{2,1,0:T(8,128)} custom-call(bf16[2048,768]{1,0:T(8,128)(2,1)} %get-tuple-element.38.refs_0_, bf16[2048,1024]{1,0:T(8,128)(2,1)} %turn.1.refs_1_, bf16[768,2048]{1,0:T(8,128)(2,1)} %get-tuple-element.40.refs_2_, bf16[3,256,256]{2,1,0:T(8,128)(2,1)} %get-tuple-element.41.refs_3_, bf16[192,1024]{1,0:T(8,128)(2,1)} %bitcast.11, ...), custom_call_target="tpu_custom_call" | custom-call | flops 6442450944 | bytes 12582912 | tf_op jit(solution)/shard_map/direct/pallas_call | solution.py:600
  88.8 0.6 copy-done.16
  89.4 4.1 %exchange.2 = bf16[32,16,128]{2,1,0:T(8,128)(2,1)} custom-call(f32[32,2,128]{2,1,0:T(2,128)} %copy-done.16, f32[6,128,128]{2,1,0:T(8,128)} %direct.2.refs_1_, bf16[256,8192]{1,0:T(8,128)(2,1)} %refs_2_.3, bf16[768,256]{1,0:T(8,128)(2,1)} %get-tuple-element.35.refs_1_.refs_3_, bf16[4,192,256]{2,1,0:T(8,128)(2,1)} %copy-done.4), custom_call_target="tpu_custom_call" | custom-call | tf_op jit(solution)/shard_map/exchange/pallas_call | solution.py:623
  93.6 14.1 %all_to_all.35.recv_ref = bf16[32,16,128]{2,1,0:T(8,128)(2,1)S(1)} all-to-all(bf16[32,16,128]{2,1,0:T(8,128)(2,1)} %exchange.2), channel_id=1, replica_groups=mesh['ka'=4,'band'=8] {'ka','band'}, dimensions={0} | all-to-all | bytes 262144 | tf_op jit(solution)/shard_map/all_to_all | solution.py:30
  107.7 0.8 first_owner.1
  108.5 10.6 %all_to_all.36.refs_0_.msgs_ref = bf16[32,16,128]{2,1,0:T(8,128)(2,1)} all-to-all(bf16[32,16,128]{2,1,0:T(8,128)(2,1)S(1)} %get-tuple-element.48), channel_id=1, replica_groups=mesh['ka'=4,'band'=8] {'ka','band'}, dimensions={0} | all-to-all | bytes 262144 | tf_op jit(solution)/shard_map/all_to_all | solution.py:30
  119.2 2.2 %density.3 = (bf16[3,256,256]{2,1,0:T(8,128)(2,1)}, f32[32,2,128]{2,1,0:T(2,128)}) custom-call(bf16[32,16,128]{2,1,0:T(8,128)(2,1)} %all_to_all.36.refs_0_.msgs_ref, bf16[768,256]{1,0:T(8,128)(2,1)} %get-tuple-element.35.refs_1_.refs_3_, bf16[4,192,256]{2,1,0:T(8,128)(2,1)} %copy-done.4), custom_call_target="tpu_custom_call" | custom-call | tf_op jit(solution)/shard_map/density/pallas_call | solution.py:581
  121.3 2.8 %all-to-all-start.4 = ((f32[32,2,128]{2,1,0:T(2,128)}), f32[32,2,128]{2,1,0:T(2,128)S(1)}, u32[]{:S(2)}, u32[]{:S(2)}) async-start(f32[32,2,128]{2,1,0:T(2,128)} %get-tuple-element.49), calls=%async_computation.4 | async-start | bytes 65536 | tf_op jit(solution)/shard_map/all_to_all | solution.py:30
  124.1 12.6 %direct.3.refs_1_ = f32[6,128,128]{2,1,0:T(8,128)} custom-call(bf16[2048,768]{1,0:T(8,128)(2,1)} %get-tuple-element.38.refs_0_, bf16[2048,1024]{1,0:T(8,128)(2,1)} %turn.1.refs_1_, bf16[768,2048]{1,0:T(8,128)(2,1)} %get-tuple-element.40.refs_2_, bf16[3,256,256]{2,1,0:T(8,128)(2,1)} %get-tuple-element.50.refs_3_, bf16[192,1024]{1,0:T(8,128)(2,1)} %bitcast.12, ...), custom_call_target="tpu_custom_call" | custom-call | flops 6442450944 | bytes 12582912 | tf_op jit(solution)/shard_map/direct/pallas_call | solution.py:600
  136.7 0.6 copy-done.15
  137.3 4.1 %exchange.3 = bf16[32,16,128]{2,1,0:T(8,128)(2,1)} custom-call(f32[32,2,128]{2,1,0:T(2,128)} %copy-done.15, f32[6,128,128]{2,1,0:T(8,128)} %direct.3.refs_1_, bf16[256,8192]{1,0:T(8,128)(2,1)} %refs_2_.3, bf16[768,256]{1,0:T(8,128)(2,1)} %get-tuple-element.35.refs_1_.refs_3_, bf16[4,192,256]{2,1,0:T(8,128)(2,1)} %copy-done.4), custom_call_target="tpu_custom_call" | custom-call | tf_op jit(solution)/shard_map/exchange/pallas_call | solution.py:623
  141.4 14.1 %all_to_all.37.recv_ref = bf16[32,16,128]{2,1,0:T(8,128)(2,1)S(1)} all-to-all(bf16[32,16,128]{2,1,0:T(8,128)(2,1)} %exchange.3), channel_id=1, replica_groups=mesh['ka'=4,'band'=8] {'ka','band'}, dimensions={0} | all-to-all | bytes 262144 | tf_op jit(solution)/shard_map/all_to_all | solution.py:30
  155.5 1.3 second_owner.1
  156.8 9.0 %all_to_all.38.msgs_ref = f32[32,2,128]{2,1,0:T(2,128)S(1)} all-to-all(f32[32,2,128]{2,1,0:T(2,128)S(1)} %get-tuple-element.53), channel_id=1, replica_groups=mesh['ka'=4,'band'=8] {'ka','band'}, dimensions={0} | all-to-all | bytes 65536 | tf_op jit(solution)/shard_map/all_to_all | solution.py:30
  165.9 1.3 finish.1
  (59 shorter events, 0.3 us)
Async XLA Ops:
  4.1 12.6 %collective-permute-start = (bf16[24,2176]{1,0:T(8,128)(2,1)S(1)}, bf16[24,2176]{1,0:T(8,128)(2,1)S(1)}, u32[]{:S(2)}, u32[]{:S(2)}) collective-permute-start(bf16[24,2176]{1,0:T(8,128)(2,1)S(1)} %get-tuple-element.60), channel_id=1, source_target_pairs={{0,8},{8,0},{16,24},{24,16},{1,9},{9,1},{17,25},{25,17},{2,10},{10... | collective-permute-start | bytes 313352 | tf_op jit(solution)/shard_map/ppermute | solution.py:448
  7.2 10.9 %collective-permute-start.1 = (bf16[24,2176]{1,0:T(8,128)(2,1)S(1)}, bf16[24,2176]{1,0:T(8,128)(2,1)S(1)}, u32[]{:S(2)}, u32[]{:S(2)}) collective-permute-start(bf16[24,2176]{1,0:T(8,128)(2,1)S(1)} %get-tuple-element.61), channel_id=1, source_target_pairs={{0,16},{8,24},{16,0},{24,8},{1,17},{9,25},{17,1},{25,9},{2,18},{10... | collective-permute-start | bytes 313352 | tf_op jit(solution)/shard_map/ppermute | solution.py:448
  9.8 8.3 %collective-permute-start.2 = (bf16[24,2176]{1,0:T(8,128)(2,1)S(1)}, bf16[24,2176]{1,0:T(8,128)(2,1)S(1)}, u32[]{:S(2)}, u32[]{:S(2)}) collective-permute-start(bf16[24,2176]{1,0:T(8,128)(2,1)S(1)} %get-tuple-element.62), channel_id=1, source_target_pairs={{0,24},{8,16},{16,8},{24,0},{1,25},{9,17},{17,9},{25,1},{2,26},{10... | collective-permute-start | bytes 313352 | tf_op jit(solution)/shard_map/ppermute | solution.py:448
  11.6 32.5 %all-to-all-start = ((bf16[4,192,256]{2,1,0:T(8,128)(2,1)}), bf16[4,192,256]{2,1,0:T(8,128)(2,1)S(1)}, u32[]{:S(2)}, u32[]{:S(2)}) async-start(bf16[4,192,256]{2,1,0:T(8,128)(2,1)} %cut.1), calls=%async_computation | async-start | bytes 786432 | tf_op jit(solution)/shard_map/all_to_all | solution.py:535
  18.1 14.6 %copy-start.5 = (bf16[96,2176]{1,0:T(8,128)(2,1)}, bf16[96,2176]{1,0:T(8,128)(2,1)S(1)}, u32[]{:S(2)}) copy-start(bf16[96,2176]{1,0:T(8,128)(2,1)S(1)} %pad_maximum_fusion.refs_0_) | copy-start | bytes 1253380
  18.1 25.9 %collective-permute-start.3 = (bf16[96,2176]{1,0:T(8,128)(2,1)S(1)}, bf16[96,2176]{1,0:T(8,128)(2,1)S(1)}, u32[]{:S(2)}, u32[]{:S(2)}) collective-permute-start(bf16[96,2176]{1,0:T(8,128)(2,1)S(1)} %pad_maximum_fusion.refs_0_), channel_id=1, source_target_pairs={{0,2},{1,3},{2,0},{3,1},{4,6},{5,7},{6,4},{7,5},{8,10},{9,11},{10,... | collective-permute-start | bytes 1253384 | tf_op jit(solution)/shard_map/ppermute | solution.py:448
  19.7 24.4 %collective-permute-start.4 = (bf16[96,2176]{1,0:T(8,128)(2,1)S(1)}, bf16[96,2176]{1,0:T(8,128)(2,1)S(1)}, u32[]{:S(2)}, u32[]{:S(2)}) collective-permute-start(bf16[96,2176]{1,0:T(8,128)(2,1)S(1)} %pad_maximum_fusion.refs_0_), channel_id=1, source_target_pairs={{0,4},{1,5},{2,6},{3,7},{4,0},{5,1},{6,2},{7,3},{8,12},{9,13},{10,... | collective-permute-start | bytes 1253384 | tf_op jit(solution)/shard_map/ppermute | solution.py:448
  21.2 22.9 %collective-permute-start.5 = (bf16[96,2176]{1,0:T(8,128)(2,1)S(1)}, bf16[96,2176]{1,0:T(8,128)(2,1)S(1)}, u32[]{:S(2)}, u32[]{:S(2)}) collective-permute-start(bf16[96,2176]{1,0:T(8,128)(2,1)S(1)} %pad_maximum_fusion.refs_0_), channel_id=1, source_target_pairs={{0,1},{1,0},{2,3},{3,2},{4,5},{5,4},{6,7},{7,6},{8,9},{9,8},{10,11... | collective-permute-start | bytes 1253384 | tf_op jit(solution)/shard_map/ppermute | solution.py:448
  22.2 10.5 %copy-start.14 = (bf16[3,64,1024]{2,1,0:T(8,128)(2,1)}, bf16[3,64,1024]{2,1,0:T(8,128)(2,1)S(1)}, u32[]{:S(2)}) copy-start(bf16[3,64,1024]{2,1,0:T(8,128)(2,1)S(1)} %constant_dynamic-slice_fusion) | copy-start | bytes 1179652
  22.2 14.4 %collective-permute-start.6 = (bf16[192,1024]{1,0:T(8,128)(2,1)S(1)}, bf16[192,1024]{1,0:T(8,128)(2,1)S(1)}, u32[]{:S(2)}, u32[]{:S(2)}) collective-permute-start(bf16[192,1024]{1,0:T(8,128)(2,1)S(1)} %bitcast.9), channel_id=1, source_target_pairs={{0,8},{8,16},{16,24},{1,9},{9,17},{17,25},{2,10},{10,18},{18,26},{... | collective-permute-start | bytes 1179656 | tf_op jit(solution)/shard_map/ppermute | solution.py:458
  27.7 16.3 %collective-permute-start.7 = (bf16[192,1024]{1,0:T(8,128)(2,1)S(1)}, bf16[192,1024]{1,0:T(8,128)(2,1)S(1)}, u32[]{:S(2)}, u32[]{:S(2)}) collective-permute-start(bf16[192,1024]{1,0:T(8,128)(2,1)S(1)} %bitcast.10), channel_id=1, source_target_pairs={{8,0},{16,8},{24,16},{9,1},{17,9},{25,17},{10,2},{18,10},{26,18},{... | collective-permute-start | bytes 1179656 | tf_op jit(solution)/shard_map/ppermute | solution.py:458
  36.7 39.5 %copy-start.17 = (bf16[192,1024]{1,0:T(8,128)(2,1)}, bf16[192,1024]{1,0:T(8,128)(2,1)S(1)}, u32[]{:S(2)}) copy-start(bf16[192,1024]{1,0:T(8,128)(2,1)S(1)} %collective-permute-done.6.refs_5_) | copy-start | bytes 1179652
  44.0 32.2 %copy-start.18 = (bf16[192,1024]{1,0:T(8,128)(2,1)}, bf16[192,1024]{1,0:T(8,128)(2,1)S(1)}, u32[]{:S(2)}) copy-start(bf16[192,1024]{1,0:T(8,128)(2,1)S(1)} %collective-permute-done.7.refs_8_) | copy-start | bytes 1179652
  44.0 16.6 %copy-start.6 = (bf16[96,2176]{1,0:T(8,128)(2,1)}, bf16[96,2176]{1,0:T(8,128)(2,1)S(1)}, u32[]{:S(2)}) copy-start(bf16[96,2176]{1,0:T(8,128)(2,1)S(1)} %collective-permute-done.3.refs_2_) | copy-start | bytes 1253380
  44.0 16.6 %copy-start.7 = (bf16[96,2176]{1,0:T(8,128)(2,1)}, bf16[96,2176]{1,0:T(8,128)(2,1)S(1)}, u32[]{:S(2)}) copy-start(bf16[96,2176]{1,0:T(8,128)(2,1)S(1)} %collective-permute-done.4.refs_4_) | copy-start | bytes 1253380
  44.1 16.6 %copy-start.10 = (bf16[96,2176]{1,0:T(8,128)(2,1)}, bf16[96,2176]{1,0:T(8,128)(2,1)S(1)}, u32[]{:S(2)}) copy-start(bf16[96,2176]{1,0:T(8,128)(2,1)S(1)} %collective-permute-done.5.refs_1_) | copy-start | bytes 1253380
  44.1 24.1 %copy-start.4 = (bf16[4,192,256]{2,1,0:T(8,128)(2,1)}, bf16[4,192,256]{2,1,0:T(8,128)(2,1)S(1)}, u32[]{:S(2)}) copy-start(bf16[4,192,256]{2,1,0:T(8,128)(2,1)S(1)} %all-to-all-done.refs_2_.refs_4_) | copy-start | bytes 1179652
  44.1 6.9 %collective-permute-start.10 = (bf16[48,2176]{1,0:T(8,128)(2,1)S(1)}, bf16[48,2176]{1,0:T(8,128)(2,1)S(1)}, u32[]{:S(2)}, u32[]{:S(2)}) collective-permute-start(bf16[48,2176]{1,0:T(8,128)(2,1)S(1)} %slice.6), channel_id=1, source_target_pairs={{0,4},{1,5},{2,6},{3,7},{4,0},{5,1},{6,2},{7,3},{8,12},{9,13},{10,... | collective-permute-start | bytes 626696 | tf_op jit(solution)/shard_map/ppermute | solution.py:448
  44.7 6.6 %collective-permute-start.11 = (bf16[48,2176]{1,0:T(8,128)(2,1)S(1)}, bf16[48,2176]{1,0:T(8,128)(2,1)S(1)}, u32[]{:S(2)}, u32[]{:S(2)}) collective-permute-start(bf16[48,2176]{1,0:T(8,128)(2,1)S(1)} %slice.7), channel_id=1, source_target_pairs={{0,2},{1,3},{2,0},{3,1},{4,6},{5,7},{6,4},{7,5},{8,10},{9,11},{10,... | collective-permute-start | bytes 626696 | tf_op jit(solution)/shard_map/ppermute | solution.py:448
  45.3 6.3 %collective-permute-start.13 = (bf16[192,1024]{1,0:T(8,128)(2,1)S(1)}, bf16[192,1024]{1,0:T(8,128)(2,1)S(1)}, u32[]{:S(2)}, u32[]{:S(2)}) collective-permute-start(bf16[192,1024]{1,0:T(8,128)(2,1)S(1)} %collective-permute-done.6.refs_5_), channel_id=1, source_target_pairs={{8,16},{16,24},{9,17},{17,25},{10,18},{18,26},{11,19},{19,27},{12,... | collective-permute-start | bytes 1179656 | tf_op jit(solution)/shard_map/ppermute | solution.py:458
  46.0 13.3 %collective-permute-start.14 = (bf16[192,1024]{1,0:T(8,128)(2,1)S(1)}, bf16[192,1024]{1,0:T(8,128)(2,1)S(1)}, u32[]{:S(2)}, u32[]{:S(2)}) collective-permute-start(bf16[192,1024]{1,0:T(8,128)(2,1)S(1)} %collective-permute-done.7.refs_8_), channel_id=1, source_target_pairs={{8,0},{16,8},{9,1},{17,9},{10,2},{18,10},{11,3},{19,11},{12,4},{20... | collective-permute-start | bytes 1179656 | tf_op jit(solution)/shard_map/ppermute | solution.py:458
  47.3 13.3 %collective-permute-start.8 = (bf16[96,2176]{1,0:T(8,128)(2,1)S(1)}, bf16[96,2176]{1,0:T(8,128)(2,1)S(1)}, u32[]{:S(2)}, u32[]{:S(2)}) collective-permute-start(bf16[96,2176]{1,0:T(8,128)(2,1)S(1)} %collective-permute-done.3.refs_2_), channel_id=1, source_target_pairs={{0,1},{1,0},{2,3},{3,2},{4,5},{5,4},{6,7},{7,6},{8,9},{9,8},{10,11... | collective-permute-start | bytes 1253384 | tf_op jit(solution)/shard_map/ppermute | solution.py:448
  51.0 9.7 %copy-start.8 = (bf16[48,2176]{1,0:T(8,128)(2,1)}, bf16[48,2176]{1,0:T(8,128)(2,1)S(1)}, u32[]{:S(2)}) copy-start(bf16[48,2176]{1,0:T(8,128)(2,1)S(1)} %collective-permute-done.10.refs_6_) | copy-start | bytes 626692
  51.0 9.7 %collective-permute-start.9 = (bf16[96,2176]{1,0:T(8,128)(2,1)S(1)}, bf16[96,2176]{1,0:T(8,128)(2,1)S(1)}, u32[]{:S(2)}, u32[]{:S(2)}) collective-permute-start(bf16[96,2176]{1,0:T(8,128)(2,1)S(1)} %collective-permute-done.4.refs_4_), channel_id=1, source_target_pairs={{0,1},{1,0},{2,3},{3,2},{4,5},{5,4},{6,7},{7,6},{8,9},{9,8},{10,11... | collective-permute-start | bytes 1253384 | tf_op jit(solution)/shard_map/ppermute | solution.py:448
  51.3 9.4 %copy-start.9 = (bf16[48,2176]{1,0:T(8,128)(2,1)}, bf16[48,2176]{1,0:T(8,128)(2,1)S(1)}, u32[]{:S(2)}) copy-start(bf16[48,2176]{1,0:T(8,128)(2,1)S(1)} %collective-permute-done.11.refs_7_) | copy-start | bytes 626692
  51.3 9.3 %collective-permute-start.12 = (bf16[96,2176]{1,0:T(8,128)(2,1)S(1)}, bf16[96,2176]{1,0:T(8,128)(2,1)S(1)}, u32[]{:S(2)}, u32[]{:S(2)}) collective-permute-start(bf16[96,2176]{1,0:T(8,128)(2,1)S(1)} %pad_maximum_fusion.1), channel_id=1, source_target_pairs={{0,1},{1,0},{2,3},{3,2},{4,5},{5,4},{6,7},{7,6},{8,9},{9,8},{10,11... | collective-permute-start | bytes 1253384 | tf_op jit(solution)/shard_map/ppermute | solution.py:448
  51.6 24.6 %copy-start.19 = (bf16[192,1024]{1,0:T(8,128)(2,1)}, bf16[192,1024]{1,0:T(8,128)(2,1)S(1)}, u32[]{:S(2)}) copy-start(bf16[192,1024]{1,0:T(8,128)(2,1)S(1)} %collective-permute-done.13.refs_6_) | copy-start | bytes 1179652
  51.6 24.6 %collective-permute-start.15 = (bf16[192,1024]{1,0:T(8,128)(2,1)S(1)}, bf16[192,1024]{1,0:T(8,128)(2,1)}, u32[]{:S(2)}, u32[]{:S(2)}) collective-permute-start(bf16[192,1024]{1,0:T(8,128)(2,1)S(1)} %collective-permute-done.13.refs_6_), channel_id=1, source_target_pairs={{16,24},{17,25},{18,26},{19,27},{20,28},{21,29},{22,30},{23,31}} | collective-permute-start | bytes 1179656 | tf_op jit(solution)/shard_map/ppermute | solution.py:458
  59.3 16.9 %copy-start.20 = (bf16[192,1024]{1,0:T(8,128)(2,1)}, bf16[192,1024]{1,0:T(8,128)(2,1)S(1)}, u32[]{:S(2)}) copy-start(bf16[192,1024]{1,0:T(8,128)(2,1)S(1)} %collective-permute-done.14.refs_9_) | copy-start | bytes 1179652
  59.3 16.8 %collective-permute-start.16 = (bf16[192,1024]{1,0:T(8,128)(2,1)S(1)}, bf16[192,1024]{1,0:T(8,128)(2,1)}, u32[]{:S(2)}, u32[]{:S(2)}) collective-permute-start(bf16[192,1024]{1,0:T(8,128)(2,1)S(1)} %collective-permute-done.14.refs_9_), channel_id=1, source_target_pairs={{8,0},{9,1},{10,2},{11,3},{12,4},{13,5},{14,6},{15,7}} | collective-permute-start | bytes 1179656 | tf_op jit(solution)/shard_map/ppermute | solution.py:458
  60.6 0.8 copy-start.11
  60.6 1.0 copy-start.12
  61.6 0.8 copy-start.13
  70.3 18.5 %all-to-all-start.1 = ((f32[32,2,128]{2,1,0:T(2,128)}), f32[32,2,128]{2,1,0:T(2,128)S(1)}, u32[]{:S(2)}, u32[]{:S(2)}) async-start(f32[32,2,128]{2,1,0:T(2,128)} %get-tuple-element.37), calls=%async_computation.1 | async-start | bytes 65536 | tf_op jit(solution)/shard_map/all_to_all | solution.py:30
  88.8 18.9 %copy-start.1 = (bf16[32,16,128]{2,1,0:T(8,128)(2,1)S(1)}, bf16[32,16,128]{2,1,0:T(8,128)(2,1)}, u32[]{:S(2)}) copy-start(bf16[32,16,128]{2,1,0:T(8,128)(2,1)} %get-tuple-element.34.refs_0_.msgs_ref) | copy-start | bytes 393220
  88.8 18.9 %copy-start.2 = (f32[16,128]{1,0:T(8,128)S(1)}, f32[16,128]{1,0:T(8,128)}, u32[]{:S(2)}) copy-start(f32[16,128]{1,0:T(8,128)} %get-tuple-element.46.gap_ref) | copy-start | bytes 24580
  88.8 18.9 %copy-start.3 = (f32[16,128]{1,0:T(8,128)S(1)}, f32[16,128]{1,0:T(8,128)}, u32[]{:S(2)}) copy-start(f32[16,128]{1,0:T(8,128)} %get-tuple-element.47.own_ref) | copy-start | bytes 24580
  88.8 0.6 copy-start.16
  121.3 15.4 %all-to-all-start.4 = ((f32[32,2,128]{2,1,0:T(2,128)}), f32[32,2,128]{2,1,0:T(2,128)S(1)}, u32[]{:S(2)}, u32[]{:S(2)}) async-start(f32[32,2,128]{2,1,0:T(2,128)} %get-tuple-element.49), calls=%async_computation.4 | async-start | bytes 65536 | tf_op jit(solution)/shard_map/all_to_all | solution.py:30
  136.7 18.8 %copy-start = (bf16[32,16,128]{2,1,0:T(8,128)(2,1)S(1)}, bf16[32,16,128]{2,1,0:T(8,128)(2,1)}, u32[]{:S(2)}) copy-start(bf16[32,16,128]{2,1,0:T(8,128)(2,1)} %all_to_all.36.refs_0_.msgs_ref) | copy-start | bytes 393220
  136.7 0.6 copy-start.15

commit v12 on v11

--- a/solution.py
+++ b/solution.py
@@ -102,58 +102,61 @@
     return ka * n_band + jnp.bitwise_xor(lax.axis_index("band"), d)
 
 
-def own_copies(ref, dest, sems):
-    return [
-        pltpu.make_async_copy(
-            ref.at[jnp.bitwise_xor(lax.axis_index("ka"), j)], dest.at[j], sems.at[j]
-        )
-        for j in range(dest.shape[0])
-    ]
-
-
 def pair_rows(ref, kp):
     part = ref[:, kp * 2 * ROWS : (kp + 1) * 2 * ROWS, :]
     return part.reshape(part.shape[0] * 2 * ROWS, part.shape[2])
 
 
-def pack_kernel(start_in, cond_in, val_in, own_ref, gap_ref, msg_ref, start_ref, cond_ref, val_ref, sems):
-    ins = ((start_in, start_ref), (cond_in, cond_ref), (val_in, val_ref))
-    copies = [pltpu.make_async_copy(ref, to, sems.at[i]) for i, (ref, to) in enumerate(ins)]
-    start_all(copies)
-    wait_all(copies)
+def pack_kernel(n_ka, nu, *refs):
+    start_in, cond_in, val_in, val_ref, orb_ref = refs[:5]
+    own_ref, gap_ref, outs, refs = refs[5], refs[6], refs[7 : 7 + n_ka], refs[7 + n_ka :]
+    start_ref, cond_ref, energy_ref, cuts, sems, cut_sems = refs
+    own = cuts.shape[-1]
+    ins = ((start_in, start_ref), (cond_in, cond_ref), (val_in, energy_ref))
+    small = [pltpu.make_async_copy(ref, to, sems.at[i]) for i, (ref, to) in enumerate(ins)]
+    k_dev = val_ref.shape[0]
+    val_copies, cut_copies = [], []
+    for j in range(n_ka):
+        at = pl.multiple_of(jnp.bitwise_xor(lax.axis_index("ka"), j) * nu, nu)
+        point = pl.multiple_of(at + lax.axis_index("band") * own, LANES)
+        val_copies.append(
+            pltpu.make_async_copy(
+                val_ref.at[:, :, pl.ds(at, nu)], outs[j].at[:, :, pl.ds(0, nu)], cut_sems.at[0, j]
+            )
+        )
+        cut_copies.append(
+            pltpu.make_async_copy(
+                orb_ref.at[:, :, pl.ds(point, own)], cuts.at[j], cut_sems.at[1, j]
+            )
+        )
+    start_all(small + cut_copies + val_copies)
+    wait_all(small)
     own_ref[...] = jnp.zeros_like(own_ref)
     gap_ref[...] = jnp.zeros_like(gap_ref)
     cond = jnp.concatenate([cond_ref[...], cond_ref[...]], axis=1)
-    for kl in range(start_ref.shape[0]):
+    for kl in range(k_dev):
         half = kl % 2
         for v in range(ROWS):
             at = pl.ds(kl // 2 * ROWS + v, 1)
             row = start_ref[pl.ds(kl, 1), pl.ds(v // 2 * LANES, LANES)]
             own_ref[at, :] = own_ref[at, :] + lane_half(row, v % 2, half)
-            gap = cond[kl : kl + 1, :] - val_ref[kl, v]
+            gap = cond[kl : kl + 1, :] - energy_ref[kl, v]
             gap_ref[at, :] = gap_ref[at, :] + lane_half(gap, half, half)
-    own = own_ref[...]
-    square = own * own
-    block = with_sums(own, [jnp.sum(square), jnp.sum(gap_ref[...] * square)])
-    msg_ref[...] = block.astype(BF)
-
-
-def cut_kernel(cond_ref, out_ref, sems):
-    n_ka, _, own = out_ref.shape
-    k_dev, n_cond, npt = cond_ref.shape
-    copies = []
-    for z in range(n_ka):
-        at = z * (npt // n_ka) + lax.axis_index("band") * own
+    mine = own_ref[...]
+    square = mine * mine
+    block = with_sums(mine, [jnp.sum(square), jnp.sum(gap_ref[...] * square)])
+    for j in range(n_ka):
+        for g in range(k_dev):
+            head = jnp.zeros((ROWS, LANES), F32)
+            if (g + 1) * ROWS <= block.shape[0]:
+                head = block[g * ROWS : (g + 1) * ROWS, :]
+            outs[j][g, :, nu : nu + LANES] = head.astype(BF)
+        cut_copies[j].wait()
         for kl in range(k_dev):
-            copies.append(
-                pltpu.make_async_copy(
-                    cond_ref.at[kl, :, pl.ds(pl.multiple_of(at, LANES), own)],
-                    out_ref.at[z, pl.ds(kl * n_cond, n_cond), :],
-                    sems.at[len(copies)],
-                )
-            )
-    start_all(copies)
-    wait_all(copies)
+            cut = cuts[j, kl].astype(F32)
+            wide = [cut[q * ROWS : (q + 1) * ROWS, :] for q in range(cut.shape[0] // ROWS)]
+            outs[j][kl, :, nu + LANES :] = jnp.concatenate(wide, axis=1).astype(BF)
+    wait_all(val_copies)
 
 
 def turn_kernel(tile, scr_ref, out_ref, scrs, turned, in_sems, out_sems):
@@ -172,13 +175,28 @@
 
 
 def order_kernel(parts, n_ka, *refs):
-    val_refs, refs = refs[:-10], refs[-10:]
-    rows_out, turned_out, own_out, msgs_out, vals, heads, ordered, turned, val_sems, out_sems = refs
+    got_refs, val_refs, refs = refs[:n_ka], refs[n_ka:-13], refs[-13:]
+    rows_out, turned_out, own_out, cond_out, msgs_out = refs[:5]
+    vals, heads, ordered, turned, cuts, val_sems, out_sems, cut_sems = refs[5:]
     own = own_out.shape[1]
     nu = ordered.shape[1]
     copies = piece_copies(val_refs, parts, 0, nu, vals, val_sems.at[0])
     head_copies = piece_copies(val_refs, parts, nu, LANES, heads, val_sems.at[1])
-    start_all(copies + head_copies)
+    cut_copies = [
+        pltpu.make_async_copy(
+            ref.at[:, :, pl.ds(nu + LANES, cuts.shape[-1])], cuts.at[j], cut_sems.at[j]
+        )
+        for j, ref in enumerate(got_refs)
+    ]
+    start_all(copies + head_copies + cut_copies)
+    wait_all(cut_copies)
+    k_dev, points = cuts.shape[1], cuts.shape[-1] // own
+    for j in range(n_ka):
+        for kl in range(k_dev):
+            cut = cuts[j, kl].astype(F32)
+            tall = [cut[:, q * own : (q + 1) * own] for q in range(points)]
+            at = (j * k_dev + kl) * points * ROWS
+            cond_out[at : at + points * ROWS, :] = jnp.concatenate(tall, axis=0).astype(BF)
     wait_all(copies)
     n_band, group = vals.shape[0], vals.shape[0] * 2 * ROWS
     column = pl.multiple_of(lax.axis_index("band") * own, LANES)
@@ -209,12 +227,13 @@
 def density_kernel(cfg, *refs):
     n_ka, n_band, k_dev = cfg
     k_points = n_ka * k_dev
-    msgs_ref, vown_ref, cond_ref, qx_ref, rho_ref = refs[:5]
-    xs, msgs, vown, conds, cond_sems, sems = refs[5:]
+    msgs_ref, vown_ref, cond_ref, qx_ref, rho_ref, xs, msgs, vown, conds, sems = refs
     own = vown_ref.shape[1]
     msg_copy = pltpu.make_async_copy(msgs_ref, msgs, sems.at[0])
-    copies = own_copies(cond_ref, conds, cond_sems)
-    copies.append(pltpu.make_async_copy(vown_ref, vown, sems.at[1]))
+    copies = [
+        pltpu.make_async_copy(vown_ref, vown, sems.at[1]),
+        pltpu.make_async_copy(cond_ref, conds, sems.at[2]),
+    ]
     start_all([msg_copy] + copies)
     xs[...] = jnp.zeros_like(xs)
     msg_copy.wait()
@@ -228,13 +247,12 @@
             xs[k // 4, at, pl.ds(base, LANES)] = lane_half(tile, kl % 2, k % 2)
     qx_ref[...] = xs[...].astype(BF)
     wait_all(copies)
-    cond_rows = conds[...].reshape(-1, own)
     rho = jnp.zeros((1, own), F32)
     quad = 2 * LANES
     for kq in range(k_points // 4):
         at = slice(kq * quad, (kq + 1) * quad)
         mixed = dot_tn(qx_ref[kq], vown[at, :])
-        rho = rho + jnp.sum(mixed * cond_rows[at, :].astype(F32), axis=0, keepdims=True)
+        rho = rho + jnp.sum(mixed * conds[at, :].astype(F32), axis=0, keepdims=True)
     for r in range(own // LANES):
         part = rho[:, r * LANES : (r + 1) * LANES]
         rho_ref[:, r, :] = jnp.broadcast_to(part, (rho_ref.shape[0], LANES))
@@ -274,14 +292,11 @@
     row_copy = pltpu.make_async_copy(rows_ref, vals, row_sem.at[0])
     start_all([qx_copy, turned_copies[0]])
     each_cond(lambda copy: copy.start())
-    scr_copies[0].start()
-    for i in range(1, nu // tile):
-        start_all([turned_copies[i], scr_copies[i]])
-    row_copy.start()
     qx_copy.wait()
     for i in range(nu // tile):
         rows = slice(i * tile, (i + 1) * tile)
         turned_copies[i].wait()
+        scr_copies[i].start()
         for kq in range(qx.shape[0]):
             cols = slice(kq * quad, (kq + 1) * quad)
             mixed[rows, cols] = jnp.dot(
@@ -290,6 +305,7 @@
         if i == 0:
             each_cond(lambda copy: copy.wait())
             cond_rows = conds[...].reshape(-1, mu)
+        start_all(turned_copies[i + 1 : i + 2] or [row_copy])
         scr_copies[i].wait()
         amp = jnp.dot(mixed[rows, :], cond_rows, preferred_element_type=F32)
         kern[rows, :] = (scrs[rows, :].astype(F32) * amp * scale).astype(BF)
@@ -303,8 +319,8 @@
 def exchange_kernel(cfg, chunk, scale, *refs):
     n_ka, n_band, k_dev = cfg
     k_points = n_ka * k_dev
-    rho_ref, di_ref, coul_ref, vown_ref, cond_ref, refs = refs[:5] + (refs[5:],)
-    msg_ref, rhos, di, coul, conds, vown, part, msg, coul_sems, cond_sems, sems = refs
+    rho_ref, di_ref, coul_ref, vown_ref, cond_ref, msg_ref = refs[:6]
+    rhos, di, coul, conds, vown, part, msg, coul_sems, sems = refs[6:]
     own, npt = coul_ref.shape
     coul_copies = [
         pltpu.make_async_copy(
@@ -313,25 +329,30 @@
         for i in range(npt // chunk)
     ]
     rho_copy = pltpu.make_async_copy(rho_ref, rhos, sems.at[0])
-    copies = own_copies(cond_ref, conds, cond_sems)
-    copies.append(pltpu.make_async_copy(vown_ref, vown, sems.at[1]))
-    copies.append(pltpu.make_async_copy(di_ref, di, sems.at[2]))
-    start_all([rho_copy] + coul_copies + copies)
+    copies = [
+        pltpu.make_async_copy(vown_ref, vown, sems.at[1]),
+        pltpu.make_async_copy(di_ref, di, sems.at[2]),
+        pltpu.make_async_copy(cond_ref, conds, sems.at[3]),
+    ]
+    ahead = 2
+    start_all([rho_copy] + coul_copies[:ahead])
     rho_copy.wait()
     acc = jnp.zeros((own, LANES), F32)
     per_dev = own // LANES
     for i in range(npt // chunk):
         coul_copies[i].wait()
+        start_all(coul_copies[i + ahead : i + ahead + 1])
+        if i + ahead == npt // chunk:
+            start_all(copies)
         for j in range(i * chunk // LANES, (i + 1) * chunk // LANES):
             rho = rhos[j // per_dev, pl.ds(j % per_dev, 1), :].astype(BF).astype(F32)
             acc = acc + coul[:, j * LANES : (j + 1) * LANES].astype(F32) * rho
     potential = scale * jnp.sum(acc.T, axis=0, keepdims=True)
     wait_all(copies)
-    cond_rows = conds[...].reshape(-1, own)
     for kp in range(k_points // 2):
         at = slice(kp * LANES, (kp + 1) * LANES)
         weighted = (vown[at, :].astype(F32) * potential).astype(BF)
-        part[kp] = 2.0 * dot_nt(weighted, cond_rows[at, :]) - di[kp]
+        part[kp] = 2.0 * dot_nt(weighted, conds[at, :]) - di[kp]
     for d in range(n_band):
         for j in range(n_ka):
             for g in range((k_dev + 1) // 2):
@@ -461,7 +482,7 @@
     return flows
 
 
-def plane_pieces(own_piece, others):
+def plane_pieces(own_piece, others, later):
     def move(block, d):
         return swap(block, "band", d)
 
@@ -471,11 +492,12 @@
     by_x, by_y, core, others = lax.optimization_barrier((by_x, by_y, core, others))
     diag = [move(by_x[:half], 4), move(by_y[half:], 2)]
     near_x, near_y = move(by_x, 1), move(by_y, 1)
+    diag, later = lax.optimization_barrier((diag, later))
     far = move(jnp.concatenate(diag, axis=0), 1)
     arrays = [own_piece, core, by_x, near_x, by_y, near_y, diag[0], diag[1], far]
     parts = tuple(((i, 0, rows),) for i in range(6))
     parts += (((6, 0, half), (7, 0, half)), ((8, 0, rows),))
-    return arrays, parts, others
+    return arrays, parts, others, later
 
 
 def kernel_path(start_vec, val_energy, cond_energy, val_orb, cond_orb, coulomb, screened):
@@ -497,42 +519,31 @@
 
     block = ((k_dev + 1) // 2 * ROWS, LANES)
     msg_shape = shape_of((devices,) + block, BF)
-    start_own, gap, message = call(
-        pack_kernel,
+    wide = nu_blk + LANES
+    cut_lanes = n_cond // ROWS * own
+    start_own, gap, *payloads = call(
+        functools.partial(pack_kernel, n_ka, nu_blk),
         "pack",
-        (shape_of(block), shape_of(block), shape_of(block, BF)),
-        [ANY] * 3,
-        (VMEM, VMEM, VMEM),
+        (shape_of(block), shape_of(block))
+        + (shape_of((k_dev, nv_blk, wide + cut_lanes), BF),) * n_ka,
+        [ANY] * 5,
+        (VMEM,) * (2 + n_ka),
         [
             pltpu.VMEM(start_vec.shape, F32),
             pltpu.VMEM(cond_energy.shape, F32),
             pltpu.SMEM(val_energy.shape, F32),
+            pltpu.VMEM((n_ka, k_dev, n_cond, own), BF),
             dma(3),
+            dma(2, n_ka),
         ],
-    )(start_vec, cond_energy, val_energy)
-
-    head = jnp.pad(message, ((0, k_dev * nv_blk - block[0]), (0, 0)))
-
-    def val_to(j):
-        part = lax.dynamic_slice_in_dim(val_orb, jnp.bitwise_xor(ka, j) * nu_blk, nu_blk, 2)
-        return jnp.concatenate([part.reshape(k_dev * nv_blk, nu_blk), head], axis=1)
-
-    val_cut = jnp.concatenate(
-        [val_to(0)] + [swap(val_to(j), "ka", j) for j in range(1, n_ka)], axis=0
-    )
-    cond_local = lax.dynamic_slice_in_dim(cond_orb, band * mu_blk, mu_blk, 2)
+    )(start_vec, cond_energy, val_energy, val_orb, cond_orb)
+    base, payloads = lax.optimization_barrier((band * mu_blk, payloads))
+    got = [payloads[0]] + [swap(payloads[j], "ka", j) for j in range(1, n_ka)]
+    val_cut = jnp.concatenate([part[:, :, :wide] for part in got], axis=0)
+    val_cut = val_cut.reshape(piece_rows, wide)
+    cond_local = lax.dynamic_slice_in_dim(cond_orb, base, mu_blk, 2)
     cond_local = cond_local.reshape(k_dev * n_cond, mu_blk)
     below, above = line_gather(cond_local, "ka")
-    own_rows = k_dev * n_cond
-    cuts = call(
-        cut_kernel,
-        "cut",
-        shape_of((n_ka, own_rows, own), BF),
-        [ANY],
-        VMEM,
-        [dma(n_ka * k_dev)],
-    )(cond_orb)
-    cond_own = lax.all_to_all(cuts, "ka", split_axis=0, concat_axis=0, tiled=True)
 
     chunk, tile = 1024, 1024
     rows_all, conds_all = k_points * nv_blk * n_band, k_points * n_cond
@@ -546,32 +557,36 @@
         + [dma(2 * nu_blk // tile)] * 2,
         moved=8 * MIB,
     )(screened)
-    pieces, parts, (scr_turned, cond_own, below[0], above[0]) = plane_pieces(
-        val_cut, (scr_turned, cond_own, below[0], above[0])
+    pieces, parts, others, later = plane_pieces(
+        val_cut, (scr_turned, below[0], above[0]), (below[1:-1], above[1:-1])
     )
-    val_rows, val_turned, val_own, msgs = call(
+    scr_turned, below[0], above[0] = others
+    below[1:-1], above[1:-1] = later
+    val_rows, val_turned, val_own, cond_own, msgs = call(
         functools.partial(order_kernel, parts, n_ka),
         "order",
         (
             shape_of((rows_all, nu_blk), BF),
             shape_of((nu_blk, rows_all), BF),
             shape_of((rows_all, own), BF),
+            shape_of((conds_all, own), BF),
             msg_shape,
         ),
-        [ANY] * len(pieces),
-        (ANY, ANY, ANY, VMEM),
+        [ANY] * (n_ka + len(pieces)),
+        (ANY, ANY, ANY, VMEM, VMEM),
         [
             pltpu.VMEM((n_band, piece_rows, nu_blk), BF),
             pltpu.VMEM((n_band, piece_rows, LANES), BF),
             pltpu.VMEM((rows_all, nu_blk), BF),
             pltpu.VMEM((nu_blk, rows_all), BF),
+            pltpu.VMEM((n_ka, k_dev, nv_blk, cut_lanes), BF),
             dma(2, sum(len(piece) for piece in parts)),
             dma(3, pairs),
+            dma(n_ka),
         ],
         moved=9 * MIB,
-    )(*pieces)
-
-    msgs, below[1:-1], above[1:-1] = lax.optimization_barrier((msgs, below[1:-1], above[1:-1]))
+    )(*got, *pieces)
+
     cond_pts = [cond_local] + below + above
     cfg = (n_ka, n_band, k_dev)
     quads = k_points // 4
@@ -591,9 +606,8 @@
                 pltpu.VMEM((quads, 2 * LANES, 2 * LANES), F32),
                 pltpu.VMEM((devices,) + block, BF),
                 pltpu.VMEM((rows_all, own), BF),
-                pltpu.VMEM((n_ka, own_rows, own), BF),
-                dma(n_ka),
-                dma(2),
+                pltpu.VMEM((conds_all, own), BF),
+                dma(3),
             ],
         )(msgs, val_own, cond_own)
         density = exchange_all(rho)
@@ -606,7 +620,7 @@
             [
                 pltpu.VMEM((quads, 2 * LANES, 2 * LANES), BF),
                 pltpu.VMEM((nu_blk, rows_all), BF),
-                pltpu.VMEM((n_ka, own_rows, mu_blk), BF),
+                pltpu.VMEM((n_ka, k_dev * n_cond, mu_blk), BF),
                 pltpu.VMEM((nu_blk, mu_blk), BF),
                 pltpu.VMEM((rows_all, nu_blk), BF),
                 pltpu.VMEM((nu_blk, conds_all), BF),
@@ -630,13 +644,12 @@
                 pltpu.VMEM((devices, own // LANES, LANES), F32),
                 pltpu.VMEM((pairs, LANES, LANES), F32),
                 pltpu.VMEM((own, npt_all), BF),
-                pltpu.VMEM((n_ka, own_rows, own), BF),
+                pltpu.VMEM((conds_all, own), BF),
                 pltpu.VMEM((rows_all, own), BF),
                 pltpu.VMEM((pairs, LANES, LANES), F32),
                 pltpu.VMEM((devices,) + block, F32),
                 dma(npt_all // chunk),
-                dma(n_ka),
-                dma(3),
+                dma(4),
             ],
         )(density, direct, coulomb, val_own, cond_own)
         recv = exchange_all(summed)

time: 168 us -> 166 us (0.988)
  starting transfers between devices: 35.4 us -> 30 us
  Pallas kernels: 54.1 us -> 59.4 us
    ppermute x6, waiting for transfers between devices: 17.6 us -> 12.3 us  [line_gather(): moving = lax.ppermute(moving, axis, [(i, i - way) for i in senders])]
    pallas_call x2, Pallas kernels: 8.16 us -> 13.3 us  [kernel_path(): call(functools.partial(exchange_kernel, cfg, chunk, scale), 'exchange', m...]
    all_to_all x1 -> x0, starting transfers between devices: 5.1 us -> none  [kernel_path(): lax.all_to_all(cuts, 'ka', split_axis=0, concat_axis=0, tiled=True)]
    ppermute x11, waiting for transfers between devices: 5.28 us -> 8.96 us  [swap(): lax.ppermute(block, axis, [(i, i ^ d) for i in range(lax.axis_size(axis))])]
    ppermute x6, starting transfers between devices: 11.4 us -> 8.05 us  [line_gather(): moving = lax.ppermute(moving, axis, [(i, i - way) for i in senders])]
    ppermute x11, starting transfers between devices: 10.3 us -> 12.5 us  [swap(): lax.ppermute(block, axis, [(i, i ^ d) for i in range(lax.axis_size(axis))])]
    pallas_call x2 -> x1, Pallas kernels: 3.49 us -> 2.26 us  [kernel_path(): call(functools.partial(pack_kernel, n_ka, nu_blk), 'pack', (shape_of(bloc...]
    unnamed x42 -> x50, local copies, waits for them, and re-layouts: 2.92 us -> 3.73 us
  transfers between devices with their start and end apart: 20 -> 19, of which waited for: 6 -> 4; matrix products, arithmetic and copies ran while one was open for 1% -> 1% of each run, Pallas kernels for 23% -> 23%
where the time goes in v12:
time: 166 us
  Pallas kernels  59.4 us (36%)
  blocking collectives  47.4 us (29%)
  starting transfers between devices  30 us (18%)
  waiting for transfers between devices  21.3 us (13%)
  local copies, waits for them, and re-layouts  5.89 us (4%)
    all_to_all x4, blocking collectives, exchange_all(): return lax.all_to_all(parts, AXES, split_axis=0, concat_axis=0, tiled=True)  47.4 us
    pallas_call x2, Pallas kernels, kernel_path(): call(functools.partial(direct_kernel, n_ka, tile, scale), 'direct', shape...  26.2 us
    pallas_call x2, Pallas kernels, kernel_path(): call(functools.partial(exchange_kernel, cfg, chunk, scale), 'exchange', m...  13.3 us
    ppermute x11, starting transfers between devices, swap(): lax.ppermute(block, axis, [(i, i ^ d) for i in range(lax.axis_size(axis))])  12.5 us
    ppermute x6, waiting for transfers between devices, line_gather(): moving = lax.ppermute(moving, axis, [(i, i - way) for i in senders])  12.3 us
    all_to_all x2, starting transfers between devices, exchange_all(): return lax.all_to_all(parts, AXES, split_axis=0, concat_axis=0, tiled=True)  9.51 us
    ppermute x11, waiting for transfers between devices, swap(): lax.ppermute(block, axis, [(i, i ^ d) for i in range(lax.axis_size(axis))])  8.96 us
    ppermute x6, starting transfers between devices, line_gather(): moving = lax.ppermute(moving, axis, [(i, i - way) for i in senders])  8.05 us
  transfers between devices with their start and end apart: 19, of which 4 were waited for; matrix products, arithmetic and copies ran while one was open for 1% of the time, Pallas kernels for 23%

profile of v12, /device:TPU:0, one launch (start us, length us, event | category | flops | bytes accessed | tf_op | source)
XLA Modules:
  0.0 165.5 jit_solution(7543672397531396262)
XLA Ops:
  0.6 2.3 %pack.1 = (f32[16,128]{1,0:T(8,128)}, f32[16,128]{1,0:T(8,128)}, bf16[3,8,4224]{2,1,0:T(8,128)(2,1)}, bf16[3,8,4224]{2,1,0:T(8,128)(2,1)}, bf16[3,8,4224]{2,1,0:T(8,128)(2,1)}, /*index=5*/bf16[3,8,4224]{2,1,0:T(8,128)(2,1)}) custom-call(f32[3,512]{1,0:T(4,128)} %refs_0_.1, f32[3,64]{1,0:T(4,128)} %refs_1_.1, f32[3,8]{1,0:T(4,128)} %refs_2_.3, ...), custom_call_target="tpu_custom_call" | custom-call | tf_op jit(solution)/shard_map/pack/pallas_call | solution.py:524
  2.9 3.1 %collective-permute-start = (bf16[3,8,4224]{2,1,0:T(8,128)(2,1)}, bf16[3,8,4224]{2,1,0:T(8,128)(2,1)S(1)}, u32[]{:S(2)}, u32[]{:S(2)}) collective-permute-start(bf16[3,8,4224]{2,1,0:T(8,128)(2,1)} %get-tuple-element.43), channel_id=1, source_target_pairs={{0,8},{8,0},{16,24},{24,16},{1,9},{9,1},{17,25},{25,17},{2,10},{10... | collective-permute-start | bytes 608264 | tf_op jit(solution)/shard_map/ppermute | solution.py:469
  6.0 2.6 %collective-permute-start.1 = (bf16[3,8,4224]{2,1,0:T(8,128)(2,1)}, bf16[3,8,4224]{2,1,0:T(8,128)(2,1)S(1)}, u32[]{:S(2)}, u32[]{:S(2)}) collective-permute-start(bf16[3,8,4224]{2,1,0:T(8,128)(2,1)} %get-tuple-element.44), channel_id=1, source_target_pairs={{0,16},{8,24},{16,0},{24,8},{1,17},{9,25},{17,1},{25,9},{2,18},{10... | collective-permute-start | bytes 608264 | tf_op jit(solution)/shard_map/ppermute | solution.py:469
  8.6 1.2 constant_dynamic-slice_fusion
  9.8 2.8 %collective-permute-start.6 = (bf16[192,1024]{1,0:T(8,128)(2,1)S(1)}, bf16[192,1024]{1,0:T(8,128)(2,1)S(1)}, u32[]{:S(2)}, u32[]{:S(2)}) collective-permute-start(bf16[192,1024]{1,0:T(8,128)(2,1)S(1)} %bitcast.3), channel_id=1, source_target_pairs={{0,8},{8,16},{16,24},{1,9},{9,17},{17,25},{2,10},{10,18},{18,26},{... | collective-permute-start | bytes 1179656 | tf_op jit(solution)/shard_map/ppermute | solution.py:479
  12.6 1.3 collective-permute-start.7
  13.9 0.9 slice.18
  14.8 0.0 collective-permute-done.refs_1_
  14.9 8.9 %collective-permute-done.1.refs_2_ = bf16[3,8,4224]{2,1,0:T(8,128)(2,1)S(1)} collective-permute-done((bf16[3,8,4224]{2,1,0:T(8,128)(2,1)}, bf16[3,8,4224]{2,1,0:T(8,128)(2,1)S(1)}, u32[]{:S(2)}, u32[]{:S(2)}) %collective-permute-start.1) | collective-permute-done | bytes 202784 | tf_op jit(solution)/shard_map/ppermute | solution.py:469
  23.8 0.1 maximum_bitcast_fusion.refs_4_
  23.9 1.6 collective-permute-start.3
  25.5 1.5 collective-permute-start.4
  27.0 0.7 collective-permute-done.6.refs_5_
  27.7 0.7 collective-permute-start.12
  28.4 1.0 collective-permute-done.7.refs_8_
  29.4 1.3 collective-permute-start.13
  30.7 3.7 %turn.1.refs_1_ = bf16[2048,1024]{1,0:T(8,128)(2,1)} custom-call(bf16[1024,2048]{1,0:T(8,128)(2,1)} %scr_ref.1), custom_call_target="tpu_custom_call" | custom-call | bytes 8388608 | tf_op jit(solution)/shard_map/turn/pallas_call | solution.py:550
  34.5 1.6 collective-permute-start.10
  36.1 1.5 collective-permute-start.11
  37.7 0.5 collective-permute-start.9
  38.2 10.6 %collective-permute-done.13.refs_9_ = bf16[192,1024]{1,0:T(8,128)(2,1)S(1)} collective-permute-done((bf16[192,1024]{1,0:T(8,128)(2,1)S(1)}, bf16[192,1024]{1,0:T(8,128)(2,1)S(1)}, u32[]{:S(2)}, u32[]{:S(2)}) %collective-permute-start.13) | collective-permute-done | bytes 393248 | tf_op jit(solution)/shard_map/ppermute | solution.py:479
  48.9 0.1 collective-permute-start.14
  49.0 0.7 collective-permute-start.15
  49.7 1.3 collective-permute-start.16
  51.1 0.7 copy-done.13
  51.8 0.2 copy-done.14
  51.9 0.8 copy-done.15
  52.7 6.1 %order.1 = (bf16[768,2048]{1,0:T(8,128)(2,1)}, bf16[2048,768]{1,0:T(8,128)(2,1)}, bf16[768,256]{1,0:T(8,128)(2,1)}, bf16[768,256]{1,0:T(8,128)(2,1)}, bf16[32,16,128]{2,1,0:T(8,128)(2,1)}) custom-call(bf16[3,8,4224]{2,1,0:T(8,128)(2,1)} %get-tuple-element.42.refs_0_, bf16[3,8,4224]{2,1,0:T(8,128)(2,1)} %copy-done.9, bf16[3,8,4224]{2,1,0:T(8,128)(2,1)} %copy-done.10, ...), custom_call_target="tpu_custom_call" | custom-call | bytes 9437184 | tf_op jit(solution)/shard_map/order/pallas_call | solution.py:565
  58.8 2.2 %density.2 = (bf16[3,256,256]{2,1,0:T(8,128)(2,1)}, f32[32,2,128]{2,1,0:T(2,128)}) custom-call(bf16[32,16,128]{2,1,0:T(8,128)(2,1)} %get-tuple-element.52.refs_0_.msgs_ref, bf16[768,256]{1,0:T(8,128)(2,1)} %get-tuple-element.53.refs_1_.refs_3_, bf16[768,256]{1,0:T(8,128)(2,1)} %get-tuple-element.54.refs_2_.refs_4_), custom_call_target="tpu_custom_call" | custom-call | tf_op jit(solution)/shard_map/density/pallas_call | solution.py:596
  61.0 6.7 %all-to-all-start = ((f32[32,2,128]{2,1,0:T(2,128)}), f32[32,2,128]{2,1,0:T(2,128)S(1)}, u32[]{:S(2)}, u32[]{:S(2)}) async-start(f32[32,2,128]{2,1,0:T(2,128)} %get-tuple-element.55), calls=%async_computation | async-start | bytes 65536 | tf_op jit(solution)/shard_map/all_to_all | solution.py:30
  67.8 0.7 copy-done.23
  68.5 0.1 copy-done.24
  68.6 13.1 %direct.2.refs_1_ = f32[6,128,128]{2,1,0:T(8,128)} custom-call(bf16[2048,768]{1,0:T(8,128)(2,1)} %get-tuple-element.56.refs_0_, bf16[2048,1024]{1,0:T(8,128)(2,1)} %turn.1.refs_1_, bf16[768,2048]{1,0:T(8,128)(2,1)} %get-tuple-element.58.refs_2_, bf16[3,256,256]{2,1,0:T(8,128)(2,1)} %get-tuple-element.59.refs_3_, bf16[192,1024]{1,0:T(8,128)(2,1)} %bitcast.5, ...), custom_call_target="tpu_custom_call" | custom-call | flops 6442450944 | bytes 12582912 | tf_op jit(solution)/shard_map/direct/pallas_call | solution.py:614
  81.7 0.0 copy-start.3
  81.8 0.6 copy-done.18
  82.4 6.7 %exchange.2 = bf16[32,16,128]{2,1,0:T(8,128)(2,1)} custom-call(f32[32,2,128]{2,1,0:T(2,128)} %copy-done.18, f32[6,128,128]{2,1,0:T(8,128)} %direct.2.refs_1_, bf16[256,8192]{1,0:T(8,128)(2,1)} %refs_2_.5, bf16[768,256]{1,0:T(8,128)(2,1)} %get-tuple-element.53.refs_1_.refs_3_, bf16[768,256]{1,0:T(8,128)(2,1)} %get-tuple-element.54.refs_2_.refs_4_), custom_call_target="tpu_custom_call" | custom-call | tf_op jit(solution)/shard_map/exchange/pallas_call | solution.py:637
  89.0 13.9 %all_to_all.30.recv_ref = bf16[32,16,128]{2,1,0:T(8,128)(2,1)S(1)} all-to-all(bf16[32,16,128]{2,1,0:T(8,128)(2,1)} %exchange.2), channel_id=1, replica_groups=mesh['ka'=4,'band'=8] {'ka','band'}, dimensions={0} | all-to-all | bytes 262144 | tf_op jit(solution)/shard_map/all_to_all | solution.py:30
  102.9 0.8 first_owner.1
  103.8 10.6 %all_to_all.31.refs_0_.msgs_ref = bf16[32,16,128]{2,1,0:T(8,128)(2,1)} all-to-all(bf16[32,16,128]{2,1,0:T(8,128)(2,1)S(1)} %get-tuple-element.66), channel_id=1, replica_groups=mesh['ka'=4,'band'=8] {'ka','band'}, dimensions={0} | all-to-all | bytes 262144 | tf_op jit(solution)/shard_map/all_to_all | solution.py:30
  114.4 2.1 %density.3 = (bf16[3,256,256]{2,1,0:T(8,128)(2,1)}, f32[32,2,128]{2,1,0:T(2,128)}) custom-call(bf16[32,16,128]{2,1,0:T(8,128)(2,1)} %all_to_all.31.refs_0_.msgs_ref, bf16[768,256]{1,0:T(8,128)(2,1)} %get-tuple-element.53.refs_1_.refs_3_, bf16[768,256]{1,0:T(8,128)(2,1)} %get-tuple-element.54.refs_2_.refs_4_), custom_call_target="tpu_custom_call" | custom-call | tf_op jit(solution)/shard_map/density/pallas_call | solution.py:596
  116.5 2.8 %all-to-all-start.3 = ((f32[32,2,128]{2,1,0:T(2,128)}), f32[32,2,128]{2,1,0:T(2,128)S(1)}, u32[]{:S(2)}, u32[]{:S(2)}) async-start(f32[32,2,128]{2,1,0:T(2,128)} %get-tuple-element.67), calls=%async_computation.3 | async-start | bytes 65536 | tf_op jit(solution)/shard_map/all_to_all | solution.py:30
  119.4 13.1 %direct.3.refs_1_ = f32[6,128,128]{2,1,0:T(8,128)} custom-call(bf16[2048,768]{1,0:T(8,128)(2,1)} %get-tuple-element.56.refs_0_, bf16[2048,1024]{1,0:T(8,128)(2,1)} %turn.1.refs_1_, bf16[768,2048]{1,0:T(8,128)(2,1)} %get-tuple-element.58.refs_2_, bf16[3,256,256]{2,1,0:T(8,128)(2,1)} %get-tuple-element.68.refs_3_, bf16[192,1024]{1,0:T(8,128)(2,1)} %bitcast.6, ...), custom_call_target="tpu_custom_call" | custom-call | flops 6442450944 | bytes 12582912 | tf_op jit(solution)/shard_map/direct/pallas_call | solution.py:614
  132.5 0.6 copy-done.17
  133.1 6.6 %exchange.3 = bf16[32,16,128]{2,1,0:T(8,128)(2,1)} custom-call(f32[32,2,128]{2,1,0:T(2,128)} %copy-done.17, f32[6,128,128]{2,1,0:T(8,128)} %direct.3.refs_1_, bf16[256,8192]{1,0:T(8,128)(2,1)} %refs_2_.5, bf16[768,256]{1,0:T(8,128)(2,1)} %get-tuple-element.53.refs_1_.refs_3_, bf16[768,256]{1,0:T(8,128)(2,1)} %get-tuple-element.54.refs_2_.refs_4_), custom_call_target="tpu_custom_call" | custom-call | tf_op jit(solution)/shard_map/exchange/pallas_call | solution.py:637
  139.7 13.9 %all_to_all.32.recv_ref = bf16[32,16,128]{2,1,0:T(8,128)(2,1)S(1)} all-to-all(bf16[32,16,128]{2,1,0:T(8,128)(2,1)} %exchange.3), channel_id=1, replica_groups=mesh['ka'=4,'band'=8] {'ka','band'}, dimensions={0} | all-to-all | bytes 262144 | tf_op jit(solution)/shard_map/all_to_all | solution.py:30
  153.6 1.3 second_owner.1
  155.0 9.0 %all_to_all.33.msgs_ref = f32[32,2,128]{2,1,0:T(2,128)S(1)} all-to-all(f32[32,2,128]{2,1,0:T(2,128)S(1)} %get-tuple-element.71), channel_id=1, replica_groups=mesh['ka'=4,'band'=8] {'ka','band'}, dimensions={0} | all-to-all | bytes 65536 | tf_op jit(solution)/shard_map/all_to_all | solution.py:30
  164.0 1.3 finish.1
  (65 shorter events, 0.2 us)
Async XLA Ops:
  2.9 11.9 %collective-permute-start = (bf16[3,8,4224]{2,1,0:T(8,128)(2,1)}, bf16[3,8,4224]{2,1,0:T(8,128)(2,1)S(1)}, u32[]{:S(2)}, u32[]{:S(2)}) collective-permute-start(bf16[3,8,4224]{2,1,0:T(8,128)(2,1)} %get-tuple-element.43), channel_id=1, source_target_pairs={{0,8},{8,0},{16,24},{24,16},{1,9},{9,1},{17,25},{25,17},{2,10},{10... | collective-permute-start | bytes 608264 | tf_op jit(solution)/shard_map/ppermute | solution.py:469
  6.0 17.8 %collective-permute-start.1 = (bf16[3,8,4224]{2,1,0:T(8,128)(2,1)}, bf16[3,8,4224]{2,1,0:T(8,128)(2,1)S(1)}, u32[]{:S(2)}, u32[]{:S(2)}) collective-permute-start(bf16[3,8,4224]{2,1,0:T(8,128)(2,1)} %get-tuple-element.44), channel_id=1, source_target_pairs={{0,16},{8,24},{16,0},{24,8},{1,17},{9,25},{17,1},{25,9},{2,18},{10... | collective-permute-start | bytes 608264 | tf_op jit(solution)/shard_map/ppermute | solution.py:469
  8.6 15.2 %collective-permute-start.2 = (bf16[3,8,4224]{2,1,0:T(8,128)(2,1)}, bf16[3,8,4224]{2,1,0:T(8,128)(2,1)S(1)}, u32[]{:S(2)}, u32[]{:S(2)}) collective-permute-start(bf16[3,8,4224]{2,1,0:T(8,128)(2,1)} %get-tuple-element.45), channel_id=1, source_target_pairs={{0,24},{8,16},{16,8},{24,0},{1,25},{9,17},{17,9},{25,1},{2,26},{10... | collective-permute-start | bytes 608264 | tf_op jit(solution)/shard_map/ppermute | solution.py:469
  9.8 24.6 %copy-start.16 = (bf16[3,64,1024]{2,1,0:T(8,128)(2,1)}, bf16[3,64,1024]{2,1,0:T(8,128)(2,1)S(1)}, u32[]{:S(2)}) copy-start(bf16[3,64,1024]{2,1,0:T(8,128)(2,1)S(1)} %constant_dynamic-slice_fusion) | copy-start | bytes 1179652
  9.8 17.9 %collective-permute-start.6 = (bf16[192,1024]{1,0:T(8,128)(2,1)S(1)}, bf16[192,1024]{1,0:T(8,128)(2,1)S(1)}, u32[]{:S(2)}, u32[]{:S(2)}) collective-permute-start(bf16[192,1024]{1,0:T(8,128)(2,1)S(1)} %bitcast.3), channel_id=1, source_target_pairs={{0,8},{8,16},{16,24},{1,9},{9,17},{17,25},{2,10},{10,18},{18,26},{... | collective-permute-start | bytes 1179656 | tf_op jit(solution)/shard_map/ppermute | solution.py:479
  12.6 16.7 %collective-permute-start.7 = (bf16[192,1024]{1,0:T(8,128)(2,1)S(1)}, bf16[192,1024]{1,0:T(8,128)(2,1)S(1)}, u32[]{:S(2)}, u32[]{:S(2)}) collective-permute-start(bf16[192,1024]{1,0:T(8,128)(2,1)S(1)} %bitcast.4), channel_id=1, source_target_pairs={{8,0},{16,8},{24,16},{9,1},{17,9},{25,17},{10,2},{18,10},{26,18},{... | collective-permute-start | bytes 1179656 | tf_op jit(solution)/shard_map/ppermute | solution.py:479
  14.8 19.5 %copy-start.9 = (bf16[3,8,4224]{2,1,0:T(8,128)(2,1)}, bf16[3,8,4224]{2,1,0:T(8,128)(2,1)S(1)}, u32[]{:S(2)}) copy-start(bf16[3,8,4224]{2,1,0:T(8,128)(2,1)S(1)} %collective-permute-done.refs_1_) | copy-start | bytes 608260
  23.8 10.6 %copy-start.10 = (bf16[3,8,4224]{2,1,0:T(8,128)(2,1)}, bf16[3,8,4224]{2,1,0:T(8,128)(2,1)S(1)}, u32[]{:S(2)}) copy-start(bf16[3,8,4224]{2,1,0:T(8,128)(2,1)S(1)} %collective-permute-done.1.refs_2_) | copy-start | bytes 608260
  23.8 10.6 %copy-start.11 = (bf16[3,8,4224]{2,1,0:T(8,128)(2,1)}, bf16[3,8,4224]{2,1,0:T(8,128)(2,1)S(1)}, u32[]{:S(2)}) copy-start(bf16[3,8,4224]{2,1,0:T(8,128)(2,1)S(1)} %collective-permute-done.2.refs_3_) | copy-start | bytes 608260
  23.9 10.5 %copy-start.4 = (bf16[96,2176]{1,0:T(8,128)(2,1)}, bf16[96,2176]{1,0:T(8,128)(2,1)S(1)}, u32[]{:S(2)}) copy-start(bf16[96,2176]{1,0:T(8,128)(2,1)S(1)} %maximum_bitcast_fusion.refs_4_) | copy-start | bytes 1253380
  23.9 10.5 %collective-permute-start.3 = (bf16[96,2176]{1,0:T(8,128)(2,1)S(1)}, bf16[96,2176]{1,0:T(8,128)(2,1)S(1)}, u32[]{:S(2)}, u32[]{:S(2)}) collective-permute-start(bf16[96,2176]{1,0:T(8,128)(2,1)S(1)} %maximum_bitcast_fusion.refs_4_), channel_id=1, source_target_pairs={{0,2},{1,3},{2,0},{3,1},{4,6},{5,7},{6,4},{7,5},{8,10},{9,11},{10,... | collective-permute-start | bytes 1253384 | tf_op jit(solution)/shard_map/ppermute | solution.py:469
  25.5 9.0 %collective-permute-start.4 = (bf16[96,2176]{1,0:T(8,128)(2,1)S(1)}, bf16[96,2176]{1,0:T(8,128)(2,1)S(1)}, u32[]{:S(2)}, u32[]{:S(2)}) collective-permute-start(bf16[96,2176]{1,0:T(8,128)(2,1)S(1)} %maximum_bitcast_fusion.refs_4_), channel_id=1, source_target_pairs={{0,4},{1,5},{2,6},{3,7},{4,0},{5,1},{6,2},{7,3},{8,12},{9,13},{10,... | collective-permute-start | bytes 1253384 | tf_op jit(solution)/shard_map/ppermute | solution.py:469
  27.0 7.5 %collective-permute-start.5 = (bf16[96,2176]{1,0:T(8,128)(2,1)S(1)}, bf16[96,2176]{1,0:T(8,128)(2,1)S(1)}, u32[]{:S(2)}, u32[]{:S(2)}) collective-permute-start(bf16[96,2176]{1,0:T(8,128)(2,1)S(1)} %maximum_bitcast_fusion.refs_4_), channel_id=1, source_target_pairs={{0,1},{1,0},{2,3},{3,2},{4,5},{5,4},{6,7},{7,6},{8,9},{9,8},{10,11... | collective-permute-start | bytes 1253384 | tf_op jit(solution)/shard_map/ppermute | solution.py:469
  27.7 6.7 %copy-start.19 = (bf16[192,1024]{1,0:T(8,128)(2,1)}, bf16[192,1024]{1,0:T(8,128)(2,1)S(1)}, u32[]{:S(2)}) copy-start(bf16[192,1024]{1,0:T(8,128)(2,1)S(1)} %collective-permute-done.6.refs_5_) | copy-start | bytes 1179652
  27.7 10.0 %collective-permute-start.12 = (bf16[192,1024]{1,0:T(8,128)(2,1)S(1)}, bf16[192,1024]{1,0:T(8,128)(2,1)S(1)}, u32[]{:S(2)}, u32[]{:S(2)}) collective-permute-start(bf16[192,1024]{1,0:T(8,128)(2,1)S(1)} %collective-permute-done.6.refs_5_), channel_id=1, source_target_pairs={{8,16},{16,24},{9,17},{17,25},{10,18},{18,26},{11,19},{19,27},{12,... | collective-permute-start | bytes 1179656 | tf_op jit(solution)/shard_map/ppermute | solution.py:479
  29.4 5.0 %copy-start.20 = (bf16[192,1024]{1,0:T(8,128)(2,1)}, bf16[192,1024]{1,0:T(8,128)(2,1)S(1)}, u32[]{:S(2)}) copy-start(bf16[192,1024]{1,0:T(8,128)(2,1)S(1)} %collective-permute-done.7.refs_8_) | copy-start | bytes 1179652
  29.4 19.5 %collective-permute-start.13 = (bf16[192,1024]{1,0:T(8,128)(2,1)S(1)}, bf16[192,1024]{1,0:T(8,128)(2,1)S(1)}, u32[]{:S(2)}, u32[]{:S(2)}) collective-permute-start(bf16[192,1024]{1,0:T(8,128)(2,1)S(1)} %collective-permute-done.7.refs_8_), channel_id=1, source_target_pairs={{8,0},{16,8},{9,1},{17,9},{10,2},{18,10},{11,3},{19,11},{12,4},{20... | collective-permute-start | bytes 1179656 | tf_op jit(solution)/shard_map/ppermute | solution.py:479
  34.4 16.6 %copy-start.5 = (bf16[96,2176]{1,0:T(8,128)(2,1)}, bf16[96,2176]{1,0:T(8,128)(2,1)S(1)}, u32[]{:S(2)}) copy-start(bf16[96,2176]{1,0:T(8,128)(2,1)S(1)} %collective-permute-done.3.refs_6_) | copy-start | bytes 1253380
  34.5 16.6 %copy-start.6 = (bf16[96,2176]{1,0:T(8,128)(2,1)}, bf16[96,2176]{1,0:T(8,128)(2,1)S(1)}, u32[]{:S(2)}) copy-start(bf16[96,2176]{1,0:T(8,128)(2,1)S(1)} %collective-permute-done.4.refs_8_) | copy-start | bytes 1253380
  34.5 16.6 %copy-start.12 = (bf16[96,2176]{1,0:T(8,128)(2,1)}, bf16[96,2176]{1,0:T(8,128)(2,1)S(1)}, u32[]{:S(2)}) copy-start(bf16[96,2176]{1,0:T(8,128)(2,1)S(1)} %collective-permute-done.5.refs_5_) | copy-start | bytes 1253380
  34.5 14.3 %collective-permute-start.10 = (bf16[48,2176]{1,0:T(8,128)(2,1)S(1)}, bf16[48,2176]{1,0:T(8,128)(2,1)S(1)}, u32[]{:S(2)}, u32[]{:S(2)}) collective-permute-start(bf16[48,2176]{1,0:T(8,128)(2,1)S(1)} %slice.22), channel_id=1, source_target_pairs={{0,4},{1,5},{2,6},{3,7},{4,0},{5,1},{6,2},{7,3},{8,12},{9,13},{10,... | collective-permute-start | bytes 626696 | tf_op jit(solution)/shard_map/ppermute | solution.py:469
  36.1 12.7 %collective-permute-start.11 = (bf16[48,2176]{1,0:T(8,128)(2,1)S(1)}, bf16[48,2176]{1,0:T(8,128)(2,1)S(1)}, u32[]{:S(2)}, u32[]{:S(2)}) collective-permute-start(bf16[48,2176]{1,0:T(8,128)(2,1)S(1)} %slice.23), channel_id=1, source_target_pairs={{0,2},{1,3},{2,0},{3,1},{4,6},{5,7},{6,4},{7,5},{8,10},{9,11},{10,... | collective-permute-start | bytes 626696 | tf_op jit(solution)/shard_map/ppermute | solution.py:469
  37.7 13.3 %collective-permute-start.8 = (bf16[96,2176]{1,0:T(8,128)(2,1)S(1)}, bf16[96,2176]{1,0:T(8,128)(2,1)S(1)}, u32[]{:S(2)}, u32[]{:S(2)}) collective-permute-start(bf16[96,2176]{1,0:T(8,128)(2,1)S(1)} %collective-permute-done.3.refs_6_), channel_id=1, source_target_pairs={{0,1},{1,0},{2,3},{3,2},{4,5},{5,4},{6,7},{7,6},{8,9},{9,8},{10,11... | collective-permute-start | bytes 1253384 | tf_op jit(solution)/shard_map/ppermute | solution.py:469
  37.7 30.1 %copy-start.21 = (bf16[192,1024]{1,0:T(8,128)(2,1)}, bf16[192,1024]{1,0:T(8,128)(2,1)S(1)}, u32[]{:S(2)}) copy-start(bf16[192,1024]{1,0:T(8,128)(2,1)S(1)} %collective-permute-done.12.refs_6_) | copy-start | bytes 1179652
  37.7 13.3 %collective-permute-start.9 = (bf16[96,2176]{1,0:T(8,128)(2,1)S(1)}, bf16[96,2176]{1,0:T(8,128)(2,1)S(1)}, u32[]{:S(2)}, u32[]{:S(2)}) collective-permute-start(bf16[96,2176]{1,0:T(8,128)(2,1)S(1)} %collective-permute-done.4.refs_8_), channel_id=1, source_target_pairs={{0,1},{1,0},{2,3},{3,2},{4,5},{5,4},{6,7},{7,6},{8,9},{9,8},{10,11... | collective-permute-start | bytes 1253384 | tf_op jit(solution)/shard_map/ppermute | solution.py:469
  48.8 18.9 %copy-start.22 = (bf16[192,1024]{1,0:T(8,128)(2,1)}, bf16[192,1024]{1,0:T(8,128)(2,1)S(1)}, u32[]{:S(2)}) copy-start(bf16[192,1024]{1,0:T(8,128)(2,1)S(1)} %collective-permute-done.13.refs_9_) | copy-start | bytes 1179652
  48.8 2.2 %copy-start.7 = (bf16[48,2176]{1,0:T(8,128)(2,1)}, bf16[48,2176]{1,0:T(8,128)(2,1)S(1)}, u32[]{:S(2)}) copy-start(bf16[48,2176]{1,0:T(8,128)(2,1)S(1)} %collective-permute-done.10.refs_10_) | copy-start | bytes 626692
  48.8 2.2 %copy-start.8 = (bf16[48,2176]{1,0:T(8,128)(2,1)}, bf16[48,2176]{1,0:T(8,128)(2,1)S(1)}, u32[]{:S(2)}) copy-start(bf16[48,2176]{1,0:T(8,128)(2,1)S(1)} %collective-permute-done.11.refs_11_) | copy-start | bytes 626692
  48.9 2.1 %collective-permute-start.14 = (bf16[96,2176]{1,0:T(8,128)(2,1)S(1)}, bf16[96,2176]{1,0:T(8,128)(2,1)S(1)}, u32[]{:S(2)}, u32[]{:S(2)}) collective-permute-start(bf16[96,2176]{1,0:T(8,128)(2,1)S(1)} %pad_maximum_fusion), channel_id=1, source_target_pairs={{0,1},{1,0},{2,3},{3,2},{4,5},{5,4},{6,7},{7,6},{8,9},{9,8},{10,11... | collective-permute-start | bytes 1253384 | tf_op jit(solution)/shard_map/ppermute | solution.py:469
  49.0 18.7 %collective-permute-start.15 = (bf16[192,1024]{1,0:T(8,128)(2,1)S(1)}, bf16[192,1024]{1,0:T(8,128)(2,1)S(1)}, u32[]{:S(2)}, u32[]{:S(2)}) collective-permute-start(bf16[192,1024]{1,0:T(8,128)(2,1)S(1)} %collective-permute-done.12.refs_6_), channel_id=1, source_target_pairs={{16,24},{17,25},{18,26},{19,27},{20,28},{21,29},{22,30},{23,31}} | collective-permute-start | bytes 1179656 | tf_op jit(solution)/shard_map/ppermute | solution.py:479
  49.7 18.1 %collective-permute-start.16 = (bf16[192,1024]{1,0:T(8,128)(2,1)S(1)}, bf16[192,1024]{1,0:T(8,128)(2,1)S(1)}, u32[]{:S(2)}, u32[]{:S(2)}) collective-permute-start(bf16[192,1024]{1,0:T(8,128)(2,1)S(1)} %collective-permute-done.13.refs_9_), channel_id=1, source_target_pairs={{8,0},{9,1},{10,2},{11,3},{12,4},{13,5},{14,6},{15,7}} | collective-permute-start | bytes 1179656 | tf_op jit(solution)/shard_map/ppermute | solution.py:479
  51.0 0.8 copy-start.13
  51.0 1.0 copy-start.14
  51.9 0.8 copy-start.15
  61.0 20.8 %all-to-all-start = ((f32[32,2,128]{2,1,0:T(2,128)}), f32[32,2,128]{2,1,0:T(2,128)S(1)}, u32[]{:S(2)}, u32[]{:S(2)}) async-start(f32[32,2,128]{2,1,0:T(2,128)} %get-tuple-element.55), calls=%async_computation | async-start | bytes 65536 | tf_op jit(solution)/shard_map/all_to_all | solution.py:30
  67.7 0.7 copy-start.23
  67.7 0.8 copy-start.24
  81.7 21.2 %copy-start.1 = (bf16[32,16,128]{2,1,0:T(8,128)(2,1)S(1)}, bf16[32,16,128]{2,1,0:T(8,128)(2,1)}, u32[]{:S(2)}) copy-start(bf16[32,16,128]{2,1,0:T(8,128)(2,1)} %get-tuple-element.52.refs_0_.msgs_ref) | copy-start | bytes 393220
  81.7 21.2 %copy-start.2 = (f32[16,128]{1,0:T(8,128)S(1)}, f32[16,128]{1,0:T(8,128)}, u32[]{:S(2)}) copy-start(f32[16,128]{1,0:T(8,128)} %get-tuple-element.64.gap_ref) | copy-start | bytes 24580
  81.7 21.2 %copy-start.3 = (f32[16,128]{1,0:T(8,128)S(1)}, f32[16,128]{1,0:T(8,128)}, u32[]{:S(2)}) copy-start(f32[16,128]{1,0:T(8,128)} %get-tuple-element.65.own_ref) | copy-start | bytes 24580
  81.8 0.6 copy-start.18
  116.5 15.9 %all-to-all-start.3 = ((f32[32,2,128]{2,1,0:T(2,128)}), f32[32,2,128]{2,1,0:T(2,128)S(1)}, u32[]{:S(2)}, u32[]{:S(2)}) async-start(f32[32,2,128]{2,1,0:T(2,128)} %get-tuple-element.67), calls=%async_computation.3 | async-start | bytes 65536 | tf_op jit(solution)/shard_map/all_to_all | solution.py:30
  132.5 21.1 %copy-start = (bf16[32,16,128]{2,1,0:T(8,128)(2,1)S(1)}, bf16[32,16,128]{2,1,0:T(8,128)(2,1)}, u32[]{:S(2)}) copy-start(bf16[32,16,128]{2,1,0:T(8,128)(2,1)} %all_to_all.31.refs_0_.msgs_ref) | copy-start | bytes 393220
  132.5 0.6 copy-start.17

commit v13 on v12

--- a/solution.py
+++ b/solution.py
@@ -292,11 +292,14 @@
     row_copy = pltpu.make_async_copy(rows_ref, vals, row_sem.at[0])
     start_all([qx_copy, turned_copies[0]])
     each_cond(lambda copy: copy.start())
+    scr_copies[0].start()
+    for i in range(1, nu // tile):
+        start_all([turned_copies[i], scr_copies[i]])
+    row_copy.start()
     qx_copy.wait()
     for i in range(nu // tile):
         rows = slice(i * tile, (i + 1) * tile)
         turned_copies[i].wait()
-        scr_copies[i].start()
         for kq in range(qx.shape[0]):
             cols = slice(kq * quad, (kq + 1) * quad)
             mixed[rows, cols] = jnp.dot(
@@ -305,7 +308,6 @@
         if i == 0:
             each_cond(lambda copy: copy.wait())
             cond_rows = conds[...].reshape(-1, mu)
-        start_all(turned_copies[i + 1 : i + 2] or [row_copy])
         scr_copies[i].wait()
         amp = jnp.dot(mixed[rows, :], cond_rows, preferred_element_type=F32)
         kern[rows, :] = (scrs[rows, :].astype(F32) * amp * scale).astype(BF)
@@ -334,16 +336,12 @@
         pltpu.make_async_copy(di_ref, di, sems.at[2]),
         pltpu.make_async_copy(cond_ref, conds, sems.at[3]),
     ]
-    ahead = 2
-    start_all([rho_copy] + coul_copies[:ahead])
+    start_all([rho_copy] + coul_copies + copies)
     rho_copy.wait()
     acc = jnp.zeros((own, LANES), F32)
     per_dev = own // LANES
     for i in range(npt // chunk):
         coul_copies[i].wait()
-        start_all(coul_copies[i + ahead : i + ahead + 1])
-        if i + ahead == npt // chunk:
-            start_all(copies)
         for j in range(i * chunk // LANES, (i + 1) * chunk // LANES):
             rho = rhos[j // per_dev, pl.ds(j % per_dev, 1), :].astype(BF).astype(F32)
             acc = acc + coul[:, j * LANES : (j + 1) * LANES].astype(F32) * rho
@@ -471,33 +469,51 @@
 
 def line_gather(block, axis):
     n = lax.axis_size(axis)
-    flows = []
-    for way in (-1, 1):
+    flows = [[], []]
+    for hop in range(3, n):
+        up = [(i, i + hop) for i in range(n - hop)]
+        down = [(i, j) for j, i in up]
+        if hop == n - 1:
+            both = lax.ppermute(block, axis, up + down)
+            block, both = lax.optimization_barrier((block, both))
+            far = (both, both)
+        else:
+            far = (lax.ppermute(block, axis, up), lax.ppermute(block, axis, down))
+        for flow, part in zip(flows, far):
+            flow.append(part)
+    for side, way in enumerate((-1, 1)):
         moving, flow = block, []
-        for hop in range(1, n):
+        for hop in range(1, min(n, 3)):
             senders = [i for i in range(n) if 0 <= i + way * (hop - 1) < n and 0 <= i - way < n]
             moving = lax.ppermute(moving, axis, [(i, i - way) for i in senders])
             flow.append(moving)
-        flows.append(flow)
+        flows[side] = flow + flows[side]
     return flows
 
 
-def plane_pieces(own_piece, others, later):
+def plane_pieces(own_piece, others):
     def move(block, d):
         return swap(block, "band", d)
 
     rows = own_piece.shape[0]
     half = rows // 2
-    by_x, by_y, core = move(own_piece, 2), move(own_piece, 4), move(own_piece, 1)
-    by_x, by_y, core, others = lax.optimization_barrier((by_x, by_y, core, others))
+    by_x, by_y = move(own_piece, 2), move(own_piece, 4)
+    by_x, by_y, others = lax.optimization_barrier((by_x, by_y, others))
     diag = [move(by_x[:half], 4), move(by_y[half:], 2)]
-    near_x, near_y = move(by_x, 1), move(by_y, 1)
-    diag, later = lax.optimization_barrier((diag, later))
+    near = move(jnp.concatenate([own_piece, by_x, by_y], axis=0), 1)
     far = move(jnp.concatenate(diag, axis=0), 1)
-    arrays = [own_piece, core, by_x, near_x, by_y, near_y, diag[0], diag[1], far]
-    parts = tuple(((i, 0, rows),) for i in range(6))
-    parts += (((6, 0, half), (7, 0, half)), ((8, 0, rows),))
-    return arrays, parts, others, later
+    arrays = [own_piece, near, by_x, by_y, diag[0], diag[1], far]
+    parts = (
+        ((0, 0, rows),),
+        ((1, 0, rows),),
+        ((2, 0, rows),),
+        ((1, rows, rows),),
+        ((3, 0, rows),),
+        ((1, 2 * rows, rows),),
+        ((4, 0, half), (5, 0, half)),
+        ((6, 0, rows),),
+    )
+    return arrays, parts, others
 
 
 def kernel_path(start_vec, val_energy, cond_energy, val_orb, cond_orb, coulomb, screened):
@@ -557,11 +573,9 @@
         + [dma(2 * nu_blk // tile)] * 2,
         moved=8 * MIB,
     )(screened)
-    pieces, parts, others, later = plane_pieces(
-        val_cut, (scr_turned, below[0], above[0]), (below[1:-1], above[1:-1])
+    pieces, parts, (scr_turned, below[0], above[0]) = plane_pieces(
+        val_cut, (scr_turned, below[0], above[0])
     )
-    scr_turned, below[0], above[0] = others
-    below[1:-1], above[1:-1] = later
     val_rows, val_turned, val_own, cond_own, msgs = call(
         functools.partial(order_kernel, parts, n_ka),
         "order",
@@ -587,6 +601,7 @@
         moved=9 * MIB,
     )(*got, *pieces)
 
+    msgs, below, above = lax.optimization_barrier((msgs, below, above))
     cond_pts = [cond_local] + below + above
     cfg = (n_ka, n_band, k_dev)
     quads = k_points // 4

time: 166 us -> 172 us (1.036)
  waiting for transfers between devices: 21.3 us -> 33.3 us
  Pallas kernels: 59.4 us -> 53 us
    ppermute x11 -> x9, waiting for transfers between devices: 8.96 us -> 22.5 us  [swap(): lax.ppermute(block, axis, [(i, i ^ d) for i in range(lax.axis_size(axis))])]
    ppermute x0 -> x1, starting transfers between devices: none -> 5.73 us  [line_gather(): both = lax.ppermute(block, axis, up + down)]
    pallas_call x2, Pallas kernels: 13.3 us -> 7.8 us  [kernel_path(): call(functools.partial(exchange_kernel, cfg, chunk, scale), 'exchange', m...]
    all_to_all x2, starting transfers between devices: 9.51 us -> 5.97 us  [exchange_all(): return lax.all_to_all(parts, AXES, split_axis=0, concat_axis=0, tiled=True)]
    ppermute x11 -> x9, starting transfers between devices: 12.5 us -> 10 us  [swap(): lax.ppermute(block, axis, [(i, i ^ d) for i in range(lax.axis_size(axis))])]
    ppermute x6 -> x4, waiting for transfers between devices: 12.3 us -> 10.8 us  [line_gather(): moving = lax.ppermute(moving, axis, [(i, i - way) for i in senders])]
    unnamed x50 -> x44, local copies, waits for them, and re-layouts: 3.73 us -> 2.99 us
    ppermute x6 -> x4, starting transfers between devices: 8.05 us -> 8.64 us  [line_gather(): moving = lax.ppermute(moving, axis, [(i, i - way) for i in senders])]
  transfers between devices with their start and end apart: 19 -> 16, of which waited for: 4 -> 6; matrix products, arithmetic and copies ran while one was open for 1% -> 1% of each run, Pallas kernels for 23% -> 20%
where the time goes in v13:
time: 172 us; the launch traced here: 171 us
  Pallas kernels  53 us (31%)
  blocking collectives  47.9 us (28%)
  waiting for transfers between devices  33.3 us (19%)
  starting transfers between devices  30.3 us (18%)
  local copies, waits for them, and re-layouts  5.15 us (3%)
    all_to_all x4, blocking collectives, exchange_all(): return lax.all_to_all(parts, AXES, split_axis=0, concat_axis=0, tiled=True)  47.9 us
    pallas_call x2, Pallas kernels, kernel_path(): call(functools.partial(direct_kernel, n_ka, tile, scale), 'direct', shape...  25.1 us
    ppermute x9, waiting for transfers between devices, swap(): lax.ppermute(block, axis, [(i, i ^ d) for i in range(lax.axis_size(axis))])  22.5 us
    ppermute x4, waiting for transfers between devices, line_gather(): moving = lax.ppermute(moving, axis, [(i, i - way) for i in senders])  10.8 us
    ppermute x9, starting transfers between devices, swap(): lax.ppermute(block, axis, [(i, i ^ d) for i in range(lax.axis_size(axis))])  10 us
    ppermute x4, starting transfers between devices, line_gather(): moving = lax.ppermute(moving, axis, [(i, i - way) for i in senders])  8.64 us
    pallas_call x2, Pallas kernels, kernel_path(): call(functools.partial(exchange_kernel, cfg, chunk, scale), 'exchange', m...  7.8 us
    pallas_call x1, Pallas kernels, kernel_path(): call(functools.partial(order_kernel, parts, n_ka), 'order', (shape_of((ro...  6.2 us
  transfers between devices with their start and end apart: 16, of which 6 were waited for; matrix products, arithmetic and copies ran while one was open for 1% of the time, Pallas kernels for 20%

profile of v13, /device:TPU:0, one launch (start us, length us, event | category | flops | bytes accessed | tf_op | source)
XLA Modules:
  0.0 171.2 jit_solution(2191759191895160912)
XLA Ops:
  0.6 2.2 %pack.1 = (f32[16,128]{1,0:T(8,128)}, f32[16,128]{1,0:T(8,128)}, bf16[3,8,4224]{2,1,0:T(8,128)(2,1)}, bf16[3,8,4224]{2,1,0:T(8,128)(2,1)}, bf16[3,8,4224]{2,1,0:T(8,128)(2,1)}, /*index=5*/bf16[3,8,4224]{2,1,0:T(8,128)(2,1)}) custom-call(f32[3,512]{1,0:T(4,128)} %refs_0_.1, f32[3,64]{1,0:T(4,128)} %refs_1_.1, f32[3,8]{1,0:T(4,128)} %refs_2_.3, ...), custom_call_target="tpu_custom_call" | custom-call | tf_op jit(solution)/shard_map/pack/pallas_call | solution.py:540
  2.9 3.1 %collective-permute-start = (bf16[3,8,4224]{2,1,0:T(8,128)(2,1)}, bf16[3,8,4224]{2,1,0:T(8,128)(2,1)S(1)}, u32[]{:S(2)}, u32[]{:S(2)}) collective-permute-start(bf16[3,8,4224]{2,1,0:T(8,128)(2,1)} %get-tuple-element.47), channel_id=1, source_target_pairs={{0,8},{8,0},{16,24},{24,16},{1,9},{9,1},{17,25},{25,17},{2,10},{10... | collective-permute-start | bytes 608264 | tf_op jit(solution)/shard_map/ppermute | solution.py:467
  6.0 2.6 %collective-permute-start.1 = (bf16[3,8,4224]{2,1,0:T(8,128)(2,1)}, bf16[3,8,4224]{2,1,0:T(8,128)(2,1)S(1)}, u32[]{:S(2)}, u32[]{:S(2)}) collective-permute-start(bf16[3,8,4224]{2,1,0:T(8,128)(2,1)} %get-tuple-element.48), channel_id=1, source_target_pairs={{0,16},{8,24},{16,0},{24,8},{1,17},{9,25},{17,1},{25,9},{2,18},{10... | collective-permute-start | bytes 608264 | tf_op jit(solution)/shard_map/ppermute | solution.py:467
  8.6 0.0 collective-permute-start.2
  8.6 1.2 constant_dynamic-slice_fusion
  9.8 5.7 %collective-permute-start.5 = (bf16[192,1024]{1,0:T(8,128)(2,1)S(1)}, bf16[192,1024]{1,0:T(8,128)(2,1)S(1)}, u32[]{:S(2)}, u32[]{:S(2)}) collective-permute-start(bf16[192,1024]{1,0:T(8,128)(2,1)S(1)} %bitcast.3), channel_id=1, source_target_pairs={{0,24},{24,0},{1,25},{25,1},{2,26},{26,2},{3,27},{27,3},{4,28},{28... | collective-permute-start | bytes 1179656 | tf_op jit(solution)/shard_map/ppermute | solution.py:477
  15.5 0.9 slice.18
  16.5 15.7 %collective-permute-done.1.refs_2_ = bf16[3,8,4224]{2,1,0:T(8,128)(2,1)S(1)} collective-permute-done((bf16[3,8,4224]{2,1,0:T(8,128)(2,1)}, bf16[3,8,4224]{2,1,0:T(8,128)(2,1)S(1)}, u32[]{:S(2)}, u32[]{:S(2)}) %collective-permute-start.1) | collective-permute-done | bytes 202784 | tf_op jit(solution)/shard_map/ppermute | solution.py:467
  32.2 0.0 collective-permute-done.2.refs_3_
  32.2 0.1 maximum_bitcast_fusion.refs_4_
  32.3 1.6 collective-permute-start.3
  33.9 1.5 collective-permute-start.4
  35.4 5.4 %collective-permute-start.6 = (bf16[192,1024]{1,0:T(8,128)(2,1)S(1)}, bf16[192,1024]{1,0:T(8,128)(2,1)S(1)}, u32[]{:S(2)}, u32[]{:S(2)}) collective-permute-start(bf16[192,1024]{1,0:T(8,128)(2,1)S(1)} %bitcast.4), channel_id=1, source_target_pairs={{0,8},{8,16},{16,24},{1,9},{9,17},{17,25},{2,10},{10,18},{18,26},{... | collective-permute-start | bytes 1179656 | tf_op jit(solution)/shard_map/ppermute | solution.py:488
  40.8 1.3 collective-permute-start.7
  42.1 3.7 %turn.1.refs_1_ = bf16[2048,1024]{1,0:T(8,128)(2,1)} custom-call(bf16[1024,2048]{1,0:T(8,128)(2,1)} %scr_ref.1), custom_call_target="tpu_custom_call" | custom-call | bytes 8388608 | tf_op jit(solution)/shard_map/turn/pallas_call | solution.py:566
  45.8 1.5 collective-permute-done.6.refs_5_
  47.4 4.1 %collective-permute-done.7.refs_8_ = bf16[192,1024]{1,0:T(8,128)(2,1)S(1)} collective-permute-done((bf16[192,1024]{1,0:T(8,128)(2,1)S(1)}, bf16[192,1024]{1,0:T(8,128)(2,1)S(1)}, u32[]{:S(2)}, u32[]{:S(2)}) %collective-permute-start.7) | collective-permute-done | bytes 393248 | tf_op jit(solution)/shard_map/ppermute | solution.py:488
  51.5 0.1 pad_maximum_fusion
  51.6 0.1 collective-permute-start.8
  51.8 0.6 collective-permute-start.10
  52.4 0.5 collective-permute-start.9
  52.9 6.5 %collective-permute-done.10.refs_9_ = bf16[48,2176]{1,0:T(8,128)(2,1)S(1)} collective-permute-done((bf16[48,2176]{1,0:T(8,128)(2,1)S(1)}, bf16[48,2176]{1,0:T(8,128)(2,1)S(1)}, u32[]{:S(2)}, u32[]{:S(2)}) %collective-permute-start.10) | collective-permute-done | bytes 208928 | tf_op jit(solution)/shard_map/ppermute | solution.py:467
  59.4 0.3 collective-permute-done.9.refs_8_
  59.7 0.1 collective-permute-start.11
  59.7 0.7 collective-permute-start.12
  60.4 1.3 collective-permute-start.13
  61.8 0.7 copy-done.13
  62.5 1.0 copy-done.7
  63.5 6.2 %order.1 = (bf16[768,2048]{1,0:T(8,128)(2,1)}, bf16[2048,768]{1,0:T(8,128)(2,1)}, bf16[768,256]{1,0:T(8,128)(2,1)}, bf16[768,256]{1,0:T(8,128)(2,1)}, bf16[32,16,128]{2,1,0:T(8,128)(2,1)}) custom-call(bf16[3,8,4224]{2,1,0:T(8,128)(2,1)} %get-tuple-element.46.refs_0_, bf16[3,8,4224]{2,1,0:T(8,128)(2,1)} %copy-done.10, bf16[3,8,4224]{2,1,0:T(8,128)(2,1)} %copy-done.11, ...), custom_call_target="tpu_custom_call" | custom-call | bytes 9437184 | tf_op jit(solution)/shard_map/order/pallas_call | solution.py:579
  69.8 5.1 %collective-permute-done.13.refs_9_ = bf16[192,1024]{1,0:T(8,128)(2,1)S(1)} collective-permute-done((bf16[192,1024]{1,0:T(8,128)(2,1)S(1)}, bf16[192,1024]{1,0:T(8,128)(2,1)S(1)}, u32[]{:S(2)}, u32[]{:S(2)}) %collective-permute-start.13) | collective-permute-done | bytes 393248 | tf_op jit(solution)/shard_map/ppermute | solution.py:488
  74.9 2.3 %density.2 = (bf16[3,256,256]{2,1,0:T(8,128)(2,1)}, f32[32,2,128]{2,1,0:T(2,128)}) custom-call(bf16[32,16,128]{2,1,0:T(8,128)(2,1)} %get-tuple-element.58.refs_0_.msgs_ref, bf16[768,256]{1,0:T(8,128)(2,1)} %get-tuple-element.59.refs_1_.refs_3_, bf16[768,256]{1,0:T(8,128)(2,1)} %get-tuple-element.60.refs_2_.refs_4_), custom_call_target="tpu_custom_call" | custom-call | tf_op jit(solution)/shard_map/density/pallas_call | solution.py:611
  77.2 3.2 %all-to-all-start = ((f32[32,2,128]{2,1,0:T(2,128)}), f32[32,2,128]{2,1,0:T(2,128)S(1)}, u32[]{:S(2)}, u32[]{:S(2)}) async-start(f32[32,2,128]{2,1,0:T(2,128)} %get-tuple-element.61), calls=%async_computation | async-start | bytes 65536 | tf_op jit(solution)/shard_map/all_to_all | solution.py:30
  80.5 12.6 %direct.2.refs_1_ = f32[6,128,128]{2,1,0:T(8,128)} custom-call(bf16[2048,768]{1,0:T(8,128)(2,1)} %get-tuple-element.62.refs_0_, bf16[2048,1024]{1,0:T(8,128)(2,1)} %turn.1.refs_1_, bf16[768,2048]{1,0:T(8,128)(2,1)} %get-tuple-element.64.refs_2_, bf16[3,256,256]{2,1,0:T(8,128)(2,1)} %get-tuple-element.65.refs_3_, bf16[192,1024]{1,0:T(8,128)(2,1)} %bitcast.6, ...), custom_call_target="tpu_custom_call" | custom-call | flops 6442450944 | bytes 12582912 | tf_op jit(solution)/shard_map/direct/pallas_call | solution.py:629
  93.0 0.0 copy-start.3
  93.1 0.6 copy-done.16
  93.7 3.9 %exchange.2 = bf16[32,16,128]{2,1,0:T(8,128)(2,1)} custom-call(f32[32,2,128]{2,1,0:T(2,128)} %copy-done.16, f32[6,128,128]{2,1,0:T(8,128)} %direct.2.refs_1_, bf16[256,8192]{1,0:T(8,128)(2,1)} %refs_2_.5, bf16[768,256]{1,0:T(8,128)(2,1)} %get-tuple-element.59.refs_1_.refs_3_, bf16[768,256]{1,0:T(8,128)(2,1)} %get-tuple-element.60.refs_2_.refs_4_), custom_call_target="tpu_custom_call" | custom-call | tf_op jit(solution)/shard_map/exchange/pallas_call | solution.py:652
  97.6 14.1 %all_to_all.30.recv_ref = bf16[32,16,128]{2,1,0:T(8,128)(2,1)S(1)} all-to-all(bf16[32,16,128]{2,1,0:T(8,128)(2,1)} %exchange.2), channel_id=1, replica_groups=mesh['ka'=4,'band'=8] {'ka','band'}, dimensions={0} | all-to-all | bytes 262144 | tf_op jit(solution)/shard_map/all_to_all | solution.py:30
  111.7 0.8 first_owner.1
  112.6 10.6 %all_to_all.31.refs_0_.msgs_ref = bf16[32,16,128]{2,1,0:T(8,128)(2,1)} all-to-all(bf16[32,16,128]{2,1,0:T(8,128)(2,1)S(1)} %get-tuple-element.74), channel_id=1, replica_groups=mesh['ka'=4,'band'=8] {'ka','band'}, dimensions={0} | all-to-all | bytes 262144 | tf_op jit(solution)/shard_map/all_to_all | solution.py:30
  123.2 2.1 %density.3 = (bf16[3,256,256]{2,1,0:T(8,128)(2,1)}, f32[32,2,128]{2,1,0:T(2,128)}) custom-call(bf16[32,16,128]{2,1,0:T(8,128)(2,1)} %all_to_all.31.refs_0_.msgs_ref, bf16[768,256]{1,0:T(8,128)(2,1)} %get-tuple-element.59.refs_1_.refs_3_, bf16[768,256]{1,0:T(8,128)(2,1)} %get-tuple-element.60.refs_2_.refs_4_), custom_call_target="tpu_custom_call" | custom-call | tf_op jit(solution)/shard_map/density/pallas_call | solution.py:611
  125.4 2.8 %all-to-all-start.3 = ((f32[32,2,128]{2,1,0:T(2,128)}), f32[32,2,128]{2,1,0:T(2,128)S(1)}, u32[]{:S(2)}, u32[]{:S(2)}) async-start(f32[32,2,128]{2,1,0:T(2,128)} %get-tuple-element.75), calls=%async_computation.3 | async-start | bytes 65536 | tf_op jit(solution)/shard_map/all_to_all | solution.py:30
  128.1 12.6 %direct.3.refs_1_ = f32[6,128,128]{2,1,0:T(8,128)} custom-call(bf16[2048,768]{1,0:T(8,128)(2,1)} %get-tuple-element.62.refs_0_, bf16[2048,1024]{1,0:T(8,128)(2,1)} %turn.1.refs_1_, bf16[768,2048]{1,0:T(8,128)(2,1)} %get-tuple-element.64.refs_2_, bf16[3,256,256]{2,1,0:T(8,128)(2,1)} %get-tuple-element.76.refs_3_, bf16[192,1024]{1,0:T(8,128)(2,1)} %bitcast.7, ...), custom_call_target="tpu_custom_call" | custom-call | flops 6442450944 | bytes 12582912 | tf_op jit(solution)/shard_map/direct/pallas_call | solution.py:629
  140.7 0.6 copy-done.15
  141.3 3.9 %exchange.3 = bf16[32,16,128]{2,1,0:T(8,128)(2,1)} custom-call(f32[32,2,128]{2,1,0:T(2,128)} %copy-done.15, f32[6,128,128]{2,1,0:T(8,128)} %direct.3.refs_1_, bf16[256,8192]{1,0:T(8,128)(2,1)} %refs_2_.5, bf16[768,256]{1,0:T(8,128)(2,1)} %get-tuple-element.59.refs_1_.refs_3_, bf16[768,256]{1,0:T(8,128)(2,1)} %get-tuple-element.60.refs_2_.refs_4_), custom_call_target="tpu_custom_call" | custom-call | tf_op jit(solution)/shard_map/exchange/pallas_call | solution.py:652
  145.2 14.1 %all_to_all.32.recv_ref = bf16[32,16,128]{2,1,0:T(8,128)(2,1)S(1)} all-to-all(bf16[32,16,128]{2,1,0:T(8,128)(2,1)} %exchange.3), channel_id=1, replica_groups=mesh['ka'=4,'band'=8] {'ka','band'}, dimensions={0} | all-to-all | bytes 262144 | tf_op jit(solution)/shard_map/all_to_all | solution.py:30
  159.3 1.3 second_owner.1
  160.7 9.0 %all_to_all.33.msgs_ref = f32[32,2,128]{2,1,0:T(2,128)S(1)} all-to-all(f32[32,2,128]{2,1,0:T(2,128)S(1)} %get-tuple-element.79), channel_id=1, replica_groups=mesh['ka'=4,'band'=8] {'ka','band'}, dimensions={0} | all-to-all | bytes 65536 | tf_op jit(solution)/shard_map/all_to_all | solution.py:30
  169.7 1.3 finish.1
  (54 shorter events, 0.2 us)
Async XLA Ops:
  2.9 13.5 %collective-permute-start = (bf16[3,8,4224]{2,1,0:T(8,128)(2,1)}, bf16[3,8,4224]{2,1,0:T(8,128)(2,1)S(1)}, u32[]{:S(2)}, u32[]{:S(2)}) collective-permute-start(bf16[3,8,4224]{2,1,0:T(8,128)(2,1)} %get-tuple-element.47), channel_id=1, source_target_pairs={{0,8},{8,0},{16,24},{24,16},{1,9},{9,1},{17,25},{25,17},{2,10},{10... | collective-permute-start | bytes 608264 | tf_op jit(solution)/shard_map/ppermute | solution.py:467
  6.0 26.2 %collective-permute-start.1 = (bf16[3,8,4224]{2,1,0:T(8,128)(2,1)}, bf16[3,8,4224]{2,1,0:T(8,128)(2,1)S(1)}, u32[]{:S(2)}, u32[]{:S(2)}) collective-permute-start(bf16[3,8,4224]{2,1,0:T(8,128)(2,1)} %get-tuple-element.48), channel_id=1, source_target_pairs={{0,16},{8,24},{16,0},{24,8},{1,17},{9,25},{17,1},{25,9},{2,18},{10... | collective-permute-start | bytes 608264 | tf_op jit(solution)/shard_map/ppermute | solution.py:467
  8.6 23.6 %collective-permute-start.2 = (bf16[3,8,4224]{2,1,0:T(8,128)(2,1)}, bf16[3,8,4224]{2,1,0:T(8,128)(2,1)S(1)}, u32[]{:S(2)}, u32[]{:S(2)}) collective-permute-start(bf16[3,8,4224]{2,1,0:T(8,128)(2,1)} %get-tuple-element.49), channel_id=1, source_target_pairs={{0,24},{8,16},{16,8},{24,0},{1,25},{9,17},{17,9},{25,1},{2,26},{10... | collective-permute-start | bytes 608264 | tf_op jit(solution)/shard_map/ppermute | solution.py:467
  9.8 36.0 %copy-start.14 = (bf16[3,64,1024]{2,1,0:T(8,128)(2,1)}, bf16[3,64,1024]{2,1,0:T(8,128)(2,1)S(1)}, u32[]{:S(2)}) copy-start(bf16[3,64,1024]{2,1,0:T(8,128)(2,1)S(1)} %constant_dynamic-slice_fusion) | copy-start | bytes 1179652
  9.8 25.6 %collective-permute-start.5 = (bf16[192,1024]{1,0:T(8,128)(2,1)S(1)}, bf16[192,1024]{1,0:T(8,128)(2,1)S(1)}, u32[]{:S(2)}, u32[]{:S(2)}) collective-permute-start(bf16[192,1024]{1,0:T(8,128)(2,1)S(1)} %bitcast.3), channel_id=1, source_target_pairs={{0,24},{24,0},{1,25},{25,1},{2,26},{26,2},{3,27},{27,3},{4,28},{28... | collective-permute-start | bytes 1179656 | tf_op jit(solution)/shard_map/ppermute | solution.py:477
  16.4 29.3 %copy-start.10 = (bf16[3,8,4224]{2,1,0:T(8,128)(2,1)}, bf16[3,8,4224]{2,1,0:T(8,128)(2,1)S(1)}, u32[]{:S(2)}) copy-start(bf16[3,8,4224]{2,1,0:T(8,128)(2,1)S(1)} %collective-permute-done.refs_1_) | copy-start | bytes 608260
  32.2 13.6 %copy-start.11 = (bf16[3,8,4224]{2,1,0:T(8,128)(2,1)}, bf16[3,8,4224]{2,1,0:T(8,128)(2,1)S(1)}, u32[]{:S(2)}) copy-start(bf16[3,8,4224]{2,1,0:T(8,128)(2,1)S(1)} %collective-permute-done.1.refs_2_) | copy-start | bytes 608260
  32.2 13.6 %copy-start.12 = (bf16[3,8,4224]{2,1,0:T(8,128)(2,1)}, bf16[3,8,4224]{2,1,0:T(8,128)(2,1)S(1)}, u32[]{:S(2)}) copy-start(bf16[3,8,4224]{2,1,0:T(8,128)(2,1)S(1)} %collective-permute-done.2.refs_3_) | copy-start | bytes 608260
  32.3 19.2 %copy-start.4 = (bf16[96,2176]{1,0:T(8,128)(2,1)}, bf16[96,2176]{1,0:T(8,128)(2,1)S(1)}, u32[]{:S(2)}) copy-start(bf16[96,2176]{1,0:T(8,128)(2,1)S(1)} %maximum_bitcast_fusion.refs_4_) | copy-start | bytes 1253380
  32.3 13.5 %collective-permute-start.3 = (bf16[96,2176]{1,0:T(8,128)(2,1)S(1)}, bf16[96,2176]{1,0:T(8,128)(2,1)S(1)}, u32[]{:S(2)}, u32[]{:S(2)}) collective-permute-start(bf16[96,2176]{1,0:T(8,128)(2,1)S(1)} %maximum_bitcast_fusion.refs_4_), channel_id=1, source_target_pairs={{0,2},{1,3},{2,0},{3,1},{4,6},{5,7},{6,4},{7,5},{8,10},{9,11},{10,... | collective-permute-start | bytes 1253384 | tf_op jit(solution)/shard_map/ppermute | solution.py:467
  33.9 12.0 %collective-permute-start.4 = (bf16[96,2176]{1,0:T(8,128)(2,1)S(1)}, bf16[96,2176]{1,0:T(8,128)(2,1)S(1)}, u32[]{:S(2)}, u32[]{:S(2)}) collective-permute-start(bf16[96,2176]{1,0:T(8,128)(2,1)S(1)} %maximum_bitcast_fusion.refs_4_), channel_id=1, source_target_pairs={{0,4},{1,5},{2,6},{3,7},{4,0},{5,1},{6,2},{7,3},{8,12},{9,13},{10,... | collective-permute-start | bytes 1253384 | tf_op jit(solution)/shard_map/ppermute | solution.py:467
  35.4 10.4 %copy-start.17 = (bf16[192,1024]{1,0:T(8,128)(2,1)}, bf16[192,1024]{1,0:T(8,128)(2,1)S(1)}, u32[]{:S(2)}) copy-start(bf16[192,1024]{1,0:T(8,128)(2,1)S(1)} %collective-permute-done.5.refs_7_.refs_10_) | copy-start | bytes 1179652
  35.4 12.0 %collective-permute-start.6 = (bf16[192,1024]{1,0:T(8,128)(2,1)S(1)}, bf16[192,1024]{1,0:T(8,128)(2,1)S(1)}, u32[]{:S(2)}, u32[]{:S(2)}) collective-permute-start(bf16[192,1024]{1,0:T(8,128)(2,1)S(1)} %bitcast.4), channel_id=1, source_target_pairs={{0,8},{8,16},{16,24},{1,9},{9,17},{17,25},{2,10},{10,18},{18,26},{... | collective-permute-start | bytes 1179656 | tf_op jit(solution)/shard_map/ppermute | solution.py:488
  40.8 10.8 %collective-permute-start.7 = (bf16[192,1024]{1,0:T(8,128)(2,1)S(1)}, bf16[192,1024]{1,0:T(8,128)(2,1)S(1)}, u32[]{:S(2)}, u32[]{:S(2)}) collective-permute-start(bf16[192,1024]{1,0:T(8,128)(2,1)S(1)} %bitcast.5), channel_id=1, source_target_pairs={{8,0},{16,8},{24,16},{9,1},{17,9},{25,17},{10,2},{18,10},{26,18},{... | collective-permute-start | bytes 1179656 | tf_op jit(solution)/shard_map/ppermute | solution.py:488
  45.8 16.0 %copy-start.5 = (bf16[96,2176]{1,0:T(8,128)(2,1)}, bf16[96,2176]{1,0:T(8,128)(2,1)S(1)}, u32[]{:S(2)}) copy-start(bf16[96,2176]{1,0:T(8,128)(2,1)S(1)} %collective-permute-done.3.refs_6_) | copy-start | bytes 1253380
  45.8 16.0 %copy-start.6 = (bf16[96,2176]{1,0:T(8,128)(2,1)}, bf16[96,2176]{1,0:T(8,128)(2,1)S(1)}, u32[]{:S(2)}) copy-start(bf16[96,2176]{1,0:T(8,128)(2,1)S(1)} %collective-permute-done.4.refs_7_) | copy-start | bytes 1253380
  47.4 22.3 %copy-start.18 = (bf16[192,1024]{1,0:T(8,128)(2,1)}, bf16[192,1024]{1,0:T(8,128)(2,1)S(1)}, u32[]{:S(2)}) copy-start(bf16[192,1024]{1,0:T(8,128)(2,1)S(1)} %collective-permute-done.6.refs_5_) | copy-start | bytes 1179652
  51.5 18.2 %copy-start.19 = (bf16[192,1024]{1,0:T(8,128)(2,1)}, bf16[192,1024]{1,0:T(8,128)(2,1)S(1)}, u32[]{:S(2)}) copy-start(bf16[192,1024]{1,0:T(8,128)(2,1)S(1)} %collective-permute-done.7.refs_8_) | copy-start | bytes 1179652
  51.6 10.1 %collective-permute-start.8 = (bf16[288,2176]{1,0:T(8,128)(2,1)S(1)}, bf16[288,2176]{1,0:T(8,128)(2,1)S(1)}, u32[]{:S(2)}, u32[]{:S(2)}) collective-permute-start(bf16[288,2176]{1,0:T(8,128)(2,1)S(1)} %pad_maximum_fusion), channel_id=1, source_target_pairs={{0,1},{1,0},{2,3},{3,2},{4,5},{5,4},{6,7},{7,6},{8,9},{9,8},{10,11... | collective-permute-start | bytes 3760136 | tf_op jit(solution)/shard_map/ppermute | solution.py:467
  51.8 7.6 %collective-permute-start.10 = (bf16[48,2176]{1,0:T(8,128)(2,1)S(1)}, bf16[48,2176]{1,0:T(8,128)(2,1)S(1)}, u32[]{:S(2)}, u32[]{:S(2)}) collective-permute-start(bf16[48,2176]{1,0:T(8,128)(2,1)S(1)} %slice.23), channel_id=1, source_target_pairs={{0,2},{1,3},{2,0},{3,1},{4,6},{5,7},{6,4},{7,5},{8,10},{9,11},{10,... | collective-permute-start | bytes 626696 | tf_op jit(solution)/shard_map/ppermute | solution.py:467
  52.4 7.3 %collective-permute-start.9 = (bf16[48,2176]{1,0:T(8,128)(2,1)S(1)}, bf16[48,2176]{1,0:T(8,128)(2,1)S(1)}, u32[]{:S(2)}, u32[]{:S(2)}) collective-permute-start(bf16[48,2176]{1,0:T(8,128)(2,1)S(1)} %slice.22), channel_id=1, source_target_pairs={{0,4},{1,5},{2,6},{3,7},{4,0},{5,1},{6,2},{7,3},{8,12},{9,13},{10,... | collective-permute-start | bytes 626696 | tf_op jit(solution)/shard_map/ppermute | solution.py:467
  59.4 2.4 %copy-start.8 = (bf16[48,2176]{1,0:T(8,128)(2,1)}, bf16[48,2176]{1,0:T(8,128)(2,1)S(1)}, u32[]{:S(2)}) copy-start(bf16[48,2176]{1,0:T(8,128)(2,1)S(1)} %collective-permute-done.10.refs_9_) | copy-start | bytes 626692
  59.6 2.2 %copy-start.9 = (bf16[48,2176]{1,0:T(8,128)(2,1)}, bf16[48,2176]{1,0:T(8,128)(2,1)S(1)}, u32[]{:S(2)}) copy-start(bf16[48,2176]{1,0:T(8,128)(2,1)S(1)} %collective-permute-done.9.refs_8_) | copy-start | bytes 626692
  59.7 2.1 %collective-permute-start.11 = (bf16[96,2176]{1,0:T(8,128)(2,1)S(1)}, bf16[96,2176]{1,0:T(8,128)(2,1)S(1)}, u32[]{:S(2)}, u32[]{:S(2)}) collective-permute-start(bf16[96,2176]{1,0:T(8,128)(2,1)S(1)} %pad_maximum_fusion.1), channel_id=1, source_target_pairs={{0,1},{1,0},{2,3},{3,2},{4,5},{5,4},{6,7},{7,6},{8,9},{9,8},{10,11... | collective-permute-start | bytes 1253384 | tf_op jit(solution)/shard_map/ppermute | solution.py:467
  59.7 10.0 %collective-permute-start.12 = (bf16[192,1024]{1,0:T(8,128)(2,1)S(1)}, bf16[192,1024]{1,0:T(8,128)(2,1)S(1)}, u32[]{:S(2)}, u32[]{:S(2)}) collective-permute-start(bf16[192,1024]{1,0:T(8,128)(2,1)S(1)} %collective-permute-done.6.refs_5_), channel_id=1, source_target_pairs={{8,16},{16,24},{9,17},{17,25},{10,18},{18,26},{11,19},{19,27},{12,... | collective-permute-start | bytes 1179656 | tf_op jit(solution)/shard_map/ppermute | solution.py:488
  60.4 14.5 %collective-permute-start.13 = (bf16[192,1024]{1,0:T(8,128)(2,1)S(1)}, bf16[192,1024]{1,0:T(8,128)(2,1)S(1)}, u32[]{:S(2)}, u32[]{:S(2)}) collective-permute-start(bf16[192,1024]{1,0:T(8,128)(2,1)S(1)} %collective-permute-done.7.refs_8_), channel_id=1, source_target_pairs={{8,0},{16,8},{9,1},{17,9},{10,2},{18,10},{11,3},{19,11},{12,4},{20... | collective-permute-start | bytes 1179656 | tf_op jit(solution)/shard_map/ppermute | solution.py:488
  61.8 0.7 copy-start.13
  62.5 1.0 copy-start.7
  69.8 10.7 %copy-start.20 = (bf16[192,1024]{1,0:T(8,128)(2,1)}, bf16[192,1024]{1,0:T(8,128)(2,1)S(1)}, u32[]{:S(2)}) copy-start(bf16[192,1024]{1,0:T(8,128)(2,1)S(1)} %collective-permute-done.12.refs_6_) | copy-start | bytes 1179652
  74.9 5.5 %copy-start.21 = (bf16[192,1024]{1,0:T(8,128)(2,1)}, bf16[192,1024]{1,0:T(8,128)(2,1)S(1)}, u32[]{:S(2)}) copy-start(bf16[192,1024]{1,0:T(8,128)(2,1)S(1)} %collective-permute-done.13.refs_9_) | copy-start | bytes 1179652
  77.2 15.8 %all-to-all-start = ((f32[32,2,128]{2,1,0:T(2,128)}), f32[32,2,128]{2,1,0:T(2,128)S(1)}, u32[]{:S(2)}, u32[]{:S(2)}) async-start(f32[32,2,128]{2,1,0:T(2,128)} %get-tuple-element.61), calls=%async_computation | async-start | bytes 65536 | tf_op jit(solution)/shard_map/all_to_all | solution.py:30
  93.0 18.7 %copy-start.1 = (bf16[32,16,128]{2,1,0:T(8,128)(2,1)S(1)}, bf16[32,16,128]{2,1,0:T(8,128)(2,1)}, u32[]{:S(2)}) copy-start(bf16[32,16,128]{2,1,0:T(8,128)(2,1)} %get-tuple-element.58.refs_0_.msgs_ref) | copy-start | bytes 393220
  93.0 18.7 %copy-start.2 = (f32[16,128]{1,0:T(8,128)S(1)}, f32[16,128]{1,0:T(8,128)}, u32[]{:S(2)}) copy-start(f32[16,128]{1,0:T(8,128)} %get-tuple-element.72.gap_ref) | copy-start | bytes 24580
  93.0 18.7 %copy-start.3 = (f32[16,128]{1,0:T(8,128)S(1)}, f32[16,128]{1,0:T(8,128)}, u32[]{:S(2)}) copy-start(f32[16,128]{1,0:T(8,128)} %get-tuple-element.73.own_ref) | copy-start | bytes 24580
  93.1 0.6 copy-start.16
  125.4 15.4 %all-to-all-start.3 = ((f32[32,2,128]{2,1,0:T(2,128)}), f32[32,2,128]{2,1,0:T(2,128)S(1)}, u32[]{:S(2)}, u32[]{:S(2)}) async-start(f32[32,2,128]{2,1,0:T(2,128)} %get-tuple-element.75), calls=%async_computation.3 | async-start | bytes 65536 | tf_op jit(solution)/shard_map/all_to_all | solution.py:30
  140.7 18.6 %copy-start = (bf16[32,16,128]{2,1,0:T(8,128)(2,1)S(1)}, bf16[32,16,128]{2,1,0:T(8,128)(2,1)}, u32[]{:S(2)}) copy-start(bf16[32,16,128]{2,1,0:T(8,128)(2,1)} %all_to_all.31.refs_0_.msgs_ref) | copy-start | bytes 393220
  140.7 0.6 copy-start.15

commit v14 on v12

--- a/solution.py
+++ b/solution.py
@@ -292,11 +292,14 @@
     row_copy = pltpu.make_async_copy(rows_ref, vals, row_sem.at[0])
     start_all([qx_copy, turned_copies[0]])
     each_cond(lambda copy: copy.start())
+    scr_copies[0].start()
+    for i in range(1, nu // tile):
+        start_all([turned_copies[i], scr_copies[i]])
+    row_copy.start()
     qx_copy.wait()
     for i in range(nu // tile):
         rows = slice(i * tile, (i + 1) * tile)
         turned_copies[i].wait()
-        scr_copies[i].start()
         for kq in range(qx.shape[0]):
             cols = slice(kq * quad, (kq + 1) * quad)
             mixed[rows, cols] = jnp.dot(
@@ -305,7 +308,6 @@
         if i == 0:
             each_cond(lambda copy: copy.wait())
             cond_rows = conds[...].reshape(-1, mu)
-        start_all(turned_copies[i + 1 : i + 2] or [row_copy])
         scr_copies[i].wait()
         amp = jnp.dot(mixed[rows, :], cond_rows, preferred_element_type=F32)
         kern[rows, :] = (scrs[rows, :].astype(F32) * amp * scale).astype(BF)
@@ -319,8 +321,8 @@
 def exchange_kernel(cfg, chunk, scale, *refs):
     n_ka, n_band, k_dev = cfg
     k_points = n_ka * k_dev
-    rho_ref, di_ref, coul_ref, vown_ref, cond_ref, msg_ref = refs[:6]
-    rhos, di, coul, conds, vown, part, msg, coul_sems, sems = refs[6:]
+    rhos, di_ref, coul_ref, vown_ref, cond_ref, msg_ref = refs[:6]
+    di, coul, conds, vown, part, msg, coul_sems, sems = refs[6:]
     own, npt = coul_ref.shape
     coul_copies = [
         pltpu.make_async_copy(
@@ -328,22 +330,16 @@
         )
         for i in range(npt // chunk)
     ]
-    rho_copy = pltpu.make_async_copy(rho_ref, rhos, sems.at[0])
     copies = [
-        pltpu.make_async_copy(vown_ref, vown, sems.at[1]),
-        pltpu.make_async_copy(di_ref, di, sems.at[2]),
-        pltpu.make_async_copy(cond_ref, conds, sems.at[3]),
+        pltpu.make_async_copy(vown_ref, vown, sems.at[0]),
+        pltpu.make_async_copy(di_ref, di, sems.at[1]),
+        pltpu.make_async_copy(cond_ref, conds, sems.at[2]),
     ]
-    ahead = 2
-    start_all([rho_copy] + coul_copies[:ahead])
-    rho_copy.wait()
+    start_all(coul_copies + copies)
     acc = jnp.zeros((own, LANES), F32)
     per_dev = own // LANES
     for i in range(npt // chunk):
         coul_copies[i].wait()
-        start_all(coul_copies[i + ahead : i + ahead + 1])
-        if i + ahead == npt // chunk:
-            start_all(copies)
         for j in range(i * chunk // LANES, (i + 1) * chunk // LANES):
             rho = rhos[j // per_dev, pl.ds(j % per_dev, 1), :].astype(BF).astype(F32)
             acc = acc + coul[:, j * LANES : (j + 1) * LANES].astype(F32) * rho
@@ -482,7 +478,7 @@
     return flows
 
 
-def plane_pieces(own_piece, others, later):
+def plane_pieces(own_piece, others):
     def move(block, d):
         return swap(block, "band", d)
 
@@ -492,12 +488,11 @@
     by_x, by_y, core, others = lax.optimization_barrier((by_x, by_y, core, others))
     diag = [move(by_x[:half], 4), move(by_y[half:], 2)]
     near_x, near_y = move(by_x, 1), move(by_y, 1)
-    diag, later = lax.optimization_barrier((diag, later))
     far = move(jnp.concatenate(diag, axis=0), 1)
     arrays = [own_piece, core, by_x, near_x, by_y, near_y, diag[0], diag[1], far]
     parts = tuple(((i, 0, rows),) for i in range(6))
     parts += (((6, 0, half), (7, 0, half)), ((8, 0, rows),))
-    return arrays, parts, others, later
+    return arrays, parts, others
 
 
 def kernel_path(start_vec, val_energy, cond_energy, val_orb, cond_orb, coulomb, screened):
@@ -545,23 +540,22 @@
     cond_local = cond_local.reshape(k_dev * n_cond, mu_blk)
     below, above = line_gather(cond_local, "ka")
 
-    chunk, tile = 1024, 1024
+    chunk, tile = 1024, nu_blk
     rows_all, conds_all = k_points * nv_blk * n_band, k_points * n_cond
     scr_turned = call(
-        functools.partial(turn_kernel, tile // 2),
+        functools.partial(turn_kernel, nu_blk // 4),
         "turn",
         shape_of((nu_blk, mu_blk), BF),
         [ANY],
         ANY,
         [pltpu.VMEM((mu_blk, nu_blk), BF), pltpu.VMEM((nu_blk, mu_blk), BF)]
-        + [dma(2 * nu_blk // tile)] * 2,
+        + [dma(4)] * 2,
         moved=8 * MIB,
     )(screened)
-    pieces, parts, others, later = plane_pieces(
-        val_cut, (scr_turned, below[0], above[0]), (below[1:-1], above[1:-1])
+    val_cut, below[0], above[0] = lax.optimization_barrier((val_cut, below[0], above[0]))
+    pieces, parts, (scr_turned, below[1], above[1]) = plane_pieces(
+        val_cut, (scr_turned, below[1], above[1])
     )
-    scr_turned, below[0], above[0] = others
-    below[1:-1], above[1:-1] = later
     val_rows, val_turned, val_own, cond_own, msgs = call(
         functools.partial(order_kernel, parts, n_ka),
         "order",
@@ -638,10 +632,9 @@
             functools.partial(exchange_kernel, cfg, chunk, scale),
             "exchange",
             msg_shape,
-            [ANY] * 5,
+            [VMEM] + [ANY] * 4,
             VMEM,
             [
-                pltpu.VMEM((devices, own // LANES, LANES), F32),
                 pltpu.VMEM((pairs, LANES, LANES), F32),
                 pltpu.VMEM((own, npt_all), BF),
                 pltpu.VMEM((conds_all, own), BF),
@@ -649,7 +642,7 @@
                 pltpu.VMEM((pairs, LANES, LANES), F32),
                 pltpu.VMEM((devices,) + block, F32),
                 dma(npt_all // chunk),
-                dma(4),
+                dma(3),
             ],
         )(density, direct, coulomb, val_own, cond_own)
         recv = exchange_all(summed)

time: 166 us -> 169 us (1.018)
  waiting for transfers between devices: 21.3 us -> 35.4 us
  Pallas kernels: 59.4 us -> 52.9 us
  starting transfers between devices: 30 us -> 25.5 us
    ppermute x6, waiting for transfers between devices: 12.3 us -> 21 us  [line_gather(): moving = lax.ppermute(moving, axis, [(i, i - way) for i in senders])]
    ppermute x11, waiting for transfers between devices: 8.96 us -> 14.4 us  [swap(): lax.ppermute(block, axis, [(i, i ^ d) for i in range(lax.axis_size(axis))])]
    pallas_call x2, Pallas kernels: 13.3 us -> 8.87 us  [kernel_path(): call(functools.partial(exchange_kernel, cfg, chunk, scale), 'exchange', m...]
    all_to_all x2, starting transfers between devices: 9.51 us -> 6.97 us  [exchange_all(): return lax.all_to_all(parts, AXES, split_axis=0, concat_axis=0, tiled=True)]
    pallas_call x2, Pallas kernels: 26.2 us -> 24.1 us  [kernel_path(): call(functools.partial(direct_kernel, n_ka, tile, scale), 'direct', shape...]
    ppermute x11, starting transfers between devices: 12.5 us -> 10.4 us  [swap(): lax.ppermute(block, axis, [(i, i ^ d) for i in range(lax.axis_size(axis))])]
  transfers between devices with their start and end apart: 19 -> 19, of which waited for: 4 -> 6; matrix products, arithmetic and copies ran while one was open for 1% -> 1% of each run, Pallas kernels for 23% -> 21%
where the time goes in v14:
time: 169 us
  Pallas kernels  52.9 us (31%)
  blocking collectives  47.4 us (28%)
  waiting for transfers between devices  35.4 us (21%)
  starting transfers between devices  25.5 us (15%)
  local copies, waits for them, and re-layouts  5.81 us (3%)
    all_to_all x4, blocking collectives, exchange_all(): return lax.all_to_all(parts, AXES, split_axis=0, concat_axis=0, tiled=True)  47.4 us
    pallas_call x2, Pallas kernels, kernel_path(): call(functools.partial(direct_kernel, n_ka, tile, scale), 'direct', shape...  24.1 us
    ppermute x6, waiting for transfers between devices, line_gather(): moving = lax.ppermute(moving, axis, [(i, i - way) for i in senders])  21 us
    ppermute x11, waiting for transfers between devices, swap(): lax.ppermute(block, axis, [(i, i ^ d) for i in range(lax.axis_size(axis))])  14.4 us
    ppermute x11, starting transfers between devices, swap(): lax.ppermute(block, axis, [(i, i ^ d) for i in range(lax.axis_size(axis))])  10.4 us
    pallas_call x2, Pallas kernels, kernel_path(): call(functools.partial(exchange_kernel, cfg, chunk, scale), 'exchange', m...  8.87 us
    ppermute x6, starting transfers between devices, line_gather(): moving = lax.ppermute(moving, axis, [(i, i - way) for i in senders])  8.06 us
    all_to_all x2, starting transfers between devices, exchange_all(): return lax.all_to_all(parts, AXES, split_axis=0, concat_axis=0, tiled=True)  6.97 us
  transfers between devices with their start and end apart: 19, of which 6 were waited for; matrix products, arithmetic and copies ran while one was open for 1% of the time, Pallas kernels for 21%

profile of v14, /device:TPU:0, one launch (start us, length us, event | category | flops | bytes accessed | tf_op | source)
XLA Modules:
  0.0 168.5 jit_solution(5862587983850293952)
XLA Ops:
  0.6 2.3 %pack.1 = (f32[16,128]{1,0:T(8,128)}, f32[16,128]{1,0:T(8,128)}, bf16[3,8,4224]{2,1,0:T(8,128)(2,1)}, bf16[3,8,4224]{2,1,0:T(8,128)(2,1)}, bf16[3,8,4224]{2,1,0:T(8,128)(2,1)}, /*index=5*/bf16[3,8,4224]{2,1,0:T(8,128)(2,1)}) custom-call(f32[3,512]{1,0:T(4,128)} %refs_0_.1, f32[3,64]{1,0:T(4,128)} %refs_1_.1, f32[3,8]{1,0:T(4,128)} %refs_2_.3, ...), custom_call_target="tpu_custom_call" | custom-call | tf_op jit(solution)/shard_map/pack/pallas_call | solution.py:519
  2.9 3.1 %collective-permute-start = (bf16[3,8,4224]{2,1,0:T(8,128)(2,1)}, bf16[3,8,4224]{2,1,0:T(8,128)(2,1)S(1)}, u32[]{:S(2)}, u32[]{:S(2)}) collective-permute-start(bf16[3,8,4224]{2,1,0:T(8,128)(2,1)} %get-tuple-element.42), channel_id=1, source_target_pairs={{0,8},{8,0},{16,24},{24,16},{1,9},{9,1},{17,25},{25,17},{2,10},{10... | collective-permute-start | bytes 608264 | tf_op jit(solution)/shard_map/ppermute | solution.py:465
  6.0 2.6 %collective-permute-start.1 = (bf16[3,8,4224]{2,1,0:T(8,128)(2,1)}, bf16[3,8,4224]{2,1,0:T(8,128)(2,1)S(1)}, u32[]{:S(2)}, u32[]{:S(2)}) collective-permute-start(bf16[3,8,4224]{2,1,0:T(8,128)(2,1)} %get-tuple-element.43), channel_id=1, source_target_pairs={{0,16},{8,24},{16,0},{24,8},{1,17},{9,25},{17,1},{25,9},{2,18},{10... | collective-permute-start | bytes 608264 | tf_op jit(solution)/shard_map/ppermute | solution.py:465
  8.6 1.2 constant_dynamic-slice_fusion
  9.8 2.8 %collective-permute-start.3 = (bf16[192,1024]{1,0:T(8,128)(2,1)S(1)}, bf16[192,1024]{1,0:T(8,128)(2,1)S(1)}, u32[]{:S(2)}, u32[]{:S(2)}) collective-permute-start(bf16[192,1024]{1,0:T(8,128)(2,1)S(1)} %bitcast.3), channel_id=1, source_target_pairs={{0,8},{8,16},{16,24},{1,9},{9,17},{17,25},{2,10},{10,18},{18,26},{... | collective-permute-start | bytes 1179656 | tf_op jit(solution)/shard_map/ppermute | solution.py:475
  12.6 1.3 collective-permute-start.4
  13.9 0.9 slice.18
  14.9 8.9 %collective-permute-done.1.refs_2_ = bf16[3,8,4224]{2,1,0:T(8,128)(2,1)S(1)} collective-permute-done((bf16[3,8,4224]{2,1,0:T(8,128)(2,1)}, bf16[3,8,4224]{2,1,0:T(8,128)(2,1)S(1)}, u32[]{:S(2)}, u32[]{:S(2)}) %collective-permute-start.1) | collective-permute-done | bytes 202784 | tf_op jit(solution)/shard_map/ppermute | solution.py:465
  23.8 0.1 maximum_bitcast_fusion.refs_4_
  23.9 3.8 %collective-permute-done.3.refs_5_ = bf16[192,1024]{1,0:T(8,128)(2,1)S(1)} collective-permute-done((bf16[192,1024]{1,0:T(8,128)(2,1)S(1)}, bf16[192,1024]{1,0:T(8,128)(2,1)S(1)}, u32[]{:S(2)}, u32[]{:S(2)}) %collective-permute-start.3) | collective-permute-done | bytes 393248 | tf_op jit(solution)/shard_map/ppermute | solution.py:475
  27.7 1.7 collective-permute-done.4.refs_8_
  29.4 1.5 collective-permute-start.5
  30.9 1.5 collective-permute-start.6
  32.4 0.7 collective-permute-start.8
  33.0 1.3 collective-permute-start.9
  34.4 3.7 %turn.1.refs_1_ = bf16[2048,1024]{1,0:T(8,128)(2,1)} custom-call(bf16[1024,2048]{1,0:T(8,128)(2,1)} %scr_ref.1), custom_call_target="tpu_custom_call" | custom-call | bytes 8388608 | tf_op jit(solution)/shard_map/turn/pallas_call | solution.py:545
  38.1 15.6 %collective-permute-done.9.refs_9_ = bf16[192,1024]{1,0:T(8,128)(2,1)S(1)} collective-permute-done((bf16[192,1024]{1,0:T(8,128)(2,1)S(1)}, bf16[192,1024]{1,0:T(8,128)(2,1)S(1)}, u32[]{:S(2)}, u32[]{:S(2)}) %collective-permute-start.9) | collective-permute-done | bytes 393248 | tf_op jit(solution)/shard_map/ppermute | solution.py:475
  53.8 0.6 collective-permute-start.12
  54.4 0.6 collective-permute-start.13
  55.0 0.5 collective-permute-start.11
  55.5 5.2 %collective-permute-done.12.refs_10_ = bf16[48,2176]{1,0:T(8,128)(2,1)S(1)} collective-permute-done((bf16[48,2176]{1,0:T(8,128)(2,1)S(1)}, bf16[48,2176]{1,0:T(8,128)(2,1)S(1)}, u32[]{:S(2)}, u32[]{:S(2)}) %collective-permute-start.12) | collective-permute-done | bytes 208928 | tf_op jit(solution)/shard_map/ppermute | solution.py:465
  60.6 0.3 collective-permute-done.13.refs_11_
  61.0 0.1 collective-permute-start.14
  61.1 0.7 collective-permute-start.15
  61.8 1.3 collective-permute-start.16
  63.2 0.7 copy-done.13
  63.8 0.1 copy-done.14
  64.0 0.8 copy-done.15
  64.7 6.2 %order.1 = (bf16[768,2048]{1,0:T(8,128)(2,1)}, bf16[2048,768]{1,0:T(8,128)(2,1)}, bf16[768,256]{1,0:T(8,128)(2,1)}, bf16[768,256]{1,0:T(8,128)(2,1)}, bf16[32,16,128]{2,1,0:T(8,128)(2,1)}) custom-call(bf16[3,8,4224]{2,1,0:T(8,128)(2,1)} %get-tuple-element.41.refs_0_, bf16[3,8,4224]{2,1,0:T(8,128)(2,1)} %copy-done.9, bf16[3,8,4224]{2,1,0:T(8,128)(2,1)} %copy-done.10, ...), custom_call_target="tpu_custom_call" | custom-call | bytes 9437184 | tf_op jit(solution)/shard_map/order/pallas_call | solution.py:559
  70.9 2.2 %density.2 = (bf16[3,256,256]{2,1,0:T(8,128)(2,1)}, f32[32,2,128]{2,1,0:T(2,128)}) custom-call(bf16[32,16,128]{2,1,0:T(8,128)(2,1)} %get-tuple-element.50.refs_0_.msgs_ref, bf16[768,256]{1,0:T(8,128)(2,1)} %get-tuple-element.51.refs_1_.refs_3_, bf16[768,256]{1,0:T(8,128)(2,1)} %get-tuple-element.52.refs_2_.refs_4_), custom_call_target="tpu_custom_call" | custom-call | tf_op jit(solution)/shard_map/density/pallas_call | solution.py:590
  73.1 4.2 %all-to-all-start = ((f32[32,2,128]{2,1,0:T(2,128)}), f32[32,2,128]{2,1,0:T(2,128)S(1)}, u32[]{:S(2)}, u32[]{:S(2)}) async-start(f32[32,2,128]{2,1,0:T(2,128)} %get-tuple-element.53), calls=%async_computation | async-start | bytes 65536 | tf_op jit(solution)/shard_map/all_to_all | solution.py:30
  77.3 0.7 copy-done.23
  78.0 0.1 copy-done.24
  78.1 12.1 %direct.2.refs_1_ = f32[6,128,128]{2,1,0:T(8,128)} custom-call(bf16[2048,768]{1,0:T(8,128)(2,1)} %get-tuple-element.54.refs_0_, bf16[2048,1024]{1,0:T(8,128)(2,1)} %turn.1.refs_1_, bf16[768,2048]{1,0:T(8,128)(2,1)} %get-tuple-element.56.refs_2_, bf16[3,256,256]{2,1,0:T(8,128)(2,1)} %get-tuple-element.57.refs_3_, bf16[192,1024]{1,0:T(8,128)(2,1)} %bitcast.5, ...), custom_call_target="tpu_custom_call" | custom-call | flops 6442450944 | bytes 12582912 | tf_op jit(solution)/shard_map/direct/pallas_call | solution.py:608
  90.3 0.6 copy-done.18
  90.8 4.4 %exchange.2 = bf16[32,16,128]{2,1,0:T(8,128)(2,1)} custom-call(f32[32,2,128]{2,1,0:T(2,128)} %copy-done.18, f32[6,128,128]{2,1,0:T(8,128)} %direct.2.refs_1_, bf16[256,8192]{1,0:T(8,128)(2,1)} %refs_2_.5, bf16[768,256]{1,0:T(8,128)(2,1)} %get-tuple-element.51.refs_1_.refs_3_, bf16[768,256]{1,0:T(8,128)(2,1)} %get-tuple-element.52.refs_2_.refs_4_), custom_call_target="tpu_custom_call" | custom-call | tf_op jit(solution)/shard_map/exchange/pallas_call | solution.py:631
  95.3 13.9 %all_to_all.30.recv_ref = bf16[32,16,128]{2,1,0:T(8,128)(2,1)S(1)} all-to-all(bf16[32,16,128]{2,1,0:T(8,128)(2,1)} %exchange.2), channel_id=1, replica_groups=mesh['ka'=4,'band'=8] {'ka','band'}, dimensions={0} | all-to-all | bytes 262144 | tf_op jit(solution)/shard_map/all_to_all | solution.py:30
  109.2 0.8 first_owner.1
  110.1 10.6 %all_to_all.31.refs_0_.msgs_ref = bf16[32,16,128]{2,1,0:T(8,128)(2,1)} all-to-all(bf16[32,16,128]{2,1,0:T(8,128)(2,1)S(1)} %get-tuple-element.64), channel_id=1, replica_groups=mesh['ka'=4,'band'=8] {'ka','band'}, dimensions={0} | all-to-all | bytes 262144 | tf_op jit(solution)/shard_map/all_to_all | solution.py:30
  120.7 2.1 %density.3 = (bf16[3,256,256]{2,1,0:T(8,128)(2,1)}, f32[32,2,128]{2,1,0:T(2,128)}) custom-call(bf16[32,16,128]{2,1,0:T(8,128)(2,1)} %all_to_all.31.refs_0_.msgs_ref, bf16[768,256]{1,0:T(8,128)(2,1)} %get-tuple-element.51.refs_1_.refs_3_, bf16[768,256]{1,0:T(8,128)(2,1)} %get-tuple-element.52.refs_2_.refs_4_), custom_call_target="tpu_custom_call" | custom-call | tf_op jit(solution)/shard_map/density/pallas_call | solution.py:590
  122.8 2.8 %all-to-all-start.3 = ((f32[32,2,128]{2,1,0:T(2,128)}), f32[32,2,128]{2,1,0:T(2,128)S(1)}, u32[]{:S(2)}, u32[]{:S(2)}) async-start(f32[32,2,128]{2,1,0:T(2,128)} %get-tuple-element.65), calls=%async_computation.3 | async-start | bytes 65536 | tf_op jit(solution)/shard_map/all_to_all | solution.py:30
  125.6 12.1 %direct.3.refs_1_ = f32[6,128,128]{2,1,0:T(8,128)} custom-call(bf16[2048,768]{1,0:T(8,128)(2,1)} %get-tuple-element.54.refs_0_, bf16[2048,1024]{1,0:T(8,128)(2,1)} %turn.1.refs_1_, bf16[768,2048]{1,0:T(8,128)(2,1)} %get-tuple-element.56.refs_2_, bf16[3,256,256]{2,1,0:T(8,128)(2,1)} %get-tuple-element.66.refs_3_, bf16[192,1024]{1,0:T(8,128)(2,1)} %bitcast.6, ...), custom_call_target="tpu_custom_call" | custom-call | flops 6442450944 | bytes 12582912 | tf_op jit(solution)/shard_map/direct/pallas_call | solution.py:608
  137.7 0.6 copy-done.17
  138.3 4.4 %exchange.3 = bf16[32,16,128]{2,1,0:T(8,128)(2,1)} custom-call(f32[32,2,128]{2,1,0:T(2,128)} %copy-done.17, f32[6,128,128]{2,1,0:T(8,128)} %direct.3.refs_1_, bf16[256,8192]{1,0:T(8,128)(2,1)} %refs_2_.5, bf16[768,256]{1,0:T(8,128)(2,1)} %get-tuple-element.51.refs_1_.refs_3_, bf16[768,256]{1,0:T(8,128)(2,1)} %get-tuple-element.52.refs_2_.refs_4_), custom_call_target="tpu_custom_call" | custom-call | tf_op jit(solution)/shard_map/exchange/pallas_call | solution.py:631
  142.8 13.9 %all_to_all.32.recv_ref = bf16[32,16,128]{2,1,0:T(8,128)(2,1)S(1)} all-to-all(bf16[32,16,128]{2,1,0:T(8,128)(2,1)} %exchange.3), channel_id=1, replica_groups=mesh['ka'=4,'band'=8] {'ka','band'}, dimensions={0} | all-to-all | bytes 262144 | tf_op jit(solution)/shard_map/all_to_all | solution.py:30
  156.6 1.3 second_owner.1
  158.0 9.0 %all_to_all.33.msgs_ref = f32[32,2,128]{2,1,0:T(2,128)S(1)} all-to-all(f32[32,2,128]{2,1,0:T(2,128)S(1)} %get-tuple-element.69), channel_id=1, replica_groups=mesh['ka'=4,'band'=8] {'ka','band'}, dimensions={0} | all-to-all | bytes 65536 | tf_op jit(solution)/shard_map/all_to_all | solution.py:30
  167.0 1.3 finish.1
  (65 shorter events, 0.2 us)
Async XLA Ops:
  2.9 11.9 %collective-permute-start = (bf16[3,8,4224]{2,1,0:T(8,128)(2,1)}, bf16[3,8,4224]{2,1,0:T(8,128)(2,1)S(1)}, u32[]{:S(2)}, u32[]{:S(2)}) collective-permute-start(bf16[3,8,4224]{2,1,0:T(8,128)(2,1)} %get-tuple-element.42), channel_id=1, source_target_pairs={{0,8},{8,0},{16,24},{24,16},{1,9},{9,1},{17,25},{25,17},{2,10},{10... | collective-permute-start | bytes 608264 | tf_op jit(solution)/shard_map/ppermute | solution.py:465
  6.0 17.8 %collective-permute-start.1 = (bf16[3,8,4224]{2,1,0:T(8,128)(2,1)}, bf16[3,8,4224]{2,1,0:T(8,128)(2,1)S(1)}, u32[]{:S(2)}, u32[]{:S(2)}) collective-permute-start(bf16[3,8,4224]{2,1,0:T(8,128)(2,1)} %get-tuple-element.43), channel_id=1, source_target_pairs={{0,16},{8,24},{16,0},{24,8},{1,17},{9,25},{17,1},{25,9},{2,18},{10... | collective-permute-start | bytes 608264 | tf_op jit(solution)/shard_map/ppermute | solution.py:465
  8.6 15.2 %collective-permute-start.2 = (bf16[3,8,4224]{2,1,0:T(8,128)(2,1)}, bf16[3,8,4224]{2,1,0:T(8,128)(2,1)S(1)}, u32[]{:S(2)}, u32[]{:S(2)}) collective-permute-start(bf16[3,8,4224]{2,1,0:T(8,128)(2,1)} %get-tuple-element.44), channel_id=1, source_target_pairs={{0,24},{8,16},{16,8},{24,0},{1,25},{9,17},{17,9},{25,1},{2,26},{10... | collective-permute-start | bytes 608264 | tf_op jit(solution)/shard_map/ppermute | solution.py:465
  9.8 28.3 %copy-start.16 = (bf16[3,64,1024]{2,1,0:T(8,128)(2,1)}, bf16[3,64,1024]{2,1,0:T(8,128)(2,1)S(1)}, u32[]{:S(2)}) copy-start(bf16[3,64,1024]{2,1,0:T(8,128)(2,1)S(1)} %constant_dynamic-slice_fusion) | copy-start | bytes 1179652
  9.8 17.9 %collective-permute-start.3 = (bf16[192,1024]{1,0:T(8,128)(2,1)S(1)}, bf16[192,1024]{1,0:T(8,128)(2,1)S(1)}, u32[]{:S(2)}, u32[]{:S(2)}) collective-permute-start(bf16[192,1024]{1,0:T(8,128)(2,1)S(1)} %bitcast.3), channel_id=1, source_target_pairs={{0,8},{8,16},{16,24},{1,9},{9,17},{17,25},{2,10},{10,18},{18,26},{... | collective-permute-start | bytes 1179656 | tf_op jit(solution)/shard_map/ppermute | solution.py:475
  12.6 16.7 %collective-permute-start.4 = (bf16[192,1024]{1,0:T(8,128)(2,1)S(1)}, bf16[192,1024]{1,0:T(8,128)(2,1)S(1)}, u32[]{:S(2)}, u32[]{:S(2)}) collective-permute-start(bf16[192,1024]{1,0:T(8,128)(2,1)S(1)} %bitcast.4), channel_id=1, source_target_pairs={{8,0},{16,8},{24,16},{9,1},{17,9},{25,17},{10,2},{18,10},{26,18},{... | collective-permute-start | bytes 1179656 | tf_op jit(solution)/shard_map/ppermute | solution.py:475
  14.8 23.2 %copy-start.9 = (bf16[3,8,4224]{2,1,0:T(8,128)(2,1)}, bf16[3,8,4224]{2,1,0:T(8,128)(2,1)S(1)}, u32[]{:S(2)}) copy-start(bf16[3,8,4224]{2,1,0:T(8,128)(2,1)S(1)} %collective-permute-done.refs_1_) | copy-start | bytes 608260
  23.8 14.3 %copy-start.10 = (bf16[3,8,4224]{2,1,0:T(8,128)(2,1)}, bf16[3,8,4224]{2,1,0:T(8,128)(2,1)S(1)}, u32[]{:S(2)}) copy-start(bf16[3,8,4224]{2,1,0:T(8,128)(2,1)S(1)} %collective-permute-done.1.refs_2_) | copy-start | bytes 608260
  23.8 14.3 %copy-start.11 = (bf16[3,8,4224]{2,1,0:T(8,128)(2,1)}, bf16[3,8,4224]{2,1,0:T(8,128)(2,1)S(1)}, u32[]{:S(2)}) copy-start(bf16[3,8,4224]{2,1,0:T(8,128)(2,1)S(1)} %collective-permute-done.2.refs_3_) | copy-start | bytes 608260
  23.9 14.2 %copy-start.4 = (bf16[96,2176]{1,0:T(8,128)(2,1)}, bf16[96,2176]{1,0:T(8,128)(2,1)S(1)}, u32[]{:S(2)}) copy-start(bf16[96,2176]{1,0:T(8,128)(2,1)S(1)} %maximum_bitcast_fusion.refs_4_) | copy-start | bytes 1253380
  27.7 10.4 %copy-start.19 = (bf16[192,1024]{1,0:T(8,128)(2,1)}, bf16[192,1024]{1,0:T(8,128)(2,1)S(1)}, u32[]{:S(2)}) copy-start(bf16[192,1024]{1,0:T(8,128)(2,1)S(1)} %collective-permute-done.3.refs_5_) | copy-start | bytes 1179652
  29.4 8.7 %copy-start.20 = (bf16[192,1024]{1,0:T(8,128)(2,1)}, bf16[192,1024]{1,0:T(8,128)(2,1)S(1)}, u32[]{:S(2)}) copy-start(bf16[192,1024]{1,0:T(8,128)(2,1)S(1)} %collective-permute-done.4.refs_8_) | copy-start | bytes 1179652
  29.4 24.3 %collective-permute-start.5 = (bf16[96,2176]{1,0:T(8,128)(2,1)S(1)}, bf16[96,2176]{1,0:T(8,128)(2,1)S(1)}, u32[]{:S(2)}, u32[]{:S(2)}) collective-permute-start(bf16[96,2176]{1,0:T(8,128)(2,1)S(1)} %maximum_bitcast_fusion.refs_4_), channel_id=1, source_target_pairs={{0,2},{1,3},{2,0},{3,1},{4,6},{5,7},{6,4},{7,5},{8,10},{9,11},{10,... | collective-permute-start | bytes 1253384 | tf_op jit(solution)/shard_map/ppermute | solution.py:465
  30.9 22.8 %collective-permute-start.6 = (bf16[96,2176]{1,0:T(8,128)(2,1)S(1)}, bf16[96,2176]{1,0:T(8,128)(2,1)S(1)}, u32[]{:S(2)}, u32[]{:S(2)}) collective-permute-start(bf16[96,2176]{1,0:T(8,128)(2,1)S(1)} %maximum_bitcast_fusion.refs_4_), channel_id=1, source_target_pairs={{0,4},{1,5},{2,6},{3,7},{4,0},{5,1},{6,2},{7,3},{8,12},{9,13},{10,... | collective-permute-start | bytes 1253384 | tf_op jit(solution)/shard_map/ppermute | solution.py:465
  32.4 21.4 %collective-permute-start.7 = (bf16[96,2176]{1,0:T(8,128)(2,1)S(1)}, bf16[96,2176]{1,0:T(8,128)(2,1)S(1)}, u32[]{:S(2)}, u32[]{:S(2)}) collective-permute-start(bf16[96,2176]{1,0:T(8,128)(2,1)S(1)} %maximum_bitcast_fusion.refs_4_), channel_id=1, source_target_pairs={{0,1},{1,0},{2,3},{3,2},{4,5},{5,4},{6,7},{7,6},{8,9},{9,8},{10,11... | collective-permute-start | bytes 1253384 | tf_op jit(solution)/shard_map/ppermute | solution.py:465
  32.4 5.8 %collective-permute-start.8 = (bf16[192,1024]{1,0:T(8,128)(2,1)S(1)}, bf16[192,1024]{1,0:T(8,128)(2,1)S(1)}, u32[]{:S(2)}, u32[]{:S(2)}) collective-permute-start(bf16[192,1024]{1,0:T(8,128)(2,1)S(1)} %collective-permute-done.3.refs_5_), channel_id=1, source_target_pairs={{8,16},{16,24},{9,17},{17,25},{10,18},{18,26},{11,19},{19,27},{12,... | collective-permute-start | bytes 1179656 | tf_op jit(solution)/shard_map/ppermute | solution.py:475
  33.0 20.6 %collective-permute-start.9 = (bf16[192,1024]{1,0:T(8,128)(2,1)S(1)}, bf16[192,1024]{1,0:T(8,128)(2,1)S(1)}, u32[]{:S(2)}, u32[]{:S(2)}) collective-permute-start(bf16[192,1024]{1,0:T(8,128)(2,1)S(1)} %collective-permute-done.4.refs_8_), channel_id=1, source_target_pairs={{8,0},{16,8},{9,1},{17,9},{10,2},{18,10},{11,3},{19,11},{12,4},{20... | collective-permute-start | bytes 1179656 | tf_op jit(solution)/shard_map/ppermute | solution.py:475
  38.1 39.2 %copy-start.21 = (bf16[192,1024]{1,0:T(8,128)(2,1)}, bf16[192,1024]{1,0:T(8,128)(2,1)S(1)}, u32[]{:S(2)}) copy-start(bf16[192,1024]{1,0:T(8,128)(2,1)S(1)} %collective-permute-done.8.refs_6_) | copy-start | bytes 1179652
  53.7 23.6 %copy-start.22 = (bf16[192,1024]{1,0:T(8,128)(2,1)}, bf16[192,1024]{1,0:T(8,128)(2,1)S(1)}, u32[]{:S(2)}) copy-start(bf16[192,1024]{1,0:T(8,128)(2,1)S(1)} %collective-permute-done.9.refs_9_) | copy-start | bytes 1179652
  53.7 9.4 %copy-start.5 = (bf16[96,2176]{1,0:T(8,128)(2,1)}, bf16[96,2176]{1,0:T(8,128)(2,1)S(1)}, u32[]{:S(2)}) copy-start(bf16[96,2176]{1,0:T(8,128)(2,1)S(1)} %collective-permute-done.5.refs_6_) | copy-start | bytes 1253380
  53.7 9.4 %copy-start.6 = (bf16[96,2176]{1,0:T(8,128)(2,1)}, bf16[96,2176]{1,0:T(8,128)(2,1)S(1)}, u32[]{:S(2)}) copy-start(bf16[96,2176]{1,0:T(8,128)(2,1)S(1)} %collective-permute-done.6.refs_8_) | copy-start | bytes 1253380
  53.7 9.4 %copy-start.12 = (bf16[96,2176]{1,0:T(8,128)(2,1)}, bf16[96,2176]{1,0:T(8,128)(2,1)S(1)}, u32[]{:S(2)}) copy-start(bf16[96,2176]{1,0:T(8,128)(2,1)S(1)} %collective-permute-done.7.refs_5_) | copy-start | bytes 1253380
  53.8 6.9 %collective-permute-start.12 = (bf16[48,2176]{1,0:T(8,128)(2,1)S(1)}, bf16[48,2176]{1,0:T(8,128)(2,1)S(1)}, u32[]{:S(2)}, u32[]{:S(2)}) collective-permute-start(bf16[48,2176]{1,0:T(8,128)(2,1)S(1)} %slice.22), channel_id=1, source_target_pairs={{0,4},{1,5},{2,6},{3,7},{4,0},{5,1},{6,2},{7,3},{8,12},{9,13},{10,... | collective-permute-start | bytes 626696 | tf_op jit(solution)/shard_map/ppermute | solution.py:465
  54.4 6.6 %collective-permute-start.13 = (bf16[48,2176]{1,0:T(8,128)(2,1)S(1)}, bf16[48,2176]{1,0:T(8,128)(2,1)S(1)}, u32[]{:S(2)}, u32[]{:S(2)}) collective-permute-start(bf16[48,2176]{1,0:T(8,128)(2,1)S(1)} %slice.23), channel_id=1, source_target_pairs={{0,2},{1,3},{2,0},{3,1},{4,6},{5,7},{6,4},{7,5},{8,10},{9,11},{10,... | collective-permute-start | bytes 626696 | tf_op jit(solution)/shard_map/ppermute | solution.py:465
  55.0 8.1 %collective-permute-start.10 = (bf16[96,2176]{1,0:T(8,128)(2,1)S(1)}, bf16[96,2176]{1,0:T(8,128)(2,1)S(1)}, u32[]{:S(2)}, u32[]{:S(2)}) collective-permute-start(bf16[96,2176]{1,0:T(8,128)(2,1)S(1)} %collective-permute-done.5.refs_6_), channel_id=1, source_target_pairs={{0,1},{1,0},{2,3},{3,2},{4,5},{5,4},{6,7},{7,6},{8,9},{9,8},{10,11... | collective-permute-start | bytes 1253384 | tf_op jit(solution)/shard_map/ppermute | solution.py:465
  55.0 8.1 %collective-permute-start.11 = (bf16[96,2176]{1,0:T(8,128)(2,1)S(1)}, bf16[96,2176]{1,0:T(8,128)(2,1)S(1)}, u32[]{:S(2)}, u32[]{:S(2)}) collective-permute-start(bf16[96,2176]{1,0:T(8,128)(2,1)S(1)} %collective-permute-done.6.refs_8_), channel_id=1, source_target_pairs={{0,1},{1,0},{2,3},{3,2},{4,5},{5,4},{6,7},{7,6},{8,9},{9,8},{10,11... | collective-permute-start | bytes 1253384 | tf_op jit(solution)/shard_map/ppermute | solution.py:465
  60.6 2.5 %copy-start.7 = (bf16[48,2176]{1,0:T(8,128)(2,1)}, bf16[48,2176]{1,0:T(8,128)(2,1)S(1)}, u32[]{:S(2)}) copy-start(bf16[48,2176]{1,0:T(8,128)(2,1)S(1)} %collective-permute-done.12.refs_10_) | copy-start | bytes 626692
  60.9 2.2 %copy-start.8 = (bf16[48,2176]{1,0:T(8,128)(2,1)}, bf16[48,2176]{1,0:T(8,128)(2,1)S(1)}, u32[]{:S(2)}) copy-start(bf16[48,2176]{1,0:T(8,128)(2,1)S(1)} %collective-permute-done.13.refs_11_) | copy-start | bytes 626692
  61.0 2.1 %collective-permute-start.14 = (bf16[96,2176]{1,0:T(8,128)(2,1)S(1)}, bf16[96,2176]{1,0:T(8,128)(2,1)S(1)}, u32[]{:S(2)}, u32[]{:S(2)}) collective-permute-start(bf16[96,2176]{1,0:T(8,128)(2,1)S(1)} %pad_maximum_fusion), channel_id=1, source_target_pairs={{0,1},{1,0},{2,3},{3,2},{4,5},{5,4},{6,7},{7,6},{8,9},{9,8},{10,11... | collective-permute-start | bytes 1253384 | tf_op jit(solution)/shard_map/ppermute | solution.py:465
  61.1 16.2 %collective-permute-start.15 = (bf16[192,1024]{1,0:T(8,128)(2,1)S(1)}, bf16[192,1024]{1,0:T(8,128)(2,1)S(1)}, u32[]{:S(2)}, u32[]{:S(2)}) collective-permute-start(bf16[192,1024]{1,0:T(8,128)(2,1)S(1)} %collective-permute-done.8.refs_6_), channel_id=1, source_target_pairs={{16,24},{17,25},{18,26},{19,27},{20,28},{21,29},{22,30},{23,31}} | collective-permute-start | bytes 1179656 | tf_op jit(solution)/shard_map/ppermute | solution.py:475
  61.8 15.5 %collective-permute-start.16 = (bf16[192,1024]{1,0:T(8,128)(2,1)S(1)}, bf16[192,1024]{1,0:T(8,128)(2,1)S(1)}, u32[]{:S(2)}, u32[]{:S(2)}) collective-permute-start(bf16[192,1024]{1,0:T(8,128)(2,1)S(1)} %collective-permute-done.9.refs_9_), channel_id=1, source_target_pairs={{8,0},{9,1},{10,2},{11,3},{12,4},{13,5},{14,6},{15,7}} | collective-permute-start | bytes 1179656 | tf_op jit(solution)/shard_map/ppermute | solution.py:475
  63.1 0.8 copy-start.13
  63.1 0.9 copy-start.14
  64.0 0.8 copy-start.15
  73.1 17.2 %all-to-all-start = ((f32[32,2,128]{2,1,0:T(2,128)}), f32[32,2,128]{2,1,0:T(2,128)S(1)}, u32[]{:S(2)}, u32[]{:S(2)}) async-start(f32[32,2,128]{2,1,0:T(2,128)} %get-tuple-element.53), calls=%async_computation | async-start | bytes 65536 | tf_op jit(solution)/shard_map/all_to_all | solution.py:30
  77.3 0.7 copy-start.23
  77.3 0.8 copy-start.24
  90.2 19.0 %copy-start.1 = (bf16[32,16,128]{2,1,0:T(8,128)(2,1)S(1)}, bf16[32,16,128]{2,1,0:T(8,128)(2,1)}, u32[]{:S(2)}) copy-start(bf16[32,16,128]{2,1,0:T(8,128)(2,1)} %get-tuple-element.50.refs_0_.msgs_ref) | copy-start | bytes 393220
  90.2 19.0 %copy-start.2 = (f32[16,128]{1,0:T(8,128)S(1)}, f32[16,128]{1,0:T(8,128)}, u32[]{:S(2)}) copy-start(f32[16,128]{1,0:T(8,128)} %get-tuple-element.62.gap_ref) | copy-start | bytes 24580
  90.2 19.0 %copy-start.3 = (f32[16,128]{1,0:T(8,128)S(1)}, f32[16,128]{1,0:T(8,128)}, u32[]{:S(2)}) copy-start(f32[16,128]{1,0:T(8,128)} %get-tuple-element.63.own_ref) | copy-start | bytes 24580
  90.2 0.6 copy-start.18
  122.8 14.9 %all-to-all-start.3 = ((f32[32,2,128]{2,1,0:T(2,128)}), f32[32,2,128]{2,1,0:T(2,128)S(1)}, u32[]{:S(2)}, u32[]{:S(2)}) async-start(f32[32,2,128]{2,1,0:T(2,128)} %get-tuple-element.65), calls=%async_computation.3 | async-start | bytes 65536 | tf_op jit(solution)/shard_map/all_to_all | solution.py:30
  137.7 18.9 %copy-start = (bf16[32,16,128]{2,1,0:T(8,128)(2,1)S(1)}, bf16[32,16,128]{2,1,0:T(8,128)(2,1)}, u32[]{:S(2)}) copy-start(bf16[32,16,128]{2,1,0:T(8,128)(2,1)} %all_to_all.31.refs_0_.msgs_ref) | copy-start | bytes 393220
  137.7 0.6 copy-start.17

commit v15 on v14

--- a/solution.py
+++ b/solution.py
@@ -260,26 +260,18 @@
 
 def direct_kernel(n_ka, tile, scale, *refs):
     turned_ref, scr_ref, rows_ref, qx_ref, refs = refs[0], refs[1], refs[2], refs[3], refs[4:]
-    hops = [(0, 0)] + [(way, hop) for way in (-1, 1) for hop in range(1, n_ka)]
-    cond_refs, refs = refs[: len(hops)], refs[len(hops) :]
+    cond_ref, refs = refs[0], refs[1:]
     di_ref, qx, turned, conds, scrs, vals, mixed, kern, folded = refs[:9]
     qx_sem, cond_sems, row_sem, chunk_sems = refs[9:]
     nu, mu = scr_ref.shape
     quad = 2 * LANES
     qx_copy = pltpu.make_async_copy(qx_ref, qx, qx_sem.at[0])
-    ka = lax.axis_index("ka")
-
-    def each_cond(act):
-        for i, (way, hop) in enumerate(hops):
-            origin = ka + way * hop
-            pl.when((origin >= 0) & (origin < n_ka))(
-                lambda i=i, origin=origin: act(
-                    pltpu.make_async_copy(
-                        cond_refs[i], conds.at[jnp.bitwise_xor(ka, origin)], cond_sems.at[i]
-                    )
-                )
-            )
-
+    cond_copies = [
+        pltpu.make_async_copy(
+            cond_ref.at[jnp.bitwise_xor(lax.axis_index("ka"), j)], conds.at[j], cond_sems.at[j]
+        )
+        for j in range(n_ka)
+    ]
     turned_copies, scr_copies = [], []
     for i in range(nu // tile):
         at = pl.ds(i * tile, tile)
@@ -290,9 +282,7 @@
             pltpu.make_async_copy(scr_ref.at[at, :], scrs.at[at, :], chunk_sems.at[1, i])
         )
     row_copy = pltpu.make_async_copy(rows_ref, vals, row_sem.at[0])
-    start_all([qx_copy, turned_copies[0]])
-    each_cond(lambda copy: copy.start())
-    scr_copies[0].start()
+    start_all([qx_copy, turned_copies[0]] + cond_copies + [scr_copies[0]])
     for i in range(1, nu // tile):
         start_all([turned_copies[i], scr_copies[i]])
     row_copy.start()
@@ -306,7 +296,7 @@
                 turned[rows, cols], qx[kq], preferred_element_type=F32
             ).astype(BF)
         if i == 0:
-            each_cond(lambda copy: copy.wait())
+            wait_all(cond_copies)
             cond_rows = conds[...].reshape(-1, mu)
         scr_copies[i].wait()
         amp = jnp.dot(mixed[rows, :], cond_rows, preferred_element_type=F32)
@@ -321,8 +311,9 @@
 def exchange_kernel(cfg, chunk, scale, *refs):
     n_ka, n_band, k_dev = cfg
     k_points = n_ka * k_dev
-    rhos, di_ref, coul_ref, vown_ref, cond_ref, msg_ref = refs[:6]
-    di, coul, conds, vown, part, msg, coul_sems, sems = refs[6:]
+    rho_ref, di_ref, coul_ref, vown_ref, cond_ref, msg_ref = refs[:6]
+    rhos, di, coul, conds, vown, part, msg, coul_sems, sems = refs[6:]
+    rho_copy = pltpu.make_async_copy(rho_ref, rhos, sems.at[3])
     own, npt = coul_ref.shape
     coul_copies = [
         pltpu.make_async_copy(
@@ -335,7 +326,8 @@
         pltpu.make_async_copy(di_ref, di, sems.at[1]),
         pltpu.make_async_copy(cond_ref, conds, sems.at[2]),
     ]
-    start_all(coul_copies + copies)
+    start_all([rho_copy] + coul_copies + copies)
+    rho_copy.wait()
     acc = jnp.zeros((own, LANES), F32)
     per_dev = own // LANES
     for i in range(npt // chunk):
@@ -463,19 +455,6 @@
 
 def swap(block, axis, d):
     return lax.ppermute(block, axis, [(i, i ^ d) for i in range(lax.axis_size(axis))])
-
-
-def line_gather(block, axis):
-    n = lax.axis_size(axis)
-    flows = []
-    for way in (-1, 1):
-        moving, flow = block, []
-        for hop in range(1, n):
-            senders = [i for i in range(n) if 0 <= i + way * (hop - 1) < n and 0 <= i - way < n]
-            moving = lax.ppermute(moving, axis, [(i, i - way) for i in senders])
-            flow.append(moving)
-        flows.append(flow)
-    return flows
 
 
 def plane_pieces(own_piece, others):
@@ -538,7 +517,8 @@
     val_cut = val_cut.reshape(piece_rows, wide)
     cond_local = lax.dynamic_slice_in_dim(cond_orb, base, mu_blk, 2)
     cond_local = cond_local.reshape(k_dev * n_cond, mu_blk)
-    below, above = line_gather(cond_local, "ka")
+    cond_wide = jnp.broadcast_to(cond_local[None], (n_ka,) + cond_local.shape)
+    cond_pts = lax.all_to_all(cond_wide, "ka", split_axis=0, concat_axis=0, tiled=True)
 
     chunk, tile = 1024, nu_blk
     rows_all, conds_all = k_points * nv_blk * n_band, k_points * n_cond
@@ -552,10 +532,7 @@
         + [dma(4)] * 2,
         moved=8 * MIB,
     )(screened)
-    val_cut, below[0], above[0] = lax.optimization_barrier((val_cut, below[0], above[0]))
-    pieces, parts, (scr_turned, below[1], above[1]) = plane_pieces(
-        val_cut, (scr_turned, below[1], above[1])
-    )
+    pieces, parts, scr_turned = plane_pieces(val_cut, scr_turned)
     val_rows, val_turned, val_own, cond_own, msgs = call(
         functools.partial(order_kernel, parts, n_ka),
         "order",
@@ -581,7 +558,6 @@
         moved=9 * MIB,
     )(*got, *pieces)
 
-    cond_pts = [cond_local] + below + above
     cfg = (n_ka, n_band, k_dev)
     quads = k_points // 4
     state, coef = None, None
@@ -609,7 +585,7 @@
             functools.partial(direct_kernel, n_ka, tile, scale),
             "direct",
             shape_of((pairs, LANES, LANES)),
-            [ANY] * (4 + len(cond_pts)),
+            [ANY] * 5,
             VMEM,
             [
                 pltpu.VMEM((quads, 2 * LANES, 2 * LANES), BF),
@@ -621,20 +597,21 @@
                 pltpu.VMEM((nu_blk, mu_blk), BF),
                 pltpu.VMEM((rows_all, mu_blk), BF),
                 dma(1),
-                dma(len(cond_pts)),
+                dma(n_ka),
                 dma(1),
                 dma(2, nu_blk // tile),
             ],
             flops=4 * mu_blk * nu_blk * conds_all,
             moved=12 * MIB,
-        )(val_turned, scr_turned, val_rows, qx, *cond_pts)
+        )(val_turned, scr_turned, val_rows, qx, cond_pts)
         summed = call(
             functools.partial(exchange_kernel, cfg, chunk, scale),
             "exchange",
             msg_shape,
-            [VMEM] + [ANY] * 4,
+            [ANY] * 5,
             VMEM,
             [
+                pltpu.VMEM((devices, own // LANES, LANES), F32),
                 pltpu.VMEM((pairs, LANES, LANES), F32),
                 pltpu.VMEM((own, npt_all), BF),
                 pltpu.VMEM((conds_all, own), BF),
@@ -642,7 +619,7 @@
                 pltpu.VMEM((pairs, LANES, LANES), F32),
                 pltpu.VMEM((devices,) + block, F32),
                 dma(npt_all // chunk),
-                dma(3),
+                dma(4),
             ],
         )(density, direct, coulomb, val_own, cond_own)
         recv = exchange_all(summed)

time: 169 us -> 188 us (1.11)
  waiting for transfers between devices: 35.4 us -> 57.5 us
    ppermute x11, waiting for transfers between devices: 14.4 us -> 57.5 us  [swap(): lax.ppermute(block, axis, [(i, i ^ d) for i in range(lax.axis_size(axis))])]
    ppermute x6 -> x0, waiting for transfers between devices: 21 us -> none  [line_gather(): moving = lax.ppermute(moving, axis, [(i, i - way) for i in senders])]
    ppermute x6 -> x0, starting transfers between devices: 8.06 us -> none  [line_gather(): moving = lax.ppermute(moving, axis, [(i, i - way) for i in senders])]
    all_to_all x0 -> x1, starting transfers between devices: none -> 6.32 us  [kernel_path(): lax.all_to_all(cond_wide, 'ka', split_axis=0, concat_axis=0, tiled=True)]
  transfers between devices with their start and end apart: 19 -> 14, of which waited for: 6 -> 7; matrix products, arithmetic and copies ran while one was open for 1% -> 0% of each run, Pallas kernels for 21% -> 19%
where the time goes in v15:
time: 188 us; the launch traced here: 187 us
  waiting for transfers between devices  57.5 us (31%)
  Pallas kernels  52 us (28%)
  blocking collectives  47.4 us (25%)
  starting transfers between devices  24.4 us (13%)
  local copies, waits for them, and re-layouts  4.75 us (3%)
    ppermute x11, waiting for transfers between devices, swap(): lax.ppermute(block, axis, [(i, i ^ d) for i in range(lax.axis_size(axis))])  57.5 us
    all_to_all x4, blocking collectives, exchange_all(): return lax.all_to_all(parts, AXES, split_axis=0, concat_axis=0, tiled=True)  47.4 us
    pallas_call x2, Pallas kernels, kernel_path(): call(functools.partial(direct_kernel, n_ka, tile, scale), 'direct', shape...  24.3 us
    ppermute x11, starting transfers between devices, swap(): lax.ppermute(block, axis, [(i, i ^ d) for i in range(lax.axis_size(axis))])  10.3 us
    pallas_call x2, Pallas kernels, kernel_path(): call(functools.partial(exchange_kernel, cfg, chunk, scale), 'exchange', m...  7.77 us
    all_to_all x2, starting transfers between devices, exchange_all(): return lax.all_to_all(parts, AXES, split_axis=0, concat_axis=0, tiled=True)  7.77 us
    all_to_all x1, starting transfers between devices, kernel_path(): lax.all_to_all(cond_wide, 'ka', split_axis=0, concat_axis=0, tiled=True)  6.32 us
    pallas_call x1, Pallas kernels, kernel_path(): call(functools.partial(order_kernel, parts, n_ka), 'order', (shape_of((ro...  6.13 us
  transfers between devices with their start and end apart: 14, of which 7 were waited for; matrix products, arithmetic and copies ran while one was open for 0% of the time, Pallas kernels for 19%

profile of v15, /device:TPU:0, one launch (start us, length us, event | category | flops | bytes accessed | tf_op | source)
XLA Modules:
  0.0 187.4 jit_solution(10118335355759869615)
XLA Ops:
  0.6 2.3 %pack.1 = (f32[16,128]{1,0:T(8,128)}, f32[16,128]{1,0:T(8,128)}, bf16[3,8,4224]{2,1,0:T(8,128)(2,1)}, bf16[3,8,4224]{2,1,0:T(8,128)(2,1)}, bf16[3,8,4224]{2,1,0:T(8,128)(2,1)}, /*index=5*/bf16[3,8,4224]{2,1,0:T(8,128)(2,1)}) custom-call(f32[3,512]{1,0:T(4,128)} %refs_0_.1, f32[3,64]{1,0:T(4,128)} %refs_1_.1, f32[3,8]{1,0:T(4,128)} %refs_2_.3, ...), custom_call_target="tpu_custom_call" | custom-call | tf_op jit(solution)/shard_map/pack/pallas_call | solution.py:498
  3.0 1.3 constant_dynamic-slice_fusion
  4.2 1.4 broadcast_in_dim.8
  5.6 6.3 %all-to-all-start.1 = ((bf16[4,192,1024]{2,1,0:T(8,128)(2,1)}), bf16[4,192,1024]{2,1,0:T(8,128)(2,1)S(1)}, u32[]{:S(2)}, u32[]{:S(2)}) async-start(bf16[4,192,1024]{2,1,0:T(8,128)(2,1)} %broadcast_in_dim.8), calls=%async_computation.1 | async-start | bytes 3145728 | tf_op jit(solution)/shard_map/all_to_all | solution.py:521
  11.9 2.0 %collective-permute-start = (bf16[3,8,4224]{2,1,0:T(8,128)(2,1)S(1)}, bf16[3,8,4224]{2,1,0:T(8,128)(2,1)S(1)}, u32[]{:S(2)}, u32[]{:S(2)}) collective-permute-start(bf16[3,8,4224]{2,1,0:T(8,128)(2,1)S(1)} %copy-done.22), channel_id=1, source_target_pairs={{0,8},{8,0},{16,24},{24,16},{1,9},{9,1},{17,25},{25,17},{2,10},{10... | collective-permute-start | bytes 608264 | tf_op jit(solution)/shard_map/ppermute | solution.py:457
  14.0 2.4 %collective-permute-start.1 = (bf16[3,8,4224]{2,1,0:T(8,128)(2,1)S(1)}, bf16[3,8,4224]{2,1,0:T(8,128)(2,1)S(1)}, u32[]{:S(2)}, u32[]{:S(2)}) collective-permute-start(bf16[3,8,4224]{2,1,0:T(8,128)(2,1)S(1)} %copy-done.21), channel_id=1, source_target_pairs={{0,16},{8,24},{16,0},{24,8},{1,17},{9,25},{17,1},{25,9},{2,18},{10... | collective-permute-start | bytes 608264 | tf_op jit(solution)/shard_map/ppermute | solution.py:457
  16.3 0.1 collective-permute-start.2
  16.4 26.5 %collective-permute-done.refs_1_ = bf16[3,8,4224]{2,1,0:T(8,128)(2,1)S(1)} collective-permute-done((bf16[3,8,4224]{2,1,0:T(8,128)(2,1)S(1)}, bf16[3,8,4224]{2,1,0:T(8,128)(2,1)S(1)}, u32[]{:S(2)}, u32[]{:S(2)}) %collective-permute-start) | collective-permute-done | bytes 202784 | tf_op jit(solution)/shard_map/ppermute | solution.py:457
  42.9 20.1 %collective-permute-done.1.refs_2_ = bf16[3,8,4224]{2,1,0:T(8,128)(2,1)S(1)} collective-permute-done((bf16[3,8,4224]{2,1,0:T(8,128)(2,1)S(1)}, bf16[3,8,4224]{2,1,0:T(8,128)(2,1)S(1)}, u32[]{:S(2)}, u32[]{:S(2)}) %collective-permute-start.1) | collective-permute-done | bytes 202784 | tf_op jit(solution)/shard_map/ppermute | solution.py:457
  63.0 0.0 collective-permute-done.2.refs_3_
  63.0 0.1 maximum_bitcast_fusion.refs_4_
  63.1 1.6 collective-permute-start.3
  64.7 1.5 collective-permute-start.4
  66.2 0.0 collective-permute-start.5
  66.2 3.7 %turn.1.refs_1_ = bf16[2048,1024]{1,0:T(8,128)(2,1)} custom-call(bf16[1024,2048]{1,0:T(8,128)(2,1)} %scr_ref.1), custom_call_target="tpu_custom_call" | custom-call | bytes 8388608 | tf_op jit(solution)/shard_map/turn/pallas_call | solution.py:525
  69.9 2.8 %collective-permute-done.3.refs_6_ = bf16[96,2176]{1,0:T(8,128)(2,1)S(1)} collective-permute-done((bf16[96,2176]{1,0:T(8,128)(2,1)S(1)}, bf16[96,2176]{1,0:T(8,128)(2,1)S(1)}, u32[]{:S(2)}, u32[]{:S(2)}) %collective-permute-start.3) | collective-permute-done | bytes 417824 | tf_op jit(solution)/shard_map/ppermute | solution.py:457
  72.7 1.6 collective-permute-done.4.refs_8_
  74.4 1.6 collective-permute-start.8
  76.0 0.6 collective-permute-start.9
  76.6 0.0 collective-permute-start.6
  76.6 0.5 collective-permute-start.7
  77.1 3.2 %collective-permute-done.8.refs_10_ = bf16[48,2176]{1,0:T(8,128)(2,1)S(1)} collective-permute-done((bf16[48,2176]{1,0:T(8,128)(2,1)S(1)}, bf16[48,2176]{1,0:T(8,128)(2,1)S(1)}, u32[]{:S(2)}, u32[]{:S(2)}) %collective-permute-start.8) | collective-permute-done | bytes 208928 | tf_op jit(solution)/shard_map/ppermute | solution.py:457
  80.3 1.6 collective-permute-done.9.refs_11_
  81.9 0.1 collective-permute-start.10
  82.0 0.0 collective-permute-done.6.refs_7_
  82.0 1.7 collective-permute-done.10.refs_12_
  83.8 0.8 copy-done.17
  84.6 6.1 %order.1 = (bf16[768,2048]{1,0:T(8,128)(2,1)}, bf16[2048,768]{1,0:T(8,128)(2,1)}, bf16[768,256]{1,0:T(8,128)(2,1)}, bf16[768,256]{1,0:T(8,128)(2,1)}, bf16[32,16,128]{2,1,0:T(8,128)(2,1)}) custom-call(bf16[3,8,4224]{2,1,0:T(8,128)(2,1)} %get-tuple-element.36.refs_0_, bf16[3,8,4224]{2,1,0:T(8,128)(2,1)} %copy-done.11, bf16[3,8,4224]{2,1,0:T(8,128)(2,1)} %copy-done.12, ...), custom_call_target="tpu_custom_call" | custom-call | bytes 9437184 | tf_op jit(solution)/shard_map/order/pallas_call | solution.py:536
  90.7 2.1 %density.2 = (bf16[3,256,256]{2,1,0:T(8,128)(2,1)}, f32[32,2,128]{2,1,0:T(2,128)}) custom-call(bf16[32,16,128]{2,1,0:T(8,128)(2,1)} %get-tuple-element.43.refs_0_.msgs_ref, bf16[768,256]{1,0:T(8,128)(2,1)} %get-tuple-element.44.refs_1_.refs_3_, bf16[768,256]{1,0:T(8,128)(2,1)} %get-tuple-element.45.refs_2_.refs_4_), custom_call_target="tpu_custom_call" | custom-call | tf_op jit(solution)/shard_map/density/pallas_call | solution.py:566
  92.8 0.0 all-to-all-done.1.refs_4_
  92.9 5.0 %all-to-all-start = ((f32[32,2,128]{2,1,0:T(2,128)}), f32[32,2,128]{2,1,0:T(2,128)S(1)}, u32[]{:S(2)}, u32[]{:S(2)}) async-start(f32[32,2,128]{2,1,0:T(2,128)} %get-tuple-element.46), calls=%async_computation | async-start | bytes 65536 | tf_op jit(solution)/shard_map/all_to_all | solution.py:30
  97.9 12.2 %direct.2.refs_1_ = f32[6,128,128]{2,1,0:T(8,128)} custom-call(bf16[2048,768]{1,0:T(8,128)(2,1)} %get-tuple-element.47.refs_0_, bf16[2048,1024]{1,0:T(8,128)(2,1)} %turn.1.refs_1_, bf16[768,2048]{1,0:T(8,128)(2,1)} %get-tuple-element.49.refs_2_, bf16[3,256,256]{2,1,0:T(8,128)(2,1)} %get-tuple-element.50.refs_3_, bf16[4,192,1024]{2,1,0:T(8,128)(2,1)} %copy-done.5), custom_call_target="tpu_custom_call" | custom-call | flops 6442450944 | bytes 12582912 | tf_op jit(solution)/shard_map/direct/pallas_call | solution.py:584
  110.1 0.0 copy-start.3
  110.1 0.6 copy-done.19
  110.7 3.9 %exchange.2 = bf16[32,16,128]{2,1,0:T(8,128)(2,1)} custom-call(f32[32,2,128]{2,1,0:T(2,128)} %copy-done.19, f32[6,128,128]{2,1,0:T(8,128)} %direct.2.refs_1_, bf16[256,8192]{1,0:T(8,128)(2,1)} %refs_2_.5, bf16[768,256]{1,0:T(8,128)(2,1)} %get-tuple-element.44.refs_1_.refs_3_, bf16[768,256]{1,0:T(8,128)(2,1)} %get-tuple-element.45.refs_2_.refs_4_), custom_call_target="tpu_custom_call" | custom-call | tf_op jit(solution)/shard_map/exchange/pallas_call | solution.py:607
  114.6 13.9 %all_to_all.35.recv_ref = bf16[32,16,128]{2,1,0:T(8,128)(2,1)S(1)} all-to-all(bf16[32,16,128]{2,1,0:T(8,128)(2,1)} %exchange.2), channel_id=1, replica_groups=mesh['ka'=4,'band'=8] {'ka','band'}, dimensions={0} | all-to-all | bytes 262144 | tf_op jit(solution)/shard_map/all_to_all | solution.py:30
  128.5 0.8 first_owner.1
  129.3 10.6 %all_to_all.36.refs_0_.msgs_ref = bf16[32,16,128]{2,1,0:T(8,128)(2,1)} all-to-all(bf16[32,16,128]{2,1,0:T(8,128)(2,1)S(1)} %get-tuple-element.54), channel_id=1, replica_groups=mesh['ka'=4,'band'=8] {'ka','band'}, dimensions={0} | all-to-all | bytes 262144 | tf_op jit(solution)/shard_map/all_to_all | solution.py:30
  139.9 2.1 %density.3 = (bf16[3,256,256]{2,1,0:T(8,128)(2,1)}, f32[32,2,128]{2,1,0:T(2,128)}) custom-call(bf16[32,16,128]{2,1,0:T(8,128)(2,1)} %all_to_all.36.refs_0_.msgs_ref, bf16[768,256]{1,0:T(8,128)(2,1)} %get-tuple-element.44.refs_1_.refs_3_, bf16[768,256]{1,0:T(8,128)(2,1)} %get-tuple-element.45.refs_2_.refs_4_), custom_call_target="tpu_custom_call" | custom-call | tf_op jit(solution)/shard_map/density/pallas_call | solution.py:566
  142.1 2.8 %all-to-all-start.4 = ((f32[32,2,128]{2,1,0:T(2,128)}), f32[32,2,128]{2,1,0:T(2,128)S(1)}, u32[]{:S(2)}, u32[]{:S(2)}) async-start(f32[32,2,128]{2,1,0:T(2,128)} %get-tuple-element.55), calls=%async_computation.4 | async-start | bytes 65536 | tf_op jit(solution)/shard_map/all_to_all | solution.py:30
  144.9 12.2 %direct.3.refs_1_ = f32[6,128,128]{2,1,0:T(8,128)} custom-call(bf16[2048,768]{1,0:T(8,128)(2,1)} %get-tuple-element.47.refs_0_, bf16[2048,1024]{1,0:T(8,128)(2,1)} %turn.1.refs_1_, bf16[768,2048]{1,0:T(8,128)(2,1)} %get-tuple-element.49.refs_2_, bf16[3,256,256]{2,1,0:T(8,128)(2,1)} %get-tuple-element.56.refs_3_, bf16[4,192,1024]{2,1,0:T(8,128)(2,1)} %copy-done.5), custom_call_target="tpu_custom_call" | custom-call | flops 6442450944 | bytes 12582912 | tf_op jit(solution)/shard_map/direct/pallas_call | solution.py:584
  157.1 0.0 all-to-all-done.4.refs_0_
  157.1 0.6 copy-done.18
  157.7 3.9 %exchange.3 = bf16[32,16,128]{2,1,0:T(8,128)(2,1)} custom-call(f32[32,2,128]{2,1,0:T(2,128)} %copy-done.18, f32[6,128,128]{2,1,0:T(8,128)} %direct.3.refs_1_, bf16[256,8192]{1,0:T(8,128)(2,1)} %refs_2_.5, bf16[768,256]{1,0:T(8,128)(2,1)} %get-tuple-element.44.refs_1_.refs_3_, bf16[768,256]{1,0:T(8,128)(2,1)} %get-tuple-element.45.refs_2_.refs_4_), custom_call_target="tpu_custom_call" | custom-call | tf_op jit(solution)/shard_map/exchange/pallas_call | solution.py:607
  161.6 13.9 %all_to_all.37.recv_ref = bf16[32,16,128]{2,1,0:T(8,128)(2,1)S(1)} all-to-all(bf16[32,16,128]{2,1,0:T(8,128)(2,1)} %exchange.3), channel_id=1, replica_groups=mesh['ka'=4,'band'=8] {'ka','band'}, dimensions={0} | all-to-all | bytes 262144 | tf_op jit(solution)/shard_map/all_to_all | solution.py:30
  175.5 1.3 second_owner.1
  176.8 9.0 %all_to_all.38.msgs_ref = f32[32,2,128]{2,1,0:T(2,128)S(1)} all-to-all(f32[32,2,128]{2,1,0:T(2,128)S(1)} %get-tuple-element.59), channel_id=1, replica_groups=mesh['ka'=4,'band'=8] {'ka','band'}, dimensions={0} | all-to-all | bytes 65536 | tf_op jit(solution)/shard_map/all_to_all | solution.py:30
  185.8 1.3 finish.1
  (52 shorter events, 0.2 us)
Async XLA Ops:
  2.9 9.0 %copy-start.22 = (bf16[3,8,4224]{2,1,0:T(8,128)(2,1)S(1)}, bf16[3,8,4224]{2,1,0:T(8,128)(2,1)}, u32[]{:S(2)}) copy-start(bf16[3,8,4224]{2,1,0:T(8,128)(2,1)} %get-tuple-element.37) | copy-start | bytes 608260
  2.9 11.0 %copy-start.21 = (bf16[3,8,4224]{2,1,0:T(8,128)(2,1)S(1)}, bf16[3,8,4224]{2,1,0:T(8,128)(2,1)}, u32[]{:S(2)}) copy-start(bf16[3,8,4224]{2,1,0:T(8,128)(2,1)} %get-tuple-element.38) | copy-start | bytes 608260
  2.9 13.4 %copy-start.20 = (bf16[3,8,4224]{2,1,0:T(8,128)(2,1)S(1)}, bf16[3,8,4224]{2,1,0:T(8,128)(2,1)}, u32[]{:S(2)}) copy-start(bf16[3,8,4224]{2,1,0:T(8,128)(2,1)} %get-tuple-element.39) | copy-start | bytes 608260
  2.9 13.4 %copy-start.10 = (bf16[3,8,4224]{2,1,0:T(8,128)(2,1)S(1)}, bf16[3,8,4224]{2,1,0:T(8,128)(2,1)}, u32[]{:S(2)}) copy-start(bf16[3,8,4224]{2,1,0:T(8,128)(2,1)} %get-tuple-element.36.refs_0_) | copy-start | bytes 608260
  5.6 87.2 %all-to-all-start.1 = ((bf16[4,192,1024]{2,1,0:T(8,128)(2,1)}), bf16[4,192,1024]{2,1,0:T(8,128)(2,1)S(1)}, u32[]{:S(2)}, u32[]{:S(2)}) async-start(bf16[4,192,1024]{2,1,0:T(8,128)(2,1)} %broadcast_in_dim.8), calls=%async_computation.1 | async-start | bytes 3145728 | tf_op jit(solution)/shard_map/all_to_all | solution.py:521
  11.9 31.0 %collective-permute-start = (bf16[3,8,4224]{2,1,0:T(8,128)(2,1)S(1)}, bf16[3,8,4224]{2,1,0:T(8,128)(2,1)S(1)}, u32[]{:S(2)}, u32[]{:S(2)}) collective-permute-start(bf16[3,8,4224]{2,1,0:T(8,128)(2,1)S(1)} %copy-done.22), channel_id=1, source_target_pairs={{0,8},{8,0},{16,24},{24,16},{1,9},{9,1},{17,25},{25,17},{2,10},{10... | collective-permute-start | bytes 608264 | tf_op jit(solution)/shard_map/ppermute | solution.py:457
  14.0 49.0 %collective-permute-start.1 = (bf16[3,8,4224]{2,1,0:T(8,128)(2,1)S(1)}, bf16[3,8,4224]{2,1,0:T(8,128)(2,1)S(1)}, u32[]{:S(2)}, u32[]{:S(2)}) collective-permute-start(bf16[3,8,4224]{2,1,0:T(8,128)(2,1)S(1)} %copy-done.21), channel_id=1, source_target_pairs={{0,16},{8,24},{16,0},{24,8},{1,17},{9,25},{17,1},{25,9},{2,18},{10... | collective-permute-start | bytes 608264 | tf_op jit(solution)/shard_map/ppermute | solution.py:457
  16.3 46.7 %collective-permute-start.2 = (bf16[3,8,4224]{2,1,0:T(8,128)(2,1)S(1)}, bf16[3,8,4224]{2,1,0:T(8,128)(2,1)S(1)}, u32[]{:S(2)}, u32[]{:S(2)}) collective-permute-start(bf16[3,8,4224]{2,1,0:T(8,128)(2,1)S(1)} %copy-done.20), channel_id=1, source_target_pairs={{0,24},{8,16},{16,8},{24,0},{1,25},{9,17},{17,9},{25,1},{2,26},{10... | collective-permute-start | bytes 608264 | tf_op jit(solution)/shard_map/ppermute | solution.py:457
  42.9 27.0 %copy-start.11 = (bf16[3,8,4224]{2,1,0:T(8,128)(2,1)}, bf16[3,8,4224]{2,1,0:T(8,128)(2,1)S(1)}, u32[]{:S(2)}) copy-start(bf16[3,8,4224]{2,1,0:T(8,128)(2,1)S(1)} %collective-permute-done.refs_1_) | copy-start | bytes 608260
  63.0 6.9 %copy-start.12 = (bf16[3,8,4224]{2,1,0:T(8,128)(2,1)}, bf16[3,8,4224]{2,1,0:T(8,128)(2,1)S(1)}, u32[]{:S(2)}) copy-start(bf16[3,8,4224]{2,1,0:T(8,128)(2,1)S(1)} %collective-permute-done.1.refs_2_) | copy-start | bytes 608260
  63.0 6.9 %copy-start.13 = (bf16[3,8,4224]{2,1,0:T(8,128)(2,1)}, bf16[3,8,4224]{2,1,0:T(8,128)(2,1)S(1)}, u32[]{:S(2)}) copy-start(bf16[3,8,4224]{2,1,0:T(8,128)(2,1)S(1)} %collective-permute-done.2.refs_3_) | copy-start | bytes 608260
  63.1 6.8 %copy-start.4 = (bf16[96,2176]{1,0:T(8,128)(2,1)}, bf16[96,2176]{1,0:T(8,128)(2,1)S(1)}, u32[]{:S(2)}) copy-start(bf16[96,2176]{1,0:T(8,128)(2,1)S(1)} %maximum_bitcast_fusion.refs_4_) | copy-start | bytes 1253380
  63.1 9.6 %collective-permute-start.3 = (bf16[96,2176]{1,0:T(8,128)(2,1)S(1)}, bf16[96,2176]{1,0:T(8,128)(2,1)S(1)}, u32[]{:S(2)}, u32[]{:S(2)}) collective-permute-start(bf16[96,2176]{1,0:T(8,128)(2,1)S(1)} %maximum_bitcast_fusion.refs_4_), channel_id=1, source_target_pairs={{0,2},{1,3},{2,0},{3,1},{4,6},{5,7},{6,4},{7,5},{8,10},{9,11},{10,... | collective-permute-start | bytes 1253384 | tf_op jit(solution)/shard_map/ppermute | solution.py:457
  64.7 9.7 %collective-permute-start.4 = (bf16[96,2176]{1,0:T(8,128)(2,1)S(1)}, bf16[96,2176]{1,0:T(8,128)(2,1)S(1)}, u32[]{:S(2)}, u32[]{:S(2)}) collective-permute-start(bf16[96,2176]{1,0:T(8,128)(2,1)S(1)} %maximum_bitcast_fusion.refs_4_), channel_id=1, source_target_pairs={{0,4},{1,5},{2,6},{3,7},{4,0},{5,1},{6,2},{7,3},{8,12},{9,13},{10,... | collective-permute-start | bytes 1253384 | tf_op jit(solution)/shard_map/ppermute | solution.py:457
  66.2 8.2 %collective-permute-start.5 = (bf16[96,2176]{1,0:T(8,128)(2,1)S(1)}, bf16[96,2176]{1,0:T(8,128)(2,1)S(1)}, u32[]{:S(2)}, u32[]{:S(2)}) collective-permute-start(bf16[96,2176]{1,0:T(8,128)(2,1)S(1)} %maximum_bitcast_fusion.refs_4_), channel_id=1, source_target_pairs={{0,1},{1,0},{2,3},{3,2},{4,5},{5,4},{6,7},{7,6},{8,9},{9,8},{10,11... | collective-permute-start | bytes 1253384 | tf_op jit(solution)/shard_map/ppermute | solution.py:457
  72.7 11.0 %copy-start.6 = (bf16[96,2176]{1,0:T(8,128)(2,1)}, bf16[96,2176]{1,0:T(8,128)(2,1)S(1)}, u32[]{:S(2)}) copy-start(bf16[96,2176]{1,0:T(8,128)(2,1)S(1)} %collective-permute-done.3.refs_6_) | copy-start | bytes 1253380
  74.4 9.4 %copy-start.7 = (bf16[96,2176]{1,0:T(8,128)(2,1)}, bf16[96,2176]{1,0:T(8,128)(2,1)S(1)}, u32[]{:S(2)}) copy-start(bf16[96,2176]{1,0:T(8,128)(2,1)S(1)} %collective-permute-done.4.refs_8_) | copy-start | bytes 1253380
  74.4 9.4 %copy-start.14 = (bf16[96,2176]{1,0:T(8,128)(2,1)}, bf16[96,2176]{1,0:T(8,128)(2,1)S(1)}, u32[]{:S(2)}) copy-start(bf16[96,2176]{1,0:T(8,128)(2,1)S(1)} %collective-permute-done.5.refs_5_) | copy-start | bytes 1253380
  74.4 5.9 %collective-permute-start.8 = (bf16[48,2176]{1,0:T(8,128)(2,1)S(1)}, bf16[48,2176]{1,0:T(8,128)(2,1)S(1)}, u32[]{:S(2)}, u32[]{:S(2)}) collective-permute-start(bf16[48,2176]{1,0:T(8,128)(2,1)S(1)} %slice.22), channel_id=1, source_target_pairs={{0,4},{1,5},{2,6},{3,7},{4,0},{5,1},{6,2},{7,3},{8,12},{9,13},{10,... | collective-permute-start | bytes 626696 | tf_op jit(solution)/shard_map/ppermute | solution.py:457
  76.0 5.9 %collective-permute-start.9 = (bf16[48,2176]{1,0:T(8,128)(2,1)S(1)}, bf16[48,2176]{1,0:T(8,128)(2,1)S(1)}, u32[]{:S(2)}, u32[]{:S(2)}) collective-permute-start(bf16[48,2176]{1,0:T(8,128)(2,1)S(1)} %slice.23), channel_id=1, source_target_pairs={{0,2},{1,3},{2,0},{3,1},{4,6},{5,7},{6,4},{7,5},{8,10},{9,11},{10,... | collective-permute-start | bytes 626696 | tf_op jit(solution)/shard_map/ppermute | solution.py:457
  76.6 5.4 %collective-permute-start.6 = (bf16[96,2176]{1,0:T(8,128)(2,1)S(1)}, bf16[96,2176]{1,0:T(8,128)(2,1)S(1)}, u32[]{:S(2)}, u32[]{:S(2)}) collective-permute-start(bf16[96,2176]{1,0:T(8,128)(2,1)S(1)} %collective-permute-done.3.refs_6_), channel_id=1, source_target_pairs={{0,1},{1,0},{2,3},{3,2},{4,5},{5,4},{6,7},{7,6},{8,9},{9,8},{10,11... | collective-permute-start | bytes 1253384 | tf_op jit(solution)/shard_map/ppermute | solution.py:457
  76.6 5.4 %collective-permute-start.7 = (bf16[96,2176]{1,0:T(8,128)(2,1)S(1)}, bf16[96,2176]{1,0:T(8,128)(2,1)S(1)}, u32[]{:S(2)}, u32[]{:S(2)}) collective-permute-start(bf16[96,2176]{1,0:T(8,128)(2,1)S(1)} %collective-permute-done.4.refs_8_), channel_id=1, source_target_pairs={{0,1},{1,0},{2,3},{3,2},{4,5},{5,4},{6,7},{7,6},{8,9},{9,8},{10,11... | collective-permute-start | bytes 1253384 | tf_op jit(solution)/shard_map/ppermute | solution.py:457
  80.3 3.5 %copy-start.8 = (bf16[48,2176]{1,0:T(8,128)(2,1)}, bf16[48,2176]{1,0:T(8,128)(2,1)S(1)}, u32[]{:S(2)}) copy-start(bf16[48,2176]{1,0:T(8,128)(2,1)S(1)} %collective-permute-done.8.refs_10_) | copy-start | bytes 626692
  81.9 1.9 %copy-start.9 = (bf16[48,2176]{1,0:T(8,128)(2,1)}, bf16[48,2176]{1,0:T(8,128)(2,1)S(1)}, u32[]{:S(2)}) copy-start(bf16[48,2176]{1,0:T(8,128)(2,1)S(1)} %collective-permute-done.9.refs_11_) | copy-start | bytes 626692
  81.9 1.8 collective-permute-start.10
  82.0 1.8 copy-start.15
  82.0 1.8 copy-start.16
  83.8 0.8 copy-start.17
  92.9 5.0 %copy-start.5 = (bf16[4,192,1024]{2,1,0:T(8,128)(2,1)}, bf16[4,192,1024]{2,1,0:T(8,128)(2,1)S(1)}, u32[]{:S(2)}) copy-start(bf16[4,192,1024]{2,1,0:T(8,128)(2,1)S(1)} %all-to-all-done.1.refs_4_) | copy-start | bytes 4718596
  92.9 17.2 %all-to-all-start = ((f32[32,2,128]{2,1,0:T(2,128)}), f32[32,2,128]{2,1,0:T(2,128)S(1)}, u32[]{:S(2)}, u32[]{:S(2)}) async-start(f32[32,2,128]{2,1,0:T(2,128)} %get-tuple-element.46), calls=%async_computation | async-start | bytes 65536 | tf_op jit(solution)/shard_map/all_to_all | solution.py:30
  110.0 18.4 %copy-start.1 = (bf16[32,16,128]{2,1,0:T(8,128)(2,1)S(1)}, bf16[32,16,128]{2,1,0:T(8,128)(2,1)}, u32[]{:S(2)}) copy-start(bf16[32,16,128]{2,1,0:T(8,128)(2,1)} %get-tuple-element.43.refs_0_.msgs_ref) | copy-start | bytes 393220
  110.0 18.4 %copy-start.2 = (f32[16,128]{1,0:T(8,128)S(1)}, f32[16,128]{1,0:T(8,128)}, u32[]{:S(2)}) copy-start(f32[16,128]{1,0:T(8,128)} %get-tuple-element.52.gap_ref) | copy-start | bytes 24580
  110.1 18.4 %copy-start.3 = (f32[16,128]{1,0:T(8,128)S(1)}, f32[16,128]{1,0:T(8,128)}, u32[]{:S(2)}) copy-start(f32[16,128]{1,0:T(8,128)} %get-tuple-element.53.own_ref) | copy-start | bytes 24580
  110.1 0.6 copy-start.19
  142.1 15.0 %all-to-all-start.4 = ((f32[32,2,128]{2,1,0:T(2,128)}), f32[32,2,128]{2,1,0:T(2,128)S(1)}, u32[]{:S(2)}, u32[]{:S(2)}) async-start(f32[32,2,128]{2,1,0:T(2,128)} %get-tuple-element.55), calls=%async_computation.4 | async-start | bytes 65536 | tf_op jit(solution)/shard_map/all_to_all | solution.py:30
  157.1 18.4 %copy-start = (bf16[32,16,128]{2,1,0:T(8,128)(2,1)S(1)}, bf16[32,16,128]{2,1,0:T(8,128)(2,1)}, u32[]{:S(2)}) copy-start(bf16[32,16,128]{2,1,0:T(8,128)(2,1)} %all_to_all.36.refs_0_.msgs_ref) | copy-start | bytes 393220
  157.1 0.6 copy-start.18

commit v16 on v15

--- a/solution.py
+++ b/solution.py
@@ -67,7 +67,7 @@
     out = []
     for i in range(count):
         mine = (row == 0) & (lane >= HALF + 3 * i) & (lane < HALF + 3 * i + 3)
-        out.append(jnp.sum(jnp.where(mine, tile, 0.0)))
+        out.append(jnp.sum(jnp.where(mine, tile, 0.0), keepdims=True))
     return out
 
 
@@ -260,17 +260,14 @@
 
 def direct_kernel(n_ka, tile, scale, *refs):
     turned_ref, scr_ref, rows_ref, qx_ref, refs = refs[0], refs[1], refs[2], refs[3], refs[4:]
-    cond_ref, refs = refs[0], refs[1:]
+    cond_refs, refs = refs[:n_ka], refs[n_ka:]
     di_ref, qx, turned, conds, scrs, vals, mixed, kern, folded = refs[:9]
     qx_sem, cond_sems, row_sem, chunk_sems = refs[9:]
     nu, mu = scr_ref.shape
     quad = 2 * LANES
     qx_copy = pltpu.make_async_copy(qx_ref, qx, qx_sem.at[0])
     cond_copies = [
-        pltpu.make_async_copy(
-            cond_ref.at[jnp.bitwise_xor(lax.axis_index("ka"), j)], conds.at[j], cond_sems.at[j]
-        )
-        for j in range(n_ka)
+        pltpu.make_async_copy(ref, conds.at[j], cond_sems.at[j]) for j, ref in enumerate(cond_refs)
     ]
     turned_copies, scr_copies = [], []
     for i in range(nu // tile):
@@ -379,9 +376,9 @@
     state_ref[0] = cur
     state_ref[1] = resid
     state_ref[2] = inter
-    coef_ref[0] = shift
-    coef_ref[1] = square
-    coef_ref[2] = gap_sq * inv * inv
+    coef_ref[0] = shift[0, 0]
+    coef_ref[1] = square[0, 0]
+    coef_ref[2] = (gap_sq * inv * inv)[0, 0]
     sums = [
         jnp.sum(cur * resid),
         jnp.sum(resid * resid),
@@ -404,10 +401,10 @@
     resid = (gap_ref[...] - shift) * cur + inter - beta * prev
     out_ref[0] = cur
     out_ref[1] = resid
-    coef_out[0] = alpha
-    coef_out[1] = beta
-    coef_out[2] = shift
-    coef_out[3] = square
+    coef_out[0] = alpha[0, 0]
+    coef_out[1] = beta[0, 0]
+    coef_out[2] = shift[0, 0]
+    coef_out[3] = square[0, 0]
     dims = msg_ref.shape[:1] + msg_ref.shape[2:]
     msg_ref[:, 0, :] = jnp.full(dims, jnp.sum(cur * resid), F32)
     msg_ref[:, 1, :] = jnp.full(dims, jnp.sum(resid * resid), F32)
@@ -415,13 +412,13 @@
 
 def finish_kernel(count_all, msgs_ref, state_ref, coef_ref, out_ref, coeffs_ref):
     sums = jnp.sum(msgs_ref[...], axis=0)
-    alpha, d, mean_sq = shifted(count_all, coef_ref[2], coef_ref[3], sums[0, 0], sums[1, 0])
+    alpha, d, mean_sq = shifted(count_all, coef_ref[2], coef_ref[3], sums[0:1, 0:1], sums[1:2, 0:1])
     beta = jnp.sqrt(mean_sq + 1e-06)
     own = (state_ref[1] - d * state_ref[0]) / beta
     coeffs_ref[0] = coef_ref[0]
-    coeffs_ref[1] = alpha
+    coeffs_ref[1] = alpha[0, 0]
     coeffs_ref[2] = coef_ref[1]
-    coeffs_ref[3] = beta
+    coeffs_ref[3] = beta[0, 0]
     for kl in range(out_ref.shape[0]):
         tile = own[kl // 2 * ROWS : (kl // 2 + 1) * ROWS, :]
         other = pltpu.roll(tile, HALF, axis=1)
@@ -467,10 +464,10 @@
     by_x, by_y, core, others = lax.optimization_barrier((by_x, by_y, core, others))
     diag = [move(by_x[:half], 4), move(by_y[half:], 2)]
     near_x, near_y = move(by_x, 1), move(by_y, 1)
-    far = move(jnp.concatenate(diag, axis=0), 1)
-    arrays = [own_piece, core, by_x, near_x, by_y, near_y, diag[0], diag[1], far]
+    far = [move(part, 1) for part in diag]
+    arrays = [own_piece, core, by_x, near_x, by_y, near_y] + diag + far
     parts = tuple(((i, 0, rows),) for i in range(6))
-    parts += (((6, 0, half), (7, 0, half)), ((8, 0, rows),))
+    parts += (((6, 0, half), (7, 0, half)), ((8, 0, half), (9, 0, half)))
     return arrays, parts, others
 
 
@@ -517,8 +514,7 @@
     val_cut = val_cut.reshape(piece_rows, wide)
     cond_local = lax.dynamic_slice_in_dim(cond_orb, base, mu_blk, 2)
     cond_local = cond_local.reshape(k_dev * n_cond, mu_blk)
-    cond_wide = jnp.broadcast_to(cond_local[None], (n_ka,) + cond_local.shape)
-    cond_pts = lax.all_to_all(cond_wide, "ka", split_axis=0, concat_axis=0, tiled=True)
+    cond_pts = [cond_local] + [swap(cond_local, "ka", j) for j in range(1, n_ka)]
 
     chunk, tile = 1024, nu_blk
     rows_all, conds_all = k_points * nv_blk * n_band, k_points * n_cond
@@ -533,6 +529,7 @@
         moved=8 * MIB,
     )(screened)
     pieces, parts, scr_turned = plane_pieces(val_cut, scr_turned)
+    pieces, cond_pts[1:-1] = lax.optimization_barrier((pieces, cond_pts[1:-1]))
     val_rows, val_turned, val_own, cond_own, msgs = call(
         functools.partial(order_kernel, parts, n_ka),
         "order",
@@ -585,7 +582,7 @@
             functools.partial(direct_kernel, n_ka, tile, scale),
             "direct",
             shape_of((pairs, LANES, LANES)),
-            [ANY] * 5,
+            [ANY] * (4 + n_ka),
             VMEM,
             [
                 pltpu.VMEM((quads, 2 * LANES, 2 * LANES), BF),
@@ -603,7 +600,7 @@
             ],
             flops=4 * mu_blk * nu_blk * conds_all,
             moved=12 * MIB,
-        )(val_turned, scr_turned, val_rows, qx, cond_pts)
+        )(val_turned, scr_turned, val_rows, qx, *cond_pts)
         summed = call(
             functools.partial(exchange_kernel, cfg, chunk, scale),
             "exchange",

time: 188 us -> 160 us (0.85)
  waiting for transfers between devices: 57.5 us -> 30 us
    ppermute x11 -> x15, waiting for transfers between devices: 57.5 us -> 30 us  [swap(): lax.ppermute(block, axis, [(i, i ^ d) for i in range(lax.axis_size(axis))])]
    ppermute x11 -> x15, starting transfers between devices: 10.3 us -> 17.5 us  [swap(): lax.ppermute(block, axis, [(i, i ^ d) for i in range(lax.axis_size(axis))])]
    all_to_all x1 -> x0, starting transfers between devices: 6.32 us -> none  [kernel_path(): lax.all_to_all(cond_wide, 'ka', split_axis=0, concat_axis=0, tiled=True)]
    all_to_all x2, starting transfers between devices: 7.77 us -> 5.48 us  [exchange_all(): return lax.all_to_all(parts, AXES, split_axis=0, concat_axis=0, tiled=True)]
  transfers between devices with their start and end apart: 14 -> 17, of which waited for: 7 -> 6; matrix products, arithmetic and copies ran while one was open for 0% -> 1% of each run, Pallas kernels for 19% -> 23%
where the time goes in v16:
time: 160 us; the launch traced here: 159 us
  Pallas kernels  51.9 us (32%)
  blocking collectives  47.4 us (30%)
  waiting for transfers between devices  30 us (19%)
  starting transfers between devices  23 us (14%)
  local copies, waits for them, and re-layouts  5.71 us (4%)
    all_to_all x4, blocking collectives, exchange_all(): return lax.all_to_all(parts, AXES, split_axis=0, concat_axis=0, tiled=True)  47.4 us
    ppermute x15, waiting for transfers between devices, swap(): lax.ppermute(block, axis, [(i, i ^ d) for i in range(lax.axis_size(axis))])  30 us
    pallas_call x2, Pallas kernels, kernel_path(): call(functools.partial(direct_kernel, n_ka, tile, scale), 'direct', shape...  24.3 us
    ppermute x15, starting transfers between devices, swap(): lax.ppermute(block, axis, [(i, i ^ d) for i in range(lax.axis_size(axis))])  17.5 us
    pallas_call x2, Pallas kernels, kernel_path(): call(functools.partial(exchange_kernel, cfg, chunk, scale), 'exchange', m...  7.78 us
    pallas_call x1, Pallas kernels, kernel_path(): call(functools.partial(order_kernel, parts, n_ka), 'order', (shape_of((ro...  6.1 us
    all_to_all x2, starting transfers between devices, exchange_all(): return lax.all_to_all(parts, AXES, split_axis=0, concat_axis=0, tiled=True)  5.48 us
    pallas_call x2, Pallas kernels, kernel_path(): call(functools.partial(density_kernel, cfg), 'density', (shape_of((quads,...  4.29 us
  transfers between devices with their start and end apart: 17, of which 6 were waited for; matrix products, arithmetic and copies ran while one was open for 1% of the time, Pallas kernels for 23%

profile of v16, /device:TPU:0, one launch (start us, length us, event | category | flops | bytes accessed | tf_op | source)
XLA Modules:
  0.0 159.4 jit_solution(5197826354175108274)
XLA Ops:
  0.6 2.3 %pack.1 = (f32[16,128]{1,0:T(8,128)}, f32[16,128]{1,0:T(8,128)}, bf16[3,8,4224]{2,1,0:T(8,128)(2,1)}, bf16[3,8,4224]{2,1,0:T(8,128)(2,1)}, bf16[3,8,4224]{2,1,0:T(8,128)(2,1)}, /*index=5*/bf16[3,8,4224]{2,1,0:T(8,128)(2,1)}) custom-call(f32[3,512]{1,0:T(4,128)} %refs_0_.1, f32[3,64]{1,0:T(4,128)} %refs_1_.1, f32[3,8]{1,0:T(4,128)} %refs_2_.3, ...), custom_call_target="tpu_custom_call" | custom-call | tf_op jit(solution)/shard_map/pack/pallas_call | solution.py:495
  2.9 3.1 %collective-permute-start = (bf16[3,8,4224]{2,1,0:T(8,128)(2,1)}, bf16[3,8,4224]{2,1,0:T(8,128)(2,1)S(1)}, u32[]{:S(2)}, u32[]{:S(2)}) collective-permute-start(bf16[3,8,4224]{2,1,0:T(8,128)(2,1)} %get-tuple-element.49), channel_id=1, source_target_pairs={{0,8},{8,0},{16,24},{24,16},{1,9},{9,1},{17,25},{25,17},{2,10},{10... | collective-permute-start | bytes 608264 | tf_op jit(solution)/shard_map/ppermute | solution.py:454
  6.0 2.6 %collective-permute-start.1 = (bf16[3,8,4224]{2,1,0:T(8,128)(2,1)}, bf16[3,8,4224]{2,1,0:T(8,128)(2,1)S(1)}, u32[]{:S(2)}, u32[]{:S(2)}) collective-permute-start(bf16[3,8,4224]{2,1,0:T(8,128)(2,1)} %get-tuple-element.50), channel_id=1, source_target_pairs={{0,16},{8,24},{16,0},{24,8},{1,17},{9,25},{17,1},{25,9},{2,18},{10... | collective-permute-start | bytes 608264 | tf_op jit(solution)/shard_map/ppermute | solution.py:454
  8.6 0.0 collective-permute-start.2
  8.6 0.9 slice.18
  9.5 5.3 %collective-permute-done.refs_1_ = bf16[3,8,4224]{2,1,0:T(8,128)(2,1)S(1)} collective-permute-done((bf16[3,8,4224]{2,1,0:T(8,128)(2,1)}, bf16[3,8,4224]{2,1,0:T(8,128)(2,1)S(1)}, u32[]{:S(2)}, u32[]{:S(2)}) %collective-permute-start) | collective-permute-done | bytes 202784 | tf_op jit(solution)/shard_map/ppermute | solution.py:454
  14.8 8.9 %collective-permute-done.1.refs_2_ = bf16[3,8,4224]{2,1,0:T(8,128)(2,1)S(1)} collective-permute-done((bf16[3,8,4224]{2,1,0:T(8,128)(2,1)}, bf16[3,8,4224]{2,1,0:T(8,128)(2,1)S(1)}, u32[]{:S(2)}, u32[]{:S(2)}) %collective-permute-start.1) | collective-permute-done | bytes 202784 | tf_op jit(solution)/shard_map/ppermute | solution.py:454
  23.8 0.0 collective-permute-done.2.refs_3_
  23.8 0.1 maximum_bitcast_fusion.refs_4_
  23.9 1.6 collective-permute-start.3
  25.4 1.5 collective-permute-start.4
  27.0 1.2 constant_dynamic-slice_fusion
  28.2 3.5 %collective-permute-start.12 = (bf16[192,1024]{1,0:T(8,128)(2,1)S(1)}, bf16[192,1024]{1,0:T(8,128)(2,1)S(1)}, u32[]{:S(2)}, u32[]{:S(2)}) collective-permute-start(bf16[192,1024]{1,0:T(8,128)(2,1)S(1)} %bitcast.3), channel_id=1, source_target_pairs={{0,8},{8,0},{16,24},{24,16},{1,9},{9,1},{17,25},{25,17},{2,10},{10... | collective-permute-start | bytes 1179656 | tf_op jit(solution)/shard_map/ppermute | solution.py:454
  31.7 1.1 collective-permute-start.13
  32.8 3.7 %turn.1.refs_1_ = bf16[2048,1024]{1,0:T(8,128)(2,1)} custom-call(bf16[1024,2048]{1,0:T(8,128)(2,1)} %scr_ref.1), custom_call_target="tpu_custom_call" | custom-call | bytes 8388608 | tf_op jit(solution)/shard_map/turn/pallas_call | solution.py:521
  36.5 0.0 collective-permute-done.3.refs_6_
  36.6 0.6 collective-permute-start.8
  37.2 0.6 collective-permute-start.9
  37.8 12.0 %collective-permute-done.12.refs_5_ = bf16[192,1024]{1,0:T(8,128)(2,1)S(1)} collective-permute-done((bf16[192,1024]{1,0:T(8,128)(2,1)S(1)}, bf16[192,1024]{1,0:T(8,128)(2,1)S(1)}, u32[]{:S(2)}, u32[]{:S(2)}) %collective-permute-start.12) | collective-permute-done | bytes 393248 | tf_op jit(solution)/shard_map/ppermute | solution.py:454
  49.8 2.5 %collective-permute-done.13.refs_6_ = bf16[192,1024]{1,0:T(8,128)(2,1)S(1)} collective-permute-done((bf16[192,1024]{1,0:T(8,128)(2,1)S(1)}, bf16[192,1024]{1,0:T(8,128)(2,1)S(1)}, u32[]{:S(2)}, u32[]{:S(2)}) %collective-permute-start.13) | collective-permute-done | bytes 393248 | tf_op jit(solution)/shard_map/ppermute | solution.py:454
  52.3 2.5 %collective-permute-start.14 = (bf16[192,1024]{1,0:T(8,128)(2,1)S(1)}, bf16[192,1024]{1,0:T(8,128)(2,1)S(1)}, u32[]{:S(2)}, u32[]{:S(2)}) collective-permute-start(bf16[192,1024]{1,0:T(8,128)(2,1)S(1)} %bitcast.5), channel_id=1, source_target_pairs={{0,24},{8,16},{16,8},{24,0},{1,25},{9,17},{17,9},{25,1},{2,26},{10... | collective-permute-start | bytes 1179656 | tf_op jit(solution)/shard_map/ppermute | solution.py:454
  54.8 0.5 collective-permute-start.11
  55.3 0.9 collective-permute-done.10.refs_12_
  56.3 0.3 collective-permute-done.11.refs_13_
  56.6 0.3 copy-done.16
  56.9 0.3 copy-done.17
  57.2 0.2 copy-done.11
  57.4 0.8 copy-done.12
  58.2 6.1 %order.1 = (bf16[768,2048]{1,0:T(8,128)(2,1)}, bf16[2048,768]{1,0:T(8,128)(2,1)}, bf16[768,256]{1,0:T(8,128)(2,1)}, bf16[768,256]{1,0:T(8,128)(2,1)}, bf16[32,16,128]{2,1,0:T(8,128)(2,1)}) custom-call(bf16[3,8,4224]{2,1,0:T(8,128)(2,1)} %get-tuple-element.48.refs_0_, bf16[3,8,4224]{2,1,0:T(8,128)(2,1)} %copy-done.7, bf16[3,8,4224]{2,1,0:T(8,128)(2,1)} %copy-done.8, ...), custom_call_target="tpu_custom_call" | custom-call | bytes 9437184 | tf_op jit(solution)/shard_map/order/pallas_call | solution.py:533
  64.3 2.1 %density.2 = (bf16[3,256,256]{2,1,0:T(8,128)(2,1)}, f32[32,2,128]{2,1,0:T(2,128)}) custom-call(bf16[32,16,128]{2,1,0:T(8,128)(2,1)} %get-tuple-element.66.refs_0_.msgs_ref, bf16[768,256]{1,0:T(8,128)(2,1)} %get-tuple-element.67.refs_1_.refs_3_, bf16[768,256]{1,0:T(8,128)(2,1)} %get-tuple-element.68.refs_2_.refs_4_), custom_call_target="tpu_custom_call" | custom-call | tf_op jit(solution)/shard_map/density/pallas_call | solution.py:563
  66.5 2.7 %all-to-all-start = ((f32[32,2,128]{2,1,0:T(2,128)}), f32[32,2,128]{2,1,0:T(2,128)S(1)}, u32[]{:S(2)}, u32[]{:S(2)}) async-start(f32[32,2,128]{2,1,0:T(2,128)} %get-tuple-element.69), calls=%async_computation | async-start | bytes 65536 | tf_op jit(solution)/shard_map/all_to_all | solution.py:30
  69.2 0.7 copy-done.22
  69.9 12.2 %direct.2.refs_1_ = f32[6,128,128]{2,1,0:T(8,128)} custom-call(bf16[2048,768]{1,0:T(8,128)(2,1)} %get-tuple-element.70.refs_0_, bf16[2048,1024]{1,0:T(8,128)(2,1)} %turn.1.refs_1_, bf16[768,2048]{1,0:T(8,128)(2,1)} %get-tuple-element.72.refs_2_, bf16[3,256,256]{2,1,0:T(8,128)(2,1)} %get-tuple-element.73.refs_3_, bf16[192,1024]{1,0:T(8,128)(2,1)} %bitcast.6, ...), custom_call_target="tpu_custom_call" | custom-call | flops 6442450944 | bytes 12582912 | tf_op jit(solution)/shard_map/direct/pallas_call | solution.py:581
  82.1 0.0 copy-start.3
  82.1 0.6 copy-done.19
  82.7 3.9 %exchange.2 = bf16[32,16,128]{2,1,0:T(8,128)(2,1)} custom-call(f32[32,2,128]{2,1,0:T(2,128)} %copy-done.19, f32[6,128,128]{2,1,0:T(8,128)} %direct.2.refs_1_, bf16[256,8192]{1,0:T(8,128)(2,1)} %refs_2_.5, bf16[768,256]{1,0:T(8,128)(2,1)} %get-tuple-element.67.refs_1_.refs_3_, bf16[768,256]{1,0:T(8,128)(2,1)} %get-tuple-element.68.refs_2_.refs_4_), custom_call_target="tpu_custom_call" | custom-call | tf_op jit(solution)/shard_map/exchange/pallas_call | solution.py:604
  86.6 13.9 %all_to_all.30.recv_ref = bf16[32,16,128]{2,1,0:T(8,128)(2,1)S(1)} all-to-all(bf16[32,16,128]{2,1,0:T(8,128)(2,1)} %exchange.2), channel_id=1, replica_groups=mesh['ka'=4,'band'=8] {'ka','band'}, dimensions={0} | all-to-all | bytes 262144 | tf_op jit(solution)/shard_map/all_to_all | solution.py:30
  100.5 0.8 first_owner.1
  101.4 10.6 %all_to_all.31.refs_0_.msgs_ref = bf16[32,16,128]{2,1,0:T(8,128)(2,1)} all-to-all(bf16[32,16,128]{2,1,0:T(8,128)(2,1)S(1)} %get-tuple-element.78), channel_id=1, replica_groups=mesh['ka'=4,'band'=8] {'ka','band'}, dimensions={0} | all-to-all | bytes 262144 | tf_op jit(solution)/shard_map/all_to_all | solution.py:30
  112.0 2.1 %density.3 = (bf16[3,256,256]{2,1,0:T(8,128)(2,1)}, f32[32,2,128]{2,1,0:T(2,128)}) custom-call(bf16[32,16,128]{2,1,0:T(8,128)(2,1)} %all_to_all.31.refs_0_.msgs_ref, bf16[768,256]{1,0:T(8,128)(2,1)} %get-tuple-element.67.refs_1_.refs_3_, bf16[768,256]{1,0:T(8,128)(2,1)} %get-tuple-element.68.refs_2_.refs_4_), custom_call_target="tpu_custom_call" | custom-call | tf_op jit(solution)/shard_map/density/pallas_call | solution.py:563
  114.1 2.8 %all-to-all-start.3 = ((f32[32,2,128]{2,1,0:T(2,128)}), f32[32,2,128]{2,1,0:T(2,128)S(1)}, u32[]{:S(2)}, u32[]{:S(2)}) async-start(f32[32,2,128]{2,1,0:T(2,128)} %get-tuple-element.79), calls=%async_computation.3 | async-start | bytes 65536 | tf_op jit(solution)/shard_map/all_to_all | solution.py:30
  116.9 12.2 %direct.3.refs_1_ = f32[6,128,128]{2,1,0:T(8,128)} custom-call(bf16[2048,768]{1,0:T(8,128)(2,1)} %get-tuple-element.70.refs_0_, bf16[2048,1024]{1,0:T(8,128)(2,1)} %turn.1.refs_1_, bf16[768,2048]{1,0:T(8,128)(2,1)} %get-tuple-element.72.refs_2_, bf16[3,256,256]{2,1,0:T(8,128)(2,1)} %get-tuple-element.80.refs_3_, bf16[192,1024]{1,0:T(8,128)(2,1)} %bitcast.7, ...), custom_call_target="tpu_custom_call" | custom-call | flops 6442450944 | bytes 12582912 | tf_op jit(solution)/shard_map/direct/pallas_call | solution.py:581
  129.1 0.6 copy-done.18
  129.7 3.9 %exchange.3 = bf16[32,16,128]{2,1,0:T(8,128)(2,1)} custom-call(f32[32,2,128]{2,1,0:T(2,128)} %copy-done.18, f32[6,128,128]{2,1,0:T(8,128)} %direct.3.refs_1_, bf16[256,8192]{1,0:T(8,128)(2,1)} %refs_2_.5, bf16[768,256]{1,0:T(8,128)(2,1)} %get-tuple-element.67.refs_1_.refs_3_, bf16[768,256]{1,0:T(8,128)(2,1)} %get-tuple-element.68.refs_2_.refs_4_), custom_call_target="tpu_custom_call" | custom-call | tf_op jit(solution)/shard_map/exchange/pallas_call | solution.py:604
  133.6 13.9 %all_to_all.32.recv_ref = bf16[32,16,128]{2,1,0:T(8,128)(2,1)S(1)} all-to-all(bf16[32,16,128]{2,1,0:T(8,128)(2,1)} %exchange.3), channel_id=1, replica_groups=mesh['ka'=4,'band'=8] {'ka','band'}, dimensions={0} | all-to-all | bytes 262144 | tf_op jit(solution)/shard_map/all_to_all | solution.py:30
  147.5 1.3 second_owner.1
  148.8 9.0 %all_to_all.33.msgs_ref = f32[32,2,128]{2,1,0:T(2,128)S(1)} all-to-all(f32[32,2,128]{2,1,0:T(2,128)S(1)} %get-tuple-element.83), channel_id=1, replica_groups=mesh['ka'=4,'band'=8] {'ka','band'}, dimensions={0} | all-to-all | bytes 65536 | tf_op jit(solution)/shard_map/all_to_all | solution.py:30
  157.9 1.3 finish.1
  (56 shorter events, 0.2 us)
Async XLA Ops:
  2.9 11.9 %collective-permute-start = (bf16[3,8,4224]{2,1,0:T(8,128)(2,1)}, bf16[3,8,4224]{2,1,0:T(8,128)(2,1)S(1)}, u32[]{:S(2)}, u32[]{:S(2)}) collective-permute-start(bf16[3,8,4224]{2,1,0:T(8,128)(2,1)} %get-tuple-element.49), channel_id=1, source_target_pairs={{0,8},{8,0},{16,24},{24,16},{1,9},{9,1},{17,25},{25,17},{2,10},{10... | collective-permute-start | bytes 608264 | tf_op jit(solution)/shard_map/ppermute | solution.py:454
  6.0 17.8 %collective-permute-start.1 = (bf16[3,8,4224]{2,1,0:T(8,128)(2,1)}, bf16[3,8,4224]{2,1,0:T(8,128)(2,1)S(1)}, u32[]{:S(2)}, u32[]{:S(2)}) collective-permute-start(bf16[3,8,4224]{2,1,0:T(8,128)(2,1)} %get-tuple-element.50), channel_id=1, source_target_pairs={{0,16},{8,24},{16,0},{24,8},{1,17},{9,25},{17,1},{25,9},{2,18},{10... | collective-permute-start | bytes 608264 | tf_op jit(solution)/shard_map/ppermute | solution.py:454
  8.6 15.2 %collective-permute-start.2 = (bf16[3,8,4224]{2,1,0:T(8,128)(2,1)}, bf16[3,8,4224]{2,1,0:T(8,128)(2,1)S(1)}, u32[]{:S(2)}, u32[]{:S(2)}) collective-permute-start(bf16[3,8,4224]{2,1,0:T(8,128)(2,1)} %get-tuple-element.51), channel_id=1, source_target_pairs={{0,24},{8,16},{16,8},{24,0},{1,25},{9,17},{17,9},{25,1},{2,26},{10... | collective-permute-start | bytes 608264 | tf_op jit(solution)/shard_map/ppermute | solution.py:454
  14.8 21.7 %copy-start.7 = (bf16[3,8,4224]{2,1,0:T(8,128)(2,1)}, bf16[3,8,4224]{2,1,0:T(8,128)(2,1)S(1)}, u32[]{:S(2)}) copy-start(bf16[3,8,4224]{2,1,0:T(8,128)(2,1)S(1)} %collective-permute-done.refs_1_) | copy-start | bytes 608260
  23.8 12.7 %copy-start.8 = (bf16[3,8,4224]{2,1,0:T(8,128)(2,1)}, bf16[3,8,4224]{2,1,0:T(8,128)(2,1)S(1)}, u32[]{:S(2)}) copy-start(bf16[3,8,4224]{2,1,0:T(8,128)(2,1)S(1)} %collective-permute-done.1.refs_2_) | copy-start | bytes 608260
  23.8 12.7 %copy-start.9 = (bf16[3,8,4224]{2,1,0:T(8,128)(2,1)}, bf16[3,8,4224]{2,1,0:T(8,128)(2,1)S(1)}, u32[]{:S(2)}) copy-start(bf16[3,8,4224]{2,1,0:T(8,128)(2,1)S(1)} %collective-permute-done.2.refs_3_) | copy-start | bytes 608260
  23.9 12.6 %copy-start.4 = (bf16[96,2176]{1,0:T(8,128)(2,1)}, bf16[96,2176]{1,0:T(8,128)(2,1)S(1)}, u32[]{:S(2)}) copy-start(bf16[96,2176]{1,0:T(8,128)(2,1)S(1)} %maximum_bitcast_fusion.refs_4_) | copy-start | bytes 1253380
  23.9 12.6 %collective-permute-start.3 = (bf16[96,2176]{1,0:T(8,128)(2,1)S(1)}, bf16[96,2176]{1,0:T(8,128)(2,1)S(1)}, u32[]{:S(2)}, u32[]{:S(2)}) collective-permute-start(bf16[96,2176]{1,0:T(8,128)(2,1)S(1)} %maximum_bitcast_fusion.refs_4_), channel_id=1, source_target_pairs={{0,2},{1,3},{2,0},{3,1},{4,6},{5,7},{6,4},{7,5},{8,10},{9,11},{10,... | collective-permute-start | bytes 1253384 | tf_op jit(solution)/shard_map/ppermute | solution.py:454
  25.4 11.1 %collective-permute-start.4 = (bf16[96,2176]{1,0:T(8,128)(2,1)S(1)}, bf16[96,2176]{1,0:T(8,128)(2,1)S(1)}, u32[]{:S(2)}, u32[]{:S(2)}) collective-permute-start(bf16[96,2176]{1,0:T(8,128)(2,1)S(1)} %maximum_bitcast_fusion.refs_4_), channel_id=1, source_target_pairs={{0,4},{1,5},{2,6},{3,7},{4,0},{5,1},{6,2},{7,3},{8,12},{9,13},{10,... | collective-permute-start | bytes 1253384 | tf_op jit(solution)/shard_map/ppermute | solution.py:454
  27.0 9.6 %collective-permute-start.5 = (bf16[96,2176]{1,0:T(8,128)(2,1)S(1)}, bf16[96,2176]{1,0:T(8,128)(2,1)S(1)}, u32[]{:S(2)}, u32[]{:S(2)}) collective-permute-start(bf16[96,2176]{1,0:T(8,128)(2,1)S(1)} %maximum_bitcast_fusion.refs_4_), channel_id=1, source_target_pairs={{0,1},{1,0},{2,3},{3,2},{4,5},{5,4},{6,7},{7,6},{8,9},{9,8},{10,11... | collective-permute-start | bytes 1253384 | tf_op jit(solution)/shard_map/ppermute | solution.py:454
  28.2 24.1 %copy-start.13 = (bf16[3,64,1024]{2,1,0:T(8,128)(2,1)}, bf16[3,64,1024]{2,1,0:T(8,128)(2,1)S(1)}, u32[]{:S(2)}) copy-start(bf16[3,64,1024]{2,1,0:T(8,128)(2,1)S(1)} %constant_dynamic-slice_fusion) | copy-start | bytes 1179652
  28.2 21.6 %collective-permute-start.12 = (bf16[192,1024]{1,0:T(8,128)(2,1)S(1)}, bf16[192,1024]{1,0:T(8,128)(2,1)S(1)}, u32[]{:S(2)}, u32[]{:S(2)}) collective-permute-start(bf16[192,1024]{1,0:T(8,128)(2,1)S(1)} %bitcast.3), channel_id=1, source_target_pairs={{0,8},{8,0},{16,24},{24,16},{1,9},{9,1},{17,25},{25,17},{2,10},{10... | collective-permute-start | bytes 1179656 | tf_op jit(solution)/shard_map/ppermute | solution.py:454
  31.7 20.6 %collective-permute-start.13 = (bf16[192,1024]{1,0:T(8,128)(2,1)S(1)}, bf16[192,1024]{1,0:T(8,128)(2,1)S(1)}, u32[]{:S(2)}, u32[]{:S(2)}) collective-permute-start(bf16[192,1024]{1,0:T(8,128)(2,1)S(1)} %bitcast.4), channel_id=1, source_target_pairs={{0,16},{8,24},{16,0},{24,8},{1,17},{9,25},{17,1},{25,9},{2,18},{10... | collective-permute-start | bytes 1179656 | tf_op jit(solution)/shard_map/ppermute | solution.py:454
  36.5 20.0 %copy-start.5 = (bf16[96,2176]{1,0:T(8,128)(2,1)}, bf16[96,2176]{1,0:T(8,128)(2,1)S(1)}, u32[]{:S(2)}) copy-start(bf16[96,2176]{1,0:T(8,128)(2,1)S(1)} %collective-permute-done.3.refs_6_) | copy-start | bytes 1253380
  36.5 20.0 %copy-start.6 = (bf16[96,2176]{1,0:T(8,128)(2,1)}, bf16[96,2176]{1,0:T(8,128)(2,1)S(1)}, u32[]{:S(2)}) copy-start(bf16[96,2176]{1,0:T(8,128)(2,1)S(1)} %collective-permute-done.4.refs_8_) | copy-start | bytes 1253380
  36.6 20.0 %copy-start.10 = (bf16[96,2176]{1,0:T(8,128)(2,1)}, bf16[96,2176]{1,0:T(8,128)(2,1)S(1)}, u32[]{:S(2)}) copy-start(bf16[96,2176]{1,0:T(8,128)(2,1)S(1)} %collective-permute-done.5.refs_5_) | copy-start | bytes 1253380
  36.6 18.2 %collective-permute-start.8 = (bf16[48,2176]{1,0:T(8,128)(2,1)S(1)}, bf16[48,2176]{1,0:T(8,128)(2,1)S(1)}, u32[]{:S(2)}, u32[]{:S(2)}) collective-permute-start(bf16[48,2176]{1,0:T(8,128)(2,1)S(1)} %slice.22), channel_id=1, source_target_pairs={{0,4},{1,5},{2,6},{3,7},{4,0},{5,1},{6,2},{7,3},{8,12},{9,13},{10,... | collective-permute-start | bytes 626696 | tf_op jit(solution)/shard_map/ppermute | solution.py:454
  37.2 17.6 %collective-permute-start.9 = (bf16[48,2176]{1,0:T(8,128)(2,1)S(1)}, bf16[48,2176]{1,0:T(8,128)(2,1)S(1)}, u32[]{:S(2)}, u32[]{:S(2)}) collective-permute-start(bf16[48,2176]{1,0:T(8,128)(2,1)S(1)} %slice.23), channel_id=1, source_target_pairs={{0,2},{1,3},{2,0},{3,1},{4,6},{5,7},{6,4},{7,5},{8,10},{9,11},{10,... | collective-permute-start | bytes 626696 | tf_op jit(solution)/shard_map/ppermute | solution.py:454
  37.8 18.8 %collective-permute-start.6 = (bf16[96,2176]{1,0:T(8,128)(2,1)S(1)}, bf16[96,2176]{1,0:T(8,128)(2,1)S(1)}, u32[]{:S(2)}, u32[]{:S(2)}) collective-permute-start(bf16[96,2176]{1,0:T(8,128)(2,1)S(1)} %collective-permute-done.3.refs_6_), channel_id=1, source_target_pairs={{0,1},{1,0},{2,3},{3,2},{4,5},{5,4},{6,7},{7,6},{8,9},{9,8},{10,11... | collective-permute-start | bytes 1253384 | tf_op jit(solution)/shard_map/ppermute | solution.py:454
  49.8 19.4 %copy-start.20 = (bf16[192,1024]{1,0:T(8,128)(2,1)}, bf16[192,1024]{1,0:T(8,128)(2,1)S(1)}, u32[]{:S(2)}) copy-start(bf16[192,1024]{1,0:T(8,128)(2,1)S(1)} %collective-permute-done.12.refs_5_) | copy-start | bytes 1179652
  49.8 6.8 %collective-permute-start.7 = (bf16[96,2176]{1,0:T(8,128)(2,1)S(1)}, bf16[96,2176]{1,0:T(8,128)(2,1)S(1)}, u32[]{:S(2)}, u32[]{:S(2)}) collective-permute-start(bf16[96,2176]{1,0:T(8,128)(2,1)S(1)} %collective-permute-done.4.refs_8_), channel_id=1, source_target_pairs={{0,1},{1,0},{2,3},{3,2},{4,5},{5,4},{6,7},{7,6},{8,9},{9,8},{10,11... | collective-permute-start | bytes 1253384 | tf_op jit(solution)/shard_map/ppermute | solution.py:454
  52.3 16.9 %copy-start.21 = (bf16[192,1024]{1,0:T(8,128)(2,1)}, bf16[192,1024]{1,0:T(8,128)(2,1)S(1)}, u32[]{:S(2)}) copy-start(bf16[192,1024]{1,0:T(8,128)(2,1)S(1)} %collective-permute-done.13.refs_6_) | copy-start | bytes 1179652
  52.3 16.8 %collective-permute-start.14 = (bf16[192,1024]{1,0:T(8,128)(2,1)S(1)}, bf16[192,1024]{1,0:T(8,128)(2,1)S(1)}, u32[]{:S(2)}, u32[]{:S(2)}) collective-permute-start(bf16[192,1024]{1,0:T(8,128)(2,1)S(1)} %bitcast.5), channel_id=1, source_target_pairs={{0,24},{8,16},{16,8},{24,0},{1,25},{9,17},{17,9},{25,1},{2,26},{10... | collective-permute-start | bytes 1179656 | tf_op jit(solution)/shard_map/ppermute | solution.py:454
  54.8 1.8 %copy-start.14 = (bf16[48,2176]{1,0:T(8,128)(2,1)}, bf16[48,2176]{1,0:T(8,128)(2,1)S(1)}, u32[]{:S(2)}) copy-start(bf16[48,2176]{1,0:T(8,128)(2,1)S(1)} %collective-permute-done.8.refs_10_) | copy-start | bytes 626692
  54.8 1.5 collective-permute-start.10
  54.8 1.8 %copy-start.15 = (bf16[48,2176]{1,0:T(8,128)(2,1)}, bf16[48,2176]{1,0:T(8,128)(2,1)S(1)}, u32[]{:S(2)}) copy-start(bf16[48,2176]{1,0:T(8,128)(2,1)S(1)} %collective-permute-done.9.refs_11_) | copy-start | bytes 626692
  54.8 1.7 %collective-permute-start.11 = (bf16[48,2176]{1,0:T(8,128)(2,1)S(1)}, bf16[48,2176]{1,0:T(8,128)(2,1)S(1)}, u32[]{:S(2)}, u32[]{:S(2)}) collective-permute-start(bf16[48,2176]{1,0:T(8,128)(2,1)S(1)} %collective-permute-done.9.refs_11_), channel_id=1, source_target_pairs={{0,1},{1,0},{2,3},{3,2},{4,5},{5,4},{6,7},{7,6},{8,9},{9,8},{10,11... | collective-permute-start | bytes 626696 | tf_op jit(solution)/shard_map/ppermute | solution.py:454
  56.3 0.7 copy-start.16
  56.6 0.7 copy-start.17
  56.6 0.9 copy-start.11
  57.4 0.8 copy-start.12
  66.5 15.7 %all-to-all-start = ((f32[32,2,128]{2,1,0:T(2,128)}), f32[32,2,128]{2,1,0:T(2,128)S(1)}, u32[]{:S(2)}, u32[]{:S(2)}) async-start(f32[32,2,128]{2,1,0:T(2,128)} %get-tuple-element.69), calls=%async_computation | async-start | bytes 65536 | tf_op jit(solution)/shard_map/all_to_all | solution.py:30
  69.2 0.7 copy-start.22
  82.1 18.4 %copy-start.1 = (bf16[32,16,128]{2,1,0:T(8,128)(2,1)S(1)}, bf16[32,16,128]{2,1,0:T(8,128)(2,1)}, u32[]{:S(2)}) copy-start(bf16[32,16,128]{2,1,0:T(8,128)(2,1)} %get-tuple-element.66.refs_0_.msgs_ref) | copy-start | bytes 393220
  82.1 18.4 %copy-start.2 = (f32[16,128]{1,0:T(8,128)S(1)}, f32[16,128]{1,0:T(8,128)}, u32[]{:S(2)}) copy-start(f32[16,128]{1,0:T(8,128)} %get-tuple-element.76.gap_ref) | copy-start | bytes 24580
  82.1 18.4 %copy-start.3 = (f32[16,128]{1,0:T(8,128)S(1)}, f32[16,128]{1,0:T(8,128)}, u32[]{:S(2)}) copy-start(f32[16,128]{1,0:T(8,128)} %get-tuple-element.77.own_ref) | copy-start | bytes 24580
  82.1 0.6 copy-start.19
  114.1 15.0 %all-to-all-start.3 = ((f32[32,2,128]{2,1,0:T(2,128)}), f32[32,2,128]{2,1,0:T(2,128)S(1)}, u32[]{:S(2)}, u32[]{:S(2)}) async-start(f32[32,2,128]{2,1,0:T(2,128)} %get-tuple-element.79), calls=%async_computation.3 | async-start | bytes 65536 | tf_op jit(solution)/shard_map/all_to_all | solution.py:30
  129.1 18.4 %copy-start = (bf16[32,16,128]{2,1,0:T(8,128)(2,1)S(1)}, bf16[32,16,128]{2,1,0:T(8,128)(2,1)}, u32[]{:S(2)}) copy-start(bf16[32,16,128]{2,1,0:T(8,128)(2,1)} %all_to_all.31.refs_0_.msgs_ref) | copy-start | bytes 393220
  129.1 0.6 copy-start.18

commit v17 on v16

--- a/solution.py
+++ b/solution.py
@@ -102,34 +102,36 @@
     return ka * n_band + jnp.bitwise_xor(lax.axis_index("band"), d)
 
 
+def own_copies(ref, dest, sems):
+    return [
+        pltpu.make_async_copy(
+            ref.at[jnp.bitwise_xor(lax.axis_index("ka"), j)], dest.at[j], sems.at[j]
+        )
+        for j in range(dest.shape[0])
+    ]
+
+
 def pair_rows(ref, kp):
     part = ref[:, kp * 2 * ROWS : (kp + 1) * 2 * ROWS, :]
     return part.reshape(part.shape[0] * 2 * ROWS, part.shape[2])
 
 
 def pack_kernel(n_ka, nu, *refs):
-    start_in, cond_in, val_in, val_ref, orb_ref = refs[:5]
-    own_ref, gap_ref, outs, refs = refs[5], refs[6], refs[7 : 7 + n_ka], refs[7 + n_ka :]
-    start_ref, cond_ref, energy_ref, cuts, sems, cut_sems = refs
-    own = cuts.shape[-1]
+    start_in, cond_in, val_in, val_ref = refs[:4]
+    own_ref, gap_ref, outs, refs = refs[4], refs[5], refs[6 : 6 + n_ka], refs[6 + n_ka :]
+    start_ref, cond_ref, energy_ref, sems, val_sems = refs
     ins = ((start_in, start_ref), (cond_in, cond_ref), (val_in, energy_ref))
     small = [pltpu.make_async_copy(ref, to, sems.at[i]) for i, (ref, to) in enumerate(ins)]
     k_dev = val_ref.shape[0]
-    val_copies, cut_copies = [], []
+    val_copies = []
     for j in range(n_ka):
         at = pl.multiple_of(jnp.bitwise_xor(lax.axis_index("ka"), j) * nu, nu)
-        point = pl.multiple_of(at + lax.axis_index("band") * own, LANES)
         val_copies.append(
             pltpu.make_async_copy(
-                val_ref.at[:, :, pl.ds(at, nu)], outs[j].at[:, :, pl.ds(0, nu)], cut_sems.at[0, j]
+                val_ref.at[:, :, pl.ds(at, nu)], outs[j].at[:, :, pl.ds(0, nu)], val_sems.at[j]
             )
         )
-        cut_copies.append(
-            pltpu.make_async_copy(
-                orb_ref.at[:, :, pl.ds(point, own)], cuts.at[j], cut_sems.at[1, j]
-            )
-        )
-    start_all(small + cut_copies + val_copies)
+    start_all(small + val_copies)
     wait_all(small)
     own_ref[...] = jnp.zeros_like(own_ref)
     gap_ref[...] = jnp.zeros_like(gap_ref)
@@ -150,13 +152,26 @@
             head = jnp.zeros((ROWS, LANES), F32)
             if (g + 1) * ROWS <= block.shape[0]:
                 head = block[g * ROWS : (g + 1) * ROWS, :]
-            outs[j][g, :, nu : nu + LANES] = head.astype(BF)
-        cut_copies[j].wait()
+            outs[j][g, :, nu:] = head.astype(BF)
+    wait_all(val_copies)
+
+
+def cut_kernel(cond_ref, out_ref, sems):
+    n_ka, _, own = out_ref.shape
+    k_dev, n_cond, npt = cond_ref.shape
+    copies = []
+    for z in range(n_ka):
+        at = z * (npt // n_ka) + lax.axis_index("band") * own
         for kl in range(k_dev):
-            cut = cuts[j, kl].astype(F32)
-            wide = [cut[q * ROWS : (q + 1) * ROWS, :] for q in range(cut.shape[0] // ROWS)]
-            outs[j][kl, :, nu + LANES :] = jnp.concatenate(wide, axis=1).astype(BF)
-    wait_all(val_copies)
+            copies.append(
+                pltpu.make_async_copy(
+                    cond_ref.at[kl, :, pl.ds(pl.multiple_of(at, LANES), own)],
+                    out_ref.at[z, pl.ds(kl * n_cond, n_cond), :],
+                    sems.at[len(copies)],
+                )
+            )
+    start_all(copies)
+    wait_all(copies)
 
 
 def turn_kernel(tile, scr_ref, out_ref, scrs, turned, in_sems, out_sems):
@@ -175,28 +190,13 @@
 
 
 def order_kernel(parts, n_ka, *refs):
-    got_refs, val_refs, refs = refs[:n_ka], refs[n_ka:-13], refs[-13:]
-    rows_out, turned_out, own_out, cond_out, msgs_out = refs[:5]
-    vals, heads, ordered, turned, cuts, val_sems, out_sems, cut_sems = refs[5:]
+    val_refs, refs = refs[:-10], refs[-10:]
+    rows_out, turned_out, own_out, msgs_out, vals, heads, ordered, turned, val_sems, out_sems = refs
     own = own_out.shape[1]
     nu = ordered.shape[1]
     copies = piece_copies(val_refs, parts, 0, nu, vals, val_sems.at[0])
     head_copies = piece_copies(val_refs, parts, nu, LANES, heads, val_sems.at[1])
-    cut_copies = [
-        pltpu.make_async_copy(
-            ref.at[:, :, pl.ds(nu + LANES, cuts.shape[-1])], cuts.at[j], cut_sems.at[j]
-        )
-        for j, ref in enumerate(got_refs)
-    ]
-    start_all(copies + head_copies + cut_copies)
-    wait_all(cut_copies)
-    k_dev, points = cuts.shape[1], cuts.shape[-1] // own
-    for j in range(n_ka):
-        for kl in range(k_dev):
-            cut = cuts[j, kl].astype(F32)
-            tall = [cut[:, q * own : (q + 1) * own] for q in range(points)]
-            at = (j * k_dev + kl) * points * ROWS
-            cond_out[at : at + points * ROWS, :] = jnp.concatenate(tall, axis=0).astype(BF)
+    start_all(copies + head_copies)
     wait_all(copies)
     n_band, group = vals.shape[0], vals.shape[0] * 2 * ROWS
     column = pl.multiple_of(lax.axis_index("band") * own, LANES)
@@ -229,11 +229,9 @@
     k_points = n_ka * k_dev
     msgs_ref, vown_ref, cond_ref, qx_ref, rho_ref, xs, msgs, vown, conds, sems = refs
     own = vown_ref.shape[1]
-    msg_copy = pltpu.make_async_copy(msgs_ref, msgs, sems.at[0])
-    copies = [
-        pltpu.make_async_copy(vown_ref, vown, sems.at[1]),
-        pltpu.make_async_copy(cond_ref, conds, sems.at[2]),
-    ]
+    msg_copy = pltpu.make_async_copy(msgs_ref, msgs, sems.at[n_ka])
+    copies = own_copies(cond_ref, conds, sems)
+    copies.append(pltpu.make_async_copy(vown_ref, vown, sems.at[n_ka + 1]))
     start_all([msg_copy] + copies)
     xs[...] = jnp.zeros_like(xs)
     msg_copy.wait()
@@ -247,12 +245,13 @@
             xs[k // 4, at, pl.ds(base, LANES)] = lane_half(tile, kl % 2, k % 2)
     qx_ref[...] = xs[...].astype(BF)
     wait_all(copies)
+    cond_rows = conds[...].reshape(-1, own)
     rho = jnp.zeros((1, own), F32)
     quad = 2 * LANES
     for kq in range(k_points // 4):
         at = slice(kq * quad, (kq + 1) * quad)
         mixed = dot_tn(qx_ref[kq], vown[at, :])
-        rho = rho + jnp.sum(mixed * conds[at, :].astype(F32), axis=0, keepdims=True)
+        rho = rho + jnp.sum(mixed * cond_rows[at, :].astype(F32), axis=0, keepdims=True)
     for r in range(own // LANES):
         part = rho[:, r * LANES : (r + 1) * LANES]
         rho_ref[:, r, :] = jnp.broadcast_to(part, (rho_ref.shape[0], LANES))
@@ -297,12 +296,14 @@
             cond_rows = conds[...].reshape(-1, mu)
         scr_copies[i].wait()
         amp = jnp.dot(mixed[rows, :], cond_rows, preferred_element_type=F32)
-        kern[rows, :] = (scrs[rows, :].astype(F32) * amp * scale).astype(BF)
+        kern[rows, :] = (scrs[rows, :].astype(F32) * amp).astype(BF)
     row_copy.wait()
     folded[...] = jnp.dot(vals[...], kern[...], preferred_element_type=F32).astype(BF)
-    for kp in range(di_ref.shape[0]):
-        at = slice(kp * LANES, (kp + 1) * LANES)
-        di_ref[kp] = dot_nt(folded[at, :], cond_rows[at, :])
+    for kq in range(qx.shape[0]):
+        at = slice(kq * quad, (kq + 1) * quad)
+        both = scale * dot_nt(folded[at, :], cond_rows[at, :])
+        di_ref[2 * kq] = both[:LANES, :LANES]
+        di_ref[2 * kq + 1] = both[LANES:, LANES:]
 
 
 def exchange_kernel(cfg, chunk, scale, *refs):
@@ -310,7 +311,7 @@
     k_points = n_ka * k_dev
     rho_ref, di_ref, coul_ref, vown_ref, cond_ref, msg_ref = refs[:6]
     rhos, di, coul, conds, vown, part, msg, coul_sems, sems = refs[6:]
-    rho_copy = pltpu.make_async_copy(rho_ref, rhos, sems.at[3])
+    rho_copy = pltpu.make_async_copy(rho_ref, rhos, sems.at[n_ka])
     own, npt = coul_ref.shape
     coul_copies = [
         pltpu.make_async_copy(
@@ -318,11 +319,9 @@
         )
         for i in range(npt // chunk)
     ]
-    copies = [
-        pltpu.make_async_copy(vown_ref, vown, sems.at[0]),
-        pltpu.make_async_copy(di_ref, di, sems.at[1]),
-        pltpu.make_async_copy(cond_ref, conds, sems.at[2]),
-    ]
+    copies = own_copies(cond_ref, conds, sems)
+    copies.append(pltpu.make_async_copy(vown_ref, vown, sems.at[n_ka + 1]))
+    copies.append(pltpu.make_async_copy(di_ref, di, sems.at[n_ka + 2]))
     start_all([rho_copy] + coul_copies + copies)
     rho_copy.wait()
     acc = jnp.zeros((own, LANES), F32)
@@ -334,10 +333,11 @@
             acc = acc + coul[:, j * LANES : (j + 1) * LANES].astype(F32) * rho
     potential = scale * jnp.sum(acc.T, axis=0, keepdims=True)
     wait_all(copies)
+    cond_rows = conds[...].reshape(-1, own)
     for kp in range(k_points // 2):
         at = slice(kp * LANES, (kp + 1) * LANES)
         weighted = (vown[at, :].astype(F32) * potential).astype(BF)
-        part[kp] = 2.0 * dot_nt(weighted, conds[at, :]) - di[kp]
+        part[kp] = 2.0 * dot_nt(weighted, cond_rows[at, :]) - di[kp]
     for d in range(n_band):
         for j in range(n_ka):
             for g in range((k_dev + 1) // 2):
@@ -349,6 +349,11 @@
                     tile = piece if tile is None else tile + piece
                 msg[device_at(n_band, j, d), pl.ds(g * ROWS, ROWS), :] = tile
     msg_ref[...] = msg[...].astype(BF)
+
+
+def write_rows(ref, values):
+    for i, value in enumerate(values):
+        ref[i : i + 1, :] = jnp.broadcast_to(value, (1, ref.shape[1]))
 
 
 def received(recv_ref):
@@ -376,9 +381,7 @@
     state_ref[0] = cur
     state_ref[1] = resid
     state_ref[2] = inter
-    coef_ref[0] = shift[0, 0]
-    coef_ref[1] = square[0, 0]
-    coef_ref[2] = (gap_sq * inv * inv)[0, 0]
+    write_rows(coef_ref, (shift, square, gap_sq * inv * inv))
     sums = [
         jnp.sum(cur * resid),
         jnp.sum(resid * resid),
@@ -390,10 +393,10 @@
 
 def second_owner_kernel(count_all, recv_ref, msgs_ref, gap_ref, state_ref, coef_ref, out_ref, coef_out, msg_ref):
     cross, total, gap_rr, gap_rq = read_sums(msgs_ref, 4)
-    alpha, d, mean_sq = shifted(count_all, coef_ref[0], coef_ref[1], cross, total)
+    alpha, d, mean_sq = shifted(count_all, coef_ref[0:1, 0:1], coef_ref[1:2, 0:1], cross, total)
     beta = jnp.sqrt(mean_sq + 1e-06)
     square = mean_sq / (mean_sq + 1e-06)
-    gap_qq = gap_rr - 2.0 * d * gap_rq + d * d * coef_ref[2]
+    gap_qq = gap_rr - 2.0 * d * gap_rq + d * d * coef_ref[2:3, 0:1]
     shift = gap_qq / (mean_sq + 1e-06) / count_all
     prev = state_ref[0]
     cur = (state_ref[1] - d * prev) / beta
@@ -401,10 +404,7 @@
     resid = (gap_ref[...] - shift) * cur + inter - beta * prev
     out_ref[0] = cur
     out_ref[1] = resid
-    coef_out[0] = alpha[0, 0]
-    coef_out[1] = beta[0, 0]
-    coef_out[2] = shift[0, 0]
-    coef_out[3] = square[0, 0]
+    write_rows(coef_out, (alpha, beta, shift, square))
     dims = msg_ref.shape[:1] + msg_ref.shape[2:]
     msg_ref[:, 0, :] = jnp.full(dims, jnp.sum(cur * resid), F32)
     msg_ref[:, 1, :] = jnp.full(dims, jnp.sum(resid * resid), F32)
@@ -412,12 +412,12 @@
 
 def finish_kernel(count_all, msgs_ref, state_ref, coef_ref, out_ref, coeffs_ref):
     sums = jnp.sum(msgs_ref[...], axis=0)
-    alpha, d, mean_sq = shifted(count_all, coef_ref[2], coef_ref[3], sums[0:1, 0:1], sums[1:2, 0:1])
+    alpha, d, mean_sq = shifted(count_all, coef_ref[2:3, 0:1], coef_ref[3:4, 0:1], sums[0:1, 0:1], sums[1:2, 0:1])
     beta = jnp.sqrt(mean_sq + 1e-06)
     own = (state_ref[1] - d * state_ref[0]) / beta
-    coeffs_ref[0] = coef_ref[0]
+    coeffs_ref[0] = coef_ref[0, 0]
     coeffs_ref[1] = alpha[0, 0]
-    coeffs_ref[2] = coef_ref[1]
+    coeffs_ref[2] = coef_ref[1, 0]
     coeffs_ref[3] = beta[0, 0]
     for kl in range(out_ref.shape[0]):
         tile = own[kl // 2 * ROWS : (kl // 2 + 1) * ROWS, :]
@@ -461,7 +461,7 @@
     rows = own_piece.shape[0]
     half = rows // 2
     by_x, by_y, core = move(own_piece, 2), move(own_piece, 4), move(own_piece, 1)
-    by_x, by_y, core, others = lax.optimization_barrier((by_x, by_y, core, others))
+    by_x, by_y, others = lax.optimization_barrier((by_x, by_y, others))
     diag = [move(by_x[:half], 4), move(by_y[half:], 2)]
     near_x, near_y = move(by_x, 1), move(by_y, 1)
     far = [move(part, 1) for part in diag]
@@ -491,30 +491,37 @@
     block = ((k_dev + 1) // 2 * ROWS, LANES)
     msg_shape = shape_of((devices,) + block, BF)
     wide = nu_blk + LANES
-    cut_lanes = n_cond // ROWS * own
     start_own, gap, *payloads = call(
         functools.partial(pack_kernel, n_ka, nu_blk),
         "pack",
-        (shape_of(block), shape_of(block))
-        + (shape_of((k_dev, nv_blk, wide + cut_lanes), BF),) * n_ka,
-        [ANY] * 5,
+        (shape_of(block), shape_of(block)) + (shape_of((k_dev, nv_blk, wide), BF),) * n_ka,
+        [ANY] * 4,
         (VMEM,) * (2 + n_ka),
         [
             pltpu.VMEM(start_vec.shape, F32),
             pltpu.VMEM(cond_energy.shape, F32),
             pltpu.SMEM(val_energy.shape, F32),
-            pltpu.VMEM((n_ka, k_dev, n_cond, own), BF),
             dma(3),
-            dma(2, n_ka),
+            dma(n_ka),
         ],
-    )(start_vec, cond_energy, val_energy, val_orb, cond_orb)
+    )(start_vec, cond_energy, val_energy, val_orb)
     base, payloads = lax.optimization_barrier((band * mu_blk, payloads))
     got = [payloads[0]] + [swap(payloads[j], "ka", j) for j in range(1, n_ka)]
-    val_cut = jnp.concatenate([part[:, :, :wide] for part in got], axis=0)
-    val_cut = val_cut.reshape(piece_rows, wide)
+    own_rows = k_dev * n_cond
+    cuts = call(
+        cut_kernel,
+        "cut",
+        shape_of((n_ka, own_rows, own), BF),
+        [ANY],
+        VMEM,
+        [dma(n_ka * k_dev)],
+    )(cond_orb)
     cond_local = lax.dynamic_slice_in_dim(cond_orb, base, mu_blk, 2)
     cond_local = cond_local.reshape(k_dev * n_cond, mu_blk)
+    got, cuts, cond_local = lax.optimization_barrier((got, cuts, cond_local))
+    val_cut = jnp.concatenate(got, axis=0).reshape(piece_rows, wide)
     cond_pts = [cond_local] + [swap(cond_local, "ka", j) for j in range(1, n_ka)]
+    cond_own = lax.all_to_all(cuts, "ka", split_axis=0, concat_axis=0, tiled=True)
 
     chunk, tile = 1024, nu_blk
     rows_all, conds_all = k_points * nv_blk * n_band, k_points * n_cond
@@ -530,30 +537,27 @@
     )(screened)
     pieces, parts, scr_turned = plane_pieces(val_cut, scr_turned)
     pieces, cond_pts[1:-1] = lax.optimization_barrier((pieces, cond_pts[1:-1]))
-    val_rows, val_turned, val_own, cond_own, msgs = call(
+    val_rows, val_turned, val_own, msgs = call(
         functools.partial(order_kernel, parts, n_ka),
         "order",
         (
             shape_of((rows_all, nu_blk), BF),
             shape_of((nu_blk, rows_all), BF),
             shape_of((rows_all, own), BF),
-            shape_of((conds_all, own), BF),
             msg_shape,
         ),
-        [ANY] * (n_ka + len(pieces)),
-        (ANY, ANY, ANY, VMEM, VMEM),
+        [ANY] * len(pieces),
+        (ANY, ANY, ANY, VMEM),
         [
             pltpu.VMEM((n_band, piece_rows, nu_blk), BF),
             pltpu.VMEM((n_band, piece_rows, LANES), BF),
             pltpu.VMEM((rows_all, nu_blk), BF),
             pltpu.VMEM((nu_blk, rows_all), BF),
-            pltpu.VMEM((n_ka, k_dev, nv_blk, cut_lanes), BF),
             dma(2, sum(len(piece) for piece in parts)),
             dma(3, pairs),
-            dma(n_ka),
         ],
         moved=9 * MIB,
-    )(*got, *pieces)
+    )(*pieces)
 
     cfg = (n_ka, n_band, k_dev)
     quads = k_points // 4
@@ -573,8 +577,8 @@
                 pltpu.VMEM((quads, 2 * LANES, 2 * LANES), F32),
                 pltpu.VMEM((devices,) + block, BF),
                 pltpu.VMEM((rows_all, own), BF),
-                pltpu.VMEM((conds_all, own), BF),
-                dma(3),
+                pltpu.VMEM((n_ka, own_rows, own), BF),
+                dma(n_ka + 2),
             ],
         )(msgs, val_own, cond_own)
         density = exchange_all(rho)
@@ -611,12 +615,12 @@
                 pltpu.VMEM((devices, own // LANES, LANES), F32),
                 pltpu.VMEM((pairs, LANES, LANES), F32),
                 pltpu.VMEM((own, npt_all), BF),
-                pltpu.VMEM((conds_all, own), BF),
+                pltpu.VMEM((n_ka, own_rows, own), BF),
                 pltpu.VMEM((rows_all, own), BF),
                 pltpu.VMEM((pairs, LANES, LANES), F32),
                 pltpu.VMEM((devices,) + block, F32),
                 dma(npt_all // chunk),
-                dma(4),
+                dma(n_ka + 3),
             ],
         )(density, direct, coulomb, val_own, cond_own)
         recv = exchange_all(summed)
@@ -624,18 +628,18 @@
             state, coef, message = call(
                 functools.partial(first_owner_kernel, count_all),
                 "first_owner",
-                (shape_of((3,) + block), shape_of((3,)), msg_shape),
+                (shape_of((3,) + block), shape_of((ROWS, LANES)), msg_shape),
                 [VMEM] * 4,
-                (VMEM, SMEM, VMEM),
+                (VMEM, VMEM, VMEM),
                 mib=8,
             )(recv, msgs, gap, start_own)
         else:
             state, coef, message = call(
                 functools.partial(second_owner_kernel, count_all),
                 "second_owner",
-                (shape_of((2,) + block), shape_of((4,)), shape_of((devices, 2, LANES))),
-                [VMEM] * 4 + [SMEM],
-                (VMEM, SMEM, VMEM),
+                (shape_of((2,) + block), shape_of((ROWS, LANES)), shape_of((devices, 2, LANES))),
+                [VMEM] * 5,
+                (VMEM, VMEM, VMEM),
                 mib=8,
             )(recv, msgs, gap, state, coef)
         msgs = exchange_all(message)
@@ -643,7 +647,7 @@
         functools.partial(finish_kernel, count_all),
         "finish",
         (shape_of(start_vec.shape), shape_of((2 * STEPS,))),
-        [VMEM] * 2 + [SMEM],
+        [VMEM] * 3,
         (VMEM, SMEM),
         mib=8,
     )(msgs, state, coef)

time: 160 us -> 152 us (0.950)
  waiting for transfers between devices: 30 us -> 20.1 us
  starting transfers between devices: 23 us -> 26.4 us
    ppermute x15, waiting for transfers between devices: 30 us -> 20.1 us  [swap(): lax.ppermute(block, axis, [(i, i ^ d) for i in range(lax.axis_size(axis))])]
    all_to_all x0 -> x1, starting transfers between devices: none -> 3.46 us  [kernel_path(): lax.all_to_all(cuts, 'ka', split_axis=0, concat_axis=0, tiled=True)]
    pallas_call x0 -> x1, Pallas kernels: none -> 1.79 us  [kernel_path(): call(cut_kernel, 'cut', shape_of((n_ka, own_rows, own), BF), [ANY], VMEM,...]
    unnamed x46 -> x44, local copies, waits for them, and re-layouts: 3.56 us -> 4.29 us
  transfers between devices with their start and end apart: 17 -> 18, of which waited for: 6 -> 5; matrix products, arithmetic and copies ran while one was open for 1% -> 1% of each run, Pallas kernels for 23% -> 25%
where the time goes in v17:
time: 152 us; the launch traced here: 151 us
  Pallas kernels  50.5 us (33%)
  blocking collectives  47.4 us (31%)
  starting transfers between devices  26.4 us (17%)
  waiting for transfers between devices  20.1 us (13%)
  local copies, waits for them, and re-layouts  5.53 us (4%)
    all_to_all x4, blocking collectives, exchange_all(): return lax.all_to_all(parts, AXES, split_axis=0, concat_axis=0, tiled=True)  47.4 us
    pallas_call x2, Pallas kernels, kernel_path(): call(functools.partial(direct_kernel, n_ka, tile, scale), 'direct', shape...  23.9 us
    ppermute x15, waiting for transfers between devices, swap(): lax.ppermute(block, axis, [(i, i ^ d) for i in range(lax.axis_size(axis))])  20.1 us
    ppermute x15, starting transfers between devices, swap(): lax.ppermute(block, axis, [(i, i ^ d) for i in range(lax.axis_size(axis))])  17.4 us
    pallas_call x2, Pallas kernels, kernel_path(): call(functools.partial(exchange_kernel, cfg, chunk, scale), 'exchange', m...  7.48 us
    pallas_call x1, Pallas kernels, kernel_path(): call(functools.partial(order_kernel, parts, n_ka), 'order', (shape_of((ro...  5.77 us
    all_to_all x2, starting transfers between devices, exchange_all(): return lax.all_to_all(parts, AXES, split_axis=0, concat_axis=0, tiled=True)  5.56 us
    pallas_call x2, Pallas kernels, kernel_path(): call(functools.partial(density_kernel, cfg), 'density', (shape_of((quads,...  4.51 us
  transfers between devices with their start and end apart: 18, of which 5 were waited for; matrix products, arithmetic and copies ran while one was open for 1% of the time, Pallas kernels for 25%

profile of v17, /device:TPU:0, one launch (start us, length us, event | category | flops | bytes accessed | tf_op | source)
XLA Modules:
  0.0 151.2 jit_solution(17447396612362025979)
XLA Ops:
  0.6 1.9 %pack.1 = (f32[16,128]{1,0:T(8,128)}, f32[16,128]{1,0:T(8,128)}, bf16[3,8,2176]{2,1,0:T(8,128)(2,1)}, bf16[3,8,2176]{2,1,0:T(8,128)(2,1)}, bf16[3,8,2176]{2,1,0:T(8,128)(2,1)}, /*index=5*/bf16[3,8,2176]{2,1,0:T(8,128)(2,1)}) custom-call(f32[3,512]{1,0:T(4,128)} %refs_0_.1, f32[3,64]{1,0:T(4,128)} %refs_1_.1, f32[3,8]{1,0:T(4,128)} %refs_2_.3, ...), custom_call_target="tpu_custom_call" | custom-call | tf_op jit(solution)/shard_map/pack/pallas_call | solution.py:494
  2.5 3.1 %collective-permute-start = (bf16[3,8,2176]{2,1,0:T(8,128)(2,1)}, bf16[3,8,2176]{2,1,0:T(8,128)(2,1)S(1)}, u32[]{:S(2)}, u32[]{:S(2)}) collective-permute-start(bf16[3,8,2176]{2,1,0:T(8,128)(2,1)} %get-tuple-element.53), channel_id=1, source_target_pairs={{0,8},{8,0},{16,24},{24,16},{1,9},{9,1},{17,25},{25,17},{2,10},{10... | collective-permute-start | bytes 313352 | tf_op jit(solution)/shard_map/ppermute | solution.py:454
  5.6 2.6 %collective-permute-start.1 = (bf16[3,8,2176]{2,1,0:T(8,128)(2,1)}, bf16[3,8,2176]{2,1,0:T(8,128)(2,1)S(1)}, u32[]{:S(2)}, u32[]{:S(2)}) collective-permute-start(bf16[3,8,2176]{2,1,0:T(8,128)(2,1)} %get-tuple-element.54), channel_id=1, source_target_pairs={{0,16},{8,24},{16,0},{24,8},{1,17},{9,25},{17,1},{25,9},{2,18},{10... | collective-permute-start | bytes 313352 | tf_op jit(solution)/shard_map/ppermute | solution.py:454
  8.2 0.0 collective-permute-start.2
  8.2 1.8 %cut.1 = bf16[4,192,256]{2,1,0:T(8,128)(2,1)} custom-call(bf16[3,64,8192]{2,1,0:T(8,128)(2,1)} %cond_ref.1), custom_call_target="tpu_custom_call" | custom-call | tf_op jit(solution)/shard_map/cut/pallas_call | solution.py:511
  10.0 1.2 constant_dynamic-slice_fusion
  11.2 5.5 %collective-permute-done.1 = bf16[3,8,2176]{2,1,0:T(8,128)(2,1)S(1)} collective-permute-done((bf16[3,8,2176]{2,1,0:T(8,128)(2,1)}, bf16[3,8,2176]{2,1,0:T(8,128)(2,1)S(1)}, u32[]{:S(2)}, u32[]{:S(2)}) %collective-permute-start.1) | collective-permute-done | bytes 104480 | tf_op jit(solution)/shard_map/ppermute | solution.py:454
  16.7 0.1 maximum_bitcast_fusion.refs_0_
  16.8 1.6 %collective-permute-start.4 = (bf16[96,2176]{1,0:T(8,128)(2,1)S(1)}, bf16[96,2176]{1,0:T(8,128)(2,1)S(1)}, u32[]{:S(2)}, u32[]{:S(2)}) collective-permute-start(bf16[96,2176]{1,0:T(8,128)(2,1)S(1)} %maximum_bitcast_fusion.refs_0_), channel_id=1, source_target_pairs={{0,2},{1,3},{2,0},{3,1},{4,6},{5,7},{6,4},{7,5},{8,10},{9,11},{10,... | collective-permute-start | bytes 1253384 | tf_op jit(solution)/shard_map/ppermute | solution.py:454
  18.4 1.5 %collective-permute-start.5 = (bf16[96,2176]{1,0:T(8,128)(2,1)S(1)}, bf16[96,2176]{1,0:T(8,128)(2,1)S(1)}, u32[]{:S(2)}, u32[]{:S(2)}) collective-permute-start(bf16[96,2176]{1,0:T(8,128)(2,1)S(1)} %maximum_bitcast_fusion.refs_0_), channel_id=1, source_target_pairs={{0,4},{1,5},{2,6},{3,7},{4,0},{5,1},{6,2},{7,3},{8,12},{9,13},{10,... | collective-permute-start | bytes 1253384 | tf_op jit(solution)/shard_map/ppermute | solution.py:454
  19.9 1.7 %collective-permute-start.12 = (bf16[192,1024]{1,0:T(8,128)(2,1)S(1)}, bf16[192,1024]{1,0:T(8,128)(2,1)S(1)}, u32[]{:S(2)}, u32[]{:S(2)}) collective-permute-start(bf16[192,1024]{1,0:T(8,128)(2,1)S(1)} %bitcast.3), channel_id=1, source_target_pairs={{0,8},{8,0},{16,24},{24,16},{1,9},{9,1},{17,25},{25,17},{2,10},{10... | collective-permute-start | bytes 1179656 | tf_op jit(solution)/shard_map/ppermute | solution.py:454
  21.6 1.4 collective-permute-start.13
  22.9 3.5 %all-to-all-start = ((bf16[4,192,256]{2,1,0:T(8,128)(2,1)}), bf16[4,192,256]{2,1,0:T(8,128)(2,1)S(1)}, u32[]{:S(2)}, u32[]{:S(2)}) async-start(bf16[4,192,256]{2,1,0:T(8,128)(2,1)} %cut.1), calls=%async_computation | async-start | bytes 786432 | tf_op jit(solution)/shard_map/all_to_all | solution.py:524
  26.4 3.7 %turn.1.refs_1_ = bf16[2048,1024]{1,0:T(8,128)(2,1)} custom-call(bf16[1024,2048]{1,0:T(8,128)(2,1)} %scr_ref.1), custom_call_target="tpu_custom_call" | custom-call | bytes 8388608 | tf_op jit(solution)/shard_map/turn/pallas_call | solution.py:528
  30.2 0.6 collective-permute-start.8
  30.7 0.6 collective-permute-start.9
  31.4 6.7 %collective-permute-done.12.refs_5_ = bf16[192,1024]{1,0:T(8,128)(2,1)S(1)} collective-permute-done((bf16[192,1024]{1,0:T(8,128)(2,1)S(1)}, bf16[192,1024]{1,0:T(8,128)(2,1)S(1)}, u32[]{:S(2)}, u32[]{:S(2)}) %collective-permute-start.12) | collective-permute-done | bytes 393248 | tf_op jit(solution)/shard_map/ppermute | solution.py:454
  38.1 6.6 %collective-permute-done.13.refs_6_ = bf16[192,1024]{1,0:T(8,128)(2,1)S(1)} collective-permute-done((bf16[192,1024]{1,0:T(8,128)(2,1)S(1)}, bf16[192,1024]{1,0:T(8,128)(2,1)S(1)}, u32[]{:S(2)}, u32[]{:S(2)}) %collective-permute-start.13) | collective-permute-done | bytes 393248 | tf_op jit(solution)/shard_map/ppermute | solution.py:454
  44.7 3.9 %collective-permute-start.14 = (bf16[192,1024]{1,0:T(8,128)(2,1)S(1)}, bf16[192,1024]{1,0:T(8,128)(2,1)S(1)}, u32[]{:S(2)}, u32[]{:S(2)}) collective-permute-start(bf16[192,1024]{1,0:T(8,128)(2,1)S(1)} %bitcast.5), channel_id=1, source_target_pairs={{0,24},{8,16},{16,8},{24,0},{1,25},{9,17},{17,9},{25,1},{2,26},{10... | collective-permute-start | bytes 1179656 | tf_op jit(solution)/shard_map/ppermute | solution.py:454
  48.7 0.2 collective-permute-start.10
  48.9 0.3 collective-permute-start.11
  49.2 0.9 collective-permute-done.10.refs_8_
  50.1 0.3 collective-permute-done.11.refs_9_
  50.5 0.3 copy-done.14
  50.8 0.3 copy-done.15
  51.1 0.2 copy-done.9
  51.3 0.8 copy-done.10
  52.0 5.8 %order.1 = (bf16[768,2048]{1,0:T(8,128)(2,1)}, bf16[2048,768]{1,0:T(8,128)(2,1)}, bf16[768,256]{1,0:T(8,128)(2,1)}, bf16[32,16,128]{2,1,0:T(8,128)(2,1)}) custom-call(bf16[96,2176]{1,0:T(8,128)(2,1)} %copy-done.5, bf16[96,2176]{1,0:T(8,128)(2,1)} %copy-done.8, bf16[96,2176]{1,0:T(8,128)(2,1)} %copy-done.6, bf16[96,2176]{1,0:T(8,128)(2,1)} %copy-done.9, ...), custom_call_target="tpu_custom_call" | custom-call | bytes 9437184 | tf_op jit(solution)/shard_map/order/pallas_call | solution.py:540
  57.8 0.7 copy-done.4
  58.6 2.3 %density.2 = (bf16[3,256,256]{2,1,0:T(8,128)(2,1)}, f32[32,2,128]{2,1,0:T(2,128)}) custom-call(bf16[32,16,128]{2,1,0:T(8,128)(2,1)} %get-tuple-element.74.refs_0_.msgs_ref, bf16[768,256]{1,0:T(8,128)(2,1)} %get-tuple-element.75.refs_1_.refs_3_, bf16[4,192,256]{2,1,0:T(8,128)(2,1)} %copy-done.4), custom_call_target="tpu_custom_call" | custom-call | tf_op jit(solution)/shard_map/density/pallas_call | solution.py:567
  60.8 2.8 %all-to-all-start.1 = ((f32[32,2,128]{2,1,0:T(2,128)}), f32[32,2,128]{2,1,0:T(2,128)S(1)}, u32[]{:S(2)}, u32[]{:S(2)}) async-start(f32[32,2,128]{2,1,0:T(2,128)} %get-tuple-element.77), calls=%async_computation.1 | async-start | bytes 65536 | tf_op jit(solution)/shard_map/all_to_all | solution.py:30
  63.7 0.7 copy-done.21
  64.4 11.9 %direct.2.refs_1_ = f32[6,128,128]{2,1,0:T(8,128)} custom-call(bf16[2048,768]{1,0:T(8,128)(2,1)} %get-tuple-element.78.refs_0_, bf16[2048,1024]{1,0:T(8,128)(2,1)} %turn.1.refs_1_, bf16[768,2048]{1,0:T(8,128)(2,1)} %get-tuple-element.80.refs_2_, bf16[3,256,256]{2,1,0:T(8,128)(2,1)} %get-tuple-element.81.refs_3_, bf16[192,1024]{1,0:T(8,128)(2,1)} %bitcast.6, ...), custom_call_target="tpu_custom_call" | custom-call | flops 6442450944 | bytes 12582912 | tf_op jit(solution)/shard_map/direct/pallas_call | solution.py:585
  76.3 0.0 copy-start.3
  76.4 0.6 copy-done.17
  77.0 3.7 %exchange.2 = bf16[32,16,128]{2,1,0:T(8,128)(2,1)} custom-call(f32[32,2,128]{2,1,0:T(2,128)} %copy-done.17, f32[6,128,128]{2,1,0:T(8,128)} %direct.2.refs_1_, bf16[256,8192]{1,0:T(8,128)(2,1)} %refs_2_.5, bf16[768,256]{1,0:T(8,128)(2,1)} %get-tuple-element.75.refs_1_.refs_3_, bf16[4,192,256]{2,1,0:T(8,128)(2,1)} %copy-done.4), custom_call_target="tpu_custom_call" | custom-call | tf_op jit(solution)/shard_map/exchange/pallas_call | solution.py:608
  80.7 13.9 %all_to_all.35.recv_ref = bf16[32,16,128]{2,1,0:T(8,128)(2,1)S(1)} all-to-all(bf16[32,16,128]{2,1,0:T(8,128)(2,1)} %exchange.2), channel_id=1, replica_groups=mesh['ka'=4,'band'=8] {'ka','band'}, dimensions={0} | all-to-all | bytes 262144 | tf_op jit(solution)/shard_map/all_to_all | solution.py:30
  94.6 0.3 first_owner.1
  95.0 10.6 %all_to_all.36.refs_0_.msgs_ref = bf16[32,16,128]{2,1,0:T(8,128)(2,1)} all-to-all(bf16[32,16,128]{2,1,0:T(8,128)(2,1)S(1)} %get-tuple-element.86), channel_id=1, replica_groups=mesh['ka'=4,'band'=8] {'ka','band'}, dimensions={0} | all-to-all | bytes 262144 | tf_op jit(solution)/shard_map/all_to_all | solution.py:30
  105.6 2.3 %density.3 = (bf16[3,256,256]{2,1,0:T(8,128)(2,1)}, f32[32,2,128]{2,1,0:T(2,128)}) custom-call(bf16[32,16,128]{2,1,0:T(8,128)(2,1)} %all_to_all.36.refs_0_.msgs_ref, bf16[768,256]{1,0:T(8,128)(2,1)} %get-tuple-element.75.refs_1_.refs_3_, bf16[4,192,256]{2,1,0:T(8,128)(2,1)} %copy-done.4), custom_call_target="tpu_custom_call" | custom-call | tf_op jit(solution)/shard_map/density/pallas_call | solution.py:567
  107.8 2.8 %all-to-all-start.4 = ((f32[32,2,128]{2,1,0:T(2,128)}), f32[32,2,128]{2,1,0:T(2,128)S(1)}, u32[]{:S(2)}, u32[]{:S(2)}) async-start(f32[32,2,128]{2,1,0:T(2,128)} %get-tuple-element.87), calls=%async_computation.4 | async-start | bytes 65536 | tf_op jit(solution)/shard_map/all_to_all | solution.py:30
  110.7 11.9 %direct.3.refs_1_ = f32[6,128,128]{2,1,0:T(8,128)} custom-call(bf16[2048,768]{1,0:T(8,128)(2,1)} %get-tuple-element.78.refs_0_, bf16[2048,1024]{1,0:T(8,128)(2,1)} %turn.1.refs_1_, bf16[768,2048]{1,0:T(8,128)(2,1)} %get-tuple-element.80.refs_2_, bf16[3,256,256]{2,1,0:T(8,128)(2,1)} %get-tuple-element.88.refs_3_, bf16[192,1024]{1,0:T(8,128)(2,1)} %bitcast.7, ...), custom_call_target="tpu_custom_call" | custom-call | flops 6442450944 | bytes 12582912 | tf_op jit(solution)/shard_map/direct/pallas_call | solution.py:585
  122.6 0.6 copy-done.16
  123.2 3.7 %exchange.3 = bf16[32,16,128]{2,1,0:T(8,128)(2,1)} custom-call(f32[32,2,128]{2,1,0:T(2,128)} %copy-done.16, f32[6,128,128]{2,1,0:T(8,128)} %direct.3.refs_1_, bf16[256,8192]{1,0:T(8,128)(2,1)} %refs_2_.5, bf16[768,256]{1,0:T(8,128)(2,1)} %get-tuple-element.75.refs_1_.refs_3_, bf16[4,192,256]{2,1,0:T(8,128)(2,1)} %copy-done.4), custom_call_target="tpu_custom_call" | custom-call | tf_op jit(solution)/shard_map/exchange/pallas_call | solution.py:608
  127.0 13.9 %all_to_all.37.recv_ref = bf16[32,16,128]{2,1,0:T(8,128)(2,1)S(1)} all-to-all(bf16[32,16,128]{2,1,0:T(8,128)(2,1)} %exchange.3), channel_id=1, replica_groups=mesh['ka'=4,'band'=8] {'ka','band'}, dimensions={0} | all-to-all | bytes 262144 | tf_op jit(solution)/shard_map/all_to_all | solution.py:30
  140.9 0.4 second_owner.1
  141.2 9.0 %all_to_all.38.msgs_ref = f32[32,2,128]{2,1,0:T(2,128)S(1)} all-to-all(f32[32,2,128]{2,1,0:T(2,128)S(1)} %get-tuple-element.91), channel_id=1, replica_groups=mesh['ka'=4,'band'=8] {'ka','band'}, dimensions={0} | all-to-all | bytes 65536 | tf_op jit(solution)/shard_map/all_to_all | solution.py:30
  150.3 0.8 finish.1
  (53 shorter events, 0.1 us)
Async XLA Ops:
  2.5 14.2 %copy-start.18 = (bf16[3,8,2176]{2,1,0:T(8,128)(2,1)S(1)}, bf16[3,8,2176]{2,1,0:T(8,128)(2,1)}, u32[]{:S(2)}) copy-start(bf16[3,8,2176]{2,1,0:T(8,128)(2,1)} %get-tuple-element.57) | copy-start | bytes 313348
  2.5 8.7 %collective-permute-start = (bf16[3,8,2176]{2,1,0:T(8,128)(2,1)}, bf16[3,8,2176]{2,1,0:T(8,128)(2,1)S(1)}, u32[]{:S(2)}, u32[]{:S(2)}) collective-permute-start(bf16[3,8,2176]{2,1,0:T(8,128)(2,1)} %get-tuple-element.53), channel_id=1, source_target_pairs={{0,8},{8,0},{16,24},{24,16},{1,9},{9,1},{17,25},{25,17},{2,10},{10... | collective-permute-start | bytes 313352 | tf_op jit(solution)/shard_map/ppermute | solution.py:454
  5.6 11.1 %collective-permute-start.1 = (bf16[3,8,2176]{2,1,0:T(8,128)(2,1)}, bf16[3,8,2176]{2,1,0:T(8,128)(2,1)S(1)}, u32[]{:S(2)}, u32[]{:S(2)}) collective-permute-start(bf16[3,8,2176]{2,1,0:T(8,128)(2,1)} %get-tuple-element.54), channel_id=1, source_target_pairs={{0,16},{8,24},{16,0},{24,8},{1,17},{9,25},{17,1},{25,9},{2,18},{10... | collective-permute-start | bytes 313352 | tf_op jit(solution)/shard_map/ppermute | solution.py:454
  8.2 8.5 %collective-permute-start.2 = (bf16[3,8,2176]{2,1,0:T(8,128)(2,1)}, bf16[3,8,2176]{2,1,0:T(8,128)(2,1)S(1)}, u32[]{:S(2)}, u32[]{:S(2)}) collective-permute-start(bf16[3,8,2176]{2,1,0:T(8,128)(2,1)} %get-tuple-element.55), channel_id=1, source_target_pairs={{0,24},{8,16},{16,8},{24,0},{1,25},{9,17},{17,9},{25,1},{2,26},{10... | collective-permute-start | bytes 313352 | tf_op jit(solution)/shard_map/ppermute | solution.py:454
  11.2 33.5 %copy-start.11 = (bf16[3,64,1024]{2,1,0:T(8,128)(2,1)}, bf16[3,64,1024]{2,1,0:T(8,128)(2,1)S(1)}, u32[]{:S(2)}) copy-start(bf16[3,64,1024]{2,1,0:T(8,128)(2,1)S(1)} %constant_dynamic-slice_fusion) | copy-start | bytes 1179652
  16.8 13.3 %copy-start.5 = (bf16[96,2176]{1,0:T(8,128)(2,1)}, bf16[96,2176]{1,0:T(8,128)(2,1)S(1)}, u32[]{:S(2)}) copy-start(bf16[96,2176]{1,0:T(8,128)(2,1)S(1)} %maximum_bitcast_fusion.refs_0_) | copy-start | bytes 1253380
  16.8 13.3 %collective-permute-start.4 = (bf16[96,2176]{1,0:T(8,128)(2,1)S(1)}, bf16[96,2176]{1,0:T(8,128)(2,1)S(1)}, u32[]{:S(2)}, u32[]{:S(2)}) collective-permute-start(bf16[96,2176]{1,0:T(8,128)(2,1)S(1)} %maximum_bitcast_fusion.refs_0_), channel_id=1, source_target_pairs={{0,2},{1,3},{2,0},{3,1},{4,6},{5,7},{6,4},{7,5},{8,10},{9,11},{10,... | collective-permute-start | bytes 1253384 | tf_op jit(solution)/shard_map/ppermute | solution.py:454
  18.4 11.8 %collective-permute-start.5 = (bf16[96,2176]{1,0:T(8,128)(2,1)S(1)}, bf16[96,2176]{1,0:T(8,128)(2,1)S(1)}, u32[]{:S(2)}, u32[]{:S(2)}) collective-permute-start(bf16[96,2176]{1,0:T(8,128)(2,1)S(1)} %maximum_bitcast_fusion.refs_0_), channel_id=1, source_target_pairs={{0,4},{1,5},{2,6},{3,7},{4,0},{5,1},{6,2},{7,3},{8,12},{9,13},{10,... | collective-permute-start | bytes 1253384 | tf_op jit(solution)/shard_map/ppermute | solution.py:454
  19.9 18.2 %collective-permute-start.12 = (bf16[192,1024]{1,0:T(8,128)(2,1)S(1)}, bf16[192,1024]{1,0:T(8,128)(2,1)S(1)}, u32[]{:S(2)}, u32[]{:S(2)}) collective-permute-start(bf16[192,1024]{1,0:T(8,128)(2,1)S(1)} %bitcast.3), channel_id=1, source_target_pairs={{0,8},{8,0},{16,24},{24,16},{1,9},{9,1},{17,25},{25,17},{2,10},{10... | collective-permute-start | bytes 1179656 | tf_op jit(solution)/shard_map/ppermute | solution.py:454
  21.6 23.2 %collective-permute-start.13 = (bf16[192,1024]{1,0:T(8,128)(2,1)S(1)}, bf16[192,1024]{1,0:T(8,128)(2,1)S(1)}, u32[]{:S(2)}, u32[]{:S(2)}) collective-permute-start(bf16[192,1024]{1,0:T(8,128)(2,1)S(1)} %bitcast.4), channel_id=1, source_target_pairs={{0,16},{8,24},{16,0},{24,8},{1,17},{9,25},{17,1},{25,9},{2,18},{10... | collective-permute-start | bytes 1179656 | tf_op jit(solution)/shard_map/ppermute | solution.py:454
  22.9 21.8 %collective-permute-start.3 = (bf16[96,2176]{1,0:T(8,128)(2,1)S(1)}, bf16[96,2176]{1,0:T(8,128)(2,1)S(1)}, u32[]{:S(2)}, u32[]{:S(2)}) collective-permute-start(bf16[96,2176]{1,0:T(8,128)(2,1)S(1)} %maximum_bitcast_fusion.refs_0_), channel_id=1, source_target_pairs={{0,1},{1,0},{2,3},{3,2},{4,5},{5,4},{6,7},{7,6},{8,9},{9,8},{10,11... | collective-permute-start | bytes 1253384 | tf_op jit(solution)/shard_map/ppermute | solution.py:454
  22.9 34.9 %all-to-all-start = ((bf16[4,192,256]{2,1,0:T(8,128)(2,1)}), bf16[4,192,256]{2,1,0:T(8,128)(2,1)S(1)}, u32[]{:S(2)}, u32[]{:S(2)}) async-start(bf16[4,192,256]{2,1,0:T(8,128)(2,1)} %cut.1), calls=%async_computation | async-start | bytes 786432 | tf_op jit(solution)/shard_map/all_to_all | solution.py:524
  30.1 20.3 %copy-start.6 = (bf16[96,2176]{1,0:T(8,128)(2,1)}, bf16[96,2176]{1,0:T(8,128)(2,1)S(1)}, u32[]{:S(2)}) copy-start(bf16[96,2176]{1,0:T(8,128)(2,1)S(1)} %collective-permute-done.4.refs_2_) | copy-start | bytes 1253380
  30.1 20.3 %copy-start.7 = (bf16[96,2176]{1,0:T(8,128)(2,1)}, bf16[96,2176]{1,0:T(8,128)(2,1)S(1)}, u32[]{:S(2)}) copy-start(bf16[96,2176]{1,0:T(8,128)(2,1)S(1)} %collective-permute-done.5.refs_4_) | copy-start | bytes 1253380
  30.2 18.5 %collective-permute-start.8 = (bf16[48,2176]{1,0:T(8,128)(2,1)S(1)}, bf16[48,2176]{1,0:T(8,128)(2,1)S(1)}, u32[]{:S(2)}, u32[]{:S(2)}) collective-permute-start(bf16[48,2176]{1,0:T(8,128)(2,1)S(1)} %slice.6), channel_id=1, source_target_pairs={{0,4},{1,5},{2,6},{3,7},{4,0},{5,1},{6,2},{7,3},{8,12},{9,13},{10,... | collective-permute-start | bytes 626696 | tf_op jit(solution)/shard_map/ppermute | solution.py:454
  30.7 18.1 %collective-permute-start.9 = (bf16[48,2176]{1,0:T(8,128)(2,1)S(1)}, bf16[48,2176]{1,0:T(8,128)(2,1)S(1)}, u32[]{:S(2)}, u32[]{:S(2)}) collective-permute-start(bf16[48,2176]{1,0:T(8,128)(2,1)S(1)} %slice.7), channel_id=1, source_target_pairs={{0,2},{1,3},{2,0},{3,1},{4,6},{5,7},{6,4},{7,5},{8,10},{9,11},{10,... | collective-permute-start | bytes 626696 | tf_op jit(solution)/shard_map/ppermute | solution.py:454
  38.1 25.5 %copy-start.19 = (bf16[192,1024]{1,0:T(8,128)(2,1)}, bf16[192,1024]{1,0:T(8,128)(2,1)S(1)}, u32[]{:S(2)}) copy-start(bf16[192,1024]{1,0:T(8,128)(2,1)S(1)} %collective-permute-done.12.refs_5_) | copy-start | bytes 1179652
  38.1 12.3 %collective-permute-start.6 = (bf16[96,2176]{1,0:T(8,128)(2,1)S(1)}, bf16[96,2176]{1,0:T(8,128)(2,1)S(1)}, u32[]{:S(2)}, u32[]{:S(2)}) collective-permute-start(bf16[96,2176]{1,0:T(8,128)(2,1)S(1)} %collective-permute-done.4.refs_2_), channel_id=1, source_target_pairs={{0,1},{1,0},{2,3},{3,2},{4,5},{5,4},{6,7},{7,6},{8,9},{9,8},{10,11... | collective-permute-start | bytes 1253384 | tf_op jit(solution)/shard_map/ppermute | solution.py:454
  44.7 18.9 %copy-start.20 = (bf16[192,1024]{1,0:T(8,128)(2,1)}, bf16[192,1024]{1,0:T(8,128)(2,1)S(1)}, u32[]{:S(2)}) copy-start(bf16[192,1024]{1,0:T(8,128)(2,1)S(1)} %collective-permute-done.13.refs_6_) | copy-start | bytes 1179652
  44.7 5.7 %collective-permute-start.7 = (bf16[96,2176]{1,0:T(8,128)(2,1)S(1)}, bf16[96,2176]{1,0:T(8,128)(2,1)S(1)}, u32[]{:S(2)}, u32[]{:S(2)}) collective-permute-start(bf16[96,2176]{1,0:T(8,128)(2,1)S(1)} %collective-permute-done.5.refs_4_), channel_id=1, source_target_pairs={{0,1},{1,0},{2,3},{3,2},{4,5},{5,4},{6,7},{7,6},{8,9},{9,8},{10,11... | collective-permute-start | bytes 1253384 | tf_op jit(solution)/shard_map/ppermute | solution.py:454
  44.7 5.7 %copy-start.8 = (bf16[96,2176]{1,0:T(8,128)(2,1)}, bf16[96,2176]{1,0:T(8,128)(2,1)S(1)}, u32[]{:S(2)}) copy-start(bf16[96,2176]{1,0:T(8,128)(2,1)S(1)} %collective-permute-done.3.refs_1_) | copy-start | bytes 1253380
  44.7 18.9 %collective-permute-start.14 = (bf16[192,1024]{1,0:T(8,128)(2,1)S(1)}, bf16[192,1024]{1,0:T(8,128)(2,1)S(1)}, u32[]{:S(2)}, u32[]{:S(2)}) collective-permute-start(bf16[192,1024]{1,0:T(8,128)(2,1)S(1)} %bitcast.5), channel_id=1, source_target_pairs={{0,24},{8,16},{16,8},{24,0},{1,25},{9,17},{17,9},{25,1},{2,26},{10... | collective-permute-start | bytes 1179656 | tf_op jit(solution)/shard_map/ppermute | solution.py:454
  48.7 1.8 %copy-start.12 = (bf16[48,2176]{1,0:T(8,128)(2,1)}, bf16[48,2176]{1,0:T(8,128)(2,1)S(1)}, u32[]{:S(2)}) copy-start(bf16[48,2176]{1,0:T(8,128)(2,1)S(1)} %collective-permute-done.8.refs_6_) | copy-start | bytes 626692
  48.7 1.5 collective-permute-start.10
  48.9 1.6 %copy-start.13 = (bf16[48,2176]{1,0:T(8,128)(2,1)}, bf16[48,2176]{1,0:T(8,128)(2,1)S(1)}, u32[]{:S(2)}) copy-start(bf16[48,2176]{1,0:T(8,128)(2,1)S(1)} %collective-permute-done.9.refs_7_) | copy-start | bytes 626692
  48.9 1.5 %collective-permute-start.11 = (bf16[48,2176]{1,0:T(8,128)(2,1)S(1)}, bf16[48,2176]{1,0:T(8,128)(2,1)S(1)}, u32[]{:S(2)}, u32[]{:S(2)}) collective-permute-start(bf16[48,2176]{1,0:T(8,128)(2,1)S(1)} %collective-permute-done.9.refs_7_), channel_id=1, source_target_pairs={{0,1},{1,0},{2,3},{3,2},{4,5},{5,4},{6,7},{7,6},{8,9},{9,8},{10,11... | collective-permute-start | bytes 626696 | tf_op jit(solution)/shard_map/ppermute | solution.py:454
  50.1 0.7 copy-start.14
  50.4 0.7 copy-start.15
  50.4 0.8 copy-start.9
  51.3 0.8 copy-start.10
  57.8 0.8 copy-start.4
  60.8 15.5 %all-to-all-start.1 = ((f32[32,2,128]{2,1,0:T(2,128)}), f32[32,2,128]{2,1,0:T(2,128)S(1)}, u32[]{:S(2)}, u32[]{:S(2)}) async-start(f32[32,2,128]{2,1,0:T(2,128)} %get-tuple-element.77), calls=%async_computation.1 | async-start | bytes 65536 | tf_op jit(solution)/shard_map/all_to_all | solution.py:30
  63.6 0.7 copy-start.21
  76.3 18.3 %copy-start.1 = (bf16[32,16,128]{2,1,0:T(8,128)(2,1)S(1)}, bf16[32,16,128]{2,1,0:T(8,128)(2,1)}, u32[]{:S(2)}) copy-start(bf16[32,16,128]{2,1,0:T(8,128)(2,1)} %get-tuple-element.74.refs_0_.msgs_ref) | copy-start | bytes 393220
  76.3 18.3 %copy-start.2 = (f32[16,128]{1,0:T(8,128)S(1)}, f32[16,128]{1,0:T(8,128)}, u32[]{:S(2)}) copy-start(f32[16,128]{1,0:T(8,128)} %get-tuple-element.84.gap_ref) | copy-start | bytes 24580
  76.3 18.3 %copy-start.3 = (f32[16,128]{1,0:T(8,128)S(1)}, f32[16,128]{1,0:T(8,128)}, u32[]{:S(2)}) copy-start(f32[16,128]{1,0:T(8,128)} %get-tuple-element.85.own_ref) | copy-start | bytes 24580
  76.4 0.6 copy-start.17
  107.8 14.8 %all-to-all-start.4 = ((f32[32,2,128]{2,1,0:T(2,128)}), f32[32,2,128]{2,1,0:T(2,128)S(1)}, u32[]{:S(2)}, u32[]{:S(2)}) async-start(f32[32,2,128]{2,1,0:T(2,128)} %get-tuple-element.87), calls=%async_computation.4 | async-start | bytes 65536 | tf_op jit(solution)/shard_map/all_to_all | solution.py:30
  122.6 18.3 %copy-start = (bf16[32,16,128]{2,1,0:T(8,128)(2,1)S(1)}, bf16[32,16,128]{2,1,0:T(8,128)(2,1)}, u32[]{:S(2)}) copy-start(bf16[32,16,128]{2,1,0:T(8,128)(2,1)} %all_to_all.36.refs_0_.msgs_ref) | copy-start | bytes 393220
  122.6 0.6 copy-start.16

commit v18 on v17

--- a/solution.py
+++ b/solution.py
@@ -454,21 +454,29 @@
     return lax.ppermute(block, axis, [(i, i ^ d) for i in range(lax.axis_size(axis))])
 
 
-def plane_pieces(own_piece, others):
+def plane_pieces(own_piece):
     def move(block, d):
         return swap(block, "band", d)
 
     rows = own_piece.shape[0]
     half = rows // 2
     by_x, by_y, core = move(own_piece, 2), move(own_piece, 4), move(own_piece, 1)
-    by_x, by_y, others = lax.optimization_barrier((by_x, by_y, others))
+    by_x, by_y, core = lax.optimization_barrier((by_x, by_y, core))
     diag = [move(by_x[:half], 4), move(by_y[half:], 2)]
-    near_x, near_y = move(by_x, 1), move(by_y, 1)
-    far = [move(part, 1) for part in diag]
-    arrays = [own_piece, core, by_x, near_x, by_y, near_y] + diag + far
-    parts = tuple(((i, 0, rows),) for i in range(6))
-    parts += (((6, 0, half), (7, 0, half)), ((8, 0, half), (9, 0, half)))
-    return arrays, parts, others
+    near = move(jnp.concatenate([by_x, by_y], axis=0), 1)
+    far = move(jnp.concatenate(diag, axis=0), 1)
+    arrays = [own_piece, core, by_x, by_y, near] + diag + [far]
+    parts = (
+        ((0, 0, rows),),
+        ((1, 0, rows),),
+        ((2, 0, rows),),
+        ((4, 0, rows),),
+        ((3, 0, rows),),
+        ((4, rows, rows),),
+        ((5, 0, half), (6, 0, half)),
+        ((7, 0, rows),),
+    )
+    return arrays, parts
 
 
 def kernel_path(start_vec, val_energy, cond_energy, val_orb, cond_orb, coulomb, screened):
@@ -518,13 +526,6 @@
     )(cond_orb)
     cond_local = lax.dynamic_slice_in_dim(cond_orb, base, mu_blk, 2)
     cond_local = cond_local.reshape(k_dev * n_cond, mu_blk)
-    got, cuts, cond_local = lax.optimization_barrier((got, cuts, cond_local))
-    val_cut = jnp.concatenate(got, axis=0).reshape(piece_rows, wide)
-    cond_pts = [cond_local] + [swap(cond_local, "ka", j) for j in range(1, n_ka)]
-    cond_own = lax.all_to_all(cuts, "ka", split_axis=0, concat_axis=0, tiled=True)
-
-    chunk, tile = 1024, nu_blk
-    rows_all, conds_all = k_points * nv_blk * n_band, k_points * n_cond
     scr_turned = call(
         functools.partial(turn_kernel, nu_blk // 4),
         "turn",
@@ -535,7 +536,16 @@
         + [dma(4)] * 2,
         moved=8 * MIB,
     )(screened)
-    pieces, parts, scr_turned = plane_pieces(val_cut, scr_turned)
+    got, cuts, cond_local, scr_turned = lax.optimization_barrier(
+        (got, cuts, cond_local, scr_turned)
+    )
+    val_cut = jnp.concatenate(got, axis=0).reshape(piece_rows, wide)
+    cond_pts = [cond_local] + [swap(cond_local, "ka", j) for j in range(1, n_ka)]
+    cond_own = lax.all_to_all(cuts, "ka", split_axis=0, concat_axis=0, tiled=True)
+
+    chunk, tile = 1024, nu_blk
+    rows_all, conds_all = k_points * nv_blk * n_band, k_points * n_cond
+    pieces, parts = plane_pieces(val_cut)
     pieces, cond_pts[1:-1] = lax.optimization_barrier((pieces, cond_pts[1:-1]))
     val_rows, val_turned, val_own, msgs = call(
         functools.partial(order_kernel, parts, n_ka),

time: 152 us -> 176 us (1.16)
  waiting for transfers between devices: 20.1 us -> 42.8 us
    ppermute x15 -> x13, waiting for transfers between devices: 20.1 us -> 42.8 us  [swap(): lax.ppermute(block, axis, [(i, i ^ d) for i in range(lax.axis_size(axis))])]
    ppermute x15 -> x13, starting transfers between devices: 17.4 us -> 15.5 us  [swap(): lax.ppermute(block, axis, [(i, i ^ d) for i in range(lax.axis_size(axis))])]
    unnamed x44 -> x36, local copies, waits for them, and re-layouts: 4.29 us -> 3.69 us
  transfers between devices with their start and end apart: 18 -> 16, of which waited for: 5 -> 5; matrix products, arithmetic and copies ran while one was open for 1% -> 2% of each run, Pallas kernels for 25% -> 21%
where the time goes in v18:
time: 176 us; the launch traced here: 175 us
  Pallas kernels  50.5 us (29%)
  blocking collectives  47.4 us (27%)
  waiting for transfers between devices  42.8 us (24%)
  starting transfers between devices  25.9 us (15%)
  local copies, waits for them, and re-layouts  6.36 us (4%)
    all_to_all x4, blocking collectives, exchange_all(): return lax.all_to_all(parts, AXES, split_axis=0, concat_axis=0, tiled=True)  47.4 us
    ppermute x13, waiting for transfers between devices, swap(): lax.ppermute(block, axis, [(i, i ^ d) for i in range(lax.axis_size(axis))])  42.8 us
    pallas_call x2, Pallas kernels, kernel_path(): call(functools.partial(direct_kernel, n_ka, tile, scale), 'direct', shape...  23.9 us
    ppermute x13, starting transfers between devices, swap(): lax.ppermute(block, axis, [(i, i ^ d) for i in range(lax.axis_size(axis))])  15.5 us
    pallas_call x2, Pallas kernels, kernel_path(): call(functools.partial(exchange_kernel, cfg, chunk, scale), 'exchange', m...  7.48 us
    pallas_call x1, Pallas kernels, kernel_path(): call(functools.partial(order_kernel, parts, n_ka), 'order', (shape_of((ro...  5.76 us
    all_to_all x2, starting transfers between devices, exchange_all(): return lax.all_to_all(parts, AXES, split_axis=0, concat_axis=0, tiled=True)  5.66 us
    all_to_all x1, starting transfers between devices, kernel_path(): lax.all_to_all(cuts, 'ka', split_axis=0, concat_axis=0, tiled=True)  4.67 us
  transfers between devices with their start and end apart: 16, of which 5 were waited for; matrix products, arithmetic and copies ran while one was open for 2% of the time, Pallas kernels for 21%

profile of v18, /device:TPU:0, one launch (start us, length us, event | category | flops | bytes accessed | tf_op | source)
XLA Modules:
  0.0 175.3 jit_solution(16314453375521787253)
XLA Ops:
  0.6 1.9 %pack.1 = (f32[16,128]{1,0:T(8,128)}, f32[16,128]{1,0:T(8,128)}, bf16[3,8,2176]{2,1,0:T(8,128)(2,1)}, bf16[3,8,2176]{2,1,0:T(8,128)(2,1)}, bf16[3,8,2176]{2,1,0:T(8,128)(2,1)}, /*index=5*/bf16[3,8,2176]{2,1,0:T(8,128)(2,1)}) custom-call(f32[3,512]{1,0:T(4,128)} %refs_0_.1, f32[3,64]{1,0:T(4,128)} %refs_1_.1, f32[3,8]{1,0:T(4,128)} %refs_2_.3, ...), custom_call_target="tpu_custom_call" | custom-call | tf_op jit(solution)/shard_map/pack/pallas_call | solution.py:502
  2.5 3.1 %collective-permute-start = (bf16[3,8,2176]{2,1,0:T(8,128)(2,1)}, bf16[3,8,2176]{2,1,0:T(8,128)(2,1)S(1)}, u32[]{:S(2)}, u32[]{:S(2)}) collective-permute-start(bf16[3,8,2176]{2,1,0:T(8,128)(2,1)} %get-tuple-element.52), channel_id=1, source_target_pairs={{0,8},{8,0},{16,24},{24,16},{1,9},{9,1},{17,25},{25,17},{2,10},{10... | collective-permute-start | bytes 313352 | tf_op jit(solution)/shard_map/ppermute | solution.py:454
  5.6 2.6 %collective-permute-start.1 = (bf16[3,8,2176]{2,1,0:T(8,128)(2,1)}, bf16[3,8,2176]{2,1,0:T(8,128)(2,1)S(1)}, u32[]{:S(2)}, u32[]{:S(2)}) collective-permute-start(bf16[3,8,2176]{2,1,0:T(8,128)(2,1)} %get-tuple-element.53), channel_id=1, source_target_pairs={{0,16},{8,24},{16,0},{24,8},{1,17},{9,25},{17,1},{25,9},{2,18},{10... | collective-permute-start | bytes 313352 | tf_op jit(solution)/shard_map/ppermute | solution.py:454
  8.2 0.0 collective-permute-start.2
  8.2 3.7 %turn.1.refs_1_ = bf16[2048,1024]{1,0:T(8,128)(2,1)} custom-call(bf16[1024,2048]{1,0:T(8,128)(2,1)} %scr_ref.1), custom_call_target="tpu_custom_call" | custom-call | bytes 8388608 | tf_op jit(solution)/shard_map/turn/pallas_call | solution.py:529
  11.9 1.8 %cut.1 = bf16[4,192,256]{2,1,0:T(8,128)(2,1)} custom-call(bf16[3,64,8192]{2,1,0:T(8,128)(2,1)} %cond_ref.1), custom_call_target="tpu_custom_call" | custom-call | tf_op jit(solution)/shard_map/cut/pallas_call | solution.py:519
  13.8 2.0 %constant_dynamic-slice_fusion = bf16[3,64,1024]{2,1,0:T(8,128)(2,1)} fusion(bf16[3,64,8192]{2,1,0:T(8,128)(2,1)} %cond_ref.1, s32[]{:T(128)S(6)} %select_n.3), kind=kLoop, calls=%fused_computation.3 | loop fusion | bytes 786436 | tf_op jit(solution)/shard_map/dynamic_slice | solution.py:527
  15.7 1.0 collective-permute-done.1
  16.7 0.1 maximum_bitcast_fusion.refs_0_
  16.8 1.6 collective-permute-start.3
  18.4 1.5 collective-permute-start.4
  19.9 6.8 %collective-permute-done.3.refs_2_ = bf16[96,2176]{1,0:T(8,128)(2,1)S(1)} collective-permute-done((bf16[96,2176]{1,0:T(8,128)(2,1)S(1)}, bf16[96,2176]{1,0:T(8,128)(2,1)S(1)}, u32[]{:S(2)}, u32[]{:S(2)}) %collective-permute-start.3) | collective-permute-done | bytes 417824 | tf_op jit(solution)/shard_map/ppermute | solution.py:454
  26.7 1.4 collective-permute-done.4.refs_3_
  28.1 0.0 collective-permute-done.5.refs_1_
  28.1 1.6 collective-permute-start.7
  29.7 0.7 slice.7
  30.4 0.5 collective-permute-start.8
  30.9 1.0 pad_maximum_fusion
  31.9 4.7 %all-to-all-start = ((bf16[4,192,256]{2,1,0:T(8,128)(2,1)}), bf16[4,192,256]{2,1,0:T(8,128)(2,1)S(1)}, u32[]{:S(2)}, u32[]{:S(2)}) async-start(bf16[4,192,256]{2,1,0:T(8,128)(2,1)} %cut.1), calls=%async_computation | async-start | bytes 786432 | tf_op jit(solution)/shard_map/all_to_all | solution.py:544
  36.7 0.3 collective-permute-start.9
  37.0 1.9 %collective-permute-start.10 = (bf16[192,1024]{1,0:T(8,128)(2,1)}, bf16[192,1024]{1,0:T(8,128)(2,1)S(1)}, u32[]{:S(2)}, u32[]{:S(2)}) collective-permute-start(bf16[192,1024]{1,0:T(8,128)(2,1)} %bitcast.3), channel_id=1, source_target_pairs={{0,8},{8,0},{16,24},{24,16},{1,9},{9,1},{17,25},{25,17},{2,10},{10... | collective-permute-start | bytes 1179656 | tf_op jit(solution)/shard_map/ppermute | solution.py:454
  38.8 2.4 %collective-permute-start.11 = (bf16[192,1024]{1,0:T(8,128)(2,1)}, bf16[192,1024]{1,0:T(8,128)(2,1)S(1)}, u32[]{:S(2)}, u32[]{:S(2)}) collective-permute-start(bf16[192,1024]{1,0:T(8,128)(2,1)} %bitcast.4), channel_id=1, source_target_pairs={{0,16},{8,24},{16,0},{24,8},{1,17},{9,25},{17,1},{25,9},{2,18},{10... | collective-permute-start | bytes 1179656 | tf_op jit(solution)/shard_map/ppermute | solution.py:454
  41.2 0.1 collective-permute-start.12
  41.4 20.3 %collective-permute-done.10.refs_5_ = bf16[192,1024]{1,0:T(8,128)(2,1)S(1)} collective-permute-done((bf16[192,1024]{1,0:T(8,128)(2,1)}, bf16[192,1024]{1,0:T(8,128)(2,1)S(1)}, u32[]{:S(2)}, u32[]{:S(2)}) %collective-permute-start.10) | collective-permute-done | bytes 393248 | tf_op jit(solution)/shard_map/ppermute | solution.py:454
  61.7 13.3 %collective-permute-done.11.refs_6_ = bf16[192,1024]{1,0:T(8,128)(2,1)S(1)} collective-permute-done((bf16[192,1024]{1,0:T(8,128)(2,1)}, bf16[192,1024]{1,0:T(8,128)(2,1)S(1)}, u32[]{:S(2)}, u32[]{:S(2)}) %collective-permute-start.11) | collective-permute-done | bytes 393248 | tf_op jit(solution)/shard_map/ppermute | solution.py:454
  75.1 0.7 copy-done.17
  75.7 0.1 copy-done.12
  75.9 0.9 copy-done.10
  76.8 5.8 %order.1 = (bf16[768,2048]{1,0:T(8,128)(2,1)}, bf16[2048,768]{1,0:T(8,128)(2,1)}, bf16[768,256]{1,0:T(8,128)(2,1)}, bf16[32,16,128]{2,1,0:T(8,128)(2,1)}) custom-call(bf16[96,2176]{1,0:T(8,128)(2,1)} %copy-done.7, bf16[96,2176]{1,0:T(8,128)(2,1)} %copy-done.11, bf16[96,2176]{1,0:T(8,128)(2,1)} %copy-done.5, bf16[96,2176]{1,0:T(8,128)(2,1)} %copy-done.6, ...), custom_call_target="tpu_custom_call" | custom-call | bytes 9437184 | tf_op jit(solution)/shard_map/order/pallas_call | solution.py:550
  82.6 0.8 copy-done.4
  83.3 2.2 %density.2 = (bf16[3,256,256]{2,1,0:T(8,128)(2,1)}, f32[32,2,128]{2,1,0:T(2,128)}) custom-call(bf16[32,16,128]{2,1,0:T(8,128)(2,1)} %get-tuple-element.72.refs_0_.msgs_ref, bf16[768,256]{1,0:T(8,128)(2,1)} %get-tuple-element.73.refs_1_.refs_3_, bf16[4,192,256]{2,1,0:T(8,128)(2,1)} %copy-done.4), custom_call_target="tpu_custom_call" | custom-call | tf_op jit(solution)/shard_map/density/pallas_call | solution.py:577
  85.5 2.9 %all-to-all-start.1 = ((f32[32,2,128]{2,1,0:T(2,128)}), f32[32,2,128]{2,1,0:T(2,128)S(1)}, u32[]{:S(2)}, u32[]{:S(2)}) async-start(f32[32,2,128]{2,1,0:T(2,128)} %get-tuple-element.75), calls=%async_computation.1 | async-start | bytes 65536 | tf_op jit(solution)/shard_map/all_to_all | solution.py:30
  88.5 12.0 %direct.2.refs_1_ = f32[6,128,128]{2,1,0:T(8,128)} custom-call(bf16[2048,768]{1,0:T(8,128)(2,1)} %get-tuple-element.76.refs_0_, bf16[2048,1024]{1,0:T(8,128)(2,1)} %turn.1.refs_1_, bf16[768,2048]{1,0:T(8,128)(2,1)} %get-tuple-element.78.refs_2_, bf16[3,256,256]{2,1,0:T(8,128)(2,1)} %get-tuple-element.79.refs_3_, bf16[192,1024]{1,0:T(8,128)(2,1)} %bitcast.6, ...), custom_call_target="tpu_custom_call" | custom-call | flops 6442450944 | bytes 12582912 | tf_op jit(solution)/shard_map/direct/pallas_call | solution.py:595
  100.5 0.0 copy-start.3
  100.5 0.6 copy-done.14
  101.1 3.7 %exchange.2 = bf16[32,16,128]{2,1,0:T(8,128)(2,1)} custom-call(f32[32,2,128]{2,1,0:T(2,128)} %copy-done.14, f32[6,128,128]{2,1,0:T(8,128)} %direct.2.refs_1_, bf16[256,8192]{1,0:T(8,128)(2,1)} %refs_2_.5, bf16[768,256]{1,0:T(8,128)(2,1)} %get-tuple-element.73.refs_1_.refs_3_, bf16[4,192,256]{2,1,0:T(8,128)(2,1)} %copy-done.4), custom_call_target="tpu_custom_call" | custom-call | tf_op jit(solution)/shard_map/exchange/pallas_call | solution.py:618
  104.9 13.9 %all_to_all.35.recv_ref = bf16[32,16,128]{2,1,0:T(8,128)(2,1)S(1)} all-to-all(bf16[32,16,128]{2,1,0:T(8,128)(2,1)} %exchange.2), channel_id=1, replica_groups=mesh['ka'=4,'band'=8] {'ka','band'}, dimensions={0} | all-to-all | bytes 262144 | tf_op jit(solution)/shard_map/all_to_all | solution.py:30
  118.8 0.3 first_owner.1
  119.1 10.6 %all_to_all.36.refs_0_.msgs_ref = bf16[32,16,128]{2,1,0:T(8,128)(2,1)} all-to-all(bf16[32,16,128]{2,1,0:T(8,128)(2,1)S(1)} %get-tuple-element.84), channel_id=1, replica_groups=mesh['ka'=4,'band'=8] {'ka','band'}, dimensions={0} | all-to-all | bytes 262144 | tf_op jit(solution)/shard_map/all_to_all | solution.py:30
  129.7 2.3 %density.3 = (bf16[3,256,256]{2,1,0:T(8,128)(2,1)}, f32[32,2,128]{2,1,0:T(2,128)}) custom-call(bf16[32,16,128]{2,1,0:T(8,128)(2,1)} %all_to_all.36.refs_0_.msgs_ref, bf16[768,256]{1,0:T(8,128)(2,1)} %get-tuple-element.73.refs_1_.refs_3_, bf16[4,192,256]{2,1,0:T(8,128)(2,1)} %copy-done.4), custom_call_target="tpu_custom_call" | custom-call | tf_op jit(solution)/shard_map/density/pallas_call | solution.py:577
  132.0 2.7 %all-to-all-start.4 = ((f32[32,2,128]{2,1,0:T(2,128)}), f32[32,2,128]{2,1,0:T(2,128)S(1)}, u32[]{:S(2)}, u32[]{:S(2)}) async-start(f32[32,2,128]{2,1,0:T(2,128)} %get-tuple-element.85), calls=%async_computation.4 | async-start | bytes 65536 | tf_op jit(solution)/shard_map/all_to_all | solution.py:30
  134.7 12.0 %direct.3.refs_1_ = f32[6,128,128]{2,1,0:T(8,128)} custom-call(bf16[2048,768]{1,0:T(8,128)(2,1)} %get-tuple-element.76.refs_0_, bf16[2048,1024]{1,0:T(8,128)(2,1)} %turn.1.refs_1_, bf16[768,2048]{1,0:T(8,128)(2,1)} %get-tuple-element.78.refs_2_, bf16[3,256,256]{2,1,0:T(8,128)(2,1)} %get-tuple-element.86.refs_3_, bf16[192,1024]{1,0:T(8,128)(2,1)} %bitcast.7, ...), custom_call_target="tpu_custom_call" | custom-call | flops 6442450944 | bytes 12582912 | tf_op jit(solution)/shard_map/direct/pallas_call | solution.py:595
  146.7 0.6 copy-done.13
  147.3 3.7 %exchange.3 = bf16[32,16,128]{2,1,0:T(8,128)(2,1)} custom-call(f32[32,2,128]{2,1,0:T(2,128)} %copy-done.13, f32[6,128,128]{2,1,0:T(8,128)} %direct.3.refs_1_, bf16[256,8192]{1,0:T(8,128)(2,1)} %refs_2_.5, bf16[768,256]{1,0:T(8,128)(2,1)} %get-tuple-element.73.refs_1_.refs_3_, bf16[4,192,256]{2,1,0:T(8,128)(2,1)} %copy-done.4), custom_call_target="tpu_custom_call" | custom-call | tf_op jit(solution)/shard_map/exchange/pallas_call | solution.py:618
  151.1 13.9 %all_to_all.37.recv_ref = bf16[32,16,128]{2,1,0:T(8,128)(2,1)S(1)} all-to-all(bf16[32,16,128]{2,1,0:T(8,128)(2,1)} %exchange.3), channel_id=1, replica_groups=mesh['ka'=4,'band'=8] {'ka','band'}, dimensions={0} | all-to-all | bytes 262144 | tf_op jit(solution)/shard_map/all_to_all | solution.py:30
  165.0 0.4 second_owner.1
  165.3 9.0 %all_to_all.38.msgs_ref = f32[32,2,128]{2,1,0:T(2,128)S(1)} all-to-all(f32[32,2,128]{2,1,0:T(2,128)S(1)} %get-tuple-element.89), channel_id=1, replica_groups=mesh['ka'=4,'band'=8] {'ka','band'}, dimensions={0} | all-to-all | bytes 65536 | tf_op jit(solution)/shard_map/all_to_all | solution.py:30
  174.4 0.8 finish.1
  (43 shorter events, 0.1 us)
Async XLA Ops:
  2.5 13.2 %collective-permute-start = (bf16[3,8,2176]{2,1,0:T(8,128)(2,1)}, bf16[3,8,2176]{2,1,0:T(8,128)(2,1)S(1)}, u32[]{:S(2)}, u32[]{:S(2)}) collective-permute-start(bf16[3,8,2176]{2,1,0:T(8,128)(2,1)} %get-tuple-element.52), channel_id=1, source_target_pairs={{0,8},{8,0},{16,24},{24,16},{1,9},{9,1},{17,25},{25,17},{2,10},{10... | collective-permute-start | bytes 313352 | tf_op jit(solution)/shard_map/ppermute | solution.py:454
  5.6 11.1 %collective-permute-start.1 = (bf16[3,8,2176]{2,1,0:T(8,128)(2,1)}, bf16[3,8,2176]{2,1,0:T(8,128)(2,1)S(1)}, u32[]{:S(2)}, u32[]{:S(2)}) collective-permute-start(bf16[3,8,2176]{2,1,0:T(8,128)(2,1)} %get-tuple-element.53), channel_id=1, source_target_pairs={{0,16},{8,24},{16,0},{24,8},{1,17},{9,25},{17,1},{25,9},{2,18},{10... | collective-permute-start | bytes 313352 | tf_op jit(solution)/shard_map/ppermute | solution.py:454
  8.2 8.5 %collective-permute-start.2 = (bf16[3,8,2176]{2,1,0:T(8,128)(2,1)}, bf16[3,8,2176]{2,1,0:T(8,128)(2,1)S(1)}, u32[]{:S(2)}, u32[]{:S(2)}) collective-permute-start(bf16[3,8,2176]{2,1,0:T(8,128)(2,1)} %get-tuple-element.54), channel_id=1, source_target_pairs={{0,24},{8,16},{16,8},{24,0},{1,25},{9,17},{17,9},{25,1},{2,26},{10... | collective-permute-start | bytes 313352 | tf_op jit(solution)/shard_map/ppermute | solution.py:454
  11.9 4.8 %copy-start.15 = (bf16[3,8,2176]{2,1,0:T(8,128)(2,1)S(1)}, bf16[3,8,2176]{2,1,0:T(8,128)(2,1)}, u32[]{:S(2)}) copy-start(bf16[3,8,2176]{2,1,0:T(8,128)(2,1)} %get-tuple-element.56) | copy-start | bytes 313348
  16.8 58.2 %copy-start.7 = (bf16[96,2176]{1,0:T(8,128)(2,1)}, bf16[96,2176]{1,0:T(8,128)(2,1)S(1)}, u32[]{:S(2)}) copy-start(bf16[96,2176]{1,0:T(8,128)(2,1)S(1)} %maximum_bitcast_fusion.refs_0_) | copy-start | bytes 1253380
  16.8 9.9 %collective-permute-start.3 = (bf16[96,2176]{1,0:T(8,128)(2,1)S(1)}, bf16[96,2176]{1,0:T(8,128)(2,1)S(1)}, u32[]{:S(2)}, u32[]{:S(2)}) collective-permute-start(bf16[96,2176]{1,0:T(8,128)(2,1)S(1)} %maximum_bitcast_fusion.refs_0_), channel_id=1, source_target_pairs={{0,2},{1,3},{2,0},{3,1},{4,6},{5,7},{6,4},{7,5},{8,10},{9,11},{10,... | collective-permute-start | bytes 1253384 | tf_op jit(solution)/shard_map/ppermute | solution.py:454
  18.4 9.7 %collective-permute-start.4 = (bf16[96,2176]{1,0:T(8,128)(2,1)S(1)}, bf16[96,2176]{1,0:T(8,128)(2,1)S(1)}, u32[]{:S(2)}, u32[]{:S(2)}) collective-permute-start(bf16[96,2176]{1,0:T(8,128)(2,1)S(1)} %maximum_bitcast_fusion.refs_0_), channel_id=1, source_target_pairs={{0,4},{1,5},{2,6},{3,7},{4,0},{5,1},{6,2},{7,3},{8,12},{9,13},{10,... | collective-permute-start | bytes 1253384 | tf_op jit(solution)/shard_map/ppermute | solution.py:454
  19.9 8.2 %collective-permute-start.5 = (bf16[96,2176]{1,0:T(8,128)(2,1)S(1)}, bf16[96,2176]{1,0:T(8,128)(2,1)S(1)}, u32[]{:S(2)}, u32[]{:S(2)}) collective-permute-start(bf16[96,2176]{1,0:T(8,128)(2,1)S(1)} %maximum_bitcast_fusion.refs_0_), channel_id=1, source_target_pairs={{0,1},{1,0},{2,3},{3,2},{4,5},{5,4},{6,7},{7,6},{8,9},{9,8},{10,11... | collective-permute-start | bytes 1253384 | tf_op jit(solution)/shard_map/ppermute | solution.py:454
  26.7 48.3 %copy-start.5 = (bf16[96,2176]{1,0:T(8,128)(2,1)}, bf16[96,2176]{1,0:T(8,128)(2,1)S(1)}, u32[]{:S(2)}) copy-start(bf16[96,2176]{1,0:T(8,128)(2,1)S(1)} %collective-permute-done.3.refs_2_) | copy-start | bytes 1253380
  28.1 46.9 %copy-start.6 = (bf16[96,2176]{1,0:T(8,128)(2,1)}, bf16[96,2176]{1,0:T(8,128)(2,1)S(1)}, u32[]{:S(2)}) copy-start(bf16[96,2176]{1,0:T(8,128)(2,1)S(1)} %collective-permute-done.4.refs_3_) | copy-start | bytes 1253380
  28.1 46.9 %copy-start.11 = (bf16[96,2176]{1,0:T(8,128)(2,1)}, bf16[96,2176]{1,0:T(8,128)(2,1)S(1)}, u32[]{:S(2)}) copy-start(bf16[96,2176]{1,0:T(8,128)(2,1)S(1)} %collective-permute-done.5.refs_1_) | copy-start | bytes 1253380
  28.1 8.5 %collective-permute-start.7 = (bf16[48,2176]{1,0:T(8,128)(2,1)S(1)}, bf16[48,2176]{1,0:T(8,128)(2,1)S(1)}, u32[]{:S(2)}, u32[]{:S(2)}) collective-permute-start(bf16[48,2176]{1,0:T(8,128)(2,1)S(1)} %slice.6), channel_id=1, source_target_pairs={{0,4},{1,5},{2,6},{3,7},{4,0},{5,1},{6,2},{7,3},{8,12},{9,13},{10,... | collective-permute-start | bytes 626696 | tf_op jit(solution)/shard_map/ppermute | solution.py:454
  30.4 6.2 %collective-permute-start.8 = (bf16[48,2176]{1,0:T(8,128)(2,1)}, bf16[48,2176]{1,0:T(8,128)(2,1)S(1)}, u32[]{:S(2)}, u32[]{:S(2)}) collective-permute-start(bf16[48,2176]{1,0:T(8,128)(2,1)} %slice.7), channel_id=1, source_target_pairs={{0,2},{1,3},{2,0},{3,1},{4,6},{5,7},{6,4},{7,5},{8,10},{9,11},{10,... | collective-permute-start | bytes 626696 | tf_op jit(solution)/shard_map/ppermute | solution.py:454
  31.9 43.1 %collective-permute-start.6 = (bf16[192,2176]{1,0:T(8,128)(2,1)}, bf16[192,2176]{1,0:T(8,128)(2,1)S(1)}, u32[]{:S(2)}, u32[]{:S(2)}) collective-permute-start(bf16[192,2176]{1,0:T(8,128)(2,1)} %pad_maximum_fusion), channel_id=1, source_target_pairs={{0,1},{1,0},{2,3},{3,2},{4,5},{5,4},{6,7},{7,6},{8,9},{9,8},{10,11... | collective-permute-start | bytes 2506760 | tf_op jit(solution)/shard_map/ppermute | solution.py:454
  31.9 50.6 %all-to-all-start = ((bf16[4,192,256]{2,1,0:T(8,128)(2,1)}), bf16[4,192,256]{2,1,0:T(8,128)(2,1)S(1)}, u32[]{:S(2)}, u32[]{:S(2)}) async-start(bf16[4,192,256]{2,1,0:T(8,128)(2,1)} %cut.1), calls=%async_computation | async-start | bytes 786432 | tf_op jit(solution)/shard_map/all_to_all | solution.py:544
  36.6 38.4 %copy-start.8 = (bf16[48,2176]{1,0:T(8,128)(2,1)}, bf16[48,2176]{1,0:T(8,128)(2,1)S(1)}, u32[]{:S(2)}) copy-start(bf16[48,2176]{1,0:T(8,128)(2,1)S(1)} %collective-permute-done.7.refs_5_) | copy-start | bytes 626692
  36.6 38.4 %copy-start.9 = (bf16[48,2176]{1,0:T(8,128)(2,1)}, bf16[48,2176]{1,0:T(8,128)(2,1)S(1)}, u32[]{:S(2)}) copy-start(bf16[48,2176]{1,0:T(8,128)(2,1)S(1)} %collective-permute-done.8.refs_6_) | copy-start | bytes 626692
  36.7 38.3 %collective-permute-start.9 = (bf16[96,2176]{1,0:T(8,128)(2,1)S(1)}, bf16[96,2176]{1,0:T(8,128)(2,1)S(1)}, u32[]{:S(2)}, u32[]{:S(2)}) collective-permute-start(bf16[96,2176]{1,0:T(8,128)(2,1)S(1)} %pad_maximum_fusion.1), channel_id=1, source_target_pairs={{0,1},{1,0},{2,3},{3,2},{4,5},{5,4},{6,7},{7,6},{8,9},{9,8},{10,11... | collective-permute-start | bytes 1253384 | tf_op jit(solution)/shard_map/ppermute | solution.py:454
  37.0 24.7 %collective-permute-start.10 = (bf16[192,1024]{1,0:T(8,128)(2,1)}, bf16[192,1024]{1,0:T(8,128)(2,1)S(1)}, u32[]{:S(2)}, u32[]{:S(2)}) collective-permute-start(bf16[192,1024]{1,0:T(8,128)(2,1)} %bitcast.3), channel_id=1, source_target_pairs={{0,8},{8,0},{16,24},{24,16},{1,9},{9,1},{17,25},{25,17},{2,10},{10... | collective-permute-start | bytes 1179656 | tf_op jit(solution)/shard_map/ppermute | solution.py:454
  38.8 36.1 %collective-permute-start.11 = (bf16[192,1024]{1,0:T(8,128)(2,1)}, bf16[192,1024]{1,0:T(8,128)(2,1)S(1)}, u32[]{:S(2)}, u32[]{:S(2)}) collective-permute-start(bf16[192,1024]{1,0:T(8,128)(2,1)} %bitcast.4), channel_id=1, source_target_pairs={{0,16},{8,24},{16,0},{24,8},{1,17},{9,25},{17,1},{25,9},{2,18},{10... | collective-permute-start | bytes 1179656 | tf_op jit(solution)/shard_map/ppermute | solution.py:454
  41.2 47.3 %collective-permute-start.12 = (bf16[192,1024]{1,0:T(8,128)(2,1)}, bf16[192,1024]{1,0:T(8,128)(2,1)}, u32[]{:S(2)}, u32[]{:S(2)}) collective-permute-start(bf16[192,1024]{1,0:T(8,128)(2,1)} %bitcast.5), channel_id=1, source_target_pairs={{0,24},{8,16},{16,8},{24,0},{1,25},{9,17},{17,9},{25,1},{2,26},{10... | collective-permute-start | bytes 1179656 | tf_op jit(solution)/shard_map/ppermute | solution.py:454
  61.7 13.4 %copy-start.16 = (bf16[192,1024]{1,0:T(8,128)(2,1)}, bf16[192,1024]{1,0:T(8,128)(2,1)S(1)}, u32[]{:S(2)}) copy-start(bf16[192,1024]{1,0:T(8,128)(2,1)S(1)} %collective-permute-done.10.refs_5_) | copy-start | bytes 1179652
  75.0 0.8 copy-start.17
  75.0 0.9 copy-start.12
  75.9 0.9 copy-start.10
  82.5 0.8 copy-start.4
  85.5 15.0 %all-to-all-start.1 = ((f32[32,2,128]{2,1,0:T(2,128)}), f32[32,2,128]{2,1,0:T(2,128)S(1)}, u32[]{:S(2)}, u32[]{:S(2)}) async-start(f32[32,2,128]{2,1,0:T(2,128)} %get-tuple-element.75), calls=%async_computation.1 | async-start | bytes 65536 | tf_op jit(solution)/shard_map/all_to_all | solution.py:30
  100.5 18.3 %copy-start.1 = (bf16[32,16,128]{2,1,0:T(8,128)(2,1)S(1)}, bf16[32,16,128]{2,1,0:T(8,128)(2,1)}, u32[]{:S(2)}) copy-start(bf16[32,16,128]{2,1,0:T(8,128)(2,1)} %get-tuple-element.72.refs_0_.msgs_ref) | copy-start | bytes 393220
  100.5 18.3 %copy-start.2 = (f32[16,128]{1,0:T(8,128)S(1)}, f32[16,128]{1,0:T(8,128)}, u32[]{:S(2)}) copy-start(f32[16,128]{1,0:T(8,128)} %get-tuple-element.82.gap_ref) | copy-start | bytes 24580
  100.5 18.3 %copy-start.3 = (f32[16,128]{1,0:T(8,128)S(1)}, f32[16,128]{1,0:T(8,128)}, u32[]{:S(2)}) copy-start(f32[16,128]{1,0:T(8,128)} %get-tuple-element.83.own_ref) | copy-start | bytes 24580
  100.5 0.6 copy-start.14
  132.0 14.7 %all-to-all-start.4 = ((f32[32,2,128]{2,1,0:T(2,128)}), f32[32,2,128]{2,1,0:T(2,128)S(1)}, u32[]{:S(2)}, u32[]{:S(2)}) async-start(f32[32,2,128]{2,1,0:T(2,128)} %get-tuple-element.85), calls=%async_computation.4 | async-start | bytes 65536 | tf_op jit(solution)/shard_map/all_to_all | solution.py:30
  146.7 18.2 %copy-start = (bf16[32,16,128]{2,1,0:T(8,128)(2,1)S(1)}, bf16[32,16,128]{2,1,0:T(8,128)(2,1)}, u32[]{:S(2)}) copy-start(bf16[32,16,128]{2,1,0:T(8,128)(2,1)} %all_to_all.36.refs_0_.msgs_ref) | copy-start | bytes 393220
  146.7 0.6 copy-start.13

commit v19 on v17

--- a/solution.py
+++ b/solution.py
@@ -15,6 +15,7 @@
 HALF = 64
 ROWS = 8
 MIB = 1 << 20
+VMEM_ALL = 63_400_000
 
 VMEM = pl.BlockSpec(memory_space=pltpu.VMEM)
 SMEM = pl.BlockSpec(memory_space=pltpu.SMEM)
@@ -433,14 +434,14 @@
     return jax.ShapeDtypeStruct(dims, kind)
 
 
-def call(kernel, name, out_shape, in_specs, out_specs, scratch=(), mib=58, flops=0, moved=0):
+def call(kernel, name, out_shape, in_specs, out_specs, scratch=(), mib=None, flops=0, moved=0):
     return pl.pallas_call(
         kernel,
         out_shape=out_shape,
         in_specs=in_specs,
         out_specs=out_specs,
         scratch_shapes=list(scratch),
-        compiler_params=pltpu.CompilerParams(vmem_limit_bytes=mib * MIB),
+        compiler_params=pltpu.CompilerParams(vmem_limit_bytes=mib * MIB if mib else VMEM_ALL),
         cost_estimate=pl.CostEstimate(flops=flops, bytes_accessed=moved, transcendentals=0),
         name=name,
     )

time: 152 us -> 151 us (level)
    unnamed x44 -> x38, local copies, waits for them, and re-layouts: 4.29 us -> 3.57 us
where the time goes in v19:
time: 151 us; the launch traced here: 150 us
  Pallas kernels  50.4 us (33%)
  blocking collectives  47.4 us (31%)
  starting transfers between devices  26.4 us (17%)
  waiting for transfers between devices  20.2 us (13%)
  local copies, waits for them, and re-layouts  4.8 us (3%)
    all_to_all x4, blocking collectives, exchange_all(): return lax.all_to_all(parts, AXES, split_axis=0, concat_axis=0, tiled=True)  47.4 us
    pallas_call x2, Pallas kernels, kernel_path(): call(functools.partial(direct_kernel, n_ka, tile, scale), 'direct', shape...  23.9 us
    ppermute x15, waiting for transfers between devices, swap(): lax.ppermute(block, axis, [(i, i ^ d) for i in range(lax.axis_size(axis))])  20.2 us
    ppermute x15, starting transfers between devices, swap(): lax.ppermute(block, axis, [(i, i ^ d) for i in range(lax.axis_size(axis))])  17.4 us
    pallas_call x2, Pallas kernels, kernel_path(): call(functools.partial(exchange_kernel, cfg, chunk, scale), 'exchange', m...  7.47 us
    pallas_call x1, Pallas kernels, kernel_path(): call(functools.partial(order_kernel, parts, n_ka), 'order', (shape_of((ro...  5.69 us
    all_to_all x2, starting transfers between devices, exchange_all(): return lax.all_to_all(parts, AXES, split_axis=0, concat_axis=0, tiled=True)  5.5 us
    pallas_call x2, Pallas kernels, kernel_path(): call(functools.partial(density_kernel, cfg), 'density', (shape_of((quads,...  4.49 us
  transfers between devices with their start and end apart: 18, of which 5 were waited for; matrix products, arithmetic and copies ran while one was open for 1% of the time, Pallas kernels for 25%

profile of v19, /device:TPU:0, one launch (start us, length us, event | category | flops | bytes accessed | tf_op | source)
XLA Modules:
  0.0 150.4 jit_solution(3830976992188487016)
XLA Ops:
  0.6 1.9 %pack.1 = (f32[16,128]{1,0:T(8,128)}, f32[16,128]{1,0:T(8,128)}, bf16[3,8,2176]{2,1,0:T(8,128)(2,1)}, bf16[3,8,2176]{2,1,0:T(8,128)(2,1)}, bf16[3,8,2176]{2,1,0:T(8,128)(2,1)}, /*index=5*/bf16[3,8,2176]{2,1,0:T(8,128)(2,1)}) custom-call(f32[3,512]{1,0:T(4,128)} %refs_0_.1, f32[3,64]{1,0:T(4,128)} %refs_1_.1, f32[3,8]{1,0:T(4,128)} %refs_2_.3, ...), custom_call_target="tpu_custom_call" | custom-call | tf_op jit(solution)/shard_map/pack/pallas_call | solution.py:495
  2.5 3.1 %collective-permute-start = (bf16[3,8,2176]{2,1,0:T(8,128)(2,1)}, bf16[3,8,2176]{2,1,0:T(8,128)(2,1)S(1)}, u32[]{:S(2)}, u32[]{:S(2)}) collective-permute-start(bf16[3,8,2176]{2,1,0:T(8,128)(2,1)} %get-tuple-element.53), channel_id=1, source_target_pairs={{0,8},{8,0},{16,24},{24,16},{1,9},{9,1},{17,25},{25,17},{2,10},{10... | collective-permute-start | bytes 313352 | tf_op jit(solution)/shard_map/ppermute | solution.py:455
  5.6 2.6 %collective-permute-start.1 = (bf16[3,8,2176]{2,1,0:T(8,128)(2,1)}, bf16[3,8,2176]{2,1,0:T(8,128)(2,1)S(1)}, u32[]{:S(2)}, u32[]{:S(2)}) collective-permute-start(bf16[3,8,2176]{2,1,0:T(8,128)(2,1)} %get-tuple-element.54), channel_id=1, source_target_pairs={{0,16},{8,24},{16,0},{24,8},{1,17},{9,25},{17,1},{25,9},{2,18},{10... | collective-permute-start | bytes 313352 | tf_op jit(solution)/shard_map/ppermute | solution.py:455
  8.2 1.8 %cut.1 = bf16[4,192,256]{2,1,0:T(8,128)(2,1)} custom-call(bf16[3,64,8192]{2,1,0:T(8,128)(2,1)} %cond_ref.1), custom_call_target="tpu_custom_call" | custom-call | tf_op jit(solution)/shard_map/cut/pallas_call | solution.py:512
  10.0 1.2 constant_dynamic-slice_fusion
  11.2 0.0 collective-permute-done
  11.3 5.5 %collective-permute-done.1 = bf16[3,8,2176]{2,1,0:T(8,128)(2,1)S(1)} collective-permute-done((bf16[3,8,2176]{2,1,0:T(8,128)(2,1)}, bf16[3,8,2176]{2,1,0:T(8,128)(2,1)S(1)}, u32[]{:S(2)}, u32[]{:S(2)}) %collective-permute-start.1) | collective-permute-done | bytes 104480 | tf_op jit(solution)/shard_map/ppermute | solution.py:455
  16.7 0.0 collective-permute-done.2
  16.7 0.1 maximum_bitcast_fusion.refs_0_
  16.8 1.6 %collective-permute-start.4 = (bf16[96,2176]{1,0:T(8,128)(2,1)S(1)}, bf16[96,2176]{1,0:T(8,128)(2,1)S(1)}, u32[]{:S(2)}, u32[]{:S(2)}) collective-permute-start(bf16[96,2176]{1,0:T(8,128)(2,1)S(1)} %maximum_bitcast_fusion.refs_0_), channel_id=1, source_target_pairs={{0,2},{1,3},{2,0},{3,1},{4,6},{5,7},{6,4},{7,5},{8,10},{9,11},{10,... | collective-permute-start | bytes 1253384 | tf_op jit(solution)/shard_map/ppermute | solution.py:455
  18.4 1.5 %collective-permute-start.5 = (bf16[96,2176]{1,0:T(8,128)(2,1)S(1)}, bf16[96,2176]{1,0:T(8,128)(2,1)S(1)}, u32[]{:S(2)}, u32[]{:S(2)}) collective-permute-start(bf16[96,2176]{1,0:T(8,128)(2,1)S(1)} %maximum_bitcast_fusion.refs_0_), channel_id=1, source_target_pairs={{0,4},{1,5},{2,6},{3,7},{4,0},{5,1},{6,2},{7,3},{8,12},{9,13},{10,... | collective-permute-start | bytes 1253384 | tf_op jit(solution)/shard_map/ppermute | solution.py:455
  19.9 1.7 %collective-permute-start.12 = (bf16[192,1024]{1,0:T(8,128)(2,1)S(1)}, bf16[192,1024]{1,0:T(8,128)(2,1)}, u32[]{:S(2)}, u32[]{:S(2)}) collective-permute-start(bf16[192,1024]{1,0:T(8,128)(2,1)S(1)} %bitcast.3), channel_id=1, source_target_pairs={{0,8},{8,0},{16,24},{24,16},{1,9},{9,1},{17,25},{25,17},{2,10},{10... | collective-permute-start | bytes 1179656 | tf_op jit(solution)/shard_map/ppermute | solution.py:455
  21.6 1.4 collective-permute-start.13
  22.9 3.5 %all-to-all-start = ((bf16[4,192,256]{2,1,0:T(8,128)(2,1)}), bf16[4,192,256]{2,1,0:T(8,128)(2,1)S(1)}, u32[]{:S(2)}, u32[]{:S(2)}) async-start(bf16[4,192,256]{2,1,0:T(8,128)(2,1)} %cut.1), calls=%async_computation | async-start | bytes 786432 | tf_op jit(solution)/shard_map/all_to_all | solution.py:525
  26.4 3.7 %turn.1.refs_1_ = bf16[2048,1024]{1,0:T(8,128)(2,1)} custom-call(bf16[1024,2048]{1,0:T(8,128)(2,1)} %scr_ref.1), custom_call_target="tpu_custom_call" | custom-call | bytes 8388608 | tf_op jit(solution)/shard_map/turn/pallas_call | solution.py:529
  30.2 0.6 collective-permute-start.8
  30.8 0.6 collective-permute-start.9
  31.4 6.8 %collective-permute-done.12.refs_5_ = bf16[192,1024]{1,0:T(8,128)(2,1)} collective-permute-done((bf16[192,1024]{1,0:T(8,128)(2,1)S(1)}, bf16[192,1024]{1,0:T(8,128)(2,1)}, u32[]{:S(2)}, u32[]{:S(2)}) %collective-permute-start.12) | collective-permute-done | bytes 393248 | tf_op jit(solution)/shard_map/ppermute | solution.py:455
  38.2 6.6 %collective-permute-done.13.refs_6_ = bf16[192,1024]{1,0:T(8,128)(2,1)} collective-permute-done((bf16[192,1024]{1,0:T(8,128)(2,1)S(1)}, bf16[192,1024]{1,0:T(8,128)(2,1)}, u32[]{:S(2)}, u32[]{:S(2)}) %collective-permute-start.13) | collective-permute-done | bytes 393248 | tf_op jit(solution)/shard_map/ppermute | solution.py:455
  44.8 3.9 %collective-permute-start.14 = (bf16[192,1024]{1,0:T(8,128)(2,1)S(1)}, bf16[192,1024]{1,0:T(8,128)(2,1)}, u32[]{:S(2)}, u32[]{:S(2)}) collective-permute-start(bf16[192,1024]{1,0:T(8,128)(2,1)S(1)} %bitcast.5), channel_id=1, source_target_pairs={{0,24},{8,16},{16,8},{24,0},{1,25},{9,17},{17,9},{25,1},{2,26},{10... | collective-permute-start | bytes 1179656 | tf_op jit(solution)/shard_map/ppermute | solution.py:455
  48.8 0.2 collective-permute-start.10
  49.0 0.3 collective-permute-start.11
  49.3 0.9 collective-permute-done.10.refs_8_
  50.2 0.3 collective-permute-done.11.refs_9_
  50.6 0.3 copy-done.14
  50.9 0.3 copy-done.15
  51.2 0.2 copy-done.9
  51.4 0.8 copy-done.10
  52.2 5.7 %order.1 = (bf16[768,2048]{1,0:T(8,128)(2,1)}, bf16[2048,768]{1,0:T(8,128)(2,1)}, bf16[768,256]{1,0:T(8,128)(2,1)}, bf16[32,16,128]{2,1,0:T(8,128)(2,1)}) custom-call(bf16[96,2176]{1,0:T(8,128)(2,1)} %copy-done.5, bf16[96,2176]{1,0:T(8,128)(2,1)} %copy-done.8, bf16[96,2176]{1,0:T(8,128)(2,1)} %copy-done.6, bf16[96,2176]{1,0:T(8,128)(2,1)} %copy-done.9, ...), custom_call_target="tpu_custom_call" | custom-call | bytes 9437184 | tf_op jit(solution)/shard_map/order/pallas_call | solution.py:541
  57.9 0.7 copy-done.4
  58.6 2.2 %density.2 = (bf16[3,256,256]{2,1,0:T(8,128)(2,1)}, f32[32,2,128]{2,1,0:T(2,128)}) custom-call(bf16[32,16,128]{2,1,0:T(8,128)(2,1)} %get-tuple-element.74.refs_0_.msgs_ref, bf16[768,256]{1,0:T(8,128)(2,1)} %get-tuple-element.75.refs_1_.refs_3_, bf16[4,192,256]{2,1,0:T(8,128)(2,1)} %copy-done.4), custom_call_target="tpu_custom_call" | custom-call | tf_op jit(solution)/shard_map/density/pallas_call | solution.py:568
  60.9 2.7 %all-to-all-start.1 = ((f32[32,2,128]{2,1,0:T(2,128)}), f32[32,2,128]{2,1,0:T(2,128)S(1)}, u32[]{:S(2)}, u32[]{:S(2)}) async-start(f32[32,2,128]{2,1,0:T(2,128)} %get-tuple-element.77), calls=%async_computation.1 | async-start | bytes 65536 | tf_op jit(solution)/shard_map/all_to_all | solution.py:31
  63.6 12.0 %direct.2.refs_1_ = f32[6,128,128]{2,1,0:T(8,128)} custom-call(bf16[2048,768]{1,0:T(8,128)(2,1)} %get-tuple-element.78.refs_0_, bf16[2048,1024]{1,0:T(8,128)(2,1)} %turn.1.refs_1_, bf16[768,2048]{1,0:T(8,128)(2,1)} %get-tuple-element.80.refs_2_, bf16[3,256,256]{2,1,0:T(8,128)(2,1)} %get-tuple-element.81.refs_3_, bf16[192,1024]{1,0:T(8,128)(2,1)} %bitcast.6, ...), custom_call_target="tpu_custom_call" | custom-call | flops 6442450944 | bytes 12582912 | tf_op jit(solution)/shard_map/direct/pallas_call | solution.py:586
  75.6 0.0 copy-start.3
  75.6 0.6 copy-done.17
  76.2 3.7 %exchange.2 = bf16[32,16,128]{2,1,0:T(8,128)(2,1)} custom-call(f32[32,2,128]{2,1,0:T(2,128)} %copy-done.17, f32[6,128,128]{2,1,0:T(8,128)} %direct.2.refs_1_, bf16[256,8192]{1,0:T(8,128)(2,1)} %refs_2_.5, bf16[768,256]{1,0:T(8,128)(2,1)} %get-tuple-element.75.refs_1_.refs_3_, bf16[4,192,256]{2,1,0:T(8,128)(2,1)} %copy-done.4), custom_call_target="tpu_custom_call" | custom-call | tf_op jit(solution)/shard_map/exchange/pallas_call | solution.py:609
  79.9 13.9 %all_to_all.35.recv_ref = bf16[32,16,128]{2,1,0:T(8,128)(2,1)S(1)} all-to-all(bf16[32,16,128]{2,1,0:T(8,128)(2,1)} %exchange.2), channel_id=1, replica_groups=mesh['ka'=4,'band'=8] {'ka','band'}, dimensions={0} | all-to-all | bytes 262144 | tf_op jit(solution)/shard_map/all_to_all | solution.py:31
  93.9 0.3 first_owner.1
  94.2 10.6 %all_to_all.36.refs_0_.msgs_ref = bf16[32,16,128]{2,1,0:T(8,128)(2,1)} all-to-all(bf16[32,16,128]{2,1,0:T(8,128)(2,1)S(1)} %get-tuple-element.86), channel_id=1, replica_groups=mesh['ka'=4,'band'=8] {'ka','band'}, dimensions={0} | all-to-all | bytes 262144 | tf_op jit(solution)/shard_map/all_to_all | solution.py:31
  104.8 2.2 %density.3 = (bf16[3,256,256]{2,1,0:T(8,128)(2,1)}, f32[32,2,128]{2,1,0:T(2,128)}) custom-call(bf16[32,16,128]{2,1,0:T(8,128)(2,1)} %all_to_all.36.refs_0_.msgs_ref, bf16[768,256]{1,0:T(8,128)(2,1)} %get-tuple-element.75.refs_1_.refs_3_, bf16[4,192,256]{2,1,0:T(8,128)(2,1)} %copy-done.4), custom_call_target="tpu_custom_call" | custom-call | tf_op jit(solution)/shard_map/density/pallas_call | solution.py:568
  107.1 2.8 %all-to-all-start.4 = ((f32[32,2,128]{2,1,0:T(2,128)}), f32[32,2,128]{2,1,0:T(2,128)S(1)}, u32[]{:S(2)}, u32[]{:S(2)}) async-start(f32[32,2,128]{2,1,0:T(2,128)} %get-tuple-element.87), calls=%async_computation.4 | async-start | bytes 65536 | tf_op jit(solution)/shard_map/all_to_all | solution.py:31
  109.9 12.0 %direct.3.refs_1_ = f32[6,128,128]{2,1,0:T(8,128)} custom-call(bf16[2048,768]{1,0:T(8,128)(2,1)} %get-tuple-element.78.refs_0_, bf16[2048,1024]{1,0:T(8,128)(2,1)} %turn.1.refs_1_, bf16[768,2048]{1,0:T(8,128)(2,1)} %get-tuple-element.80.refs_2_, bf16[3,256,256]{2,1,0:T(8,128)(2,1)} %get-tuple-element.88.refs_3_, bf16[192,1024]{1,0:T(8,128)(2,1)} %bitcast.7, ...), custom_call_target="tpu_custom_call" | custom-call | flops 6442450944 | bytes 12582912 | tf_op jit(solution)/shard_map/direct/pallas_call | solution.py:586
  121.9 0.6 copy-done.16
  122.5 3.7 %exchange.3 = bf16[32,16,128]{2,1,0:T(8,128)(2,1)} custom-call(f32[32,2,128]{2,1,0:T(2,128)} %copy-done.16, f32[6,128,128]{2,1,0:T(8,128)} %direct.3.refs_1_, bf16[256,8192]{1,0:T(8,128)(2,1)} %refs_2_.5, bf16[768,256]{1,0:T(8,128)(2,1)} %get-tuple-element.75.refs_1_.refs_3_, bf16[4,192,256]{2,1,0:T(8,128)(2,1)} %copy-done.4), custom_call_target="tpu_custom_call" | custom-call | tf_op jit(solution)/shard_map/exchange/pallas_call | solution.py:609
  126.2 13.9 %all_to_all.37.recv_ref = bf16[32,16,128]{2,1,0:T(8,128)(2,1)S(1)} all-to-all(bf16[32,16,128]{2,1,0:T(8,128)(2,1)} %exchange.3), channel_id=1, replica_groups=mesh['ka'=4,'band'=8] {'ka','band'}, dimensions={0} | all-to-all | bytes 262144 | tf_op jit(solution)/shard_map/all_to_all | solution.py:31
  140.1 0.4 second_owner.1
  140.4 9.0 %all_to_all.38.msgs_ref = f32[32,2,128]{2,1,0:T(2,128)S(1)} all-to-all(f32[32,2,128]{2,1,0:T(2,128)S(1)} %get-tuple-element.91), channel_id=1, replica_groups=mesh['ka'=4,'band'=8] {'ka','band'}, dimensions={0} | all-to-all | bytes 65536 | tf_op jit(solution)/shard_map/all_to_all | solution.py:31
  149.5 0.8 finish.1
  (47 shorter events, 0.1 us)
Async XLA Ops:
  2.5 14.2 %copy-start.18 = (bf16[3,8,2176]{2,1,0:T(8,128)(2,1)S(1)}, bf16[3,8,2176]{2,1,0:T(8,128)(2,1)}, u32[]{:S(2)}) copy-start(bf16[3,8,2176]{2,1,0:T(8,128)(2,1)} %get-tuple-element.57) | copy-start | bytes 313348
  2.5 8.7 %collective-permute-start = (bf16[3,8,2176]{2,1,0:T(8,128)(2,1)}, bf16[3,8,2176]{2,1,0:T(8,128)(2,1)S(1)}, u32[]{:S(2)}, u32[]{:S(2)}) collective-permute-start(bf16[3,8,2176]{2,1,0:T(8,128)(2,1)} %get-tuple-element.53), channel_id=1, source_target_pairs={{0,8},{8,0},{16,24},{24,16},{1,9},{9,1},{17,25},{25,17},{2,10},{10... | collective-permute-start | bytes 313352 | tf_op jit(solution)/shard_map/ppermute | solution.py:455
  5.6 11.1 %collective-permute-start.1 = (bf16[3,8,2176]{2,1,0:T(8,128)(2,1)}, bf16[3,8,2176]{2,1,0:T(8,128)(2,1)S(1)}, u32[]{:S(2)}, u32[]{:S(2)}) collective-permute-start(bf16[3,8,2176]{2,1,0:T(8,128)(2,1)} %get-tuple-element.54), channel_id=1, source_target_pairs={{0,16},{8,24},{16,0},{24,8},{1,17},{9,25},{17,1},{25,9},{2,18},{10... | collective-permute-start | bytes 313352 | tf_op jit(solution)/shard_map/ppermute | solution.py:455
  8.2 8.5 %collective-permute-start.2 = (bf16[3,8,2176]{2,1,0:T(8,128)(2,1)}, bf16[3,8,2176]{2,1,0:T(8,128)(2,1)S(1)}, u32[]{:S(2)}, u32[]{:S(2)}) collective-permute-start(bf16[3,8,2176]{2,1,0:T(8,128)(2,1)} %get-tuple-element.55), channel_id=1, source_target_pairs={{0,24},{8,16},{16,8},{24,0},{1,25},{9,17},{17,9},{25,1},{2,26},{10... | collective-permute-start | bytes 313352 | tf_op jit(solution)/shard_map/ppermute | solution.py:455
  11.2 33.6 %copy-start.11 = (bf16[3,64,1024]{2,1,0:T(8,128)(2,1)}, bf16[3,64,1024]{2,1,0:T(8,128)(2,1)S(1)}, u32[]{:S(2)}) copy-start(bf16[3,64,1024]{2,1,0:T(8,128)(2,1)S(1)} %constant_dynamic-slice_fusion) | copy-start | bytes 1179652
  16.8 13.3 %copy-start.5 = (bf16[96,2176]{1,0:T(8,128)(2,1)}, bf16[96,2176]{1,0:T(8,128)(2,1)S(1)}, u32[]{:S(2)}) copy-start(bf16[96,2176]{1,0:T(8,128)(2,1)S(1)} %maximum_bitcast_fusion.refs_0_) | copy-start | bytes 1253380
  16.8 13.3 %collective-permute-start.4 = (bf16[96,2176]{1,0:T(8,128)(2,1)S(1)}, bf16[96,2176]{1,0:T(8,128)(2,1)S(1)}, u32[]{:S(2)}, u32[]{:S(2)}) collective-permute-start(bf16[96,2176]{1,0:T(8,128)(2,1)S(1)} %maximum_bitcast_fusion.refs_0_), channel_id=1, source_target_pairs={{0,2},{1,3},{2,0},{3,1},{4,6},{5,7},{6,4},{7,5},{8,10},{9,11},{10,... | collective-permute-start | bytes 1253384 | tf_op jit(solution)/shard_map/ppermute | solution.py:455
  18.4 11.8 %collective-permute-start.5 = (bf16[96,2176]{1,0:T(8,128)(2,1)S(1)}, bf16[96,2176]{1,0:T(8,128)(2,1)S(1)}, u32[]{:S(2)}, u32[]{:S(2)}) collective-permute-start(bf16[96,2176]{1,0:T(8,128)(2,1)S(1)} %maximum_bitcast_fusion.refs_0_), channel_id=1, source_target_pairs={{0,4},{1,5},{2,6},{3,7},{4,0},{5,1},{6,2},{7,3},{8,12},{9,13},{10,... | collective-permute-start | bytes 1253384 | tf_op jit(solution)/shard_map/ppermute | solution.py:455
  19.9 18.3 %collective-permute-start.12 = (bf16[192,1024]{1,0:T(8,128)(2,1)S(1)}, bf16[192,1024]{1,0:T(8,128)(2,1)}, u32[]{:S(2)}, u32[]{:S(2)}) collective-permute-start(bf16[192,1024]{1,0:T(8,128)(2,1)S(1)} %bitcast.3), channel_id=1, source_target_pairs={{0,8},{8,0},{16,24},{24,16},{1,9},{9,1},{17,25},{25,17},{2,10},{10... | collective-permute-start | bytes 1179656 | tf_op jit(solution)/shard_map/ppermute | solution.py:455
  21.6 23.3 %collective-permute-start.13 = (bf16[192,1024]{1,0:T(8,128)(2,1)S(1)}, bf16[192,1024]{1,0:T(8,128)(2,1)}, u32[]{:S(2)}, u32[]{:S(2)}) collective-permute-start(bf16[192,1024]{1,0:T(8,128)(2,1)S(1)} %bitcast.4), channel_id=1, source_target_pairs={{0,16},{8,24},{16,0},{24,8},{1,17},{9,25},{17,1},{25,9},{2,18},{10... | collective-permute-start | bytes 1179656 | tf_op jit(solution)/shard_map/ppermute | solution.py:455
  22.9 21.9 %collective-permute-start.3 = (bf16[96,2176]{1,0:T(8,128)(2,1)S(1)}, bf16[96,2176]{1,0:T(8,128)(2,1)S(1)}, u32[]{:S(2)}, u32[]{:S(2)}) collective-permute-start(bf16[96,2176]{1,0:T(8,128)(2,1)S(1)} %maximum_bitcast_fusion.refs_0_), channel_id=1, source_target_pairs={{0,1},{1,0},{2,3},{3,2},{4,5},{5,4},{6,7},{7,6},{8,9},{9,8},{10,11... | collective-permute-start | bytes 1253384 | tf_op jit(solution)/shard_map/ppermute | solution.py:455
  22.9 34.9 %all-to-all-start = ((bf16[4,192,256]{2,1,0:T(8,128)(2,1)}), bf16[4,192,256]{2,1,0:T(8,128)(2,1)S(1)}, u32[]{:S(2)}, u32[]{:S(2)}) async-start(bf16[4,192,256]{2,1,0:T(8,128)(2,1)} %cut.1), calls=%async_computation | async-start | bytes 786432 | tf_op jit(solution)/shard_map/all_to_all | solution.py:525
  30.1 20.4 %copy-start.6 = (bf16[96,2176]{1,0:T(8,128)(2,1)}, bf16[96,2176]{1,0:T(8,128)(2,1)S(1)}, u32[]{:S(2)}) copy-start(bf16[96,2176]{1,0:T(8,128)(2,1)S(1)} %collective-permute-done.4.refs_2_) | copy-start | bytes 1253380
  30.1 20.4 %copy-start.7 = (bf16[96,2176]{1,0:T(8,128)(2,1)}, bf16[96,2176]{1,0:T(8,128)(2,1)S(1)}, u32[]{:S(2)}) copy-start(bf16[96,2176]{1,0:T(8,128)(2,1)S(1)} %collective-permute-done.5.refs_4_) | copy-start | bytes 1253380
  30.2 18.6 %collective-permute-start.8 = (bf16[48,2176]{1,0:T(8,128)(2,1)S(1)}, bf16[48,2176]{1,0:T(8,128)(2,1)S(1)}, u32[]{:S(2)}, u32[]{:S(2)}) collective-permute-start(bf16[48,2176]{1,0:T(8,128)(2,1)S(1)} %slice.6), channel_id=1, source_target_pairs={{0,4},{1,5},{2,6},{3,7},{4,0},{5,1},{6,2},{7,3},{8,12},{9,13},{10,... | collective-permute-start | bytes 626696 | tf_op jit(solution)/shard_map/ppermute | solution.py:455
  30.8 18.2 %collective-permute-start.9 = (bf16[48,2176]{1,0:T(8,128)(2,1)S(1)}, bf16[48,2176]{1,0:T(8,128)(2,1)S(1)}, u32[]{:S(2)}, u32[]{:S(2)}) collective-permute-start(bf16[48,2176]{1,0:T(8,128)(2,1)S(1)} %slice.7), channel_id=1, source_target_pairs={{0,2},{1,3},{2,0},{3,1},{4,6},{5,7},{6,4},{7,5},{8,10},{9,11},{10,... | collective-permute-start | bytes 626696 | tf_op jit(solution)/shard_map/ppermute | solution.py:455
  38.2 12.3 %collective-permute-start.6 = (bf16[96,2176]{1,0:T(8,128)(2,1)S(1)}, bf16[96,2176]{1,0:T(8,128)(2,1)S(1)}, u32[]{:S(2)}, u32[]{:S(2)}) collective-permute-start(bf16[96,2176]{1,0:T(8,128)(2,1)S(1)} %collective-permute-done.4.refs_2_), channel_id=1, source_target_pairs={{0,1},{1,0},{2,3},{3,2},{4,5},{5,4},{6,7},{7,6},{8,9},{9,8},{10,11... | collective-permute-start | bytes 1253384 | tf_op jit(solution)/shard_map/ppermute | solution.py:455
  44.8 5.7 %collective-permute-start.7 = (bf16[96,2176]{1,0:T(8,128)(2,1)S(1)}, bf16[96,2176]{1,0:T(8,128)(2,1)S(1)}, u32[]{:S(2)}, u32[]{:S(2)}) collective-permute-start(bf16[96,2176]{1,0:T(8,128)(2,1)S(1)} %collective-permute-done.5.refs_4_), channel_id=1, source_target_pairs={{0,1},{1,0},{2,3},{3,2},{4,5},{5,4},{6,7},{7,6},{8,9},{9,8},{10,11... | collective-permute-start | bytes 1253384 | tf_op jit(solution)/shard_map/ppermute | solution.py:455
  44.8 5.7 %copy-start.8 = (bf16[96,2176]{1,0:T(8,128)(2,1)}, bf16[96,2176]{1,0:T(8,128)(2,1)S(1)}, u32[]{:S(2)}) copy-start(bf16[96,2176]{1,0:T(8,128)(2,1)S(1)} %collective-permute-done.3.refs_1_) | copy-start | bytes 1253380
  44.8 18.7 %collective-permute-start.14 = (bf16[192,1024]{1,0:T(8,128)(2,1)S(1)}, bf16[192,1024]{1,0:T(8,128)(2,1)}, u32[]{:S(2)}, u32[]{:S(2)}) collective-permute-start(bf16[192,1024]{1,0:T(8,128)(2,1)S(1)} %bitcast.5), channel_id=1, source_target_pairs={{0,24},{8,16},{16,8},{24,0},{1,25},{9,17},{17,9},{25,1},{2,26},{10... | collective-permute-start | bytes 1179656 | tf_op jit(solution)/shard_map/ppermute | solution.py:455
  48.8 1.8 %copy-start.12 = (bf16[48,2176]{1,0:T(8,128)(2,1)}, bf16[48,2176]{1,0:T(8,128)(2,1)S(1)}, u32[]{:S(2)}) copy-start(bf16[48,2176]{1,0:T(8,128)(2,1)S(1)} %collective-permute-done.8.refs_6_) | copy-start | bytes 626692
  48.8 1.5 collective-permute-start.10
  49.0 1.6 %copy-start.13 = (bf16[48,2176]{1,0:T(8,128)(2,1)}, bf16[48,2176]{1,0:T(8,128)(2,1)S(1)}, u32[]{:S(2)}) copy-start(bf16[48,2176]{1,0:T(8,128)(2,1)S(1)} %collective-permute-done.9.refs_7_) | copy-start | bytes 626692
  49.0 1.5 %collective-permute-start.11 = (bf16[48,2176]{1,0:T(8,128)(2,1)S(1)}, bf16[48,2176]{1,0:T(8,128)(2,1)S(1)}, u32[]{:S(2)}, u32[]{:S(2)}) collective-permute-start(bf16[48,2176]{1,0:T(8,128)(2,1)S(1)} %collective-permute-done.9.refs_7_), channel_id=1, source_target_pairs={{0,1},{1,0},{2,3},{3,2},{4,5},{5,4},{6,7},{7,6},{8,9},{9,8},{10,11... | collective-permute-start | bytes 626696 | tf_op jit(solution)/shard_map/ppermute | solution.py:455
  50.2 0.7 copy-start.14
  50.5 0.7 copy-start.15
  50.5 0.9 copy-start.9
  51.4 0.8 copy-start.10
  57.9 0.7 copy-start.4
  60.9 14.7 %all-to-all-start.1 = ((f32[32,2,128]{2,1,0:T(2,128)}), f32[32,2,128]{2,1,0:T(2,128)S(1)}, u32[]{:S(2)}, u32[]{:S(2)}) async-start(f32[32,2,128]{2,1,0:T(2,128)} %get-tuple-element.77), calls=%async_computation.1 | async-start | bytes 65536 | tf_op jit(solution)/shard_map/all_to_all | solution.py:31
  75.6 18.3 %copy-start.1 = (bf16[32,16,128]{2,1,0:T(8,128)(2,1)S(1)}, bf16[32,16,128]{2,1,0:T(8,128)(2,1)}, u32[]{:S(2)}) copy-start(bf16[32,16,128]{2,1,0:T(8,128)(2,1)} %get-tuple-element.74.refs_0_.msgs_ref) | copy-start | bytes 393220
  75.6 18.3 %copy-start.2 = (f32[16,128]{1,0:T(8,128)S(1)}, f32[16,128]{1,0:T(8,128)}, u32[]{:S(2)}) copy-start(f32[16,128]{1,0:T(8,128)} %get-tuple-element.84.gap_ref) | copy-start | bytes 24580
  75.6 18.3 %copy-start.3 = (f32[16,128]{1,0:T(8,128)S(1)}, f32[16,128]{1,0:T(8,128)}, u32[]{:S(2)}) copy-start(f32[16,128]{1,0:T(8,128)} %get-tuple-element.85.own_ref) | copy-start | bytes 24580
  75.6 0.6 copy-start.17
  107.1 14.8 %all-to-all-start.4 = ((f32[32,2,128]{2,1,0:T(2,128)}), f32[32,2,128]{2,1,0:T(2,128)S(1)}, u32[]{:S(2)}, u32[]{:S(2)}) async-start(f32[32,2,128]{2,1,0:T(2,128)} %get-tuple-element.87), calls=%async_computation.4 | async-start | bytes 65536 | tf_op jit(solution)/shard_map/all_to_all | solution.py:31
  121.8 18.2 %copy-start = (bf16[32,16,128]{2,1,0:T(8,128)(2,1)S(1)}, bf16[32,16,128]{2,1,0:T(8,128)(2,1)}, u32[]{:S(2)}) copy-start(bf16[32,16,128]{2,1,0:T(8,128)(2,1)} %all_to_all.36.refs_0_.msgs_ref) | copy-start | bytes 393220
  121.8 0.6 copy-start.16

commit v20 on v19

--- a/solution.py
+++ b/solution.py
@@ -455,21 +455,22 @@
     return lax.ppermute(block, axis, [(i, i ^ d) for i in range(lax.axis_size(axis))])
 
 
-def plane_pieces(own_piece, others):
+def plane_pieces(own_piece, others, after):
     def move(block, d):
         return swap(block, "band", d)
 
     rows = own_piece.shape[0]
     half = rows // 2
     by_x, by_y, core = move(own_piece, 2), move(own_piece, 4), move(own_piece, 1)
-    by_x, by_y, others = lax.optimization_barrier((by_x, by_y, others))
+    by_x, by_y, core, others = lax.optimization_barrier((by_x, by_y, core, others))
     diag = [move(by_x[:half], 4), move(by_y[half:], 2)]
     near_x, near_y = move(by_x, 1), move(by_y, 1)
+    diag, after = lax.optimization_barrier((diag, after))
     far = [move(part, 1) for part in diag]
     arrays = [own_piece, core, by_x, near_x, by_y, near_y] + diag + far
     parts = tuple(((i, 0, rows),) for i in range(6))
     parts += (((6, 0, half), (7, 0, half)), ((8, 0, half), (9, 0, half)))
-    return arrays, parts, others
+    return arrays, parts, others, after
 
 
 def kernel_path(start_vec, val_energy, cond_energy, val_orb, cond_orb, coulomb, screened):
@@ -521,7 +522,7 @@
     cond_local = cond_local.reshape(k_dev * n_cond, mu_blk)
     got, cuts, cond_local = lax.optimization_barrier((got, cuts, cond_local))
     val_cut = jnp.concatenate(got, axis=0).reshape(piece_rows, wide)
-    cond_pts = [cond_local] + [swap(cond_local, "ka", j) for j in range(1, n_ka)]
+    cond_pts = [cond_local] + [swap(cond_local, "ka", j) for j in range(1, n_ka - 1)]
     cond_own = lax.all_to_all(cuts, "ka", split_axis=0, concat_axis=0, tiled=True)
 
     chunk, tile = 1024, nu_blk
@@ -536,7 +537,8 @@
         + [dma(4)] * 2,
         moved=8 * MIB,
     )(screened)
-    pieces, parts, scr_turned = plane_pieces(val_cut, scr_turned)
+    pieces, parts, scr_turned, cond_last = plane_pieces(val_cut, scr_turned, cond_local)
+    cond_pts.append(swap(cond_last, "ka", n_ka - 1))
     pieces, cond_pts[1:-1] = lax.optimization_barrier((pieces, cond_pts[1:-1]))
     val_rows, val_turned, val_own, msgs = call(
         functools.partial(order_kernel, parts, n_ka),

time: 151 us -> 168 us (1.11)
  waiting for transfers between devices: 20.2 us -> 36.5 us
    ppermute x15, waiting for transfers between devices: 20.2 us -> 36.5 us  [swap(): lax.ppermute(block, axis, [(i, i ^ d) for i in range(lax.axis_size(axis))])]
  transfers between devices with their start and end apart: 18 -> 18, of which waited for: 5 -> 7; matrix products, arithmetic and copies ran while one was open for 1% -> 1% of each run, Pallas kernels for 25% -> 22%
where the time goes in v20:
time: 168 us
  Pallas kernels  50.4 us (30%)
  blocking collectives  47.4 us (28%)
  waiting for transfers between devices  36.5 us (22%)
  starting transfers between devices  26.5 us (16%)
  local copies, waits for them, and re-layouts  5.4 us (3%)
    all_to_all x4, blocking collectives, exchange_all(): return lax.all_to_all(parts, AXES, split_axis=0, concat_axis=0, tiled=True)  47.4 us
    ppermute x15, waiting for transfers between devices, swap(): lax.ppermute(block, axis, [(i, i ^ d) for i in range(lax.axis_size(axis))])  36.5 us
    pallas_call x2, Pallas kernels, kernel_path(): call(functools.partial(direct_kernel, n_ka, tile, scale), 'direct', shape...  23.9 us
    ppermute x15, starting transfers between devices, swap(): lax.ppermute(block, axis, [(i, i ^ d) for i in range(lax.axis_size(axis))])  17.2 us
    pallas_call x2, Pallas kernels, kernel_path(): call(functools.partial(exchange_kernel, cfg, chunk, scale), 'exchange', m...  7.47 us
    all_to_all x2, starting transfers between devices, exchange_all(): return lax.all_to_all(parts, AXES, split_axis=0, concat_axis=0, tiled=True)  5.92 us
    pallas_call x1, Pallas kernels, kernel_path(): call(functools.partial(order_kernel, parts, n_ka), 'order', (shape_of((ro...  5.69 us
    pallas_call x2, Pallas kernels, kernel_path(): call(functools.partial(density_kernel, cfg), 'density', (shape_of((quads,...  4.49 us
  transfers between devices with their start and end apart: 18, of which 7 were waited for; matrix products, arithmetic and copies ran while one was open for 1% of the time, Pallas kernels for 22%

profile of v20, /device:TPU:0, one launch (start us, length us, event | category | flops | bytes accessed | tf_op | source)
XLA Modules:
  0.0 167.5 jit_solution(16381064921869461831)
XLA Ops:
  0.6 1.9 %pack.1 = (f32[16,128]{1,0:T(8,128)}, f32[16,128]{1,0:T(8,128)}, bf16[3,8,2176]{2,1,0:T(8,128)(2,1)}, bf16[3,8,2176]{2,1,0:T(8,128)(2,1)}, bf16[3,8,2176]{2,1,0:T(8,128)(2,1)}, /*index=5*/bf16[3,8,2176]{2,1,0:T(8,128)(2,1)}) custom-call(f32[3,512]{1,0:T(4,128)} %refs_0_.1, f32[3,64]{1,0:T(4,128)} %refs_1_.1, f32[3,8]{1,0:T(4,128)} %refs_2_.3, ...), custom_call_target="tpu_custom_call" | custom-call | tf_op jit(solution)/shard_map/pack/pallas_call | solution.py:496
  2.5 3.1 %collective-permute-start = (bf16[3,8,2176]{2,1,0:T(8,128)(2,1)}, bf16[3,8,2176]{2,1,0:T(8,128)(2,1)S(1)}, u32[]{:S(2)}, u32[]{:S(2)}) collective-permute-start(bf16[3,8,2176]{2,1,0:T(8,128)(2,1)} %get-tuple-element.57), channel_id=1, source_target_pairs={{0,8},{8,0},{16,24},{24,16},{1,9},{9,1},{17,25},{25,17},{2,10},{10... | collective-permute-start | bytes 313352 | tf_op jit(solution)/shard_map/ppermute | solution.py:455
  5.6 2.6 %collective-permute-start.1 = (bf16[3,8,2176]{2,1,0:T(8,128)(2,1)}, bf16[3,8,2176]{2,1,0:T(8,128)(2,1)S(1)}, u32[]{:S(2)}, u32[]{:S(2)}) collective-permute-start(bf16[3,8,2176]{2,1,0:T(8,128)(2,1)} %get-tuple-element.58), channel_id=1, source_target_pairs={{0,16},{8,24},{16,0},{24,8},{1,17},{9,25},{17,1},{25,9},{2,18},{10... | collective-permute-start | bytes 313352 | tf_op jit(solution)/shard_map/ppermute | solution.py:455
  8.2 1.8 %cut.1 = bf16[4,192,256]{2,1,0:T(8,128)(2,1)} custom-call(bf16[3,64,8192]{2,1,0:T(8,128)(2,1)} %cond_ref.1), custom_call_target="tpu_custom_call" | custom-call | tf_op jit(solution)/shard_map/cut/pallas_call | solution.py:513
  10.0 1.2 constant_dynamic-slice_fusion
  11.2 0.0 collective-permute-done
  11.3 5.5 %collective-permute-done.1 = bf16[3,8,2176]{2,1,0:T(8,128)(2,1)S(1)} collective-permute-done((bf16[3,8,2176]{2,1,0:T(8,128)(2,1)}, bf16[3,8,2176]{2,1,0:T(8,128)(2,1)S(1)}, u32[]{:S(2)}, u32[]{:S(2)}) %collective-permute-start.1) | collective-permute-done | bytes 104480 | tf_op jit(solution)/shard_map/ppermute | solution.py:455
  16.7 0.1 maximum_bitcast_fusion.refs_0_
  16.8 1.6 collective-permute-start.3
  18.4 1.5 collective-permute-start.4
  19.9 3.7 %turn.1.refs_1_ = bf16[2048,1024]{1,0:T(8,128)(2,1)} custom-call(bf16[1024,2048]{1,0:T(8,128)(2,1)} %scr_ref.1), custom_call_target="tpu_custom_call" | custom-call | bytes 8388608 | tf_op jit(solution)/shard_map/turn/pallas_call | solution.py:530
  23.6 2.6 %collective-permute-done.3.refs_2_ = bf16[96,2176]{1,0:T(8,128)(2,1)S(1)} collective-permute-done((bf16[96,2176]{1,0:T(8,128)(2,1)S(1)}, bf16[96,2176]{1,0:T(8,128)(2,1)S(1)}, u32[]{:S(2)}, u32[]{:S(2)}) %collective-permute-start.3) | collective-permute-done | bytes 417824 | tf_op jit(solution)/shard_map/ppermute | solution.py:455
  26.2 1.7 %collective-permute-done.4.refs_4_ = bf16[96,2176]{1,0:T(8,128)(2,1)S(1)} collective-permute-done((bf16[96,2176]{1,0:T(8,128)(2,1)S(1)}, bf16[96,2176]{1,0:T(8,128)(2,1)S(1)}, u32[]{:S(2)}, u32[]{:S(2)}) %collective-permute-start.4) | collective-permute-done | bytes 417824 | tf_op jit(solution)/shard_map/ppermute | solution.py:455
  28.0 1.7 %collective-permute-start.8 = (bf16[48,2176]{1,0:T(8,128)(2,1)S(1)}, bf16[48,2176]{1,0:T(8,128)(2,1)S(1)}, u32[]{:S(2)}, u32[]{:S(2)}) collective-permute-start(bf16[48,2176]{1,0:T(8,128)(2,1)S(1)} %slice.6), channel_id=1, source_target_pairs={{0,4},{1,5},{2,6},{3,7},{4,0},{5,1},{6,2},{7,3},{8,12},{9,13},{10,... | collective-permute-start | bytes 626696 | tf_op jit(solution)/shard_map/ppermute | solution.py:455
  29.7 1.8 %collective-permute-start.12 = (bf16[192,1024]{1,0:T(8,128)(2,1)S(1)}, bf16[192,1024]{1,0:T(8,128)(2,1)}, u32[]{:S(2)}, u32[]{:S(2)}) collective-permute-start(bf16[192,1024]{1,0:T(8,128)(2,1)S(1)} %bitcast.3), channel_id=1, source_target_pairs={{0,8},{8,0},{16,24},{24,16},{1,9},{9,1},{17,25},{25,17},{2,10},{10... | collective-permute-start | bytes 1179656 | tf_op jit(solution)/shard_map/ppermute | solution.py:455
  31.5 1.2 collective-permute-start.13
  32.7 0.6 collective-permute-start.9
  33.3 3.5 %all-to-all-start = ((bf16[4,192,256]{2,1,0:T(8,128)(2,1)}), bf16[4,192,256]{2,1,0:T(8,128)(2,1)S(1)}, u32[]{:S(2)}, u32[]{:S(2)}) async-start(bf16[4,192,256]{2,1,0:T(8,128)(2,1)} %cut.1), calls=%async_computation | async-start | bytes 786432 | tf_op jit(solution)/shard_map/all_to_all | solution.py:526
  36.8 0.1 collective-permute-start.6
  36.9 0.5 collective-permute-start.7
  37.3 1.3 collective-permute-done.9.refs_7_
  38.6 2.5 %collective-permute-start.14 = (bf16[192,1024]{1,0:T(8,128)(2,1)S(1)}, bf16[192,1024]{1,0:T(8,128)(2,1)}, u32[]{:S(2)}, u32[]{:S(2)}) collective-permute-start(bf16[192,1024]{1,0:T(8,128)(2,1)S(1)} %bitcast.5), channel_id=1, source_target_pairs={{0,24},{8,16},{16,8},{24,0},{1,25},{9,17},{17,9},{25,1},{2,26},{10... | collective-permute-start | bytes 1179656 | tf_op jit(solution)/shard_map/ppermute | solution.py:455
  41.1 6.7 %collective-permute-done.12.refs_5_ = bf16[192,1024]{1,0:T(8,128)(2,1)} collective-permute-done((bf16[192,1024]{1,0:T(8,128)(2,1)S(1)}, bf16[192,1024]{1,0:T(8,128)(2,1)}, u32[]{:S(2)}, u32[]{:S(2)}) %collective-permute-start.12) | collective-permute-done | bytes 393248 | tf_op jit(solution)/shard_map/ppermute | solution.py:455
  47.8 17.3 %collective-permute-done.13.refs_6_ = bf16[192,1024]{1,0:T(8,128)(2,1)} collective-permute-done((bf16[192,1024]{1,0:T(8,128)(2,1)S(1)}, bf16[192,1024]{1,0:T(8,128)(2,1)}, u32[]{:S(2)}, u32[]{:S(2)}) %collective-permute-start.13) | collective-permute-done | bytes 393248 | tf_op jit(solution)/shard_map/ppermute | solution.py:455
  65.2 1.4 collective-permute-done.11.refs_9_
  66.6 0.7 copy-done.15
  67.3 0.7 copy-done.9
  68.1 0.8 copy-done.10
  68.8 5.7 %order.1 = (bf16[768,2048]{1,0:T(8,128)(2,1)}, bf16[2048,768]{1,0:T(8,128)(2,1)}, bf16[768,256]{1,0:T(8,128)(2,1)}, bf16[32,16,128]{2,1,0:T(8,128)(2,1)}) custom-call(bf16[96,2176]{1,0:T(8,128)(2,1)} %copy-done.5, bf16[96,2176]{1,0:T(8,128)(2,1)} %copy-done.8, bf16[96,2176]{1,0:T(8,128)(2,1)} %copy-done.6, bf16[96,2176]{1,0:T(8,128)(2,1)} %copy-done.9, ...), custom_call_target="tpu_custom_call" | custom-call | bytes 9437184 | tf_op jit(solution)/shard_map/order/pallas_call | solution.py:543
  74.6 0.7 copy-done.4
  75.3 2.2 %density.2 = (bf16[3,256,256]{2,1,0:T(8,128)(2,1)}, f32[32,2,128]{2,1,0:T(2,128)}) custom-call(bf16[32,16,128]{2,1,0:T(8,128)(2,1)} %get-tuple-element.81.refs_0_.msgs_ref, bf16[768,256]{1,0:T(8,128)(2,1)} %get-tuple-element.82.refs_1_.refs_3_, bf16[4,192,256]{2,1,0:T(8,128)(2,1)} %copy-done.4), custom_call_target="tpu_custom_call" | custom-call | tf_op jit(solution)/shard_map/density/pallas_call | solution.py:570
  77.5 3.1 %all-to-all-start.1 = ((f32[32,2,128]{2,1,0:T(2,128)}), f32[32,2,128]{2,1,0:T(2,128)S(1)}, u32[]{:S(2)}, u32[]{:S(2)}) async-start(f32[32,2,128]{2,1,0:T(2,128)} %get-tuple-element.84), calls=%async_computation.1 | async-start | bytes 65536 | tf_op jit(solution)/shard_map/all_to_all | solution.py:31
  80.7 12.0 %direct.2.refs_1_ = f32[6,128,128]{2,1,0:T(8,128)} custom-call(bf16[2048,768]{1,0:T(8,128)(2,1)} %get-tuple-element.85.refs_0_, bf16[2048,1024]{1,0:T(8,128)(2,1)} %turn.1.refs_1_, bf16[768,2048]{1,0:T(8,128)(2,1)} %get-tuple-element.87.refs_2_, bf16[3,256,256]{2,1,0:T(8,128)(2,1)} %get-tuple-element.88.refs_3_, bf16[192,1024]{1,0:T(8,128)(2,1)} %bitcast.6, ...), custom_call_target="tpu_custom_call" | custom-call | flops 6442450944 | bytes 12582912 | tf_op jit(solution)/shard_map/direct/pallas_call | solution.py:588
  92.7 0.0 copy-start.3
  92.7 0.6 copy-done.17
  93.3 3.7 %exchange.2 = bf16[32,16,128]{2,1,0:T(8,128)(2,1)} custom-call(f32[32,2,128]{2,1,0:T(2,128)} %copy-done.17, f32[6,128,128]{2,1,0:T(8,128)} %direct.2.refs_1_, bf16[256,8192]{1,0:T(8,128)(2,1)} %refs_2_.5, bf16[768,256]{1,0:T(8,128)(2,1)} %get-tuple-element.82.refs_1_.refs_3_, bf16[4,192,256]{2,1,0:T(8,128)(2,1)} %copy-done.4), custom_call_target="tpu_custom_call" | custom-call | tf_op jit(solution)/shard_map/exchange/pallas_call | solution.py:611
  97.0 13.9 %all_to_all.35.recv_ref = bf16[32,16,128]{2,1,0:T(8,128)(2,1)S(1)} all-to-all(bf16[32,16,128]{2,1,0:T(8,128)(2,1)} %exchange.2), channel_id=1, replica_groups=mesh['ka'=4,'band'=8] {'ka','band'}, dimensions={0} | all-to-all | bytes 262144 | tf_op jit(solution)/shard_map/all_to_all | solution.py:31
  110.9 0.3 first_owner.1
  111.3 10.6 %all_to_all.36.refs_0_.msgs_ref = bf16[32,16,128]{2,1,0:T(8,128)(2,1)} all-to-all(bf16[32,16,128]{2,1,0:T(8,128)(2,1)S(1)} %get-tuple-element.94), channel_id=1, replica_groups=mesh['ka'=4,'band'=8] {'ka','band'}, dimensions={0} | all-to-all | bytes 262144 | tf_op jit(solution)/shard_map/all_to_all | solution.py:31
  121.9 2.2 %density.3 = (bf16[3,256,256]{2,1,0:T(8,128)(2,1)}, f32[32,2,128]{2,1,0:T(2,128)}) custom-call(bf16[32,16,128]{2,1,0:T(8,128)(2,1)} %all_to_all.36.refs_0_.msgs_ref, bf16[768,256]{1,0:T(8,128)(2,1)} %get-tuple-element.82.refs_1_.refs_3_, bf16[4,192,256]{2,1,0:T(8,128)(2,1)} %copy-done.4), custom_call_target="tpu_custom_call" | custom-call | tf_op jit(solution)/shard_map/density/pallas_call | solution.py:570
  124.1 2.8 %all-to-all-start.4 = ((f32[32,2,128]{2,1,0:T(2,128)}), f32[32,2,128]{2,1,0:T(2,128)S(1)}, u32[]{:S(2)}, u32[]{:S(2)}) async-start(f32[32,2,128]{2,1,0:T(2,128)} %get-tuple-element.95), calls=%async_computation.4 | async-start | bytes 65536 | tf_op jit(solution)/shard_map/all_to_all | solution.py:31
  126.9 12.0 %direct.3.refs_1_ = f32[6,128,128]{2,1,0:T(8,128)} custom-call(bf16[2048,768]{1,0:T(8,128)(2,1)} %get-tuple-element.85.refs_0_, bf16[2048,1024]{1,0:T(8,128)(2,1)} %turn.1.refs_1_, bf16[768,2048]{1,0:T(8,128)(2,1)} %get-tuple-element.87.refs_2_, bf16[3,256,256]{2,1,0:T(8,128)(2,1)} %get-tuple-element.96.refs_3_, bf16[192,1024]{1,0:T(8,128)(2,1)} %bitcast.7, ...), custom_call_target="tpu_custom_call" | custom-call | flops 6442450944 | bytes 12582912 | tf_op jit(solution)/shard_map/direct/pallas_call | solution.py:588
  138.9 0.6 copy-done.16
  139.5 3.7 %exchange.3 = bf16[32,16,128]{2,1,0:T(8,128)(2,1)} custom-call(f32[32,2,128]{2,1,0:T(2,128)} %copy-done.16, f32[6,128,128]{2,1,0:T(8,128)} %direct.3.refs_1_, bf16[256,8192]{1,0:T(8,128)(2,1)} %refs_2_.5, bf16[768,256]{1,0:T(8,128)(2,1)} %get-tuple-element.82.refs_1_.refs_3_, bf16[4,192,256]{2,1,0:T(8,128)(2,1)} %copy-done.4), custom_call_target="tpu_custom_call" | custom-call | tf_op jit(solution)/shard_map/exchange/pallas_call | solution.py:611
  143.3 13.9 %all_to_all.37.recv_ref = bf16[32,16,128]{2,1,0:T(8,128)(2,1)S(1)} all-to-all(bf16[32,16,128]{2,1,0:T(8,128)(2,1)} %exchange.3), channel_id=1, replica_groups=mesh['ka'=4,'band'=8] {'ka','band'}, dimensions={0} | all-to-all | bytes 262144 | tf_op jit(solution)/shard_map/all_to_all | solution.py:31
  157.2 0.4 second_owner.1
  157.5 9.0 %all_to_all.38.msgs_ref = f32[32,2,128]{2,1,0:T(2,128)S(1)} all-to-all(f32[32,2,128]{2,1,0:T(2,128)S(1)} %get-tuple-element.99), channel_id=1, replica_groups=mesh['ka'=4,'band'=8] {'ka','band'}, dimensions={0} | all-to-all | bytes 65536 | tf_op jit(solution)/shard_map/all_to_all | solution.py:31
  166.6 0.8 finish.1
  (47 shorter events, 0.1 us)
Async XLA Ops:
  2.5 14.2 %copy-start.18 = (bf16[3,8,2176]{2,1,0:T(8,128)(2,1)S(1)}, bf16[3,8,2176]{2,1,0:T(8,128)(2,1)}, u32[]{:S(2)}) copy-start(bf16[3,8,2176]{2,1,0:T(8,128)(2,1)} %get-tuple-element.61) | copy-start | bytes 313348
  2.5 8.7 %collective-permute-start = (bf16[3,8,2176]{2,1,0:T(8,128)(2,1)}, bf16[3,8,2176]{2,1,0:T(8,128)(2,1)S(1)}, u32[]{:S(2)}, u32[]{:S(2)}) collective-permute-start(bf16[3,8,2176]{2,1,0:T(8,128)(2,1)} %get-tuple-element.57), channel_id=1, source_target_pairs={{0,8},{8,0},{16,24},{24,16},{1,9},{9,1},{17,25},{25,17},{2,10},{10... | collective-permute-start | bytes 313352 | tf_op jit(solution)/shard_map/ppermute | solution.py:455
  5.6 11.1 %collective-permute-start.1 = (bf16[3,8,2176]{2,1,0:T(8,128)(2,1)}, bf16[3,8,2176]{2,1,0:T(8,128)(2,1)S(1)}, u32[]{:S(2)}, u32[]{:S(2)}) collective-permute-start(bf16[3,8,2176]{2,1,0:T(8,128)(2,1)} %get-tuple-element.58), channel_id=1, source_target_pairs={{0,16},{8,24},{16,0},{24,8},{1,17},{9,25},{17,1},{25,9},{2,18},{10... | collective-permute-start | bytes 313352 | tf_op jit(solution)/shard_map/ppermute | solution.py:455
  8.2 8.5 %collective-permute-start.2 = (bf16[3,8,2176]{2,1,0:T(8,128)(2,1)}, bf16[3,8,2176]{2,1,0:T(8,128)(2,1)S(1)}, u32[]{:S(2)}, u32[]{:S(2)}) collective-permute-start(bf16[3,8,2176]{2,1,0:T(8,128)(2,1)} %get-tuple-element.59), channel_id=1, source_target_pairs={{0,24},{8,16},{16,8},{24,0},{1,25},{9,17},{17,9},{25,1},{2,26},{10... | collective-permute-start | bytes 313352 | tf_op jit(solution)/shard_map/ppermute | solution.py:455
  11.2 27.4 %copy-start.11 = (bf16[3,64,1024]{2,1,0:T(8,128)(2,1)}, bf16[3,64,1024]{2,1,0:T(8,128)(2,1)S(1)}, u32[]{:S(2)}) copy-start(bf16[3,64,1024]{2,1,0:T(8,128)(2,1)S(1)} %constant_dynamic-slice_fusion) | copy-start | bytes 1179652
  16.8 6.8 %copy-start.5 = (bf16[96,2176]{1,0:T(8,128)(2,1)}, bf16[96,2176]{1,0:T(8,128)(2,1)S(1)}, u32[]{:S(2)}) copy-start(bf16[96,2176]{1,0:T(8,128)(2,1)S(1)} %maximum_bitcast_fusion.refs_0_) | copy-start | bytes 1253380
  16.8 9.4 %collective-permute-start.3 = (bf16[96,2176]{1,0:T(8,128)(2,1)S(1)}, bf16[96,2176]{1,0:T(8,128)(2,1)S(1)}, u32[]{:S(2)}, u32[]{:S(2)}) collective-permute-start(bf16[96,2176]{1,0:T(8,128)(2,1)S(1)} %maximum_bitcast_fusion.refs_0_), channel_id=1, source_target_pairs={{0,2},{1,3},{2,0},{3,1},{4,6},{5,7},{6,4},{7,5},{8,10},{9,11},{10,... | collective-permute-start | bytes 1253384 | tf_op jit(solution)/shard_map/ppermute | solution.py:455
  18.4 9.6 %collective-permute-start.4 = (bf16[96,2176]{1,0:T(8,128)(2,1)S(1)}, bf16[96,2176]{1,0:T(8,128)(2,1)S(1)}, u32[]{:S(2)}, u32[]{:S(2)}) collective-permute-start(bf16[96,2176]{1,0:T(8,128)(2,1)S(1)} %maximum_bitcast_fusion.refs_0_), channel_id=1, source_target_pairs={{0,4},{1,5},{2,6},{3,7},{4,0},{5,1},{6,2},{7,3},{8,12},{9,13},{10,... | collective-permute-start | bytes 1253384 | tf_op jit(solution)/shard_map/ppermute | solution.py:455
  19.9 8.0 %collective-permute-start.5 = (bf16[96,2176]{1,0:T(8,128)(2,1)S(1)}, bf16[96,2176]{1,0:T(8,128)(2,1)S(1)}, u32[]{:S(2)}, u32[]{:S(2)}) collective-permute-start(bf16[96,2176]{1,0:T(8,128)(2,1)S(1)} %maximum_bitcast_fusion.refs_0_), channel_id=1, source_target_pairs={{0,1},{1,0},{2,3},{3,2},{4,5},{5,4},{6,7},{7,6},{8,9},{9,8},{10,11... | collective-permute-start | bytes 1253384 | tf_op jit(solution)/shard_map/ppermute | solution.py:455
  26.2 41.1 %copy-start.6 = (bf16[96,2176]{1,0:T(8,128)(2,1)}, bf16[96,2176]{1,0:T(8,128)(2,1)S(1)}, u32[]{:S(2)}) copy-start(bf16[96,2176]{1,0:T(8,128)(2,1)S(1)} %collective-permute-done.3.refs_2_) | copy-start | bytes 1253380
  27.9 39.4 %copy-start.7 = (bf16[96,2176]{1,0:T(8,128)(2,1)}, bf16[96,2176]{1,0:T(8,128)(2,1)S(1)}, u32[]{:S(2)}) copy-start(bf16[96,2176]{1,0:T(8,128)(2,1)S(1)} %collective-permute-done.4.refs_4_) | copy-start | bytes 1253380
  27.9 39.4 %copy-start.8 = (bf16[96,2176]{1,0:T(8,128)(2,1)}, bf16[96,2176]{1,0:T(8,128)(2,1)S(1)}, u32[]{:S(2)}) copy-start(bf16[96,2176]{1,0:T(8,128)(2,1)S(1)} %collective-permute-done.5.refs_1_) | copy-start | bytes 1253380
  28.0 8.9 %collective-permute-start.8 = (bf16[48,2176]{1,0:T(8,128)(2,1)S(1)}, bf16[48,2176]{1,0:T(8,128)(2,1)S(1)}, u32[]{:S(2)}, u32[]{:S(2)}) collective-permute-start(bf16[48,2176]{1,0:T(8,128)(2,1)S(1)} %slice.6), channel_id=1, source_target_pairs={{0,4},{1,5},{2,6},{3,7},{4,0},{5,1},{6,2},{7,3},{8,12},{9,13},{10,... | collective-permute-start | bytes 626696 | tf_op jit(solution)/shard_map/ppermute | solution.py:455
  29.7 18.1 %collective-permute-start.12 = (bf16[192,1024]{1,0:T(8,128)(2,1)S(1)}, bf16[192,1024]{1,0:T(8,128)(2,1)}, u32[]{:S(2)}, u32[]{:S(2)}) collective-permute-start(bf16[192,1024]{1,0:T(8,128)(2,1)S(1)} %bitcast.3), channel_id=1, source_target_pairs={{0,8},{8,0},{16,24},{24,16},{1,9},{9,1},{17,25},{25,17},{2,10},{10... | collective-permute-start | bytes 1179656 | tf_op jit(solution)/shard_map/ppermute | solution.py:455
  31.5 33.6 %collective-permute-start.13 = (bf16[192,1024]{1,0:T(8,128)(2,1)S(1)}, bf16[192,1024]{1,0:T(8,128)(2,1)}, u32[]{:S(2)}, u32[]{:S(2)}) collective-permute-start(bf16[192,1024]{1,0:T(8,128)(2,1)S(1)} %bitcast.4), channel_id=1, source_target_pairs={{0,16},{8,24},{16,0},{24,8},{1,17},{9,25},{17,1},{25,9},{2,18},{10... | collective-permute-start | bytes 1179656 | tf_op jit(solution)/shard_map/ppermute | solution.py:455
  32.7 5.9 %collective-permute-start.9 = (bf16[48,2176]{1,0:T(8,128)(2,1)S(1)}, bf16[48,2176]{1,0:T(8,128)(2,1)S(1)}, u32[]{:S(2)}, u32[]{:S(2)}) collective-permute-start(bf16[48,2176]{1,0:T(8,128)(2,1)S(1)} %slice.7), channel_id=1, source_target_pairs={{0,2},{1,3},{2,0},{3,1},{4,6},{5,7},{6,4},{7,5},{8,10},{9,11},{10,... | collective-permute-start | bytes 626696 | tf_op jit(solution)/shard_map/ppermute | solution.py:455
  33.3 41.2 %all-to-all-start = ((bf16[4,192,256]{2,1,0:T(8,128)(2,1)}), bf16[4,192,256]{2,1,0:T(8,128)(2,1)S(1)}, u32[]{:S(2)}, u32[]{:S(2)}) async-start(bf16[4,192,256]{2,1,0:T(8,128)(2,1)} %cut.1), calls=%async_computation | async-start | bytes 786432 | tf_op jit(solution)/shard_map/all_to_all | solution.py:526
  36.8 29.8 %collective-permute-start.6 = (bf16[96,2176]{1,0:T(8,128)(2,1)S(1)}, bf16[96,2176]{1,0:T(8,128)(2,1)S(1)}, u32[]{:S(2)}, u32[]{:S(2)}) collective-permute-start(bf16[96,2176]{1,0:T(8,128)(2,1)S(1)} %collective-permute-done.3.refs_2_), channel_id=1, source_target_pairs={{0,1},{1,0},{2,3},{3,2},{4,5},{5,4},{6,7},{7,6},{8,9},{9,8},{10,11... | collective-permute-start | bytes 1253384 | tf_op jit(solution)/shard_map/ppermute | solution.py:455
  36.9 30.4 %copy-start.12 = (bf16[48,2176]{1,0:T(8,128)(2,1)}, bf16[48,2176]{1,0:T(8,128)(2,1)S(1)}, u32[]{:S(2)}) copy-start(bf16[48,2176]{1,0:T(8,128)(2,1)S(1)} %collective-permute-done.8.refs_6_) | copy-start | bytes 626692
  36.9 30.4 %collective-permute-start.7 = (bf16[96,2176]{1,0:T(8,128)(2,1)S(1)}, bf16[96,2176]{1,0:T(8,128)(2,1)S(1)}, u32[]{:S(2)}, u32[]{:S(2)}) collective-permute-start(bf16[96,2176]{1,0:T(8,128)(2,1)S(1)} %collective-permute-done.4.refs_4_), channel_id=1, source_target_pairs={{0,1},{1,0},{2,3},{3,2},{4,5},{5,4},{6,7},{7,6},{8,9},{9,8},{10,11... | collective-permute-start | bytes 1253384 | tf_op jit(solution)/shard_map/ppermute | solution.py:455
  38.6 28.7 %copy-start.13 = (bf16[48,2176]{1,0:T(8,128)(2,1)}, bf16[48,2176]{1,0:T(8,128)(2,1)S(1)}, u32[]{:S(2)}) copy-start(bf16[48,2176]{1,0:T(8,128)(2,1)S(1)} %collective-permute-done.9.refs_7_) | copy-start | bytes 626692
  38.6 42.0 %collective-permute-start.14 = (bf16[192,1024]{1,0:T(8,128)(2,1)S(1)}, bf16[192,1024]{1,0:T(8,128)(2,1)}, u32[]{:S(2)}, u32[]{:S(2)}) collective-permute-start(bf16[192,1024]{1,0:T(8,128)(2,1)S(1)} %bitcast.5), channel_id=1, source_target_pairs={{0,24},{8,16},{16,8},{24,0},{1,25},{9,17},{17,9},{25,1},{2,26},{10... | collective-permute-start | bytes 1179656 | tf_op jit(solution)/shard_map/ppermute | solution.py:455
  47.8 17.3 %collective-permute-start.10 = (bf16[48,2176]{1,0:T(8,128)(2,1)S(1)}, bf16[48,2176]{1,0:T(8,128)(2,1)S(1)}, u32[]{:S(2)}, u32[]{:S(2)}) collective-permute-start(bf16[48,2176]{1,0:T(8,128)(2,1)S(1)} %collective-permute-done.8.refs_6_), channel_id=1, source_target_pairs={{0,1},{1,0},{2,3},{3,2},{4,5},{5,4},{6,7},{7,6},{8,9},{9,8},{10,11... | collective-permute-start | bytes 626696 | tf_op jit(solution)/shard_map/ppermute | solution.py:455
  65.1 1.5 collective-permute-start.11
  65.1 2.2 %copy-start.14 = (bf16[48,2176]{1,0:T(8,128)(2,1)}, bf16[48,2176]{1,0:T(8,128)(2,1)S(1)}, u32[]{:S(2)}) copy-start(bf16[48,2176]{1,0:T(8,128)(2,1)S(1)} %collective-permute-done.10.refs_8_) | copy-start | bytes 626692
  66.6 0.7 copy-start.15
  67.3 0.8 copy-start.9
  68.1 0.8 copy-start.10
  74.5 0.7 copy-start.4
  77.5 15.1 %all-to-all-start.1 = ((f32[32,2,128]{2,1,0:T(2,128)}), f32[32,2,128]{2,1,0:T(2,128)S(1)}, u32[]{:S(2)}, u32[]{:S(2)}) async-start(f32[32,2,128]{2,1,0:T(2,128)} %get-tuple-element.84), calls=%async_computation.1 | async-start | bytes 65536 | tf_op jit(solution)/shard_map/all_to_all | solution.py:31
  92.6 18.3 %copy-start.1 = (bf16[32,16,128]{2,1,0:T(8,128)(2,1)S(1)}, bf16[32,16,128]{2,1,0:T(8,128)(2,1)}, u32[]{:S(2)}) copy-start(bf16[32,16,128]{2,1,0:T(8,128)(2,1)} %get-tuple-element.81.refs_0_.msgs_ref) | copy-start | bytes 393220
  92.7 18.3 %copy-start.2 = (f32[16,128]{1,0:T(8,128)S(1)}, f32[16,128]{1,0:T(8,128)}, u32[]{:S(2)}) copy-start(f32[16,128]{1,0:T(8,128)} %get-tuple-element.92.gap_ref) | copy-start | bytes 24580
  92.7 18.3 %copy-start.3 = (f32[16,128]{1,0:T(8,128)S(1)}, f32[16,128]{1,0:T(8,128)}, u32[]{:S(2)}) copy-start(f32[16,128]{1,0:T(8,128)} %get-tuple-element.93.own_ref) | copy-start | bytes 24580
  92.7 0.6 copy-start.17
  124.1 14.8 %all-to-all-start.4 = ((f32[32,2,128]{2,1,0:T(2,128)}), f32[32,2,128]{2,1,0:T(2,128)S(1)}, u32[]{:S(2)}, u32[]{:S(2)}) async-start(f32[32,2,128]{2,1,0:T(2,128)} %get-tuple-element.95), calls=%async_computation.4 | async-start | bytes 65536 | tf_op jit(solution)/shard_map/all_to_all | solution.py:31
  138.9 18.2 %copy-start = (bf16[32,16,128]{2,1,0:T(8,128)(2,1)S(1)}, bf16[32,16,128]{2,1,0:T(8,128)(2,1)}, u32[]{:S(2)}) copy-start(bf16[32,16,128]{2,1,0:T(8,128)(2,1)} %all_to_all.36.refs_0_.msgs_ref) | copy-start | bytes 393220
  138.9 0.6 copy-start.16

commit v21 on v19

--- a/solution.py
+++ b/solution.py
@@ -262,27 +262,22 @@
     turned_ref, scr_ref, rows_ref, qx_ref, refs = refs[0], refs[1], refs[2], refs[3], refs[4:]
     cond_refs, refs = refs[:n_ka], refs[n_ka:]
     di_ref, qx, turned, conds, scrs, vals, mixed, kern, folded = refs[:9]
-    qx_sem, cond_sems, row_sem, chunk_sems = refs[9:]
+    qx_sem, cond_sems, row_sems, chunk_sems = refs[9:]
     nu, mu = scr_ref.shape
     quad = 2 * LANES
     qx_copy = pltpu.make_async_copy(qx_ref, qx, qx_sem.at[0])
     cond_copies = [
         pltpu.make_async_copy(ref, conds.at[j], cond_sems.at[j]) for j, ref in enumerate(cond_refs)
     ]
-    turned_copies, scr_copies = [], []
+    turned_copies = []
     for i in range(nu // tile):
         at = pl.ds(i * tile, tile)
         turned_copies.append(
-            pltpu.make_async_copy(turned_ref.at[at, :], turned.at[at, :], chunk_sems.at[0, i])
+            pltpu.make_async_copy(turned_ref.at[at, :], turned.at[at, :], chunk_sems.at[i])
         )
-        scr_copies.append(
-            pltpu.make_async_copy(scr_ref.at[at, :], scrs.at[at, :], chunk_sems.at[1, i])
-        )
-    row_copy = pltpu.make_async_copy(rows_ref, vals, row_sem.at[0])
-    start_all([qx_copy, turned_copies[0]] + cond_copies + [scr_copies[0]])
-    for i in range(1, nu // tile):
-        start_all([turned_copies[i], scr_copies[i]])
-    row_copy.start()
+    scr_copy = pltpu.make_async_copy(scr_ref, scrs, row_sems.at[0])
+    row_copy = pltpu.make_async_copy(rows_ref, vals, row_sems.at[1])
+    start_all([qx_copy] + turned_copies + cond_copies + [scr_copy, row_copy])
     qx_copy.wait()
     for i in range(nu // tile):
         rows = slice(i * tile, (i + 1) * tile)
@@ -292,12 +287,11 @@
             mixed[rows, cols] = jnp.dot(
                 turned[rows, cols], qx[kq], preferred_element_type=F32
             ).astype(BF)
-        if i == 0:
-            wait_all(cond_copies)
-            cond_rows = conds[...].reshape(-1, mu)
-        scr_copies[i].wait()
-        amp = jnp.dot(mixed[rows, :], cond_rows, preferred_element_type=F32)
-        kern[rows, :] = (scrs[rows, :].astype(F32) * amp).astype(BF)
+    wait_all(cond_copies)
+    cond_rows = conds[...].reshape(-1, mu)
+    scr_copy.wait()
+    amp = jnp.dot(mixed[...], cond_rows, preferred_element_type=F32)
+    kern[...] = (scrs[...].astype(F32) * amp).astype(BF)
     row_copy.wait()
     folded[...] = jnp.dot(vals[...], kern[...], preferred_element_type=F32).astype(BF)
     for kq in range(qx.shape[0]):
@@ -524,7 +518,7 @@
     cond_pts = [cond_local] + [swap(cond_local, "ka", j) for j in range(1, n_ka)]
     cond_own = lax.all_to_all(cuts, "ka", split_axis=0, concat_axis=0, tiled=True)
 
-    chunk, tile = 1024, nu_blk
+    chunk, tile = 1024, nu_blk // 4
     rows_all, conds_all = k_points * nv_blk * n_band, k_points * n_cond
     scr_turned = call(
         functools.partial(turn_kernel, nu_blk // 4),
@@ -600,8 +594,8 @@
                 pltpu.VMEM((rows_all, mu_blk), BF),
                 dma(1),
                 dma(n_ka),
-                dma(1),
-                dma(2, nu_blk // tile),
+                dma(2),
+                dma(nu_blk // tile),
             ],
             flops=4 * mu_blk * nu_blk * conds_all,
             moved=12 * MIB,

time: 151 us -> 154 us (1.020)
  Pallas kernels: 50.4 us -> 53 us
    pallas_call x2, Pallas kernels: 23.9 us -> 26.6 us  [kernel_path(): call(functools.partial(direct_kernel, n_ka, tile, scale), 'direct', shape...]
  transfers between devices with their start and end apart: 18 -> 18, of which waited for: 5 -> 5; matrix products, arithmetic and copies ran while one was open for 1% -> 1% of each run, Pallas kernels for 25% -> 26%
where the time goes in v21:
time: 154 us; the launch traced here: 153 us
  Pallas kernels  53 us (34%)
  blocking collectives  47.4 us (31%)
  starting transfers between devices  26.4 us (17%)
  waiting for transfers between devices  20.2 us (13%)
  local copies, waits for them, and re-layouts  4.8 us (3%)
    all_to_all x4, blocking collectives, exchange_all(): return lax.all_to_all(parts, AXES, split_axis=0, concat_axis=0, tiled=True)  47.4 us
    pallas_call x2, Pallas kernels, kernel_path(): call(functools.partial(direct_kernel, n_ka, tile, scale), 'direct', shape...  26.6 us
    ppermute x15, waiting for transfers between devices, swap(): lax.ppermute(block, axis, [(i, i ^ d) for i in range(lax.axis_size(axis))])  20.2 us
    ppermute x15, starting transfers between devices, swap(): lax.ppermute(block, axis, [(i, i ^ d) for i in range(lax.axis_size(axis))])  17.4 us
    pallas_call x2, Pallas kernels, kernel_path(): call(functools.partial(exchange_kernel, cfg, chunk, scale), 'exchange', m...  7.47 us
    pallas_call x1, Pallas kernels, kernel_path(): call(functools.partial(order_kernel, parts, n_ka), 'order', (shape_of((ro...  5.69 us
    all_to_all x2, starting transfers between devices, exchange_all(): return lax.all_to_all(parts, AXES, split_axis=0, concat_axis=0, tiled=True)  5.5 us
    pallas_call x2, Pallas kernels, kernel_path(): call(functools.partial(density_kernel, cfg), 'density', (shape_of((quads,...  4.49 us
  transfers between devices with their start and end apart: 18, of which 5 were waited for; matrix products, arithmetic and copies ran while one was open for 1% of the time, Pallas kernels for 26%

profile of v21, /device:TPU:0, one launch (start us, length us, event | category | flops | bytes accessed | tf_op | source)
XLA Modules:
  0.0 153.1 jit_solution(14930160493718690010)
XLA Ops:
  0.6 1.9 %pack.1 = (f32[16,128]{1,0:T(8,128)}, f32[16,128]{1,0:T(8,128)}, bf16[3,8,2176]{2,1,0:T(8,128)(2,1)}, bf16[3,8,2176]{2,1,0:T(8,128)(2,1)}, bf16[3,8,2176]{2,1,0:T(8,128)(2,1)}, /*index=5*/bf16[3,8,2176]{2,1,0:T(8,128)(2,1)}) custom-call(f32[3,512]{1,0:T(4,128)} %refs_0_.1, f32[3,64]{1,0:T(4,128)} %refs_1_.1, f32[3,8]{1,0:T(4,128)} %refs_2_.3, ...), custom_call_target="tpu_custom_call" | custom-call | tf_op jit(solution)/shard_map/pack/pallas_call | solution.py:489
  2.5 3.1 %collective-permute-start = (bf16[3,8,2176]{2,1,0:T(8,128)(2,1)}, bf16[3,8,2176]{2,1,0:T(8,128)(2,1)S(1)}, u32[]{:S(2)}, u32[]{:S(2)}) collective-permute-start(bf16[3,8,2176]{2,1,0:T(8,128)(2,1)} %get-tuple-element.53), channel_id=1, source_target_pairs={{0,8},{8,0},{16,24},{24,16},{1,9},{9,1},{17,25},{25,17},{2,10},{10... | collective-permute-start | bytes 313352 | tf_op jit(solution)/shard_map/ppermute | solution.py:449
  5.6 2.6 %collective-permute-start.1 = (bf16[3,8,2176]{2,1,0:T(8,128)(2,1)}, bf16[3,8,2176]{2,1,0:T(8,128)(2,1)S(1)}, u32[]{:S(2)}, u32[]{:S(2)}) collective-permute-start(bf16[3,8,2176]{2,1,0:T(8,128)(2,1)} %get-tuple-element.54), channel_id=1, source_target_pairs={{0,16},{8,24},{16,0},{24,8},{1,17},{9,25},{17,1},{25,9},{2,18},{10... | collective-permute-start | bytes 313352 | tf_op jit(solution)/shard_map/ppermute | solution.py:449
  8.2 1.8 %cut.1 = bf16[4,192,256]{2,1,0:T(8,128)(2,1)} custom-call(bf16[3,64,8192]{2,1,0:T(8,128)(2,1)} %cond_ref.1), custom_call_target="tpu_custom_call" | custom-call | tf_op jit(solution)/shard_map/cut/pallas_call | solution.py:506
  10.0 1.2 constant_dynamic-slice_fusion
  11.2 0.0 collective-permute-done
  11.3 5.5 %collective-permute-done.1 = bf16[3,8,2176]{2,1,0:T(8,128)(2,1)S(1)} collective-permute-done((bf16[3,8,2176]{2,1,0:T(8,128)(2,1)}, bf16[3,8,2176]{2,1,0:T(8,128)(2,1)S(1)}, u32[]{:S(2)}, u32[]{:S(2)}) %collective-permute-start.1) | collective-permute-done | bytes 104480 | tf_op jit(solution)/shard_map/ppermute | solution.py:449
  16.7 0.0 collective-permute-done.2
  16.7 0.1 maximum_bitcast_fusion.refs_0_
  16.8 1.6 %collective-permute-start.4 = (bf16[96,2176]{1,0:T(8,128)(2,1)S(1)}, bf16[96,2176]{1,0:T(8,128)(2,1)S(1)}, u32[]{:S(2)}, u32[]{:S(2)}) collective-permute-start(bf16[96,2176]{1,0:T(8,128)(2,1)S(1)} %maximum_bitcast_fusion.refs_0_), channel_id=1, source_target_pairs={{0,2},{1,3},{2,0},{3,1},{4,6},{5,7},{6,4},{7,5},{8,10},{9,11},{10,... | collective-permute-start | bytes 1253384 | tf_op jit(solution)/shard_map/ppermute | solution.py:449
  18.4 1.5 collective-permute-start.5
  19.9 1.7 %collective-permute-start.12 = (bf16[192,1024]{1,0:T(8,128)(2,1)S(1)}, bf16[192,1024]{1,0:T(8,128)(2,1)}, u32[]{:S(2)}, u32[]{:S(2)}) collective-permute-start(bf16[192,1024]{1,0:T(8,128)(2,1)S(1)} %bitcast.3), channel_id=1, source_target_pairs={{0,8},{8,0},{16,24},{24,16},{1,9},{9,1},{17,25},{25,17},{2,10},{10... | collective-permute-start | bytes 1179656 | tf_op jit(solution)/shard_map/ppermute | solution.py:449
  21.6 1.4 collective-permute-start.13
  22.9 3.5 %all-to-all-start = ((bf16[4,192,256]{2,1,0:T(8,128)(2,1)}), bf16[4,192,256]{2,1,0:T(8,128)(2,1)S(1)}, u32[]{:S(2)}, u32[]{:S(2)}) async-start(bf16[4,192,256]{2,1,0:T(8,128)(2,1)} %cut.1), calls=%async_computation | async-start | bytes 786432 | tf_op jit(solution)/shard_map/all_to_all | solution.py:519
  26.4 3.7 %turn.1.refs_1_ = bf16[2048,1024]{1,0:T(8,128)(2,1)} custom-call(bf16[1024,2048]{1,0:T(8,128)(2,1)} %scr_ref.1), custom_call_target="tpu_custom_call" | custom-call | bytes 8388608 | tf_op jit(solution)/shard_map/turn/pallas_call | solution.py:523
  30.2 0.6 collective-permute-start.8
  30.8 0.6 collective-permute-start.9
  31.4 6.8 %collective-permute-done.12.refs_5_ = bf16[192,1024]{1,0:T(8,128)(2,1)} collective-permute-done((bf16[192,1024]{1,0:T(8,128)(2,1)S(1)}, bf16[192,1024]{1,0:T(8,128)(2,1)}, u32[]{:S(2)}, u32[]{:S(2)}) %collective-permute-start.12) | collective-permute-done | bytes 393248 | tf_op jit(solution)/shard_map/ppermute | solution.py:449
  38.2 6.6 %collective-permute-done.13.refs_6_ = bf16[192,1024]{1,0:T(8,128)(2,1)} collective-permute-done((bf16[192,1024]{1,0:T(8,128)(2,1)S(1)}, bf16[192,1024]{1,0:T(8,128)(2,1)}, u32[]{:S(2)}, u32[]{:S(2)}) %collective-permute-start.13) | collective-permute-done | bytes 393248 | tf_op jit(solution)/shard_map/ppermute | solution.py:449
  44.8 3.9 %collective-permute-start.14 = (bf16[192,1024]{1,0:T(8,128)(2,1)S(1)}, bf16[192,1024]{1,0:T(8,128)(2,1)}, u32[]{:S(2)}, u32[]{:S(2)}) collective-permute-start(bf16[192,1024]{1,0:T(8,128)(2,1)S(1)} %bitcast.5), channel_id=1, source_target_pairs={{0,24},{8,16},{16,8},{24,0},{1,25},{9,17},{17,9},{25,1},{2,26},{10... | collective-permute-start | bytes 1179656 | tf_op jit(solution)/shard_map/ppermute | solution.py:449
  48.8 0.2 collective-permute-start.10
  49.0 0.3 collective-permute-start.11
  49.3 0.9 collective-permute-done.10.refs_8_
  50.2 0.3 collective-permute-done.11.refs_9_
  50.6 0.3 copy-done.14
  50.9 0.3 copy-done.15
  51.2 0.2 copy-done.9
  51.4 0.8 copy-done.10
  52.2 5.7 %order.1 = (bf16[768,2048]{1,0:T(8,128)(2,1)}, bf16[2048,768]{1,0:T(8,128)(2,1)}, bf16[768,256]{1,0:T(8,128)(2,1)}, bf16[32,16,128]{2,1,0:T(8,128)(2,1)}) custom-call(bf16[96,2176]{1,0:T(8,128)(2,1)} %copy-done.5, bf16[96,2176]{1,0:T(8,128)(2,1)} %copy-done.8, bf16[96,2176]{1,0:T(8,128)(2,1)} %copy-done.6, bf16[96,2176]{1,0:T(8,128)(2,1)} %copy-done.9, ...), custom_call_target="tpu_custom_call" | custom-call | bytes 9437184 | tf_op jit(solution)/shard_map/order/pallas_call | solution.py:535
  57.9 0.7 copy-done.4
  58.6 2.2 %density.2 = (bf16[3,256,256]{2,1,0:T(8,128)(2,1)}, f32[32,2,128]{2,1,0:T(2,128)}) custom-call(bf16[32,16,128]{2,1,0:T(8,128)(2,1)} %get-tuple-element.74.refs_0_.msgs_ref, bf16[768,256]{1,0:T(8,128)(2,1)} %get-tuple-element.75.refs_1_.refs_3_, bf16[4,192,256]{2,1,0:T(8,128)(2,1)} %copy-done.4), custom_call_target="tpu_custom_call" | custom-call | tf_op jit(solution)/shard_map/density/pallas_call | solution.py:562
  60.9 2.7 %all-to-all-start.1 = ((f32[32,2,128]{2,1,0:T(2,128)}), f32[32,2,128]{2,1,0:T(2,128)S(1)}, u32[]{:S(2)}, u32[]{:S(2)}) async-start(f32[32,2,128]{2,1,0:T(2,128)} %get-tuple-element.77), calls=%async_computation.1 | async-start | bytes 65536 | tf_op jit(solution)/shard_map/all_to_all | solution.py:31
  63.6 13.3 %direct.2.refs_1_ = f32[6,128,128]{2,1,0:T(8,128)} custom-call(bf16[2048,768]{1,0:T(8,128)(2,1)} %get-tuple-element.78.refs_0_, bf16[2048,1024]{1,0:T(8,128)(2,1)} %turn.1.refs_1_, bf16[768,2048]{1,0:T(8,128)(2,1)} %get-tuple-element.80.refs_2_, bf16[3,256,256]{2,1,0:T(8,128)(2,1)} %get-tuple-element.81.refs_3_, bf16[192,1024]{1,0:T(8,128)(2,1)} %bitcast.6, ...), custom_call_target="tpu_custom_call" | custom-call | flops 6442450944 | bytes 12582912 | tf_op jit(solution)/shard_map/direct/pallas_call | solution.py:580
  76.9 0.0 copy-start.3
  76.9 0.6 copy-done.17
  77.5 3.7 %exchange.2 = bf16[32,16,128]{2,1,0:T(8,128)(2,1)} custom-call(f32[32,2,128]{2,1,0:T(2,128)} %copy-done.17, f32[6,128,128]{2,1,0:T(8,128)} %direct.2.refs_1_, bf16[256,8192]{1,0:T(8,128)(2,1)} %refs_2_.5, bf16[768,256]{1,0:T(8,128)(2,1)} %get-tuple-element.75.refs_1_.refs_3_, bf16[4,192,256]{2,1,0:T(8,128)(2,1)} %copy-done.4), custom_call_target="tpu_custom_call" | custom-call | tf_op jit(solution)/shard_map/exchange/pallas_call | solution.py:603
  81.3 13.9 %all_to_all.35.recv_ref = bf16[32,16,128]{2,1,0:T(8,128)(2,1)S(1)} all-to-all(bf16[32,16,128]{2,1,0:T(8,128)(2,1)} %exchange.2), channel_id=1, replica_groups=mesh['ka'=4,'band'=8] {'ka','band'}, dimensions={0} | all-to-all | bytes 262144 | tf_op jit(solution)/shard_map/all_to_all | solution.py:31
  95.2 0.3 first_owner.1
  95.5 10.6 %all_to_all.36.refs_0_.msgs_ref = bf16[32,16,128]{2,1,0:T(8,128)(2,1)} all-to-all(bf16[32,16,128]{2,1,0:T(8,128)(2,1)S(1)} %get-tuple-element.86), channel_id=1, replica_groups=mesh['ka'=4,'band'=8] {'ka','band'}, dimensions={0} | all-to-all | bytes 262144 | tf_op jit(solution)/shard_map/all_to_all | solution.py:31
  106.1 2.2 %density.3 = (bf16[3,256,256]{2,1,0:T(8,128)(2,1)}, f32[32,2,128]{2,1,0:T(2,128)}) custom-call(bf16[32,16,128]{2,1,0:T(8,128)(2,1)} %all_to_all.36.refs_0_.msgs_ref, bf16[768,256]{1,0:T(8,128)(2,1)} %get-tuple-element.75.refs_1_.refs_3_, bf16[4,192,256]{2,1,0:T(8,128)(2,1)} %copy-done.4), custom_call_target="tpu_custom_call" | custom-call | tf_op jit(solution)/shard_map/density/pallas_call | solution.py:562
  108.4 2.8 %all-to-all-start.4 = ((f32[32,2,128]{2,1,0:T(2,128)}), f32[32,2,128]{2,1,0:T(2,128)S(1)}, u32[]{:S(2)}, u32[]{:S(2)}) async-start(f32[32,2,128]{2,1,0:T(2,128)} %get-tuple-element.87), calls=%async_computation.4 | async-start | bytes 65536 | tf_op jit(solution)/shard_map/all_to_all | solution.py:31
  111.2 13.3 %direct.3.refs_1_ = f32[6,128,128]{2,1,0:T(8,128)} custom-call(bf16[2048,768]{1,0:T(8,128)(2,1)} %get-tuple-element.78.refs_0_, bf16[2048,1024]{1,0:T(8,128)(2,1)} %turn.1.refs_1_, bf16[768,2048]{1,0:T(8,128)(2,1)} %get-tuple-element.80.refs_2_, bf16[3,256,256]{2,1,0:T(8,128)(2,1)} %get-tuple-element.88.refs_3_, bf16[192,1024]{1,0:T(8,128)(2,1)} %bitcast.7, ...), custom_call_target="tpu_custom_call" | custom-call | flops 6442450944 | bytes 12582912 | tf_op jit(solution)/shard_map/direct/pallas_call | solution.py:580
  124.5 0.6 copy-done.16
  125.1 3.7 %exchange.3 = bf16[32,16,128]{2,1,0:T(8,128)(2,1)} custom-call(f32[32,2,128]{2,1,0:T(2,128)} %copy-done.16, f32[6,128,128]{2,1,0:T(8,128)} %direct.3.refs_1_, bf16[256,8192]{1,0:T(8,128)(2,1)} %refs_2_.5, bf16[768,256]{1,0:T(8,128)(2,1)} %get-tuple-element.75.refs_1_.refs_3_, bf16[4,192,256]{2,1,0:T(8,128)(2,1)} %copy-done.4), custom_call_target="tpu_custom_call" | custom-call | tf_op jit(solution)/shard_map/exchange/pallas_call | solution.py:603
  128.8 13.9 %all_to_all.37.recv_ref = bf16[32,16,128]{2,1,0:T(8,128)(2,1)S(1)} all-to-all(bf16[32,16,128]{2,1,0:T(8,128)(2,1)} %exchange.3), channel_id=1, replica_groups=mesh['ka'=4,'band'=8] {'ka','band'}, dimensions={0} | all-to-all | bytes 262144 | tf_op jit(solution)/shard_map/all_to_all | solution.py:31
  142.7 0.4 second_owner.1
  143.1 9.0 %all_to_all.38.msgs_ref = f32[32,2,128]{2,1,0:T(2,128)S(1)} all-to-all(f32[32,2,128]{2,1,0:T(2,128)S(1)} %get-tuple-element.91), channel_id=1, replica_groups=mesh['ka'=4,'band'=8] {'ka','band'}, dimensions={0} | all-to-all | bytes 65536 | tf_op jit(solution)/shard_map/all_to_all | solution.py:31
  152.1 0.8 finish.1
  (47 shorter events, 0.1 us)
Async XLA Ops:
  2.5 14.2 %copy-start.18 = (bf16[3,8,2176]{2,1,0:T(8,128)(2,1)S(1)}, bf16[3,8,2176]{2,1,0:T(8,128)(2,1)}, u32[]{:S(2)}) copy-start(bf16[3,8,2176]{2,1,0:T(8,128)(2,1)} %get-tuple-element.57) | copy-start | bytes 313348
  2.5 8.7 %collective-permute-start = (bf16[3,8,2176]{2,1,0:T(8,128)(2,1)}, bf16[3,8,2176]{2,1,0:T(8,128)(2,1)S(1)}, u32[]{:S(2)}, u32[]{:S(2)}) collective-permute-start(bf16[3,8,2176]{2,1,0:T(8,128)(2,1)} %get-tuple-element.53), channel_id=1, source_target_pairs={{0,8},{8,0},{16,24},{24,16},{1,9},{9,1},{17,25},{25,17},{2,10},{10... | collective-permute-start | bytes 313352 | tf_op jit(solution)/shard_map/ppermute | solution.py:449
  5.6 11.1 %collective-permute-start.1 = (bf16[3,8,2176]{2,1,0:T(8,128)(2,1)}, bf16[3,8,2176]{2,1,0:T(8,128)(2,1)S(1)}, u32[]{:S(2)}, u32[]{:S(2)}) collective-permute-start(bf16[3,8,2176]{2,1,0:T(8,128)(2,1)} %get-tuple-element.54), channel_id=1, source_target_pairs={{0,16},{8,24},{16,0},{24,8},{1,17},{9,25},{17,1},{25,9},{2,18},{10... | collective-permute-start | bytes 313352 | tf_op jit(solution)/shard_map/ppermute | solution.py:449
  8.2 8.5 %collective-permute-start.2 = (bf16[3,8,2176]{2,1,0:T(8,128)(2,1)}, bf16[3,8,2176]{2,1,0:T(8,128)(2,1)S(1)}, u32[]{:S(2)}, u32[]{:S(2)}) collective-permute-start(bf16[3,8,2176]{2,1,0:T(8,128)(2,1)} %get-tuple-element.55), channel_id=1, source_target_pairs={{0,24},{8,16},{16,8},{24,0},{1,25},{9,17},{17,9},{25,1},{2,26},{10... | collective-permute-start | bytes 313352 | tf_op jit(solution)/shard_map/ppermute | solution.py:449
  11.2 33.6 %copy-start.11 = (bf16[3,64,1024]{2,1,0:T(8,128)(2,1)}, bf16[3,64,1024]{2,1,0:T(8,128)(2,1)S(1)}, u32[]{:S(2)}) copy-start(bf16[3,64,1024]{2,1,0:T(8,128)(2,1)S(1)} %constant_dynamic-slice_fusion) | copy-start | bytes 1179652
  16.8 13.3 %copy-start.5 = (bf16[96,2176]{1,0:T(8,128)(2,1)}, bf16[96,2176]{1,0:T(8,128)(2,1)S(1)}, u32[]{:S(2)}) copy-start(bf16[96,2176]{1,0:T(8,128)(2,1)S(1)} %maximum_bitcast_fusion.refs_0_) | copy-start | bytes 1253380
  16.8 13.3 %collective-permute-start.4 = (bf16[96,2176]{1,0:T(8,128)(2,1)S(1)}, bf16[96,2176]{1,0:T(8,128)(2,1)S(1)}, u32[]{:S(2)}, u32[]{:S(2)}) collective-permute-start(bf16[96,2176]{1,0:T(8,128)(2,1)S(1)} %maximum_bitcast_fusion.refs_0_), channel_id=1, source_target_pairs={{0,2},{1,3},{2,0},{3,1},{4,6},{5,7},{6,4},{7,5},{8,10},{9,11},{10,... | collective-permute-start | bytes 1253384 | tf_op jit(solution)/shard_map/ppermute | solution.py:449
  18.4 11.8 %collective-permute-start.5 = (bf16[96,2176]{1,0:T(8,128)(2,1)S(1)}, bf16[96,2176]{1,0:T(8,128)(2,1)S(1)}, u32[]{:S(2)}, u32[]{:S(2)}) collective-permute-start(bf16[96,2176]{1,0:T(8,128)(2,1)S(1)} %maximum_bitcast_fusion.refs_0_), channel_id=1, source_target_pairs={{0,4},{1,5},{2,6},{3,7},{4,0},{5,1},{6,2},{7,3},{8,12},{9,13},{10,... | collective-permute-start | bytes 1253384 | tf_op jit(solution)/shard_map/ppermute | solution.py:449
  19.9 18.3 %collective-permute-start.12 = (bf16[192,1024]{1,0:T(8,128)(2,1)S(1)}, bf16[192,1024]{1,0:T(8,128)(2,1)}, u32[]{:S(2)}, u32[]{:S(2)}) collective-permute-start(bf16[192,1024]{1,0:T(8,128)(2,1)S(1)} %bitcast.3), channel_id=1, source_target_pairs={{0,8},{8,0},{16,24},{24,16},{1,9},{9,1},{17,25},{25,17},{2,10},{10... | collective-permute-start | bytes 1179656 | tf_op jit(solution)/shard_map/ppermute | solution.py:449
  21.6 23.3 %collective-permute-start.13 = (bf16[192,1024]{1,0:T(8,128)(2,1)S(1)}, bf16[192,1024]{1,0:T(8,128)(2,1)}, u32[]{:S(2)}, u32[]{:S(2)}) collective-permute-start(bf16[192,1024]{1,0:T(8,128)(2,1)S(1)} %bitcast.4), channel_id=1, source_target_pairs={{0,16},{8,24},{16,0},{24,8},{1,17},{9,25},{17,1},{25,9},{2,18},{10... | collective-permute-start | bytes 1179656 | tf_op jit(solution)/shard_map/ppermute | solution.py:449
  22.9 21.9 %collective-permute-start.3 = (bf16[96,2176]{1,0:T(8,128)(2,1)S(1)}, bf16[96,2176]{1,0:T(8,128)(2,1)S(1)}, u32[]{:S(2)}, u32[]{:S(2)}) collective-permute-start(bf16[96,2176]{1,0:T(8,128)(2,1)S(1)} %maximum_bitcast_fusion.refs_0_), channel_id=1, source_target_pairs={{0,1},{1,0},{2,3},{3,2},{4,5},{5,4},{6,7},{7,6},{8,9},{9,8},{10,11... | collective-permute-start | bytes 1253384 | tf_op jit(solution)/shard_map/ppermute | solution.py:449
  22.9 34.9 %all-to-all-start = ((bf16[4,192,256]{2,1,0:T(8,128)(2,1)}), bf16[4,192,256]{2,1,0:T(8,128)(2,1)S(1)}, u32[]{:S(2)}, u32[]{:S(2)}) async-start(bf16[4,192,256]{2,1,0:T(8,128)(2,1)} %cut.1), calls=%async_computation | async-start | bytes 786432 | tf_op jit(solution)/shard_map/all_to_all | solution.py:519
  30.1 20.4 %copy-start.6 = (bf16[96,2176]{1,0:T(8,128)(2,1)}, bf16[96,2176]{1,0:T(8,128)(2,1)S(1)}, u32[]{:S(2)}) copy-start(bf16[96,2176]{1,0:T(8,128)(2,1)S(1)} %collective-permute-done.4.refs_2_) | copy-start | bytes 1253380
  30.1 20.4 %copy-start.7 = (bf16[96,2176]{1,0:T(8,128)(2,1)}, bf16[96,2176]{1,0:T(8,128)(2,1)S(1)}, u32[]{:S(2)}) copy-start(bf16[96,2176]{1,0:T(8,128)(2,1)S(1)} %collective-permute-done.5.refs_4_) | copy-start | bytes 1253380
  30.2 18.6 %collective-permute-start.8 = (bf16[48,2176]{1,0:T(8,128)(2,1)S(1)}, bf16[48,2176]{1,0:T(8,128)(2,1)S(1)}, u32[]{:S(2)}, u32[]{:S(2)}) collective-permute-start(bf16[48,2176]{1,0:T(8,128)(2,1)S(1)} %slice.6), channel_id=1, source_target_pairs={{0,4},{1,5},{2,6},{3,7},{4,0},{5,1},{6,2},{7,3},{8,12},{9,13},{10,... | collective-permute-start | bytes 626696 | tf_op jit(solution)/shard_map/ppermute | solution.py:449
  30.8 18.2 %collective-permute-start.9 = (bf16[48,2176]{1,0:T(8,128)(2,1)S(1)}, bf16[48,2176]{1,0:T(8,128)(2,1)S(1)}, u32[]{:S(2)}, u32[]{:S(2)}) collective-permute-start(bf16[48,2176]{1,0:T(8,128)(2,1)S(1)} %slice.7), channel_id=1, source_target_pairs={{0,2},{1,3},{2,0},{3,1},{4,6},{5,7},{6,4},{7,5},{8,10},{9,11},{10,... | collective-permute-start | bytes 626696 | tf_op jit(solution)/shard_map/ppermute | solution.py:449
  38.2 12.3 %collective-permute-start.6 = (bf16[96,2176]{1,0:T(8,128)(2,1)S(1)}, bf16[96,2176]{1,0:T(8,128)(2,1)S(1)}, u32[]{:S(2)}, u32[]{:S(2)}) collective-permute-start(bf16[96,2176]{1,0:T(8,128)(2,1)S(1)} %collective-permute-done.4.refs_2_), channel_id=1, source_target_pairs={{0,1},{1,0},{2,3},{3,2},{4,5},{5,4},{6,7},{7,6},{8,9},{9,8},{10,11... | collective-permute-start | bytes 1253384 | tf_op jit(solution)/shard_map/ppermute | solution.py:449
  44.8 5.7 %collective-permute-start.7 = (bf16[96,2176]{1,0:T(8,128)(2,1)S(1)}, bf16[96,2176]{1,0:T(8,128)(2,1)S(1)}, u32[]{:S(2)}, u32[]{:S(2)}) collective-permute-start(bf16[96,2176]{1,0:T(8,128)(2,1)S(1)} %collective-permute-done.5.refs_4_), channel_id=1, source_target_pairs={{0,1},{1,0},{2,3},{3,2},{4,5},{5,4},{6,7},{7,6},{8,9},{9,8},{10,11... | collective-permute-start | bytes 1253384 | tf_op jit(solution)/shard_map/ppermute | solution.py:449
  44.8 5.7 %copy-start.8 = (bf16[96,2176]{1,0:T(8,128)(2,1)}, bf16[96,2176]{1,0:T(8,128)(2,1)S(1)}, u32[]{:S(2)}) copy-start(bf16[96,2176]{1,0:T(8,128)(2,1)S(1)} %collective-permute-done.3.refs_1_) | copy-start | bytes 1253380
  44.8 18.7 %collective-permute-start.14 = (bf16[192,1024]{1,0:T(8,128)(2,1)S(1)}, bf16[192,1024]{1,0:T(8,128)(2,1)}, u32[]{:S(2)}, u32[]{:S(2)}) collective-permute-start(bf16[192,1024]{1,0:T(8,128)(2,1)S(1)} %bitcast.5), channel_id=1, source_target_pairs={{0,24},{8,16},{16,8},{24,0},{1,25},{9,17},{17,9},{25,1},{2,26},{10... | collective-permute-start | bytes 1179656 | tf_op jit(solution)/shard_map/ppermute | solution.py:449
  48.8 1.8 %copy-start.12 = (bf16[48,2176]{1,0:T(8,128)(2,1)}, bf16[48,2176]{1,0:T(8,128)(2,1)S(1)}, u32[]{:S(2)}) copy-start(bf16[48,2176]{1,0:T(8,128)(2,1)S(1)} %collective-permute-done.8.refs_6_) | copy-start | bytes 626692
  48.8 1.5 collective-permute-start.10
  49.0 1.6 %copy-start.13 = (bf16[48,2176]{1,0:T(8,128)(2,1)}, bf16[48,2176]{1,0:T(8,128)(2,1)S(1)}, u32[]{:S(2)}) copy-start(bf16[48,2176]{1,0:T(8,128)(2,1)S(1)} %collective-permute-done.9.refs_7_) | copy-start | bytes 626692
  49.0 1.5 %collective-permute-start.11 = (bf16[48,2176]{1,0:T(8,128)(2,1)S(1)}, bf16[48,2176]{1,0:T(8,128)(2,1)S(1)}, u32[]{:S(2)}, u32[]{:S(2)}) collective-permute-start(bf16[48,2176]{1,0:T(8,128)(2,1)S(1)} %collective-permute-done.9.refs_7_), channel_id=1, source_target_pairs={{0,1},{1,0},{2,3},{3,2},{4,5},{5,4},{6,7},{7,6},{8,9},{9,8},{10,11... | collective-permute-start | bytes 626696 | tf_op jit(solution)/shard_map/ppermute | solution.py:449
  50.2 0.7 copy-start.14
  50.5 0.7 copy-start.15
  50.5 0.9 copy-start.9
  51.4 0.8 copy-start.10
  57.9 0.7 copy-start.4
  60.9 16.0 %all-to-all-start.1 = ((f32[32,2,128]{2,1,0:T(2,128)}), f32[32,2,128]{2,1,0:T(2,128)S(1)}, u32[]{:S(2)}, u32[]{:S(2)}) async-start(f32[32,2,128]{2,1,0:T(2,128)} %get-tuple-element.77), calls=%async_computation.1 | async-start | bytes 65536 | tf_op jit(solution)/shard_map/all_to_all | solution.py:31
  76.9 18.3 %copy-start.1 = (bf16[32,16,128]{2,1,0:T(8,128)(2,1)S(1)}, bf16[32,16,128]{2,1,0:T(8,128)(2,1)}, u32[]{:S(2)}) copy-start(bf16[32,16,128]{2,1,0:T(8,128)(2,1)} %get-tuple-element.74.refs_0_.msgs_ref) | copy-start | bytes 393220
  76.9 18.3 %copy-start.2 = (f32[16,128]{1,0:T(8,128)S(1)}, f32[16,128]{1,0:T(8,128)}, u32[]{:S(2)}) copy-start(f32[16,128]{1,0:T(8,128)} %get-tuple-element.84.gap_ref) | copy-start | bytes 24580
  76.9 18.3 %copy-start.3 = (f32[16,128]{1,0:T(8,128)S(1)}, f32[16,128]{1,0:T(8,128)}, u32[]{:S(2)}) copy-start(f32[16,128]{1,0:T(8,128)} %get-tuple-element.85.own_ref) | copy-start | bytes 24580
  76.9 0.6 copy-start.17
  108.4 16.1 %all-to-all-start.4 = ((f32[32,2,128]{2,1,0:T(2,128)}), f32[32,2,128]{2,1,0:T(2,128)S(1)}, u32[]{:S(2)}, u32[]{:S(2)}) async-start(f32[32,2,128]{2,1,0:T(2,128)} %get-tuple-element.87), calls=%async_computation.4 | async-start | bytes 65536 | tf_op jit(solution)/shard_map/all_to_all | solution.py:31
  124.5 18.2 %copy-start = (bf16[32,16,128]{2,1,0:T(8,128)(2,1)S(1)}, bf16[32,16,128]{2,1,0:T(8,128)(2,1)}, u32[]{:S(2)}) copy-start(bf16[32,16,128]{2,1,0:T(8,128)(2,1)} %all_to_all.36.refs_0_.msgs_ref) | copy-start | bytes 393220
  124.5 0.6 copy-start.16

commit v22 on v19

--- a/solution.py
+++ b/solution.py
@@ -335,10 +335,13 @@
     potential = scale * jnp.sum(acc.T, axis=0, keepdims=True)
     wait_all(copies)
     cond_rows = conds[...].reshape(-1, own)
-    for kp in range(k_points // 2):
-        at = slice(kp * LANES, (kp + 1) * LANES)
+    quad = 2 * LANES
+    for kq in range(k_points // 4):
+        at = slice(kq * quad, (kq + 1) * quad)
         weighted = (vown[at, :].astype(F32) * potential).astype(BF)
-        part[kp] = 2.0 * dot_nt(weighted, cond_rows[at, :]) - di[kp]
+        both = 2.0 * dot_nt(weighted, cond_rows[at, :])
+        part[2 * kq] = both[:LANES, :LANES] - di[2 * kq]
+        part[2 * kq + 1] = both[LANES:, LANES:] - di[2 * kq + 1]
     for d in range(n_band):
         for j in range(n_ka):
             for g in range((k_dev + 1) // 2):

time: 151 us -> 151 us (level)
  no operation moved by 1% of the time
where the time goes in v22:
time: 151 us; the launch traced here: 150 us
  Pallas kernels  50.5 us (33%)
  blocking collectives  47.4 us (31%)
  starting transfers between devices  26.4 us (17%)
  waiting for transfers between devices  20.2 us (13%)
  local copies, waits for them, and re-layouts  4.8 us (3%)
    all_to_all x4, blocking collectives, exchange_all(): return lax.all_to_all(parts, AXES, split_axis=0, concat_axis=0, tiled=True)  47.4 us
    pallas_call x2, Pallas kernels, kernel_path(): call(functools.partial(direct_kernel, n_ka, tile, scale), 'direct', shape...  23.9 us
    ppermute x15, waiting for transfers between devices, swap(): lax.ppermute(block, axis, [(i, i ^ d) for i in range(lax.axis_size(axis))])  20.2 us
    ppermute x15, starting transfers between devices, swap(): lax.ppermute(block, axis, [(i, i ^ d) for i in range(lax.axis_size(axis))])  17.4 us
    pallas_call x2, Pallas kernels, kernel_path(): call(functools.partial(exchange_kernel, cfg, chunk, scale), 'exchange', m...  7.55 us
    pallas_call x1, Pallas kernels, kernel_path(): call(functools.partial(order_kernel, parts, n_ka), 'order', (shape_of((ro...  5.69 us
    all_to_all x2, starting transfers between devices, exchange_all(): return lax.all_to_all(parts, AXES, split_axis=0, concat_axis=0, tiled=True)  5.5 us
    pallas_call x2, Pallas kernels, kernel_path(): call(functools.partial(density_kernel, cfg), 'density', (shape_of((quads,...  4.49 us
  transfers between devices with their start and end apart: 18, of which 5 were waited for; matrix products, arithmetic and copies ran while one was open for 1% of the time, Pallas kernels for 25%

profile of v22, /device:TPU:0, one launch (start us, length us, event | category | flops | bytes accessed | tf_op | source)
XLA Modules:
  0.0 150.5 jit_solution(15287527374951154558)
XLA Ops:
  0.6 1.9 %pack.1 = (f32[16,128]{1,0:T(8,128)}, f32[16,128]{1,0:T(8,128)}, bf16[3,8,2176]{2,1,0:T(8,128)(2,1)}, bf16[3,8,2176]{2,1,0:T(8,128)(2,1)}, bf16[3,8,2176]{2,1,0:T(8,128)(2,1)}, /*index=5*/bf16[3,8,2176]{2,1,0:T(8,128)(2,1)}) custom-call(f32[3,512]{1,0:T(4,128)} %refs_0_.1, f32[3,64]{1,0:T(4,128)} %refs_1_.1, f32[3,8]{1,0:T(4,128)} %refs_2_.3, ...), custom_call_target="tpu_custom_call" | custom-call | tf_op jit(solution)/shard_map/pack/pallas_call | solution.py:498
  2.5 3.1 %collective-permute-start = (bf16[3,8,2176]{2,1,0:T(8,128)(2,1)}, bf16[3,8,2176]{2,1,0:T(8,128)(2,1)S(1)}, u32[]{:S(2)}, u32[]{:S(2)}) collective-permute-start(bf16[3,8,2176]{2,1,0:T(8,128)(2,1)} %get-tuple-element.53), channel_id=1, source_target_pairs={{0,8},{8,0},{16,24},{24,16},{1,9},{9,1},{17,25},{25,17},{2,10},{10... | collective-permute-start | bytes 313352 | tf_op jit(solution)/shard_map/ppermute | solution.py:458
  5.6 2.6 %collective-permute-start.1 = (bf16[3,8,2176]{2,1,0:T(8,128)(2,1)}, bf16[3,8,2176]{2,1,0:T(8,128)(2,1)S(1)}, u32[]{:S(2)}, u32[]{:S(2)}) collective-permute-start(bf16[3,8,2176]{2,1,0:T(8,128)(2,1)} %get-tuple-element.54), channel_id=1, source_target_pairs={{0,16},{8,24},{16,0},{24,8},{1,17},{9,25},{17,1},{25,9},{2,18},{10... | collective-permute-start | bytes 313352 | tf_op jit(solution)/shard_map/ppermute | solution.py:458
  8.2 1.8 %cut.1 = bf16[4,192,256]{2,1,0:T(8,128)(2,1)} custom-call(bf16[3,64,8192]{2,1,0:T(8,128)(2,1)} %cond_ref.1), custom_call_target="tpu_custom_call" | custom-call | tf_op jit(solution)/shard_map/cut/pallas_call | solution.py:515
  10.0 1.2 constant_dynamic-slice_fusion
  11.2 0.0 collective-permute-done
  11.3 5.5 %collective-permute-done.1 = bf16[3,8,2176]{2,1,0:T(8,128)(2,1)S(1)} collective-permute-done((bf16[3,8,2176]{2,1,0:T(8,128)(2,1)}, bf16[3,8,2176]{2,1,0:T(8,128)(2,1)S(1)}, u32[]{:S(2)}, u32[]{:S(2)}) %collective-permute-start.1) | collective-permute-done | bytes 104480 | tf_op jit(solution)/shard_map/ppermute | solution.py:458
  16.7 0.0 collective-permute-done.2
  16.7 0.1 maximum_bitcast_fusion.refs_0_
  16.8 1.6 %collective-permute-start.4 = (bf16[96,2176]{1,0:T(8,128)(2,1)S(1)}, bf16[96,2176]{1,0:T(8,128)(2,1)S(1)}, u32[]{:S(2)}, u32[]{:S(2)}) collective-permute-start(bf16[96,2176]{1,0:T(8,128)(2,1)S(1)} %maximum_bitcast_fusion.refs_0_), channel_id=1, source_target_pairs={{0,2},{1,3},{2,0},{3,1},{4,6},{5,7},{6,4},{7,5},{8,10},{9,11},{10,... | collective-permute-start | bytes 1253384 | tf_op jit(solution)/shard_map/ppermute | solution.py:458
  18.4 1.5 %collective-permute-start.5 = (bf16[96,2176]{1,0:T(8,128)(2,1)S(1)}, bf16[96,2176]{1,0:T(8,128)(2,1)S(1)}, u32[]{:S(2)}, u32[]{:S(2)}) collective-permute-start(bf16[96,2176]{1,0:T(8,128)(2,1)S(1)} %maximum_bitcast_fusion.refs_0_), channel_id=1, source_target_pairs={{0,4},{1,5},{2,6},{3,7},{4,0},{5,1},{6,2},{7,3},{8,12},{9,13},{10,... | collective-permute-start | bytes 1253384 | tf_op jit(solution)/shard_map/ppermute | solution.py:458
  19.9 1.7 %collective-permute-start.12 = (bf16[192,1024]{1,0:T(8,128)(2,1)S(1)}, bf16[192,1024]{1,0:T(8,128)(2,1)}, u32[]{:S(2)}, u32[]{:S(2)}) collective-permute-start(bf16[192,1024]{1,0:T(8,128)(2,1)S(1)} %bitcast.3), channel_id=1, source_target_pairs={{0,8},{8,0},{16,24},{24,16},{1,9},{9,1},{17,25},{25,17},{2,10},{10... | collective-permute-start | bytes 1179656 | tf_op jit(solution)/shard_map/ppermute | solution.py:458
  21.6 1.4 collective-permute-start.13
  22.9 3.5 %all-to-all-start = ((bf16[4,192,256]{2,1,0:T(8,128)(2,1)}), bf16[4,192,256]{2,1,0:T(8,128)(2,1)S(1)}, u32[]{:S(2)}, u32[]{:S(2)}) async-start(bf16[4,192,256]{2,1,0:T(8,128)(2,1)} %cut.1), calls=%async_computation | async-start | bytes 786432 | tf_op jit(solution)/shard_map/all_to_all | solution.py:528
  26.4 3.7 %turn.1.refs_1_ = bf16[2048,1024]{1,0:T(8,128)(2,1)} custom-call(bf16[1024,2048]{1,0:T(8,128)(2,1)} %scr_ref.1), custom_call_target="tpu_custom_call" | custom-call | bytes 8388608 | tf_op jit(solution)/shard_map/turn/pallas_call | solution.py:532
  30.2 0.6 collective-permute-start.8
  30.8 0.6 collective-permute-start.9
  31.4 6.8 %collective-permute-done.12.refs_5_ = bf16[192,1024]{1,0:T(8,128)(2,1)} collective-permute-done((bf16[192,1024]{1,0:T(8,128)(2,1)S(1)}, bf16[192,1024]{1,0:T(8,128)(2,1)}, u32[]{:S(2)}, u32[]{:S(2)}) %collective-permute-start.12) | collective-permute-done | bytes 393248 | tf_op jit(solution)/shard_map/ppermute | solution.py:458
  38.2 6.6 %collective-permute-done.13.refs_6_ = bf16[192,1024]{1,0:T(8,128)(2,1)} collective-permute-done((bf16[192,1024]{1,0:T(8,128)(2,1)S(1)}, bf16[192,1024]{1,0:T(8,128)(2,1)}, u32[]{:S(2)}, u32[]{:S(2)}) %collective-permute-start.13) | collective-permute-done | bytes 393248 | tf_op jit(solution)/shard_map/ppermute | solution.py:458
  44.8 3.9 %collective-permute-start.14 = (bf16[192,1024]{1,0:T(8,128)(2,1)S(1)}, bf16[192,1024]{1,0:T(8,128)(2,1)}, u32[]{:S(2)}, u32[]{:S(2)}) collective-permute-start(bf16[192,1024]{1,0:T(8,128)(2,1)S(1)} %bitcast.5), channel_id=1, source_target_pairs={{0,24},{8,16},{16,8},{24,0},{1,25},{9,17},{17,9},{25,1},{2,26},{10... | collective-permute-start | bytes 1179656 | tf_op jit(solution)/shard_map/ppermute | solution.py:458
  48.8 0.2 collective-permute-start.10
  49.0 0.3 collective-permute-start.11
  49.3 0.9 collective-permute-done.10.refs_8_
  50.2 0.3 collective-permute-done.11.refs_9_
  50.6 0.3 copy-done.14
  50.9 0.3 copy-done.15
  51.2 0.2 copy-done.9
  51.4 0.8 copy-done.10
  52.2 5.7 %order.1 = (bf16[768,2048]{1,0:T(8,128)(2,1)}, bf16[2048,768]{1,0:T(8,128)(2,1)}, bf16[768,256]{1,0:T(8,128)(2,1)}, bf16[32,16,128]{2,1,0:T(8,128)(2,1)}) custom-call(bf16[96,2176]{1,0:T(8,128)(2,1)} %copy-done.5, bf16[96,2176]{1,0:T(8,128)(2,1)} %copy-done.8, bf16[96,2176]{1,0:T(8,128)(2,1)} %copy-done.6, bf16[96,2176]{1,0:T(8,128)(2,1)} %copy-done.9, ...), custom_call_target="tpu_custom_call" | custom-call | bytes 9437184 | tf_op jit(solution)/shard_map/order/pallas_call | solution.py:544
  57.9 0.7 copy-done.4
  58.6 2.2 %density.2 = (bf16[3,256,256]{2,1,0:T(8,128)(2,1)}, f32[32,2,128]{2,1,0:T(2,128)}) custom-call(bf16[32,16,128]{2,1,0:T(8,128)(2,1)} %get-tuple-element.74.refs_0_.msgs_ref, bf16[768,256]{1,0:T(8,128)(2,1)} %get-tuple-element.75.refs_1_.refs_3_, bf16[4,192,256]{2,1,0:T(8,128)(2,1)} %copy-done.4), custom_call_target="tpu_custom_call" | custom-call | tf_op jit(solution)/shard_map/density/pallas_call | solution.py:571
  60.9 2.7 %all-to-all-start.1 = ((f32[32,2,128]{2,1,0:T(2,128)}), f32[32,2,128]{2,1,0:T(2,128)S(1)}, u32[]{:S(2)}, u32[]{:S(2)}) async-start(f32[32,2,128]{2,1,0:T(2,128)} %get-tuple-element.77), calls=%async_computation.1 | async-start | bytes 65536 | tf_op jit(solution)/shard_map/all_to_all | solution.py:31
  63.6 12.0 %direct.2.refs_1_ = f32[6,128,128]{2,1,0:T(8,128)} custom-call(bf16[2048,768]{1,0:T(8,128)(2,1)} %get-tuple-element.78.refs_0_, bf16[2048,1024]{1,0:T(8,128)(2,1)} %turn.1.refs_1_, bf16[768,2048]{1,0:T(8,128)(2,1)} %get-tuple-element.80.refs_2_, bf16[3,256,256]{2,1,0:T(8,128)(2,1)} %get-tuple-element.81.refs_3_, bf16[192,1024]{1,0:T(8,128)(2,1)} %bitcast.6, ...), custom_call_target="tpu_custom_call" | custom-call | flops 6442450944 | bytes 12582912 | tf_op jit(solution)/shard_map/direct/pallas_call | solution.py:589
  75.6 0.0 copy-start.3
  75.6 0.6 copy-done.17
  76.2 3.8 %exchange.2 = bf16[32,16,128]{2,1,0:T(8,128)(2,1)} custom-call(f32[32,2,128]{2,1,0:T(2,128)} %copy-done.17, f32[6,128,128]{2,1,0:T(8,128)} %direct.2.refs_1_, bf16[256,8192]{1,0:T(8,128)(2,1)} %refs_2_.5, bf16[768,256]{1,0:T(8,128)(2,1)} %get-tuple-element.75.refs_1_.refs_3_, bf16[4,192,256]{2,1,0:T(8,128)(2,1)} %copy-done.4), custom_call_target="tpu_custom_call" | custom-call | tf_op jit(solution)/shard_map/exchange/pallas_call | solution.py:612
  80.0 13.9 %all_to_all.35.recv_ref = bf16[32,16,128]{2,1,0:T(8,128)(2,1)S(1)} all-to-all(bf16[32,16,128]{2,1,0:T(8,128)(2,1)} %exchange.2), channel_id=1, replica_groups=mesh['ka'=4,'band'=8] {'ka','band'}, dimensions={0} | all-to-all | bytes 262144 | tf_op jit(solution)/shard_map/all_to_all | solution.py:31
  93.9 0.3 first_owner.1
  94.2 10.6 %all_to_all.36.refs_0_.msgs_ref = bf16[32,16,128]{2,1,0:T(8,128)(2,1)} all-to-all(bf16[32,16,128]{2,1,0:T(8,128)(2,1)S(1)} %get-tuple-element.86), channel_id=1, replica_groups=mesh['ka'=4,'band'=8] {'ka','band'}, dimensions={0} | all-to-all | bytes 262144 | tf_op jit(solution)/shard_map/all_to_all | solution.py:31
  104.8 2.2 %density.3 = (bf16[3,256,256]{2,1,0:T(8,128)(2,1)}, f32[32,2,128]{2,1,0:T(2,128)}) custom-call(bf16[32,16,128]{2,1,0:T(8,128)(2,1)} %all_to_all.36.refs_0_.msgs_ref, bf16[768,256]{1,0:T(8,128)(2,1)} %get-tuple-element.75.refs_1_.refs_3_, bf16[4,192,256]{2,1,0:T(8,128)(2,1)} %copy-done.4), custom_call_target="tpu_custom_call" | custom-call | tf_op jit(solution)/shard_map/density/pallas_call | solution.py:571
  107.1 2.8 %all-to-all-start.4 = ((f32[32,2,128]{2,1,0:T(2,128)}), f32[32,2,128]{2,1,0:T(2,128)S(1)}, u32[]{:S(2)}, u32[]{:S(2)}) async-start(f32[32,2,128]{2,1,0:T(2,128)} %get-tuple-element.87), calls=%async_computation.4 | async-start | bytes 65536 | tf_op jit(solution)/shard_map/all_to_all | solution.py:31
  109.9 12.0 %direct.3.refs_1_ = f32[6,128,128]{2,1,0:T(8,128)} custom-call(bf16[2048,768]{1,0:T(8,128)(2,1)} %get-tuple-element.78.refs_0_, bf16[2048,1024]{1,0:T(8,128)(2,1)} %turn.1.refs_1_, bf16[768,2048]{1,0:T(8,128)(2,1)} %get-tuple-element.80.refs_2_, bf16[3,256,256]{2,1,0:T(8,128)(2,1)} %get-tuple-element.88.refs_3_, bf16[192,1024]{1,0:T(8,128)(2,1)} %bitcast.7, ...), custom_call_target="tpu_custom_call" | custom-call | flops 6442450944 | bytes 12582912 | tf_op jit(solution)/shard_map/direct/pallas_call | solution.py:589
  121.9 0.6 copy-done.16
  122.5 3.8 %exchange.3 = bf16[32,16,128]{2,1,0:T(8,128)(2,1)} custom-call(f32[32,2,128]{2,1,0:T(2,128)} %copy-done.16, f32[6,128,128]{2,1,0:T(8,128)} %direct.3.refs_1_, bf16[256,8192]{1,0:T(8,128)(2,1)} %refs_2_.5, bf16[768,256]{1,0:T(8,128)(2,1)} %get-tuple-element.75.refs_1_.refs_3_, bf16[4,192,256]{2,1,0:T(8,128)(2,1)} %copy-done.4), custom_call_target="tpu_custom_call" | custom-call | tf_op jit(solution)/shard_map/exchange/pallas_call | solution.py:612
  126.3 13.9 %all_to_all.37.recv_ref = bf16[32,16,128]{2,1,0:T(8,128)(2,1)S(1)} all-to-all(bf16[32,16,128]{2,1,0:T(8,128)(2,1)} %exchange.3), channel_id=1, replica_groups=mesh['ka'=4,'band'=8] {'ka','band'}, dimensions={0} | all-to-all | bytes 262144 | tf_op jit(solution)/shard_map/all_to_all | solution.py:31
  140.1 0.4 second_owner.1
  140.5 9.0 %all_to_all.38.msgs_ref = f32[32,2,128]{2,1,0:T(2,128)S(1)} all-to-all(f32[32,2,128]{2,1,0:T(2,128)S(1)} %get-tuple-element.91), channel_id=1, replica_groups=mesh['ka'=4,'band'=8] {'ka','band'}, dimensions={0} | all-to-all | bytes 65536 | tf_op jit(solution)/shard_map/all_to_all | solution.py:31
  149.5 0.8 finish.1
  (47 shorter events, 0.1 us)
Async XLA Ops:
  2.5 14.2 %copy-start.18 = (bf16[3,8,2176]{2,1,0:T(8,128)(2,1)S(1)}, bf16[3,8,2176]{2,1,0:T(8,128)(2,1)}, u32[]{:S(2)}) copy-start(bf16[3,8,2176]{2,1,0:T(8,128)(2,1)} %get-tuple-element.57) | copy-start | bytes 313348
  2.5 8.7 %collective-permute-start = (bf16[3,8,2176]{2,1,0:T(8,128)(2,1)}, bf16[3,8,2176]{2,1,0:T(8,128)(2,1)S(1)}, u32[]{:S(2)}, u32[]{:S(2)}) collective-permute-start(bf16[3,8,2176]{2,1,0:T(8,128)(2,1)} %get-tuple-element.53), channel_id=1, source_target_pairs={{0,8},{8,0},{16,24},{24,16},{1,9},{9,1},{17,25},{25,17},{2,10},{10... | collective-permute-start | bytes 313352 | tf_op jit(solution)/shard_map/ppermute | solution.py:458
  5.6 11.1 %collective-permute-start.1 = (bf16[3,8,2176]{2,1,0:T(8,128)(2,1)}, bf16[3,8,2176]{2,1,0:T(8,128)(2,1)S(1)}, u32[]{:S(2)}, u32[]{:S(2)}) collective-permute-start(bf16[3,8,2176]{2,1,0:T(8,128)(2,1)} %get-tuple-element.54), channel_id=1, source_target_pairs={{0,16},{8,24},{16,0},{24,8},{1,17},{9,25},{17,1},{25,9},{2,18},{10... | collective-permute-start | bytes 313352 | tf_op jit(solution)/shard_map/ppermute | solution.py:458
  8.2 8.5 %collective-permute-start.2 = (bf16[3,8,2176]{2,1,0:T(8,128)(2,1)}, bf16[3,8,2176]{2,1,0:T(8,128)(2,1)S(1)}, u32[]{:S(2)}, u32[]{:S(2)}) collective-permute-start(bf16[3,8,2176]{2,1,0:T(8,128)(2,1)} %get-tuple-element.55), channel_id=1, source_target_pairs={{0,24},{8,16},{16,8},{24,0},{1,25},{9,17},{17,9},{25,1},{2,26},{10... | collective-permute-start | bytes 313352 | tf_op jit(solution)/shard_map/ppermute | solution.py:458
  11.2 33.6 %copy-start.11 = (bf16[3,64,1024]{2,1,0:T(8,128)(2,1)}, bf16[3,64,1024]{2,1,0:T(8,128)(2,1)S(1)}, u32[]{:S(2)}) copy-start(bf16[3,64,1024]{2,1,0:T(8,128)(2,1)S(1)} %constant_dynamic-slice_fusion) | copy-start | bytes 1179652
  16.8 13.3 %copy-start.5 = (bf16[96,2176]{1,0:T(8,128)(2,1)}, bf16[96,2176]{1,0:T(8,128)(2,1)S(1)}, u32[]{:S(2)}) copy-start(bf16[96,2176]{1,0:T(8,128)(2,1)S(1)} %maximum_bitcast_fusion.refs_0_) | copy-start | bytes 1253380
  16.8 13.3 %collective-permute-start.4 = (bf16[96,2176]{1,0:T(8,128)(2,1)S(1)}, bf16[96,2176]{1,0:T(8,128)(2,1)S(1)}, u32[]{:S(2)}, u32[]{:S(2)}) collective-permute-start(bf16[96,2176]{1,0:T(8,128)(2,1)S(1)} %maximum_bitcast_fusion.refs_0_), channel_id=1, source_target_pairs={{0,2},{1,3},{2,0},{3,1},{4,6},{5,7},{6,4},{7,5},{8,10},{9,11},{10,... | collective-permute-start | bytes 1253384 | tf_op jit(solution)/shard_map/ppermute | solution.py:458
  18.4 11.8 %collective-permute-start.5 = (bf16[96,2176]{1,0:T(8,128)(2,1)S(1)}, bf16[96,2176]{1,0:T(8,128)(2,1)S(1)}, u32[]{:S(2)}, u32[]{:S(2)}) collective-permute-start(bf16[96,2176]{1,0:T(8,128)(2,1)S(1)} %maximum_bitcast_fusion.refs_0_), channel_id=1, source_target_pairs={{0,4},{1,5},{2,6},{3,7},{4,0},{5,1},{6,2},{7,3},{8,12},{9,13},{10,... | collective-permute-start | bytes 1253384 | tf_op jit(solution)/shard_map/ppermute | solution.py:458
  19.9 18.3 %collective-permute-start.12 = (bf16[192,1024]{1,0:T(8,128)(2,1)S(1)}, bf16[192,1024]{1,0:T(8,128)(2,1)}, u32[]{:S(2)}, u32[]{:S(2)}) collective-permute-start(bf16[192,1024]{1,0:T(8,128)(2,1)S(1)} %bitcast.3), channel_id=1, source_target_pairs={{0,8},{8,0},{16,24},{24,16},{1,9},{9,1},{17,25},{25,17},{2,10},{10... | collective-permute-start | bytes 1179656 | tf_op jit(solution)/shard_map/ppermute | solution.py:458
  21.6 23.3 %collective-permute-start.13 = (bf16[192,1024]{1,0:T(8,128)(2,1)S(1)}, bf16[192,1024]{1,0:T(8,128)(2,1)}, u32[]{:S(2)}, u32[]{:S(2)}) collective-permute-start(bf16[192,1024]{1,0:T(8,128)(2,1)S(1)} %bitcast.4), channel_id=1, source_target_pairs={{0,16},{8,24},{16,0},{24,8},{1,17},{9,25},{17,1},{25,9},{2,18},{10... | collective-permute-start | bytes 1179656 | tf_op jit(solution)/shard_map/ppermute | solution.py:458
  22.9 21.9 %collective-permute-start.3 = (bf16[96,2176]{1,0:T(8,128)(2,1)S(1)}, bf16[96,2176]{1,0:T(8,128)(2,1)S(1)}, u32[]{:S(2)}, u32[]{:S(2)}) collective-permute-start(bf16[96,2176]{1,0:T(8,128)(2,1)S(1)} %maximum_bitcast_fusion.refs_0_), channel_id=1, source_target_pairs={{0,1},{1,0},{2,3},{3,2},{4,5},{5,4},{6,7},{7,6},{8,9},{9,8},{10,11... | collective-permute-start | bytes 1253384 | tf_op jit(solution)/shard_map/ppermute | solution.py:458
  22.9 34.9 %all-to-all-start = ((bf16[4,192,256]{2,1,0:T(8,128)(2,1)}), bf16[4,192,256]{2,1,0:T(8,128)(2,1)S(1)}, u32[]{:S(2)}, u32[]{:S(2)}) async-start(bf16[4,192,256]{2,1,0:T(8,128)(2,1)} %cut.1), calls=%async_computation | async-start | bytes 786432 | tf_op jit(solution)/shard_map/all_to_all | solution.py:528
  30.1 20.4 %copy-start.6 = (bf16[96,2176]{1,0:T(8,128)(2,1)}, bf16[96,2176]{1,0:T(8,128)(2,1)S(1)}, u32[]{:S(2)}) copy-start(bf16[96,2176]{1,0:T(8,128)(2,1)S(1)} %collective-permute-done.4.refs_2_) | copy-start | bytes 1253380
  30.1 20.4 %copy-start.7 = (bf16[96,2176]{1,0:T(8,128)(2,1)}, bf16[96,2176]{1,0:T(8,128)(2,1)S(1)}, u32[]{:S(2)}) copy-start(bf16[96,2176]{1,0:T(8,128)(2,1)S(1)} %collective-permute-done.5.refs_4_) | copy-start | bytes 1253380
  30.2 18.6 %collective-permute-start.8 = (bf16[48,2176]{1,0:T(8,128)(2,1)S(1)}, bf16[48,2176]{1,0:T(8,128)(2,1)S(1)}, u32[]{:S(2)}, u32[]{:S(2)}) collective-permute-start(bf16[48,2176]{1,0:T(8,128)(2,1)S(1)} %slice.6), channel_id=1, source_target_pairs={{0,4},{1,5},{2,6},{3,7},{4,0},{5,1},{6,2},{7,3},{8,12},{9,13},{10,... | collective-permute-start | bytes 626696 | tf_op jit(solution)/shard_map/ppermute | solution.py:458
  30.8 18.2 %collective-permute-start.9 = (bf16[48,2176]{1,0:T(8,128)(2,1)S(1)}, bf16[48,2176]{1,0:T(8,128)(2,1)S(1)}, u32[]{:S(2)}, u32[]{:S(2)}) collective-permute-start(bf16[48,2176]{1,0:T(8,128)(2,1)S(1)} %slice.7), channel_id=1, source_target_pairs={{0,2},{1,3},{2,0},{3,1},{4,6},{5,7},{6,4},{7,5},{8,10},{9,11},{10,... | collective-permute-start | bytes 626696 | tf_op jit(solution)/shard_map/ppermute | solution.py:458
  38.2 12.3 %collective-permute-start.6 = (bf16[96,2176]{1,0:T(8,128)(2,1)S(1)}, bf16[96,2176]{1,0:T(8,128)(2,1)S(1)}, u32[]{:S(2)}, u32[]{:S(2)}) collective-permute-start(bf16[96,2176]{1,0:T(8,128)(2,1)S(1)} %collective-permute-done.4.refs_2_), channel_id=1, source_target_pairs={{0,1},{1,0},{2,3},{3,2},{4,5},{5,4},{6,7},{7,6},{8,9},{9,8},{10,11... | collective-permute-start | bytes 1253384 | tf_op jit(solution)/shard_map/ppermute | solution.py:458
  44.8 5.7 %collective-permute-start.7 = (bf16[96,2176]{1,0:T(8,128)(2,1)S(1)}, bf16[96,2176]{1,0:T(8,128)(2,1)S(1)}, u32[]{:S(2)}, u32[]{:S(2)}) collective-permute-start(bf16[96,2176]{1,0:T(8,128)(2,1)S(1)} %collective-permute-done.5.refs_4_), channel_id=1, source_target_pairs={{0,1},{1,0},{2,3},{3,2},{4,5},{5,4},{6,7},{7,6},{8,9},{9,8},{10,11... | collective-permute-start | bytes 1253384 | tf_op jit(solution)/shard_map/ppermute | solution.py:458
  44.8 5.7 %copy-start.8 = (bf16[96,2176]{1,0:T(8,128)(2,1)}, bf16[96,2176]{1,0:T(8,128)(2,1)S(1)}, u32[]{:S(2)}) copy-start(bf16[96,2176]{1,0:T(8,128)(2,1)S(1)} %collective-permute-done.3.refs_1_) | copy-start | bytes 1253380
  44.8 18.7 %collective-permute-start.14 = (bf16[192,1024]{1,0:T(8,128)(2,1)S(1)}, bf16[192,1024]{1,0:T(8,128)(2,1)}, u32[]{:S(2)}, u32[]{:S(2)}) collective-permute-start(bf16[192,1024]{1,0:T(8,128)(2,1)S(1)} %bitcast.5), channel_id=1, source_target_pairs={{0,24},{8,16},{16,8},{24,0},{1,25},{9,17},{17,9},{25,1},{2,26},{10... | collective-permute-start | bytes 1179656 | tf_op jit(solution)/shard_map/ppermute | solution.py:458
  48.8 1.8 %copy-start.12 = (bf16[48,2176]{1,0:T(8,128)(2,1)}, bf16[48,2176]{1,0:T(8,128)(2,1)S(1)}, u32[]{:S(2)}) copy-start(bf16[48,2176]{1,0:T(8,128)(2,1)S(1)} %collective-permute-done.8.refs_6_) | copy-start | bytes 626692
  48.8 1.5 collective-permute-start.10
  49.0 1.6 %copy-start.13 = (bf16[48,2176]{1,0:T(8,128)(2,1)}, bf16[48,2176]{1,0:T(8,128)(2,1)S(1)}, u32[]{:S(2)}) copy-start(bf16[48,2176]{1,0:T(8,128)(2,1)S(1)} %collective-permute-done.9.refs_7_) | copy-start | bytes 626692
  49.0 1.5 %collective-permute-start.11 = (bf16[48,2176]{1,0:T(8,128)(2,1)S(1)}, bf16[48,2176]{1,0:T(8,128)(2,1)S(1)}, u32[]{:S(2)}, u32[]{:S(2)}) collective-permute-start(bf16[48,2176]{1,0:T(8,128)(2,1)S(1)} %collective-permute-done.9.refs_7_), channel_id=1, source_target_pairs={{0,1},{1,0},{2,3},{3,2},{4,5},{5,4},{6,7},{7,6},{8,9},{9,8},{10,11... | collective-permute-start | bytes 626696 | tf_op jit(solution)/shard_map/ppermute | solution.py:458
  50.2 0.7 copy-start.14
  50.5 0.7 copy-start.15
  50.5 0.9 copy-start.9
  51.4 0.8 copy-start.10
  57.9 0.7 copy-start.4
  60.9 14.7 %all-to-all-start.1 = ((f32[32,2,128]{2,1,0:T(2,128)}), f32[32,2,128]{2,1,0:T(2,128)S(1)}, u32[]{:S(2)}, u32[]{:S(2)}) async-start(f32[32,2,128]{2,1,0:T(2,128)} %get-tuple-element.77), calls=%async_computation.1 | async-start | bytes 65536 | tf_op jit(solution)/shard_map/all_to_all | solution.py:31
  75.6 18.3 %copy-start.1 = (bf16[32,16,128]{2,1,0:T(8,128)(2,1)S(1)}, bf16[32,16,128]{2,1,0:T(8,128)(2,1)}, u32[]{:S(2)}) copy-start(bf16[32,16,128]{2,1,0:T(8,128)(2,1)} %get-tuple-element.74.refs_0_.msgs_ref) | copy-start | bytes 393220
  75.6 18.3 %copy-start.2 = (f32[16,128]{1,0:T(8,128)S(1)}, f32[16,128]{1,0:T(8,128)}, u32[]{:S(2)}) copy-start(f32[16,128]{1,0:T(8,128)} %get-tuple-element.84.gap_ref) | copy-start | bytes 24580
  75.6 18.3 %copy-start.3 = (f32[16,128]{1,0:T(8,128)S(1)}, f32[16,128]{1,0:T(8,128)}, u32[]{:S(2)}) copy-start(f32[16,128]{1,0:T(8,128)} %get-tuple-element.85.own_ref) | copy-start | bytes 24580
  75.6 0.6 copy-start.17
  107.1 14.8 %all-to-all-start.4 = ((f32[32,2,128]{2,1,0:T(2,128)}), f32[32,2,128]{2,1,0:T(2,128)S(1)}, u32[]{:S(2)}, u32[]{:S(2)}) async-start(f32[32,2,128]{2,1,0:T(2,128)} %get-tuple-element.87), calls=%async_computation.4 | async-start | bytes 65536 | tf_op jit(solution)/shard_map/all_to_all | solution.py:31
  121.9 18.3 %copy-start = (bf16[32,16,128]{2,1,0:T(8,128)(2,1)S(1)}, bf16[32,16,128]{2,1,0:T(8,128)(2,1)}, u32[]{:S(2)}) copy-start(bf16[32,16,128]{2,1,0:T(8,128)(2,1)} %all_to_all.36.refs_0_.msgs_ref) | copy-start | bytes 393220
  121.9 0.6 copy-start.16
